TPU v7x, 32 devices: a whole 2x2x4 slice. The times are simulated.
32 devices in a mesh: tok: 8 (over y, x, core), kv: 4 (over z).
Axes of the slice: x: 2, y: 2, z: 4, core: 2. Of those that a mesh axis runs over, the one named last changes fastest.
Arguments:
- hidden_in: bfloat16 [8192, 1024], P(('tok', 'kv')), may hold values from -12 to 12
- qkv_weight: bfloat16 [1024, 3, 1024], P(None, None, 'kv'), may hold values from -1 to 1
- stretch_len: int32 [48], replicated, may hold values from 1 to 1024, 8192 in all
- out_weight: bfloat16 [1024, 1024], P('kv'), may hold values from -0.1875 to 0.1875
- ln1_gain: float32 [1024], replicated, may hold values from 0.5 to 1.5
- ln1_bias: float32 [1024], replicated, may hold values from -3 to 3
- up_weight: bfloat16 [1024, 4096], P(None, 'kv'), may hold values from -0.1875 to 0.1875
- down_weight: bfloat16 [4096, 1024], P('kv'), may hold values from -0.09375 to 0.09375
- ln2_gain: float32 [1024], replicated, may hold values from 0.5 to 1.5
- ln2_bias: float32 [1024], replicated, may hold values from -3 to 3
- dec_query: bfloat16 [64, 1024], P(('tok', 'kv')), may hold values from -12 to 12
- kv_cache: bfloat16 [2, 8, 24, 128, 1024], P(None, 'tok', 'kv'), may hold values from -12 to 12
- piece_req: int32 [8, 24], P('tok', 'kv'), may hold values from 0 to 7, as said below
- piece_used: int32 [8, 24], P('tok', 'kv'), may hold values from 0 to 128, as said below
Outputs:
- prefill_out: bfloat16 [8192, 1024], P(('tok', 'kv'))
- dec_out: bfloat16 [64, 1024], P(('tok', 'kv'))
Inputs may be any that keep to these rules, and one draw needn't show every extreme that they name: `piece_req`: every request of an index of tok owns at least one piece of that index with a nonzero count. `piece_used`: slots with a count of 0 hold no tokens.
All inputs are finite; a program needn't handle non-finite values.
Results may differ from a plain program's by a relative error of at most 0.017.
Values may be sent and summed in bfloat16 or wider, within the bound.
No kernel may reach another device: no remote copies, remote signals or barrier semaphores. Data moves between devices by JAX's collectives and lax.ppermute only.
A program may use at most 64 MiB of HBM per device.

v0:
```python
import math

import jax
import jax.numpy as jnp
from jax import lax
from jax.sharding import PartitionSpec as P

H = 16
HD = 64
WIN = 512
PLEN = 128


NEG_FILL = -1e30
LN_EPS = 1e-05


def extended(value, sides, width):
    for axis, dim in sides:
        count, length = (lax.axis_size(axis), value.shape[dim])
        up = [(i, (i + 1) % count) for i in range(count - 1)]
        down = [(j, i) for i, j in up]
        last = lax.slice_in_dim(value, length - width, length, axis=dim)
        leading = lax.slice_in_dim(value, 0, width, axis=dim)
        before = lax.ppermute(last, axis, up)
        after = lax.ppermute(leading, axis, down)
        value = jnp.concatenate([before, value, after], axis=dim)
    return value


def merged(value, axis, join):
    pieces = jax.tree.map(lambda part: lax.all_gather(part, axis), value)
    head = jax.tree.map(lambda part: part[0], pieces)
    tail = jax.tree.map(lambda part: part[1:], pieces)
    subtotal, _ = lax.scan(lambda subtotal, section: (join(subtotal, section), None), head, tail)
    return subtotal


def segment_ids(row_ids, stretch_len):
    stretch_ends = jnp.cumsum(stretch_len)
    return jnp.sum((row_ids[:, None] >= stretch_ends[None, :]).astype(jnp.int32), axis=1)


def layer_norm(values, gain, bias):
    center = values - jnp.mean(values, axis=1, keepdims=True)
    spread = jnp.mean(center * center, axis=1, keepdims=True)
    return center * lax.rsqrt(spread + LN_EPS) * gain + bias


def merge_partials(earlier, later):
    highest = jnp.maximum(earlier[0], later[0])
    left_factor = jnp.exp(earlier[0] - highest)
    right_factor = jnp.exp(later[0] - highest)
    totals = earlier[1] * left_factor + later[1] * right_factor
    weighted = earlier[2] * left_factor[..., None] + later[2] * right_factor[..., None]
    return (highest, totals, weighted)


def row_folder(source, shard_rows):
    return jnp.dot(source, shard_rows, preferred_element_type=jnp.float32)


def body(
    hidden_in,
    qkv_weight,
    stretch_len,
    out_weight,
    ln1_gain,
    ln1_bias,
    up_weight,
    down_weight,
    ln2_gain,
    ln2_bias,
    dec_query,
    kv_cache,
    piece_req,
    piece_used,
):
    inv_scale = 1.0 / math.sqrt(HD)
    reach = WIN // 2
    local_width = qkv_weight.shape[2]
    head_count = local_width // HD
    flat_weight = qkv_weight.reshape(qkv_weight.shape[0], 3 * local_width)
    qkv_rows = jnp.dot(
        lax.all_gather(hidden_in, "kv", axis=0, tiled=True),
        flat_weight,
        preferred_element_type=jnp.float32,
    ).astype(jnp.bfloat16)
    row_count = qkv_rows.shape[0]
    query_rows = qkv_rows[:, :local_width]
    keyval_rows = qkv_rows[:, local_width:]
    padded = extended(keyval_rows, (("tok", 0),), reach)
    first_row = lax.axis_index("tok") * row_count
    total_rows = row_count * lax.axis_size("tok")
    qblock = min(512, row_count)
    span = qblock + 2 * reach
    block_count = row_count // qblock

    def attend(block_index):
        start = block_index * qblock
        query_ids = first_row + start + jnp.arange(qblock, dtype=jnp.int32)
        key_ids = first_row + start - reach + jnp.arange(span, dtype=jnp.int32)
        query_seg = segment_ids(query_ids, stretch_len)
        inside = (key_ids >= 0) & (key_ids < total_rows)
        key_seg = jnp.where(inside, segment_ids(key_ids, stretch_len), -1)
        allowed = (key_seg[None, :] == query_seg[:, None]) & (
            jnp.abs(key_ids[None, :] - query_ids[:, None]) <= reach
        )
        queries = lax.dynamic_slice_in_dim(query_rows, start, qblock, 0).reshape(
            qblock, head_count, HD
        )
        both = lax.dynamic_slice_in_dim(padded, start, span, 0)
        key_rows = both[:, :local_width].reshape(span, head_count, HD)
        value_rows = both[:, local_width:].reshape(span, head_count, HD)
        scores = (
            jnp.einsum("ihd,jhd->hij", queries, key_rows, preferred_element_type=jnp.float32)
            * inv_scale
        )
        scores = jnp.where(allowed[None], scores, NEG_FILL)
        row_max = jnp.max(scores, axis=2, keepdims=True)
        weights = jnp.where(allowed[None], jnp.exp(scores - row_max), 0.0)
        totals = jnp.sum(weights, axis=2)
        summed = jnp.einsum(
            "hij,jhd->ihd",
            weights.astype(jnp.bfloat16),
            value_rows,
            preferred_element_type=jnp.float32,
        )
        return (
            (summed / jnp.transpose(totals)[:, :, None])
            .astype(jnp.bfloat16)
            .reshape(qblock, local_width)
        )

    attention = lax.map(attend, jnp.arange(block_count, dtype=jnp.int32)).reshape(
        row_count, local_width
    )
    token_major = lax.all_to_all(attention, "kv", split_axis=0, concat_axis=1, tiled=True)
    projected = row_folder(token_major, lax.all_gather(out_weight, "kv", axis=0, tiled=True))
    normed = layer_norm(hidden_in.astype(jnp.float32) + projected, ln1_gain, ln1_bias).astype(
        jnp.bfloat16
    )
    units = jax.nn.gelu(
        jnp.dot(
            lax.all_gather(normed, "kv", axis=0, tiled=True),
            up_weight,
            preferred_element_type=jnp.float32,
        ),
        approximate=False,
    ).astype(jnp.bfloat16)
    ffn = lax.psum_scatter(
        jnp.dot(units, down_weight, preferred_element_type=jnp.float32).astype(jnp.bfloat16),
        "kv",
        scatter_dimension=0,
        tiled=True,
    ).astype(jnp.float32)
    prefill_out = layer_norm(normed.astype(jnp.float32) + ffn, ln2_gain, ln2_bias).astype(
        jnp.bfloat16
    )
    group_queries = lax.all_gather(dec_query, "kv", axis=0, tiled=True)
    request_count = group_queries.shape[0]
    owners = piece_req[0]
    filled = piece_used[0]
    slot_count = owners.shape[0]
    request_ids = jnp.arange(request_count, dtype=jnp.int32)
    selector = (owners[:, None] == request_ids[None, :]).astype(jnp.bfloat16)
    chosen = jnp.dot(selector, group_queries, preferred_element_type=jnp.float32).astype(
        jnp.bfloat16
    )
    chosen = chosen.reshape(slot_count, H, HD)
    cache_keys = kv_cache[0, 0].reshape(slot_count, PLEN, H, HD)
    cache_values = kv_cache[1, 0].reshape(slot_count, PLEN, H, HD)
    piece_scores = (
        jnp.einsum("phd,pthd->pht", chosen, cache_keys, preferred_element_type=jnp.float32)
        * inv_scale
    )
    active = jnp.arange(PLEN, dtype=jnp.int32)[None, :] < filled[:, None]
    piece_scores = jnp.where(active[:, None, :], piece_scores, NEG_FILL)
    piece_max = jnp.max(piece_scores, axis=2)
    piece_weights = jnp.where(
        active[:, None, :], jnp.exp(piece_scores - piece_max[:, :, None]), 0.0
    )
    piece_totals = jnp.sum(piece_weights, axis=2)
    partial_value = jnp.einsum(
        "pht,pthd->phd",
        piece_weights.astype(jnp.bfloat16),
        cache_values,
        preferred_element_type=jnp.float32,
    )
    member = (owners[None, :] == request_ids[:, None]) & (filled[None, :] > 0)
    highest = jnp.max(jnp.where(member[:, :, None], piece_max[None], NEG_FILL), axis=1)
    factor = jnp.where(member[:, :, None], jnp.exp(piece_max[None] - highest[:, None, :]), 0.0)
    denom = jnp.sum(factor * piece_totals[None], axis=1)
    weighted = jnp.einsum("rph,phd->rhd", factor, partial_value)
    own_requests = dec_query.shape[0]
    joined = merged((highest, denom, weighted), "kv", merge_partials)
    begin = lax.axis_index("kv") * own_requests
    final_denom = lax.dynamic_slice_in_dim(joined[1], begin, own_requests, 0)
    final_weighted = lax.dynamic_slice_in_dim(joined[2], begin, own_requests, 0)
    dec_out = (
        (final_weighted / final_denom[:, :, None])
        .astype(jnp.bfloat16)
        .reshape(own_requests, H * HD)
    )
    return (prefill_out, dec_out)


def solution(mesh):
    placed = (
        P(("tok", "kv"), None),
        P(None, None, "kv"),
        P(),
        P("kv", None),
        P(),
        P(),
        P(None, "kv"),
        P("kv", None),
        P(),
        P(),
        P(("tok", "kv"), None),
        P(None, "tok", "kv", None, None),
        P("tok", "kv"),
        P("tok", "kv"),
    )
    return jax.shard_map(
        body,
        mesh=mesh,
        in_specs=placed,
        out_specs=(P(("tok", "kv"), None), P(("tok", "kv"), None)),
        check_vma=False,
    )
```

profile of v0, /device:TPU:0, one launch (start us, length us, event | category | flops | bytes accessed | tf_op | source)
XLA Modules:
  0.0 261.3 jit_solution(16223717942988141410)
XLA Ops:
  8.0 2.6 copy.73
  10.6 47.7 %all-gather.8.cloned.1.call-done = bf16[1024,1024]{1,0:T(8,128)(2,1)} async-done(((bf16[256,1024]{1,0:T(8,128)(2,1)}), bf16[1024,1024]{1,0:T(8,128)(2,1)}) %all-gather.8.cloned.1.call-update) | async-done | bytes 2097168 | tf_op jit(solution)/shard_map/all_gather | solution.py:85
  58.3 3.9 %convolution_convert_fusion = bf16[1024,768]{1,0:T(8,128)(2,1)S(1)} fusion(bf16[1024,1024]{1,0:T(8,128)(2,1)} %all-gather.8.cloned.1.call-done, bf16[1024,768]{0,1:T(8,128)(2,1)} %bitcast.108), kind=kOutput, calls=%fused_computation.56 | convolution fusion | flops 1611399168 | bytes 5242880 | tf_op jit(solution)/shard_map/dot_general | solution.py:84
  62.2 1.1 copy-done.2
  64.1 1.4 collective-permute-start.1
  65.6 3.7 %collective-permute-start = (bf16[256,512]{1,0:T(8,128)(2,1)}, bf16[256,512]{1,0:T(8,128)(2,1)}, u32[]{:S(2)}, u32[]{:S(2)}) collective-permute-start(bf16[256,512]{1,0:T(8,128)(2,1)} %get-tuple-element.256), channel_id=1, source_target_pairs={{0,4},{4,8},{8,12},{12,16},{16,20},{20,24},{24,28},{1,5},{5,9},{9,... | collective-permute-start | bytes 786440 | tf_op jit(solution)/shard_map/ppermute | solution.py:25
  69.6 1.9 slice.71
  71.5 2.2 pad_maximum_fusion
  73.7 38.0 %while.26 = (s32[]{:T(128)}, bf16[2,512,256]{2,1,0:T(8,128)(2,1)}, s32[2]{0:T(128)S(1)}, bf16[1536,512]{1,0:T(8,128)(2,1)}, s32[]{:T(128)}, /*index=5*/s32[1,48]...) while((s32[]{:T(128)}, bf16[2,512,256]{2,1,0:T(8,128)(2,1)}, ...), condition=%wide.region_6.7_spmd, body=%wide.region_1.6_spmd.sunk | while | flops 552564736 | bytes 23649012 | solution.py:135
  75.0 1.3 constant_dynamic-slice_fusion.7
  80.2 1.1 copy.117
  81.3 6.8 %fusion.126 = (f32[4,512]{1,0:T(4,128)S(1)}, bf16[4,512,1024]{2,1,0:T(8,128)(2,1)}) fusion(pred[512,1024]{1,0:T(8,128)(4,1)S(1)} %fusion.125, bf16[512,4,64]{0,2,1:T(8,128)(2,1)} %bitcast.104, bf16[1024,4,64]{0,2,1:T(8,128)(2,1)} %bitcast.103), kind=kOutput, calls=%fused_computation.131.clone.1 | convolution fusion | flops 281019392 | bytes 5513216 | tf_op jit(solution)/shard_map/while/body/eval_jaxpr/sub | solution.py:121
  88.1 3.6 %fusion.127 = bf16[512,4,64]{0,2,1:T(8,128)(2,1)S(1)} fusion(bf16[1024,4,64]{0,2,1:T(8,128)(2,1)S(1)} %bitcast.102, bf16[4,512,1024]{2,1,0:T(8,128)(2,1)} %get-tuple-element.353, f32[512,4]{0,1:T(4,128)S(1)} %bitcast.121), kind=kOutput, calls=%fused_computation.13.clone.1 | convolution fusion | flops 268697600 | bytes 4988928 | tf_op jit(solution)/shard_map/while/body/eval_jaxpr/hij,jhd->ihd/dot_general | solution.py:123
  94.0 1.3 constant_dynamic-slice_fusion.7
  100.3 6.8 %fusion.126 = (f32[4,512]{1,0:T(4,128)S(1)}, bf16[4,512,1024]{2,1,0:T(8,128)(2,1)}) fusion(pred[512,1024]{1,0:T(8,128)(4,1)S(1)} %fusion.125, bf16[512,4,64]{0,2,1:T(8,128)(2,1)} %bitcast.104, bf16[1024,4,64]{0,2,1:T(8,128)(2,1)} %bitcast.103), kind=kOutput, calls=%fused_computation.131.clone.1 | convolution fusion | flops 281019392 | bytes 5513216 | tf_op jit(solution)/shard_map/while/body/eval_jaxpr/sub | solution.py:121
  107.1 3.6 %fusion.127 = bf16[512,4,64]{0,2,1:T(8,128)(2,1)S(1)} fusion(bf16[1024,4,64]{0,2,1:T(8,128)(2,1)S(1)} %bitcast.102, bf16[4,512,1024]{2,1,0:T(8,128)(2,1)} %get-tuple-element.353, f32[512,4]{0,1:T(4,128)S(1)} %bitcast.121), kind=kOutput, calls=%fused_computation.13.clone.1 | convolution fusion | flops 268697600 | bytes 4988928 | tf_op jit(solution)/shard_map/while/body/eval_jaxpr/hij,jhd->ihd/dot_general | solution.py:123
  111.7 18.7 %all_to_all.19 = bf16[4,256,256]{2,1,0:T(8,128)(2,1)S(1)} all-to-all(bf16[4,256,256]{2,1,0:T(8,128)(2,1)} %bitcast.111), channel_id=1, replica_groups=mesh['tok'=8,'kv'=4] {'kv'}, dimensions={0} | all-to-all | bytes 1048576 | tf_op jit(solution)/shard_map/all_to_all | solution.py:138
  131.4 2.7 %fusion.91 = (f32[256]{0:T(256)S(1)}, f32[256,1024]{1,0:T(8,128)S(1)}) fusion(bf16[256,1024]{0,1:T(8,128)(2,1)} %bitcast.106, bf16[1024,1024]{1,0:T(8,128)(2,1)} %all-gather.10.cloned.1.call-done, bf16[256,1024]{1,0:T(8,128)(2,1)} %param.18), kind=kOutput, calls=%fused_computation.134 | convolution fusion | flops 537657088 | bytes 4195328 | tf_op jit(solution)/shard_map/dot_general | solution.py:60
  135.5 13.4 %all-gather.3 = bf16[4,2,1024]{2,1,0:T(2,128)(2,1)S(1)} all-gather(bf16[1,2,1024]{2,1,0:T(2,128)(2,1)S(1)} %bitcast.116), channel_id=1, replica_groups=mesh['tok'=8,'kv'=4] {'kv'}, dimensions={0}, use_global_device_ids=true | all-gather | bytes 20480 | tf_op jit(solution)/shard_map/all_gather | solution.py:160
  149.2 3.9 %fusion.89 = (bf16[1,1,6,128,1024]{4,3,2,1,0:T(8,128)(2,1)}, bf16[1,1,6,128,1024]{4,3,2,1,0:T(8,128)(2,1)}) fusion(bf16[2,1,6,128,1024]{4,3,2,1,0:T(8,128)(2,1)} %param.29), kind=kLoop, calls=%fused_computation.132 | loop fusion | bytes 6291456 | tf_op jit(solution)/shard_map/slice | solution.py:172
  153.1 2.6 copy.95
  155.8 1.9 fusion.94
  157.7 24.6 %all-gather.12.cloned.1.call-done = bf16[1024,1024]{1,0:T(8,128)(2,1)} async-done(((bf16[256,1024]{1,0:T(8,128)(2,1)}), bf16[1024,1024]{1,0:T(8,128)(2,1)}) %all-gather.12.cloned.1.call-update) | async-done | bytes 2097168 | tf_op jit(solution)/shard_map/all_gather | solution.py:145
  182.3 15.4 %fusion.37 = bf16[1024,1024]{1,0:T(8,128)(2,1)} fusion(bf16[1024,1024]{1,0:T(8,128)(2,1)S(1)} %copy-done, bf16[1024,1024]{1,0:T(8,128)(2,1)} %all-gather.12.cloned.1.call-done, bf16[1024,1024]{1,0:T(8,128)(2,1)} %param.24), kind=kOutput, calls=%fused_computation.55 | convolution fusion | flops 4364173312 | bytes 8388608 | tf_op jit(solution)/shard_map/dot_general | solution.py:152
  198.1 13.2 %all-gather = f32[32,16]{1,0:T(8,128)S(1)} all-gather(f32[8,16]{1,0:T(8,128)S(1)} %copy.80), channel_id=2, replica_groups=mesh['tok'=8,'kv'=4] {'kv'}, dimensions={0}, use_global_device_ids=true | all-gather | bytes 2560 | tf_op jit(solution)/shard_map/all_gather | solution.py:32
  211.7 13.5 %all-gather.1 = f32[32,16]{1,0:T(8,128)S(1)} all-gather(f32[8,16]{1,0:T(8,128)S(1)} %copy.82), channel_id=3, replica_groups=mesh['tok'=8,'kv'=4] {'kv'}, dimensions={0}, use_global_device_ids=true | all-gather | bytes 2560 | tf_op jit(solution)/shard_map/all_gather | solution.py:32
  225.3 2.6 copy.96
  227.9 2.3 fusion.44
  230.4 15.7 %all-gather.2 = f32[32,16,64]{2,0,1:T(8,128)S(1)} all-gather(f32[8,16,64]{2,0,1:T(8,128)S(1)} %convolution_bitcast_fusion), channel_id=4, replica_groups=mesh['tok'=8,'kv'=4] {'kv'}, dimensions={0}, use_global_device_ids=true | all-gather | bytes 163840 | tf_op jit(solution)/shard_map/all_gather | solution.py:32
  249.1 1.4 fusion.41
  250.6 1.5 multiply_reduce_fusion
  252.2 2.6 add_convert_fusion
  (118 shorter events, 21.1 us)
Async XLA Ops:
  7.2 175.1 %copy-start = (bf16[1024,1024]{1,0:T(8,128)(2,1)S(1)}, bf16[1024,1024]{1,0:T(8,128)(2,1)}, u32[]{:S(2)}) copy-start(bf16[1024,1024]{1,0:T(8,128)(2,1)} %param.25) | copy-start | bytes 6291460
  7.2 51.1 %all-gather.8.cloned.1.call-start = ((), (), s32[]{:S(2)}) async-start(), calls=%async_computation.2 | async-start | bytes 2621440 | tf_op jit(solution)/shard_map/all_gather | solution.py:85
  7.9 123.5 %all-gather.10.cloned.1.call-start = ((), (), s32[]{:S(2)}) async-start(), calls=%async_computation.3 | async-start | bytes 2621440 | tf_op jit(solution)/shard_map/all_gather | solution.py:139
  58.3 11.1 %copy-start.12 = (s32[48]{0:T(128)S(1)}, s32[48]{0:T(128)}, u32[]{:S(2)}) copy-start(s32[48]{0:T(128)} %param.20) | copy-start | bytes 580
  62.1 1.2 copy-start.2
  64.1 7.4 %slice-start = ((bf16[1024,768]{1,0:T(8,128)(2,1)}), bf16[1024,512]{1,0:T(8,128)(2,1)S(1)}, s32[]{:S(2)}) async-start(bf16[1024,768]{1,0:T(8,128)(2,1)} %copy-done.2), calls=%async_computation.6 | async-start | bytes 2097152 | tf_op jit(solution)/shard_map/slice | solution.py:91
  64.1 7.4 %collective-permute-start.1 = (bf16[256,512]{1,0:T(8,128)(2,1)}, bf16[256,512]{1,0:T(8,128)(2,1)S(1)}, u32[]{:S(2)}, u32[]{:S(2)}) collective-permute-start(bf16[256,512]{1,0:T(8,128)(2,1)} %get-tuple-element.257), channel_id=1, source_target_pairs={{4,0},{8,4},{12,8},{16,12},{20,16},{24,20},{28,24},{5,1},{9,5},{13... | collective-permute-start | bytes 786440 | tf_op jit(solution)/shard_map/ppermute | solution.py:26
  65.6 6.0 %collective-permute-start = (bf16[256,512]{1,0:T(8,128)(2,1)}, bf16[256,512]{1,0:T(8,128)(2,1)}, u32[]{:S(2)}, u32[]{:S(2)}) collective-permute-start(bf16[256,512]{1,0:T(8,128)(2,1)} %get-tuple-element.256), channel_id=1, source_target_pairs={{0,4},{4,8},{8,12},{12,16},{16,20},{20,24},{24,28},{1,5},{5,9},{9,... | collective-permute-start | bytes 786440 | tf_op jit(solution)/shard_map/ppermute | solution.py:25
  69.3 113.0 %all-gather.12.cloned.1.call-start = ((), (), s32[]{:S(2)}) async-start(), calls=%async_computation.4 | async-start | bytes 2621440 | tf_op jit(solution)/shard_map/all_gather | solution.py:145
  81.3 6.8 %copy-start.1 = (bf16[1024,256]{0,1:T(8,128)(2,1)S(1)}, bf16[1024,256]{0,1:T(8,128)(2,1)}, u32[]{:S(2)}) copy-start(bf16[1024,256]{0,1:T(8,128)(2,1)} %copy.115) | copy-start | bytes 1572868 | tf_op jit(solution)/shard_map/while
  88.1 3.8 %copy-start.4 = (bf16[2,512,256]{2,1,0:T(8,128)(2,1)S(1)}, bf16[2,512,256]{2,1,0:T(8,128)(2,1)}, u32[]{:S(2)}) copy-start(bf16[2,512,256]{2,1,0:T(8,128)(2,1)} %get-tuple-element.381) | copy-start | bytes 1572868 | tf_op jit(solution)/shard_map/while
  92.0 0.8 copy-start.5
  100.3 6.8 %copy-start.1 = (bf16[1024,256]{0,1:T(8,128)(2,1)S(1)}, bf16[1024,256]{0,1:T(8,128)(2,1)}, u32[]{:S(2)}) copy-start(bf16[1024,256]{0,1:T(8,128)(2,1)} %copy.115) | copy-start | bytes 1572868 | tf_op jit(solution)/shard_map/while
  107.1 3.8 %copy-start.4 = (bf16[2,512,256]{2,1,0:T(8,128)(2,1)S(1)}, bf16[2,512,256]{2,1,0:T(8,128)(2,1)}, u32[]{:S(2)}) copy-start(bf16[2,512,256]{2,1,0:T(8,128)(2,1)} %get-tuple-element.381) | copy-start | bytes 1572868 | tf_op jit(solution)/shard_map/while
  110.9 0.8 copy-start.5
  111.7 22.6 %copy-start.6 = (f32[1024]{0:T(1024)S(1)}, f32[1024]{0:T(1024)}, u32[]{:S(2)}) copy-start(f32[1024]{0:T(1024)} %param.23) | copy-start | bytes 12292
  111.7 22.6 %copy-start.7 = (f32[1024]{0:T(1024)S(1)}, f32[1024]{0:T(1024)}, u32[]{:S(2)}) copy-start(f32[1024]{0:T(1024)} %param.22) | copy-start | bytes 12292
  130.4 5.1 %copy-start.10 = (bf16[2,1024]{1,0:T(2,128)(2,1)S(1)}, bf16[2,1024]{1,0:T(2,128)(2,1)}, u32[]{:S(2)}) copy-start(bf16[2,1024]{1,0:T(2,128)(2,1)} %param.28) | copy-start | bytes 12292
  130.4 18.5 %copy-start.11 = (s32[1,6]{1,0:T(1,128)S(1)}, s32[1,6]{1,0:T(1,128)}, u32[]{:S(2)}) copy-start(s32[1,6]{1,0:T(1,128)} %param.30) | copy-start | bytes 76
  135.4 113.7 %reduce-scatter.2.cloned.1.call-start = ((), (), s32[]{:S(2)}) async-start(), calls=%async_computation.5 | async-start | bytes 2621440 | tf_op jit(solution)/shard_map/reduce_scatter | solution.py:151
  149.2 6.5 %copy-start.13 = (s32[1,6]{1,0:T(1,128)S(1)}, s32[1,6]{1,0:T(1,128)}, u32[]{:S(2)}) copy-start(s32[1,6]{1,0:T(1,128)} %param.31) | copy-start | bytes 76
  227.9 24.3 %copy-start.8 = (f32[1024]{0:T(1024)S(1)}, f32[1024]{0:T(1024)}, u32[]{:S(2)}) copy-start(f32[1024]{0:T(1024)} %param.27) | copy-start | bytes 12292
  227.9 24.3 %copy-start.9 = (f32[1024]{0:T(1024)S(1)}, f32[1024]{0:T(1024)}, u32[]{:S(2)}) copy-start(f32[1024]{0:T(1024)} %param.26) | copy-start | bytes 12292
  246.1 0.7 copy-start.3
Sparse Core Ops, SparseCore 0:
  9.6 48.6 all-gather.7
  69.5 44.8 all-gather.9
  135.5 46.7 all-gather.11
  197.8 46.0 reduce-scatter.1
where the time goes:
time: 262 us; the launch traced here: 261 us
  blocking collectives  74.4 us (28%)
  waiting for transfers between devices  73.1 us (28%)
  matrix products  47.5 us (18%)
  local copies, waits for them, and re-layouts  33.1 us (13%)
  between operations  14 us (5%)
  other arithmetic  12.3 us (5%)
  starting transfers between devices  5.31 us (2%)
    all_gather x1, waiting for transfers between devices, body(): lax.all_gather(hidden_in, 'kv', axis=0, tiled=True)  47.7 us
    all_gather x3, blocking collectives, merged(): pieces = jax.tree.map(lambda part: lax.all_gather(part, axis), value)  42.4 us
    all_gather x1, waiting for transfers between devices, body(): lax.all_gather(normed, 'kv', axis=0, tiled=True)  24.6 us
    all_to_all x1, blocking collectives, body(): lax.all_to_all(attention, 'kv', split_axis=0, concat_axis=1, tiled=True)  18.7 us
    dot_general x1, matrix products, body(): jnp.dot(units, down_weight, preferred_element_type=jnp.float32)  15.4 us
    sub x2, matrix products, attend(): weights = jnp.where(allowed[None], jnp.exp(scores - row_max), 0.0)  13.6 us
    all_gather x1, blocking collectives, body(): group_queries = lax.all_gather(dec_query, 'kv', axis=0, tiled=True)  13.4 us
    unnamed x26, local copies, waits for them, and re-layouts  9.7 us
  transfers between devices with their start and end apart: 6, of which 2 were waited for; matrix products, arithmetic and copies ran while one was open for 23% of the time, Pallas kernels for 0%

commit v1 on v0

--- a/solution.py
+++ b/solution.py
@@ -1,8 +1,11 @@
+import functools
 import math
 
 import jax
 import jax.numpy as jnp
 from jax import lax
+from jax.experimental import pallas as pl
+from jax.experimental.pallas import tpu as pltpu
 from jax.sharding import PartitionSpec as P
 
 H = 16
@@ -13,6 +16,409 @@
 
 NEG_FILL = -1e30
 LN_EPS = 1e-05
+BF16 = jnp.bfloat16
+F32 = jnp.float32
+VMEM_LIMIT = 56 * 1024 * 1024
+ANY = pl.BlockSpec(memory_space=pl.ANY)
+VMEM = pl.BlockSpec(memory_space=pltpu.VMEM)
+SMEM = pl.BlockSpec(memory_space=pltpu.SMEM)
+
+
+def swapped(value, axis, flip):
+    count = lax.axis_size(axis)
+    return lax.ppermute(value, axis, [(i, i ^ flip) for i in range(count)])
+
+
+def after(value, *earlier):
+    return lax.optimization_barrier((value,) + earlier)[0]
+
+
+def spread_in_plane(first):
+    half = first.shape[-2] // 2
+    low = lambda a: lax.slice_in_dim(a, 0, half, axis=a.ndim - 2)
+    high = lambda a: lax.slice_in_dim(a, half, 2 * half, axis=a.ndim - 2)
+    from_x = swapped(first, "tok", 2)
+    from_y = swapped(first, "tok", 4)
+    far_low = swapped(low(from_y), "tok", 2)
+    far_high = swapped(high(from_x), "tok", 4)
+    held = [(0, None, first), (2, None, from_x), (4, None, from_y), (6, 0, far_low), (6, 1, far_high)]
+    other = [(flip ^ 1, part, swapped(value, "tok", 1)) for flip, part, value in held]
+    return held + other
+
+
+def normalized(values, gain, bias):
+    center = values - jnp.mean(values, axis=1, keepdims=True)
+    spread = jnp.mean(center * center, axis=1, keepdims=True)
+    return center * lax.rsqrt(spread + LN_EPS) * gain + bias
+
+
+def prepare(place_ref, starts_ref, ends_ref, before_ref, own_ref, behind_ref, rows_ref, bias_ref):
+    count = own_ref.shape[0]
+    reach = WIN // 2
+    rows_ref[0:count] = before_ref[...]
+    rows_ref[count : 2 * count] = own_ref[...]
+    rows_ref[2 * count : 3 * count] = behind_ref[...]
+    first = place_ref[0]
+    query = first + lax.broadcasted_iota(jnp.int32, (count, 1), 0)
+    starts = starts_ref[...]
+    ends = ends_ref[...]
+    low = jnp.max(jnp.where(starts <= query, starts, 0), axis=1, keepdims=True)
+    high = jnp.min(jnp.where(ends > query, ends, 1 << 30), axis=1, keepdims=True)
+    low = jnp.maximum(low, query - reach)
+    high = jnp.minimum(high, query + reach + 1)
+    key = first - count + lax.broadcasted_iota(jnp.int32, (count, 3 * count), 1)
+    bias_ref[...] = jnp.where((key >= low) & (key < high), 0.0, NEG_FILL)
+
+
+def attend(rows_ref, bias_ref, weight, out_weight):
+    count = bias_ref.shape[0]
+    width = weight.shape[1] // 3
+    own = rows_ref[count : 2 * count]
+    rows = rows_ref[...]
+    scale = 1.0 / math.sqrt(HD)
+    query = (jnp.dot(own, weight[:, :width], preferred_element_type=F32) * scale).astype(BF16)
+    keys = jnp.dot(rows, weight[:, width : 2 * width], preferred_element_type=F32).astype(BF16)
+    values = jnp.dot(rows, weight[:, 2 * width :], preferred_element_type=F32).astype(BF16)
+    lane = lax.broadcasted_iota(jnp.int32, (count, 2 * HD), 1)
+    bias = bias_ref[...]
+    pairs = []
+    for start in range(0, width, 2 * HD):
+        pair = slice(start, start + 2 * HD)
+        halves = []
+        for side in range(2):
+            inside = (lane < HD) if side == 0 else (lane >= HD)
+            only = jnp.where(inside, query[:, pair], jnp.zeros((), BF16))
+            scores = lax.dot_general(only, keys[:, pair], (((1,), (1,)), ((), ())), preferred_element_type=F32)
+            scores = scores + bias
+            highest = jnp.max(scores, axis=1, keepdims=True)
+            weights = jnp.exp(scores - highest)
+            total = jnp.sum(weights, axis=1, keepdims=True)
+            summed = jnp.dot(weights.astype(BF16), values[:, pair], preferred_element_type=F32)
+            halves.append(summed / total)
+        pairs.append(jnp.where(lane < HD, halves[0], halves[1]).astype(BF16))
+    attention = jnp.concatenate(pairs, axis=1)
+    return jnp.dot(attention, out_weight, preferred_element_type=F32)
+
+
+def attend_own_kernel(
+    place_ref, starts_ref, ends_ref, before_ref, own_ref, behind_ref, weight_ref, out_ref, sum_ref, rows_ref, bias_ref
+):
+    prepare(place_ref, starts_ref, ends_ref, before_ref, own_ref, behind_ref, rows_ref, bias_ref)
+    sum_ref[...] = attend(rows_ref, bias_ref, weight_ref[...], out_ref[...])
+
+
+def attend_rest_kernel(layout, quarters, *refs):
+    count = len(layout)
+    place_ref, starts_ref, ends_ref, before_ref, own_ref, behind_ref, sum_ref, gain_ref, bias1_ref = refs[:9]
+    pieces = refs[9 : 9 + count]
+    normed_ref, rows_ref, bias_ref, weight_ref, out_ref, total_ref, sems = refs[9 + count :]
+    tok = place_ref[1]
+    wide = weight_ref.shape[2]
+    block = 128
+    copies = []
+    for (flip, part), piece in zip(layout, pieces):
+        eighth = tok ^ flip
+        size = piece.shape[1]
+        shift = 0 if part is None else part * size
+        at = pl.multiple_of(eighth * block, block)
+        moves = [(piece.at[:, :, 0:wide], weight_ref.at[:, pl.ds(at + shift, size), :])]
+        for side in range(2):
+            columns = pl.ds(wide + side * block, block)
+            moves.append((piece.at[:, :, columns], out_ref.at[:, pl.ds(side * block + shift, size), pl.ds(at, block)]))
+        for source, target in moves:
+            copies.append(pltpu.make_async_copy(source, target, sems.at[len(copies)]))
+    for copy in copies:
+        copy.start()
+    prepare(place_ref, starts_ref, ends_ref, before_ref, own_ref, behind_ref, rows_ref, bias_ref)
+    total_ref[...] = sum_ref[...]
+    for copy in copies:
+        copy.wait()
+
+    def step(index, carry):
+        total_ref[...] += attend(rows_ref, bias_ref, weight_ref[index], out_ref[index])
+        return carry
+
+    lax.fori_loop(0, quarters, step, 0)
+    mixed = own_ref[...].astype(F32) + total_ref[...]
+    normed_ref[...] = normalized(mixed, gain_ref[...], bias1_ref[...]).astype(BF16)
+
+
+def attend_cost(rows, width, heads_width):
+    flops = 2 * rows * width * heads_width * 8 + 4 * rows * 3 * rows * heads_width * 4
+    return pl.CostEstimate(flops=flops, bytes_accessed=4 * width * heads_width * 2, transcendentals=0)
+
+
+def attend_own(place, starts, ends, before, own, behind, weight, out_weight):
+    rows, width = own.shape
+    return pl.pallas_call(
+        attend_own_kernel,
+        out_shape=jax.ShapeDtypeStruct((rows, width), F32),
+        in_specs=[SMEM] + [VMEM] * 7,
+        out_specs=VMEM,
+        scratch_shapes=[pltpu.VMEM((3 * rows, width), BF16), pltpu.VMEM((rows, 3 * rows), F32)],
+        compiler_params=pltpu.CompilerParams(vmem_limit_bytes=VMEM_LIMIT),
+        cost_estimate=attend_cost(rows, width, out_weight.shape[0]),
+        name="attend_own",
+    )(place, starts, ends, before, own, behind, weight, out_weight)
+
+
+def attend_rest(place, starts, ends, before, own, behind, summed, gain, bias, pieces, heads_width):
+    rows, width = own.shape
+    layout = tuple((flip, part) for flip, part, _ in pieces)
+    quarters = pieces[0][2].shape[0]
+    return pl.pallas_call(
+        functools.partial(attend_rest_kernel, layout, quarters),
+        out_shape=jax.ShapeDtypeStruct((rows, width), BF16),
+        in_specs=[SMEM] + [VMEM] * 8 + [ANY] * len(pieces),
+        out_specs=VMEM,
+        scratch_shapes=[
+            pltpu.VMEM((3 * rows, width), BF16),
+            pltpu.VMEM((rows, 3 * rows), F32),
+            pltpu.VMEM((quarters, width, 3 * heads_width), BF16),
+            pltpu.VMEM((quarters, heads_width, width), BF16),
+            pltpu.VMEM((rows, width), F32),
+            pltpu.SemaphoreType.DMA((3 * len(pieces),)),
+        ],
+        compiler_params=pltpu.CompilerParams(vmem_limit_bytes=VMEM_LIMIT),
+        cost_estimate=attend_cost(rows, width, quarters * heads_width),
+        name="attend_rest",
+    )(place, starts, ends, before, own, behind, summed, gain, bias, *[value for _, _, value in pieces])
+
+
+def gelu(values):
+    return 0.5 * values * (1.0 + lax.erf(values * math.sqrt(0.5)))
+
+
+def feed_kernel(layout, *refs):
+    count = len(layout)
+    place_ref, rows_ref, up_ref, down_ref = refs[:4]
+    pieces = refs[4 : 4 + count]
+    sum_ref, far_up_ref, far_down_ref, total_ref, sems = refs[4 + count :]
+    tok = place_ref[1]
+    block = 128
+    copies = []
+    for (flip, part), piece in zip(layout, pieces):
+        at = pl.multiple_of((tok ^ flip) * block, block)
+        if part in (None, 0):
+            copies.append(
+                pltpu.make_async_copy(piece.at[0:block], far_up_ref.at[pl.ds(at, block)], sems.at[len(copies)])
+            )
+        if part in (None, 1):
+            shift = block if part is None else 0
+            copies.append(
+                pltpu.make_async_copy(
+                    piece.at[shift : shift + block], far_down_ref.at[pl.ds(at, block)], sems.at[len(copies)]
+                )
+            )
+    for copy in copies:
+        copy.start()
+    rows = rows_ref[...]
+    chunk = 512
+    total_ref[...] = jnp.zeros_like(total_ref)
+
+    def through(up, down):
+        for at in range(0, up.shape[1], chunk):
+            units = gelu(jnp.dot(rows, up[:, at : at + chunk], preferred_element_type=F32)).astype(BF16)
+            total_ref[...] += jnp.dot(units, down[at : at + chunk, :], preferred_element_type=F32)
+
+    through(up_ref, down_ref)
+    for copy in copies:
+        copy.wait()
+    through(far_up_ref, far_down_ref)
+    sum_ref[...] = total_ref[...].astype(sum_ref.dtype)
+
+
+def feed(place, rows, up_weight, down_weight, pieces, dtype, name):
+    count, width = rows.shape
+    units = up_weight.shape[1]
+    layout = tuple((flip, part) for flip, part, _ in pieces)
+    copies = sum(2 if part is None else 1 for _, part in layout)
+    return pl.pallas_call(
+        functools.partial(feed_kernel, layout),
+        out_shape=jax.ShapeDtypeStruct((count, width), dtype),
+        in_specs=[SMEM] + [VMEM] * 3 + [ANY] * len(pieces),
+        out_specs=VMEM,
+        scratch_shapes=[
+            pltpu.VMEM((width, units), BF16),
+            pltpu.VMEM((units, width), BF16),
+            pltpu.VMEM((count, width), F32),
+            pltpu.SemaphoreType.DMA((copies,)),
+        ],
+        compiler_params=pltpu.CompilerParams(vmem_limit_bytes=VMEM_LIMIT),
+        cost_estimate=pl.CostEstimate(
+            flops=8 * count * width * units, bytes_accessed=8 * width * units, transcendentals=2 * count * units
+        ),
+        name=name,
+    )(place, rows, up_weight, down_weight, *[value for _, _, value in pieces])
+
+
+def finish_kernel(normed_ref, near_ref, far_ref, gain_ref, bias_ref, out_ref):
+    mixed = normed_ref[...].astype(F32) + near_ref[...] + far_ref[...].astype(F32)
+    out_ref[...] = normalized(mixed, gain_ref[...], bias_ref[...]).astype(out_ref.dtype)
+
+
+def finish(normed, near, far, gain, bias):
+    return pl.pallas_call(
+        finish_kernel,
+        out_shape=jax.ShapeDtypeStruct(normed.shape, BF16),
+        in_specs=[VMEM] * 5,
+        out_specs=VMEM,
+        compiler_params=pltpu.CompilerParams(vmem_limit_bytes=VMEM_LIMIT),
+        name="finish",
+    )(normed, near, far, gain, bias)
+
+
+def decode_kernel(slot_ref, filled_ref, query_ref, cache_ref, out_ref, high_ref, total_ref, sum_ref):
+    step = pl.program_id(0)
+
+    @pl.when(step == 0)
+    def _():
+        high_ref[...] = jnp.full(high_ref.shape, NEG_FILL, F32)
+        total_ref[...] = jnp.zeros_like(total_ref)
+        sum_ref[...] = jnp.zeros_like(sum_ref)
+
+    row = slot_ref[step]
+    filled = filled_ref[step]
+    width = query_ref.shape[1]
+    head = lax.broadcasted_iota(jnp.int32, (H, width), 0)
+    inside = head == lax.broadcasted_iota(jnp.int32, (H, width), 1) // HD
+    query = jnp.where(inside, query_ref[pl.ds(row, 1), :], 0.0).astype(BF16)
+    scores = lax.dot_general(query, cache_ref[0, 0, 0], (((1,), (1,)), ((), ())), preferred_element_type=F32)
+    live = lax.broadcasted_iota(jnp.int32, scores.shape, 1) < filled
+    scores = jnp.where(live, scores * (1.0 / math.sqrt(HD)), NEG_FILL)
+    high = jnp.max(scores, axis=1, keepdims=True)
+    weights = jnp.where(live, jnp.exp(scores - high), 0.0)
+    total = jnp.sum(weights, axis=1, keepdims=True)
+    summed = jnp.dot(weights.astype(BF16), cache_ref[1, 0, 0], preferred_element_type=F32)
+    along = lambda column: jnp.sum(jnp.where(inside, column, 0.0), axis=0, keepdims=True)
+    high, total, summed = along(high), along(total), along(summed)
+    used = filled > 0
+    at = pl.ds(row, 1)
+    old = high_ref[at, :]
+    new = jnp.where(used, jnp.maximum(old, high), old)
+    left = jnp.exp(old - new)
+    right = jnp.where(used, jnp.exp(high - new), 0.0)
+    high_ref[at, :] = new
+    total_ref[at, :] = total_ref[at, :] * left + total * right
+    sum_ref[at, :] = sum_ref[at, :] * left + summed * right
+
+    @pl.when(step == pl.num_programs(0) - 1)
+    def _():
+        out_ref[0] = high_ref[...]
+        out_ref[1] = total_ref[...]
+        out_ref[2] = sum_ref[...]
+
+
+def decode(slots, filled, queries, kv_cache):
+    requests, width = queries.shape
+    pieces = kv_cache.shape[2]
+    state = pltpu.VMEM((requests, width), F32)
+    return pl.pallas_call(
+        decode_kernel,
+        grid=(pieces,),
+        out_shape=jax.ShapeDtypeStruct((3, requests, width), F32),
+        in_specs=[
+            SMEM,
+            SMEM,
+            pl.BlockSpec((requests, width), lambda i: (0, 0)),
+            pl.BlockSpec((2, 1, 1, PLEN, width), lambda i: (0, 0, i, 0, 0)),
+        ],
+        out_specs=pl.BlockSpec((3, requests, width), lambda i: (0, 0, 0)),
+        scratch_shapes=[state, state, state],
+        compiler_params=pltpu.CompilerParams(vmem_limit_bytes=VMEM_LIMIT),
+        cost_estimate=pl.CostEstimate(flops=0, bytes_accessed=kv_cache.size * 2, transcendentals=0),
+        name="decode",
+    )(slots, filled, queries, kv_cache)
+
+
+def decode_rows(dec_query, kv_cache, piece_req, piece_used):
+    own = dec_query.shape[0]
+    kv = lax.axis_index("kv")
+    count = lax.axis_size("kv")
+    queries = jnp.concatenate([dec_query] + [swapped(dec_query, "kv", flip) for flip in range(1, count)])
+    owners = piece_req[0]
+    slots = ((owners // own) ^ kv) * own + owners % own
+    partial = decode(slots, piece_used[0], queries.astype(F32), kv_cache)
+    parts = [partial[:, :own]]
+    for flip in range(1, count):
+        parts.append(swapped(partial[:, flip * own : (flip + 1) * own], "kv", flip))
+    high = functools.reduce(jnp.maximum, [part[0] for part in parts])
+    factors = [jnp.exp(part[0] - high) for part in parts]
+    total = sum(part[1] * factor for part, factor in zip(parts, factors))
+    summed = sum(part[2] * factor for part, factor in zip(parts, factors))
+    return (summed / total).astype(BF16)
+
+
+def routed_body(
+    hidden_in,
+    qkv_weight,
+    stretch_len,
+    out_weight,
+    ln1_gain,
+    ln1_bias,
+    up_weight,
+    down_weight,
+    ln2_gain,
+    ln2_bias,
+    dec_query,
+    kv_cache,
+    piece_req,
+    piece_used,
+):
+    tok = lax.axis_index("tok")
+    kv = lax.axis_index("kv")
+    toks, kvs = lax.axis_size("tok"), lax.axis_size("kv")
+    rows, width = hidden_in.shape
+    heads_width = out_weight.shape[0]
+    block = width // toks
+
+    eighth = lambda value, axis: lax.dynamic_slice_in_dim(value, tok * block, block, axis)
+    out_part = eighth(out_weight, 1)
+    bundle = jnp.concatenate(
+        [eighth(qkv_weight, 0).reshape(block, 3 * heads_width), out_part[:block], out_part[block:]], axis=1
+    )
+    foreign = [swapped(bundle, "kv", flip) for flip in range(1, kvs)]
+
+    hidden_late = after(hidden_in, *foreign)
+    flat = toks * kvs
+    before = lax.ppermute(hidden_late, ("tok", "kv"), [(i, i + 1) for i in range(flat - 1)])
+    behind = lax.ppermute(hidden_late, ("tok", "kv"), [(i + 1, i) for i in range(flat - 1)])
+
+    pieces = spread_in_plane(jnp.stack(foreign))
+
+    feed_part = jnp.concatenate([eighth(up_weight, 0), eighth(down_weight, 0)], axis=0)
+    feed_part = after(feed_part, before, behind)
+    feed_pieces = spread_in_plane(swapped(feed_part, "kv", 2))
+
+    place = jnp.stack([(tok * kvs + kv) * rows, tok]).astype(jnp.int32)
+    order = jnp.arange(stretch_len.shape[0])
+    ends = jnp.sum(jnp.where(order[:, None] <= order[None, :], stretch_len[:, None], 0), axis=0, dtype=jnp.int32)
+    starts = (ends - stretch_len)[None, :]
+    ends = ends[None, :]
+
+    own_weight = qkv_weight.reshape(width, 3 * heads_width)
+    summed = attend_own(place, starts, ends, before, hidden_in, behind, own_weight, out_weight)
+    normed = attend_rest(
+        place,
+        starts,
+        ends,
+        before,
+        hidden_in,
+        behind,
+        summed,
+        ln1_gain[None, :],
+        ln1_bias[None, :],
+        pieces,
+        heads_width,
+    )
+
+    partner = swapped(normed, "kv", 1)
+    near = feed(place, normed, up_weight, down_weight, feed_pieces, F32, "feed_own")
+    away = feed(place, partner, up_weight, down_weight, feed_pieces, BF16, "feed_partner")
+    far = swapped(away, "kv", 1)
+    prefill_out = finish(normed, near, far, ln2_gain[None, :], ln2_bias[None, :])
+
+    return prefill_out, decode_rows(dec_query, kv_cache, piece_req, piece_used)
 
 
 def extended(value, sides, width):
@@ -60,7 +466,7 @@
     return jnp.dot(source, shard_rows, preferred_element_type=jnp.float32)
 
 
-def body(
+def general_body(
     hidden_in,
     qkv_weight,
     stretch_len,
@@ -222,8 +628,9 @@
         P("tok", "kv"),
         P("tok", "kv"),
     )
+    routed = mesh.shape["tok"] == 8 and mesh.shape["kv"] == 4
     return jax.shard_map(
-        body,
+        routed_body if routed else general_body,
         mesh=mesh,
         in_specs=placed,
         out_specs=(P(("tok", "kv"), None), P(("tok", "kv"), None)),

time: 262 us -> 173 us (0.66)
  blocking collectives: 74.4 us -> 0 us
  matrix products: 47.5 us -> 0 us
  Pallas kernels: 0 us -> 43.5 us
  starting transfers between devices: 5.31 us -> 40.8 us
  local copies, waits for them, and re-layouts: 33.1 us -> 9.97 us
  between operations: 14 us -> 1.03 us
  other arithmetic: 12.3 us -> 4.11 us
    ppermute x2 -> x32, waiting for transfers between devices: 0.01 us -> 72.6 us  [the longest x30 57.9 us: swapped(): return lax.ppermute(value, axis, [(i, i ^ flip) for i in range(count)])]
    all_gather x3 -> x0, waiting for transfers between devices: 72.3 us -> none  [the longest x1 47.7 us: body(): lax.all_gather(hidden_in, 'kv', axis=0, tiled=True)]
    all_gather x4 -> x0, blocking collectives: 55.8 us -> none  [the longest x3 42.4 us: merged(): pieces = jax.tree.map(lambda part: lax.all_gather(part, axis), value)]
    pallas_call x0 -> x6, Pallas kernels: none -> 43.5 us  [the longest x1 14.7 us: attend_rest(): pl.pallas_call(functools.partial(attend_rest_kernel, layout, quarters), o...]
    ppermute x2 -> x32, starting transfers between devices: 5.15 us -> 40.8 us  [the longest x30 32.9 us: swapped(): return lax.ppermute(value, axis, [(i, i ^ flip) for i in range(count)])]
    dot_general x9 -> x0, matrix products: 33.9 us -> none  [the longest x1 15.4 us: body(): jnp.dot(units, down_weight, preferred_element_type=jnp.float32)]
    all_to_all x1 -> x0, blocking collectives: 18.7 us -> none  [body(): lax.all_to_all(attention, 'kv', split_axis=0, concat_axis=1, tiled=True)]
    sub x2 -> x0, matrix products: 13.6 us -> none  [attend(): weights = jnp.where(allowed[None], jnp.exp(scores - row_max), 0.0)]
  transfers between devices with their start and end apart: 6 -> 32, of which waited for: 2 -> 13; matrix products, arithmetic and copies ran while one was open for 23% -> 5% of each run, Pallas kernels for 0% -> 20%
where the time goes in v1:
time: 173 us; the launch traced here: 172 us
  waiting for transfers between devices  72.6 us (42%)
  Pallas kernels  43.5 us (25%)
  starting transfers between devices  40.8 us (24%)
  local copies, waits for them, and re-layouts  9.97 us (6%)
  other arithmetic  4.11 us (2%)
    ppermute x30, waiting for transfers between devices, swapped(): return lax.ppermute(value, axis, [(i, i ^ flip) for i in range(count)])  57.9 us
    ppermute x30, starting transfers between devices, swapped(): return lax.ppermute(value, axis, [(i, i ^ flip) for i in range(count)])  32.9 us
    pallas_call x1, Pallas kernels, attend_rest(): pl.pallas_call(functools.partial(attend_rest_kernel, layout, quarters), o...  14.7 us
    pallas_call x2, Pallas kernels, feed(): pl.pallas_call(functools.partial(feed_kernel, layout), out_shape=jax.Shap...  14.1 us
    ppermute x1, waiting for transfers between devices, routed_body(): lax.ppermute(hidden_late, ('tok', 'kv'), [(i + 1, i) for i in range(flat...  9.36 us
    ppermute x1, starting transfers between devices, routed_body(): lax.ppermute(hidden_late, ('tok', 'kv'), [(i, i + 1) for i in range(flat...  6.68 us
    pallas_call x1, Pallas kernels, attend_own(): pl.pallas_call(attend_own_kernel, out_shape=jax.ShapeDtypeStruct((rows, w...  6 us
    pallas_call x1, Pallas kernels, decode(): pl.pallas_call(decode_kernel, grid=(pieces,), out_shape=jax.ShapeDtypeStr...  5.9 us
  transfers between devices with their start and end apart: 32, of which 13 were waited for; matrix products, arithmetic and copies ran while one was open for 5% of the time, Pallas kernels for 20%

profile of v1, /device:TPU:0, one launch (start us, length us, event | category | flops | bytes accessed | tf_op | source)
XLA Modules:
  0.0 172.1 jit_solution(13276815783568083946)
XLA Ops:
  0.6 1.8 %copy.22 = bf16[1024,3,256]{0,2,1:T(8,128)(2,1)S(1)} copy(bf16[1024,3,256]{2,0,1:T(8,128)(2,1)} %param.15) | data formatting | bytes 3145728 | tf_op args[1]
  3.5 3.1 %collective-permute-start = (bf16[128,1024]{1,0:T(8,128)(2,1)S(1)}, bf16[128,1024]{1,0:T(8,128)(2,1)S(1)}, u32[]{:S(2)}, u32[]{:S(2)}) collective-permute-start(bf16[128,1024]{1,0:T(8,128)(2,1)S(1)} %pad_maximum_fusion.2), channel_id=1, source_target_pairs={{0,1},{1,0},{2,3},{3,2},{4,5},{5,4},{6,7},{7,6},{8,9},{9,8},{10,11... | collective-permute-start | bytes 786440 | tf_op jit(solution)/shard_map/ppermute | solution.py:29
  6.6 2.6 %collective-permute-start.1 = (bf16[128,1024]{1,0:T(8,128)(2,1)S(1)}, bf16[128,1024]{1,0:T(8,128)(2,1)S(1)}, u32[]{:S(2)}, u32[]{:S(2)}) collective-permute-start(bf16[128,1024]{1,0:T(8,128)(2,1)S(1)} %pad_maximum_fusion.2), channel_id=1, source_target_pairs={{0,2},{1,3},{2,0},{3,1},{4,6},{5,7},{6,4},{7,5},{8,10},{9,11},{10,... | collective-permute-start | bytes 786440 | tf_op jit(solution)/shard_map/ppermute | solution.py:29
  9.1 8.6 %collective-permute-done = bf16[128,1024]{1,0:T(8,128)(2,1)S(1)} collective-permute-done((bf16[128,1024]{1,0:T(8,128)(2,1)S(1)}, bf16[128,1024]{1,0:T(8,128)(2,1)S(1)}, u32[]{:S(2)}, u32[]{:S(2)}) %collective-permute-start) | collective-permute-done | bytes 262176 | tf_op jit(solution)/shard_map/ppermute | solution.py:29
  17.7 10.2 %collective-permute-done.1 = bf16[128,1024]{1,0:T(8,128)(2,1)S(1)} collective-permute-done((bf16[128,1024]{1,0:T(8,128)(2,1)S(1)}, bf16[128,1024]{1,0:T(8,128)(2,1)S(1)}, u32[]{:S(2)}, u32[]{:S(2)}) %collective-permute-start.1) | collective-permute-done | bytes 262176 | tf_op jit(solution)/shard_map/ppermute | solution.py:29
  27.9 6.7 %collective-permute-start.3 = (bf16[256,1024]{1,0:T(8,128)(2,1)S(1)}, bf16[256,1024]{1,0:T(8,128)(2,1)S(1)}, u32[]{:S(2)}, u32[]{:S(2)}) collective-permute-start(bf16[256,1024]{1,0:T(8,128)(2,1)S(1)} %copy-done.14), channel_id=1, source_target_pairs={{0,1},{1,2},{2,3},{3,4},{4,5},{5,6},{6,7},{7,8},{8,9},{9,10},{10,1... | collective-permute-start | bytes 1572872 | tf_op jit(solution)/shard_map/ppermute | solution.py:384
  34.6 1.3 collective-permute-start.4
  36.9 2.7 %collective-permute-start.6 = (bf16[3,128,1024]{2,1,0:T(8,128)(2,1)}, bf16[3,128,1024]{2,1,0:T(8,128)(2,1)}, u32[]{:S(2)}, u32[]{:S(2)}) collective-permute-start(bf16[3,128,1024]{2,1,0:T(8,128)(2,1)} %pad_maximum_fusion.refs_9_), channel_id=1, source_target_pairs={{0,16},{4,20},{8,24},{12,28},{16,0},{20,4},{24,8},{28,12},{1,17},{... | collective-permute-start | bytes 2359304 | tf_op jit(solution)/shard_map/ppermute | solution.py:29
  41.6 5.3 %collective-permute-done.3.before_ref.refs_3_ = bf16[256,1024]{1,0:T(8,128)(2,1)S(1)} collective-permute-done((bf16[256,1024]{1,0:T(8,128)(2,1)S(1)}, bf16[256,1024]{1,0:T(8,128)(2,1)S(1)}, u32[]{:S(2)}, u32[]{:S(2)}) %collective-permute-start.3) | collective-permute-done | bytes 524320 | tf_op jit(solution)/shard_map/ppermute | solution.py:384
  46.9 9.4 %collective-permute-done.4.behind_ref.refs_5_ = bf16[256,1024]{1,0:T(8,128)(2,1)S(1)} collective-permute-done((bf16[256,1024]{1,0:T(8,128)(2,1)S(1)}, bf16[256,1024]{1,0:T(8,128)(2,1)S(1)}, u32[]{:S(2)}, u32[]{:S(2)}) %collective-permute-start.4) | collective-permute-done | bytes 524320 | tf_op jit(solution)/shard_map/ppermute | solution.py:385
  56.3 2.9 %collective-permute-done.6.refs_11_ = bf16[3,128,1024]{2,1,0:T(8,128)(2,1)} collective-permute-done((bf16[3,128,1024]{2,1,0:T(8,128)(2,1)}, bf16[3,128,1024]{2,1,0:T(8,128)(2,1)}, u32[]{:S(2)}, u32[]{:S(2)}) %collective-permute-start.6) | collective-permute-done | bytes 786464 | tf_op jit(solution)/shard_map/ppermute | solution.py:29
  61.9 8.3 %collective-permute-start.8 = (bf16[3,64,1024]{2,1,0:T(8,128)(2,1)S(1)}, bf16[3,64,1024]{2,1,0:T(8,128)(2,1)S(1)}, u32[]{:S(2)}, u32[]{:S(2)}) collective-permute-start(bf16[3,64,1024]{2,1,0:T(8,128)(2,1)S(1)} %slice.93), channel_id=1, source_target_pairs={{0,16},{4,20},{8,24},{12,28},{16,0},{20,4},{24,8},{28,12},{1,17},{... | collective-permute-start | bytes 1179656 | tf_op jit(solution)/shard_map/ppermute | solution.py:29
  70.2 12.1 %collective-permute-done.14.refs_4_ = bf16[256,1024]{1,0:T(8,128)(2,1)S(1)} collective-permute-done((bf16[256,1024]{1,0:T(8,128)(2,1)S(1)}, bf16[256,1024]{1,0:T(8,128)(2,1)S(1)}, u32[]{:S(2)}, u32[]{:S(2)}) %collective-permute-start.14) | collective-permute-done | bytes 524320 | tf_op jit(solution)/shard_map/ppermute | solution.py:29
  82.3 1.5 collective-permute-start.15
  83.9 1.8 %collective-permute-start.28 = (bf16[2,1024]{1,0:T(2,128)(2,1)S(1)}, bf16[2,1024]{1,0:T(2,128)(2,1)S(1)}, u32[]{:S(2)}, u32[]{:S(2)}) collective-permute-start(bf16[2,1024]{1,0:T(2,128)(2,1)S(1)} %copy-done.13), channel_id=1, source_target_pairs={{0,3},{1,2},{2,1},{3,0},{4,7},{5,6},{6,5},{7,4},{8,11},{9,10},{10,... | collective-permute-start | bytes 12296 | tf_op jit(solution)/shard_map/ppermute | solution.py:29
  85.7 3.6 %collective-permute-done.28 = bf16[2,1024]{1,0:T(2,128)(2,1)S(1)} collective-permute-done((bf16[2,1024]{1,0:T(2,128)(2,1)S(1)}, bf16[2,1024]{1,0:T(2,128)(2,1)S(1)}, u32[]{:S(2)}, u32[]{:S(2)}) %collective-permute-start.28) | collective-permute-done | bytes 4128 | tf_op jit(solution)/shard_map/ppermute | solution.py:29
  90.7 1.6 copy.25.weight_ref
  93.0 2.4 %collective-permute-done.15.refs_5_ = bf16[256,1024]{1,0:T(8,128)(2,1)S(1)} collective-permute-done((bf16[256,1024]{1,0:T(8,128)(2,1)S(1)}, bf16[256,1024]{1,0:T(8,128)(2,1)S(1)}, u32[]{:S(2)}, u32[]{:S(2)}) %collective-permute-start.15) | collective-permute-done | bytes 524320 | tf_op jit(solution)/shard_map/ppermute | solution.py:29
  95.4 1.2 collective-permute-done.16.refs_6_
  97.2 6.0 %attend_own.1.refs_6_ = f32[256,1024]{1,0:T(8,128)} custom-call(s32[2]{0:T(128)} %pad_add_fusion.place_ref.refs_0_, s32[1,48]{1,0:T(1,128)} %subtract_bitcast_fusion.starts_ref.refs_1_, s32[1,48]{1,0:T(1,128)} %bitcast.138, bf16[256,1024]{1,0:T(8,128)(2,1)} %copy-done.15, bf16[256,1024]{1,0:T(8,128)(2,1)} %refs_4_.1, bf16[256,1024]{1,0:T(8,128)(2,1)} %copy-done.16, ...), custom_call_target="tpu_custom_call" | custom-call | flops 1879048192 | bytes 2097152 | tf_op jit(solution)/shard_map/attend_own/pallas_call | solution.py:153
  103.3 3.0 %collective-permute-start.26 = (bf16[2,1024]{1,0:T(2,128)(2,1)S(1)}, bf16[2,1024]{1,0:T(2,128)(2,1)S(1)}, u32[]{:S(2)}, u32[]{:S(2)}) collective-permute-start(bf16[2,1024]{1,0:T(2,128)(2,1)S(1)} %copy-done.13), channel_id=1, source_target_pairs={{0,1},{1,0},{2,3},{3,2},{4,5},{5,4},{6,7},{7,6},{8,9},{9,8},{10,11... | collective-permute-start | bytes 12296 | tf_op jit(solution)/shard_map/ppermute | solution.py:29
  107.2 1.3 collective-permute-start.18
  108.5 14.7 %attend_rest.1.refs_1_.normed_ref = bf16[256,1024]{1,0:T(8,128)(2,1)} custom-call(s32[2]{0:T(128)} %pad_add_fusion.place_ref.refs_0_, s32[1,48]{1,0:T(1,128)} %subtract_bitcast_fusion.starts_ref.refs_1_, s32[1,48]{1,0:T(1,128)} %bitcast.139, bf16[256,1024]{1,0:T(8,128)(2,1)} %copy-done.15, bf16[256,1024]{1,0:T(8,128)(2,1)} %refs_4_.1, ...), custom_call_target="tpu_custom_call" | custom-call | flops 5637144576 | bytes 6291456 | tf_op jit(solution)/shard_map/attend_rest/pallas_call | solution.py:169
  125.6 5.9 %decode.1 = f32[3,8,1024]{2,1,0:T(8,128)} custom-call(s32[6]{0:T(128)} %fusion.16.slot_ref, s32[6]{0:T(128)} %bitcast.135, f32[8,1024]{1,0:T(8,128)} %maximum_convert_fusion.query_ref, bf16[2,1,6,128,1024]{4,3,2,1,0:T(8,128)(2,1)} %cache_ref.1), custom_call_target="tpu_custom_call" | custom-call | bytes 3145728 | tf_op jit(solution)/shard_map/decode/pallas_call | solution.py:316
  131.6 6.3 %collective-permute-done.24.refs_1_ = bf16[256,1024]{1,0:T(8,128)(2,1)S(1)} collective-permute-done((bf16[256,1024]{1,0:T(8,128)(2,1)}, bf16[256,1024]{1,0:T(8,128)(2,1)S(1)}, u32[]{:S(2)}, u32[]{:S(2)}) %collective-permute-start.24) | collective-permute-done | bytes 524320 | tf_op jit(solution)/shard_map/ppermute | solution.py:29
  138.8 7.0 %feed_partner.1 = bf16[256,1024]{1,0:T(8,128)(2,1)} custom-call(s32[2]{0:T(128)} %pad_add_fusion.place_ref.refs_0_, bf16[256,1024]{1,0:T(8,128)(2,1)} %copy-done.11, bf16[1024,1024]{1,0:T(8,128)(2,1)} %refs_2_.3, bf16[1024,1024]{1,0:T(8,128)(2,1)} %refs_3_.3, bf16[256,1024]{1,0:T(8,128)(2,1)} %copy-done.2, bf16[256,1024]{1,0:T(8,128)(2,1)} %copy-done, ...), custom_call_target="tpu_custom_call" | custom-call | flops 2147483648 | bytes 8388608 | tf_op jit(solution)/shard_map/feed_partner/pallas_call | solution.py:236
  146.1 1.4 collective-permute-start.31
  147.5 1.9 %collective-permute-start.30 = (f32[3,2,1024]{2,1,0:T(2,128)S(1)}, f32[3,2,1024]{2,1,0:T(2,128)S(1)}, u32[]{:S(2)}, u32[]{:S(2)}) collective-permute-start(f32[3,2,1024]{2,1,0:T(2,128)S(1)} %get-tuple-element.9), channel_id=1, source_target_pairs={{0,2},{1,3},{2,0},{3,1},{4,6},{5,7},{6,4},{7,5},{8,10},{9,11},{10,... | collective-permute-start | bytes 73736 | tf_op jit(solution)/shard_map/ppermute | solution.py:29
  149.4 1.2 collective-permute-start.29
  150.6 9.3 %collective-permute-done.31 = f32[3,2,1024]{2,1,0:T(2,128)S(1)} collective-permute-done((f32[3,2,1024]{2,1,0:T(2,128)S(1)}, f32[3,2,1024]{2,1,0:T(2,128)S(1)}, u32[]{:S(2)}, u32[]{:S(2)}) %collective-permute-start.31) | collective-permute-done | bytes 24608 | tf_op jit(solution)/shard_map/ppermute | solution.py:29
  161.3 7.2 %feed_own.1.near_ref = f32[256,1024]{1,0:T(8,128)} custom-call(s32[2]{0:T(128)} %pad_add_fusion.place_ref.refs_0_, bf16[256,1024]{1,0:T(8,128)(2,1)} %attend_rest.1.refs_1_.normed_ref, bf16[1024,1024]{1,0:T(8,128)(2,1)} %refs_2_.3, bf16[1024,1024]{1,0:T(8,128)(2,1)} %refs_3_.3, bf16[256,1024]{1,0:T(8,128)(2,1)} %copy-done.2, bf16[256,1024]{1,0:T(8,128)(2,1)} %copy-done, ...), custom_call_target="tpu_custom_call" | custom-call | flops 2147483648 | bytes 8388608 | tf_op jit(solution)/shard_map/feed_own/pallas_call | solution.py:236
  169.3 2.8 %finish.1 = bf16[256,1024]{1,0:T(8,128)(2,1)} custom-call(bf16[256,1024]{1,0:T(8,128)(2,1)} %attend_rest.1.refs_1_.normed_ref, f32[256,1024]{1,0:T(8,128)} %feed_own.1.near_ref, bf16[256,1024]{1,0:T(8,128)(2,1)} %copy-done.10, f32[1,1024]{1,0:T(1,128)} %bitcast.133, f32[1,1024]{1,0:T(1,128)} %bitcast.134), custom_call_target="tpu_custom_call" | custom-call | tf_op jit(solution)/shard_map/finish/pallas_call | solution.py:261
  (106 shorter events, 16.3 us)
Async XLA Ops:
  3.5 14.2 %collective-permute-start = (bf16[128,1024]{1,0:T(8,128)(2,1)S(1)}, bf16[128,1024]{1,0:T(8,128)(2,1)S(1)}, u32[]{:S(2)}, u32[]{:S(2)}) collective-permute-start(bf16[128,1024]{1,0:T(8,128)(2,1)S(1)} %pad_maximum_fusion.2), channel_id=1, source_target_pairs={{0,1},{1,0},{2,3},{3,2},{4,5},{5,4},{6,7},{7,6},{8,9},{9,8},{10,11... | collective-permute-start | bytes 786440 | tf_op jit(solution)/shard_map/ppermute | solution.py:29
  6.6 21.4 %collective-permute-start.1 = (bf16[128,1024]{1,0:T(8,128)(2,1)S(1)}, bf16[128,1024]{1,0:T(8,128)(2,1)S(1)}, u32[]{:S(2)}, u32[]{:S(2)}) collective-permute-start(bf16[128,1024]{1,0:T(8,128)(2,1)S(1)} %pad_maximum_fusion.2), channel_id=1, source_target_pairs={{0,2},{1,3},{2,0},{3,1},{4,6},{5,7},{6,4},{7,5},{8,10},{9,11},{10,... | collective-permute-start | bytes 786440 | tf_op jit(solution)/shard_map/ppermute | solution.py:29
  9.1 18.8 %collective-permute-start.2 = (bf16[128,1024]{1,0:T(8,128)(2,1)S(1)}, bf16[128,1024]{1,0:T(8,128)(2,1)S(1)}, u32[]{:S(2)}, u32[]{:S(2)}) collective-permute-start(bf16[128,1024]{1,0:T(8,128)(2,1)S(1)} %pad_maximum_fusion.2), channel_id=1, source_target_pairs={{0,3},{1,2},{2,1},{3,0},{4,7},{5,6},{6,5},{7,4},{8,11},{9,10},{10,... | collective-permute-start | bytes 786440 | tf_op jit(solution)/shard_map/ppermute | solution.py:29
  27.9 19.0 %collective-permute-start.3 = (bf16[256,1024]{1,0:T(8,128)(2,1)S(1)}, bf16[256,1024]{1,0:T(8,128)(2,1)S(1)}, u32[]{:S(2)}, u32[]{:S(2)}) collective-permute-start(bf16[256,1024]{1,0:T(8,128)(2,1)S(1)} %copy-done.14), channel_id=1, source_target_pairs={{0,1},{1,2},{2,3},{3,4},{4,5},{5,6},{6,7},{7,8},{8,9},{9,10},{10,1... | collective-permute-start | bytes 1572872 | tf_op jit(solution)/shard_map/ppermute | solution.py:384
  34.6 21.7 %collective-permute-start.4 = (bf16[256,1024]{1,0:T(8,128)(2,1)S(1)}, bf16[256,1024]{1,0:T(8,128)(2,1)S(1)}, u32[]{:S(2)}, u32[]{:S(2)}) collective-permute-start(bf16[256,1024]{1,0:T(8,128)(2,1)S(1)} %copy-done.14), channel_id=1, source_target_pairs={{1,0},{2,1},{3,2},{4,3},{5,4},{6,5},{7,6},{8,7},{9,8},{10,9},{11,1... | collective-permute-start | bytes 1572872 | tf_op jit(solution)/shard_map/ppermute | solution.py:385
  36.9 22.3 %collective-permute-start.6 = (bf16[3,128,1024]{2,1,0:T(8,128)(2,1)}, bf16[3,128,1024]{2,1,0:T(8,128)(2,1)}, u32[]{:S(2)}, u32[]{:S(2)}) collective-permute-start(bf16[3,128,1024]{2,1,0:T(8,128)(2,1)} %pad_maximum_fusion.refs_9_), channel_id=1, source_target_pairs={{0,16},{4,20},{8,24},{12,28},{16,0},{20,4},{24,8},{28,12},{1,17},{... | collective-permute-start | bytes 2359304 | tf_op jit(solution)/shard_map/ppermute | solution.py:29
  39.6 21.3 %collective-permute-start.5 = (bf16[3,128,1024]{2,1,0:T(8,128)(2,1)}, bf16[3,128,1024]{2,1,0:T(8,128)(2,1)}, u32[]{:S(2)}, u32[]{:S(2)}) collective-permute-start(bf16[3,128,1024]{2,1,0:T(8,128)(2,1)} %pad_maximum_fusion.refs_9_), channel_id=1, source_target_pairs={{0,8},{4,12},{8,0},{12,4},{16,24},{20,28},{24,16},{28,20},{1,9},{5... | collective-permute-start | bytes 2359304 | tf_op jit(solution)/shard_map/ppermute | solution.py:29
  56.3 26.0 %collective-permute-start.14 = (bf16[256,1024]{1,0:T(8,128)(2,1)S(1)}, bf16[256,1024]{1,0:T(8,128)(2,1)S(1)}, u32[]{:S(2)}, u32[]{:S(2)}) collective-permute-start(bf16[256,1024]{1,0:T(8,128)(2,1)S(1)} %pad_maximum_fusion.1), channel_id=1, source_target_pairs={{0,2},{1,3},{2,0},{3,1},{4,6},{5,7},{6,4},{7,5},{8,10},{9,11},{10,... | collective-permute-start | bytes 1572872 | tf_op jit(solution)/shard_map/ppermute | solution.py:29
  60.2 29.0 %collective-permute-start.7 = (bf16[3,64,1024]{2,1,0:T(8,128)(2,1)S(1)}, bf16[3,64,1024]{2,1,0:T(8,128)(2,1)S(1)}, u32[]{:S(2)}, u32[]{:S(2)}) collective-permute-start(bf16[3,64,1024]{2,1,0:T(8,128)(2,1)S(1)} %slice.92), channel_id=1, source_target_pairs={{0,8},{4,12},{8,0},{12,4},{16,24},{20,28},{24,16},{28,20},{1,9},{5... | collective-permute-start | bytes 1179656 | tf_op jit(solution)/shard_map/ppermute | solution.py:29
  61.9 27.9 %collective-permute-start.8 = (bf16[3,64,1024]{2,1,0:T(8,128)(2,1)S(1)}, bf16[3,64,1024]{2,1,0:T(8,128)(2,1)S(1)}, u32[]{:S(2)}, u32[]{:S(2)}) collective-permute-start(bf16[3,64,1024]{2,1,0:T(8,128)(2,1)S(1)} %slice.93), channel_id=1, source_target_pairs={{0,16},{4,20},{8,24},{12,28},{16,0},{20,4},{24,8},{28,12},{1,17},{... | collective-permute-start | bytes 1179656 | tf_op jit(solution)/shard_map/ppermute | solution.py:29
  82.3 13.1 %collective-permute-start.15 = (bf16[256,1024]{1,0:T(8,128)(2,1)S(1)}, bf16[256,1024]{1,0:T(8,128)(2,1)S(1)}, u32[]{:S(2)}, u32[]{:S(2)}) collective-permute-start(bf16[256,1024]{1,0:T(8,128)(2,1)S(1)} %collective-permute-done.14.refs_4_), channel_id=1, source_target_pairs={{0,8},{4,12},{8,0},{12,4},{16,24},{20,28},{24,16},{28,20},{1,9},{5... | collective-permute-start | bytes 1572872 | tf_op jit(solution)/shard_map/ppermute | solution.py:29
  83.8 12.8 %collective-permute-start.16 = (bf16[256,1024]{1,0:T(8,128)(2,1)S(1)}, bf16[256,1024]{1,0:T(8,128)(2,1)S(1)}, u32[]{:S(2)}, u32[]{:S(2)}) collective-permute-start(bf16[256,1024]{1,0:T(8,128)(2,1)S(1)} %collective-permute-done.14.refs_4_), channel_id=1, source_target_pairs={{0,16},{4,20},{8,24},{12,28},{16,0},{20,4},{24,8},{28,12},{1,17},{... | collective-permute-start | bytes 1572872 | tf_op jit(solution)/shard_map/ppermute | solution.py:29
  83.9 5.4 %collective-permute-start.28 = (bf16[2,1024]{1,0:T(2,128)(2,1)S(1)}, bf16[2,1024]{1,0:T(2,128)(2,1)S(1)}, u32[]{:S(2)}, u32[]{:S(2)}) collective-permute-start(bf16[2,1024]{1,0:T(2,128)(2,1)S(1)} %copy-done.13), channel_id=1, source_target_pairs={{0,3},{1,2},{2,1},{3,0},{4,7},{5,6},{6,5},{7,4},{8,11},{9,10},{10,... | collective-permute-start | bytes 12296 | tf_op jit(solution)/shard_map/ppermute | solution.py:29
  89.3 13.9 %collective-permute-start.9 = (bf16[3,128,1024]{2,1,0:T(8,128)(2,1)}, bf16[3,128,1024]{2,1,0:T(8,128)(2,1)}, u32[]{:S(2)}, u32[]{:S(2)}) collective-permute-start(bf16[3,128,1024]{2,1,0:T(8,128)(2,1)} %pad_maximum_fusion.refs_9_), channel_id=1, source_target_pairs={{0,4},{4,0},{8,12},{12,8},{16,20},{20,16},{24,28},{28,24},{1,5},{5... | collective-permute-start | bytes 2359304 | tf_op jit(solution)/shard_map/ppermute | solution.py:29
  89.3 14.0 %collective-permute-start.10 = (bf16[3,128,1024]{2,1,0:T(8,128)(2,1)}, bf16[3,128,1024]{2,1,0:T(8,128)(2,1)}, u32[]{:S(2)}, u32[]{:S(2)}) collective-permute-start(bf16[3,128,1024]{2,1,0:T(8,128)(2,1)} %collective-permute-done.5.refs_10_), channel_id=1, source_target_pairs={{0,4},{4,0},{8,12},{12,8},{16,20},{20,16},{24,28},{28,24},{1,5},{5... | collective-permute-start | bytes 2359304 | tf_op jit(solution)/shard_map/ppermute | solution.py:29
  90.6 15.7 %collective-permute-start.11 = (bf16[3,128,1024]{2,1,0:T(8,128)(2,1)}, bf16[3,128,1024]{2,1,0:T(8,128)(2,1)}, u32[]{:S(2)}, u32[]{:S(2)}) collective-permute-start(bf16[3,128,1024]{2,1,0:T(8,128)(2,1)} %collective-permute-done.6.refs_11_), channel_id=1, source_target_pairs={{0,4},{4,0},{8,12},{12,8},{16,20},{20,16},{24,28},{28,24},{1,5},{5... | collective-permute-start | bytes 2359304 | tf_op jit(solution)/shard_map/ppermute | solution.py:29
  95.4 10.9 %collective-permute-start.12 = (bf16[3,64,1024]{2,1,0:T(8,128)(2,1)S(1)}, bf16[3,64,1024]{2,1,0:T(8,128)(2,1)S(1)}, u32[]{:S(2)}, u32[]{:S(2)}) collective-permute-start(bf16[3,64,1024]{2,1,0:T(8,128)(2,1)S(1)} %collective-permute-done.7.refs_12_), channel_id=1, source_target_pairs={{0,4},{4,0},{8,12},{12,8},{16,20},{20,16},{24,28},{28,24},{1,5},{5... | collective-permute-start | bytes 1179656 | tf_op jit(solution)/shard_map/ppermute | solution.py:29
  96.6 10.6 %collective-permute-start.13 = (bf16[3,64,1024]{2,1,0:T(8,128)(2,1)}, bf16[3,64,1024]{2,1,0:T(8,128)(2,1)S(1)}, u32[]{:S(2)}, u32[]{:S(2)}) collective-permute-start(bf16[3,64,1024]{2,1,0:T(8,128)(2,1)} %copy-done.18), channel_id=1, source_target_pairs={{0,4},{4,0},{8,12},{12,8},{16,20},{20,16},{24,28},{28,24},{1,5},{5... | collective-permute-start | bytes 1179656 | tf_op jit(solution)/shard_map/ppermute | solution.py:29
  103.2 19.9 %collective-permute-start.27 = (bf16[2,1024]{1,0:T(2,128)(2,1)S(1)}, bf16[2,1024]{1,0:T(2,128)(2,1)S(1)}, u32[]{:S(2)}, u32[]{:S(2)}) collective-permute-start(bf16[2,1024]{1,0:T(2,128)(2,1)S(1)} %copy-done.13), channel_id=1, source_target_pairs={{0,2},{1,3},{2,0},{3,1},{4,6},{5,7},{6,4},{7,5},{8,10},{9,11},{10,... | collective-permute-start | bytes 12296 | tf_op jit(solution)/shard_map/ppermute | solution.py:29
  103.3 19.9 %collective-permute-start.26 = (bf16[2,1024]{1,0:T(2,128)(2,1)S(1)}, bf16[2,1024]{1,0:T(2,128)(2,1)S(1)}, u32[]{:S(2)}, u32[]{:S(2)}) collective-permute-start(bf16[2,1024]{1,0:T(2,128)(2,1)S(1)} %copy-done.13), channel_id=1, source_target_pairs={{0,1},{1,0},{2,3},{3,2},{4,5},{5,4},{6,7},{7,6},{8,9},{9,8},{10,11... | collective-permute-start | bytes 12296 | tf_op jit(solution)/shard_map/ppermute | solution.py:29
  106.3 17.4 %collective-permute-start.19 = (bf16[256,1024]{1,0:T(8,128)(2,1)S(1)}, bf16[256,1024]{1,0:T(8,128)(2,1)S(1)}, u32[]{:S(2)}, u32[]{:S(2)}) collective-permute-start(bf16[256,1024]{1,0:T(8,128)(2,1)S(1)} %collective-permute-done.14.refs_4_), channel_id=1, source_target_pairs={{0,4},{4,0},{8,12},{12,8},{16,20},{20,16},{24,28},{28,24},{1,5},{5... | collective-permute-start | bytes 1572872 | tf_op jit(solution)/shard_map/ppermute | solution.py:29
  106.3 17.6 %collective-permute-start.17 = (bf16[128,1024]{1,0:T(8,128)(2,1)S(1)}, bf16[128,1024]{1,0:T(8,128)(2,1)S(1)}, u32[]{:S(2)}, u32[]{:S(2)}) collective-permute-start(bf16[128,1024]{1,0:T(8,128)(2,1)S(1)} %slice.94), channel_id=1, source_target_pairs={{0,8},{4,12},{8,0},{12,4},{16,24},{20,28},{24,16},{28,20},{1,9},{5... | collective-permute-start | bytes 786440 | tf_op jit(solution)/shard_map/ppermute | solution.py:29
  107.2 16.8 %collective-permute-start.18 = (bf16[128,1024]{1,0:T(8,128)(2,1)S(1)}, bf16[128,1024]{1,0:T(8,128)(2,1)S(1)}, u32[]{:S(2)}, u32[]{:S(2)}) collective-permute-start(bf16[128,1024]{1,0:T(8,128)(2,1)S(1)} %slice.95), channel_id=1, source_target_pairs={{0,16},{4,20},{8,24},{12,28},{16,0},{20,4},{24,8},{28,12},{1,17},{... | collective-permute-start | bytes 786440 | tf_op jit(solution)/shard_map/ppermute | solution.py:29
  123.2 8.4 %collective-permute-start.20 = (bf16[256,1024]{1,0:T(8,128)(2,1)S(1)}, bf16[256,1024]{1,0:T(8,128)(2,1)S(1)}, u32[]{:S(2)}, u32[]{:S(2)}) collective-permute-start(bf16[256,1024]{1,0:T(8,128)(2,1)S(1)} %collective-permute-done.15.refs_5_), channel_id=1, source_target_pairs={{0,4},{4,0},{8,12},{12,8},{16,20},{20,16},{24,28},{28,24},{1,5},{5... | collective-permute-start | bytes 1572872 | tf_op jit(solution)/shard_map/ppermute | solution.py:29
  123.3 8.3 %collective-permute-start.21 = (bf16[256,1024]{1,0:T(8,128)(2,1)S(1)}, bf16[256,1024]{1,0:T(8,128)(2,1)S(1)}, u32[]{:S(2)}, u32[]{:S(2)}) collective-permute-start(bf16[256,1024]{1,0:T(8,128)(2,1)S(1)} %collective-permute-done.16.refs_6_), channel_id=1, source_target_pairs={{0,4},{4,0},{8,12},{12,8},{16,20},{20,16},{24,28},{28,24},{1,5},{5... | collective-permute-start | bytes 1572872 | tf_op jit(solution)/shard_map/ppermute | solution.py:29
  123.8 14.1 %collective-permute-start.24 = (bf16[256,1024]{1,0:T(8,128)(2,1)}, bf16[256,1024]{1,0:T(8,128)(2,1)S(1)}, u32[]{:S(2)}, u32[]{:S(2)}) collective-permute-start(bf16[256,1024]{1,0:T(8,128)(2,1)} %attend_rest.1.refs_1_.normed_ref), channel_id=1, source_target_pairs={{0,1},{1,0},{2,3},{3,2},{4,5},{5,4},{6,7},{7,6},{8,9},{9,8},{10,11... | collective-permute-start | bytes 1572872 | tf_op jit(solution)/shard_map/ppermute | solution.py:29
  123.9 7.6 %collective-permute-start.22 = (bf16[128,1024]{1,0:T(8,128)(2,1)S(1)}, bf16[128,1024]{1,0:T(8,128)(2,1)S(1)}, u32[]{:S(2)}, u32[]{:S(2)}) collective-permute-start(bf16[128,1024]{1,0:T(8,128)(2,1)S(1)} %collective-permute-done.17.refs_7_), channel_id=1, source_target_pairs={{0,4},{4,0},{8,12},{12,8},{16,20},{20,16},{24,28},{28,24},{1,5},{5... | collective-permute-start | bytes 786440 | tf_op jit(solution)/shard_map/ppermute | solution.py:29
  124.0 7.6 %collective-permute-start.23 = (bf16[128,1024]{1,0:T(8,128)(2,1)S(1)}, bf16[128,1024]{1,0:T(8,128)(2,1)S(1)}, u32[]{:S(2)}, u32[]{:S(2)}) collective-permute-start(bf16[128,1024]{1,0:T(8,128)(2,1)S(1)} %collective-permute-done.18.refs_8_), channel_id=1, source_target_pairs={{0,4},{4,0},{8,12},{12,8},{16,20},{20,16},{24,28},{28,24},{1,5},{5... | collective-permute-start | bytes 786440 | tf_op jit(solution)/shard_map/ppermute | solution.py:29
  145.7 22.8 %collective-permute-start.25 = (bf16[256,1024]{1,0:T(8,128)(2,1)}, bf16[256,1024]{1,0:T(8,128)(2,1)S(1)}, u32[]{:S(2)}, u32[]{:S(2)}) collective-permute-start(bf16[256,1024]{1,0:T(8,128)(2,1)} %feed_partner.1), channel_id=1, source_target_pairs={{0,1},{1,0},{2,3},{3,2},{4,5},{5,4},{6,7},{7,6},{8,9},{9,8},{10,11... | collective-permute-start | bytes 1572872 | tf_op jit(solution)/shard_map/ppermute | solution.py:29
  146.1 13.8 %collective-permute-start.31 = (f32[3,2,1024]{2,1,0:T(2,128)S(1)}, f32[3,2,1024]{2,1,0:T(2,128)S(1)}, u32[]{:S(2)}, u32[]{:S(2)}) collective-permute-start(f32[3,2,1024]{2,1,0:T(2,128)S(1)} %get-tuple-element.10), channel_id=1, source_target_pairs={{0,3},{1,2},{2,1},{3,0},{4,7},{5,6},{6,5},{7,4},{8,11},{9,10},{10,... | collective-permute-start | bytes 73736 | tf_op jit(solution)/shard_map/ppermute | solution.py:29
  147.5 12.3 %collective-permute-start.30 = (f32[3,2,1024]{2,1,0:T(2,128)S(1)}, f32[3,2,1024]{2,1,0:T(2,128)S(1)}, u32[]{:S(2)}, u32[]{:S(2)}) collective-permute-start(f32[3,2,1024]{2,1,0:T(2,128)S(1)} %get-tuple-element.9), channel_id=1, source_target_pairs={{0,2},{1,3},{2,0},{3,1},{4,6},{5,7},{6,4},{7,5},{8,10},{9,11},{10,... | collective-permute-start | bytes 73736 | tf_op jit(solution)/shard_map/ppermute | solution.py:29
  149.4 11.3 %collective-permute-start.29 = (f32[3,2,1024]{2,1,0:T(2,128)S(1)}, f32[3,2,1024]{2,1,0:T(2,128)S(1)}, u32[]{:S(2)}, u32[]{:S(2)}) collective-permute-start(f32[3,2,1024]{2,1,0:T(2,128)S(1)} %get-tuple-element.8), channel_id=1, source_target_pairs={{0,1},{1,0},{2,3},{3,2},{4,5},{5,4},{6,7},{7,6},{8,9},{9,8},{10,11... | collective-permute-start | bytes 73736 | tf_op jit(solution)/shard_map/ppermute | solution.py:29
  (24 other events, 383.6 us)

commit v2 on v1

--- a/solution.py
+++ b/solution.py
@@ -70,15 +70,15 @@
     bias_ref[...] = jnp.where((key >= low) & (key < high), 0.0, NEG_FILL)
 
 
-def attend(rows_ref, bias_ref, weight, out_weight):
+def attend(rows_ref, bias_ref, weight_ref, out_weight):
     count = bias_ref.shape[0]
-    width = weight.shape[1] // 3
+    width = weight_ref.shape[2]
     own = rows_ref[count : 2 * count]
     rows = rows_ref[...]
     scale = 1.0 / math.sqrt(HD)
-    query = (jnp.dot(own, weight[:, :width], preferred_element_type=F32) * scale).astype(BF16)
-    keys = jnp.dot(rows, weight[:, width : 2 * width], preferred_element_type=F32).astype(BF16)
-    values = jnp.dot(rows, weight[:, 2 * width :], preferred_element_type=F32).astype(BF16)
+    query = (jnp.dot(own, weight_ref[0], preferred_element_type=F32) * scale).astype(BF16)
+    keys = jnp.dot(rows, weight_ref[1], preferred_element_type=F32).astype(BF16)
+    values = jnp.dot(rows, weight_ref[2], preferred_element_type=F32).astype(BF16)
     lane = lax.broadcasted_iota(jnp.int32, (count, 2 * HD), 1)
     bias = bias_ref[...]
     pairs = []
@@ -104,43 +104,38 @@
     place_ref, starts_ref, ends_ref, before_ref, own_ref, behind_ref, weight_ref, out_ref, sum_ref, rows_ref, bias_ref
 ):
     prepare(place_ref, starts_ref, ends_ref, before_ref, own_ref, behind_ref, rows_ref, bias_ref)
-    sum_ref[...] = attend(rows_ref, bias_ref, weight_ref[...], out_ref[...])
-
-
-def attend_rest_kernel(layout, quarters, *refs):
+    sum_ref[...] = attend(rows_ref, bias_ref, weight_ref, out_ref[...])
+
+
+def attend_next_kernel(layout, last, *refs):
     count = len(layout)
-    place_ref, starts_ref, ends_ref, before_ref, own_ref, behind_ref, sum_ref, gain_ref, bias1_ref = refs[:9]
+    place_ref, starts_ref, ends_ref, before_ref, own_ref, behind_ref, sum_ref, gain_ref, shift_ref = refs[:9]
     pieces = refs[9 : 9 + count]
-    normed_ref, rows_ref, bias_ref, weight_ref, out_ref, total_ref, sems = refs[9 + count :]
+    result_ref, rows_ref, bias_ref, weight_ref, out_ref, sems = refs[9 + count :]
     tok = place_ref[1]
-    wide = weight_ref.shape[2]
     block = 128
     copies = []
     for (flip, part), piece in zip(layout, pieces):
-        eighth = tok ^ flip
         size = piece.shape[1]
         shift = 0 if part is None else part * size
-        at = pl.multiple_of(eighth * block, block)
-        moves = [(piece.at[:, :, 0:wide], weight_ref.at[:, pl.ds(at + shift, size), :])]
+        at = pl.multiple_of((tok ^ flip) * block, block)
+        moves = [(piece.at[0:3], weight_ref.at[:, pl.ds(at + shift, size), :])]
         for side in range(2):
-            columns = pl.ds(wide + side * block, block)
-            moves.append((piece.at[:, :, columns], out_ref.at[:, pl.ds(side * block + shift, size), pl.ds(at, block)]))
+            columns = slice(side * block, (side + 1) * block)
+            moves.append((piece.at[3, :, columns], out_ref.at[pl.ds(side * block + shift, size), pl.ds(at, block)]))
         for source, target in moves:
             copies.append(pltpu.make_async_copy(source, target, sems.at[len(copies)]))
     for copy in copies:
         copy.start()
     prepare(place_ref, starts_ref, ends_ref, before_ref, own_ref, behind_ref, rows_ref, bias_ref)
-    total_ref[...] = sum_ref[...]
     for copy in copies:
         copy.wait()
-
-    def step(index, carry):
-        total_ref[...] += attend(rows_ref, bias_ref, weight_ref[index], out_ref[index])
-        return carry
-
-    lax.fori_loop(0, quarters, step, 0)
-    mixed = own_ref[...].astype(F32) + total_ref[...]
-    normed_ref[...] = normalized(mixed, gain_ref[...], bias1_ref[...]).astype(BF16)
+    total = sum_ref[...] + attend(rows_ref, bias_ref, weight_ref, out_ref[...])
+    if last:
+        mixed = own_ref[...].astype(F32) + total
+        result_ref[...] = normalized(mixed, gain_ref[...], shift_ref[...]).astype(BF16)
+    else:
+        result_ref[...] = total
 
 
 def attend_cost(rows, width, heads_width):
@@ -148,8 +143,8 @@
     return pl.CostEstimate(flops=flops, bytes_accessed=4 * width * heads_width * 2, transcendentals=0)
 
 
-def attend_own(place, starts, ends, before, own, behind, weight, out_weight):
-    rows, width = own.shape
+def attend_own(shards, weight, out_weight):
+    rows, width = shards[4].shape
     return pl.pallas_call(
         attend_own_kernel,
         out_shape=jax.ShapeDtypeStruct((rows, width), F32),
@@ -159,84 +154,101 @@
         compiler_params=pltpu.CompilerParams(vmem_limit_bytes=VMEM_LIMIT),
         cost_estimate=attend_cost(rows, width, out_weight.shape[0]),
         name="attend_own",
-    )(place, starts, ends, before, own, behind, weight, out_weight)
-
-
-def attend_rest(place, starts, ends, before, own, behind, summed, gain, bias, pieces, heads_width):
-    rows, width = own.shape
+    )(*shards, weight, out_weight)
+
+
+def attend_next(shards, summed, gain, bias, pieces, heads_width, last, name):
+    rows, width = shards[4].shape
     layout = tuple((flip, part) for flip, part, _ in pieces)
-    quarters = pieces[0][2].shape[0]
     return pl.pallas_call(
-        functools.partial(attend_rest_kernel, layout, quarters),
-        out_shape=jax.ShapeDtypeStruct((rows, width), BF16),
+        functools.partial(attend_next_kernel, layout, last),
+        out_shape=jax.ShapeDtypeStruct((rows, width), BF16 if last else F32),
         in_specs=[SMEM] + [VMEM] * 8 + [ANY] * len(pieces),
         out_specs=VMEM,
         scratch_shapes=[
             pltpu.VMEM((3 * rows, width), BF16),
             pltpu.VMEM((rows, 3 * rows), F32),
-            pltpu.VMEM((quarters, width, 3 * heads_width), BF16),
-            pltpu.VMEM((quarters, heads_width, width), BF16),
-            pltpu.VMEM((rows, width), F32),
+            pltpu.VMEM((3, width, heads_width), BF16),
+            pltpu.VMEM((heads_width, width), BF16),
             pltpu.SemaphoreType.DMA((3 * len(pieces),)),
         ],
         compiler_params=pltpu.CompilerParams(vmem_limit_bytes=VMEM_LIMIT),
-        cost_estimate=attend_cost(rows, width, quarters * heads_width),
-        name="attend_rest",
-    )(place, starts, ends, before, own, behind, summed, gain, bias, *[value for _, _, value in pieces])
+        cost_estimate=attend_cost(rows, width, heads_width),
+        name=name,
+    )(*shards, summed, gain, bias, *[value for _, _, value in pieces])
 
 
 def gelu(values):
     return 0.5 * values * (1.0 + lax.erf(values * math.sqrt(0.5)))
 
 
-def feed_kernel(layout, *refs):
+def feed_into(total_ref, rows, up_ref, down_ref):
+    chunk = 512
+    for at in range(0, up_ref.shape[1], chunk):
+        units = gelu(jnp.dot(rows, up_ref[:, at : at + chunk], preferred_element_type=F32)).astype(BF16)
+        total_ref[...] += jnp.dot(units, down_ref[at : at + chunk, :], preferred_element_type=F32)
+
+
+def feed_near_kernel(rows_ref, up_ref, down_ref, sum_ref):
+    sum_ref[...] = jnp.zeros_like(sum_ref)
+    feed_into(sum_ref, rows_ref[...], up_ref, down_ref)
+
+
+def feed_cost(count, width, units):
+    return pl.CostEstimate(
+        flops=4 * count * width * units, bytes_accessed=4 * width * units, transcendentals=count * units
+    )
+
+
+def feed_near(rows, up_weight, down_weight, name):
+    count, width = rows.shape
+    return pl.pallas_call(
+        feed_near_kernel,
+        out_shape=jax.ShapeDtypeStruct((count, width), F32),
+        in_specs=[VMEM] * 3,
+        out_specs=VMEM,
+        compiler_params=pltpu.CompilerParams(vmem_limit_bytes=VMEM_LIMIT),
+        cost_estimate=feed_cost(count, width, up_weight.shape[1]),
+        name=name,
+    )(rows, up_weight, down_weight)
+
+
+def feed_far_kernel(layout, *refs):
     count = len(layout)
-    place_ref, rows_ref, up_ref, down_ref = refs[:4]
-    pieces = refs[4 : 4 + count]
-    sum_ref, far_up_ref, far_down_ref, total_ref, sems = refs[4 + count :]
+    place_ref, rows_ref, near_ref = refs[:3]
+    pieces = refs[3 : 3 + count]
+    sum_ref, up_ref, down_ref, total_ref, sems = refs[3 + count :]
     tok = place_ref[1]
     block = 128
     copies = []
     for (flip, part), piece in zip(layout, pieces):
         at = pl.multiple_of((tok ^ flip) * block, block)
         if part in (None, 0):
-            copies.append(
-                pltpu.make_async_copy(piece.at[0:block], far_up_ref.at[pl.ds(at, block)], sems.at[len(copies)])
-            )
+            copies.append(pltpu.make_async_copy(piece.at[0:block], up_ref.at[pl.ds(at, block)], sems.at[len(copies)]))
         if part in (None, 1):
             shift = block if part is None else 0
             copies.append(
                 pltpu.make_async_copy(
-                    piece.at[shift : shift + block], far_down_ref.at[pl.ds(at, block)], sems.at[len(copies)]
+                    piece.at[shift : shift + block], down_ref.at[pl.ds(at, block)], sems.at[len(copies)]
                 )
             )
     for copy in copies:
         copy.start()
-    rows = rows_ref[...]
-    chunk = 512
-    total_ref[...] = jnp.zeros_like(total_ref)
-
-    def through(up, down):
-        for at in range(0, up.shape[1], chunk):
-            units = gelu(jnp.dot(rows, up[:, at : at + chunk], preferred_element_type=F32)).astype(BF16)
-            total_ref[...] += jnp.dot(units, down[at : at + chunk, :], preferred_element_type=F32)
-
-    through(up_ref, down_ref)
+    total_ref[...] = near_ref[...]
     for copy in copies:
         copy.wait()
-    through(far_up_ref, far_down_ref)
+    feed_into(total_ref, rows_ref[...], up_ref, down_ref)
     sum_ref[...] = total_ref[...].astype(sum_ref.dtype)
 
 
-def feed(place, rows, up_weight, down_weight, pieces, dtype, name):
+def feed_far(place, rows, near, pieces, units, dtype, name):
     count, width = rows.shape
-    units = up_weight.shape[1]
     layout = tuple((flip, part) for flip, part, _ in pieces)
     copies = sum(2 if part is None else 1 for _, part in layout)
     return pl.pallas_call(
-        functools.partial(feed_kernel, layout),
+        functools.partial(feed_far_kernel, layout),
         out_shape=jax.ShapeDtypeStruct((count, width), dtype),
-        in_specs=[SMEM] + [VMEM] * 3 + [ANY] * len(pieces),
+        in_specs=[SMEM] + [VMEM] * 2 + [ANY] * len(pieces),
         out_specs=VMEM,
         scratch_shapes=[
             pltpu.VMEM((width, units), BF16),
@@ -245,11 +257,9 @@
             pltpu.SemaphoreType.DMA((copies,)),
         ],
         compiler_params=pltpu.CompilerParams(vmem_limit_bytes=VMEM_LIMIT),
-        cost_estimate=pl.CostEstimate(
-            flops=8 * count * width * units, bytes_accessed=8 * width * units, transcendentals=2 * count * units
-        ),
+        cost_estimate=feed_cost(count, width, units),
         name=name,
-    )(place, rows, up_weight, down_weight, *[value for _, _, value in pieces])
+    )(place, rows, near, *[value for _, _, value in pieces])
 
 
 def finish_kernel(normed_ref, near_ref, far_ref, gain_ref, bias_ref, out_ref):
@@ -331,16 +341,21 @@
     )(slots, filled, queries, kv_cache)
 
 
-def decode_rows(dec_query, kv_cache, piece_req, piece_used):
-    own = dec_query.shape[0]
-    kv = lax.axis_index("kv")
-    count = lax.axis_size("kv")
-    queries = jnp.concatenate([dec_query] + [swapped(dec_query, "kv", flip) for flip in range(1, count)])
+def gathered_queries(dec_query):
+    flips = range(1, lax.axis_size("kv"))
+    return [dec_query] + [swapped(dec_query, "kv", flip) for flip in flips]
+
+
+def decode_partial(queries, kv_cache, piece_req, piece_used):
+    own = queries[0].shape[0]
     owners = piece_req[0]
-    slots = ((owners // own) ^ kv) * own + owners % own
-    partial = decode(slots, piece_used[0], queries.astype(F32), kv_cache)
+    slots = ((owners // own) ^ lax.axis_index("kv")) * own + owners % own
+    return decode(slots, piece_used[0], jnp.concatenate(queries).astype(F32), kv_cache)
+
+
+def decode_merged(partial, own):
     parts = [partial[:, :own]]
-    for flip in range(1, count):
+    for flip in range(1, lax.axis_size("kv")):
         parts.append(swapped(partial[:, flip * own : (flip + 1) * own], "kv", flip))
     high = functools.reduce(jnp.maximum, [part[0] for part in parts])
     factors = [jnp.exp(part[0] - high) for part in parts]
@@ -372,53 +387,60 @@
     heads_width = out_weight.shape[0]
     block = width // toks
 
+    queries = gathered_queries(dec_query)
+    flat = toks * kvs
+    before = lax.ppermute(hidden_in, ("tok", "kv"), [(i, i + 1) for i in range(flat - 1)])
+    behind = lax.ppermute(hidden_in, ("tok", "kv"), [(i + 1, i) for i in range(flat - 1)])
+
     eighth = lambda value, axis: lax.dynamic_slice_in_dim(value, tok * block, block, axis)
     out_part = eighth(out_weight, 1)
+    qkv_part = lax.optimization_barrier(eighth(qkv_weight, 0))
     bundle = jnp.concatenate(
-        [eighth(qkv_weight, 0).reshape(block, 3 * heads_width), out_part[:block], out_part[block:]], axis=1
-    )
+        [
+            jnp.transpose(qkv_part, (1, 0, 2)),
+            jnp.concatenate([out_part[:block], out_part[block:]], axis=1)[None],
+        ],
+        axis=0,
+    )
+    bundle = after(bundle, *queries)
     foreign = [swapped(bundle, "kv", flip) for flip in range(1, kvs)]
-
-    hidden_late = after(hidden_in, *foreign)
-    flat = toks * kvs
-    before = lax.ppermute(hidden_late, ("tok", "kv"), [(i, i + 1) for i in range(flat - 1)])
-    behind = lax.ppermute(hidden_late, ("tok", "kv"), [(i + 1, i) for i in range(flat - 1)])
-
-    pieces = spread_in_plane(jnp.stack(foreign))
-
     feed_part = jnp.concatenate([eighth(up_weight, 0), eighth(down_weight, 0)], axis=0)
-    feed_part = after(feed_part, before, behind)
-    feed_pieces = spread_in_plane(swapped(feed_part, "kv", 2))
+    feed_foreign = swapped(feed_part, "kv", 2)
+
+    partial = decode_partial(queries, kv_cache, piece_req, piece_used)
+    pieces = [spread_in_plane(foreign[0])]
+    turn = partial
+    for value in foreign[1:]:
+        pieces.append(spread_in_plane(after(value, turn)))
+        turn = pieces[-1][1][2]
+    feed_pieces = spread_in_plane(after(feed_foreign, turn))
 
     place = jnp.stack([(tok * kvs + kv) * rows, tok]).astype(jnp.int32)
     order = jnp.arange(stretch_len.shape[0])
     ends = jnp.sum(jnp.where(order[:, None] <= order[None, :], stretch_len[:, None], 0), axis=0, dtype=jnp.int32)
     starts = (ends - stretch_len)[None, :]
-    ends = ends[None, :]
-
-    own_weight = qkv_weight.reshape(width, 3 * heads_width)
-    summed = attend_own(place, starts, ends, before, hidden_in, behind, own_weight, out_weight)
-    normed = attend_rest(
-        place,
-        starts,
-        ends,
-        before,
-        hidden_in,
-        behind,
-        summed,
-        ln1_gain[None, :],
-        ln1_bias[None, :],
-        pieces,
-        heads_width,
-    )
-
+    shards = (place, starts, ends[None, :], before, hidden_in, behind)
+
+    total = attend_own(shards, jnp.transpose(qkv_weight, (1, 0, 2)), out_weight)
+    for index, quarter in enumerate(pieces):
+        last = index == len(pieces) - 1
+        partial = after(partial, total) if last else partial
+        total = attend_next(
+            shards, total, ln1_gain[None, :], ln1_bias[None, :], quarter, heads_width, last, "attend_%d" % (index + 1)
+        )
+    normed = total
+
+    units = up_weight.shape[1]
     partner = swapped(normed, "kv", 1)
-    near = feed(place, normed, up_weight, down_weight, feed_pieces, F32, "feed_own")
-    away = feed(place, partner, up_weight, down_weight, feed_pieces, BF16, "feed_partner")
-    far = swapped(away, "kv", 1)
-    prefill_out = finish(normed, near, far, ln2_gain[None, :], ln2_bias[None, :])
-
-    return prefill_out, decode_rows(dec_query, kv_cache, piece_req, piece_used)
+    near = feed_near(normed, up_weight, down_weight, "feed_near_own")
+    partner = after(partner, near)
+    near_away = feed_near(partner, up_weight, down_weight, "feed_near_partner")
+    away = feed_far(place, partner, near_away, feed_pieces, units, BF16, "feed_far_partner")
+    arrived = swapped(away, "kv", 1)
+    mine = feed_far(place, after(normed, away), near, feed_pieces, units, F32, "feed_far_own")
+    prefill_out = finish(normed, mine, arrived, ln2_gain[None, :], ln2_bias[None, :])
+
+    return prefill_out, decode_merged(partial, dec_query.shape[0])
 
 
 def extended(value, sides, width):

time: 173 us -> 194 us (1.12)
  Pallas kernels: 43.5 us -> 59.5 us
  waiting for transfers between devices: 72.6 us -> 82.8 us
  starting transfers between devices: 40.8 us -> 38.2 us
    ppermute x30 -> x48, waiting for transfers between devices: 57.9 us -> 82.8 us  [swapped(): return lax.ppermute(value, axis, [(i, i ^ flip) for i in range(count)])]
    pallas_call x3 -> x7, Pallas kernels: 28.8 us -> 44.8 us  [the longest x3 22.8 us: attend_next(): pl.pallas_call(functools.partial(attend_next_kernel, layout, last), out_s...]
    ppermute x2, waiting for transfers between devices: 14.7 us -> 0.01 us  [the longest x1 0.01 us: routed_body(): lax.ppermute(hidden_in, ('tok', 'kv'), [(i, i + 1) for i in range(flat -...]
    ppermute x2, starting transfers between devices: 7.97 us -> 2.6 us  [the longest x1 1.31 us: routed_body(): lax.ppermute(hidden_in, ('tok', 'kv'), [(i, i + 1) for i in range(flat -...]
    ppermute x30 -> x48, starting transfers between devices: 32.9 us -> 35.6 us  [swapped(): return lax.ppermute(value, axis, [(i, i ^ flip) for i in range(count)])]
    unnamed x49 -> x92, local copies, waits for them, and re-layouts: 4.21 us -> 5.44 us
  transfers between devices with their start and end apart: 32 -> 50, of which waited for: 13 -> 16; matrix products, arithmetic and copies ran while one was open for 5% -> 3% of each run, Pallas kernels for 20% -> 26%
where the time goes in v2:
time: 194 us; the launch traced here: 193 us
  waiting for transfers between devices  82.8 us (43%)
  Pallas kernels  59.5 us (31%)
  starting transfers between devices  38.2 us (20%)
  local copies, waits for them, and re-layouts  8.37 us (4%)
  other arithmetic  3.28 us (2%)
    ppermute x48, waiting for transfers between devices, swapped(): return lax.ppermute(value, axis, [(i, i ^ flip) for i in range(count)])  82.8 us
    ppermute x48, starting transfers between devices, swapped(): return lax.ppermute(value, axis, [(i, i ^ flip) for i in range(count)])  35.6 us
    pallas_call x3, Pallas kernels, attend_next(): pl.pallas_call(functools.partial(attend_next_kernel, layout, last), out_s...  22.8 us
    pallas_call x2, Pallas kernels, feed_far(): pl.pallas_call(functools.partial(feed_far_kernel, layout), out_shape=jax....  12.1 us
    pallas_call x2, Pallas kernels, feed_near(): pl.pallas_call(feed_near_kernel, out_shape=jax.ShapeDtypeStruct((count, w...  9.93 us
    pallas_call x1, Pallas kernels, attend_own(): pl.pallas_call(attend_own_kernel, out_shape=jax.ShapeDtypeStruct((rows, w...  5.96 us
    pallas_call x1, Pallas kernels, decode(): pl.pallas_call(decode_kernel, grid=(pieces,), out_shape=jax.ShapeDtypeStr...  5.9 us
    unnamed x92, local copies, waits for them, and re-layouts  5.44 us
  transfers between devices with their start and end apart: 50, of which 16 were waited for; matrix products, arithmetic and copies ran while one was open for 3% of the time, Pallas kernels for 26%

profile of v2, /device:TPU:0, one launch (start us, length us, event | category | flops | bytes accessed | tf_op | source)
XLA Modules:
  0.0 193.4 jit_solution(9634730439616968903)
XLA Ops:
  0.6 3.1 %collective-permute-start.2 = (bf16[2,1024]{1,0:T(2,128)(2,1)}, bf16[2,1024]{1,0:T(2,128)(2,1)S(1)}, u32[]{:S(2)}, u32[]{:S(2)}) collective-permute-start(bf16[2,1024]{1,0:T(2,128)(2,1)} %param.24), channel_id=1, source_target_pairs={{0,1},{1,0},{2,3},{3,2},{4,5},{5,4},{6,7},{7,6},{8,9},{9,8},{10,11... | collective-permute-start | bytes 12296 | tf_op jit(solution)/shard_map/ppermute | solution.py:29
  3.7 2.6 %collective-permute-start.3 = (bf16[2,1024]{1,0:T(2,128)(2,1)}, bf16[2,1024]{1,0:T(2,128)(2,1)S(1)}, u32[]{:S(2)}, u32[]{:S(2)}) collective-permute-start(bf16[2,1024]{1,0:T(2,128)(2,1)} %param.24), channel_id=1, source_target_pairs={{0,2},{1,3},{2,0},{3,1},{4,6},{5,7},{6,4},{7,5},{8,10},{9,11},{10,... | collective-permute-start | bytes 12296 | tf_op jit(solution)/shard_map/ppermute | solution.py:29
  8.5 3.5 %collective-permute-done.4 = bf16[2,1024]{1,0:T(2,128)(2,1)S(1)} collective-permute-done((bf16[2,1024]{1,0:T(2,128)(2,1)}, bf16[2,1024]{1,0:T(2,128)(2,1)S(1)}, u32[]{:S(2)}, u32[]{:S(2)}) %collective-permute-start.4) | collective-permute-done | bytes 4128 | tf_op jit(solution)/shard_map/ppermute | solution.py:29
  12.6 3.8 %collective-permute-start.25 = (bf16[4,128,256]{2,1,0:T(8,128)(2,1)S(1)}, bf16[4,128,256]{2,1,0:T(8,128)(2,1)S(1)}, u32[]{:S(2)}, u32[]{:S(2)}) collective-permute-start(bf16[4,128,256]{2,1,0:T(8,128)(2,1)S(1)} %pad_maximum_fusion.1), channel_id=1, source_target_pairs={{0,3},{1,2},{2,1},{3,0},{4,7},{5,6},{6,5},{7,4},{8,11},{9,10},{10,... | collective-permute-start | bytes 786440 | tf_op jit(solution)/shard_map/ppermute | solution.py:29
  20.1 4.9 %collective-permute-done.5.refs_9_ = bf16[4,128,256]{2,1,0:T(8,128)(2,1)S(1)} collective-permute-done((bf16[4,128,256]{2,1,0:T(8,128)(2,1)S(1)}, bf16[4,128,256]{2,1,0:T(8,128)(2,1)S(1)}, u32[]{:S(2)}, u32[]{:S(2)}) %collective-permute-start.5) | collective-permute-done | bytes 262176 | tf_op jit(solution)/shard_map/ppermute | solution.py:29
  25.0 19.1 %collective-permute-done.15.refs_9_ = bf16[4,128,256]{2,1,0:T(8,128)(2,1)S(1)} collective-permute-done((bf16[4,128,256]{2,1,0:T(8,128)(2,1)S(1)}, bf16[4,128,256]{2,1,0:T(8,128)(2,1)S(1)}, u32[]{:S(2)}, u32[]{:S(2)}) %collective-permute-start.15) | collective-permute-done | bytes 262176 | tf_op jit(solution)/shard_map/ppermute | solution.py:29
  46.9 5.9 %decode.1 = f32[3,8,1024]{2,1,0:T(8,128)} custom-call(s32[6]{0:T(128)} %fusion.17.slot_ref, s32[6]{0:T(128)} %bitcast.136, f32[8,1024]{1,0:T(8,128)} %maximum_convert_fusion.query_ref, bf16[2,1,6,128,1024]{4,3,2,1,0:T(8,128)(2,1)} %cache_ref.1), custom_call_target="tpu_custom_call" | custom-call | bytes 3145728 | tf_op jit(solution)/shard_map/decode/pallas_call | solution.py:326
  52.8 2.0 %collective-permute-start.16 = (bf16[4,128,256]{2,1,0:T(8,128)(2,1)S(1)}, bf16[4,128,256]{2,1,0:T(8,128)(2,1)S(1)}, u32[]{:S(2)}, u32[]{:S(2)}) collective-permute-start(bf16[4,128,256]{2,1,0:T(8,128)(2,1)S(1)} %collective-permute-done.15.refs_9_), channel_id=1, source_target_pairs={{0,8},{4,12},{8,0},{12,4},{16,24},{20,28},{24,16},{28,20},{1,9},{5... | collective-permute-start | bytes 786440 | tf_op jit(solution)/shard_map/ppermute | solution.py:29
  55.9 3.9 %collective-permute-done.16.refs_10_ = bf16[4,128,256]{2,1,0:T(8,128)(2,1)S(1)} collective-permute-done((bf16[4,128,256]{2,1,0:T(8,128)(2,1)S(1)}, bf16[4,128,256]{2,1,0:T(8,128)(2,1)S(1)}, u32[]{:S(2)}, u32[]{:S(2)}) %collective-permute-start.16) | collective-permute-done | bytes 262176 | tf_op jit(solution)/shard_map/ppermute | solution.py:29
  59.8 2.4 %collective-permute-start.8 = (bf16[4,64,256]{2,1,0:T(8,128)(2,1)S(1)}, bf16[4,64,256]{2,1,0:T(8,128)(2,1)S(1)}, u32[]{:S(2)}, u32[]{:S(2)}) collective-permute-start(bf16[4,64,256]{2,1,0:T(8,128)(2,1)S(1)} %slice.108), channel_id=1, source_target_pairs={{0,8},{4,12},{8,0},{12,4},{16,24},{20,28},{24,16},{28,20},{1,9},{5... | collective-permute-start | bytes 393224 | tf_op jit(solution)/shard_map/ppermute | solution.py:29
  63.1 17.9 %collective-permute-done.36.refs_3_ = bf16[256,1024]{1,0:T(8,128)(2,1)S(1)} collective-permute-done((bf16[256,1024]{1,0:T(8,128)(2,1)S(1)}, bf16[256,1024]{1,0:T(8,128)(2,1)S(1)}, u32[]{:S(2)}, u32[]{:S(2)}) %collective-permute-start.36) | collective-permute-done | bytes 524320 | tf_op jit(solution)/shard_map/ppermute | solution.py:29
  83.2 1.9 %collective-permute-start.26 = (bf16[4,128,256]{2,1,0:T(8,128)(2,1)S(1)}, bf16[4,128,256]{2,1,0:T(8,128)(2,1)S(1)}, u32[]{:S(2)}, u32[]{:S(2)}) collective-permute-start(bf16[4,128,256]{2,1,0:T(8,128)(2,1)S(1)} %collective-permute-done.25.refs_9_), channel_id=1, source_target_pairs={{0,8},{4,12},{8,0},{12,4},{16,24},{20,28},{24,16},{28,20},{1,9},{5... | collective-permute-start | bytes 786440 | tf_op jit(solution)/shard_map/ppermute | solution.py:29
  86.0 2.9 %collective-permute-done.18.refs_12_ = bf16[4,64,256]{2,1,0:T(8,128)(2,1)S(1)} collective-permute-done((bf16[4,64,256]{2,1,0:T(8,128)(2,1)S(1)}, bf16[4,64,256]{2,1,0:T(8,128)(2,1)S(1)}, u32[]{:S(2)}, u32[]{:S(2)}) %collective-permute-start.18) | collective-permute-done | bytes 131104 | tf_op jit(solution)/shard_map/ppermute | solution.py:29
  91.4 1.7 collective-permute-done.26.refs_10_
  94.4 3.5 %collective-permute-done.27.refs_11_ = bf16[4,128,256]{2,1,0:T(8,128)(2,1)S(1)} collective-permute-done((bf16[4,128,256]{2,1,0:T(8,128)(2,1)S(1)}, bf16[4,128,256]{2,1,0:T(8,128)(2,1)S(1)}, u32[]{:S(2)}, u32[]{:S(2)}) %collective-permute-start.27) | collective-permute-done | bytes 262176 | tf_op jit(solution)/shard_map/ppermute | solution.py:29
  98.2 6.0 %attend_own.1.refs_6_ = f32[256,1024]{1,0:T(8,128)} custom-call(s32[2]{0:T(128)} %pad_add_fusion.place_ref.refs_0_, s32[1,48]{1,0:T(1,128)} %subtract_bitcast_fusion.starts_ref.refs_1_, s32[1,48]{1,0:T(1,128)} %bitcast.143, bf16[256,1024]{1,0:T(8,128)(2,1)} %copy-done.20, bf16[256,1024]{1,0:T(8,128)(2,1)} %refs_4_.5, bf16[256,1024]{1,0:T(8,128)(2,1)} %copy-done.21, ...), custom_call_target="tpu_custom_call" | custom-call | flops 1879048192 | bytes 2097152 | tf_op jit(solution)/shard_map/attend_own/pallas_call | solution.py:148
  104.2 1.6 collective-permute-start.28
  106.9 7.5 %attend_1.1.refs_6_ = f32[256,1024]{1,0:T(8,128)} custom-call(s32[2]{0:T(128)} %pad_add_fusion.place_ref.refs_0_, s32[1,48]{1,0:T(1,128)} %subtract_bitcast_fusion.starts_ref.refs_1_, s32[1,48]{1,0:T(1,128)} %bitcast.144, bf16[256,1024]{1,0:T(8,128)(2,1)} %copy-done.20, bf16[256,1024]{1,0:T(8,128)(2,1)} %refs_4_.5, bf16[256,1024]{1,0:T(8,128)(2,1)} %copy-done.21, ...), custom_call_target="tpu_custom_call" | custom-call | flops 1879048192 | bytes 2097152 | tf_op jit(solution)/shard_map/attend_1/pallas_call | solution.py:163
  114.4 2.0 %collective-permute-start.37 = (bf16[256,1024]{1,0:T(8,128)(2,1)S(1)}, bf16[256,1024]{1,0:T(8,128)(2,1)S(1)}, u32[]{:S(2)}, u32[]{:S(2)}) collective-permute-start(bf16[256,1024]{1,0:T(8,128)(2,1)S(1)} %collective-permute-done.36.refs_3_), channel_id=1, source_target_pairs={{0,8},{4,12},{8,0},{12,4},{16,24},{20,28},{24,16},{28,20},{1,9},{5... | collective-permute-start | bytes 1572872 | tf_op jit(solution)/shard_map/ppermute | solution.py:29
  116.6 7.5 %attend_2.1.refs_6_ = f32[256,1024]{1,0:T(8,128)} custom-call(s32[2]{0:T(128)} %pad_add_fusion.place_ref.refs_0_, s32[1,48]{1,0:T(1,128)} %subtract_bitcast_fusion.starts_ref.refs_1_, s32[1,48]{1,0:T(1,128)} %bitcast.145, bf16[256,1024]{1,0:T(8,128)(2,1)} %copy-done.20, bf16[256,1024]{1,0:T(8,128)(2,1)} %refs_4_.5, bf16[256,1024]{1,0:T(8,128)(2,1)} %copy-done.21, ...), custom_call_target="tpu_custom_call" | custom-call | flops 1879048192 | bytes 2097152 | tf_op jit(solution)/shard_map/attend_2/pallas_call | solution.py:163
  125.6 7.8 %attend_3.1.rows_ref.refs_1_.normed_ref = bf16[256,1024]{1,0:T(8,128)(2,1)} custom-call(s32[2]{0:T(128)} %pad_add_fusion.place_ref.refs_0_, s32[1,48]{1,0:T(1,128)} %subtract_bitcast_fusion.starts_ref.refs_1_, s32[1,48]{1,0:T(1,128)} %bitcast.146, bf16[256,1024]{1,0:T(8,128)(2,1)} %copy-done.20, bf16[256,1024]{1,0:T(8,128)(2,1)} %refs_4_.5, ...), custom_call_target="tpu_custom_call" | custom-call | flops 1879048192 | bytes 2097152 | tf_op jit(solution)/shard_map/attend_3/pallas_call | solution.py:163
  136.1 6.1 %collective-permute-done.39.refs_6_ = bf16[128,1024]{1,0:T(8,128)(2,1)S(1)} collective-permute-done((bf16[128,1024]{1,0:T(8,128)(2,1)S(1)}, bf16[128,1024]{1,0:T(8,128)(2,1)S(1)}, u32[]{:S(2)}, u32[]{:S(2)}) %collective-permute-start.39) | collective-permute-done | bytes 262176 | tf_op jit(solution)/shard_map/ppermute | solution.py:29
  142.7 5.2 %collective-permute-done.35.rows_ref.refs_1_ = bf16[256,1024]{1,0:T(8,128)(2,1)S(1)} collective-permute-done((bf16[256,1024]{1,0:T(8,128)(2,1)}, bf16[256,1024]{1,0:T(8,128)(2,1)S(1)}, u32[]{:S(2)}, u32[]{:S(2)}) %collective-permute-start.35) | collective-permute-done | bytes 524320 | tf_op jit(solution)/shard_map/ppermute | solution.py:29
  147.9 5.0 %feed_near_own.1.refs_2_ = f32[256,1024]{1,0:T(8,128)} custom-call(bf16[256,1024]{1,0:T(8,128)(2,1)} %attend_3.1.rows_ref.refs_1_.normed_ref, bf16[1024,1024]{1,0:T(8,128)(2,1)} %up_ref.3, bf16[1024,1024]{1,0:T(8,128)(2,1)} %down_ref.3), custom_call_target="tpu_custom_call" | custom-call | flops 1073741824 | bytes 4194304 | tf_op jit(solution)/shard_map/feed_near_own/pallas_call | solution.py:205
  153.0 4.9 %feed_near_partner.1.refs_2_ = f32[256,1024]{1,0:T(8,128)} custom-call(bf16[256,1024]{1,0:T(8,128)(2,1)} %copy-done.6, bf16[1024,1024]{1,0:T(8,128)(2,1)} %up_ref.3, bf16[1024,1024]{1,0:T(8,128)(2,1)} %down_ref.3), custom_call_target="tpu_custom_call" | custom-call | flops 1073741824 | bytes 4194304 | tf_op jit(solution)/shard_map/feed_near_partner/pallas_call | solution.py:205
  159.9 6.0 %feed_far_partner.1 = bf16[256,1024]{1,0:T(8,128)(2,1)} custom-call(s32[2]{0:T(128)} %pad_add_fusion.place_ref.refs_0_, bf16[256,1024]{1,0:T(8,128)(2,1)} %copy-done.6, f32[256,1024]{1,0:T(8,128)} %feed_near_partner.1.refs_2_, bf16[256,1024]{1,0:T(8,128)(2,1)} %copy-done.2, bf16[256,1024]{1,0:T(8,128)(2,1)} %copy-done.1, bf16[256,1024]{1,0:T(8,128)(2,1)} %copy-done, ...), custom_call_target="tpu_custom_call" | custom-call | flops 1073741824 | bytes 4194304 | tf_op jit(solution)/shard_map/feed_far_partner/pallas_call | solution.py:248
  166.2 1.8 collective-permute-start.47
  168.1 1.8 collective-permute-start.48
  170.7 10.6 %collective-permute-done.47 = f32[3,2,1024]{2,1,0:T(2,128)S(1)} collective-permute-done((f32[3,2,1024]{2,1,0:T(2,128)S(1)}, f32[3,2,1024]{2,1,0:T(2,128)S(1)}, u32[]{:S(2)}, u32[]{:S(2)}) %collective-permute-start.47) | collective-permute-done | bytes 24608 | tf_op jit(solution)/shard_map/ppermute | solution.py:29
  181.3 1.7 collective-permute-done.49
  183.7 6.2 %feed_far_own.1.near_ref = f32[256,1024]{1,0:T(8,128)} custom-call(s32[2]{0:T(128)} %pad_add_fusion.place_ref.refs_0_, bf16[256,1024]{1,0:T(8,128)(2,1)} %attend_3.1.rows_ref.refs_1_.normed_ref, f32[256,1024]{1,0:T(8,128)} %feed_near_own.1.refs_2_, bf16[256,1024]{1,0:T(8,128)(2,1)} %copy-done.2, bf16[256,1024]{1,0:T(8,128)(2,1)} %copy-done.1, ...), custom_call_target="tpu_custom_call" | custom-call | flops 1073741824 | bytes 4194304 | tf_op jit(solution)/shard_map/feed_far_own/pallas_call | solution.py:248
  190.7 2.8 %finish.1 = bf16[256,1024]{1,0:T(8,128)(2,1)} custom-call(bf16[256,1024]{1,0:T(8,128)(2,1)} %attend_3.1.rows_ref.refs_1_.normed_ref, f32[256,1024]{1,0:T(8,128)} %feed_far_own.1.near_ref, bf16[256,1024]{1,0:T(8,128)(2,1)} %copy-done.11, f32[1,1024]{1,0:T(1,128)} %bitcast.134, f32[1,1024]{1,0:T(1,128)} %bitcast.135), custom_call_target="tpu_custom_call" | custom-call | tf_op jit(solution)/shard_map/finish/pallas_call | solution.py:271
  (191 shorter events, 28.6 us)
Async XLA Ops:
  12.0 13.0 %collective-permute-start.5 = (bf16[4,128,256]{2,1,0:T(8,128)(2,1)S(1)}, bf16[4,128,256]{2,1,0:T(8,128)(2,1)S(1)}, u32[]{:S(2)}, u32[]{:S(2)}) collective-permute-start(bf16[4,128,256]{2,1,0:T(8,128)(2,1)S(1)} %pad_maximum_fusion.1), channel_id=1, source_target_pairs={{0,1},{1,0},{2,3},{3,2},{4,5},{5,4},{6,7},{7,6},{8,9},{9,8},{10,11... | collective-permute-start | bytes 786440 | tf_op jit(solution)/shard_map/ppermute | solution.py:29
  12.0 32.1 %collective-permute-start.15 = (bf16[4,128,256]{2,1,0:T(8,128)(2,1)S(1)}, bf16[4,128,256]{2,1,0:T(8,128)(2,1)S(1)}, u32[]{:S(2)}, u32[]{:S(2)}) collective-permute-start(bf16[4,128,256]{2,1,0:T(8,128)(2,1)S(1)} %pad_maximum_fusion.1), channel_id=1, source_target_pairs={{0,2},{1,3},{2,0},{3,1},{4,6},{5,7},{6,4},{7,5},{8,10},{9,11},{10,... | collective-permute-start | bytes 786440 | tf_op jit(solution)/shard_map/ppermute | solution.py:29
  12.6 33.0 %collective-permute-start.25 = (bf16[4,128,256]{2,1,0:T(8,128)(2,1)S(1)}, bf16[4,128,256]{2,1,0:T(8,128)(2,1)S(1)}, u32[]{:S(2)}, u32[]{:S(2)}) collective-permute-start(bf16[4,128,256]{2,1,0:T(8,128)(2,1)S(1)} %pad_maximum_fusion.1), channel_id=1, source_target_pairs={{0,3},{1,2},{2,1},{3,0},{4,7},{5,6},{6,5},{7,4},{8,11},{9,10},{10,... | collective-permute-start | bytes 786440 | tf_op jit(solution)/shard_map/ppermute | solution.py:29
  16.4 36.4 %collective-permute-start = (bf16[256,1024]{1,0:T(8,128)(2,1)}, bf16[256,1024]{1,0:T(8,128)(2,1)S(1)}, u32[]{:S(2)}, u32[]{:S(2)}) collective-permute-start(bf16[256,1024]{1,0:T(8,128)(2,1)} %refs_4_.5), channel_id=1, source_target_pairs={{0,1},{1,2},{2,3},{3,4},{4,5},{5,6},{6,7},{7,8},{8,9},{9,10},{10,1... | collective-permute-start | bytes 1572872 | tf_op jit(solution)/shard_map/ppermute | solution.py:392
  17.7 37.1 %collective-permute-start.1 = (bf16[256,1024]{1,0:T(8,128)(2,1)}, bf16[256,1024]{1,0:T(8,128)(2,1)S(1)}, u32[]{:S(2)}, u32[]{:S(2)}) collective-permute-start(bf16[256,1024]{1,0:T(8,128)(2,1)} %refs_4_.5), channel_id=1, source_target_pairs={{1,0},{2,1},{3,2},{4,3},{5,4},{6,5},{7,6},{8,7},{9,8},{10,9},{11,1... | collective-permute-start | bytes 1572872 | tf_op jit(solution)/shard_map/ppermute | solution.py:393
  25.0 56.0 %collective-permute-start.36 = (bf16[256,1024]{1,0:T(8,128)(2,1)S(1)}, bf16[256,1024]{1,0:T(8,128)(2,1)S(1)}, u32[]{:S(2)}, u32[]{:S(2)}) collective-permute-start(bf16[256,1024]{1,0:T(8,128)(2,1)S(1)} %pad_maximum_fusion), channel_id=1, source_target_pairs={{0,2},{1,3},{2,0},{3,1},{4,6},{5,7},{6,4},{7,5},{8,10},{9,11},{10,... | collective-permute-start | bytes 1572872 | tf_op jit(solution)/shard_map/ppermute | solution.py:29
  44.1 11.3 %collective-permute-start.7 = (bf16[4,128,256]{2,1,0:T(8,128)(2,1)S(1)}, bf16[4,128,256]{2,1,0:T(8,128)(2,1)S(1)}, u32[]{:S(2)}, u32[]{:S(2)}) collective-permute-start(bf16[4,128,256]{2,1,0:T(8,128)(2,1)S(1)} %collective-permute-done.5.refs_9_), channel_id=1, source_target_pairs={{0,16},{4,20},{8,24},{12,28},{16,0},{20,4},{24,8},{28,12},{1,17},{... | collective-permute-start | bytes 786440 | tf_op jit(solution)/shard_map/ppermute | solution.py:29
  45.6 9.7 %collective-permute-start.6 = (bf16[4,128,256]{2,1,0:T(8,128)(2,1)S(1)}, bf16[4,128,256]{2,1,0:T(8,128)(2,1)S(1)}, u32[]{:S(2)}, u32[]{:S(2)}) collective-permute-start(bf16[4,128,256]{2,1,0:T(8,128)(2,1)S(1)} %collective-permute-done.5.refs_9_), channel_id=1, source_target_pairs={{0,8},{4,12},{8,0},{12,4},{16,24},{20,28},{24,16},{28,20},{1,9},{5... | collective-permute-start | bytes 786440 | tf_op jit(solution)/shard_map/ppermute | solution.py:29
  55.4 27.2 %collective-permute-start.10 = (bf16[4,128,256]{2,1,0:T(8,128)(2,1)S(1)}, bf16[4,128,256]{2,1,0:T(8,128)(2,1)S(1)}, u32[]{:S(2)}, u32[]{:S(2)}) collective-permute-start(bf16[4,128,256]{2,1,0:T(8,128)(2,1)S(1)} %collective-permute-done.5.refs_9_), channel_id=1, source_target_pairs={{0,4},{4,0},{8,12},{12,8},{16,20},{20,16},{24,28},{28,24},{1,5},{5... | collective-permute-start | bytes 786440 | tf_op jit(solution)/shard_map/ppermute | solution.py:29
  55.4 27.8 %collective-permute-start.20 = (bf16[4,128,256]{2,1,0:T(8,128)(2,1)S(1)}, bf16[4,128,256]{2,1,0:T(8,128)(2,1)S(1)}, u32[]{:S(2)}, u32[]{:S(2)}) collective-permute-start(bf16[4,128,256]{2,1,0:T(8,128)(2,1)S(1)} %collective-permute-done.15.refs_9_), channel_id=1, source_target_pairs={{0,4},{4,0},{8,12},{12,8},{16,20},{20,16},{24,28},{28,24},{1,5},{5... | collective-permute-start | bytes 786440 | tf_op jit(solution)/shard_map/ppermute | solution.py:29
  59.8 22.9 %collective-permute-start.8 = (bf16[4,64,256]{2,1,0:T(8,128)(2,1)S(1)}, bf16[4,64,256]{2,1,0:T(8,128)(2,1)S(1)}, u32[]{:S(2)}, u32[]{:S(2)}) collective-permute-start(bf16[4,64,256]{2,1,0:T(8,128)(2,1)S(1)} %slice.108), channel_id=1, source_target_pairs={{0,8},{4,12},{8,0},{12,4},{16,24},{20,28},{24,16},{28,20},{1,9},{5... | collective-permute-start | bytes 393224 | tf_op jit(solution)/shard_map/ppermute | solution.py:29
  62.5 20.2 %collective-permute-start.9 = (bf16[4,64,256]{2,1,0:T(8,128)(2,1)S(1)}, bf16[4,64,256]{2,1,0:T(8,128)(2,1)S(1)}, u32[]{:S(2)}, u32[]{:S(2)}) collective-permute-start(bf16[4,64,256]{2,1,0:T(8,128)(2,1)S(1)} %slice.109), channel_id=1, source_target_pairs={{0,16},{4,20},{8,24},{12,28},{16,0},{20,4},{24,8},{28,12},{1,17},{... | collective-permute-start | bytes 393224 | tf_op jit(solution)/shard_map/ppermute | solution.py:29
  83.2 9.9 %collective-permute-start.26 = (bf16[4,128,256]{2,1,0:T(8,128)(2,1)S(1)}, bf16[4,128,256]{2,1,0:T(8,128)(2,1)S(1)}, u32[]{:S(2)}, u32[]{:S(2)}) collective-permute-start(bf16[4,128,256]{2,1,0:T(8,128)(2,1)S(1)} %collective-permute-done.25.refs_9_), channel_id=1, source_target_pairs={{0,8},{4,12},{8,0},{12,4},{16,24},{20,28},{24,16},{28,20},{1,9},{5... | collective-permute-start | bytes 786440 | tf_op jit(solution)/shard_map/ppermute | solution.py:29
  90.9 15.3 %collective-permute-start.30 = (bf16[4,128,256]{2,1,0:T(8,128)(2,1)S(1)}, bf16[4,128,256]{2,1,0:T(8,128)(2,1)S(1)}, u32[]{:S(2)}, u32[]{:S(2)}) collective-permute-start(bf16[4,128,256]{2,1,0:T(8,128)(2,1)S(1)} %collective-permute-done.25.refs_9_), channel_id=1, source_target_pairs={{0,4},{4,0},{8,12},{12,8},{16,20},{20,16},{24,28},{28,24},{1,5},{5... | collective-permute-start | bytes 786440 | tf_op jit(solution)/shard_map/ppermute | solution.py:29
  90.9 14.9 %collective-permute-start.21 = (bf16[4,128,256]{2,1,0:T(8,128)(2,1)S(1)}, bf16[4,128,256]{2,1,0:T(8,128)(2,1)S(1)}, u32[]{:S(2)}, u32[]{:S(2)}) collective-permute-start(bf16[4,128,256]{2,1,0:T(8,128)(2,1)S(1)} %collective-permute-done.16.refs_10_), channel_id=1, source_target_pairs={{0,4},{4,0},{8,12},{12,8},{16,20},{20,16},{24,28},{28,24},{1,5},{5... | collective-permute-start | bytes 786440 | tf_op jit(solution)/shard_map/ppermute | solution.py:29
  93.1 13.0 %collective-permute-start.22 = (bf16[4,128,256]{2,1,0:T(8,128)(2,1)S(1)}, bf16[4,128,256]{2,1,0:T(8,128)(2,1)S(1)}, u32[]{:S(2)}, u32[]{:S(2)}) collective-permute-start(bf16[4,128,256]{2,1,0:T(8,128)(2,1)S(1)} %collective-permute-done.17.refs_11_), channel_id=1, source_target_pairs={{0,4},{4,0},{8,12},{12,8},{16,20},{20,16},{24,28},{28,24},{1,5},{5... | collective-permute-start | bytes 786440 | tf_op jit(solution)/shard_map/ppermute | solution.py:29
  93.9 10.3 %collective-permute-start.23 = (bf16[4,64,256]{2,1,0:T(8,128)(2,1)}, bf16[4,64,256]{2,1,0:T(8,128)(2,1)S(1)}, u32[]{:S(2)}, u32[]{:S(2)}) collective-permute-start(bf16[4,64,256]{2,1,0:T(8,128)(2,1)} %copy-done.33), channel_id=1, source_target_pairs={{0,4},{4,0},{8,12},{12,8},{16,20},{20,16},{24,28},{28,24},{1,5},{5... | collective-permute-start | bytes 393224 | tf_op jit(solution)/shard_map/ppermute | solution.py:29
  104.2 10.2 %collective-permute-start.28 = (bf16[4,64,256]{2,1,0:T(8,128)(2,1)S(1)}, bf16[4,64,256]{2,1,0:T(8,128)(2,1)S(1)}, u32[]{:S(2)}, u32[]{:S(2)}) collective-permute-start(bf16[4,64,256]{2,1,0:T(8,128)(2,1)S(1)} %slice.112), channel_id=1, source_target_pairs={{0,8},{4,12},{8,0},{12,4},{16,24},{20,28},{24,16},{28,20},{1,9},{5... | collective-permute-start | bytes 393224 | tf_op jit(solution)/shard_map/ppermute | solution.py:29
  105.9 27.7 %collective-permute-start.38 = (bf16[256,1024]{1,0:T(8,128)(2,1)S(1)}, bf16[256,1024]{1,0:T(8,128)(2,1)S(1)}, u32[]{:S(2)}, u32[]{:S(2)}) collective-permute-start(bf16[256,1024]{1,0:T(8,128)(2,1)S(1)} %collective-permute-done.36.refs_3_), channel_id=1, source_target_pairs={{0,16},{4,20},{8,24},{12,28},{16,0},{20,4},{24,8},{28,12},{1,17},{... | collective-permute-start | bytes 1572872 | tf_op jit(solution)/shard_map/ppermute | solution.py:29
  106.2 17.9 %collective-permute-start.31 = (bf16[4,128,256]{2,1,0:T(8,128)(2,1)S(1)}, bf16[4,128,256]{2,1,0:T(8,128)(2,1)S(1)}, u32[]{:S(2)}, u32[]{:S(2)}) collective-permute-start(bf16[4,128,256]{2,1,0:T(8,128)(2,1)S(1)} %collective-permute-done.26.refs_10_), channel_id=1, source_target_pairs={{0,4},{4,0},{8,12},{12,8},{16,20},{20,16},{24,28},{28,24},{1,5},{5... | collective-permute-start | bytes 786440 | tf_op jit(solution)/shard_map/ppermute | solution.py:29
  106.3 17.9 %collective-permute-start.32 = (bf16[4,128,256]{2,1,0:T(8,128)(2,1)S(1)}, bf16[4,128,256]{2,1,0:T(8,128)(2,1)S(1)}, u32[]{:S(2)}, u32[]{:S(2)}) collective-permute-start(bf16[4,128,256]{2,1,0:T(8,128)(2,1)S(1)} %collective-permute-done.27.refs_11_), channel_id=1, source_target_pairs={{0,4},{4,0},{8,12},{12,8},{16,20},{20,16},{24,28},{28,24},{1,5},{5... | collective-permute-start | bytes 786440 | tf_op jit(solution)/shard_map/ppermute | solution.py:29
  114.4 19.5 %collective-permute-start.37 = (bf16[256,1024]{1,0:T(8,128)(2,1)S(1)}, bf16[256,1024]{1,0:T(8,128)(2,1)S(1)}, u32[]{:S(2)}, u32[]{:S(2)}) collective-permute-start(bf16[256,1024]{1,0:T(8,128)(2,1)S(1)} %collective-permute-done.36.refs_3_), channel_id=1, source_target_pairs={{0,8},{4,12},{8,0},{12,4},{16,24},{20,28},{24,16},{28,20},{1,9},{5... | collective-permute-start | bytes 1572872 | tf_op jit(solution)/shard_map/ppermute | solution.py:29
  133.4 14.5 %collective-permute-start.35 = (bf16[256,1024]{1,0:T(8,128)(2,1)}, bf16[256,1024]{1,0:T(8,128)(2,1)S(1)}, u32[]{:S(2)}, u32[]{:S(2)}) collective-permute-start(bf16[256,1024]{1,0:T(8,128)(2,1)} %attend_3.1.rows_ref.refs_1_.normed_ref), channel_id=1, source_target_pairs={{0,1},{1,0},{2,3},{3,2},{4,5},{5,4},{6,7},{7,6},{8,9},{9,8},{10,11... | collective-permute-start | bytes 1572872 | tf_op jit(solution)/shard_map/ppermute | solution.py:29
  135.6 22.3 %collective-permute-start.41 = (bf16[256,1024]{1,0:T(8,128)(2,1)S(1)}, bf16[256,1024]{1,0:T(8,128)(2,1)S(1)}, u32[]{:S(2)}, u32[]{:S(2)}) collective-permute-start(bf16[256,1024]{1,0:T(8,128)(2,1)S(1)} %collective-permute-done.36.refs_3_), channel_id=1, source_target_pairs={{0,4},{4,0},{8,12},{12,8},{16,20},{20,16},{24,28},{28,24},{1,5},{5... | collective-permute-start | bytes 1572872 | tf_op jit(solution)/shard_map/ppermute | solution.py:29
  135.6 22.3 %collective-permute-start.42 = (bf16[256,1024]{1,0:T(8,128)(2,1)S(1)}, bf16[256,1024]{1,0:T(8,128)(2,1)S(1)}, u32[]{:S(2)}, u32[]{:S(2)}) collective-permute-start(bf16[256,1024]{1,0:T(8,128)(2,1)S(1)} %collective-permute-done.37.refs_4_), channel_id=1, source_target_pairs={{0,4},{4,0},{8,12},{12,8},{16,20},{20,16},{24,28},{28,24},{1,5},{5... | collective-permute-start | bytes 1572872 | tf_op jit(solution)/shard_map/ppermute | solution.py:29
  142.2 15.7 %collective-permute-start.43 = (bf16[256,1024]{1,0:T(8,128)(2,1)S(1)}, bf16[256,1024]{1,0:T(8,128)(2,1)S(1)}, u32[]{:S(2)}, u32[]{:S(2)}) collective-permute-start(bf16[256,1024]{1,0:T(8,128)(2,1)S(1)} %collective-permute-done.38.refs_5_), channel_id=1, source_target_pairs={{0,4},{4,0},{8,12},{12,8},{16,20},{20,16},{24,28},{28,24},{1,5},{5... | collective-permute-start | bytes 1572872 | tf_op jit(solution)/shard_map/ppermute | solution.py:29
  142.3 15.5 %collective-permute-start.44 = (bf16[128,1024]{1,0:T(8,128)(2,1)S(1)}, bf16[128,1024]{1,0:T(8,128)(2,1)S(1)}, u32[]{:S(2)}, u32[]{:S(2)}) collective-permute-start(bf16[128,1024]{1,0:T(8,128)(2,1)S(1)} %collective-permute-done.39.refs_6_), channel_id=1, source_target_pairs={{0,4},{4,0},{8,12},{12,8},{16,20},{20,16},{24,28},{28,24},{1,5},{5... | collective-permute-start | bytes 786440 | tf_op jit(solution)/shard_map/ppermute | solution.py:29
  147.9 10.0 %collective-permute-start.45 = (bf16[128,1024]{1,0:T(8,128)(2,1)S(1)}, bf16[128,1024]{1,0:T(8,128)(2,1)S(1)}, u32[]{:S(2)}, u32[]{:S(2)}) collective-permute-start(bf16[128,1024]{1,0:T(8,128)(2,1)S(1)} %collective-permute-done.40.refs_7_), channel_id=1, source_target_pairs={{0,4},{4,0},{8,12},{12,8},{16,20},{20,16},{24,28},{28,24},{1,5},{5... | collective-permute-start | bytes 786440 | tf_op jit(solution)/shard_map/ppermute | solution.py:29
  165.9 24.0 %collective-permute-start.46 = (bf16[256,1024]{1,0:T(8,128)(2,1)}, bf16[256,1024]{1,0:T(8,128)(2,1)S(1)}, u32[]{:S(2)}, u32[]{:S(2)}) collective-permute-start(bf16[256,1024]{1,0:T(8,128)(2,1)} %feed_far_partner.1), channel_id=1, source_target_pairs={{0,1},{1,0},{2,3},{3,2},{4,5},{5,4},{6,7},{7,6},{8,9},{9,8},{10,11... | collective-permute-start | bytes 1572872 | tf_op jit(solution)/shard_map/ppermute | solution.py:29
  166.2 15.1 %collective-permute-start.47 = (f32[3,2,1024]{2,1,0:T(2,128)S(1)}, f32[3,2,1024]{2,1,0:T(2,128)S(1)}, u32[]{:S(2)}, u32[]{:S(2)}) collective-permute-start(f32[3,2,1024]{2,1,0:T(2,128)S(1)} %get-tuple-element.18), channel_id=1, source_target_pairs={{0,1},{1,0},{2,3},{3,2},{4,5},{5,4},{6,7},{7,6},{8,9},{9,8},{10,11... | collective-permute-start | bytes 73736 | tf_op jit(solution)/shard_map/ppermute | solution.py:29
  168.1 13.3 %collective-permute-start.48 = (f32[3,2,1024]{2,1,0:T(2,128)S(1)}, f32[3,2,1024]{2,1,0:T(2,128)S(1)}, u32[]{:S(2)}, u32[]{:S(2)}) collective-permute-start(f32[3,2,1024]{2,1,0:T(2,128)S(1)} %get-tuple-element.19), channel_id=1, source_target_pairs={{0,2},{1,3},{2,0},{3,1},{4,6},{5,7},{6,4},{7,5},{8,10},{9,11},{10,... | collective-permute-start | bytes 73736 | tf_op jit(solution)/shard_map/ppermute | solution.py:29
  169.8 13.2 %collective-permute-start.49 = (f32[3,2,1024]{2,1,0:T(2,128)S(1)}, f32[3,2,1024]{2,1,0:T(2,128)S(1)}, u32[]{:S(2)}, u32[]{:S(2)}) collective-permute-start(f32[3,2,1024]{2,1,0:T(2,128)S(1)} %get-tuple-element.20), channel_id=1, source_target_pairs={{0,3},{1,2},{2,1},{3,0},{4,7},{5,6},{6,5},{7,4},{8,11},{9,10},{10,... | collective-permute-start | bytes 73736 | tf_op jit(solution)/shard_map/ppermute | solution.py:29
  (64 other events, 900.0 us)

commit v3 on v2

--- a/solution.py
+++ b/solution.py
@@ -33,149 +33,203 @@
     return lax.optimization_barrier((value,) + earlier)[0]
 
 
-def spread_in_plane(first):
-    half = first.shape[-2] // 2
-    low = lambda a: lax.slice_in_dim(a, 0, half, axis=a.ndim - 2)
-    high = lambda a: lax.slice_in_dim(a, half, 2 * half, axis=a.ndim - 2)
-    from_x = swapped(first, "tok", 2)
-    from_y = swapped(first, "tok", 4)
-    far_low = swapped(low(from_y), "tok", 2)
-    far_high = swapped(high(from_x), "tok", 4)
-    held = [(0, None, first), (2, None, from_x), (4, None, from_y), (6, 0, far_low), (6, 1, far_high)]
-    other = [(flip ^ 1, part, swapped(value, "tok", 1)) for flip, part, value in held]
-    return held + other
-
-
 def normalized(values, gain, bias):
     center = values - jnp.mean(values, axis=1, keepdims=True)
     spread = jnp.mean(center * center, axis=1, keepdims=True)
     return center * lax.rsqrt(spread + LN_EPS) * gain + bias
 
 
-def prepare(place_ref, starts_ref, ends_ref, before_ref, own_ref, behind_ref, rows_ref, bias_ref):
-    count = own_ref.shape[0]
+def project_kernel(place_ref, weight_ref, *refs):
+    shards, (query_ref, keyval_ref, top_ref, bottom_ref, rows_ref, sems) = refs[:-6], refs[-6:]
+    kv = place_ref[1]
+    count = shards[0].shape[0]
+    steps = (len(shards) - 1) // 2
+    width = weight_ref.shape[2]
+    moves = [(shards[0], kv, None)]
+    for step in range(1, steps + 1):
+        moves.append((shards[step], kv - step, kv >= step))
+        moves.append((shards[steps + step], kv + step, kv + step <= steps))
+
+    def guarded(needed, act):
+        if needed is None:
+            act()
+        else:
+            pl.when(needed)(act)
+
+    copies = []
+    for index, (source, owner, needed) in enumerate(moves):
+        safe = owner if needed is None else jnp.where(needed, owner, 0)
+        at = pl.ds(pl.multiple_of(safe * count, count), count)
+        copies.append((needed, pltpu.make_async_copy(source, rows_ref.at[at], sems.at[index])))
+    for needed, copy in copies:
+        guarded(needed, copy.start)
+    for needed, copy in copies:
+        guarded(needed, copy.wait)
+    scale = 1.0 / math.sqrt(HD)
+    for block in range(steps + 1):
+        at = slice(block * count, (block + 1) * count)
+        rows = rows_ref[at]
+        query = jnp.dot(rows, weight_ref[0], preferred_element_type=F32) * scale
+        query_ref[at] = query.astype(BF16)
+        keys = jnp.dot(rows, weight_ref[1], preferred_element_type=F32).astype(BF16)
+        values = jnp.dot(rows, weight_ref[2], preferred_element_type=F32).astype(BF16)
+        keyval_ref[at, :width] = keys
+        keyval_ref[at, width:] = values
+        for edge, edge_ref in ((0, top_ref), (steps, bottom_ref)):
+            if block == edge:
+                edge_ref[:, :width] = keys
+                edge_ref[:, width:] = values
+
+
+def project(place, weight, shards):
+    rows, width = shards[0].shape
+    heads_width = weight.shape[2]
+    blocks = (len(shards) + 1) // 2
+    edge = jax.ShapeDtypeStruct((rows, 2 * heads_width), BF16)
+    return pl.pallas_call(
+        project_kernel,
+        out_shape=(
+            jax.ShapeDtypeStruct((blocks * rows, heads_width), BF16),
+            jax.ShapeDtypeStruct((blocks * rows, 2 * heads_width), BF16),
+            edge,
+            edge,
+        ),
+        in_specs=[SMEM, VMEM] + [ANY] * len(shards),
+        out_specs=(VMEM,) * 4,
+        scratch_shapes=[pltpu.VMEM((blocks * rows, width), BF16), pltpu.SemaphoreType.DMA((len(shards),))],
+        compiler_params=pltpu.CompilerParams(vmem_limit_bytes=VMEM_LIMIT),
+        cost_estimate=pl.CostEstimate(
+            flops=6 * blocks * rows * width * heads_width, bytes_accessed=6 * width * heads_width, transcendentals=0
+        ),
+        name="project",
+    )(place, weight, *shards)
+
+
+def window_bias(first, count, starts, ends):
     reach = WIN // 2
-    rows_ref[0:count] = before_ref[...]
-    rows_ref[count : 2 * count] = own_ref[...]
-    rows_ref[2 * count : 3 * count] = behind_ref[...]
-    first = place_ref[0]
     query = first + lax.broadcasted_iota(jnp.int32, (count, 1), 0)
-    starts = starts_ref[...]
-    ends = ends_ref[...]
     low = jnp.max(jnp.where(starts <= query, starts, 0), axis=1, keepdims=True)
     high = jnp.min(jnp.where(ends > query, ends, 1 << 30), axis=1, keepdims=True)
     low = jnp.maximum(low, query - reach)
     high = jnp.minimum(high, query + reach + 1)
     key = first - count + lax.broadcasted_iota(jnp.int32, (count, 3 * count), 1)
-    bias_ref[...] = jnp.where((key >= low) & (key < high), 0.0, NEG_FILL)
-
-
-def attend(rows_ref, bias_ref, weight_ref, out_weight):
-    count = bias_ref.shape[0]
-    width = weight_ref.shape[2]
-    own = rows_ref[count : 2 * count]
-    rows = rows_ref[...]
-    scale = 1.0 / math.sqrt(HD)
-    query = (jnp.dot(own, weight_ref[0], preferred_element_type=F32) * scale).astype(BF16)
-    keys = jnp.dot(rows, weight_ref[1], preferred_element_type=F32).astype(BF16)
-    values = jnp.dot(rows, weight_ref[2], preferred_element_type=F32).astype(BF16)
+    return jnp.where((key >= low) & (key < high), 0.0, NEG_FILL)
+
+
+def attend(query, keyval_ref, bias):
+    count, width = query.shape
     lane = lax.broadcasted_iota(jnp.int32, (count, 2 * HD), 1)
-    bias = bias_ref[...]
     pairs = []
     for start in range(0, width, 2 * HD):
-        pair = slice(start, start + 2 * HD)
+        keys = keyval_ref[:, start : start + 2 * HD]
+        values = keyval_ref[:, width + start : width + start + 2 * HD]
         halves = []
         for side in range(2):
             inside = (lane < HD) if side == 0 else (lane >= HD)
-            only = jnp.where(inside, query[:, pair], jnp.zeros((), BF16))
-            scores = lax.dot_general(only, keys[:, pair], (((1,), (1,)), ((), ())), preferred_element_type=F32)
+            only = jnp.where(inside, query[:, start : start + 2 * HD], jnp.zeros((), BF16))
+            scores = lax.dot_general(only, keys, (((1,), (1,)), ((), ())), preferred_element_type=F32)
             scores = scores + bias
             highest = jnp.max(scores, axis=1, keepdims=True)
             weights = jnp.exp(scores - highest)
             total = jnp.sum(weights, axis=1, keepdims=True)
-            summed = jnp.dot(weights.astype(BF16), values[:, pair], preferred_element_type=F32)
+            summed = jnp.dot(weights.astype(BF16), values, preferred_element_type=F32)
             halves.append(summed / total)
         pairs.append(jnp.where(lane < HD, halves[0], halves[1]).astype(BF16))
-    attention = jnp.concatenate(pairs, axis=1)
-    return jnp.dot(attention, out_weight, preferred_element_type=F32)
-
-
-def attend_own_kernel(
-    place_ref, starts_ref, ends_ref, before_ref, own_ref, behind_ref, weight_ref, out_ref, sum_ref, rows_ref, bias_ref
-):
-    prepare(place_ref, starts_ref, ends_ref, before_ref, own_ref, behind_ref, rows_ref, bias_ref)
-    sum_ref[...] = attend(rows_ref, bias_ref, weight_ref, out_ref[...])
-
-
-def attend_next_kernel(layout, last, *refs):
-    count = len(layout)
-    place_ref, starts_ref, ends_ref, before_ref, own_ref, behind_ref, sum_ref, gain_ref, shift_ref = refs[:9]
-    pieces = refs[9 : 9 + count]
-    result_ref, rows_ref, bias_ref, weight_ref, out_ref, sems = refs[9 + count :]
-    tok = place_ref[1]
-    block = 128
+    return jnp.concatenate(pairs, axis=1)
+
+
+def attend_kernel(flips, place_ref, starts_ref, ends_ref, query_ref, before_ref, keyval_ref, behind_ref, *refs):
+    outs, (window_ref, sems) = refs[: len(flips)], refs[len(flips) :]
+    tok, kv = place_ref[0], place_ref[1]
+    count = outs[0].shape[0]
+    blocks = query_ref.shape[0] // count
     copies = []
-    for (flip, part), piece in zip(layout, pieces):
-        size = piece.shape[1]
-        shift = 0 if part is None else part * size
-        at = pl.multiple_of((tok ^ flip) * block, block)
-        moves = [(piece.at[0:3], weight_ref.at[:, pl.ds(at + shift, size), :])]
-        for side in range(2):
-            columns = slice(side * block, (side + 1) * block)
-            moves.append((piece.at[3, :, columns], out_ref.at[pl.ds(side * block + shift, size), pl.ds(at, block)]))
-        for source, target in moves:
-            copies.append(pltpu.make_async_copy(source, target, sems.at[len(copies)]))
+    for index, flip in enumerate(flips):
+        block = kv ^ flip
+        for part in range(3):
+            target = window_ref.at[index, part * count : (part + 1) * count]
+            sem = sems.at[index, part]
+            at = block + part - 1
+            inner = (at >= 0) & (at < blocks)
+            safe = jnp.where(inner, at, 0)
+            source = keyval_ref.at[pl.ds(pl.multiple_of(safe * count, count), count)]
+            copies.append((index, inner, pltpu.make_async_copy(source, target, sem)))
+            if part == 0:
+                copies.append((index, at < 0, pltpu.make_async_copy(before_ref, target, sem)))
+            if part == 2:
+                copies.append((index, at >= blocks, pltpu.make_async_copy(behind_ref, target, sem)))
+    for _, needed, copy in copies:
+        pl.when(needed)(copy.start)
+    for index, flip in enumerate(flips):
+        block = kv ^ flip
+        first = (tok * blocks + block) * count
+        bias = window_bias(first, count, starts_ref[...], ends_ref[...])
+        for owner, needed, copy in copies:
+            if owner == index:
+                pl.when(needed)(copy.wait)
+        query = query_ref[pl.ds(pl.multiple_of(block * count, count), count)]
+        outs[index][...] = attend(query, window_ref.at[index], bias)
+
+
+def attend_blocks(place, starts, ends, query, before, keyval, behind, rows, flips, name):
+    heads_width = query.shape[1]
+    pairs = rows * 3 * rows * heads_width * len(flips)
+    return pl.pallas_call(
+        functools.partial(attend_kernel, flips),
+        out_shape=tuple(jax.ShapeDtypeStruct((rows, heads_width), BF16) for _ in flips),
+        in_specs=[SMEM, VMEM, VMEM, VMEM, ANY, ANY, ANY],
+        out_specs=(VMEM,) * len(flips),
+        scratch_shapes=[
+            pltpu.VMEM((len(flips), 3 * rows, 2 * heads_width), BF16),
+            pltpu.SemaphoreType.DMA((len(flips), 3)),
+        ],
+        compiler_params=pltpu.CompilerParams(vmem_limit_bytes=VMEM_LIMIT),
+        cost_estimate=pl.CostEstimate(flops=32 * pairs, bytes_accessed=8 * rows * heads_width, transcendentals=0),
+        name=name,
+    )(place, starts, ends, query, before, keyval, behind)
+
+
+def first_norm_kernel(place_ref, hidden_ref, out_ref, gain_ref, bias_ref, *refs):
+    parts, (normed_ref, all_ref, weight_ref, sems) = refs[:-4], refs[-4:]
+    kv = place_ref[1]
+    eighths, quarters, depth, width = out_ref.shape
+    copies = []
+    for index in range(eighths):
+        target = weight_ref.at[:, index * depth : (index + 1) * depth]
+        copies.append(pltpu.make_async_copy(out_ref.at[index], target, sems.at[index]))
     for copy in copies:
         copy.start()
-    prepare(place_ref, starts_ref, ends_ref, before_ref, own_ref, behind_ref, rows_ref, bias_ref)
+    heads_width = eighths * depth
+    for flip, part_ref in enumerate(parts):
+        at = pl.multiple_of((kv ^ flip) * heads_width, heads_width)
+        all_ref[:, pl.ds(at, heads_width)] = part_ref[...]
     for copy in copies:
         copy.wait()
-    total = sum_ref[...] + attend(rows_ref, bias_ref, weight_ref, out_ref[...])
-    if last:
-        mixed = own_ref[...].astype(F32) + total
-        result_ref[...] = normalized(mixed, gain_ref[...], shift_ref[...]).astype(BF16)
-    else:
-        result_ref[...] = total
-
-
-def attend_cost(rows, width, heads_width):
-    flops = 2 * rows * width * heads_width * 8 + 4 * rows * 3 * rows * heads_width * 4
-    return pl.CostEstimate(flops=flops, bytes_accessed=4 * width * heads_width * 2, transcendentals=0)
-
-
-def attend_own(shards, weight, out_weight):
-    rows, width = shards[4].shape
+    weight = weight_ref[...].reshape(quarters * heads_width, width)
+    projected = jnp.dot(all_ref[...], weight, preferred_element_type=F32)
+    mixed = hidden_ref[...].astype(F32) + projected
+    normed_ref[...] = normalized(mixed, gain_ref[...], bias_ref[...]).astype(BF16)
+
+
+def first_norm(place, hidden, out_pieces, gain, bias, parts):
+    rows, width = hidden.shape
+    eighths, quarters, depth, _ = out_pieces.shape
     return pl.pallas_call(
-        attend_own_kernel,
-        out_shape=jax.ShapeDtypeStruct((rows, width), F32),
-        in_specs=[SMEM] + [VMEM] * 7,
-        out_specs=VMEM,
-        scratch_shapes=[pltpu.VMEM((3 * rows, width), BF16), pltpu.VMEM((rows, 3 * rows), F32)],
-        compiler_params=pltpu.CompilerParams(vmem_limit_bytes=VMEM_LIMIT),
-        cost_estimate=attend_cost(rows, width, out_weight.shape[0]),
-        name="attend_own",
-    )(*shards, weight, out_weight)
-
-
-def attend_next(shards, summed, gain, bias, pieces, heads_width, last, name):
-    rows, width = shards[4].shape
-    layout = tuple((flip, part) for flip, part, _ in pieces)
-    return pl.pallas_call(
-        functools.partial(attend_next_kernel, layout, last),
-        out_shape=jax.ShapeDtypeStruct((rows, width), BF16 if last else F32),
-        in_specs=[SMEM] + [VMEM] * 8 + [ANY] * len(pieces),
+        first_norm_kernel,
+        out_shape=jax.ShapeDtypeStruct((rows, width), BF16),
+        in_specs=[SMEM, VMEM, ANY, VMEM, VMEM] + [VMEM] * len(parts),
         out_specs=VMEM,
         scratch_shapes=[
-            pltpu.VMEM((3 * rows, width), BF16),
-            pltpu.VMEM((rows, 3 * rows), F32),
-            pltpu.VMEM((3, width, heads_width), BF16),
-            pltpu.VMEM((heads_width, width), BF16),
-            pltpu.SemaphoreType.DMA((3 * len(pieces),)),
+            pltpu.VMEM((rows, width), BF16),
+            pltpu.VMEM((quarters, eighths * depth, width), BF16),
+            pltpu.SemaphoreType.DMA((eighths,)),
         ],
         compiler_params=pltpu.CompilerParams(vmem_limit_bytes=VMEM_LIMIT),
-        cost_estimate=attend_cost(rows, width, heads_width),
-        name=name,
-    )(*shards, summed, gain, bias, *[value for _, _, value in pieces])
+        cost_estimate=pl.CostEstimate(
+            flops=2 * rows * width * width, bytes_accessed=2 * width * width, transcendentals=0
+        ),
+        name="first_norm",
+    )(place, hidden, out_pieces, gain, bias, *parts)
 
 
 def gelu(values):
@@ -218,7 +272,7 @@
     place_ref, rows_ref, near_ref = refs[:3]
     pieces = refs[3 : 3 + count]
     sum_ref, up_ref, down_ref, total_ref, sems = refs[3 + count :]
-    tok = place_ref[1]
+    tok = place_ref[0]
     block = 128
     copies = []
     for (flip, part), piece in zip(layout, pieces):
@@ -353,10 +407,14 @@
     return decode(slots, piece_used[0], jnp.concatenate(queries).astype(F32), kv_cache)
 
 
-def decode_merged(partial, own):
+def exchanged_partials(partial, own):
     parts = [partial[:, :own]]
     for flip in range(1, lax.axis_size("kv")):
         parts.append(swapped(partial[:, flip * own : (flip + 1) * own], "kv", flip))
+    return parts
+
+
+def merged_partials(parts):
     high = functools.reduce(jnp.maximum, [part[0] for part in parts])
     factors = [jnp.exp(part[0] - high) for part in parts]
     total = sum(part[1] * factor for part, factor in zip(parts, factors))
@@ -384,63 +442,64 @@
     kv = lax.axis_index("kv")
     toks, kvs = lax.axis_size("tok"), lax.axis_size("kv")
     rows, width = hidden_in.shape
-    heads_width = out_weight.shape[0]
-    block = width // toks
+    place = jnp.stack([tok, kv]).astype(jnp.int32)
+    eighth = lambda value: lax.dynamic_slice_in_dim(value, tok * (value.shape[0] // toks), value.shape[0] // toks, 0)
 
     queries = gathered_queries(dec_query)
-    flat = toks * kvs
-    before = lax.ppermute(hidden_in, ("tok", "kv"), [(i, i + 1) for i in range(flat - 1)])
-    behind = lax.ppermute(hidden_in, ("tok", "kv"), [(i + 1, i) for i in range(flat - 1)])
-
-    eighth = lambda value, axis: lax.dynamic_slice_in_dim(value, tok * block, block, axis)
-    out_part = eighth(out_weight, 1)
-    qkv_part = lax.optimization_barrier(eighth(qkv_weight, 0))
-    bundle = jnp.concatenate(
-        [
-            jnp.transpose(qkv_part, (1, 0, 2)),
-            jnp.concatenate([out_part[:block], out_part[block:]], axis=1)[None],
-        ],
-        axis=0,
-    )
-    bundle = after(bundle, *queries)
-    foreign = [swapped(bundle, "kv", flip) for flip in range(1, kvs)]
-    feed_part = jnp.concatenate([eighth(up_weight, 0), eighth(down_weight, 0)], axis=0)
-    feed_foreign = swapped(feed_part, "kv", 2)
-
     partial = decode_partial(queries, kv_cache, piece_req, piece_used)
-    pieces = [spread_in_plane(foreign[0])]
-    turn = partial
-    for value in foreign[1:]:
-        pieces.append(spread_in_plane(after(value, turn)))
-        turn = pieces[-1][1][2]
-    feed_pieces = spread_in_plane(after(feed_foreign, turn))
-
-    place = jnp.stack([(tok * kvs + kv) * rows, tok]).astype(jnp.int32)
+    from_below, from_above = [], []
+    rising = falling = hidden_in
+    for step in range(1, kvs):
+        links = range(step - 1, kvs - 1)
+        rising = lax.ppermute(rising, "kv", [(i, i + 1) for i in links])
+        falling = lax.ppermute(falling, "kv", [(kvs - 1 - i, kvs - 2 - i) for i in links])
+        from_below.append(rising)
+        from_above.append(falling)
+        if step == 1:
+            rising, falling = after(rising, partial), after(falling, partial)
+
+    out_pieces = lax.all_gather(lax.all_gather(eighth(out_weight), "kv"), "tok")
+
+    feed_part = jnp.concatenate([eighth(up_weight), eighth(down_weight)], axis=0)
+    feed_here = swapped(after(feed_part, from_below[1], from_above[1]), "kv", 2)
+
     order = jnp.arange(stretch_len.shape[0])
     ends = jnp.sum(jnp.where(order[:, None] <= order[None, :], stretch_len[:, None], 0), axis=0, dtype=jnp.int32)
     starts = (ends - stretch_len)[None, :]
-    shards = (place, starts, ends[None, :], before, hidden_in, behind)
-
-    total = attend_own(shards, jnp.transpose(qkv_weight, (1, 0, 2)), out_weight)
-    for index, quarter in enumerate(pieces):
-        last = index == len(pieces) - 1
-        partial = after(partial, total) if last else partial
-        total = attend_next(
-            shards, total, ln1_gain[None, :], ln1_bias[None, :], quarter, heads_width, last, "attend_%d" % (index + 1)
-        )
-    normed = total
-
+    ends = ends[None, :]
+
+    shards = [hidden_in] + from_below + from_above
+    query, keyval, top, bottom = project(place, jnp.transpose(qkv_weight, (1, 0, 2)), shards)
+    before = lax.ppermute(bottom, "tok", [(i, i + 1) for i in range(toks - 1)])
+    behind = lax.ppermute(top, "tok", [(i + 1, i) for i in range(toks - 1)])
+    window = (place, starts, ends, query, before, keyval, behind, rows)
+    parts = [None] * kvs
+    parts[3], parts[2] = attend_blocks(*window, (3, 2), "attend_far")
+    feed_here = after(feed_here, parts[3], parts[2])
+    parts[3], parts[2] = swapped(parts[3], "kv", 3), swapped(parts[2], "kv", 2)
+    feed_x, feed_y = swapped(feed_here, "tok", 2), swapped(feed_here, "tok", 4)
+    window = (place, starts, ends, after(query, feed_here), before, keyval, behind, rows)
+    parts[1], parts[0] = attend_blocks(*window, (1, 0), "attend_near")
+    parts[1] = swapped(parts[1], "kv", 1)
+    half = feed_here.shape[0] // 2
+    far_up = swapped(after(feed_y, parts[0])[:half], "tok", 2)
+    far_down = swapped(after(feed_x, parts[0])[half:], "tok", 4)
+    normed = first_norm(place, hidden_in, out_pieces, ln1_gain[None, :], ln1_bias[None, :], parts)
+
+    partner = swapped(normed, "kv", 1)
+    held = [(0, None, feed_here), (2, None, feed_x), (4, None, feed_y), (6, 0, far_up), (6, 1, far_down)]
+    feed_pieces = held + [(flip ^ 1, part, swapped(after(value, normed), "tok", 1)) for flip, part, value in held]
     units = up_weight.shape[1]
-    partner = swapped(normed, "kv", 1)
     near = feed_near(normed, up_weight, down_weight, "feed_near_own")
-    partner = after(partner, near)
+    dec_out = merged_partials(exchanged_partials(after(partial, normed), dec_query.shape[0]))
+    partner = after(partner, near, dec_out)
     near_away = feed_near(partner, up_weight, down_weight, "feed_near_partner")
     away = feed_far(place, partner, near_away, feed_pieces, units, BF16, "feed_far_partner")
     arrived = swapped(away, "kv", 1)
     mine = feed_far(place, after(normed, away), near, feed_pieces, units, F32, "feed_far_own")
     prefill_out = finish(normed, mine, arrived, ln2_gain[None, :], ln2_bias[None, :])
 
-    return prefill_out, decode_merged(partial, dec_query.shape[0])
+    return prefill_out, dec_out
 
 
 def extended(value, sides, width):

time: 194 us -> 203 us (1.046)
  blocking collectives: 0 us -> 16.3 us
  between operations: 1.28 us -> 14.4 us
  waiting for transfers between devices: 82.8 us -> 69.7 us
  Pallas kernels: 59.5 us -> 55 us
  starting transfers between devices: 38.2 us -> 35.9 us
  local copies, waits for them, and re-layouts: 8.37 us -> 6.29 us
    ppermute x48 -> x21, waiting for transfers between devices: 82.8 us -> 47.7 us  [swapped(): return lax.ppermute(value, axis, [(i, i ^ flip) for i in range(count)])]
    ppermute x2 -> x8, waiting for transfers between devices: 0.01 us -> 22 us  [the longest x3 18.8 us: routed_body(): lax.ppermute(falling, 'kv', [(kvs - 1 - i, kvs - 2 - i) for i in links])]
    all_gather x0 -> x1, blocking collectives: none -> 16.3 us  [routed_body(): out_pieces = lax.all_gather(lax.all_gather(eighth(out_weight), 'kv'), 'tok')]
    ppermute x48 -> x21, starting transfers between devices: 35.6 us -> 23.9 us  [swapped(): return lax.ppermute(value, axis, [(i, i ^ flip) for i in range(count)])]
    ppermute x2 -> x8, starting transfers between devices: 2.6 us -> 12 us  [the longest x3 5.36 us: routed_body(): rising = lax.ppermute(rising, 'kv', [(i, i + 1) for i in links])]
    pallas_call x4, Pallas kernels: 28.7 us -> 24.1 us  [the longest x2 13.5 us: attend_blocks(): pl.pallas_call(functools.partial(attend_kernel, flips), out_shape=tuple((...]
    unnamed x92 -> x56, local copies, waits for them, and re-layouts: 5.44 us -> 5.16 us
  transfers between devices with their start and end apart: 50 -> 30, of which waited for: 16 -> 14; matrix products, arithmetic and copies ran while one was open for 3% -> 3% of each run, Pallas kernels for 26% -> 23%
where the time goes in v3:
time: 203 us; the launch traced here: 202 us
  waiting for transfers between devices  69.7 us (34%)
  Pallas kernels  55 us (27%)
  starting transfers between devices  35.9 us (18%)
  blocking collectives  16.3 us (8%)
  between operations  14.4 us (7%)
  local copies, waits for them, and re-layouts  6.29 us (3%)
  other arithmetic  4.4 us (2%)
    ppermute x21, waiting for transfers between devices, swapped(): return lax.ppermute(value, axis, [(i, i ^ flip) for i in range(count)])  47.7 us
    ppermute x21, starting transfers between devices, swapped(): return lax.ppermute(value, axis, [(i, i ^ flip) for i in range(count)])  23.9 us
    ppermute x3, waiting for transfers between devices, routed_body(): lax.ppermute(falling, 'kv', [(kvs - 1 - i, kvs - 2 - i) for i in links])  18.8 us
    all_gather x1, blocking collectives, routed_body(): out_pieces = lax.all_gather(lax.all_gather(eighth(out_weight), 'kv'), 'tok')  16.3 us
    pallas_call x2, Pallas kernels, attend_blocks(): pl.pallas_call(functools.partial(attend_kernel, flips), out_shape=tuple((...  13.5 us
    pallas_call x2, Pallas kernels, feed_far(): pl.pallas_call(functools.partial(feed_far_kernel, layout), out_shape=jax....  12.1 us
    pallas_call x2, Pallas kernels, feed_near(): pl.pallas_call(feed_near_kernel, out_shape=jax.ShapeDtypeStruct((count, w...  10 us
    pallas_call x1, Pallas kernels, decode(): pl.pallas_call(decode_kernel, grid=(pieces,), out_shape=jax.ShapeDtypeStr...  6.01 us
  transfers between devices with their start and end apart: 30, of which 14 were waited for; matrix products, arithmetic and copies ran while one was open for 3% of the time, Pallas kernels for 23%

profile of v3, /device:TPU:0, one launch (start us, length us, event | category | flops | bytes accessed | tf_op | source)
XLA Modules:
  0.0 202.1 jit_solution(3488437920863201286)
XLA Ops:
  8.2 16.3 %all-gather = bf16[128,1024]{1,0:T(8,128)(2,1)} all-gather(bf16[32,1024]{1,0:T(8,128)(2,1)S(1)} %constant_dynamic-slice_fusion.2), channel_id=2, replica_groups=mesh['tok'=8,'kv'=4] {'kv'}, dimensions={0}, use_global_device_ids=true | all-gather | bytes 327680 | tf_op jit(solution)/shard_map/all_gather | solution.py:461
  24.5 4.0 %collective-permute-start = (bf16[256,1024]{1,0:T(8,128)(2,1)}, bf16[256,1024]{1,0:T(8,128)(2,1)S(1)}, u32[]{:S(2)}, u32[]{:S(2)}) collective-permute-start(bf16[256,1024]{1,0:T(8,128)(2,1)} %hidden_ref.1), channel_id=1, source_target_pairs={{0,1},{1,2},{2,3},{4,5},{5,6},{6,7},{8,9},{9,10},{10,11},{12,13},{... | collective-permute-start | bytes 1572872 | tf_op jit(solution)/shard_map/ppermute | solution.py:454
  29.8 2.7 %collective-permute-start.1 = (bf16[2,1024]{1,0:T(2,128)(2,1)}, bf16[2,1024]{1,0:T(2,128)(2,1)S(1)}, u32[]{:S(2)}, u32[]{:S(2)}) collective-permute-start(bf16[2,1024]{1,0:T(2,128)(2,1)} %param.24), channel_id=1, source_target_pairs={{0,1},{1,0},{2,3},{3,2},{4,5},{5,4},{6,7},{7,6},{8,9},{9,8},{10,11... | collective-permute-start | bytes 12296 | tf_op jit(solution)/shard_map/ppermute | solution.py:29
  32.5 2.4 %collective-permute-start.2 = (bf16[2,1024]{1,0:T(2,128)(2,1)}, bf16[2,1024]{1,0:T(2,128)(2,1)S(1)}, u32[]{:S(2)}, u32[]{:S(2)}) collective-permute-start(bf16[2,1024]{1,0:T(2,128)(2,1)} %param.24), channel_id=1, source_target_pairs={{0,2},{1,3},{2,0},{3,1},{4,6},{5,7},{6,4},{7,5},{8,10},{9,11},{10,... | collective-permute-start | bytes 12296 | tf_op jit(solution)/shard_map/ppermute | solution.py:29
  36.1 4.6 %collective-permute-done.1 = bf16[2,1024]{1,0:T(2,128)(2,1)S(1)} collective-permute-done((bf16[2,1024]{1,0:T(2,128)(2,1)}, bf16[2,1024]{1,0:T(2,128)(2,1)S(1)}, u32[]{:S(2)}, u32[]{:S(2)}) %collective-permute-start.1) | collective-permute-done | bytes 4128 | tf_op jit(solution)/shard_map/ppermute | solution.py:29
  42.7 1.3 maximum_convert_fusion.query_ref
  44.0 6.0 %decode.1 = f32[3,8,1024]{2,1,0:T(8,128)} custom-call(s32[6]{0:T(128)} %fusion.17.slot_ref, s32[6]{0:T(128)} %bitcast.137, f32[8,1024]{1,0:T(8,128)} %maximum_convert_fusion.query_ref, bf16[2,1,6,128,1024]{4,3,2,1,0:T(8,128)(2,1)} %cache_ref.1), custom_call_target="tpu_custom_call" | custom-call | bytes 3145728 | tf_op jit(solution)/shard_map/decode/pallas_call | solution.py:380
  52.8 10.7 %collective-permute-done.7.refs_5_ = bf16[256,1024]{1,0:T(8,128)(2,1)S(1)} collective-permute-done((bf16[256,1024]{1,0:T(8,128)(2,1)S(1)}, bf16[256,1024]{1,0:T(8,128)(2,1)S(1)}, u32[]{:S(2)}, u32[]{:S(2)}) %collective-permute-start.7) | collective-permute-done | bytes 524320 | tf_op jit(solution)/shard_map/ppermute | solution.py:455
  66.5 8.1 %collective-permute-done.8.refs_6_ = bf16[256,1024]{1,0:T(8,128)(2,1)} collective-permute-done((bf16[256,1024]{1,0:T(8,128)(2,1)S(1)}, bf16[256,1024]{1,0:T(8,128)(2,1)}, u32[]{:S(2)}, u32[]{:S(2)}) %collective-permute-start.8) | collective-permute-done | bytes 524320 | tf_op jit(solution)/shard_map/ppermute | solution.py:455
  74.7 5.9 %project.1 = (bf16[1024,256]{1,0:T(8,128)(2,1)}, bf16[1024,512]{1,0:T(8,128)(2,1)}, bf16[256,512]{1,0:T(8,128)(2,1)}, bf16[256,512]{1,0:T(8,128)(2,1)}) custom-call(s32[2]{0:T(128)} %pad_add_fusion.place_ref.refs_0_, bf16[3,1024,256]{2,1,0:T(8,128)(2,1)} %bitcast.138, bf16[256,1024]{1,0:T(8,128)(2,1)} %hidden_ref.1, bf16[256,1024]{1,0:T(8,128)(2,1)} %copy-done.17, ...), custom_call_target="tpu_custom_call" | custom-call | flops 1610612736 | bytes 1572864 | tf_op jit(solution)/shard_map/project/pallas_call | solution.py:89
  82.0 1.5 collective-permute-start.11
  84.1 3.2 %collective-permute-done.11.behind_ref = bf16[256,512]{1,0:T(8,128)(2,1)S(1)} collective-permute-done((bf16[256,512]{1,0:T(8,128)(2,1)}, bf16[256,512]{1,0:T(8,128)(2,1)S(1)}, u32[]{:S(2)}, u32[]{:S(2)}) %collective-permute-start.11) | collective-permute-done | bytes 262176 | tf_op jit(solution)/shard_map/ppermute | solution.py:474
  88.0 6.7 %attend_far.1 = (bf16[256,256]{1,0:T(8,128)(2,1)}, bf16[256,256]{1,0:T(8,128)(2,1)}) custom-call(s32[2]{0:T(128)} %pad_add_fusion.place_ref.refs_0_, s32[1,48]{1,0:T(1,128)} %subtract_bitcast_fusion.starts_ref, s32[1,48]{1,0:T(1,128)} %bitcast.139, bf16[1024,256]{1,0:T(8,128)(2,1)} %get-tuple-element.35.query_ref, bf16[256,512]{1,0:T(8,128)(2,1)} %copy-done.22, ...), custom_call_target="tpu_custom_call" | custom-call | flops 3221225472 | bytes 524288 | tf_op jit(solution)/shard_map/attend_far/pallas_call | solution.py:177
  94.8 14.5 %collective-permute-done.9.refs_3_ = bf16[256,1024]{1,0:T(8,128)(2,1)S(1)} collective-permute-done((bf16[256,1024]{1,0:T(8,128)(2,1)S(1)}, bf16[256,1024]{1,0:T(8,128)(2,1)S(1)}, u32[]{:S(2)}, u32[]{:S(2)}) %collective-permute-start.9) | collective-permute-done | bytes 524320 | tf_op jit(solution)/shard_map/ppermute | solution.py:29
  109.3 3.5 %collective-permute-start.19 = (bf16[256,1024]{1,0:T(8,128)(2,1)S(1)}, bf16[256,1024]{1,0:T(8,128)(2,1)S(1)}, u32[]{:S(2)}, u32[]{:S(2)}) collective-permute-start(bf16[256,1024]{1,0:T(8,128)(2,1)S(1)} %collective-permute-done.9.refs_3_), channel_id=1, source_target_pairs={{0,8},{4,12},{8,0},{12,4},{16,24},{20,28},{24,16},{28,20},{1,9},{5... | collective-permute-start | bytes 1572872 | tf_op jit(solution)/shard_map/ppermute | solution.py:29
  113.2 6.7 %attend_near.1 = (bf16[256,256]{1,0:T(8,128)(2,1)}, bf16[256,256]{1,0:T(8,128)(2,1)}) custom-call(s32[2]{0:T(128)} %pad_add_fusion.place_ref.refs_0_, s32[1,48]{1,0:T(1,128)} %subtract_bitcast_fusion.starts_ref, s32[1,48]{1,0:T(1,128)} %bitcast.140, bf16[1024,256]{1,0:T(8,128)(2,1)} %get-tuple-element.35.query_ref, bf16[256,512]{1,0:T(8,128)(2,1)} %copy-done.22, ...), custom_call_target="tpu_custom_call" | custom-call | flops 3221225472 | bytes 524288 | tf_op jit(solution)/shard_map/attend_near/pallas_call | solution.py:177
  121.1 3.4 %collective-permute-start.14 = (bf16[256,256]{1,0:T(8,128)(2,1)S(1)}, bf16[256,256]{1,0:T(8,128)(2,1)S(1)}, u32[]{:S(2)}, u32[]{:S(2)}) collective-permute-start(bf16[256,256]{1,0:T(8,128)(2,1)S(1)} %copy-done.24), channel_id=1, source_target_pairs={{0,3},{1,2},{2,1},{3,0},{4,7},{5,6},{6,5},{7,4},{8,11},{9,10},{10,... | collective-permute-start | bytes 393224 | tf_op jit(solution)/shard_map/ppermute | solution.py:29
  124.9 1.8 collective-permute-start.22
  127.2 5.5 %collective-permute-done.13.refs_2_ = bf16[256,256]{1,0:T(8,128)(2,1)S(1)} collective-permute-done((bf16[256,256]{1,0:T(8,128)(2,1)S(1)}, bf16[256,256]{1,0:T(8,128)(2,1)S(1)}, u32[]{:S(2)}, u32[]{:S(2)}) %collective-permute-start.13) | collective-permute-done | bytes 131104 | tf_op jit(solution)/shard_map/ppermute | solution.py:29
  133.5 4.7 %first_norm.1.rows_ref.refs_1_.normed_ref = bf16[256,1024]{1,0:T(8,128)(2,1)} custom-call(s32[2]{0:T(128)} %pad_add_fusion.place_ref.refs_0_, bf16[256,1024]{1,0:T(8,128)(2,1)} %hidden_ref.1, bf16[8,4,32,1024]{3,2,1,0:T(8,128)(2,1)} %bitcast.131, f32[1,1024]{1,0:T(1,128)} %bitcast.135, f32[1,1024]{1,0:T(1,128)} %bitcast.136, ...), custom_call_target="tpu_custom_call" | custom-call | flops 536870912 | bytes 2097152 | tf_op jit(solution)/shard_map/first_norm/pallas_call | solution.py:217
  138.1 2.2 %collective-permute-start.15 = (bf16[256,1024]{1,0:T(8,128)(2,1)}, bf16[256,1024]{1,0:T(8,128)(2,1)S(1)}, u32[]{:S(2)}, u32[]{:S(2)}) collective-permute-start(bf16[256,1024]{1,0:T(8,128)(2,1)} %first_norm.1.rows_ref.refs_1_.normed_ref), channel_id=1, source_target_pairs={{0,1},{1,0},{2,3},{3,2},{4,5},{5,4},{6,7},{7,6},{8,9},{9,8},{10,11... | collective-permute-start | bytes 1572872 | tf_op jit(solution)/shard_map/ppermute | solution.py:29
  140.3 1.7 collective-permute-start.21
  142.7 4.5 %collective-permute-done.21.refs_6_ = bf16[128,1024]{1,0:T(8,128)(2,1)S(1)} collective-permute-done((bf16[128,1024]{1,0:T(8,128)(2,1)S(1)}, bf16[128,1024]{1,0:T(8,128)(2,1)S(1)}, u32[]{:S(2)}, u32[]{:S(2)}) %collective-permute-start.21) | collective-permute-done | bytes 262176 | tf_op jit(solution)/shard_map/ppermute | solution.py:29
  147.5 4.5 %collective-permute-done.16 = f32[3,2,1024]{2,1,0:T(2,128)S(1)} collective-permute-done((f32[3,2,1024]{2,1,0:T(2,128)S(1)}, f32[3,2,1024]{2,1,0:T(2,128)S(1)}, u32[]{:S(2)}, u32[]{:S(2)}) %collective-permute-start.16) | collective-permute-done | bytes 24608 | tf_op jit(solution)/shard_map/ppermute | solution.py:29
  153.1 3.6 %collective-permute-done.17 = f32[3,2,1024]{2,1,0:T(2,128)S(1)} collective-permute-done((f32[3,2,1024]{2,1,0:T(2,128)S(1)}, f32[3,2,1024]{2,1,0:T(2,128)S(1)}, u32[]{:S(2)}, u32[]{:S(2)}) %collective-permute-start.17) | collective-permute-done | bytes 24608 | tf_op jit(solution)/shard_map/ppermute | solution.py:29
  156.7 1.4 collective-permute-start.18
  158.2 4.9 %feed_near_own.1.refs_2_ = f32[256,1024]{1,0:T(8,128)} custom-call(bf16[256,1024]{1,0:T(8,128)(2,1)} %first_norm.1.rows_ref.refs_1_.normed_ref, bf16[1024,1024]{1,0:T(8,128)(2,1)} %up_ref.3, bf16[1024,1024]{1,0:T(8,128)(2,1)} %down_ref.3), custom_call_target="tpu_custom_call" | custom-call | flops 1073741824 | bytes 4194304 | tf_op jit(solution)/shard_map/feed_near_own/pallas_call | solution.py:259
  164.4 5.1 %feed_near_partner.1.refs_2_ = f32[256,1024]{1,0:T(8,128)} custom-call(bf16[256,1024]{1,0:T(8,128)(2,1)} %copy-done.5, bf16[1024,1024]{1,0:T(8,128)(2,1)} %up_ref.3, bf16[1024,1024]{1,0:T(8,128)(2,1)} %down_ref.3), custom_call_target="tpu_custom_call" | custom-call | flops 1073741824 | bytes 4194304 | tf_op jit(solution)/shard_map/feed_near_partner/pallas_call | solution.py:259
  171.5 6.0 %feed_far_partner.1 = bf16[256,1024]{1,0:T(8,128)(2,1)} custom-call(s32[2]{0:T(128)} %pad_add_fusion.place_ref.refs_0_, bf16[256,1024]{1,0:T(8,128)(2,1)} %copy-done.5, f32[256,1024]{1,0:T(8,128)} %feed_near_partner.1.refs_2_, bf16[256,1024]{1,0:T(8,128)(2,1)} %copy-done.3, bf16[256,1024]{1,0:T(8,128)(2,1)} %copy-done.1, bf16[256,1024]{1,0:T(8,128)(2,1)} %copy-done.2, ...), custom_call_target="tpu_custom_call" | custom-call | flops 1073741824 | bytes 4194304 | tf_op jit(solution)/shard_map/feed_far_partner/pallas_call | solution.py:302
  178.1 6.2 %feed_far_own.1.near_ref = f32[256,1024]{1,0:T(8,128)} custom-call(s32[2]{0:T(128)} %pad_add_fusion.place_ref.refs_0_, bf16[256,1024]{1,0:T(8,128)(2,1)} %first_norm.1.rows_ref.refs_1_.normed_ref, f32[256,1024]{1,0:T(8,128)} %feed_near_own.1.refs_2_, bf16[256,1024]{1,0:T(8,128)(2,1)} %copy-done.3, bf16[256,1024]{1,0:T(8,128)(2,1)} %copy-done.1, ...), custom_call_target="tpu_custom_call" | custom-call | flops 1073741824 | bytes 4194304 | tf_op jit(solution)/shard_map/feed_far_own/pallas_call | solution.py:302
  184.2 7.4 %collective-permute-done.28.far_ref = bf16[256,1024]{1,0:T(8,128)(2,1)S(1)} collective-permute-done((bf16[256,1024]{1,0:T(8,128)(2,1)}, bf16[256,1024]{1,0:T(8,128)(2,1)S(1)}, u32[]{:S(2)}, u32[]{:S(2)}) %collective-permute-start.28) | collective-permute-done | bytes 524320 | tf_op jit(solution)/shard_map/ppermute | solution.py:29
  192.5 2.8 %finish.1 = bf16[256,1024]{1,0:T(8,128)(2,1)} custom-call(bf16[256,1024]{1,0:T(8,128)(2,1)} %first_norm.1.rows_ref.refs_1_.normed_ref, f32[256,1024]{1,0:T(8,128)} %feed_far_own.1.near_ref, bf16[256,1024]{1,0:T(8,128)(2,1)} %copy-done.12, f32[1,1024]{1,0:T(1,128)} %bitcast.133, f32[1,1024]{1,0:T(1,128)} %bitcast.134), custom_call_target="tpu_custom_call" | custom-call | tf_op jit(solution)/shard_map/finish/pallas_call | solution.py:325
  (108 shorter events, 23.8 us)
Async XLA Ops:
  7.2 125.6 %all-gather.4.cloned.1.call-start = ((), (), s32[]{:S(2)}) async-start(), calls=%async_computation | async-start | bytes 2359296 | tf_op jit(solution)/shard_map/all_gather | solution.py:461
  24.5 25.5 %collective-permute-start = (bf16[256,1024]{1,0:T(8,128)(2,1)}, bf16[256,1024]{1,0:T(8,128)(2,1)S(1)}, u32[]{:S(2)}, u32[]{:S(2)}) collective-permute-start(bf16[256,1024]{1,0:T(8,128)(2,1)} %hidden_ref.1), channel_id=1, source_target_pairs={{0,1},{1,2},{2,3},{4,5},{5,6},{6,7},{8,9},{9,10},{10,11},{12,13},{... | collective-permute-start | bytes 1572872 | tf_op jit(solution)/shard_map/ppermute | solution.py:454
  28.5 22.2 %collective-permute-start.6 = (bf16[256,1024]{1,0:T(8,128)(2,1)}, bf16[256,1024]{1,0:T(8,128)(2,1)S(1)}, u32[]{:S(2)}, u32[]{:S(2)}) collective-permute-start(bf16[256,1024]{1,0:T(8,128)(2,1)} %hidden_ref.1), channel_id=1, source_target_pairs={{3,2},{2,1},{1,0},{7,6},{6,5},{5,4},{11,10},{10,9},{9,8},{15,14},{... | collective-permute-start | bytes 1572872 | tf_op jit(solution)/shard_map/ppermute | solution.py:455
  29.8 10.9 %collective-permute-start.1 = (bf16[2,1024]{1,0:T(2,128)(2,1)}, bf16[2,1024]{1,0:T(2,128)(2,1)S(1)}, u32[]{:S(2)}, u32[]{:S(2)}) collective-permute-start(bf16[2,1024]{1,0:T(2,128)(2,1)} %param.24), channel_id=1, source_target_pairs={{0,1},{1,0},{2,3},{3,2},{4,5},{5,4},{6,7},{7,6},{8,9},{9,8},{10,11... | collective-permute-start | bytes 12296 | tf_op jit(solution)/shard_map/ppermute | solution.py:29
  32.5 8.9 %collective-permute-start.2 = (bf16[2,1024]{1,0:T(2,128)(2,1)}, bf16[2,1024]{1,0:T(2,128)(2,1)S(1)}, u32[]{:S(2)}, u32[]{:S(2)}) collective-permute-start(bf16[2,1024]{1,0:T(2,128)(2,1)} %param.24), channel_id=1, source_target_pairs={{0,2},{1,3},{2,0},{3,1},{4,6},{5,7},{6,4},{7,5},{8,10},{9,11},{10,... | collective-permute-start | bytes 12296 | tf_op jit(solution)/shard_map/ppermute | solution.py:29
  35.0 7.7 %collective-permute-start.3 = (bf16[2,1024]{1,0:T(2,128)(2,1)}, bf16[2,1024]{1,0:T(2,128)(2,1)S(1)}, u32[]{:S(2)}, u32[]{:S(2)}) collective-permute-start(bf16[2,1024]{1,0:T(2,128)(2,1)} %param.24), channel_id=1, source_target_pairs={{0,3},{1,2},{2,1},{3,0},{4,7},{5,6},{6,5},{7,4},{8,11},{9,10},{10,... | collective-permute-start | bytes 12296 | tf_op jit(solution)/shard_map/ppermute | solution.py:29
  50.0 24.6 %copy-start.17 = (bf16[256,1024]{1,0:T(8,128)(2,1)}, bf16[256,1024]{1,0:T(8,128)(2,1)S(1)}, u32[]{:S(2)}) copy-start(bf16[256,1024]{1,0:T(8,128)(2,1)S(1)} %collective-permute-done.refs_1_) | copy-start | bytes 1572868
  50.0 2.0 collective-permute-start.4
  50.8 12.7 %collective-permute-start.7 = (bf16[256,1024]{1,0:T(8,128)(2,1)S(1)}, bf16[256,1024]{1,0:T(8,128)(2,1)S(1)}, u32[]{:S(2)}, u32[]{:S(2)}) collective-permute-start(bf16[256,1024]{1,0:T(8,128)(2,1)S(1)} %collective-permute-done.6.refs_4_), channel_id=1, source_target_pairs={{2,1},{1,0},{6,5},{5,4},{10,9},{9,8},{14,13},{13,12},{18,17},{17,1... | collective-permute-start | bytes 1572872 | tf_op jit(solution)/shard_map/ppermute | solution.py:455
  52.1 14.4 %collective-permute-start.5 = (bf16[256,1024]{1,0:T(8,128)(2,1)S(1)}, bf16[256,1024]{1,0:T(8,128)(2,1)S(1)}, u32[]{:S(2)}, u32[]{:S(2)}) collective-permute-start(bf16[256,1024]{1,0:T(8,128)(2,1)S(1)} %collective-permute-done.4.refs_2_), channel_id=1, source_target_pairs={{2,3},{6,7},{10,11},{14,15},{18,19},{22,23},{26,27},{30,31}} | collective-permute-start | bytes 1572872 | tf_op jit(solution)/shard_map/ppermute | solution.py:454
  63.5 11.2 %collective-permute-start.8 = (bf16[256,1024]{1,0:T(8,128)(2,1)S(1)}, bf16[256,1024]{1,0:T(8,128)(2,1)}, u32[]{:S(2)}, u32[]{:S(2)}) collective-permute-start(bf16[256,1024]{1,0:T(8,128)(2,1)S(1)} %collective-permute-done.7.refs_5_), channel_id=1, source_target_pairs={{1,0},{5,4},{9,8},{13,12},{17,16},{21,20},{25,24},{29,28}} | collective-permute-start | bytes 1572872 | tf_op jit(solution)/shard_map/ppermute | solution.py:455
  80.6 3.5 %collective-permute-start.10 = (bf16[256,512]{1,0:T(8,128)(2,1)}, bf16[256,512]{1,0:T(8,128)(2,1)S(1)}, u32[]{:S(2)}, u32[]{:S(2)}) collective-permute-start(bf16[256,512]{1,0:T(8,128)(2,1)} %get-tuple-element.29), channel_id=1, source_target_pairs={{0,4},{4,8},{8,12},{12,16},{16,20},{20,24},{24,28},{1,5},{5,9},{9,... | collective-permute-start | bytes 786440 | tf_op jit(solution)/shard_map/ppermute | solution.py:473
  82.0 5.4 %collective-permute-start.11 = (bf16[256,512]{1,0:T(8,128)(2,1)}, bf16[256,512]{1,0:T(8,128)(2,1)S(1)}, u32[]{:S(2)}, u32[]{:S(2)}) collective-permute-start(bf16[256,512]{1,0:T(8,128)(2,1)} %get-tuple-element.31), channel_id=1, source_target_pairs={{4,0},{8,4},{12,8},{16,12},{20,16},{24,20},{28,24},{5,1},{9,5},{13... | collective-permute-start | bytes 786440 | tf_op jit(solution)/shard_map/ppermute | solution.py:474
  83.5 25.8 %collective-permute-start.9 = (bf16[256,1024]{1,0:T(8,128)(2,1)S(1)}, bf16[256,1024]{1,0:T(8,128)(2,1)S(1)}, u32[]{:S(2)}, u32[]{:S(2)}) collective-permute-start(bf16[256,1024]{1,0:T(8,128)(2,1)S(1)} %pad_maximum_fusion), channel_id=1, source_target_pairs={{0,2},{1,3},{2,0},{3,1},{4,6},{5,7},{6,4},{7,5},{8,10},{9,11},{10,... | collective-permute-start | bytes 1572872 | tf_op jit(solution)/shard_map/ppermute | solution.py:29
  109.3 33.2 %copy-start.3 = (bf16[256,1024]{1,0:T(8,128)(2,1)}, bf16[256,1024]{1,0:T(8,128)(2,1)S(1)}, u32[]{:S(2)}) copy-start(bf16[256,1024]{1,0:T(8,128)(2,1)S(1)} %collective-permute-done.9.refs_3_) | copy-start | bytes 1572868
  109.3 15.6 %collective-permute-start.19 = (bf16[256,1024]{1,0:T(8,128)(2,1)S(1)}, bf16[256,1024]{1,0:T(8,128)(2,1)S(1)}, u32[]{:S(2)}, u32[]{:S(2)}) collective-permute-start(bf16[256,1024]{1,0:T(8,128)(2,1)S(1)} %collective-permute-done.9.refs_3_), channel_id=1, source_target_pairs={{0,8},{4,12},{8,0},{12,4},{16,24},{20,28},{24,16},{28,20},{1,9},{5... | collective-permute-start | bytes 1572872 | tf_op jit(solution)/shard_map/ppermute | solution.py:29
  112.8 27.5 %collective-permute-start.20 = (bf16[256,1024]{1,0:T(8,128)(2,1)S(1)}, bf16[256,1024]{1,0:T(8,128)(2,1)S(1)}, u32[]{:S(2)}, u32[]{:S(2)}) collective-permute-start(bf16[256,1024]{1,0:T(8,128)(2,1)S(1)} %collective-permute-done.9.refs_3_), channel_id=1, source_target_pairs={{0,16},{4,20},{8,24},{12,28},{16,0},{20,4},{24,8},{28,12},{1,17},{... | collective-permute-start | bytes 1572872 | tf_op jit(solution)/shard_map/ppermute | solution.py:29
  119.9 7.3 %collective-permute-start.12 = (bf16[256,256]{1,0:T(8,128)(2,1)}, bf16[256,256]{1,0:T(8,128)(2,1)S(1)}, u32[]{:S(2)}, u32[]{:S(2)}) collective-permute-start(bf16[256,256]{1,0:T(8,128)(2,1)} %get-tuple-element.37), channel_id=1, source_target_pairs={{0,1},{1,0},{2,3},{3,2},{4,5},{5,4},{6,7},{7,6},{8,9},{9,8},{10,11... | collective-permute-start | bytes 393224 | tf_op jit(solution)/shard_map/ppermute | solution.py:29
  120.0 12.7 %collective-permute-start.13 = (bf16[256,256]{1,0:T(8,128)(2,1)S(1)}, bf16[256,256]{1,0:T(8,128)(2,1)S(1)}, u32[]{:S(2)}, u32[]{:S(2)}) collective-permute-start(bf16[256,256]{1,0:T(8,128)(2,1)S(1)} %copy-done.25), channel_id=1, source_target_pairs={{0,2},{1,3},{2,0},{3,1},{4,6},{5,7},{6,4},{7,5},{8,10},{9,11},{10,... | collective-permute-start | bytes 393224 | tf_op jit(solution)/shard_map/ppermute | solution.py:29
  121.1 11.7 %collective-permute-start.14 = (bf16[256,256]{1,0:T(8,128)(2,1)S(1)}, bf16[256,256]{1,0:T(8,128)(2,1)S(1)}, u32[]{:S(2)}, u32[]{:S(2)}) collective-permute-start(bf16[256,256]{1,0:T(8,128)(2,1)S(1)} %copy-done.24), channel_id=1, source_target_pairs={{0,3},{1,2},{2,1},{3,0},{4,7},{5,6},{6,5},{7,4},{8,11},{9,10},{10,... | collective-permute-start | bytes 393224 | tf_op jit(solution)/shard_map/ppermute | solution.py:29
  124.9 17.6 %collective-permute-start.22 = (bf16[128,1024]{1,0:T(8,128)(2,1)S(1)}, bf16[128,1024]{1,0:T(8,128)(2,1)S(1)}, u32[]{:S(2)}, u32[]{:S(2)}) collective-permute-start(bf16[128,1024]{1,0:T(8,128)(2,1)S(1)} %slice.75), channel_id=1, source_target_pairs={{0,16},{4,20},{8,24},{12,28},{16,0},{20,4},{24,8},{28,12},{1,17},{... | collective-permute-start | bytes 786440 | tf_op jit(solution)/shard_map/ppermute | solution.py:29
  138.1 25.0 %collective-permute-start.15 = (bf16[256,1024]{1,0:T(8,128)(2,1)}, bf16[256,1024]{1,0:T(8,128)(2,1)S(1)}, u32[]{:S(2)}, u32[]{:S(2)}) collective-permute-start(bf16[256,1024]{1,0:T(8,128)(2,1)} %first_norm.1.rows_ref.refs_1_.normed_ref), channel_id=1, source_target_pairs={{0,1},{1,0},{2,3},{3,2},{4,5},{5,4},{6,7},{7,6},{8,9},{9,8},{10,11... | collective-permute-start | bytes 1572872 | tf_op jit(solution)/shard_map/ppermute | solution.py:29
  140.3 6.9 %collective-permute-start.21 = (bf16[128,1024]{1,0:T(8,128)(2,1)S(1)}, bf16[128,1024]{1,0:T(8,128)(2,1)S(1)}, u32[]{:S(2)}, u32[]{:S(2)}) collective-permute-start(bf16[128,1024]{1,0:T(8,128)(2,1)S(1)} %slice.74), channel_id=1, source_target_pairs={{0,8},{4,12},{8,0},{12,4},{16,24},{20,28},{24,16},{28,20},{1,9},{5... | collective-permute-start | bytes 786440 | tf_op jit(solution)/shard_map/ppermute | solution.py:29
  142.0 27.5 %collective-permute-start.25 = (bf16[256,1024]{1,0:T(8,128)(2,1)S(1)}, bf16[256,1024]{1,0:T(8,128)(2,1)S(1)}, u32[]{:S(2)}, u32[]{:S(2)}) collective-permute-start(bf16[256,1024]{1,0:T(8,128)(2,1)S(1)} %collective-permute-done.20.refs_5_), channel_id=1, source_target_pairs={{0,4},{4,0},{8,12},{12,8},{16,20},{20,16},{24,28},{28,24},{1,5},{5... | collective-permute-start | bytes 1572872 | tf_op jit(solution)/shard_map/ppermute | solution.py:29
  142.0 27.5 %collective-permute-start.24 = (bf16[256,1024]{1,0:T(8,128)(2,1)S(1)}, bf16[256,1024]{1,0:T(8,128)(2,1)S(1)}, u32[]{:S(2)}, u32[]{:S(2)}) collective-permute-start(bf16[256,1024]{1,0:T(8,128)(2,1)S(1)} %collective-permute-done.19.refs_4_), channel_id=1, source_target_pairs={{0,4},{4,0},{8,12},{12,8},{16,20},{20,16},{24,28},{28,24},{1,5},{5... | collective-permute-start | bytes 1572872 | tf_op jit(solution)/shard_map/ppermute | solution.py:29
  142.5 27.0 %collective-permute-start.23 = (bf16[256,1024]{1,0:T(8,128)(2,1)S(1)}, bf16[256,1024]{1,0:T(8,128)(2,1)S(1)}, u32[]{:S(2)}, u32[]{:S(2)}) collective-permute-start(bf16[256,1024]{1,0:T(8,128)(2,1)S(1)} %collective-permute-done.9.refs_3_), channel_id=1, source_target_pairs={{0,4},{4,0},{8,12},{12,8},{16,20},{20,16},{24,28},{28,24},{1,5},{5... | collective-permute-start | bytes 1572872 | tf_op jit(solution)/shard_map/ppermute | solution.py:29
  147.2 4.8 %collective-permute-start.16 = (f32[3,2,1024]{2,1,0:T(2,128)S(1)}, f32[3,2,1024]{2,1,0:T(2,128)S(1)}, u32[]{:S(2)}, u32[]{:S(2)}) collective-permute-start(f32[3,2,1024]{2,1,0:T(2,128)S(1)} %get-tuple-element.48), channel_id=1, source_target_pairs={{0,1},{1,0},{2,3},{3,2},{4,5},{5,4},{6,7},{7,6},{8,9},{9,8},{10,11... | collective-permute-start | bytes 73736 | tf_op jit(solution)/shard_map/ppermute | solution.py:29
  152.0 4.7 %collective-permute-start.17 = (f32[3,2,1024]{2,1,0:T(2,128)S(1)}, f32[3,2,1024]{2,1,0:T(2,128)S(1)}, u32[]{:S(2)}, u32[]{:S(2)}) collective-permute-start(f32[3,2,1024]{2,1,0:T(2,128)S(1)} %get-tuple-element.49), channel_id=1, source_target_pairs={{0,2},{1,3},{2,0},{3,1},{4,6},{5,7},{6,4},{7,5},{8,10},{9,11},{10,... | collective-permute-start | bytes 73736 | tf_op jit(solution)/shard_map/ppermute | solution.py:29
  156.7 6.4 %collective-permute-start.18 = (f32[3,2,1024]{2,1,0:T(2,128)S(1)}, f32[3,2,1024]{2,1,0:T(2,128)S(1)}, u32[]{:S(2)}, u32[]{:S(2)}) collective-permute-start(f32[3,2,1024]{2,1,0:T(2,128)S(1)} %get-tuple-element.50), channel_id=1, source_target_pairs={{0,3},{1,2},{2,1},{3,0},{4,7},{5,6},{6,5},{7,4},{8,11},{9,10},{10,... | collective-permute-start | bytes 73736 | tf_op jit(solution)/shard_map/ppermute | solution.py:29
  163.1 6.4 %collective-permute-start.27 = (bf16[128,1024]{1,0:T(8,128)(2,1)S(1)}, bf16[128,1024]{1,0:T(8,128)(2,1)S(1)}, u32[]{:S(2)}, u32[]{:S(2)}) collective-permute-start(bf16[128,1024]{1,0:T(8,128)(2,1)S(1)} %collective-permute-done.22.refs_7_), channel_id=1, source_target_pairs={{0,4},{4,0},{8,12},{12,8},{16,20},{20,16},{24,28},{28,24},{1,5},{5... | collective-permute-start | bytes 786440 | tf_op jit(solution)/shard_map/ppermute | solution.py:29
  163.2 6.3 %collective-permute-start.26 = (bf16[128,1024]{1,0:T(8,128)(2,1)S(1)}, bf16[128,1024]{1,0:T(8,128)(2,1)S(1)}, u32[]{:S(2)}, u32[]{:S(2)}) collective-permute-start(bf16[128,1024]{1,0:T(8,128)(2,1)S(1)} %collective-permute-done.21.refs_6_), channel_id=1, source_target_pairs={{0,4},{4,0},{8,12},{12,8},{16,20},{20,16},{24,28},{28,24},{1,5},{5... | collective-permute-start | bytes 786440 | tf_op jit(solution)/shard_map/ppermute | solution.py:29
  177.5 14.2 %collective-permute-start.28 = (bf16[256,1024]{1,0:T(8,128)(2,1)}, bf16[256,1024]{1,0:T(8,128)(2,1)S(1)}, u32[]{:S(2)}, u32[]{:S(2)}) collective-permute-start(bf16[256,1024]{1,0:T(8,128)(2,1)} %feed_far_partner.1), channel_id=1, source_target_pairs={{0,1},{1,0},{2,3},{3,2},{4,5},{5,4},{6,7},{7,6},{8,9},{9,8},{10,11... | collective-permute-start | bytes 1572872 | tf_op jit(solution)/shard_map/ppermute | solution.py:29
  (26 other events, 204.7 us)
Sparse Core Ops, SparseCore 0:
  24.7 29.4 all-gather.3

commit v4 on v3

--- a/solution.py
+++ b/solution.py
@@ -18,10 +18,12 @@
 LN_EPS = 1e-05
 BF16 = jnp.bfloat16
 F32 = jnp.float32
+STRIP = 32
 VMEM_LIMIT = 56 * 1024 * 1024
 ANY = pl.BlockSpec(memory_space=pl.ANY)
 VMEM = pl.BlockSpec(memory_space=pltpu.VMEM)
 SMEM = pl.BlockSpec(memory_space=pltpu.SMEM)
+SHORT = pl.CostEstimate(flops=1, bytes_accessed=1, transcendentals=0)
 
 
 def swapped(value, axis, flip):
@@ -65,20 +67,14 @@
         guarded(needed, copy.start)
     for needed, copy in copies:
         guarded(needed, copy.wait)
-    scale = 1.0 / math.sqrt(HD)
-    for block in range(steps + 1):
-        at = slice(block * count, (block + 1) * count)
-        rows = rows_ref[at]
-        query = jnp.dot(rows, weight_ref[0], preferred_element_type=F32) * scale
-        query_ref[at] = query.astype(BF16)
-        keys = jnp.dot(rows, weight_ref[1], preferred_element_type=F32).astype(BF16)
-        values = jnp.dot(rows, weight_ref[2], preferred_element_type=F32).astype(BF16)
-        keyval_ref[at, :width] = keys
-        keyval_ref[at, width:] = values
-        for edge, edge_ref in ((0, top_ref), (steps, bottom_ref)):
-            if block == edge:
-                edge_ref[:, :width] = keys
-                edge_ref[:, width:] = values
+    rows = rows_ref[...]
+    query = jnp.dot(rows, weight_ref[0], preferred_element_type=F32) * (1.0 / math.sqrt(HD))
+    query_ref[...] = query.astype(BF16)
+    for part in range(2):
+        at = slice(part * width, (part + 1) * width)
+        keyval_ref[:, at] = jnp.dot(rows, weight_ref[part + 1], preferred_element_type=F32).astype(BF16)
+    top_ref[...] = keyval_ref[:count]
+    bottom_ref[...] = keyval_ref[steps * count :]
 
 
 def project(place, weight, shards):
@@ -98,9 +94,7 @@
         out_specs=(VMEM,) * 4,
         scratch_shapes=[pltpu.VMEM((blocks * rows, width), BF16), pltpu.SemaphoreType.DMA((len(shards),))],
         compiler_params=pltpu.CompilerParams(vmem_limit_bytes=VMEM_LIMIT),
-        cost_estimate=pl.CostEstimate(
-            flops=6 * blocks * rows * width * heads_width, bytes_accessed=6 * width * heads_width, transcendentals=0
-        ),
+        cost_estimate=SHORT,
         name="project",
     )(place, weight, *shards)
 
@@ -116,30 +110,34 @@
     return jnp.where((key >= low) & (key < high), 0.0, NEG_FILL)
 
 
-def attend(query, keyval_ref, bias):
+def attend(query, keyval_ref, bias_ref, scores_ref, weights_ref, out_ref):
     count, width = query.shape
     lane = lax.broadcasted_iota(jnp.int32, (count, 2 * HD), 1)
-    pairs = []
     for start in range(0, width, 2 * HD):
-        keys = keyval_ref[:, start : start + 2 * HD]
         values = keyval_ref[:, width + start : width + start + 2 * HD]
         halves = []
         for side in range(2):
+            head = start // HD + side
             inside = (lane < HD) if side == 0 else (lane >= HD)
             only = jnp.where(inside, query[:, start : start + 2 * HD], jnp.zeros((), BF16))
-            scores = lax.dot_general(only, keys, (((1,), (1,)), ((), ())), preferred_element_type=F32)
-            scores = scores + bias
-            highest = jnp.max(scores, axis=1, keepdims=True)
-            weights = jnp.exp(scores - highest)
-            total = jnp.sum(weights, axis=1, keepdims=True)
-            summed = jnp.dot(weights.astype(BF16), values, preferred_element_type=F32)
-            halves.append(summed / total)
-        pairs.append(jnp.where(lane < HD, halves[0], halves[1]).astype(BF16))
-    return jnp.concatenate(pairs, axis=1)
+            scores_ref[head] = lax.dot_general(
+                only, keyval_ref[:, start : start + 2 * HD], (((1,), (1,)), ((), ())), preferred_element_type=F32
+            )
+            totals = []
+            for row in range(0, count, STRIP):
+                at = slice(row, row + STRIP)
+                scores = scores_ref[head, at] + bias_ref[at]
+                weights = jnp.exp(scores - jnp.max(scores, axis=1, keepdims=True))
+                totals.append(jnp.sum(weights, axis=1, keepdims=True))
+                weights_ref[head, at] = weights.astype(BF16)
+            summed = jnp.dot(weights_ref[head], values, preferred_element_type=F32)
+            halves.append(summed / jnp.concatenate(totals, axis=0))
+        out_ref[:, start : start + 2 * HD] = jnp.where(lane < HD, halves[0], halves[1]).astype(BF16)
 
 
 def attend_kernel(flips, place_ref, starts_ref, ends_ref, query_ref, before_ref, keyval_ref, behind_ref, *refs):
-    outs, (window_ref, sems) = refs[: len(flips)], refs[len(flips) :]
+    outs = refs[: len(flips)]
+    window_ref, bias_ref, scores_ref, weights_ref, sems = refs[len(flips) :]
     tok, kv = place_ref[0], place_ref[1]
     count = outs[0].shape[0]
     blocks = query_ref.shape[0] // count
@@ -163,17 +161,16 @@
     for index, flip in enumerate(flips):
         block = kv ^ flip
         first = (tok * blocks + block) * count
-        bias = window_bias(first, count, starts_ref[...], ends_ref[...])
+        bias_ref[...] = window_bias(first, count, starts_ref[...], ends_ref[...])
         for owner, needed, copy in copies:
             if owner == index:
                 pl.when(needed)(copy.wait)
         query = query_ref[pl.ds(pl.multiple_of(block * count, count), count)]
-        outs[index][...] = attend(query, window_ref.at[index], bias)
+        attend(query, window_ref.at[index], bias_ref, scores_ref, weights_ref, outs[index])
 
 
 def attend_blocks(place, starts, ends, query, before, keyval, behind, rows, flips, name):
     heads_width = query.shape[1]
-    pairs = rows * 3 * rows * heads_width * len(flips)
     return pl.pallas_call(
         functools.partial(attend_kernel, flips),
         out_shape=tuple(jax.ShapeDtypeStruct((rows, heads_width), BF16) for _ in flips),
@@ -181,144 +178,155 @@
         out_specs=(VMEM,) * len(flips),
         scratch_shapes=[
             pltpu.VMEM((len(flips), 3 * rows, 2 * heads_width), BF16),
+            pltpu.VMEM((rows, 3 * rows), F32),
+            pltpu.VMEM((heads_width // HD, rows, 3 * rows), F32),
+            pltpu.VMEM((heads_width // HD, rows, 3 * rows), BF16),
             pltpu.SemaphoreType.DMA((len(flips), 3)),
         ],
         compiler_params=pltpu.CompilerParams(vmem_limit_bytes=VMEM_LIMIT),
-        cost_estimate=pl.CostEstimate(flops=32 * pairs, bytes_accessed=8 * rows * heads_width, transcendentals=0),
+        cost_estimate=SHORT,
         name=name,
     )(place, starts, ends, query, before, keyval, behind)
 
 
-def first_norm_kernel(place_ref, hidden_ref, out_ref, gain_ref, bias_ref, *refs):
-    parts, (normed_ref, all_ref, weight_ref, sems) = refs[:-4], refs[-4:]
-    kv = place_ref[1]
-    eighths, quarters, depth, width = out_ref.shape
-    copies = []
-    for index in range(eighths):
-        target = weight_ref.at[:, index * depth : (index + 1) * depth]
-        copies.append(pltpu.make_async_copy(out_ref.at[index], target, sems.at[index]))
+def first_norm_kernel(layout, place_ref, hidden_ref, own_out_ref, gain_ref, bias_ref, *refs):
+    parts, pieces = refs[: -5 - len(layout)], refs[-5 - len(layout) : -5]
+    normed_ref, all_ref, weight_ref, mixed_ref, sems = refs[-5:]
+    tok = place_ref[0]
+    quarters, heads_width, width = weight_ref.shape
+    copies = [pltpu.make_async_copy(own_out_ref, weight_ref.at[0], sems.at[0])]
+    for flips, piece in zip(layout, pieces):
+        for index, flip in enumerate(flips):
+            depth = piece.shape[2]
+            at = pl.multiple_of((tok ^ flip) * depth, depth)
+            target = weight_ref.at[1:quarters, pl.ds(at, depth)]
+            copies.append(pltpu.make_async_copy(piece.at[index], target, sems.at[len(copies)]))
     for copy in copies:
         copy.start()
-    heads_width = eighths * depth
     for flip, part_ref in enumerate(parts):
-        at = pl.multiple_of((kv ^ flip) * heads_width, heads_width)
-        all_ref[:, pl.ds(at, heads_width)] = part_ref[...]
+        all_ref[:, flip * heads_width : (flip + 1) * heads_width] = part_ref[...]
     for copy in copies:
         copy.wait()
     weight = weight_ref[...].reshape(quarters * heads_width, width)
-    projected = jnp.dot(all_ref[...], weight, preferred_element_type=F32)
-    mixed = hidden_ref[...].astype(F32) + projected
-    normed_ref[...] = normalized(mixed, gain_ref[...], bias_ref[...]).astype(BF16)
-
-
-def first_norm(place, hidden, out_pieces, gain, bias, parts):
+    mixed_ref[...] = jnp.dot(all_ref[...], weight, preferred_element_type=F32)
+    for row in range(0, hidden_ref.shape[0], STRIP):
+        at = slice(row, row + STRIP)
+        mixed = hidden_ref[at].astype(F32) + mixed_ref[at]
+        normed_ref[at] = normalized(mixed, gain_ref[...], bias_ref[...]).astype(BF16)
+
+
+def first_norm(place, hidden, own_out, gain, bias, parts, pieces):
     rows, width = hidden.shape
-    eighths, quarters, depth, _ = out_pieces.shape
+    heads_width = own_out.shape[0]
+    layout = tuple(flips for flips, _ in pieces)
     return pl.pallas_call(
-        first_norm_kernel,
+        functools.partial(first_norm_kernel, layout),
         out_shape=jax.ShapeDtypeStruct((rows, width), BF16),
-        in_specs=[SMEM, VMEM, ANY, VMEM, VMEM] + [VMEM] * len(parts),
+        in_specs=[SMEM, VMEM, ANY, VMEM, VMEM] + [VMEM] * len(parts) + [ANY] * len(pieces),
         out_specs=VMEM,
         scratch_shapes=[
             pltpu.VMEM((rows, width), BF16),
-            pltpu.VMEM((quarters, eighths * depth, width), BF16),
-            pltpu.SemaphoreType.DMA((eighths,)),
+            pltpu.VMEM((len(parts), heads_width, width), BF16),
+            pltpu.VMEM((rows, width), F32),
+            pltpu.SemaphoreType.DMA((1 + sum(len(flips) for flips in layout),)),
         ],
         compiler_params=pltpu.CompilerParams(vmem_limit_bytes=VMEM_LIMIT),
-        cost_estimate=pl.CostEstimate(
-            flops=2 * rows * width * width, bytes_accessed=2 * width * width, transcendentals=0
-        ),
+        cost_estimate=SHORT,
         name="first_norm",
-    )(place, hidden, out_pieces, gain, bias, *parts)
+    )(place, hidden, own_out, gain, bias, *parts, *[value for _, value in pieces])
 
 
 def gelu(values):
     return 0.5 * values * (1.0 + lax.erf(values * math.sqrt(0.5)))
 
 
-def feed_into(total_ref, rows, up_ref, down_ref):
-    chunk = 512
-    for at in range(0, up_ref.shape[1], chunk):
-        units = gelu(jnp.dot(rows, up_ref[:, at : at + chunk], preferred_element_type=F32)).astype(BF16)
-        total_ref[...] += jnp.dot(units, down_ref[at : at + chunk, :], preferred_element_type=F32)
-
-
-def feed_near_kernel(rows_ref, up_ref, down_ref, sum_ref):
-    sum_ref[...] = jnp.zeros_like(sum_ref)
-    feed_into(sum_ref, rows_ref[...], up_ref, down_ref)
-
-
-def feed_cost(count, width, units):
-    return pl.CostEstimate(
-        flops=4 * count * width * units, bytes_accessed=4 * width * units, transcendentals=count * units
-    )
-
-
-def feed_near(rows, up_weight, down_weight, name):
-    count, width = rows.shape
-    return pl.pallas_call(
-        feed_near_kernel,
-        out_shape=jax.ShapeDtypeStruct((count, width), F32),
-        in_specs=[VMEM] * 3,
-        out_specs=VMEM,
-        compiler_params=pltpu.CompilerParams(vmem_limit_bytes=VMEM_LIMIT),
-        cost_estimate=feed_cost(count, width, up_weight.shape[1]),
-        name=name,
-    )(rows, up_weight, down_weight)
-
-
-def feed_far_kernel(layout, *refs):
+def feed_kernel(layout, *refs):
     count = len(layout)
-    place_ref, rows_ref, near_ref = refs[:3]
-    pieces = refs[3 : 3 + count]
-    sum_ref, up_ref, down_ref, total_ref, sems = refs[3 + count :]
+    place_ref, rows_ref, up_near_ref, down_near_ref = refs[:4]
+    pieces = refs[4 : 4 + count]
+    sum_ref, up_ref, down_ref, wide_ref, units_ref, total_ref, near_sems, sems = refs[4 + count :]
     tok = place_ref[0]
     block = 128
-    copies = []
+    chunk = wide_ref.shape[2]
+    chunks = up_ref.shape[2] // chunk
+    near = []
+    for index in range(chunks):
+        at = slice(index * chunk, (index + 1) * chunk)
+        near.append(
+            (
+                pltpu.make_async_copy(up_near_ref.at[:, at], up_ref.at[0, :, at], near_sems.at[0, index]),
+                pltpu.make_async_copy(down_near_ref.at[at], down_ref.at[0, at], near_sems.at[1, index]),
+            )
+        )
+    far = []
     for (flip, part), piece in zip(layout, pieces):
-        at = pl.multiple_of((tok ^ flip) * block, block)
+        at = pl.ds(pl.multiple_of((tok ^ flip) * block, block), block)
         if part in (None, 0):
-            copies.append(pltpu.make_async_copy(piece.at[0:block], up_ref.at[pl.ds(at, block)], sems.at[len(copies)]))
+            far.append(pltpu.make_async_copy(piece.at[0:block], up_ref.at[1, at], sems.at[len(far)]))
         if part in (None, 1):
             shift = block if part is None else 0
-            copies.append(
-                pltpu.make_async_copy(
-                    piece.at[shift : shift + block], down_ref.at[pl.ds(at, block)], sems.at[len(copies)]
-                )
-            )
-    for copy in copies:
+            far.append(pltpu.make_async_copy(piece.at[shift : shift + block], down_ref.at[1, at], sems.at[len(far)]))
+    for pair in near:
+        for copy in pair:
+            copy.start()
+    for copy in far:
         copy.start()
-    total_ref[...] = near_ref[...]
-    for copy in copies:
-        copy.wait()
-    feed_into(total_ref, rows_ref[...], up_ref, down_ref)
-    sum_ref[...] = total_ref[...].astype(sum_ref.dtype)
-
-
-def feed_far(place, rows, near, pieces, units, dtype, name):
+    rows = rows_ref[...]
+    for side in range(2):
+        for index in range(chunks):
+            at = slice(index * chunk, (index + 1) * chunk)
+            slot = index % 2
+            if side == 0:
+                near[index][0].wait()
+            elif index == 0:
+                for copy in far:
+                    copy.wait()
+            wide_ref[slot] = jnp.dot(rows, up_ref[side, :, at], preferred_element_type=F32)
+            for row in range(0, rows.shape[0], STRIP):
+                strip = slice(row, row + STRIP)
+                units_ref[slot, strip] = gelu(wide_ref[slot, strip]).astype(BF16)
+            if side == 0:
+                near[index][1].wait()
+            product = jnp.dot(units_ref[slot], down_ref[side, at], preferred_element_type=F32)
+            if side == 0 and index == 0:
+                total_ref[...] = product
+            elif side == 1 and index == chunks - 1:
+                sum_ref[...] = (total_ref[...] + product).astype(sum_ref.dtype)
+            else:
+                total_ref[...] += product
+
+
+def feed(place, rows, up_weight, down_weight, pieces, dtype, name):
     count, width = rows.shape
+    units = up_weight.shape[1]
+    chunk = 512
     layout = tuple((flip, part) for flip, part, _ in pieces)
     copies = sum(2 if part is None else 1 for _, part in layout)
     return pl.pallas_call(
-        functools.partial(feed_far_kernel, layout),
+        functools.partial(feed_kernel, layout),
         out_shape=jax.ShapeDtypeStruct((count, width), dtype),
-        in_specs=[SMEM] + [VMEM] * 2 + [ANY] * len(pieces),
+        in_specs=[SMEM, VMEM, ANY, ANY] + [ANY] * len(pieces),
         out_specs=VMEM,
         scratch_shapes=[
-            pltpu.VMEM((width, units), BF16),
-            pltpu.VMEM((units, width), BF16),
+            pltpu.VMEM((2, width, units), BF16),
+            pltpu.VMEM((2, units, width), BF16),
+            pltpu.VMEM((2, count, chunk), F32),
+            pltpu.VMEM((2, count, chunk), BF16),
             pltpu.VMEM((count, width), F32),
+            pltpu.SemaphoreType.DMA((2, units // chunk)),
             pltpu.SemaphoreType.DMA((copies,)),
         ],
         compiler_params=pltpu.CompilerParams(vmem_limit_bytes=VMEM_LIMIT),
-        cost_estimate=feed_cost(count, width, units),
+        cost_estimate=SHORT,
         name=name,
-    )(place, rows, near, *[value for _, _, value in pieces])
+    )(place, rows, up_weight, down_weight, *[value for _, _, value in pieces])
 
 
 def finish_kernel(normed_ref, near_ref, far_ref, gain_ref, bias_ref, out_ref):
-    mixed = normed_ref[...].astype(F32) + near_ref[...] + far_ref[...].astype(F32)
-    out_ref[...] = normalized(mixed, gain_ref[...], bias_ref[...]).astype(out_ref.dtype)
+    for row in range(0, normed_ref.shape[0], STRIP):
+        at = slice(row, row + STRIP)
+        mixed = normed_ref[at].astype(F32) + near_ref[at] + far_ref[at].astype(F32)
+        out_ref[at] = normalized(mixed, gain_ref[...], bias_ref[...]).astype(out_ref.dtype)
 
 
 def finish(normed, near, far, gain, bias):
@@ -390,7 +398,7 @@
         out_specs=pl.BlockSpec((3, requests, width), lambda i: (0, 0, 0)),
         scratch_shapes=[state, state, state],
         compiler_params=pltpu.CompilerParams(vmem_limit_bytes=VMEM_LIMIT),
-        cost_estimate=pl.CostEstimate(flops=0, bytes_accessed=kv_cache.size * 2, transcendentals=0),
+        cost_estimate=SHORT,
         name="decode",
     )(slots, filled, queries, kv_cache)
 
@@ -456,9 +464,12 @@
         from_below.append(rising)
         from_above.append(falling)
         if step == 1:
-            rising, falling = after(rising, partial), after(falling, partial)
-
-    out_pieces = lax.all_gather(lax.all_gather(eighth(out_weight), "kv"), "tok")
+            out_part = after(eighth(out_weight), rising, falling)
+            out_here = jnp.stack([swapped(out_part, "kv", flip) for flip in range(1, kvs)])
+        if step == 2:
+            rising, falling = after(rising, partial, out_here), after(falling, partial, out_here)
+    out_x, out_y = swapped(out_here, "tok", 2), swapped(out_here, "tok", 4)
+    out_far = swapped(after(out_y, rising), "tok", 2)
 
     feed_part = jnp.concatenate([eighth(up_weight), eighth(down_weight)], axis=0)
     feed_here = swapped(after(feed_part, from_below[1], from_above[1]), "kv", 2)
@@ -475,28 +486,28 @@
     window = (place, starts, ends, query, before, keyval, behind, rows)
     parts = [None] * kvs
     parts[3], parts[2] = attend_blocks(*window, (3, 2), "attend_far")
+    out_all = jnp.stack([out_here, out_x, out_y, after(out_far, parts[3])])
+    out_core = swapped(out_all, "tok", 1)
     feed_here = after(feed_here, parts[3], parts[2])
     parts[3], parts[2] = swapped(parts[3], "kv", 3), swapped(parts[2], "kv", 2)
     feed_x, feed_y = swapped(feed_here, "tok", 2), swapped(feed_here, "tok", 4)
     window = (place, starts, ends, after(query, feed_here), before, keyval, behind, rows)
     parts[1], parts[0] = attend_blocks(*window, (1, 0), "attend_near")
-    parts[1] = swapped(parts[1], "kv", 1)
     half = feed_here.shape[0] // 2
     far_up = swapped(after(feed_y, parts[0])[:half], "tok", 2)
     far_down = swapped(after(feed_x, parts[0])[half:], "tok", 4)
-    normed = first_norm(place, hidden_in, out_pieces, ln1_gain[None, :], ln1_bias[None, :], parts)
+    parts[1] = swapped(parts[1], "kv", 1)
+    out_pieces = [((0, 2, 4, 6), out_all), ((1, 3, 5, 7), out_core)]
+    normed = first_norm(place, hidden_in, out_weight, ln1_gain[None, :], ln1_bias[None, :], parts, out_pieces)
 
     partner = swapped(normed, "kv", 1)
     held = [(0, None, feed_here), (2, None, feed_x), (4, None, feed_y), (6, 0, far_up), (6, 1, far_down)]
     feed_pieces = held + [(flip ^ 1, part, swapped(after(value, normed), "tok", 1)) for flip, part, value in held]
-    units = up_weight.shape[1]
-    near = feed_near(normed, up_weight, down_weight, "feed_near_own")
     dec_out = merged_partials(exchanged_partials(after(partial, normed), dec_query.shape[0]))
-    partner = after(partner, near, dec_out)
-    near_away = feed_near(partner, up_weight, down_weight, "feed_near_partner")
-    away = feed_far(place, partner, near_away, feed_pieces, units, BF16, "feed_far_partner")
+    partner = after(partner, dec_out)
+    away = feed(place, partner, up_weight, down_weight, feed_pieces, BF16, "feed_partner")
     arrived = swapped(away, "kv", 1)
-    mine = feed_far(place, after(normed, away), near, feed_pieces, units, F32, "feed_far_own")
+    mine = feed(place, after(normed, away), up_weight, down_weight, feed_pieces, F32, "feed_own")
     prefill_out = finish(normed, mine, arrived, ln2_gain[None, :], ln2_bias[None, :])
 
     return prefill_out, dec_out

time: 203 us -> 167 us (0.82)
  blocking collectives: 16.3 us -> 0 us
  between operations: 14.4 us -> 1.05 us
  starting transfers between devices: 35.9 us -> 45.2 us
  waiting for transfers between devices: 69.7 us -> 61.4 us
  Pallas kernels: 55 us -> 47 us
    all_gather x1 -> x0, blocking collectives: 16.3 us -> none  [routed_body(): out_pieces = lax.all_gather(lax.all_gather(eighth(out_weight), 'kv'), 'tok')]
    ppermute x21 -> x28, starting transfers between devices: 23.9 us -> 32.3 us  [swapped(): return lax.ppermute(value, axis, [(i, i ^ flip) for i in range(count)])]
    pallas_call x5 -> x3, Pallas kernels: 26.8 us -> 18.7 us  [the longest x2 14 us: feed(): pl.pallas_call(functools.partial(feed_kernel, layout), out_shape=jax.Shap...]
    ppermute x3, waiting for transfers between devices: 18.8 us -> 12.3 us  [routed_body(): lax.ppermute(falling, 'kv', [(kvs - 1 - i, kvs - 2 - i) for i in links])]
    ppermute x3, waiting for transfers between devices: 0.01 us -> 4.98 us  [routed_body(): rising = lax.ppermute(rising, 'kv', [(i, i + 1) for i in links])]
    ppermute x21 -> x28, waiting for transfers between devices: 47.7 us -> 44.1 us  [swapped(): return lax.ppermute(value, axis, [(i, i ^ flip) for i in range(count)])]
    ppermute x1, waiting for transfers between devices: 3.17 us -> 0.01 us  [routed_body(): behind = lax.ppermute(top, 'tok', [(i + 1, i) for i in range(toks - 1)])]
    unnamed x56 -> x60, local copies, waits for them, and re-layouts: 5.16 us -> 5.11 us
  transfers between devices with their start and end apart: 30 -> 36, of which waited for: 14 -> 15; matrix products, arithmetic and copies ran while one was open for 3% -> 4% of each run, Pallas kernels for 23% -> 22%
where the time goes in v4:
time: 167 us; the launch traced here: 166 us
  waiting for transfers between devices  61.4 us (37%)
  Pallas kernels  47 us (28%)
  starting transfers between devices  45.2 us (27%)
  local copies, waits for them, and re-layouts  7.09 us (4%)
  other arithmetic  4.62 us (3%)
    ppermute x28, waiting for transfers between devices, swapped(): return lax.ppermute(value, axis, [(i, i ^ flip) for i in range(count)])  44.1 us
    ppermute x28, starting transfers between devices, swapped(): return lax.ppermute(value, axis, [(i, i ^ flip) for i in range(count)])  32.3 us
    pallas_call x2, Pallas kernels, feed(): pl.pallas_call(functools.partial(feed_kernel, layout), out_shape=jax.Shap...  14 us
    pallas_call x2, Pallas kernels, attend_blocks(): pl.pallas_call(functools.partial(attend_kernel, flips), out_shape=tuple((...  13.8 us
    ppermute x3, waiting for transfers between devices, routed_body(): lax.ppermute(falling, 'kv', [(kvs - 1 - i, kvs - 2 - i) for i in links])  12.3 us
    ppermute x3, starting transfers between devices, routed_body(): rising = lax.ppermute(rising, 'kv', [(i, i + 1) for i in links])  6.34 us
    pallas_call x1, Pallas kernels, project(): pl.pallas_call(project_kernel, out_shape=(jax.ShapeDtypeStruct((blocks *...  5.96 us
    pallas_call x1, Pallas kernels, decode(): pl.pallas_call(decode_kernel, grid=(pieces,), out_shape=jax.ShapeDtypeStr...  5.89 us
  transfers between devices with their start and end apart: 36, of which 15 were waited for; matrix products, arithmetic and copies ran while one was open for 4% of the time, Pallas kernels for 22%

profile of v4, /device:TPU:0, one launch (start us, length us, event | category | flops | bytes accessed | tf_op | source)
XLA Modules:
  0.0 166.4 jit_solution(15892672615911758820)
XLA Ops:
  0.6 5.0 %collective-permute-start = (bf16[256,1024]{1,0:T(8,128)(2,1)}, bf16[256,1024]{1,0:T(8,128)(2,1)S(1)}, u32[]{:S(2)}, u32[]{:S(2)}) collective-permute-start(bf16[256,1024]{1,0:T(8,128)(2,1)} %hidden_ref.1), channel_id=1, source_target_pairs={{0,1},{1,2},{2,3},{4,5},{5,6},{6,7},{8,9},{9,10},{10,11},{12,13},{... | collective-permute-start | bytes 1572872 | tf_op jit(solution)/shard_map/ppermute | solution.py:462
  6.9 2.7 %collective-permute-start.2 = (bf16[2,1024]{1,0:T(2,128)(2,1)}, bf16[2,1024]{1,0:T(2,128)(2,1)S(1)}, u32[]{:S(2)}, u32[]{:S(2)}) collective-permute-start(bf16[2,1024]{1,0:T(2,128)(2,1)} %param.24), channel_id=1, source_target_pairs={{0,1},{1,0},{2,3},{3,2},{4,5},{5,4},{6,7},{7,6},{8,9},{9,8},{10,11... | collective-permute-start | bytes 12296 | tf_op jit(solution)/shard_map/ppermute | solution.py:31
  9.6 2.6 %collective-permute-start.3 = (bf16[2,1024]{1,0:T(2,128)(2,1)}, bf16[2,1024]{1,0:T(2,128)(2,1)S(1)}, u32[]{:S(2)}, u32[]{:S(2)}) collective-permute-start(bf16[2,1024]{1,0:T(2,128)(2,1)} %param.24), channel_id=1, source_target_pairs={{0,2},{1,3},{2,0},{3,1},{4,6},{5,7},{6,4},{7,5},{8,10},{9,11},{10,... | collective-permute-start | bytes 12296 | tf_op jit(solution)/shard_map/ppermute | solution.py:31
  12.2 5.0 %collective-permute-done.refs_1_ = bf16[256,1024]{1,0:T(8,128)(2,1)S(1)} collective-permute-done((bf16[256,1024]{1,0:T(8,128)(2,1)}, bf16[256,1024]{1,0:T(8,128)(2,1)S(1)}, u32[]{:S(2)}, u32[]{:S(2)}) %collective-permute-start) | collective-permute-done | bytes 524320 | tf_op jit(solution)/shard_map/ppermute | solution.py:462
  17.9 3.3 %collective-permute-done.5.refs_4_ = bf16[256,1024]{1,0:T(8,128)(2,1)S(1)} collective-permute-done((bf16[256,1024]{1,0:T(8,128)(2,1)}, bf16[256,1024]{1,0:T(8,128)(2,1)S(1)}, u32[]{:S(2)}, u32[]{:S(2)}) %collective-permute-start.5) | collective-permute-done | bytes 524320 | tf_op jit(solution)/shard_map/ppermute | solution.py:463
  24.6 4.2 %collective-permute-start.7 = (bf16[32,1024]{1,0:T(8,128)(2,1)S(1)}, bf16[32,1024]{1,0:T(8,128)(2,1)S(1)}, u32[]{:S(2)}, u32[]{:S(2)}) collective-permute-start(bf16[32,1024]{1,0:T(8,128)(2,1)S(1)} %constant_dynamic-slice_fusion.2), channel_id=1, source_target_pairs={{0,2},{1,3},{2,0},{3,1},{4,6},{5,7},{6,4},{7,5},{8,10},{9,11},{10,... | collective-permute-start | bytes 196616 | tf_op jit(solution)/shard_map/ppermute | solution.py:31
  30.9 5.9 %decode.1 = f32[3,8,1024]{2,1,0:T(8,128)} custom-call(s32[6]{0:T(128)} %fusion.17.slot_ref, s32[6]{0:T(128)} %bitcast.150, f32[8,1024]{1,0:T(8,128)} %maximum_convert_fusion.query_ref, bf16[2,1,6,128,1024]{4,3,2,1,0:T(8,128)(2,1)} %cache_ref.1), custom_call_target="tpu_custom_call" | custom-call | flops 1 | bytes 1 | tf_op jit(solution)/shard_map/decode/pallas_call | solution.py:388
  36.8 4.9 %collective-permute-done.7 = bf16[32,1024]{1,0:T(8,128)(2,1)S(1)} collective-permute-done((bf16[32,1024]{1,0:T(8,128)(2,1)S(1)}, bf16[32,1024]{1,0:T(8,128)(2,1)S(1)}, u32[]{:S(2)}, u32[]{:S(2)}) %collective-permute-start.7) | collective-permute-done | bytes 65568 | tf_op jit(solution)/shard_map/ppermute | solution.py:31
  45.0 1.6 collective-permute-start.19
  47.6 9.0 %collective-permute-done.11.refs_6_ = bf16[256,1024]{1,0:T(8,128)(2,1)S(1)} collective-permute-done((bf16[256,1024]{1,0:T(8,128)(2,1)S(1)}, bf16[256,1024]{1,0:T(8,128)(2,1)S(1)}, u32[]{:S(2)}, u32[]{:S(2)}) %collective-permute-start.11) | collective-permute-done | bytes 524320 | tf_op jit(solution)/shard_map/ppermute | solution.py:463
  57.4 6.0 %project.1 = (bf16[1024,256]{1,0:T(8,128)(2,1)}, bf16[1024,512]{1,0:T(8,128)(2,1)}, bf16[256,512]{1,0:T(8,128)(2,1)}, bf16[256,512]{1,0:T(8,128)(2,1)}) custom-call(s32[2]{0:T(128)} %pad_add_fusion.place_ref.refs_0_, bf16[3,1024,256]{2,1,0:T(8,128)(2,1)} %bitcast.137, bf16[256,1024]{1,0:T(8,128)(2,1)} %hidden_ref.1, bf16[256,1024]{1,0:T(8,128)(2,1)} %copy-done.16, ...), custom_call_target="tpu_custom_call" | custom-call | flops 1 | bytes 1 | tf_op jit(solution)/shard_map/project/pallas_call | solution.py:85
  66.3 4.5 %collective-permute-start.18 = (bf16[3,32,1024]{2,1,0:T(8,128)(2,1)S(1)}, bf16[3,32,1024]{2,1,0:T(8,128)(2,1)S(1)}, u32[]{:S(2)}, u32[]{:S(2)}) collective-permute-start(bf16[3,32,1024]{2,1,0:T(8,128)(2,1)S(1)} %get-tuple-element.55), channel_id=1, source_target_pairs={{0,8},{4,12},{8,0},{12,4},{16,24},{20,28},{24,16},{28,20},{1,9},{5... | collective-permute-start | bytes 589832 | tf_op jit(solution)/shard_map/ppermute | solution.py:31
  72.2 6.9 %attend_far.1 = (bf16[256,256]{1,0:T(8,128)(2,1)}, bf16[256,256]{1,0:T(8,128)(2,1)}) custom-call(s32[2]{0:T(128)} %pad_add_fusion.place_ref.refs_0_, s32[1,48]{1,0:T(1,128)} %subtract_bitcast_fusion.starts_ref, s32[1,48]{1,0:T(1,128)} %bitcast.148, bf16[1024,256]{1,0:T(8,128)(2,1)} %get-tuple-element.39.query_ref, bf16[256,512]{1,0:T(8,128)(2,1)} %copy-done.9, ...), custom_call_target="tpu_custom_call" | custom-call | flops 1 | bytes 1 | tf_op jit(solution)/shard_map/attend_far/pallas_call | solution.py:174
  79.1 4.4 %collective-permute-done.20 = bf16[3,32,1024]{2,1,0:T(8,128)(2,1)S(1)} collective-permute-done((bf16[3,32,1024]{2,1,0:T(8,128)(2,1)S(1)}, bf16[3,32,1024]{2,1,0:T(8,128)(2,1)S(1)}, u32[]{:S(2)}, u32[]{:S(2)}) %collective-permute-start.20) | collective-permute-done | bytes 196640 | tf_op jit(solution)/shard_map/ppermute | solution.py:31
  83.6 1.9 %collective-permute-start.21 = (bf16[4,3,32,1024]{3,2,1,0:T(8,128)(2,1)S(1)}, bf16[4,3,32,1024]{3,2,1,0:T(8,128)(2,1)S(1)}, u32[]{:S(2)}, u32[]{:S(2)}) collective-permute-start(bf16[4,3,32,1024]{3,2,1,0:T(8,128)(2,1)S(1)} %pad_maximum_fusion.refs_4_), channel_id=1, source_target_pairs={{0,4},{4,0},{8,12},{12,8},{16,20},{20,16},{24,28},{28,24},{1,5},{5... | collective-permute-start | bytes 2359304 | tf_op jit(solution)/shard_map/ppermute | solution.py:31
  85.5 2.4 %collective-permute-start.26 = (bf16[256,1024]{1,0:T(8,128)(2,1)S(1)}, bf16[256,1024]{1,0:T(8,128)(2,1)S(1)}, u32[]{:S(2)}, u32[]{:S(2)}) collective-permute-start(bf16[256,1024]{1,0:T(8,128)(2,1)S(1)} %collective-permute-done.12.refs_4_), channel_id=1, source_target_pairs={{0,8},{4,12},{8,0},{12,4},{16,24},{20,28},{24,16},{28,20},{1,9},{5... | collective-permute-start | bytes 1572872 | tf_op jit(solution)/shard_map/ppermute | solution.py:31
  87.9 6.9 %attend_near.1 = (bf16[256,256]{1,0:T(8,128)(2,1)}, bf16[256,256]{1,0:T(8,128)(2,1)}) custom-call(s32[2]{0:T(128)} %pad_add_fusion.place_ref.refs_0_, s32[1,48]{1,0:T(1,128)} %subtract_bitcast_fusion.starts_ref, s32[1,48]{1,0:T(1,128)} %bitcast.149, bf16[1024,256]{1,0:T(8,128)(2,1)} %get-tuple-element.39.query_ref, bf16[256,512]{1,0:T(8,128)(2,1)} %copy-done.9, ...), custom_call_target="tpu_custom_call" | custom-call | flops 1 | bytes 1 | tf_op jit(solution)/shard_map/attend_near/pallas_call | solution.py:174
  94.9 5.1 %collective-permute-done.26.refs_5_ = bf16[256,1024]{1,0:T(8,128)(2,1)S(1)} collective-permute-done((bf16[256,1024]{1,0:T(8,128)(2,1)S(1)}, bf16[256,1024]{1,0:T(8,128)(2,1)S(1)}, u32[]{:S(2)}, u32[]{:S(2)}) %collective-permute-start.26) | collective-permute-done | bytes 524320 | tf_op jit(solution)/shard_map/ppermute | solution.py:31
  101.4 1.9 %collective-permute-start.29 = (bf16[128,1024]{1,0:T(8,128)(2,1)S(1)}, bf16[128,1024]{1,0:T(8,128)(2,1)S(1)}, u32[]{:S(2)}, u32[]{:S(2)}) collective-permute-start(bf16[128,1024]{1,0:T(8,128)(2,1)S(1)} %slice.75), channel_id=1, source_target_pairs={{0,16},{4,20},{8,24},{12,28},{16,0},{20,4},{24,8},{28,12},{1,17},{... | collective-permute-start | bytes 786440 | tf_op jit(solution)/shard_map/ppermute | solution.py:31
  103.4 4.5 %collective-permute-done.16.refs_2_ = bf16[256,256]{1,0:T(8,128)(2,1)S(1)} collective-permute-done((bf16[256,256]{1,0:T(8,128)(2,1)S(1)}, bf16[256,256]{1,0:T(8,128)(2,1)S(1)}, u32[]{:S(2)}, u32[]{:S(2)}) %collective-permute-start.16) | collective-permute-done | bytes 131104 | tf_op jit(solution)/shard_map/ppermute | solution.py:31
  108.8 4.7 %first_norm.1.refs_1_.normed_ref = bf16[256,1024]{1,0:T(8,128)(2,1)} custom-call(s32[2]{0:T(128)} %pad_add_fusion.place_ref.refs_0_, bf16[256,1024]{1,0:T(8,128)(2,1)} %hidden_ref.1, bf16[256,1024]{1,0:T(8,128)(2,1)} %own_out_ref.1, f32[1,1024]{1,0:T(1,128)} %bitcast.146, f32[1,1024]{1,0:T(1,128)} %bitcast.147, bf16[256,256]{1,0:T(8,128)(2,1)} %get-tuple-element.40.refs_0_, ...), custom_call_target="tpu_custom_call" | custom-call | flops 1 | bytes 1 | tf_op jit(solution)/shard_map/first_norm/pallas_call | solution.py:222
  113.5 2.3 %collective-permute-start.22 = (bf16[256,1024]{1,0:T(8,128)(2,1)}, bf16[256,1024]{1,0:T(8,128)(2,1)S(1)}, u32[]{:S(2)}, u32[]{:S(2)}) collective-permute-start(bf16[256,1024]{1,0:T(8,128)(2,1)} %first_norm.1.refs_1_.normed_ref), channel_id=1, source_target_pairs={{0,1},{1,0},{2,3},{3,2},{4,5},{5,4},{6,7},{7,6},{8,9},{9,8},{10,11... | collective-permute-start | bytes 1572872 | tf_op jit(solution)/shard_map/ppermute | solution.py:31
  117.2 5.6 %collective-permute-done.28.refs_7_ = bf16[128,1024]{1,0:T(8,128)(2,1)S(1)} collective-permute-done((bf16[128,1024]{1,0:T(8,128)(2,1)S(1)}, bf16[128,1024]{1,0:T(8,128)(2,1)S(1)}, u32[]{:S(2)}, u32[]{:S(2)}) %collective-permute-start.28) | collective-permute-done | bytes 262176 | tf_op jit(solution)/shard_map/ppermute | solution.py:31
  123.1 4.5 %collective-permute-done.23 = f32[3,2,1024]{2,1,0:T(2,128)S(1)} collective-permute-done((f32[3,2,1024]{2,1,0:T(2,128)S(1)}, f32[3,2,1024]{2,1,0:T(2,128)S(1)}, u32[]{:S(2)}, u32[]{:S(2)}) %collective-permute-start.23) | collective-permute-done | bytes 24608 | tf_op jit(solution)/shard_map/ppermute | solution.py:31
  127.6 2.3 %collective-permute-start.24 = (f32[3,2,1024]{2,1,0:T(2,128)S(1)}, f32[3,2,1024]{2,1,0:T(2,128)S(1)}, u32[]{:S(2)}, u32[]{:S(2)}) collective-permute-start(f32[3,2,1024]{2,1,0:T(2,128)S(1)} %get-tuple-element.57), channel_id=1, source_target_pairs={{0,2},{1,3},{2,0},{3,1},{4,6},{5,7},{6,4},{7,5},{8,10},{9,11},{10,... | collective-permute-start | bytes 73736 | tf_op jit(solution)/shard_map/ppermute | solution.py:31
  129.9 2.4 %collective-permute-done.24 = f32[3,2,1024]{2,1,0:T(2,128)S(1)} collective-permute-done((f32[3,2,1024]{2,1,0:T(2,128)S(1)}, f32[3,2,1024]{2,1,0:T(2,128)S(1)}, u32[]{:S(2)}, u32[]{:S(2)}) %collective-permute-start.24) | collective-permute-done | bytes 24608 | tf_op jit(solution)/shard_map/ppermute | solution.py:31
  132.3 2.0 %collective-permute-start.25 = (f32[3,2,1024]{2,1,0:T(2,128)S(1)}, f32[3,2,1024]{2,1,0:T(2,128)S(1)}, u32[]{:S(2)}, u32[]{:S(2)}) collective-permute-start(f32[3,2,1024]{2,1,0:T(2,128)S(1)} %get-tuple-element.58), channel_id=1, source_target_pairs={{0,3},{1,2},{2,1},{3,0},{4,7},{5,6},{6,5},{7,4},{8,11},{9,10},{10,... | collective-permute-start | bytes 73736 | tf_op jit(solution)/shard_map/ppermute | solution.py:31
  134.4 3.6 %collective-permute-done.25 = f32[3,2,1024]{2,1,0:T(2,128)S(1)} collective-permute-done((f32[3,2,1024]{2,1,0:T(2,128)S(1)}, f32[3,2,1024]{2,1,0:T(2,128)S(1)}, u32[]{:S(2)}, u32[]{:S(2)}) %collective-permute-start.25) | collective-permute-done | bytes 24608 | tf_op jit(solution)/shard_map/ppermute | solution.py:31
  141.7 6.9 %feed_partner.1 = bf16[256,1024]{1,0:T(8,128)(2,1)} custom-call(s32[2]{0:T(128)} %pad_add_fusion.place_ref.refs_0_, bf16[256,1024]{1,0:T(8,128)(2,1)} %copy-done.14, bf16[1024,1024]{1,0:T(8,128)(2,1)} %refs_2_.3, bf16[1024,1024]{1,0:T(8,128)(2,1)} %refs_3_.3, bf16[256,1024]{1,0:T(8,128)(2,1)} %copy-done.3, bf16[256,1024]{1,0:T(8,128)(2,1)} %copy-done, ...), custom_call_target="tpu_custom_call" | custom-call | flops 1 | bytes 1 | tf_op jit(solution)/shard_map/feed_partner/pallas_call | solution.py:305
  148.7 7.1 %feed_own.1.near_ref = f32[256,1024]{1,0:T(8,128)} custom-call(s32[2]{0:T(128)} %pad_add_fusion.place_ref.refs_0_, bf16[256,1024]{1,0:T(8,128)(2,1)} %first_norm.1.refs_1_.normed_ref, bf16[1024,1024]{1,0:T(8,128)(2,1)} %refs_2_.3, bf16[1024,1024]{1,0:T(8,128)(2,1)} %refs_3_.3, bf16[256,1024]{1,0:T(8,128)(2,1)} %copy-done.3, bf16[256,1024]{1,0:T(8,128)(2,1)} %copy-done, ...), custom_call_target="tpu_custom_call" | custom-call | flops 1 | bytes 1 | tf_op jit(solution)/shard_map/feed_own/pallas_call | solution.py:305
  155.8 7.0 %collective-permute-done.35.far_ref = bf16[256,1024]{1,0:T(8,128)(2,1)S(1)} collective-permute-done((bf16[256,1024]{1,0:T(8,128)(2,1)}, bf16[256,1024]{1,0:T(8,128)(2,1)S(1)}, u32[]{:S(2)}, u32[]{:S(2)}) %collective-permute-start.35) | collective-permute-done | bytes 524320 | tf_op jit(solution)/shard_map/ppermute | solution.py:31
  163.6 2.8 %finish.1 = bf16[256,1024]{1,0:T(8,128)(2,1)} custom-call(bf16[256,1024]{1,0:T(8,128)(2,1)} %first_norm.1.refs_1_.normed_ref, f32[256,1024]{1,0:T(8,128)} %feed_own.1.near_ref, bf16[256,1024]{1,0:T(8,128)(2,1)} %copy-done.15, f32[1,1024]{1,0:T(1,128)} %bitcast.144, f32[1,1024]{1,0:T(1,128)} %bitcast.145), custom_call_target="tpu_custom_call" | custom-call | tf_op jit(solution)/shard_map/finish/pallas_call | solution.py:333
  (122 shorter events, 25.7 us)
Async XLA Ops:
  0.6 16.5 %collective-permute-start = (bf16[256,1024]{1,0:T(8,128)(2,1)}, bf16[256,1024]{1,0:T(8,128)(2,1)S(1)}, u32[]{:S(2)}, u32[]{:S(2)}) collective-permute-start(bf16[256,1024]{1,0:T(8,128)(2,1)} %hidden_ref.1), channel_id=1, source_target_pairs={{0,1},{1,2},{2,3},{4,5},{5,6},{6,7},{8,9},{9,10},{10,11},{12,13},{... | collective-permute-start | bytes 1572872 | tf_op jit(solution)/shard_map/ppermute | solution.py:462
  5.6 15.6 %collective-permute-start.5 = (bf16[256,1024]{1,0:T(8,128)(2,1)}, bf16[256,1024]{1,0:T(8,128)(2,1)S(1)}, u32[]{:S(2)}, u32[]{:S(2)}) collective-permute-start(bf16[256,1024]{1,0:T(8,128)(2,1)} %hidden_ref.1), channel_id=1, source_target_pairs={{3,2},{2,1},{1,0},{7,6},{6,5},{5,4},{11,10},{10,9},{9,8},{15,14},{... | collective-permute-start | bytes 1572872 | tf_op jit(solution)/shard_map/ppermute | solution.py:463
  6.9 17.7 %collective-permute-start.2 = (bf16[2,1024]{1,0:T(2,128)(2,1)}, bf16[2,1024]{1,0:T(2,128)(2,1)S(1)}, u32[]{:S(2)}, u32[]{:S(2)}) collective-permute-start(bf16[2,1024]{1,0:T(2,128)(2,1)} %param.24), channel_id=1, source_target_pairs={{0,1},{1,0},{2,3},{3,2},{4,5},{5,4},{6,7},{7,6},{8,9},{9,8},{10,11... | collective-permute-start | bytes 12296 | tf_op jit(solution)/shard_map/ppermute | solution.py:31
  9.6 19.1 %collective-permute-start.3 = (bf16[2,1024]{1,0:T(2,128)(2,1)}, bf16[2,1024]{1,0:T(2,128)(2,1)S(1)}, u32[]{:S(2)}, u32[]{:S(2)}) collective-permute-start(bf16[2,1024]{1,0:T(2,128)(2,1)} %param.24), channel_id=1, source_target_pairs={{0,2},{1,3},{2,0},{3,1},{4,6},{5,7},{6,4},{7,5},{8,10},{9,11},{10,... | collective-permute-start | bytes 12296 | tf_op jit(solution)/shard_map/ppermute | solution.py:31
  12.2 17.4 %collective-permute-start.4 = (bf16[2,1024]{1,0:T(2,128)(2,1)}, bf16[2,1024]{1,0:T(2,128)(2,1)S(1)}, u32[]{:S(2)}, u32[]{:S(2)}) collective-permute-start(bf16[2,1024]{1,0:T(2,128)(2,1)} %param.24), channel_id=1, source_target_pairs={{0,3},{1,2},{2,1},{3,0},{4,7},{5,6},{6,5},{7,4},{8,11},{9,10},{10,... | collective-permute-start | bytes 12296 | tf_op jit(solution)/shard_map/ppermute | solution.py:31
  17.2 24.6 %collective-permute-start.1 = (bf16[256,1024]{1,0:T(8,128)(2,1)S(1)}, bf16[256,1024]{1,0:T(8,128)(2,1)S(1)}, u32[]{:S(2)}, u32[]{:S(2)}) collective-permute-start(bf16[256,1024]{1,0:T(8,128)(2,1)S(1)} %collective-permute-done.refs_1_), channel_id=1, source_target_pairs={{1,2},{2,3},{5,6},{6,7},{9,10},{10,11},{13,14},{14,15},{17,18},{18... | collective-permute-start | bytes 1572872 | tf_op jit(solution)/shard_map/ppermute | solution.py:462
  21.2 21.3 %collective-permute-start.10 = (bf16[256,1024]{1,0:T(8,128)(2,1)S(1)}, bf16[256,1024]{1,0:T(8,128)(2,1)S(1)}, u32[]{:S(2)}, u32[]{:S(2)}) collective-permute-start(bf16[256,1024]{1,0:T(8,128)(2,1)S(1)} %collective-permute-done.5.refs_4_), channel_id=1, source_target_pairs={{2,1},{1,0},{6,5},{5,4},{10,9},{9,8},{14,13},{13,12},{18,17},{17,1... | collective-permute-start | bytes 1572872 | tf_op jit(solution)/shard_map/ppermute | solution.py:463
  24.6 17.2 %collective-permute-start.7 = (bf16[32,1024]{1,0:T(8,128)(2,1)S(1)}, bf16[32,1024]{1,0:T(8,128)(2,1)S(1)}, u32[]{:S(2)}, u32[]{:S(2)}) collective-permute-start(bf16[32,1024]{1,0:T(8,128)(2,1)S(1)} %constant_dynamic-slice_fusion.2), channel_id=1, source_target_pairs={{0,2},{1,3},{2,0},{3,1},{4,6},{5,7},{6,4},{7,5},{8,10},{9,11},{10,... | collective-permute-start | bytes 196616 | tf_op jit(solution)/shard_map/ppermute | solution.py:31
  28.7 13.0 %collective-permute-start.8 = (bf16[32,1024]{1,0:T(8,128)(2,1)S(1)}, bf16[32,1024]{1,0:T(8,128)(2,1)S(1)}, u32[]{:S(2)}, u32[]{:S(2)}) collective-permute-start(bf16[32,1024]{1,0:T(8,128)(2,1)S(1)} %constant_dynamic-slice_fusion.2), channel_id=1, source_target_pairs={{0,3},{1,2},{2,1},{3,0},{4,7},{5,6},{6,5},{7,4},{8,11},{9,10},{10,... | collective-permute-start | bytes 196616 | tf_op jit(solution)/shard_map/ppermute | solution.py:31
  29.6 12.1 %collective-permute-start.6 = (bf16[32,1024]{1,0:T(8,128)(2,1)S(1)}, bf16[32,1024]{1,0:T(8,128)(2,1)S(1)}, u32[]{:S(2)}, u32[]{:S(2)}) collective-permute-start(bf16[32,1024]{1,0:T(8,128)(2,1)S(1)} %constant_dynamic-slice_fusion.2), channel_id=1, source_target_pairs={{0,1},{1,0},{2,3},{3,2},{4,5},{5,4},{6,7},{7,6},{8,9},{9,8},{10,11... | collective-permute-start | bytes 196616 | tf_op jit(solution)/shard_map/ppermute | solution.py:31
  41.8 5.8 %collective-permute-start.9 = (bf16[256,1024]{1,0:T(8,128)(2,1)S(1)}, bf16[256,1024]{1,0:T(8,128)(2,1)S(1)}, u32[]{:S(2)}, u32[]{:S(2)}) collective-permute-start(bf16[256,1024]{1,0:T(8,128)(2,1)S(1)} %collective-permute-done.1.refs_2_), channel_id=1, source_target_pairs={{2,3},{6,7},{10,11},{14,15},{18,19},{22,23},{26,27},{30,31}} | collective-permute-start | bytes 1572872 | tf_op jit(solution)/shard_map/ppermute | solution.py:462
  42.5 14.1 %collective-permute-start.11 = (bf16[256,1024]{1,0:T(8,128)(2,1)S(1)}, bf16[256,1024]{1,0:T(8,128)(2,1)S(1)}, u32[]{:S(2)}, u32[]{:S(2)}) collective-permute-start(bf16[256,1024]{1,0:T(8,128)(2,1)S(1)} %collective-permute-done.10.refs_5_), channel_id=1, source_target_pairs={{1,0},{5,4},{9,8},{13,12},{17,16},{21,20},{25,24},{29,28}} | collective-permute-start | bytes 1572872 | tf_op jit(solution)/shard_map/ppermute | solution.py:463
  45.0 25.9 %collective-permute-start.19 = (bf16[3,32,1024]{2,1,0:T(8,128)(2,1)S(1)}, bf16[3,32,1024]{2,1,0:T(8,128)(2,1)S(1)}, u32[]{:S(2)}, u32[]{:S(2)}) collective-permute-start(bf16[3,32,1024]{2,1,0:T(8,128)(2,1)S(1)} %get-tuple-element.55), channel_id=1, source_target_pairs={{0,16},{4,20},{8,24},{12,28},{16,0},{20,4},{24,8},{28,12},{1,17},{... | collective-permute-start | bytes 589832 | tf_op jit(solution)/shard_map/ppermute | solution.py:31
  47.2 38.3 %collective-permute-start.12 = (bf16[256,1024]{1,0:T(8,128)(2,1)S(1)}, bf16[256,1024]{1,0:T(8,128)(2,1)S(1)}, u32[]{:S(2)}, u32[]{:S(2)}) collective-permute-start(bf16[256,1024]{1,0:T(8,128)(2,1)S(1)} %pad_maximum_fusion.1), channel_id=1, source_target_pairs={{0,2},{1,3},{2,0},{3,1},{4,6},{5,7},{6,4},{7,5},{8,10},{9,11},{10,... | collective-permute-start | bytes 1572872 | tf_op jit(solution)/shard_map/ppermute | solution.py:31
  63.4 8.0 %collective-permute-start.13 = (bf16[256,512]{1,0:T(8,128)(2,1)}, bf16[256,512]{1,0:T(8,128)(2,1)S(1)}, u32[]{:S(2)}, u32[]{:S(2)}) collective-permute-start(bf16[256,512]{1,0:T(8,128)(2,1)} %get-tuple-element.33), channel_id=1, source_target_pairs={{0,4},{4,8},{8,12},{12,16},{16,20},{20,24},{24,28},{1,5},{5,9},{9,... | collective-permute-start | bytes 786440 | tf_op jit(solution)/shard_map/ppermute | solution.py:484
  64.7 6.7 %collective-permute-start.14 = (bf16[256,512]{1,0:T(8,128)(2,1)}, bf16[256,512]{1,0:T(8,128)(2,1)S(1)}, u32[]{:S(2)}, u32[]{:S(2)}) collective-permute-start(bf16[256,512]{1,0:T(8,128)(2,1)} %get-tuple-element.35), channel_id=1, source_target_pairs={{4,0},{8,4},{12,8},{16,12},{20,16},{24,20},{28,24},{5,1},{9,5},{13... | collective-permute-start | bytes 786440 | tf_op jit(solution)/shard_map/ppermute | solution.py:485
  66.3 17.2 %collective-permute-start.18 = (bf16[3,32,1024]{2,1,0:T(8,128)(2,1)S(1)}, bf16[3,32,1024]{2,1,0:T(8,128)(2,1)S(1)}, u32[]{:S(2)}, u32[]{:S(2)}) collective-permute-start(bf16[3,32,1024]{2,1,0:T(8,128)(2,1)S(1)} %get-tuple-element.55), channel_id=1, source_target_pairs={{0,8},{4,12},{8,0},{12,4},{16,24},{20,28},{24,16},{28,20},{1,9},{5... | collective-permute-start | bytes 589832 | tf_op jit(solution)/shard_map/ppermute | solution.py:31
  70.8 12.7 %collective-permute-start.20 = (bf16[3,32,1024]{2,1,0:T(8,128)(2,1)S(1)}, bf16[3,32,1024]{2,1,0:T(8,128)(2,1)S(1)}, u32[]{:S(2)}, u32[]{:S(2)}) collective-permute-start(bf16[3,32,1024]{2,1,0:T(8,128)(2,1)S(1)} %collective-permute-done.19), channel_id=1, source_target_pairs={{0,8},{4,12},{8,0},{12,4},{16,24},{20,28},{24,16},{28,20},{1,9},{5... | collective-permute-start | bytes 589832 | tf_op jit(solution)/shard_map/ppermute | solution.py:31
  83.6 24.2 %collective-permute-start.21 = (bf16[4,3,32,1024]{3,2,1,0:T(8,128)(2,1)S(1)}, bf16[4,3,32,1024]{3,2,1,0:T(8,128)(2,1)S(1)}, u32[]{:S(2)}, u32[]{:S(2)}) collective-permute-start(bf16[4,3,32,1024]{3,2,1,0:T(8,128)(2,1)S(1)} %pad_maximum_fusion.refs_4_), channel_id=1, source_target_pairs={{0,4},{4,0},{8,12},{12,8},{16,20},{20,16},{24,28},{28,24},{1,5},{5... | collective-permute-start | bytes 2359304 | tf_op jit(solution)/shard_map/ppermute | solution.py:31
  85.5 14.6 %collective-permute-start.26 = (bf16[256,1024]{1,0:T(8,128)(2,1)S(1)}, bf16[256,1024]{1,0:T(8,128)(2,1)S(1)}, u32[]{:S(2)}, u32[]{:S(2)}) collective-permute-start(bf16[256,1024]{1,0:T(8,128)(2,1)S(1)} %collective-permute-done.12.refs_4_), channel_id=1, source_target_pairs={{0,8},{4,12},{8,0},{12,4},{16,24},{20,28},{24,16},{28,20},{1,9},{5... | collective-permute-start | bytes 1572872 | tf_op jit(solution)/shard_map/ppermute | solution.py:31
  87.9 27.9 %collective-permute-start.27 = (bf16[256,1024]{1,0:T(8,128)(2,1)S(1)}, bf16[256,1024]{1,0:T(8,128)(2,1)S(1)}, u32[]{:S(2)}, u32[]{:S(2)}) collective-permute-start(bf16[256,1024]{1,0:T(8,128)(2,1)S(1)} %collective-permute-done.12.refs_4_), channel_id=1, source_target_pairs={{0,16},{4,20},{8,24},{12,28},{16,0},{20,4},{24,8},{28,12},{1,17},{... | collective-permute-start | bytes 1572872 | tf_op jit(solution)/shard_map/ppermute | solution.py:31
  94.8 6.6 %collective-permute-start.15 = (bf16[256,256]{1,0:T(8,128)(2,1)}, bf16[256,256]{1,0:T(8,128)(2,1)S(1)}, u32[]{:S(2)}, u32[]{:S(2)}) collective-permute-start(bf16[256,256]{1,0:T(8,128)(2,1)} %get-tuple-element.41), channel_id=1, source_target_pairs={{0,1},{1,0},{2,3},{3,2},{4,5},{5,4},{6,7},{7,6},{8,9},{9,8},{10,11... | collective-permute-start | bytes 393224 | tf_op jit(solution)/shard_map/ppermute | solution.py:31
  94.9 13.0 %collective-permute-start.16 = (bf16[256,256]{1,0:T(8,128)(2,1)S(1)}, bf16[256,256]{1,0:T(8,128)(2,1)S(1)}, u32[]{:S(2)}, u32[]{:S(2)}) collective-permute-start(bf16[256,256]{1,0:T(8,128)(2,1)S(1)} %copy-done.28), channel_id=1, source_target_pairs={{0,2},{1,3},{2,0},{3,1},{4,6},{5,7},{6,4},{7,5},{8,10},{9,11},{10,... | collective-permute-start | bytes 393224 | tf_op jit(solution)/shard_map/ppermute | solution.py:31
  100.1 7.8 %collective-permute-start.17 = (bf16[256,256]{1,0:T(8,128)(2,1)S(1)}, bf16[256,256]{1,0:T(8,128)(2,1)S(1)}, u32[]{:S(2)}, u32[]{:S(2)}) collective-permute-start(bf16[256,256]{1,0:T(8,128)(2,1)S(1)} %copy-done.27), channel_id=1, source_target_pairs={{0,3},{1,2},{2,1},{3,0},{4,7},{5,6},{6,5},{7,4},{8,11},{9,10},{10,... | collective-permute-start | bytes 393224 | tf_op jit(solution)/shard_map/ppermute | solution.py:31
  101.4 15.7 %collective-permute-start.29 = (bf16[128,1024]{1,0:T(8,128)(2,1)S(1)}, bf16[128,1024]{1,0:T(8,128)(2,1)S(1)}, u32[]{:S(2)}, u32[]{:S(2)}) collective-permute-start(bf16[128,1024]{1,0:T(8,128)(2,1)S(1)} %slice.75), channel_id=1, source_target_pairs={{0,16},{4,20},{8,24},{12,28},{16,0},{20,4},{24,8},{28,12},{1,17},{... | collective-permute-start | bytes 786440 | tf_op jit(solution)/shard_map/ppermute | solution.py:31
  113.5 24.5 %collective-permute-start.22 = (bf16[256,1024]{1,0:T(8,128)(2,1)}, bf16[256,1024]{1,0:T(8,128)(2,1)S(1)}, u32[]{:S(2)}, u32[]{:S(2)}) collective-permute-start(bf16[256,1024]{1,0:T(8,128)(2,1)} %first_norm.1.refs_1_.normed_ref), channel_id=1, source_target_pairs={{0,1},{1,0},{2,3},{3,2},{4,5},{5,4},{6,7},{7,6},{8,9},{9,8},{10,11... | collective-permute-start | bytes 1572872 | tf_op jit(solution)/shard_map/ppermute | solution.py:31
  115.8 7.0 %collective-permute-start.28 = (bf16[128,1024]{1,0:T(8,128)(2,1)S(1)}, bf16[128,1024]{1,0:T(8,128)(2,1)S(1)}, u32[]{:S(2)}, u32[]{:S(2)}) collective-permute-start(bf16[128,1024]{1,0:T(8,128)(2,1)S(1)} %slice.74), channel_id=1, source_target_pairs={{0,8},{4,12},{8,0},{12,4},{16,24},{20,28},{24,16},{28,20},{1,9},{5... | collective-permute-start | bytes 786440 | tf_op jit(solution)/shard_map/ppermute | solution.py:31
  116.6 23.3 %collective-permute-start.32 = (bf16[256,1024]{1,0:T(8,128)(2,1)S(1)}, bf16[256,1024]{1,0:T(8,128)(2,1)S(1)}, u32[]{:S(2)}, u32[]{:S(2)}) collective-permute-start(bf16[256,1024]{1,0:T(8,128)(2,1)S(1)} %collective-permute-done.27.refs_6_), channel_id=1, source_target_pairs={{0,4},{4,0},{8,12},{12,8},{16,20},{20,16},{24,28},{28,24},{1,5},{5... | collective-permute-start | bytes 1572872 | tf_op jit(solution)/shard_map/ppermute | solution.py:31
  116.6 23.3 %collective-permute-start.31 = (bf16[256,1024]{1,0:T(8,128)(2,1)S(1)}, bf16[256,1024]{1,0:T(8,128)(2,1)S(1)}, u32[]{:S(2)}, u32[]{:S(2)}) collective-permute-start(bf16[256,1024]{1,0:T(8,128)(2,1)S(1)} %collective-permute-done.26.refs_5_), channel_id=1, source_target_pairs={{0,4},{4,0},{8,12},{12,8},{16,20},{20,16},{24,28},{28,24},{1,5},{5... | collective-permute-start | bytes 1572872 | tf_op jit(solution)/shard_map/ppermute | solution.py:31
  117.1 22.8 %collective-permute-start.30 = (bf16[256,1024]{1,0:T(8,128)(2,1)S(1)}, bf16[256,1024]{1,0:T(8,128)(2,1)S(1)}, u32[]{:S(2)}, u32[]{:S(2)}) collective-permute-start(bf16[256,1024]{1,0:T(8,128)(2,1)S(1)} %collective-permute-done.12.refs_4_), channel_id=1, source_target_pairs={{0,4},{4,0},{8,12},{12,8},{16,20},{20,16},{24,28},{28,24},{1,5},{5... | collective-permute-start | bytes 1572872 | tf_op jit(solution)/shard_map/ppermute | solution.py:31
  132.3 5.6 %collective-permute-start.25 = (f32[3,2,1024]{2,1,0:T(2,128)S(1)}, f32[3,2,1024]{2,1,0:T(2,128)S(1)}, u32[]{:S(2)}, u32[]{:S(2)}) collective-permute-start(f32[3,2,1024]{2,1,0:T(2,128)S(1)} %get-tuple-element.58), channel_id=1, source_target_pairs={{0,3},{1,2},{2,1},{3,0},{4,7},{5,6},{6,5},{7,4},{8,11},{9,10},{10,... | collective-permute-start | bytes 73736 | tf_op jit(solution)/shard_map/ppermute | solution.py:31
  148.6 14.2 %collective-permute-start.35 = (bf16[256,1024]{1,0:T(8,128)(2,1)}, bf16[256,1024]{1,0:T(8,128)(2,1)S(1)}, u32[]{:S(2)}, u32[]{:S(2)}) collective-permute-start(bf16[256,1024]{1,0:T(8,128)(2,1)} %feed_partner.1), channel_id=1, source_target_pairs={{0,1},{1,0},{2,3},{3,2},{4,5},{5,4},{6,7},{7,6},{8,9},{9,8},{10,11... | collective-permute-start | bytes 1572872 | tf_op jit(solution)/shard_map/ppermute | solution.py:31
  (34 other events, 315.8 us)

commit v5 on v4

--- a/solution.py
+++ b/solution.py
@@ -19,7 +19,7 @@
 BF16 = jnp.bfloat16
 F32 = jnp.float32
 STRIP = 32
-VMEM_LIMIT = 56 * 1024 * 1024
+MIB = 1024 * 1024
 ANY = pl.BlockSpec(memory_space=pl.ANY)
 VMEM = pl.BlockSpec(memory_space=pltpu.VMEM)
 SMEM = pl.BlockSpec(memory_space=pltpu.SMEM)
@@ -93,7 +93,7 @@
         in_specs=[SMEM, VMEM] + [ANY] * len(shards),
         out_specs=(VMEM,) * 4,
         scratch_shapes=[pltpu.VMEM((blocks * rows, width), BF16), pltpu.SemaphoreType.DMA((len(shards),))],
-        compiler_params=pltpu.CompilerParams(vmem_limit_bytes=VMEM_LIMIT),
+        compiler_params=pltpu.CompilerParams(vmem_limit_bytes=14 * MIB),
         cost_estimate=SHORT,
         name="project",
     )(place, weight, *shards)
@@ -183,7 +183,7 @@
             pltpu.VMEM((heads_width // HD, rows, 3 * rows), BF16),
             pltpu.SemaphoreType.DMA((len(flips), 3)),
         ],
-        compiler_params=pltpu.CompilerParams(vmem_limit_bytes=VMEM_LIMIT),
+        compiler_params=pltpu.CompilerParams(vmem_limit_bytes=14 * MIB),
         cost_estimate=SHORT,
         name=name,
     )(place, starts, ends, query, before, keyval, behind)
@@ -230,7 +230,7 @@
             pltpu.VMEM((rows, width), F32),
             pltpu.SemaphoreType.DMA((1 + sum(len(flips) for flips in layout),)),
         ],
-        compiler_params=pltpu.CompilerParams(vmem_limit_bytes=VMEM_LIMIT),
+        compiler_params=pltpu.CompilerParams(vmem_limit_bytes=11 * MIB),
         cost_estimate=SHORT,
         name="first_norm",
     )(place, hidden, own_out, gain, bias, *parts, *[value for _, value in pieces])
@@ -316,7 +316,7 @@
             pltpu.SemaphoreType.DMA((2, units // chunk)),
             pltpu.SemaphoreType.DMA((copies,)),
         ],
-        compiler_params=pltpu.CompilerParams(vmem_limit_bytes=VMEM_LIMIT),
+        compiler_params=pltpu.CompilerParams(vmem_limit_bytes=20 * MIB),
         cost_estimate=SHORT,
         name=name,
     )(place, rows, up_weight, down_weight, *[value for _, _, value in pieces])
@@ -335,7 +335,7 @@
         out_shape=jax.ShapeDtypeStruct(normed.shape, BF16),
         in_specs=[VMEM] * 5,
         out_specs=VMEM,
-        compiler_params=pltpu.CompilerParams(vmem_limit_bytes=VMEM_LIMIT),
+        compiler_params=pltpu.CompilerParams(vmem_limit_bytes=6 * MIB),
         name="finish",
     )(normed, near, far, gain, bias)
 
@@ -397,7 +397,7 @@
         ],
         out_specs=pl.BlockSpec((3, requests, width), lambda i: (0, 0, 0)),
         scratch_shapes=[state, state, state],
-        compiler_params=pltpu.CompilerParams(vmem_limit_bytes=VMEM_LIMIT),
+        compiler_params=pltpu.CompilerParams(vmem_limit_bytes=8 * MIB),
         cost_estimate=SHORT,
         name="decode",
     )(slots, filled, queries, kv_cache)
@@ -463,36 +463,38 @@
         falling = lax.ppermute(falling, "kv", [(kvs - 1 - i, kvs - 2 - i) for i in links])
         from_below.append(rising)
         from_above.append(falling)
-        if step == 1:
-            out_part = after(eighth(out_weight), rising, falling)
-            out_here = jnp.stack([swapped(out_part, "kv", flip) for flip in range(1, kvs)])
         if step == 2:
-            rising, falling = after(rising, partial, out_here), after(falling, partial, out_here)
-    out_x, out_y = swapped(out_here, "tok", 2), swapped(out_here, "tok", 4)
-    out_far = swapped(after(out_y, rising), "tok", 2)
-
-    feed_part = jnp.concatenate([eighth(up_weight), eighth(down_weight)], axis=0)
+            rising, falling = after(rising, partial), after(falling, partial)
+    dec_parts = exchanged_partials(partial, dec_query.shape[0])
+
+    out_part = after(eighth(out_weight), from_below[1], from_above[1])
+    feed_part = jnp.concatenate([eighth(up_weight), eighth(down_weight), eighth(out_weight)], axis=0)
     feed_here = swapped(after(feed_part, from_below[1], from_above[1]), "kv", 2)
+    out_near, out_far = swapped(out_part, "kv", 1), swapped(out_part, "kv", 3)
 
     order = jnp.arange(stretch_len.shape[0])
     ends = jnp.sum(jnp.where(order[:, None] <= order[None, :], stretch_len[:, None], 0), axis=0, dtype=jnp.int32)
     starts = (ends - stretch_len)[None, :]
     ends = ends[None, :]
 
-    shards = [hidden_in] + from_below + from_above
+    shards = [after(hidden_in, *dec_parts)] + from_below + from_above
     query, keyval, top, bottom = project(place, jnp.transpose(qkv_weight, (1, 0, 2)), shards)
     before = lax.ppermute(bottom, "tok", [(i, i + 1) for i in range(toks - 1)])
     behind = lax.ppermute(top, "tok", [(i + 1, i) for i in range(toks - 1)])
     window = (place, starts, ends, query, before, keyval, behind, rows)
     parts = [None] * kvs
     parts[3], parts[2] = attend_blocks(*window, (3, 2), "attend_far")
-    out_all = jnp.stack([out_here, out_x, out_y, after(out_far, parts[3])])
-    out_core = swapped(out_all, "tok", 1)
     feed_here = after(feed_here, parts[3], parts[2])
     parts[3], parts[2] = swapped(parts[3], "kv", 3), swapped(parts[2], "kv", 2)
+    depth = out_part.shape[0]
+    out_here = jnp.stack([out_near, feed_here[-depth:], out_far])
+    feed_here = feed_here[:-depth]
+    out_x, out_y = swapped(out_here, "tok", 2), swapped(out_here, "tok", 4)
     feed_x, feed_y = swapped(feed_here, "tok", 2), swapped(feed_here, "tok", 4)
-    window = (place, starts, ends, after(query, feed_here), before, keyval, behind, rows)
+    window = (place, starts, ends, after(query, out_here), before, keyval, behind, rows)
     parts[1], parts[0] = attend_blocks(*window, (1, 0), "attend_near")
+    out_all = jnp.stack([out_here, out_x, out_y, swapped(after(out_y, parts[0]), "tok", 2)])
+    out_core = swapped(out_all, "tok", 1)
     half = feed_here.shape[0] // 2
     far_up = swapped(after(feed_y, parts[0])[:half], "tok", 2)
     far_down = swapped(after(feed_x, parts[0])[half:], "tok", 4)
@@ -503,14 +505,12 @@
     partner = swapped(normed, "kv", 1)
     held = [(0, None, feed_here), (2, None, feed_x), (4, None, feed_y), (6, 0, far_up), (6, 1, far_down)]
     feed_pieces = held + [(flip ^ 1, part, swapped(after(value, normed), "tok", 1)) for flip, part, value in held]
-    dec_out = merged_partials(exchanged_partials(after(partial, normed), dec_query.shape[0]))
-    partner = after(partner, dec_out)
     away = feed(place, partner, up_weight, down_weight, feed_pieces, BF16, "feed_partner")
     arrived = swapped(away, "kv", 1)
     mine = feed(place, after(normed, away), up_weight, down_weight, feed_pieces, F32, "feed_own")
     prefill_out = finish(normed, mine, arrived, ln2_gain[None, :], ln2_bias[None, :])
 
-    return prefill_out, dec_out
+    return prefill_out, merged_partials(dec_parts)
 
 
 def extended(value, sides, width):

time: 167 us -> 172 us (1.030)
  Pallas kernels: 47 us -> 29.7 us
  waiting for transfers between devices: 61.4 us -> 78.2 us
  starting transfers between devices: 45.2 us -> 56.9 us
  local copies, waits for them, and re-layouts: 7.09 us -> 3.78 us
  other arithmetic: 4.62 us -> 2.37 us
    ppermute x28 -> x27, waiting for transfers between devices: 44.1 us -> 63.6 us  [swapped(): return lax.ppermute(value, axis, [(i, i ^ flip) for i in range(count)])]
    ppermute x28 -> x27, starting transfers between devices: 32.3 us -> 44.1 us  [swapped(): return lax.ppermute(value, axis, [(i, i ^ flip) for i in range(count)])]
    ppermute x3, waiting for transfers between devices: 12.3 us -> 3.36 us  [routed_body(): lax.ppermute(falling, 'kv', [(kvs - 1 - i, kvs - 2 - i) for i in links])]
    ppermute x3, waiting for transfers between devices: 4.98 us -> 10.2 us  [routed_body(): rising = lax.ppermute(rising, 'kv', [(i, i + 1) for i in links])]
    pallas_call x2, Pallas kernels: 14 us -> 9.16 us  [feed(): pl.pallas_call(functools.partial(feed_kernel, layout), out_shape=jax.Shap...]
    pallas_call x2, Pallas kernels: 13.8 us -> 10.3 us  [attend_blocks(): pl.pallas_call(functools.partial(attend_kernel, flips), out_shape=tuple((...]
    pallas_call x1, Pallas kernels: 5.96 us -> 2.61 us  [project(): pl.pallas_call(project_kernel, out_shape=(jax.ShapeDtypeStruct((blocks *...]
    unnamed x60 -> x24, local copies, waits for them, and re-layouts: 5.11 us -> 2.58 us
  transfers between devices with their start and end apart: 36 -> 35, of which waited for: 15 -> 14; matrix products, arithmetic and copies ran while one was open for 4% -> 2% of each run, Pallas kernels for 22% -> 14%
where the time goes in v5:
time: 172 us
  waiting for transfers between devices  78.2 us (45%)
  starting transfers between devices  56.9 us (33%)
  Pallas kernels  29.7 us (17%)
  local copies, waits for them, and re-layouts  3.78 us (2%)
  other arithmetic  2.37 us (1%)
    ppermute x27, waiting for transfers between devices, swapped(): return lax.ppermute(value, axis, [(i, i ^ flip) for i in range(count)])  63.6 us
    ppermute x27, starting transfers between devices, swapped(): return lax.ppermute(value, axis, [(i, i ^ flip) for i in range(count)])  44.1 us
    pallas_call x2, Pallas kernels, attend_blocks(): pl.pallas_call(functools.partial(attend_kernel, flips), out_shape=tuple((...  10.3 us
    ppermute x3, waiting for transfers between devices, routed_body(): rising = lax.ppermute(rising, 'kv', [(i, i + 1) for i in links])  10.2 us
    pallas_call x2, Pallas kernels, feed(): pl.pallas_call(functools.partial(feed_kernel, layout), out_shape=jax.Shap...  9.16 us
    ppermute x3, starting transfers between devices, routed_body(): rising = lax.ppermute(rising, 'kv', [(i, i + 1) for i in links])  6.34 us
    ppermute x3, starting transfers between devices, routed_body(): lax.ppermute(falling, 'kv', [(kvs - 1 - i, kvs - 2 - i) for i in links])  3.86 us
    pallas_call x1, Pallas kernels, decode(): pl.pallas_call(decode_kernel, grid=(pieces,), out_shape=jax.ShapeDtypeStr...  3.78 us
  transfers between devices with their start and end apart: 35, of which 14 were waited for; matrix products, arithmetic and copies ran while one was open for 2% of the time, Pallas kernels for 14%

profile of v5, /device:TPU:0, one launch (start us, length us, event | category | flops | bytes accessed | tf_op | source)
XLA Modules:
  0.0 171.9 jit_solution(5086703375976286694)
XLA Ops:
  0.6 5.0 %collective-permute-start.6 = (bf16[256,1024]{1,0:T(8,128)(2,1)}, bf16[256,1024]{1,0:T(8,128)(2,1)S(1)}, u32[]{:S(2)}, u32[]{:S(2)}) collective-permute-start(bf16[256,1024]{1,0:T(8,128)(2,1)} %hidden_ref.1), channel_id=1, source_target_pairs={{0,1},{1,2},{2,3},{4,5},{5,6},{6,7},{8,9},{9,10},{10,11},{12,13},{... | collective-permute-start | bytes 1572872 | tf_op jit(solution)/shard_map/ppermute | solution.py:462
  5.6 1.3 collective-permute-start.9
  6.9 10.1 %collective-permute-done.6.refs_1_ = bf16[256,1024]{1,0:T(8,128)(2,1)S(1)} collective-permute-done((bf16[256,1024]{1,0:T(8,128)(2,1)}, bf16[256,1024]{1,0:T(8,128)(2,1)S(1)}, u32[]{:S(2)}, u32[]{:S(2)}) %collective-permute-start.6) | collective-permute-done | bytes 524320 | tf_op jit(solution)/shard_map/ppermute | solution.py:462
  17.7 3.4 %collective-permute-done.9.refs_4_ = bf16[256,1024]{1,0:T(8,128)(2,1)S(1)} collective-permute-done((bf16[256,1024]{1,0:T(8,128)(2,1)}, bf16[256,1024]{1,0:T(8,128)(2,1)S(1)}, u32[]{:S(2)}, u32[]{:S(2)}) %collective-permute-start.9) | collective-permute-done | bytes 524320 | tf_op jit(solution)/shard_map/ppermute | solution.py:463
  22.4 4.0 %collective-permute-start.1 = (bf16[2,1024]{1,0:T(2,128)(2,1)}, bf16[2,1024]{1,0:T(2,128)(2,1)S(1)}, u32[]{:S(2)}, u32[]{:S(2)}) collective-permute-start(bf16[2,1024]{1,0:T(2,128)(2,1)} %param.24), channel_id=1, source_target_pairs={{0,2},{1,3},{2,0},{3,1},{4,6},{5,7},{6,4},{7,5},{8,10},{9,11},{10,... | collective-permute-start | bytes 12296 | tf_op jit(solution)/shard_map/ppermute | solution.py:31
  26.4 1.5 collective-permute-start.2
  29.7 7.4 %collective-permute-done.1 = bf16[2,1024]{1,0:T(2,128)(2,1)S(1)} collective-permute-done((bf16[2,1024]{1,0:T(2,128)(2,1)}, bf16[2,1024]{1,0:T(2,128)(2,1)S(1)}, u32[]{:S(2)}, u32[]{:S(2)}) %collective-permute-start.1) | collective-permute-done | bytes 4128 | tf_op jit(solution)/shard_map/ppermute | solution.py:31
  37.8 1.9 %copy-done.2 = bf16[2,1,6,128,1024]{4,3,2,1,0:T(8,128)(2,1)S(1)} copy-done((bf16[2,1,6,128,1024]{4,3,2,1,0:T(8,128)(2,1)S(1)}, bf16[2,1,6,128,1024]{4,3,2,1,0:T(8,128)(2,1)}, u32[]{:S(2)}) %copy-start.2) | copy-done | bytes 3145752
  40.4 3.8 %decode.1 = f32[3,8,1024]{2,1,0:T(8,128)S(1)} custom-call(s32[6]{0:T(128)S(1)} %fusion.16.slot_ref, s32[6]{0:T(128)S(1)} %bitcast.140, f32[8,1024]{1,0:T(8,128)S(1)} %maximum_convert_fusion.query_ref, bf16[2,1,6,128,1024]{4,3,2,1,0:T(8,128)(2,1)S(1)} %copy-done.2), custom_call_target="tpu_custom_call" | custom-call | flops 1 | bytes 1 | tf_op jit(solution)/shard_map/decode/pallas_call | solution.py:388
  46.9 4.6 %collective-permute-start.5 = (f32[3,2,1024]{2,1,0:T(2,128)S(1)}, f32[3,2,1024]{2,1,0:T(2,128)S(1)}, u32[]{:S(2)}, u32[]{:S(2)}) collective-permute-start(f32[3,2,1024]{2,1,0:T(2,128)S(1)} %get-tuple-element.52), channel_id=1, source_target_pairs={{0,3},{1,2},{2,1},{3,0},{4,7},{5,6},{6,5},{7,4},{8,11},{9,10},{10,... | collective-permute-start | bytes 73736 | tf_op jit(solution)/shard_map/ppermute | solution.py:31
  51.5 11.2 %collective-permute-done.5 = f32[3,2,1024]{2,1,0:T(2,128)S(1)} collective-permute-done((f32[3,2,1024]{2,1,0:T(2,128)S(1)}, f32[3,2,1024]{2,1,0:T(2,128)S(1)}, u32[]{:S(2)}, u32[]{:S(2)}) %collective-permute-start.5) | collective-permute-done | bytes 24608 | tf_op jit(solution)/shard_map/ppermute | solution.py:31
  62.6 12.4 %collective-permute-start.3 = (f32[3,2,1024]{2,1,0:T(2,128)S(1)}, f32[3,2,1024]{2,1,0:T(2,128)S(1)}, u32[]{:S(2)}, u32[]{:S(2)}) collective-permute-start(f32[3,2,1024]{2,1,0:T(2,128)S(1)} %get-tuple-element.54), channel_id=1, source_target_pairs={{0,1},{1,0},{2,3},{3,2},{4,5},{5,4},{6,7},{7,6},{8,9},{9,8},{10,11... | collective-permute-start | bytes 73736 | tf_op jit(solution)/shard_map/ppermute | solution.py:31
  75.1 1.7 %collective-permute-done.3 = f32[3,2,1024]{2,1,0:T(2,128)S(1)} collective-permute-done((f32[3,2,1024]{2,1,0:T(2,128)S(1)}, f32[3,2,1024]{2,1,0:T(2,128)S(1)}, u32[]{:S(2)}, u32[]{:S(2)}) %collective-permute-start.3) | collective-permute-done | bytes 24608 | tf_op jit(solution)/shard_map/ppermute | solution.py:31
  76.9 2.6 %project.1 = (bf16[1024,256]{1,0:T(8,128)(2,1)S(1)}, bf16[1024,512]{1,0:T(8,128)(2,1)S(1)}, bf16[256,512]{1,0:T(8,128)(2,1)S(1)}, bf16[256,512]{1,0:T(8,128)(2,1)S(1)}) custom-call(s32[2]{0:T(128)S(1)} %pad_add_fusion.place_ref.refs_0_, bf16[3,1024,256]{2,1,0:T(8,128)(2,1)S(1)} %bitcast.133, bf16[256,1024]{1,0:T(8,128)(2,1)S(1)} %copy-done.3, ...), custom_call_target="tpu_custom_call" | custom-call | flops 1 | bytes 1 | tf_op jit(solution)/shard_map/project/pallas_call | solution.py:85
  79.5 1.3 collective-permute-start.14
  82.2 1.5 collective-permute-start.16
  85.9 5.1 %attend_far.1 = (bf16[256,256]{1,0:T(8,128)(2,1)S(1)}, bf16[256,256]{1,0:T(8,128)(2,1)S(1)}) custom-call(s32[2]{0:T(128)S(1)} %pad_add_fusion.place_ref.refs_0_, s32[1,48]{1,0:T(1,128)S(1)} %subtract_bitcast_fusion.starts_ref, s32[1,48]{1,0:T(1,128)S(1)} %bitcast.138, bf16[1024,256]{1,0:T(8,128)(2,1)S(1)} %get-tuple-element.38.query_ref, ...), custom_call_target="tpu_custom_call" | custom-call | flops 1 | bytes 1 | tf_op jit(solution)/shard_map/attend_far/pallas_call | solution.py:174
  91.1 5.5 %collective-permute-start.21 = (bf16[3,32,1024]{2,1,0:T(8,128)(2,1)S(1)}, bf16[3,32,1024]{2,1,0:T(8,128)(2,1)S(1)}, u32[]{:S(2)}, u32[]{:S(2)}) collective-permute-start(bf16[3,32,1024]{2,1,0:T(8,128)(2,1)S(1)} %get-tuple-element.51), channel_id=1, source_target_pairs={{0,16},{4,20},{8,24},{12,28},{16,0},{20,4},{24,8},{28,12},{1,17},{... | collective-permute-start | bytes 589832 | tf_op jit(solution)/shard_map/ppermute | solution.py:31
  97.2 5.2 %attend_near.1 = (bf16[256,256]{1,0:T(8,128)(2,1)S(1)}, bf16[256,256]{1,0:T(8,128)(2,1)S(1)}) custom-call(s32[2]{0:T(128)S(1)} %pad_add_fusion.place_ref.refs_0_, s32[1,48]{1,0:T(1,128)S(1)} %subtract_bitcast_fusion.starts_ref, s32[1,48]{1,0:T(1,128)S(1)} %bitcast.139, bf16[1024,256]{1,0:T(8,128)(2,1)S(1)} %get-tuple-element.38.query_ref, ...), custom_call_target="tpu_custom_call" | custom-call | flops 1 | bytes 1 | tf_op jit(solution)/shard_map/attend_near/pallas_call | solution.py:174
  102.4 1.5 collective-permute-start.22
  104.0 6.0 %collective-permute-done.22 = bf16[3,32,1024]{2,1,0:T(8,128)(2,1)S(1)} collective-permute-done((bf16[3,32,1024]{2,1,0:T(8,128)(2,1)S(1)}, bf16[3,32,1024]{2,1,0:T(8,128)(2,1)S(1)}, u32[]{:S(2)}, u32[]{:S(2)}) %collective-permute-start.22) | collective-permute-done | bytes 196640 | tf_op jit(solution)/shard_map/ppermute | solution.py:31
  110.3 1.9 %collective-permute-start.26 = (bf16[256,1024]{1,0:T(8,128)(2,1)S(1)}, bf16[256,1024]{1,0:T(8,128)(2,1)S(1)}, u32[]{:S(2)}, u32[]{:S(2)}) collective-permute-start(bf16[256,1024]{1,0:T(8,128)(2,1)S(1)} %slice.69.refs_4_), channel_id=1, source_target_pairs={{0,16},{4,20},{8,24},{12,28},{16,0},{20,4},{24,8},{28,12},{1,17},{... | collective-permute-start | bytes 1572872 | tf_op jit(solution)/shard_map/ppermute | solution.py:31
  112.3 1.4 collective-permute-start.19
  113.7 11.0 %collective-permute-done.26.refs_6_ = bf16[256,1024]{1,0:T(8,128)(2,1)S(1)} collective-permute-done((bf16[256,1024]{1,0:T(8,128)(2,1)S(1)}, bf16[256,1024]{1,0:T(8,128)(2,1)S(1)}, u32[]{:S(2)}, u32[]{:S(2)}) %collective-permute-start.26) | collective-permute-done | bytes 524320 | tf_op jit(solution)/shard_map/ppermute | solution.py:31
  126.7 2.3 %collective-permute-start.18 = (bf16[256,256]{1,0:T(8,128)(2,1)S(1)}, bf16[256,256]{1,0:T(8,128)(2,1)S(1)}, u32[]{:S(2)}, u32[]{:S(2)}) collective-permute-start(bf16[256,256]{1,0:T(8,128)(2,1)S(1)} %get-tuple-element.36), channel_id=1, source_target_pairs={{0,2},{1,3},{2,0},{3,1},{4,6},{5,7},{6,4},{7,5},{8,10},{9,11},{10,... | collective-permute-start | bytes 393224 | tf_op jit(solution)/shard_map/ppermute | solution.py:31
  129.0 5.8 %collective-permute-done.18.refs_2_ = bf16[256,256]{1,0:T(8,128)(2,1)S(1)} collective-permute-done((bf16[256,256]{1,0:T(8,128)(2,1)S(1)}, bf16[256,256]{1,0:T(8,128)(2,1)S(1)}, u32[]{:S(2)}, u32[]{:S(2)}) %collective-permute-start.18) | collective-permute-done | bytes 131104 | tf_op jit(solution)/shard_map/ppermute | solution.py:31
  135.3 2.6 %first_norm.1.refs_1_.normed_ref = bf16[256,1024]{1,0:T(8,128)(2,1)S(1)} custom-call(s32[2]{0:T(128)S(1)} %pad_add_fusion.place_ref.refs_0_, bf16[256,1024]{1,0:T(8,128)(2,1)S(1)} %copy-done.3, bf16[256,1024]{1,0:T(8,128)(2,1)S(1)} %copy-done.5, f32[1,1024]{1,0:T(1,128)S(1)} %bitcast.136, f32[1,1024]{1,0:T(1,128)S(1)} %bitcast.137, ...), custom_call_target="tpu_custom_call" | custom-call | flops 1 | bytes 1 | tf_op jit(solution)/shard_map/first_norm/pallas_call | solution.py:222
  140.1 2.0 %collective-permute-done.33.refs_13_ = bf16[128,1024]{1,0:T(8,128)(2,1)S(1)} collective-permute-done((bf16[128,1024]{1,0:T(8,128)(2,1)S(1)}, bf16[128,1024]{1,0:T(8,128)(2,1)S(1)}, u32[]{:S(2)}, u32[]{:S(2)}) %collective-permute-start.33) | collective-permute-done | bytes 262176 | tf_op jit(solution)/shard_map/ppermute | solution.py:31
  142.1 10.8 %collective-permute-done.24.refs_1_ = bf16[256,1024]{1,0:T(8,128)(2,1)S(1)} collective-permute-done((bf16[256,1024]{1,0:T(8,128)(2,1)S(1)}, bf16[256,1024]{1,0:T(8,128)(2,1)S(1)}, u32[]{:S(2)}, u32[]{:S(2)}) %collective-permute-start.24) | collective-permute-done | bytes 524320 | tf_op jit(solution)/shard_map/ppermute | solution.py:31
  152.9 4.6 %feed_partner.1 = bf16[256,1024]{1,0:T(8,128)(2,1)S(1)} custom-call(s32[2]{0:T(128)S(1)} %pad_add_fusion.place_ref.refs_0_, bf16[256,1024]{1,0:T(8,128)(2,1)S(1)} %collective-permute-done.24.refs_1_, bf16[1024,1024]{1,0:T(8,128)(2,1)S(1)} %copy-done.1, bf16[1024,1024]{1,0:T(8,128)(2,1)S(1)} %copy-done, bf16[256,1024]{1,0:T(8,128)(2,1)S(1)} %slice.69.refs_4_, ...), custom_call_target="tpu_custom_call" | custom-call | flops 1 | bytes 1 | tf_op jit(solution)/shard_map/feed_partner/pallas_call | solution.py:305
  159.3 4.6 %feed_own.1.near_ref = f32[256,1024]{1,0:T(8,128)S(1)} custom-call(s32[2]{0:T(128)S(1)} %pad_add_fusion.place_ref.refs_0_, bf16[256,1024]{1,0:T(8,128)(2,1)S(1)} %first_norm.1.refs_1_.normed_ref, bf16[1024,1024]{1,0:T(8,128)(2,1)S(1)} %copy-done.1, bf16[1024,1024]{1,0:T(8,128)(2,1)S(1)} %copy-done, bf16[256,1024]{1,0:T(8,128)(2,1)S(1)} %slice.69.refs_4_, ...), custom_call_target="tpu_custom_call" | custom-call | flops 1 | bytes 1 | tf_op jit(solution)/shard_map/feed_own/pallas_call | solution.py:305
  163.9 6.7 %collective-permute-done.34.far_ref = bf16[256,1024]{1,0:T(8,128)(2,1)S(1)} collective-permute-done((bf16[256,1024]{1,0:T(8,128)(2,1)S(1)}, bf16[256,1024]{1,0:T(8,128)(2,1)S(1)}, u32[]{:S(2)}, u32[]{:S(2)}) %collective-permute-start.34) | collective-permute-done | bytes 524320 | tf_op jit(solution)/shard_map/ppermute | solution.py:31
  (86 shorter events, 20.2 us)
Async XLA Ops:
  0.6 16.4 %collective-permute-start.6 = (bf16[256,1024]{1,0:T(8,128)(2,1)}, bf16[256,1024]{1,0:T(8,128)(2,1)S(1)}, u32[]{:S(2)}, u32[]{:S(2)}) collective-permute-start(bf16[256,1024]{1,0:T(8,128)(2,1)} %hidden_ref.1), channel_id=1, source_target_pairs={{0,1},{1,2},{2,3},{4,5},{5,6},{6,7},{8,9},{9,10},{10,11},{12,13},{... | collective-permute-start | bytes 1572872 | tf_op jit(solution)/shard_map/ppermute | solution.py:462
  5.6 15.5 %collective-permute-start.9 = (bf16[256,1024]{1,0:T(8,128)(2,1)}, bf16[256,1024]{1,0:T(8,128)(2,1)S(1)}, u32[]{:S(2)}, u32[]{:S(2)}) collective-permute-start(bf16[256,1024]{1,0:T(8,128)(2,1)} %hidden_ref.1), channel_id=1, source_target_pairs={{3,2},{2,1},{1,0},{7,6},{6,5},{5,4},{11,10},{10,9},{9,8},{15,14},{... | collective-permute-start | bytes 1572872 | tf_op jit(solution)/shard_map/ppermute | solution.py:463
  17.0 27.1 %collective-permute-start.7 = (bf16[256,1024]{1,0:T(8,128)(2,1)S(1)}, bf16[256,1024]{1,0:T(8,128)(2,1)S(1)}, u32[]{:S(2)}, u32[]{:S(2)}) collective-permute-start(bf16[256,1024]{1,0:T(8,128)(2,1)S(1)} %collective-permute-done.6.refs_1_), channel_id=1, source_target_pairs={{1,2},{2,3},{5,6},{6,7},{9,10},{10,11},{13,14},{14,15},{17,18},{18... | collective-permute-start | bytes 1572872 | tf_op jit(solution)/shard_map/ppermute | solution.py:462
  21.1 23.8 %collective-permute-start.10 = (bf16[256,1024]{1,0:T(8,128)(2,1)S(1)}, bf16[256,1024]{1,0:T(8,128)(2,1)S(1)}, u32[]{:S(2)}, u32[]{:S(2)}) collective-permute-start(bf16[256,1024]{1,0:T(8,128)(2,1)S(1)} %collective-permute-done.9.refs_4_), channel_id=1, source_target_pairs={{2,1},{1,0},{6,5},{5,4},{10,9},{9,8},{14,13},{13,12},{18,17},{17,1... | collective-permute-start | bytes 1572872 | tf_op jit(solution)/shard_map/ppermute | solution.py:463
  22.4 14.7 %collective-permute-start.1 = (bf16[2,1024]{1,0:T(2,128)(2,1)}, bf16[2,1024]{1,0:T(2,128)(2,1)S(1)}, u32[]{:S(2)}, u32[]{:S(2)}) collective-permute-start(bf16[2,1024]{1,0:T(2,128)(2,1)} %param.24), channel_id=1, source_target_pairs={{0,2},{1,3},{2,0},{3,1},{4,6},{5,7},{6,4},{7,5},{8,10},{9,11},{10,... | collective-permute-start | bytes 12296 | tf_op jit(solution)/shard_map/ppermute | solution.py:31
  26.4 10.7 %collective-permute-start = (bf16[2,1024]{1,0:T(2,128)(2,1)}, bf16[2,1024]{1,0:T(2,128)(2,1)S(1)}, u32[]{:S(2)}, u32[]{:S(2)}) collective-permute-start(bf16[2,1024]{1,0:T(2,128)(2,1)} %param.24), channel_id=1, source_target_pairs={{0,1},{1,0},{2,3},{3,2},{4,5},{5,4},{6,7},{7,6},{8,9},{9,8},{10,11... | collective-permute-start | bytes 12296 | tf_op jit(solution)/shard_map/ppermute | solution.py:31
  26.4 10.7 %collective-permute-start.2 = (bf16[2,1024]{1,0:T(2,128)(2,1)}, bf16[2,1024]{1,0:T(2,128)(2,1)S(1)}, u32[]{:S(2)}, u32[]{:S(2)}) collective-permute-start(bf16[2,1024]{1,0:T(2,128)(2,1)} %param.24), channel_id=1, source_target_pairs={{0,3},{1,2},{2,1},{3,0},{4,7},{5,6},{6,5},{7,4},{8,11},{9,10},{10,... | collective-permute-start | bytes 12296 | tf_op jit(solution)/shard_map/ppermute | solution.py:31
  44.2 32.7 %collective-permute-start.8 = (bf16[256,1024]{1,0:T(8,128)(2,1)S(1)}, bf16[256,1024]{1,0:T(8,128)(2,1)S(1)}, u32[]{:S(2)}, u32[]{:S(2)}) collective-permute-start(bf16[256,1024]{1,0:T(8,128)(2,1)S(1)} %collective-permute-done.7.refs_2_), channel_id=1, source_target_pairs={{2,3},{6,7},{10,11},{14,15},{18,19},{22,23},{26,27},{30,31}} | collective-permute-start | bytes 1572872 | tf_op jit(solution)/shard_map/ppermute | solution.py:462
  44.9 32.0 %collective-permute-start.11 = (bf16[256,1024]{1,0:T(8,128)(2,1)S(1)}, bf16[256,1024]{1,0:T(8,128)(2,1)S(1)}, u32[]{:S(2)}, u32[]{:S(2)}) collective-permute-start(bf16[256,1024]{1,0:T(8,128)(2,1)S(1)} %collective-permute-done.10.refs_5_), channel_id=1, source_target_pairs={{1,0},{5,4},{9,8},{13,12},{17,16},{21,20},{25,24},{29,28}} | collective-permute-start | bytes 1572872 | tf_op jit(solution)/shard_map/ppermute | solution.py:463
  46.3 44.7 %collective-permute-start.13 = (bf16[288,1024]{1,0:T(8,128)(2,1)S(1)}, bf16[288,1024]{1,0:T(8,128)(2,1)S(1)}, u32[]{:S(2)}, u32[]{:S(2)}) collective-permute-start(bf16[288,1024]{1,0:T(8,128)(2,1)S(1)} %pad_maximum_fusion.1), channel_id=1, source_target_pairs={{0,2},{1,3},{2,0},{3,1},{4,6},{5,7},{6,4},{7,5},{8,10},{9,11},{10,... | collective-permute-start | bytes 1769480 | tf_op jit(solution)/shard_map/ppermute | solution.py:31
  46.9 15.8 %collective-permute-start.5 = (f32[3,2,1024]{2,1,0:T(2,128)S(1)}, f32[3,2,1024]{2,1,0:T(2,128)S(1)}, u32[]{:S(2)}, u32[]{:S(2)}) collective-permute-start(f32[3,2,1024]{2,1,0:T(2,128)S(1)} %get-tuple-element.52), channel_id=1, source_target_pairs={{0,3},{1,2},{2,1},{3,0},{4,7},{5,6},{6,5},{7,4},{8,11},{9,10},{10,... | collective-permute-start | bytes 73736 | tf_op jit(solution)/shard_map/ppermute | solution.py:31
  51.5 23.6 %collective-permute-start.4 = (f32[3,2,1024]{2,1,0:T(2,128)S(1)}, f32[3,2,1024]{2,1,0:T(2,128)S(1)}, u32[]{:S(2)}, u32[]{:S(2)}) collective-permute-start(f32[3,2,1024]{2,1,0:T(2,128)S(1)} %get-tuple-element.53), channel_id=1, source_target_pairs={{0,2},{1,3},{2,0},{3,1},{4,6},{5,7},{6,4},{7,5},{8,10},{9,11},{10,... | collective-permute-start | bytes 73736 | tf_op jit(solution)/shard_map/ppermute | solution.py:31
  62.6 14.2 %collective-permute-start.3 = (f32[3,2,1024]{2,1,0:T(2,128)S(1)}, f32[3,2,1024]{2,1,0:T(2,128)S(1)}, u32[]{:S(2)}, u32[]{:S(2)}) collective-permute-start(f32[3,2,1024]{2,1,0:T(2,128)S(1)} %get-tuple-element.54), channel_id=1, source_target_pairs={{0,1},{1,0},{2,3},{3,2},{4,5},{5,4},{6,7},{7,6},{8,9},{9,8},{10,11... | collective-permute-start | bytes 73736 | tf_op jit(solution)/shard_map/ppermute | solution.py:31
  79.5 5.3 %collective-permute-start.14 = (bf16[256,512]{1,0:T(8,128)(2,1)S(1)}, bf16[256,512]{1,0:T(8,128)(2,1)S(1)}, u32[]{:S(2)}, u32[]{:S(2)}) collective-permute-start(bf16[256,512]{1,0:T(8,128)(2,1)S(1)} %get-tuple-element.32), channel_id=1, source_target_pairs={{0,4},{4,8},{8,12},{12,16},{16,20},{20,24},{24,28},{1,5},{5,9},{9,... | collective-permute-start | bytes 786440 | tf_op jit(solution)/shard_map/ppermute | solution.py:482
  80.8 5.1 %collective-permute-start.15 = (bf16[256,512]{1,0:T(8,128)(2,1)S(1)}, bf16[256,512]{1,0:T(8,128)(2,1)S(1)}, u32[]{:S(2)}, u32[]{:S(2)}) collective-permute-start(bf16[256,512]{1,0:T(8,128)(2,1)S(1)} %get-tuple-element.34), channel_id=1, source_target_pairs={{4,0},{8,4},{12,8},{16,12},{20,16},{24,20},{28,24},{5,1},{9,5},{13... | collective-permute-start | bytes 786440 | tf_op jit(solution)/shard_map/ppermute | solution.py:483
  82.2 8.8 %collective-permute-start.16 = (bf16[32,1024]{1,0:T(8,128)(2,1)S(1)}, bf16[32,1024]{1,0:T(8,128)(2,1)S(1)}, u32[]{:S(2)}, u32[]{:S(2)}) collective-permute-start(bf16[32,1024]{1,0:T(8,128)(2,1)S(1)} %constant_dynamic-slice_fusion.2), channel_id=1, source_target_pairs={{0,3},{1,2},{2,1},{3,0},{4,7},{5,6},{6,5},{7,4},{8,11},{9,10},{10,... | collective-permute-start | bytes 196616 | tf_op jit(solution)/shard_map/ppermute | solution.py:31
  83.7 7.4 %collective-permute-start.12 = (bf16[32,1024]{1,0:T(8,128)(2,1)S(1)}, bf16[32,1024]{1,0:T(8,128)(2,1)S(1)}, u32[]{:S(2)}, u32[]{:S(2)}) collective-permute-start(bf16[32,1024]{1,0:T(8,128)(2,1)S(1)} %constant_dynamic-slice_fusion.2), channel_id=1, source_target_pairs={{0,1},{1,0},{2,3},{3,2},{4,5},{5,4},{6,7},{7,6},{8,9},{9,8},{10,11... | collective-permute-start | bytes 196616 | tf_op jit(solution)/shard_map/ppermute | solution.py:31
  91.1 11.3 %collective-permute-start.21 = (bf16[3,32,1024]{2,1,0:T(8,128)(2,1)S(1)}, bf16[3,32,1024]{2,1,0:T(8,128)(2,1)S(1)}, u32[]{:S(2)}, u32[]{:S(2)}) collective-permute-start(bf16[3,32,1024]{2,1,0:T(8,128)(2,1)S(1)} %get-tuple-element.51), channel_id=1, source_target_pairs={{0,16},{4,20},{8,24},{12,28},{16,0},{20,4},{24,8},{28,12},{1,17},{... | collective-permute-start | bytes 589832 | tf_op jit(solution)/shard_map/ppermute | solution.py:31
  96.6 7.4 %collective-permute-start.20 = (bf16[3,32,1024]{2,1,0:T(8,128)(2,1)S(1)}, bf16[3,32,1024]{2,1,0:T(8,128)(2,1)S(1)}, u32[]{:S(2)}, u32[]{:S(2)}) collective-permute-start(bf16[3,32,1024]{2,1,0:T(8,128)(2,1)S(1)} %get-tuple-element.51), channel_id=1, source_target_pairs={{0,8},{4,12},{8,0},{12,4},{16,24},{20,28},{24,16},{28,20},{1,9},{5... | collective-permute-start | bytes 589832 | tf_op jit(solution)/shard_map/ppermute | solution.py:31
  102.4 7.6 %collective-permute-start.22 = (bf16[3,32,1024]{2,1,0:T(8,128)(2,1)S(1)}, bf16[3,32,1024]{2,1,0:T(8,128)(2,1)S(1)}, u32[]{:S(2)}, u32[]{:S(2)}) collective-permute-start(bf16[3,32,1024]{2,1,0:T(8,128)(2,1)S(1)} %collective-permute-done.21), channel_id=1, source_target_pairs={{0,8},{4,12},{8,0},{12,4},{16,24},{20,28},{24,16},{28,20},{1,9},{5... | collective-permute-start | bytes 589832 | tf_op jit(solution)/shard_map/ppermute | solution.py:31
  110.1 25.1 %collective-permute-start.23 = (bf16[4,3,32,1024]{3,2,1,0:T(8,128)(2,1)S(1)}, bf16[4,3,32,1024]{3,2,1,0:T(8,128)(2,1)S(1)}, u32[]{:S(2)}, u32[]{:S(2)}) collective-permute-start(bf16[4,3,32,1024]{3,2,1,0:T(8,128)(2,1)S(1)} %pad_maximum_fusion.refs_4_), channel_id=1, source_target_pairs={{0,4},{4,0},{8,12},{12,8},{16,20},{20,16},{24,28},{28,24},{1,5},{5... | collective-permute-start | bytes 2359304 | tf_op jit(solution)/shard_map/ppermute | solution.py:31
  110.3 14.4 %collective-permute-start.26 = (bf16[256,1024]{1,0:T(8,128)(2,1)S(1)}, bf16[256,1024]{1,0:T(8,128)(2,1)S(1)}, u32[]{:S(2)}, u32[]{:S(2)}) collective-permute-start(bf16[256,1024]{1,0:T(8,128)(2,1)S(1)} %slice.69.refs_4_), channel_id=1, source_target_pairs={{0,16},{4,20},{8,24},{12,28},{16,0},{20,4},{24,8},{28,12},{1,17},{... | collective-permute-start | bytes 1572872 | tf_op jit(solution)/shard_map/ppermute | solution.py:31
  112.3 13.9 %collective-permute-start.25 = (bf16[256,1024]{1,0:T(8,128)(2,1)S(1)}, bf16[256,1024]{1,0:T(8,128)(2,1)S(1)}, u32[]{:S(2)}, u32[]{:S(2)}) collective-permute-start(bf16[256,1024]{1,0:T(8,128)(2,1)S(1)} %slice.69.refs_4_), channel_id=1, source_target_pairs={{0,8},{4,12},{8,0},{12,4},{16,24},{20,28},{24,16},{28,20},{1,9},{5... | collective-permute-start | bytes 1572872 | tf_op jit(solution)/shard_map/ppermute | solution.py:31
  112.3 16.7 %collective-permute-start.19 = (bf16[256,256]{1,0:T(8,128)(2,1)S(1)}, bf16[256,256]{1,0:T(8,128)(2,1)S(1)}, u32[]{:S(2)}, u32[]{:S(2)}) collective-permute-start(bf16[256,256]{1,0:T(8,128)(2,1)S(1)} %get-tuple-element.35), channel_id=1, source_target_pairs={{0,3},{1,2},{2,1},{3,0},{4,7},{5,6},{6,5},{7,4},{8,11},{9,10},{10,... | collective-permute-start | bytes 393224 | tf_op jit(solution)/shard_map/ppermute | solution.py:31
  124.7 13.2 %collective-permute-start.27 = (bf16[128,1024]{1,0:T(8,128)(2,1)S(1)}, bf16[128,1024]{1,0:T(8,128)(2,1)S(1)}, u32[]{:S(2)}, u32[]{:S(2)}) collective-permute-start(bf16[128,1024]{1,0:T(8,128)(2,1)S(1)} %slice.70), channel_id=1, source_target_pairs={{0,8},{4,12},{8,0},{12,4},{16,24},{20,28},{24,16},{28,20},{1,9},{5... | collective-permute-start | bytes 786440 | tf_op jit(solution)/shard_map/ppermute | solution.py:31
  126.2 12.8 %collective-permute-start.28 = (bf16[128,1024]{1,0:T(8,128)(2,1)S(1)}, bf16[128,1024]{1,0:T(8,128)(2,1)S(1)}, u32[]{:S(2)}, u32[]{:S(2)}) collective-permute-start(bf16[128,1024]{1,0:T(8,128)(2,1)S(1)} %slice.71), channel_id=1, source_target_pairs={{0,16},{4,20},{8,24},{12,28},{16,0},{20,4},{24,8},{28,12},{1,17},{... | collective-permute-start | bytes 786440 | tf_op jit(solution)/shard_map/ppermute | solution.py:31
  126.7 8.1 %collective-permute-start.18 = (bf16[256,256]{1,0:T(8,128)(2,1)S(1)}, bf16[256,256]{1,0:T(8,128)(2,1)S(1)}, u32[]{:S(2)}, u32[]{:S(2)}) collective-permute-start(bf16[256,256]{1,0:T(8,128)(2,1)S(1)} %get-tuple-element.36), channel_id=1, source_target_pairs={{0,2},{1,3},{2,0},{3,1},{4,6},{5,7},{6,4},{7,5},{8,10},{9,11},{10,... | collective-permute-start | bytes 393224 | tf_op jit(solution)/shard_map/ppermute | solution.py:31
  129.0 6.3 %collective-permute-start.17 = (bf16[256,256]{1,0:T(8,128)(2,1)S(1)}, bf16[256,256]{1,0:T(8,128)(2,1)S(1)}, u32[]{:S(2)}, u32[]{:S(2)}) collective-permute-start(bf16[256,256]{1,0:T(8,128)(2,1)S(1)} %get-tuple-element.40), channel_id=1, source_target_pairs={{0,1},{1,0},{2,3},{3,2},{4,5},{5,4},{6,7},{7,6},{8,9},{9,8},{10,11... | collective-permute-start | bytes 393224 | tf_op jit(solution)/shard_map/ppermute | solution.py:31
  138.0 4.1 %collective-permute-start.29 = (bf16[256,1024]{1,0:T(8,128)(2,1)S(1)}, bf16[256,1024]{1,0:T(8,128)(2,1)S(1)}, u32[]{:S(2)}, u32[]{:S(2)}) collective-permute-start(bf16[256,1024]{1,0:T(8,128)(2,1)S(1)} %slice.69.refs_4_), channel_id=1, source_target_pairs={{0,4},{4,0},{8,12},{12,8},{16,20},{20,16},{24,28},{28,24},{1,5},{5... | collective-permute-start | bytes 1572872 | tf_op jit(solution)/shard_map/ppermute | solution.py:31
  138.5 3.7 %collective-permute-start.30 = (bf16[256,1024]{1,0:T(8,128)(2,1)S(1)}, bf16[256,1024]{1,0:T(8,128)(2,1)S(1)}, u32[]{:S(2)}, u32[]{:S(2)}) collective-permute-start(bf16[256,1024]{1,0:T(8,128)(2,1)S(1)} %collective-permute-done.25.refs_5_), channel_id=1, source_target_pairs={{0,4},{4,0},{8,12},{12,8},{16,20},{20,16},{24,28},{28,24},{1,5},{5... | collective-permute-start | bytes 1572872 | tf_op jit(solution)/shard_map/ppermute | solution.py:31
  139.0 13.9 %collective-permute-start.24 = (bf16[256,1024]{1,0:T(8,128)(2,1)S(1)}, bf16[256,1024]{1,0:T(8,128)(2,1)S(1)}, u32[]{:S(2)}, u32[]{:S(2)}) collective-permute-start(bf16[256,1024]{1,0:T(8,128)(2,1)S(1)} %first_norm.1.refs_1_.normed_ref), channel_id=1, source_target_pairs={{0,1},{1,0},{2,3},{3,2},{4,5},{5,4},{6,7},{7,6},{8,9},{9,8},{10,11... | collective-permute-start | bytes 1572872 | tf_op jit(solution)/shard_map/ppermute | solution.py:31
  157.5 13.1 %collective-permute-start.34 = (bf16[256,1024]{1,0:T(8,128)(2,1)S(1)}, bf16[256,1024]{1,0:T(8,128)(2,1)S(1)}, u32[]{:S(2)}, u32[]{:S(2)}) collective-permute-start(bf16[256,1024]{1,0:T(8,128)(2,1)S(1)} %feed_partner.1), channel_id=1, source_target_pairs={{0,1},{1,0},{2,3},{3,2},{4,5},{5,4},{6,7},{7,6},{8,9},{9,8},{10,11... | collective-permute-start | bytes 1572872 | tf_op jit(solution)/shard_map/ppermute | solution.py:31
  (15 other events, 211.8 us)

commit v6 on v5

--- a/solution.py
+++ b/solution.py
@@ -240,86 +240,122 @@
     return 0.5 * values * (1.0 + lax.erf(values * math.sqrt(0.5)))
 
 
-def feed_kernel(layout, *refs):
-    count = len(layout)
-    place_ref, rows_ref, up_near_ref, down_near_ref = refs[:4]
-    pieces = refs[4 : 4 + count]
-    sum_ref, up_ref, down_ref, wide_ref, units_ref, total_ref, near_sems, sems = refs[4 + count :]
-    tok = place_ref[0]
+CHUNK = 512
+
+
+def feed_chunk(rows, up, down_ref, wide_ref, units_ref):
+    wide_ref[...] = jnp.dot(rows, up, preferred_element_type=F32)
+    for row in range(0, rows.shape[0], STRIP):
+        strip = slice(row, row + STRIP)
+        units_ref[strip] = gelu(wide_ref[strip]).astype(BF16)
+    return jnp.dot(units_ref[...], down_ref[...], preferred_element_type=F32)
+
+
+def far_copies(tok, held_ref, core_ref, up_ref, down_ref, sems):
     block = 128
-    chunk = wide_ref.shape[2]
-    chunks = up_ref.shape[2] // chunk
-    near = []
-    for index in range(chunks):
-        at = slice(index * chunk, (index + 1) * chunk)
-        near.append(
-            (
-                pltpu.make_async_copy(up_near_ref.at[:, at], up_ref.at[0, :, at], near_sems.at[0, index]),
-                pltpu.make_async_copy(down_near_ref.at[at], down_ref.at[0, at], near_sems.at[1, index]),
-            )
-        )
-    far = []
-    for (flip, part), piece in zip(layout, pieces):
-        at = pl.ds(pl.multiple_of((tok ^ flip) * block, block), block)
-        if part in (None, 0):
-            far.append(pltpu.make_async_copy(piece.at[0:block], up_ref.at[1, at], sems.at[len(far)]))
-        if part in (None, 1):
-            shift = block if part is None else 0
-            far.append(pltpu.make_async_copy(piece.at[shift : shift + block], down_ref.at[1, at], sems.at[len(far)]))
-    for pair in near:
-        for copy in pair:
-            copy.start()
-    for copy in far:
+    copies = []
+    for side, piece in enumerate((held_ref, core_ref)):
+        for index in range(4):
+            at = pl.ds(pl.multiple_of((tok ^ (2 * index + side)) * block, block), block)
+            for part, target in enumerate((up_ref, down_ref)):
+                source = piece.at[pl.ds((2 * index + part) * block, block)]
+                copies.append(pltpu.make_async_copy(source, target.at[at], sems.at[len(copies)]))
+    return copies
+
+
+def feed_near_kernel(rows_ref, up_ref, down_ref, sum_ref, wide_ref, units_ref):
+    rows = rows_ref[...]
+    for index in range(up_ref.shape[1] // CHUNK):
+        at = slice(index * CHUNK, (index + 1) * CHUNK)
+        product = feed_chunk(rows, up_ref[:, at], down_ref.at[at], wide_ref.at[index % 2], units_ref.at[index % 2])
+        if index == 0:
+            sum_ref[...] = product
+        else:
+            sum_ref[...] += product
+
+
+def feed_far_kernel(
+    place_ref, rows_ref, near_ref, held_ref, core_ref, sum_ref, up_ref, down_ref, wide_ref, units_ref, total_ref, sems
+):
+    copies = far_copies(place_ref[0], held_ref, core_ref, up_ref, down_ref, sems)
+    for copy in copies:
         copy.start()
     rows = rows_ref[...]
-    for side in range(2):
-        for index in range(chunks):
-            at = slice(index * chunk, (index + 1) * chunk)
-            slot = index % 2
-            if side == 0:
-                near[index][0].wait()
-            elif index == 0:
-                for copy in far:
-                    copy.wait()
-            wide_ref[slot] = jnp.dot(rows, up_ref[side, :, at], preferred_element_type=F32)
-            for row in range(0, rows.shape[0], STRIP):
-                strip = slice(row, row + STRIP)
-                units_ref[slot, strip] = gelu(wide_ref[slot, strip]).astype(BF16)
-            if side == 0:
-                near[index][1].wait()
-            product = jnp.dot(units_ref[slot], down_ref[side, at], preferred_element_type=F32)
-            if side == 0 and index == 0:
-                total_ref[...] = product
-            elif side == 1 and index == chunks - 1:
-                sum_ref[...] = (total_ref[...] + product).astype(sum_ref.dtype)
-            else:
-                total_ref[...] += product
-
-
-def feed(place, rows, up_weight, down_weight, pieces, dtype, name):
+    total_ref[...] = near_ref[...]
+    for copy in copies:
+        copy.wait()
+    for index in range(up_ref.shape[1] // CHUNK):
+        at = slice(index * CHUNK, (index + 1) * CHUNK)
+        slot = index % 2
+        total_ref[...] += feed_chunk(rows, up_ref[:, at], down_ref.at[at], wide_ref.at[slot], units_ref.at[slot])
+    sum_ref[...] = total_ref[...].astype(sum_ref.dtype)
+
+
+def feed_kernel(
+    place_ref, rows_ref, up_near_ref, down_near_ref, held_ref, core_ref, sum_ref, up_ref, down_ref, wide_ref, units_ref, sems
+):
+    copies = far_copies(place_ref[0], held_ref, core_ref, up_ref, down_ref, sems)
+    for copy in copies:
+        copy.start()
+    feed_near_kernel(rows_ref, up_near_ref, down_near_ref, sum_ref, wide_ref, units_ref)
+    rows = rows_ref[...]
+    for copy in copies:
+        copy.wait()
+    for index in range(up_ref.shape[1] // CHUNK):
+        at = slice(index * CHUNK, (index + 1) * CHUNK)
+        slot = index % 2
+        sum_ref[...] += feed_chunk(rows, up_ref[:, at], down_ref.at[at], wide_ref.at[slot], units_ref.at[slot])
+
+
+def feed_scratch(count):
+    return [pltpu.VMEM((2, count, CHUNK), F32), pltpu.VMEM((2, count, CHUNK), BF16)]
+
+
+def feed_near(rows, up_weight, down_weight):
+    return pl.pallas_call(
+        feed_near_kernel,
+        out_shape=jax.ShapeDtypeStruct(rows.shape, F32),
+        in_specs=[VMEM] * 3,
+        out_specs=VMEM,
+        scratch_shapes=feed_scratch(rows.shape[0]),
+        compiler_params=pltpu.CompilerParams(vmem_limit_bytes=14 * MIB),
+        cost_estimate=SHORT,
+        name="feed_near",
+    )(rows, up_weight, down_weight)
+
+
+def feed_far(place, rows, near, pieces):
+    count, width = rows.shape
+    units = pieces[0].shape[0]
+    return pl.pallas_call(
+        feed_far_kernel,
+        out_shape=jax.ShapeDtypeStruct((count, width), BF16),
+        in_specs=[SMEM] + [VMEM] * 2 + [ANY] * 2,
+        out_specs=VMEM,
+        scratch_shapes=[pltpu.VMEM((width, units), BF16), pltpu.VMEM((units, width), BF16)]
+        + feed_scratch(count)
+        + [pltpu.VMEM((count, width), F32), pltpu.SemaphoreType.DMA((16,))],
+        compiler_params=pltpu.CompilerParams(vmem_limit_bytes=14 * MIB),
+        cost_estimate=SHORT,
+        name="feed_far",
+    )(place, rows, near, *pieces)
+
+
+def feed(place, rows, up_weight, down_weight, pieces):
     count, width = rows.shape
     units = up_weight.shape[1]
-    chunk = 512
-    layout = tuple((flip, part) for flip, part, _ in pieces)
-    copies = sum(2 if part is None else 1 for _, part in layout)
     return pl.pallas_call(
-        functools.partial(feed_kernel, layout),
-        out_shape=jax.ShapeDtypeStruct((count, width), dtype),
-        in_specs=[SMEM, VMEM, ANY, ANY] + [ANY] * len(pieces),
+        feed_kernel,
+        out_shape=jax.ShapeDtypeStruct((count, width), F32),
+        in_specs=[SMEM] + [VMEM] * 3 + [ANY] * 2,
         out_specs=VMEM,
-        scratch_shapes=[
-            pltpu.VMEM((2, width, units), BF16),
-            pltpu.VMEM((2, units, width), BF16),
-            pltpu.VMEM((2, count, chunk), F32),
-            pltpu.VMEM((2, count, chunk), BF16),
-            pltpu.VMEM((count, width), F32),
-            pltpu.SemaphoreType.DMA((2, units // chunk)),
-            pltpu.SemaphoreType.DMA((copies,)),
-        ],
-        compiler_params=pltpu.CompilerParams(vmem_limit_bytes=20 * MIB),
+        scratch_shapes=[pltpu.VMEM((width, units), BF16), pltpu.VMEM((units, width), BF16)]
+        + feed_scratch(count)
+        + [pltpu.SemaphoreType.DMA((16,))],
+        compiler_params=pltpu.CompilerParams(vmem_limit_bytes=18 * MIB),
         cost_estimate=SHORT,
-        name=name,
-    )(place, rows, up_weight, down_weight, *[value for _, _, value in pieces])
+        name="feed_own",
+    )(place, rows, up_weight, down_weight, *pieces)
 
 
 def finish_kernel(normed_ref, near_ref, far_ref, gain_ref, bias_ref, out_ref):
@@ -455,21 +491,21 @@
 
     queries = gathered_queries(dec_query)
     partial = decode_partial(queries, kv_cache, piece_req, piece_used)
+    early = {2: queries[1:], 3: [partial]}
     from_below, from_above = [], []
     rising = falling = hidden_in
     for step in range(1, kvs):
+        rising, falling = after(rising, *early.get(step, ())), after(falling, *early.get(step, ()))
         links = range(step - 1, kvs - 1)
         rising = lax.ppermute(rising, "kv", [(i, i + 1) for i in links])
         falling = lax.ppermute(falling, "kv", [(kvs - 1 - i, kvs - 2 - i) for i in links])
         from_below.append(rising)
         from_above.append(falling)
-        if step == 2:
-            rising, falling = after(rising, partial), after(falling, partial)
-    dec_parts = exchanged_partials(partial, dec_query.shape[0])
-
-    out_part = after(eighth(out_weight), from_below[1], from_above[1])
+
     feed_part = jnp.concatenate([eighth(up_weight), eighth(down_weight), eighth(out_weight)], axis=0)
-    feed_here = swapped(after(feed_part, from_below[1], from_above[1]), "kv", 2)
+    feed_inner = lax.ppermute(after(feed_part, from_below[1], from_above[1], partial), "kv", [(0, 2), (3, 1)])
+    feed_outer = lax.ppermute(after(feed_part, rising, falling, feed_inner), "kv", [(1, 3), (2, 0)])
+    out_part = after(eighth(out_weight), rising, falling)
     out_near, out_far = swapped(out_part, "kv", 1), swapped(out_part, "kv", 3)
 
     order = jnp.arange(stretch_len.shape[0])
@@ -477,40 +513,44 @@
     starts = (ends - stretch_len)[None, :]
     ends = ends[None, :]
 
-    shards = [after(hidden_in, *dec_parts)] + from_below + from_above
+    shards = [after(hidden_in, feed_inner)] + from_below + from_above
     query, keyval, top, bottom = project(place, jnp.transpose(qkv_weight, (1, 0, 2)), shards)
     before = lax.ppermute(bottom, "tok", [(i, i + 1) for i in range(toks - 1)])
     behind = lax.ppermute(top, "tok", [(i + 1, i) for i in range(toks - 1)])
     window = (place, starts, ends, query, before, keyval, behind, rows)
     parts = [None] * kvs
     parts[3], parts[2] = attend_blocks(*window, (3, 2), "attend_far")
-    feed_here = after(feed_here, parts[3], parts[2])
-    parts[3], parts[2] = swapped(parts[3], "kv", 3), swapped(parts[2], "kv", 2)
     depth = out_part.shape[0]
+    inner = (kv == 1) | (kv == 2)
+    feed_here = jnp.where(inner, feed_inner, after(feed_outer, parts[3], parts[2]))
     out_here = jnp.stack([out_near, feed_here[-depth:], out_far])
     feed_here = feed_here[:-depth]
+    parts[3], parts[2] = swapped(parts[3], "kv", 3), swapped(parts[2], "kv", 2)
     out_x, out_y = swapped(out_here, "tok", 2), swapped(out_here, "tok", 4)
-    feed_x, feed_y = swapped(feed_here, "tok", 2), swapped(feed_here, "tok", 4)
     window = (place, starts, ends, after(query, out_here), before, keyval, behind, rows)
     parts[1], parts[0] = attend_blocks(*window, (1, 0), "attend_near")
-    out_all = jnp.stack([out_here, out_x, out_y, swapped(after(out_y, parts[0]), "tok", 2)])
+    feed_here = after(feed_here, parts[0])
+    parts[1] = swapped(parts[1], "kv", 1)
+    out_all = jnp.stack([out_here, out_x, out_y, swapped(after(out_y, parts[0], parts[3], parts[2]), "tok", 2)])
     out_core = swapped(out_all, "tok", 1)
-    half = feed_here.shape[0] // 2
-    far_up = swapped(after(feed_y, parts[0])[:half], "tok", 2)
-    far_down = swapped(after(feed_x, parts[0])[half:], "tok", 4)
-    parts[1] = swapped(parts[1], "kv", 1)
+    feed_x, feed_y = swapped(feed_here, "tok", 2), swapped(feed_here, "tok", 4)
     out_pieces = [((0, 2, 4, 6), out_all), ((1, 3, 5, 7), out_core)]
     normed = first_norm(place, hidden_in, out_weight, ln1_gain[None, :], ln1_bias[None, :], parts, out_pieces)
 
     partner = swapped(normed, "kv", 1)
-    held = [(0, None, feed_here), (2, None, feed_x), (4, None, feed_y), (6, 0, far_up), (6, 1, far_down)]
-    feed_pieces = held + [(flip ^ 1, part, swapped(after(value, normed), "tok", 1)) for flip, part, value in held]
-    away = feed(place, partner, up_weight, down_weight, feed_pieces, BF16, "feed_partner")
+    half = feed_here.shape[0] // 2
+    far_up = swapped(after(feed_y, normed)[:half], "tok", 2)
+    far_down = swapped(after(feed_x, normed)[half:], "tok", 4)
+    held = jnp.concatenate([feed_here, feed_x, feed_y, far_up, far_down], axis=0)
+    near_away = feed_near(partner, up_weight, down_weight)
+    feed_pieces = (held, swapped(after(held, partner), "tok", 1))
+    away = feed_far(place, partner, near_away, feed_pieces)
     arrived = swapped(away, "kv", 1)
-    mine = feed(place, after(normed, away), up_weight, down_weight, feed_pieces, F32, "feed_own")
+    dec_parts = exchanged_partials(after(partial, away), dec_query.shape[0])
+    mine = feed(place, after(normed, away), up_weight, down_weight, feed_pieces)
     prefill_out = finish(normed, mine, arrived, ln2_gain[None, :], ln2_bias[None, :])
 
-    return prefill_out, merged_partials(dec_parts)
+    return prefill_out, merged_partials(after(tuple(dec_parts), mine))
 
 
 def extended(value, sides, width):

time: 172 us -> 150 us (0.87)
  waiting for transfers between devices: 78.2 us -> 58.3 us
  starting transfers between devices: 56.9 us -> 54.2 us
    ppermute x27 -> x22, waiting for transfers between devices: 63.6 us -> 41 us  [swapped(): return lax.ppermute(value, axis, [(i, i ^ flip) for i in range(count)])]
    ppermute x3, waiting for transfers between devices: 3.36 us -> 17.3 us  [routed_body(): lax.ppermute(falling, 'kv', [(kvs - 1 - i, kvs - 2 - i) for i in links])]
    ppermute x3, waiting for transfers between devices: 10.2 us -> 0.01 us  [routed_body(): rising = lax.ppermute(rising, 'kv', [(i, i + 1) for i in links])]
    ppermute x27 -> x22, starting transfers between devices: 44.1 us -> 37.4 us  [swapped(): return lax.ppermute(value, axis, [(i, i ^ flip) for i in range(count)])]
    ppermute x0 -> x2, starting transfers between devices: none -> 3.92 us  [the longest x1 2.64 us: routed_body(): lax.ppermute(after(feed_part, from_below[1], from_above[1], partial), 'kv...]
    pallas_call x2 -> x3, Pallas kernels: 9.16 us -> 8.03 us  [the longest x1 3.9 us: feed(): pl.pallas_call(feed_kernel, out_shape=jax.ShapeDtypeStruct((count, width)...]
  transfers between devices with their start and end apart: 35 -> 32, of which waited for: 14 -> 15; matrix products, arithmetic and copies ran while one was open for 2% -> 3% of each run, Pallas kernels for 14% -> 17%
where the time goes in v6:
time: 150 us
  waiting for transfers between devices  58.3 us (39%)
  starting transfers between devices  54.2 us (36%)
  Pallas kernels  29 us (19%)
  local copies, waits for them, and re-layouts  4.13 us (3%)
  other arithmetic  3 us (2%)
    ppermute x22, waiting for transfers between devices, swapped(): return lax.ppermute(value, axis, [(i, i ^ flip) for i in range(count)])  41 us
    ppermute x22, starting transfers between devices, swapped(): return lax.ppermute(value, axis, [(i, i ^ flip) for i in range(count)])  37.4 us
    ppermute x3, waiting for transfers between devices, routed_body(): lax.ppermute(falling, 'kv', [(kvs - 1 - i, kvs - 2 - i) for i in links])  17.3 us
    pallas_call x2, Pallas kernels, attend_blocks(): pl.pallas_call(functools.partial(attend_kernel, flips), out_shape=tuple((...  10.3 us
    ppermute x3, starting transfers between devices, routed_body(): rising = lax.ppermute(rising, 'kv', [(i, i + 1) for i in links])  6.47 us
    pallas_call x1, Pallas kernels, feed(): pl.pallas_call(feed_kernel, out_shape=jax.ShapeDtypeStruct((count, width)...  3.9 us
    ppermute x3, starting transfers between devices, routed_body(): lax.ppermute(falling, 'kv', [(kvs - 1 - i, kvs - 2 - i) for i in links])  3.88 us
    pallas_call x1, Pallas kernels, decode(): pl.pallas_call(decode_kernel, grid=(pieces,), out_shape=jax.ShapeDtypeStr...  3.78 us
  transfers between devices with their start and end apart: 32, of which 15 were waited for; matrix products, arithmetic and copies ran while one was open for 3% of the time, Pallas kernels for 17%

profile of v6, /device:TPU:0, one launch (start us, length us, event | category | flops | bytes accessed | tf_op | source)
XLA Modules:
  0.0 149.8 jit_solution(3628797201499688640)
XLA Ops:
  0.7 5.1 %collective-permute-start = (bf16[256,1024]{1,0:T(8,128)(2,1)}, bf16[256,1024]{1,0:T(8,128)(2,1)S(1)}, u32[]{:S(2)}, u32[]{:S(2)}) collective-permute-start(bf16[256,1024]{1,0:T(8,128)(2,1)} %hidden_ref.1), channel_id=1, source_target_pairs={{0,1},{1,2},{2,3},{4,5},{5,6},{6,7},{8,9},{9,10},{10,11},{12,13},{... | collective-permute-start | bytes 1572872 | tf_op jit(solution)/shard_map/ppermute | solution.py:500
  7.1 2.7 %collective-permute-start.1 = (bf16[2,1024]{1,0:T(2,128)(2,1)}, bf16[2,1024]{1,0:T(2,128)(2,1)S(1)}, u32[]{:S(2)}, u32[]{:S(2)}) collective-permute-start(bf16[2,1024]{1,0:T(2,128)(2,1)} %param.24), channel_id=1, source_target_pairs={{0,1},{1,0},{2,3},{3,2},{4,5},{5,4},{6,7},{7,6},{8,9},{9,8},{10,11... | collective-permute-start | bytes 12296 | tf_op jit(solution)/shard_map/ppermute | solution.py:31
  9.8 2.6 %collective-permute-start.2 = (bf16[2,1024]{1,0:T(2,128)(2,1)}, bf16[2,1024]{1,0:T(2,128)(2,1)S(1)}, u32[]{:S(2)}, u32[]{:S(2)}) collective-permute-start(bf16[2,1024]{1,0:T(2,128)(2,1)} %param.24), channel_id=1, source_target_pairs={{0,2},{1,3},{2,0},{3,1},{4,6},{5,7},{6,4},{7,5},{8,10},{9,11},{10,... | collective-permute-start | bytes 12296 | tf_op jit(solution)/shard_map/ppermute | solution.py:31
  13.4 7.9 %collective-permute-done.1 = bf16[2,1024]{1,0:T(2,128)(2,1)S(1)} collective-permute-done((bf16[2,1024]{1,0:T(2,128)(2,1)}, bf16[2,1024]{1,0:T(2,128)(2,1)S(1)}, u32[]{:S(2)}, u32[]{:S(2)}) %collective-permute-start.1) | collective-permute-done | bytes 4128 | tf_op jit(solution)/shard_map/ppermute | solution.py:31
  27.3 1.9 %copy-done.2 = bf16[2,1,6,128,1024]{4,3,2,1,0:T(8,128)(2,1)S(1)} copy-done((bf16[2,1,6,128,1024]{4,3,2,1,0:T(8,128)(2,1)S(1)}, bf16[2,1,6,128,1024]{4,3,2,1,0:T(8,128)(2,1)}, u32[]{:S(2)}) %copy-start.2) | copy-done | bytes 3145752
  29.2 3.8 %decode.1 = f32[3,8,1024]{2,1,0:T(8,128)S(1)} custom-call(s32[6]{0:T(128)S(1)} %fusion.12.slot_ref, s32[6]{0:T(128)S(1)} %bitcast.148, f32[8,1024]{1,0:T(8,128)S(1)} %maximum_convert_fusion.query_ref, bf16[2,1,6,128,1024]{4,3,2,1,0:T(8,128)(2,1)S(1)} %copy-done.2), custom_call_target="tpu_custom_call" | custom-call | flops 1 | bytes 1 | tf_op jit(solution)/shard_map/decode/pallas_call | solution.py:424
  33.0 5.8 %collective-permute-done.6.refs_5_ = bf16[256,1024]{1,0:T(8,128)(2,1)S(1)} collective-permute-done((bf16[256,1024]{1,0:T(8,128)(2,1)S(1)}, bf16[256,1024]{1,0:T(8,128)(2,1)S(1)}, u32[]{:S(2)}, u32[]{:S(2)}) %collective-permute-start.6) | collective-permute-done | bytes 524320 | tf_op jit(solution)/shard_map/ppermute | solution.py:501
  38.8 2.6 %collective-permute-start.7 = (bf16[288,1024]{1,0:T(8,128)(2,1)}, bf16[288,1024]{1,0:T(8,128)(2,1)S(1)}, u32[]{:S(2)}, u32[]{:S(2)}) collective-permute-start(bf16[288,1024]{1,0:T(8,128)(2,1)} %pad_maximum_fusion.1), channel_id=1, source_target_pairs={{0,2},{3,1},{4,6},{7,5},{8,10},{11,9},{12,14},{15,13},{16,18},{19,... | collective-permute-start | bytes 1769480 | tf_op jit(solution)/shard_map/ppermute | solution.py:506
  43.5 11.5 %collective-permute-done.9.refs_6_ = bf16[256,1024]{1,0:T(8,128)(2,1)S(1)} collective-permute-done((bf16[256,1024]{1,0:T(8,128)(2,1)S(1)}, bf16[256,1024]{1,0:T(8,128)(2,1)S(1)}, u32[]{:S(2)}, u32[]{:S(2)}) %collective-permute-start.9) | collective-permute-done | bytes 524320 | tf_op jit(solution)/shard_map/ppermute | solution.py:501
  56.3 3.3 %project.1 = (bf16[1024,256]{1,0:T(8,128)(2,1)S(1)}, bf16[1024,512]{1,0:T(8,128)(2,1)S(1)}, bf16[256,512]{1,0:T(8,128)(2,1)S(1)}, bf16[256,512]{1,0:T(8,128)(2,1)}) custom-call(s32[2]{0:T(128)S(1)} %pad_add_fusion.place_ref, bf16[3,1024,256]{2,1,0:T(8,128)(2,1)S(1)} %bitcast.141, bf16[256,1024]{1,0:T(8,128)(2,1)S(1)} %copy-done.3, ...), custom_call_target="tpu_custom_call" | custom-call | flops 1 | bytes 1 | tf_op jit(solution)/shard_map/project/pallas_call | solution.py:85
  62.4 2.8 %collective-permute-start.14 = (bf16[32,1024]{1,0:T(8,128)(2,1)}, bf16[32,1024]{1,0:T(8,128)(2,1)S(1)}, u32[]{:S(2)}, u32[]{:S(2)}) collective-permute-start(bf16[32,1024]{1,0:T(8,128)(2,1)} %copy-done.13), channel_id=1, source_target_pairs={{0,3},{1,2},{2,1},{3,0},{4,7},{5,6},{6,5},{7,4},{8,11},{9,10},{10,... | collective-permute-start | bytes 196616 | tf_op jit(solution)/shard_map/ppermute | solution.py:31
  65.1 2.2 %collective-permute-start.10 = (bf16[32,1024]{1,0:T(8,128)(2,1)}, bf16[32,1024]{1,0:T(8,128)(2,1)S(1)}, u32[]{:S(2)}, u32[]{:S(2)}) collective-permute-start(bf16[32,1024]{1,0:T(8,128)(2,1)} %copy-done.13), channel_id=1, source_target_pairs={{0,1},{1,0},{2,3},{3,2},{4,5},{5,4},{6,7},{7,6},{8,9},{9,8},{10,11... | collective-permute-start | bytes 196616 | tf_op jit(solution)/shard_map/ppermute | solution.py:31
  67.4 5.1 %attend_far.1 = (bf16[256,256]{1,0:T(8,128)(2,1)S(1)}, bf16[256,256]{1,0:T(8,128)(2,1)S(1)}) custom-call(s32[2]{0:T(128)S(1)} %pad_add_fusion.place_ref, s32[1,48]{1,0:T(1,128)S(1)} %subtract_bitcast_fusion.starts_ref, s32[1,48]{1,0:T(1,128)S(1)} %bitcast.146, bf16[1024,256]{1,0:T(8,128)(2,1)S(1)} %get-tuple-element.46.query_ref, ...), custom_call_target="tpu_custom_call" | custom-call | flops 1 | bytes 1 | tf_op jit(solution)/shard_map/attend_far/pallas_call | solution.py:174
  73.7 5.4 %collective-permute-start.19 = (bf16[3,32,1024]{2,1,0:T(8,128)(2,1)S(1)}, bf16[3,32,1024]{2,1,0:T(8,128)(2,1)S(1)}, u32[]{:S(2)}, u32[]{:S(2)}) collective-permute-start(bf16[3,32,1024]{2,1,0:T(8,128)(2,1)S(1)} %get-tuple-element.61), channel_id=1, source_target_pairs={{0,16},{4,20},{8,24},{12,28},{16,0},{20,4},{24,8},{28,12},{1,17},{... | collective-permute-start | bytes 589832 | tf_op jit(solution)/shard_map/ppermute | solution.py:31
  79.2 2.1 %collective-permute-start.16 = (bf16[256,256]{1,0:T(8,128)(2,1)S(1)}, bf16[256,256]{1,0:T(8,128)(2,1)S(1)}, u32[]{:S(2)}, u32[]{:S(2)}) collective-permute-start(bf16[256,256]{1,0:T(8,128)(2,1)S(1)} %get-tuple-element.44), channel_id=1, source_target_pairs={{0,2},{1,3},{2,0},{3,1},{4,6},{5,7},{6,4},{7,5},{8,10},{9,11},{10,... | collective-permute-start | bytes 393224 | tf_op jit(solution)/shard_map/ppermute | solution.py:31
  81.2 2.7 %collective-permute-start.17 = (bf16[256,256]{1,0:T(8,128)(2,1)S(1)}, bf16[256,256]{1,0:T(8,128)(2,1)S(1)}, u32[]{:S(2)}, u32[]{:S(2)}) collective-permute-start(bf16[256,256]{1,0:T(8,128)(2,1)S(1)} %get-tuple-element.43), channel_id=1, source_target_pairs={{0,3},{1,2},{2,1},{3,0},{4,7},{5,6},{6,5},{7,4},{8,11},{9,10},{10,... | collective-permute-start | bytes 393224 | tf_op jit(solution)/shard_map/ppermute | solution.py:31
  84.5 5.2 %attend_near.1 = (bf16[256,256]{1,0:T(8,128)(2,1)S(1)}, bf16[256,256]{1,0:T(8,128)(2,1)S(1)}) custom-call(s32[2]{0:T(128)S(1)} %pad_add_fusion.place_ref, s32[1,48]{1,0:T(1,128)S(1)} %subtract_bitcast_fusion.starts_ref, s32[1,48]{1,0:T(1,128)S(1)} %bitcast.147, bf16[1024,256]{1,0:T(8,128)(2,1)S(1)} %get-tuple-element.46.query_ref, ...), custom_call_target="tpu_custom_call" | custom-call | flops 1 | bytes 1 | tf_op jit(solution)/shard_map/attend_near/pallas_call | solution.py:174
  89.8 2.2 %collective-permute-done.16.refs_2_ = bf16[256,256]{1,0:T(8,128)(2,1)S(1)} collective-permute-done((bf16[256,256]{1,0:T(8,128)(2,1)S(1)}, bf16[256,256]{1,0:T(8,128)(2,1)S(1)}, u32[]{:S(2)}, u32[]{:S(2)}) %collective-permute-start.16) | collective-permute-done | bytes 131104 | tf_op jit(solution)/shard_map/ppermute | solution.py:31
  92.7 5.2 %collective-permute-done.20 = bf16[3,32,1024]{2,1,0:T(8,128)(2,1)S(1)} collective-permute-done((bf16[3,32,1024]{2,1,0:T(8,128)(2,1)S(1)}, bf16[3,32,1024]{2,1,0:T(8,128)(2,1)S(1)}, u32[]{:S(2)}, u32[]{:S(2)}) %collective-permute-start.20) | collective-permute-done | bytes 196640 | tf_op jit(solution)/shard_map/ppermute | solution.py:31
  100.0 3.4 %collective-permute-start.15 = (bf16[256,256]{1,0:T(8,128)(2,1)S(1)}, bf16[256,256]{1,0:T(8,128)(2,1)S(1)}, u32[]{:S(2)}, u32[]{:S(2)}) collective-permute-start(bf16[256,256]{1,0:T(8,128)(2,1)S(1)} %get-tuple-element.48), channel_id=1, source_target_pairs={{0,1},{1,0},{2,3},{3,2},{4,5},{5,4},{6,7},{7,6},{8,9},{9,8},{10,11... | collective-permute-start | bytes 393224 | tf_op jit(solution)/shard_map/ppermute | solution.py:31
  103.5 3.6 %collective-permute-done.15.refs_1_ = bf16[256,256]{1,0:T(8,128)(2,1)S(1)} collective-permute-done((bf16[256,256]{1,0:T(8,128)(2,1)S(1)}, bf16[256,256]{1,0:T(8,128)(2,1)S(1)}, u32[]{:S(2)}, u32[]{:S(2)}) %collective-permute-start.15) | collective-permute-done | bytes 131104 | tf_op jit(solution)/shard_map/ppermute | solution.py:31
  107.1 2.4 %first_norm.1.rows_ref.normed_ref = bf16[256,1024]{1,0:T(8,128)(2,1)S(1)} custom-call(s32[2]{0:T(128)S(1)} %pad_add_fusion.place_ref, bf16[256,1024]{1,0:T(8,128)(2,1)S(1)} %copy-done.3, bf16[256,1024]{1,0:T(8,128)(2,1)S(1)} %copy-done.5, f32[1,1024]{1,0:T(1,128)S(1)} %bitcast.144, f32[1,1024]{1,0:T(1,128)S(1)} %bitcast.145, ...), custom_call_target="tpu_custom_call" | custom-call | flops 1 | bytes 1 | tf_op jit(solution)/shard_map/first_norm/pallas_call | solution.py:222
  109.5 1.8 %collective-permute-start.22 = (bf16[256,1024]{1,0:T(8,128)(2,1)S(1)}, bf16[256,1024]{1,0:T(8,128)(2,1)S(1)}, u32[]{:S(2)}, u32[]{:S(2)}) collective-permute-start(bf16[256,1024]{1,0:T(8,128)(2,1)S(1)} %first_norm.1.rows_ref.normed_ref), channel_id=1, source_target_pairs={{0,1},{1,0},{2,3},{3,2},{4,5},{5,4},{6,7},{7,6},{8,9},{9,8},{10,11... | collective-permute-start | bytes 1572872 | tf_op jit(solution)/shard_map/ppermute | solution.py:31
  114.3 6.1 %collective-permute-done.25 = bf16[128,1024]{1,0:T(8,128)(2,1)S(1)} collective-permute-done((bf16[128,1024]{1,0:T(8,128)(2,1)S(1)}, bf16[128,1024]{1,0:T(8,128)(2,1)S(1)}, u32[]{:S(2)}, u32[]{:S(2)}) %collective-permute-start.25) | collective-permute-done | bytes 262176 | tf_op jit(solution)/shard_map/ppermute | solution.py:31
  122.8 1.5 %feed_near.1.near_ref = f32[256,1024]{1,0:T(8,128)S(1)} custom-call(bf16[256,1024]{1,0:T(8,128)(2,1)S(1)} %collective-permute-done.22.rows_ref, bf16[1024,1024]{1,0:T(8,128)(2,1)S(1)} %copy-done.1, bf16[1024,1024]{1,0:T(8,128)(2,1)S(1)} %copy-done), custom_call_target="tpu_custom_call" | custom-call | flops 1 | bytes 1 | tf_op jit(solution)/shard_map/feed_near/pallas_call | solution.py:315
  124.3 2.6 %collective-permute-done.27.core_ref = bf16[1024,1024]{1,0:T(8,128)(2,1)S(1)} collective-permute-done((bf16[1024,1024]{1,0:T(8,128)(2,1)S(1)}, bf16[1024,1024]{1,0:T(8,128)(2,1)S(1)}, u32[]{:S(2)}, u32[]{:S(2)}) %collective-permute-start.27) | collective-permute-done | bytes 2097184 | tf_op jit(solution)/shard_map/ppermute | solution.py:31
  126.9 2.6 %feed_far.1 = bf16[256,1024]{1,0:T(8,128)(2,1)S(1)} custom-call(s32[2]{0:T(128)S(1)} %pad_add_fusion.place_ref, bf16[256,1024]{1,0:T(8,128)(2,1)S(1)} %collective-permute-done.22.rows_ref, f32[256,1024]{1,0:T(8,128)S(1)} %feed_near.1.near_ref, bf16[1024,1024]{1,0:T(8,128)(2,1)S(1)} %constant_dynamic-update-slice_fusion.held_ref, ...), custom_call_target="tpu_custom_call" | custom-call | flops 1 | bytes 1 | tf_op jit(solution)/shard_map/feed_far/pallas_call | solution.py:330
  129.6 2.2 %collective-permute-start.28 = (bf16[256,1024]{1,0:T(8,128)(2,1)S(1)}, bf16[256,1024]{1,0:T(8,128)(2,1)S(1)}, u32[]{:S(2)}, u32[]{:S(2)}) collective-permute-start(bf16[256,1024]{1,0:T(8,128)(2,1)S(1)} %feed_far.1), channel_id=1, source_target_pairs={{0,1},{1,0},{2,3},{3,2},{4,5},{5,4},{6,7},{7,6},{8,9},{9,8},{10,11... | collective-permute-start | bytes 1572872 | tf_op jit(solution)/shard_map/ppermute | solution.py:31
  131.9 3.2 %collective-permute-start.30 = (f32[3,2,1024]{2,1,0:T(2,128)S(1)}, f32[3,2,1024]{2,1,0:T(2,128)S(1)}, u32[]{:S(2)}, u32[]{:S(2)}) collective-permute-start(f32[3,2,1024]{2,1,0:T(2,128)S(1)} %get-tuple-element.63), channel_id=1, source_target_pairs={{0,2},{1,3},{2,0},{3,1},{4,6},{5,7},{6,4},{7,5},{8,10},{9,11},{10,... | collective-permute-start | bytes 73736 | tf_op jit(solution)/shard_map/ppermute | solution.py:31
  136.2 3.9 %feed_own.1.near_ref = f32[256,1024]{1,0:T(8,128)S(1)} custom-call(s32[2]{0:T(128)S(1)} %pad_add_fusion.place_ref, bf16[256,1024]{1,0:T(8,128)(2,1)S(1)} %first_norm.1.rows_ref.normed_ref, bf16[1024,1024]{1,0:T(8,128)(2,1)S(1)} %copy-done.1, bf16[1024,1024]{1,0:T(8,128)(2,1)S(1)} %copy-done, ...), custom_call_target="tpu_custom_call" | custom-call | flops 1 | bytes 1 | tf_op jit(solution)/shard_map/feed_own/pallas_call | solution.py:347
  140.1 4.9 %collective-permute-done.29 = f32[3,2,1024]{2,1,0:T(2,128)S(1)} collective-permute-done((f32[3,2,1024]{2,1,0:T(2,128)S(1)}, f32[3,2,1024]{2,1,0:T(2,128)S(1)}, u32[]{:S(2)}, u32[]{:S(2)}) %collective-permute-start.29) | collective-permute-done | bytes 24608 | tf_op jit(solution)/shard_map/ppermute | solution.py:31
  145.0 2.9 %collective-permute-done.31 = f32[3,2,1024]{2,1,0:T(2,128)S(1)} collective-permute-done((f32[3,2,1024]{2,1,0:T(2,128)S(1)}, f32[3,2,1024]{2,1,0:T(2,128)S(1)}, u32[]{:S(2)}, u32[]{:S(2)}) %collective-permute-start.31) | collective-permute-done | bytes 24608 | tf_op jit(solution)/shard_map/ppermute | solution.py:31
  (97 shorter events, 27.4 us)
Async XLA Ops:
  0.7 22.9 %collective-permute-start = (bf16[256,1024]{1,0:T(8,128)(2,1)}, bf16[256,1024]{1,0:T(8,128)(2,1)S(1)}, u32[]{:S(2)}, u32[]{:S(2)}) collective-permute-start(bf16[256,1024]{1,0:T(8,128)(2,1)} %hidden_ref.1), channel_id=1, source_target_pairs={{0,1},{1,2},{2,3},{4,5},{5,6},{6,7},{8,9},{9,10},{10,11},{12,13},{... | collective-permute-start | bytes 1572872 | tf_op jit(solution)/shard_map/ppermute | solution.py:500
  5.8 18.4 %collective-permute-start.5 = (bf16[256,1024]{1,0:T(8,128)(2,1)}, bf16[256,1024]{1,0:T(8,128)(2,1)S(1)}, u32[]{:S(2)}, u32[]{:S(2)}) collective-permute-start(bf16[256,1024]{1,0:T(8,128)(2,1)} %hidden_ref.1), channel_id=1, source_target_pairs={{3,2},{2,1},{1,0},{7,6},{6,5},{5,4},{11,10},{10,9},{9,8},{15,14},{... | collective-permute-start | bytes 1572872 | tf_op jit(solution)/shard_map/ppermute | solution.py:501
  7.1 14.3 %collective-permute-start.1 = (bf16[2,1024]{1,0:T(2,128)(2,1)}, bf16[2,1024]{1,0:T(2,128)(2,1)S(1)}, u32[]{:S(2)}, u32[]{:S(2)}) collective-permute-start(bf16[2,1024]{1,0:T(2,128)(2,1)} %param.24), channel_id=1, source_target_pairs={{0,1},{1,0},{2,3},{3,2},{4,5},{5,4},{6,7},{7,6},{8,9},{9,8},{10,11... | collective-permute-start | bytes 12296 | tf_op jit(solution)/shard_map/ppermute | solution.py:31
  9.8 12.7 %collective-permute-start.2 = (bf16[2,1024]{1,0:T(2,128)(2,1)}, bf16[2,1024]{1,0:T(2,128)(2,1)S(1)}, u32[]{:S(2)}, u32[]{:S(2)}) collective-permute-start(bf16[2,1024]{1,0:T(2,128)(2,1)} %param.24), channel_id=1, source_target_pairs={{0,2},{1,3},{2,0},{3,1},{4,6},{5,7},{6,4},{7,5},{8,10},{9,11},{10,... | collective-permute-start | bytes 12296 | tf_op jit(solution)/shard_map/ppermute | solution.py:31
  12.4 11.2 %collective-permute-start.3 = (bf16[2,1024]{1,0:T(2,128)(2,1)}, bf16[2,1024]{1,0:T(2,128)(2,1)S(1)}, u32[]{:S(2)}, u32[]{:S(2)}) collective-permute-start(bf16[2,1024]{1,0:T(2,128)(2,1)} %param.24), channel_id=1, source_target_pairs={{0,3},{1,2},{2,1},{3,0},{4,7},{5,6},{6,5},{7,4},{8,11},{9,10},{10,... | collective-permute-start | bytes 12296 | tf_op jit(solution)/shard_map/ppermute | solution.py:31
  23.5 9.5 %collective-permute-start.4 = (bf16[256,1024]{1,0:T(8,128)(2,1)S(1)}, bf16[256,1024]{1,0:T(8,128)(2,1)S(1)}, u32[]{:S(2)}, u32[]{:S(2)}) collective-permute-start(bf16[256,1024]{1,0:T(8,128)(2,1)S(1)} %collective-permute-done.refs_1_), channel_id=1, source_target_pairs={{1,2},{2,3},{5,6},{6,7},{9,10},{10,11},{13,14},{14,15},{17,18},{18... | collective-permute-start | bytes 1572872 | tf_op jit(solution)/shard_map/ppermute | solution.py:500
  24.2 14.6 %collective-permute-start.6 = (bf16[256,1024]{1,0:T(8,128)(2,1)S(1)}, bf16[256,1024]{1,0:T(8,128)(2,1)S(1)}, u32[]{:S(2)}, u32[]{:S(2)}) collective-permute-start(bf16[256,1024]{1,0:T(8,128)(2,1)S(1)} %collective-permute-done.5.refs_4_), channel_id=1, source_target_pairs={{2,1},{1,0},{6,5},{5,4},{10,9},{9,8},{14,13},{13,12},{18,17},{17,1... | collective-permute-start | bytes 1572872 | tf_op jit(solution)/shard_map/ppermute | solution.py:501
  38.8 16.2 %collective-permute-start.7 = (bf16[288,1024]{1,0:T(8,128)(2,1)}, bf16[288,1024]{1,0:T(8,128)(2,1)S(1)}, u32[]{:S(2)}, u32[]{:S(2)}) collective-permute-start(bf16[288,1024]{1,0:T(8,128)(2,1)} %pad_maximum_fusion.1), channel_id=1, source_target_pairs={{0,2},{3,1},{4,6},{7,5},{8,10},{11,9},{12,14},{15,13},{16,18},{19,... | collective-permute-start | bytes 1769480 | tf_op jit(solution)/shard_map/ppermute | solution.py:506
  41.4 2.0 %collective-permute-start.8 = (bf16[256,1024]{1,0:T(8,128)(2,1)S(1)}, bf16[256,1024]{1,0:T(8,128)(2,1)S(1)}, u32[]{:S(2)}, u32[]{:S(2)}) collective-permute-start(bf16[256,1024]{1,0:T(8,128)(2,1)S(1)} %collective-permute-done.4.refs_2_), channel_id=1, source_target_pairs={{2,3},{6,7},{10,11},{14,15},{18,19},{22,23},{26,27},{30,31}} | collective-permute-start | bytes 1572872 | tf_op jit(solution)/shard_map/ppermute | solution.py:500
  42.1 12.8 %collective-permute-start.9 = (bf16[256,1024]{1,0:T(8,128)(2,1)S(1)}, bf16[256,1024]{1,0:T(8,128)(2,1)S(1)}, u32[]{:S(2)}, u32[]{:S(2)}) collective-permute-start(bf16[256,1024]{1,0:T(8,128)(2,1)S(1)} %collective-permute-done.6.refs_5_), channel_id=1, source_target_pairs={{1,0},{5,4},{9,8},{13,12},{17,16},{21,20},{25,24},{29,28}} | collective-permute-start | bytes 1572872 | tf_op jit(solution)/shard_map/ppermute | solution.py:501
  54.9 17.5 %collective-permute-start.11 = (bf16[288,1024]{1,0:T(8,128)(2,1)}, bf16[288,1024]{1,0:T(8,128)(2,1)}, u32[]{:S(2)}, u32[]{:S(2)}) collective-permute-start(bf16[288,1024]{1,0:T(8,128)(2,1)} %pad_maximum_fusion.1), channel_id=1, source_target_pairs={{1,3},{2,0},{5,7},{6,4},{9,11},{10,8},{13,15},{14,12},{17,19},{18,... | collective-permute-start | bytes 1769480 | tf_op jit(solution)/shard_map/ppermute | solution.py:507
  59.6 7.7 %collective-permute-start.12 = (bf16[256,512]{1,0:T(8,128)(2,1)}, bf16[256,512]{1,0:T(8,128)(2,1)S(1)}, u32[]{:S(2)}, u32[]{:S(2)}) collective-permute-start(bf16[256,512]{1,0:T(8,128)(2,1)} %get-tuple-element.40), channel_id=1, source_target_pairs={{0,4},{4,8},{8,12},{12,16},{16,20},{20,24},{24,28},{1,5},{5,9},{9,... | collective-permute-start | bytes 786440 | tf_op jit(solution)/shard_map/ppermute | solution.py:518
  60.9 6.4 %collective-permute-start.13 = (bf16[256,512]{1,0:T(8,128)(2,1)S(1)}, bf16[256,512]{1,0:T(8,128)(2,1)S(1)}, u32[]{:S(2)}, u32[]{:S(2)}) collective-permute-start(bf16[256,512]{1,0:T(8,128)(2,1)S(1)} %get-tuple-element.42), channel_id=1, source_target_pairs={{4,0},{8,4},{12,8},{16,12},{20,16},{24,20},{28,24},{5,1},{9,5},{13... | collective-permute-start | bytes 786440 | tf_op jit(solution)/shard_map/ppermute | solution.py:519
  62.4 11.3 %collective-permute-start.14 = (bf16[32,1024]{1,0:T(8,128)(2,1)}, bf16[32,1024]{1,0:T(8,128)(2,1)S(1)}, u32[]{:S(2)}, u32[]{:S(2)}) collective-permute-start(bf16[32,1024]{1,0:T(8,128)(2,1)} %copy-done.13), channel_id=1, source_target_pairs={{0,3},{1,2},{2,1},{3,0},{4,7},{5,6},{6,5},{7,4},{8,11},{9,10},{10,... | collective-permute-start | bytes 196616 | tf_op jit(solution)/shard_map/ppermute | solution.py:31
  65.1 8.5 %collective-permute-start.10 = (bf16[32,1024]{1,0:T(8,128)(2,1)}, bf16[32,1024]{1,0:T(8,128)(2,1)S(1)}, u32[]{:S(2)}, u32[]{:S(2)}) collective-permute-start(bf16[32,1024]{1,0:T(8,128)(2,1)} %copy-done.13), channel_id=1, source_target_pairs={{0,1},{1,0},{2,3},{3,2},{4,5},{5,4},{6,7},{7,6},{8,9},{9,8},{10,11... | collective-permute-start | bytes 196616 | tf_op jit(solution)/shard_map/ppermute | solution.py:31
  73.7 18.3 %collective-permute-start.19 = (bf16[3,32,1024]{2,1,0:T(8,128)(2,1)S(1)}, bf16[3,32,1024]{2,1,0:T(8,128)(2,1)S(1)}, u32[]{:S(2)}, u32[]{:S(2)}) collective-permute-start(bf16[3,32,1024]{2,1,0:T(8,128)(2,1)S(1)} %get-tuple-element.61), channel_id=1, source_target_pairs={{0,16},{4,20},{8,24},{12,28},{16,0},{20,4},{24,8},{28,12},{1,17},{... | collective-permute-start | bytes 589832 | tf_op jit(solution)/shard_map/ppermute | solution.py:31
  79.2 12.8 %collective-permute-start.16 = (bf16[256,256]{1,0:T(8,128)(2,1)S(1)}, bf16[256,256]{1,0:T(8,128)(2,1)S(1)}, u32[]{:S(2)}, u32[]{:S(2)}) collective-permute-start(bf16[256,256]{1,0:T(8,128)(2,1)S(1)} %get-tuple-element.44), channel_id=1, source_target_pairs={{0,2},{1,3},{2,0},{3,1},{4,6},{5,7},{6,4},{7,5},{8,10},{9,11},{10,... | collective-permute-start | bytes 393224 | tf_op jit(solution)/shard_map/ppermute | solution.py:31
  81.2 10.8 %collective-permute-start.17 = (bf16[256,256]{1,0:T(8,128)(2,1)S(1)}, bf16[256,256]{1,0:T(8,128)(2,1)S(1)}, u32[]{:S(2)}, u32[]{:S(2)}) collective-permute-start(bf16[256,256]{1,0:T(8,128)(2,1)S(1)} %get-tuple-element.43), channel_id=1, source_target_pairs={{0,3},{1,2},{2,1},{3,0},{4,7},{5,6},{6,5},{7,4},{8,11},{9,10},{10,... | collective-permute-start | bytes 393224 | tf_op jit(solution)/shard_map/ppermute | solution.py:31
  83.9 8.7 %collective-permute-start.18 = (bf16[3,32,1024]{2,1,0:T(8,128)(2,1)S(1)}, bf16[3,32,1024]{2,1,0:T(8,128)(2,1)S(1)}, u32[]{:S(2)}, u32[]{:S(2)}) collective-permute-start(bf16[3,32,1024]{2,1,0:T(8,128)(2,1)S(1)} %get-tuple-element.61), channel_id=1, source_target_pairs={{0,8},{4,12},{8,0},{12,4},{16,24},{20,28},{24,16},{28,20},{1,9},{5... | collective-permute-start | bytes 589832 | tf_op jit(solution)/shard_map/ppermute | solution.py:31
  92.0 5.8 %collective-permute-start.20 = (bf16[3,32,1024]{2,1,0:T(8,128)(2,1)S(1)}, bf16[3,32,1024]{2,1,0:T(8,128)(2,1)S(1)}, u32[]{:S(2)}, u32[]{:S(2)}) collective-permute-start(bf16[3,32,1024]{2,1,0:T(8,128)(2,1)S(1)} %collective-permute-done.19), channel_id=1, source_target_pairs={{0,8},{4,12},{8,0},{12,4},{16,24},{20,28},{24,16},{28,20},{1,9},{5... | collective-permute-start | bytes 589832 | tf_op jit(solution)/shard_map/ppermute | solution.py:31
  97.9 9.1 %collective-permute-start.21 = (bf16[4,3,32,1024]{3,2,1,0:T(8,128)(2,1)S(1)}, bf16[4,3,32,1024]{3,2,1,0:T(8,128)(2,1)S(1)}, u32[]{:S(2)}, u32[]{:S(2)}) collective-permute-start(bf16[4,3,32,1024]{3,2,1,0:T(8,128)(2,1)S(1)} %pad_maximum_fusion.refs_4_), channel_id=1, source_target_pairs={{0,4},{4,0},{8,12},{12,8},{16,20},{20,16},{24,28},{28,24},{1,5},{5... | collective-permute-start | bytes 2359304 | tf_op jit(solution)/shard_map/ppermute | solution.py:31
  98.0 14.4 %collective-permute-start.24 = (bf16[256,1024]{1,0:T(8,128)(2,1)S(1)}, bf16[256,1024]{1,0:T(8,128)(2,1)S(1)}, u32[]{:S(2)}, u32[]{:S(2)}) collective-permute-start(bf16[256,1024]{1,0:T(8,128)(2,1)S(1)} %slice.85), channel_id=1, source_target_pairs={{0,16},{4,20},{8,24},{12,28},{16,0},{20,4},{24,8},{28,12},{1,17},{... | collective-permute-start | bytes 1572872 | tf_op jit(solution)/shard_map/ppermute | solution.py:31
  99.1 14.5 %collective-permute-start.23 = (bf16[256,1024]{1,0:T(8,128)(2,1)S(1)}, bf16[256,1024]{1,0:T(8,128)(2,1)S(1)}, u32[]{:S(2)}, u32[]{:S(2)}) collective-permute-start(bf16[256,1024]{1,0:T(8,128)(2,1)S(1)} %slice.85), channel_id=1, source_target_pairs={{0,8},{4,12},{8,0},{12,4},{16,24},{20,28},{24,16},{28,20},{1,9},{5... | collective-permute-start | bytes 1572872 | tf_op jit(solution)/shard_map/ppermute | solution.py:31
  100.0 7.0 %collective-permute-start.15 = (bf16[256,256]{1,0:T(8,128)(2,1)S(1)}, bf16[256,256]{1,0:T(8,128)(2,1)S(1)}, u32[]{:S(2)}, u32[]{:S(2)}) collective-permute-start(bf16[256,256]{1,0:T(8,128)(2,1)S(1)} %get-tuple-element.48), channel_id=1, source_target_pairs={{0,1},{1,0},{2,3},{3,2},{4,5},{5,4},{6,7},{7,6},{8,9},{9,8},{10,11... | collective-permute-start | bytes 393224 | tf_op jit(solution)/shard_map/ppermute | solution.py:31
  109.5 13.3 %collective-permute-start.22 = (bf16[256,1024]{1,0:T(8,128)(2,1)S(1)}, bf16[256,1024]{1,0:T(8,128)(2,1)S(1)}, u32[]{:S(2)}, u32[]{:S(2)}) collective-permute-start(bf16[256,1024]{1,0:T(8,128)(2,1)S(1)} %first_norm.1.rows_ref.normed_ref), channel_id=1, source_target_pairs={{0,1},{1,0},{2,3},{3,2},{4,5},{5,4},{6,7},{7,6},{8,9},{9,8},{10,11... | collective-permute-start | bytes 1572872 | tf_op jit(solution)/shard_map/ppermute | solution.py:31
  112.5 8.0 %collective-permute-start.25 = (bf16[128,1024]{1,0:T(8,128)(2,1)S(1)}, bf16[128,1024]{1,0:T(8,128)(2,1)S(1)}, u32[]{:S(2)}, u32[]{:S(2)}) collective-permute-start(bf16[128,1024]{1,0:T(8,128)(2,1)S(1)} %slice.66), channel_id=1, source_target_pairs={{0,8},{4,12},{8,0},{12,4},{16,24},{20,28},{24,16},{28,20},{1,9},{5... | collective-permute-start | bytes 786440 | tf_op jit(solution)/shard_map/ppermute | solution.py:31
  113.7 7.7 %collective-permute-start.26 = (bf16[128,1024]{1,0:T(8,128)(2,1)S(1)}, bf16[128,1024]{1,0:T(8,128)(2,1)S(1)}, u32[]{:S(2)}, u32[]{:S(2)}) collective-permute-start(bf16[128,1024]{1,0:T(8,128)(2,1)S(1)} %slice.67), channel_id=1, source_target_pairs={{0,16},{4,20},{8,24},{12,28},{16,0},{20,4},{24,8},{28,12},{1,17},{... | collective-permute-start | bytes 786440 | tf_op jit(solution)/shard_map/ppermute | solution.py:31
  122.8 4.2 %collective-permute-start.27 = (bf16[1024,1024]{1,0:T(8,128)(2,1)S(1)}, bf16[1024,1024]{1,0:T(8,128)(2,1)S(1)}, u32[]{:S(2)}, u32[]{:S(2)}) collective-permute-start(bf16[1024,1024]{1,0:T(8,128)(2,1)S(1)} %constant_dynamic-update-slice_fusion.held_ref), channel_id=1, source_target_pairs={{0,4},{4,0},{8,12},{12,8},{16,20},{20,16},{24,28},{28,24},{1,5},{5... | collective-permute-start | bytes 6291464 | tf_op jit(solution)/shard_map/ppermute | solution.py:31
  129.6 19.0 %collective-permute-start.28 = (bf16[256,1024]{1,0:T(8,128)(2,1)S(1)}, bf16[256,1024]{1,0:T(8,128)(2,1)S(1)}, u32[]{:S(2)}, u32[]{:S(2)}) collective-permute-start(bf16[256,1024]{1,0:T(8,128)(2,1)S(1)} %feed_far.1), channel_id=1, source_target_pairs={{0,1},{1,0},{2,3},{3,2},{4,5},{5,4},{6,7},{7,6},{8,9},{9,8},{10,11... | collective-permute-start | bytes 1572872 | tf_op jit(solution)/shard_map/ppermute | solution.py:31
  131.8 13.2 %collective-permute-start.29 = (f32[3,2,1024]{2,1,0:T(2,128)S(1)}, f32[3,2,1024]{2,1,0:T(2,128)S(1)}, u32[]{:S(2)}, u32[]{:S(2)}) collective-permute-start(f32[3,2,1024]{2,1,0:T(2,128)S(1)} %get-tuple-element.64), channel_id=1, source_target_pairs={{0,1},{1,0},{2,3},{3,2},{4,5},{5,4},{6,7},{7,6},{8,9},{9,8},{10,11... | collective-permute-start | bytes 73736 | tf_op jit(solution)/shard_map/ppermute | solution.py:31
  131.9 13.2 %collective-permute-start.30 = (f32[3,2,1024]{2,1,0:T(2,128)S(1)}, f32[3,2,1024]{2,1,0:T(2,128)S(1)}, u32[]{:S(2)}, u32[]{:S(2)}) collective-permute-start(f32[3,2,1024]{2,1,0:T(2,128)S(1)} %get-tuple-element.63), channel_id=1, source_target_pairs={{0,2},{1,3},{2,0},{3,1},{4,6},{5,7},{6,4},{7,5},{8,10},{9,11},{10,... | collective-permute-start | bytes 73736 | tf_op jit(solution)/shard_map/ppermute | solution.py:31
  135.1 12.8 %collective-permute-start.31 = (f32[3,2,1024]{2,1,0:T(2,128)S(1)}, f32[3,2,1024]{2,1,0:T(2,128)S(1)}, u32[]{:S(2)}, u32[]{:S(2)}) collective-permute-start(f32[3,2,1024]{2,1,0:T(2,128)S(1)} %get-tuple-element.62), channel_id=1, source_target_pairs={{0,3},{1,2},{2,1},{3,0},{4,7},{5,6},{6,5},{7,4},{8,11},{9,10},{10,... | collective-permute-start | bytes 73736 | tf_op jit(solution)/shard_map/ppermute | solution.py:31
  (17 other events, 308.2 us)

commit v7 on v6

--- a/solution.py
+++ b/solution.py
@@ -44,7 +44,7 @@
 def project_kernel(place_ref, weight_ref, *refs):
     shards, (query_ref, keyval_ref, top_ref, bottom_ref, rows_ref, sems) = refs[:-6], refs[-6:]
     kv = place_ref[1]
-    count = shards[0].shape[0]
+    count = top_ref.shape[0]
     steps = (len(shards) - 1) // 2
     width = weight_ref.shape[2]
     moves = [(shards[0], kv, None)]
@@ -62,7 +62,7 @@
     for index, (source, owner, needed) in enumerate(moves):
         safe = owner if needed is None else jnp.where(needed, owner, 0)
         at = pl.ds(pl.multiple_of(safe * count, count), count)
-        copies.append((needed, pltpu.make_async_copy(source, rows_ref.at[at], sems.at[index])))
+        copies.append((needed, pltpu.make_async_copy(source.at[0:count], rows_ref.at[at], sems.at[index])))
     for needed, copy in copies:
         guarded(needed, copy.start)
     for needed, copy in copies:
@@ -376,7 +376,7 @@
     )(normed, near, far, gain, bias)
 
 
-def decode_kernel(slot_ref, filled_ref, query_ref, cache_ref, out_ref, high_ref, total_ref, sum_ref):
+def decode_kernel(source_ref, slot_ref, filled_ref, query_ref, cache_ref, out_ref, high_ref, total_ref, sum_ref):
     step = pl.program_id(0)
 
     @pl.when(step == 0)
@@ -390,7 +390,7 @@
     width = query_ref.shape[1]
     head = lax.broadcasted_iota(jnp.int32, (H, width), 0)
     inside = head == lax.broadcasted_iota(jnp.int32, (H, width), 1) // HD
-    query = jnp.where(inside, query_ref[pl.ds(row, 1), :], 0.0).astype(BF16)
+    query = jnp.where(inside, query_ref[pl.ds(source_ref[step], 1), :], 0.0).astype(BF16)
     scores = lax.dot_general(query, cache_ref[0, 0, 0], (((1,), (1,)), ((), ())), preferred_element_type=F32)
     live = lax.broadcasted_iota(jnp.int32, scores.shape, 1) < filled
     scores = jnp.where(live, scores * (1.0 / math.sqrt(HD)), NEG_FILL)
@@ -417,8 +417,8 @@
         out_ref[2] = sum_ref[...]
 
 
-def decode(slots, filled, queries, kv_cache):
-    requests, width = queries.shape
+def decode(sources, slots, filled, queries, requests, kv_cache):
+    count, width = queries.shape
     pieces = kv_cache.shape[2]
     state = pltpu.VMEM((requests, width), F32)
     return pl.pallas_call(
@@ -428,7 +428,8 @@
         in_specs=[
             SMEM,
             SMEM,
-            pl.BlockSpec((requests, width), lambda i: (0, 0)),
+            SMEM,
+            pl.BlockSpec((count, width), lambda i: (0, 0)),
             pl.BlockSpec((2, 1, 1, PLEN, width), lambda i: (0, 0, i, 0, 0)),
         ],
         out_specs=pl.BlockSpec((3, requests, width), lambda i: (0, 0, 0)),
@@ -436,19 +437,17 @@
         compiler_params=pltpu.CompilerParams(vmem_limit_bytes=8 * MIB),
         cost_estimate=SHORT,
         name="decode",
-    )(slots, filled, queries, kv_cache)
-
-
-def gathered_queries(dec_query):
-    flips = range(1, lax.axis_size("kv"))
-    return [dec_query] + [swapped(dec_query, "kv", flip) for flip in flips]
-
-
-def decode_partial(queries, kv_cache, piece_req, piece_used):
-    own = queries[0].shape[0]
+    )(sources, slots, filled, queries, kv_cache)
+
+
+def decode_partial(queries, own, kv_cache, piece_req, piece_used):
+    kv = lax.axis_index("kv")
     owners = piece_req[0]
-    slots = ((owners // own) ^ lax.axis_index("kv")) * own + owners % own
-    return decode(slots, piece_used[0], jnp.concatenate(queries).astype(F32), kv_cache)
+    home = owners // own
+    place = jnp.where(home <= kv, kv - home, lax.axis_size("kv") - 1 + home - kv)
+    sources = place * own + owners % own
+    slots = (home ^ kv) * own + owners % own
+    return decode(sources, slots, piece_used[0], queries, own * lax.axis_size("kv"), kv_cache)
 
 
 def exchanged_partials(partial, own):
@@ -489,50 +488,46 @@
     place = jnp.stack([tok, kv]).astype(jnp.int32)
     eighth = lambda value: lax.dynamic_slice_in_dim(value, tok * (value.shape[0] // toks), value.shape[0] // toks, 0)
 
-    queries = gathered_queries(dec_query)
-    partial = decode_partial(queries, kv_cache, piece_req, piece_used)
-    early = {2: queries[1:], 3: [partial]}
     from_below, from_above = [], []
-    rising = falling = hidden_in
+    rising = falling = jnp.concatenate([hidden_in, dec_query], axis=0)
     for step in range(1, kvs):
-        rising, falling = after(rising, *early.get(step, ())), after(falling, *early.get(step, ()))
         links = range(step - 1, kvs - 1)
         rising = lax.ppermute(rising, "kv", [(i, i + 1) for i in links])
         falling = lax.ppermute(falling, "kv", [(kvs - 1 - i, kvs - 2 - i) for i in links])
         from_below.append(rising)
         from_above.append(falling)
 
-    feed_part = jnp.concatenate([eighth(up_weight), eighth(down_weight), eighth(out_weight)], axis=0)
-    feed_inner = lax.ppermute(after(feed_part, from_below[1], from_above[1], partial), "kv", [(0, 2), (3, 1)])
-    feed_outer = lax.ppermute(after(feed_part, rising, falling, feed_inner), "kv", [(1, 3), (2, 0)])
-    out_part = after(eighth(out_weight), rising, falling)
-    out_near, out_far = swapped(out_part, "kv", 1), swapped(out_part, "kv", 3)
+    out_part = eighth(out_weight)
+    depth = out_part.shape[0]
+    out_one = swapped(after(out_part, from_below[0], from_above[0]), "kv", 1)
+    out_two = swapped(after(jnp.concatenate([out_part, out_one], axis=0), from_below[1], from_above[1]), "kv", 2)
+    out_here = jnp.concatenate([out_one, out_two], axis=0).reshape(kvs - 1, depth, width)
+    feed_part = jnp.concatenate([eighth(up_weight), eighth(down_weight)], axis=0)
+    feed_inner = lax.ppermute(after(feed_part, from_below[1], from_above[1]), "kv", [(0, 2), (3, 1)])
+    feed_outer = lax.ppermute(after(feed_part, rising, falling, feed_inner, out_two), "kv", [(1, 3), (2, 0)])
 
     order = jnp.arange(stretch_len.shape[0])
     ends = jnp.sum(jnp.where(order[:, None] <= order[None, :], stretch_len[:, None], 0), axis=0, dtype=jnp.int32)
     starts = (ends - stretch_len)[None, :]
     ends = ends[None, :]
 
-    shards = [after(hidden_in, feed_inner)] + from_below + from_above
+    shards = [after(hidden_in, feed_inner, out_two)] + from_below + from_above
     query, keyval, top, bottom = project(place, jnp.transpose(qkv_weight, (1, 0, 2)), shards)
     before = lax.ppermute(bottom, "tok", [(i, i + 1) for i in range(toks - 1)])
     behind = lax.ppermute(top, "tok", [(i + 1, i) for i in range(toks - 1)])
-    window = (place, starts, ends, query, before, keyval, behind, rows)
+    out_here = after(out_here, query)
+    out_x, out_y = swapped(out_here, "tok", 2), swapped(out_here, "tok", 4)
+    window = (place, starts, ends, after(query, out_x, out_y), before, keyval, behind, rows)
     parts = [None] * kvs
     parts[3], parts[2] = attend_blocks(*window, (3, 2), "attend_far")
-    depth = out_part.shape[0]
+    out_all = jnp.stack([out_here, out_x, out_y, swapped(out_y, "tok", 2)])
+    out_core = swapped(after(out_all, parts[3]), "tok", 1)
     inner = (kv == 1) | (kv == 2)
     feed_here = jnp.where(inner, feed_inner, after(feed_outer, parts[3], parts[2]))
-    out_here = jnp.stack([out_near, feed_here[-depth:], out_far])
-    feed_here = feed_here[:-depth]
     parts[3], parts[2] = swapped(parts[3], "kv", 3), swapped(parts[2], "kv", 2)
-    out_x, out_y = swapped(out_here, "tok", 2), swapped(out_here, "tok", 4)
-    window = (place, starts, ends, after(query, out_here), before, keyval, behind, rows)
+    window = (place, starts, ends, after(query, feed_here), before, keyval, behind, rows)
     parts[1], parts[0] = attend_blocks(*window, (1, 0), "attend_near")
-    feed_here = after(feed_here, parts[0])
     parts[1] = swapped(parts[1], "kv", 1)
-    out_all = jnp.stack([out_here, out_x, out_y, swapped(after(out_y, parts[0], parts[3], parts[2]), "tok", 2)])
-    out_core = swapped(out_all, "tok", 1)
     feed_x, feed_y = swapped(feed_here, "tok", 2), swapped(feed_here, "tok", 4)
     out_pieces = [((0, 2, 4, 6), out_all), ((1, 3, 5, 7), out_core)]
     normed = first_norm(place, hidden_in, out_weight, ln1_gain[None, :], ln1_bias[None, :], parts, out_pieces)
@@ -541,16 +536,21 @@
     half = feed_here.shape[0] // 2
     far_up = swapped(after(feed_y, normed)[:half], "tok", 2)
     far_down = swapped(after(feed_x, normed)[half:], "tok", 4)
-    held = jnp.concatenate([feed_here, feed_x, feed_y, far_up, far_down], axis=0)
+    own = dec_query.shape[0]
+    queries = jnp.concatenate([dec_query] + [shard[rows:] for shard in from_below + from_above], axis=0)
+    queries = after(queries.astype(F32), normed)
+    partial = decode_partial(queries, own, kv_cache, piece_req, piece_used)
+    dec_parts = exchanged_partials(after(partial, partner), own)
+    held = jnp.concatenate([feed_here, feed_x, feed_y, after(far_up, partial), far_down], axis=0)
     near_away = feed_near(partner, up_weight, down_weight)
+    near_away = after(near_away, *dec_parts)
     feed_pieces = (held, swapped(after(held, partner), "tok", 1))
     away = feed_far(place, partner, near_away, feed_pieces)
     arrived = swapped(away, "kv", 1)
-    dec_parts = exchanged_partials(after(partial, away), dec_query.shape[0])
     mine = feed(place, after(normed, away), up_weight, down_weight, feed_pieces)
     prefill_out = finish(normed, mine, arrived, ln2_gain[None, :], ln2_bias[None, :])
 
-    return prefill_out, merged_partials(after(tuple(dec_parts), mine))
+    return prefill_out, merged_partials(after(tuple(dec_parts), away))
 
 
 def extended(value, sides, width):

time: 150 us -> 166 us (1.11)
  local copies, waits for them, and re-layouts: 4.13 us -> 18.5 us
  starting transfers between devices: 54.2 us -> 48.7 us
  other arithmetic: 3 us -> 5.62 us
  waiting for transfers between devices: 58.3 us -> 60.4 us
    ppermute x22 -> x19, starting transfers between devices: 37.4 us -> 25 us  [swapped(): return lax.ppermute(value, axis, [(i, i ^ flip) for i in range(count)])]
    unnamed x38 -> x52, local copies, waits for them, and re-layouts: 2.08 us -> 9.74 us
    ppermute x2, starting transfers between devices: 3.92 us -> 8.65 us  [the longest x1 7.37 us: routed_body(): lax.ppermute(after(feed_part, from_below[1], from_above[1]), 'kv', [(0, 2...]
    slice x1 -> x6, local copies, waits for them, and re-layouts: 0.04 us -> 4.33 us  [routed_body(): shard[rows:]]
    ppermute x3, waiting for transfers between devices: 17.3 us -> 21 us  [routed_body(): lax.ppermute(falling, 'kv', [(kvs - 1 - i, kvs - 2 - i) for i in links])]
    unnamed x0 -> x1, other arithmetic: none -> 2.22 us
    ppermute x3, starting transfers between devices: 6.47 us -> 8.54 us  [routed_body(): rising = lax.ppermute(rising, 'kv', [(i, i + 1) for i in links])]
    ppermute x22 -> x19, waiting for transfers between devices: 41 us -> 39.4 us  [swapped(): return lax.ppermute(value, axis, [(i, i ^ flip) for i in range(count)])]
  transfers between devices with their start and end apart: 32 -> 29, of which waited for: 15 -> 10; matrix products, arithmetic and copies ran while one was open for 3% -> 10% of each run, Pallas kernels for 17% -> 13%
where the time goes in v7:
time: 166 us; the launch traced here: 164 us
  waiting for transfers between devices  60.4 us (36%)
  starting transfers between devices  48.7 us (29%)
  Pallas kernels  30 us (18%)
  local copies, waits for them, and re-layouts  18.5 us (11%)
  other arithmetic  5.62 us (3%)
    ppermute x19, waiting for transfers between devices, swapped(): return lax.ppermute(value, axis, [(i, i ^ flip) for i in range(count)])  39.4 us
    ppermute x19, starting transfers between devices, swapped(): return lax.ppermute(value, axis, [(i, i ^ flip) for i in range(count)])  25 us
    ppermute x3, waiting for transfers between devices, routed_body(): lax.ppermute(falling, 'kv', [(kvs - 1 - i, kvs - 2 - i) for i in links])  21 us
    pallas_call x2, Pallas kernels, attend_blocks(): pl.pallas_call(functools.partial(attend_kernel, flips), out_shape=tuple((...  10.3 us
    unnamed x52, local copies, waits for them, and re-layouts  9.74 us
    ppermute x3, starting transfers between devices, routed_body(): rising = lax.ppermute(rising, 'kv', [(i, i + 1) for i in links])  8.54 us
    ppermute x1, starting transfers between devices, routed_body(): lax.ppermute(after(feed_part, from_below[1], from_above[1]), 'kv', [(0, 2...  7.37 us
    slice x6, local copies, waits for them, and re-layouts, routed_body(): shard[rows:]  4.33 us
  transfers between devices with their start and end apart: 29, of which 10 were waited for; matrix products, arithmetic and copies ran while one was open for 10% of the time, Pallas kernels for 13%

profile of v7, /device:TPU:0, one launch (start us, length us, event | category | flops | bytes accessed | tf_op | source)
XLA Modules:
  0.0 164.4 jit_solution(4835142084186999960)
XLA Ops:
  3.8 5.6 %collective-permute-start = (bf16[258,1024]{1,0:T(8,128)(2,1)S(1)}, bf16[258,1024]{1,0:T(8,128)(2,1)S(1)}, u32[]{:S(2)}, u32[]{:S(2)}) collective-permute-start(bf16[258,1024]{1,0:T(8,128)(2,1)S(1)} %constant_dynamic-update-slice_fusion), channel_id=1, source_target_pairs={{0,1},{1,2},{2,3},{4,5},{5,6},{6,7},{8,9},{9,10},{10,11},{12,13},{... | collective-permute-start | bytes 1585160 | tf_op jit(solution)/shard_map/ppermute | solution.py:495
  9.4 10.3 %collective-permute-done.2.refs_4_ = bf16[258,1024]{1,0:T(8,128)(2,1)S(1)} collective-permute-done((bf16[258,1024]{1,0:T(8,128)(2,1)S(1)}, bf16[258,1024]{1,0:T(8,128)(2,1)S(1)}, u32[]{:S(2)}, u32[]{:S(2)}) %collective-permute-start.2) | collective-permute-done | bytes 528416 | tf_op jit(solution)/shard_map/ppermute | solution.py:496
  21.0 1.5 collective-permute-start.1
  24.4 10.7 %collective-permute-done.3.refs_5_ = bf16[258,1024]{1,0:T(8,128)(2,1)S(1)} collective-permute-done((bf16[258,1024]{1,0:T(8,128)(2,1)S(1)}, bf16[258,1024]{1,0:T(8,128)(2,1)S(1)}, u32[]{:S(2)}, u32[]{:S(2)}) %collective-permute-start.3) | collective-permute-done | bytes 528416 | tf_op jit(solution)/shard_map/ppermute | solution.py:496
  35.0 7.4 %collective-permute-start.4 = (bf16[256,1024]{1,0:T(8,128)(2,1)}, bf16[256,1024]{1,0:T(8,128)(2,1)}, u32[]{:S(2)}, u32[]{:S(2)}) collective-permute-start(bf16[256,1024]{1,0:T(8,128)(2,1)} %pad_maximum_fusion.1), channel_id=1, source_target_pairs={{0,2},{3,1},{4,6},{7,5},{8,10},{11,9},{12,14},{15,13},{16,18},{19,... | collective-permute-start | bytes 1572872 | tf_op jit(solution)/shard_map/ppermute | solution.py:506
  43.7 1.5 collective-permute-start.7
  46.0 3.5 %collective-permute-start.5 = (bf16[32,1024]{1,0:T(8,128)(2,1)S(1)}, bf16[32,1024]{1,0:T(8,128)(2,1)S(1)}, u32[]{:S(2)}, u32[]{:S(2)}) collective-permute-start(bf16[32,1024]{1,0:T(8,128)(2,1)S(1)} %constant_dynamic-slice_fusion), channel_id=1, source_target_pairs={{0,1},{1,0},{2,3},{3,2},{4,5},{5,4},{6,7},{7,6},{8,9},{9,8},{10,11... | collective-permute-start | bytes 196616 | tf_op jit(solution)/shard_map/ppermute | solution.py:31
  49.5 7.9 %collective-permute-done.5 = bf16[32,1024]{1,0:T(8,128)(2,1)S(1)} collective-permute-done((bf16[32,1024]{1,0:T(8,128)(2,1)S(1)}, bf16[32,1024]{1,0:T(8,128)(2,1)S(1)}, u32[]{:S(2)}, u32[]{:S(2)}) %collective-permute-start.5) | collective-permute-done | bytes 65568 | tf_op jit(solution)/shard_map/ppermute | solution.py:31
  57.6 6.2 %collective-permute-done.6 = bf16[64,1024]{1,0:T(8,128)(2,1)S(1)} collective-permute-done((bf16[64,1024]{1,0:T(8,128)(2,1)S(1)}, bf16[64,1024]{1,0:T(8,128)(2,1)S(1)}, u32[]{:S(2)}, u32[]{:S(2)}) %collective-permute-start.6) | collective-permute-done | bytes 131104 | tf_op jit(solution)/shard_map/ppermute | solution.py:31
  64.5 1.4 copy-done.6
  68.0 4.3 %project.1 = (bf16[1024,256]{1,0:T(8,128)(2,1)S(1)}, bf16[1024,512]{1,0:T(8,128)(2,1)S(1)}, bf16[256,512]{1,0:T(8,128)(2,1)S(1)}, bf16[256,512]{1,0:T(8,128)(2,1)}) custom-call(s32[2]{0:T(128)S(1)} %pad_add_fusion.place_ref, bf16[3,1024,256]{2,1,0:T(8,128)(2,1)S(1)} %bitcast.137, bf16[256,1024]{1,0:T(8,128)(2,1)S(1)} %copy-done.2, ...), custom_call_target="tpu_custom_call" | custom-call | flops 1 | bytes 1 | tf_op jit(solution)/shard_map/project/pallas_call | solution.py:85
  72.4 1.6 collective-permute-start.11
  75.2 1.3 collective-permute-start.12
  76.5 1.3 collective-permute-start.13
  78.0 4.5 %collective-permute-start.10 = (bf16[3,32,1024]{2,1,0:T(8,128)(2,1)}, bf16[3,32,1024]{2,1,0:T(8,128)(2,1)S(1)}, u32[]{:S(2)}, u32[]{:S(2)}) collective-permute-start(bf16[3,32,1024]{2,1,0:T(8,128)(2,1)} %bitcast.7), channel_id=1, source_target_pairs={{0,8},{4,12},{8,0},{12,4},{16,24},{20,28},{24,16},{28,20},{1,9},{5... | collective-permute-start | bytes 589832 | tf_op jit(solution)/shard_map/ppermute | solution.py:31
  82.6 10.2 %collective-permute-done.10 = bf16[3,32,1024]{2,1,0:T(8,128)(2,1)S(1)} collective-permute-done((bf16[3,32,1024]{2,1,0:T(8,128)(2,1)}, bf16[3,32,1024]{2,1,0:T(8,128)(2,1)S(1)}, u32[]{:S(2)}, u32[]{:S(2)}) %collective-permute-start.10) | collective-permute-done | bytes 196640 | tf_op jit(solution)/shard_map/ppermute | solution.py:31
  92.8 5.1 %attend_far.1 = (bf16[256,256]{1,0:T(8,128)(2,1)S(1)}, bf16[256,256]{1,0:T(8,128)(2,1)S(1)}) custom-call(s32[2]{0:T(128)S(1)} %pad_add_fusion.place_ref, s32[1,48]{1,0:T(1,128)S(1)} %subtract_bitcast_fusion.starts_ref, s32[1,48]{1,0:T(1,128)S(1)} %bitcast.142, bf16[1024,256]{1,0:T(8,128)(2,1)S(1)} %get-tuple-element.46.query_ref, ...), custom_call_target="tpu_custom_call" | custom-call | flops 1 | bytes 1 | tf_op jit(solution)/shard_map/attend_far/pallas_call | solution.py:174
  99.1 2.2 %constant_dynamic-update-slice_fusion.6 = (bf16[1024,1024]{1,0:T(8,128)(2,1)S(1)}, bf16[256,1024]{1,0:T(8,128)(2,1)}) fusion(bf16[256,1024]{1,0:T(8,128)(2,1)} %collective-permute-done.4, bf16[256,1024]{1,0:T(8,128)(2,1)} %collective-permute-done.9, pred[]{:T(512)S(6)} %or.3), kind=kLoop, calls=%fused_computation.13 | loop fusion | flops 262143 | bytes 2097153
  101.8 4.3 %collective-permute-start.15 = (bf16[256,256]{1,0:T(8,128)(2,1)S(1)}, bf16[256,256]{1,0:T(8,128)(2,1)S(1)}, u32[]{:S(2)}, u32[]{:S(2)}) collective-permute-start(bf16[256,256]{1,0:T(8,128)(2,1)S(1)} %get-tuple-element.44), channel_id=1, source_target_pairs={{0,2},{1,3},{2,0},{3,1},{4,6},{5,7},{6,4},{7,5},{8,10},{9,11},{10,... | collective-permute-start | bytes 393224 | tf_op jit(solution)/shard_map/ppermute | solution.py:31
  107.1 2.0 %collective-permute-start.16 = (bf16[256,256]{1,0:T(8,128)(2,1)S(1)}, bf16[256,256]{1,0:T(8,128)(2,1)S(1)}, u32[]{:S(2)}, u32[]{:S(2)}) collective-permute-start(bf16[256,256]{1,0:T(8,128)(2,1)S(1)} %get-tuple-element.43), channel_id=1, source_target_pairs={{0,3},{1,2},{2,1},{3,0},{4,7},{5,6},{6,5},{7,4},{8,11},{9,10},{10,... | collective-permute-start | bytes 393224 | tf_op jit(solution)/shard_map/ppermute | solution.py:31
  109.1 5.2 %attend_near.1 = (bf16[256,256]{1,0:T(8,128)(2,1)S(1)}, bf16[256,256]{1,0:T(8,128)(2,1)S(1)}) custom-call(s32[2]{0:T(128)S(1)} %pad_add_fusion.place_ref, s32[1,48]{1,0:T(1,128)S(1)} %subtract_bitcast_fusion.starts_ref, s32[1,48]{1,0:T(1,128)S(1)} %bitcast.143, bf16[1024,256]{1,0:T(8,128)(2,1)S(1)} %get-tuple-element.46.query_ref, ...), custom_call_target="tpu_custom_call" | custom-call | flops 1 | bytes 1 | tf_op jit(solution)/shard_map/attend_near/pallas_call | solution.py:174
  114.4 1.7 %collective-permute-done.15.refs_2_ = bf16[256,256]{1,0:T(8,128)(2,1)S(1)} collective-permute-done((bf16[256,256]{1,0:T(8,128)(2,1)S(1)}, bf16[256,256]{1,0:T(8,128)(2,1)S(1)}, u32[]{:S(2)}, u32[]{:S(2)}) %collective-permute-start.15) | collective-permute-done | bytes 131104 | tf_op jit(solution)/shard_map/ppermute | solution.py:31
  116.1 4.9 %collective-permute-done.14.refs_1_ = bf16[256,256]{1,0:T(8,128)(2,1)S(1)} collective-permute-done((bf16[256,256]{1,0:T(8,128)(2,1)S(1)}, bf16[256,256]{1,0:T(8,128)(2,1)S(1)}, u32[]{:S(2)}, u32[]{:S(2)}) %collective-permute-start.14) | collective-permute-done | bytes 131104 | tf_op jit(solution)/shard_map/ppermute | solution.py:31
  121.0 2.4 %first_norm.1.rows_ref.normed_ref = bf16[256,1024]{1,0:T(8,128)(2,1)S(1)} custom-call(s32[2]{0:T(128)S(1)} %pad_add_fusion.place_ref, bf16[256,1024]{1,0:T(8,128)(2,1)S(1)} %copy-done.2, bf16[256,1024]{1,0:T(8,128)(2,1)S(1)} %copy-done.9, f32[1,1024]{1,0:T(1,128)S(1)} %bitcast.140, f32[1,1024]{1,0:T(1,128)S(1)} %bitcast.141, ...), custom_call_target="tpu_custom_call" | custom-call | flops 1 | bytes 1 | tf_op jit(solution)/shard_map/first_norm/pallas_call | solution.py:222
  133.6 1.9 %copy-done.5 = bf16[2,1,6,128,1024]{4,3,2,1,0:T(8,128)(2,1)S(1)} copy-done((bf16[2,1,6,128,1024]{4,3,2,1,0:T(8,128)(2,1)S(1)}, bf16[2,1,6,128,1024]{4,3,2,1,0:T(8,128)(2,1)}, u32[]{:S(2)}) %copy-start.5) | copy-done | bytes 3145752
  135.5 3.8 %decode.1 = f32[3,8,1024]{2,1,0:T(8,128)S(1)} custom-call(s32[6]{0:T(128)S(1)} %fusion.13.source_ref, s32[6]{0:T(128)S(1)} %get-tuple-element.64.slot_ref, s32[6]{0:T(128)S(1)} %bitcast.144, f32[14,1024]{1,0:T(8,128)S(1)} %convert_element_type.6.query_ref, bf16[2,1,6,128,1024]{4,3,2,1,0:T(8,128)(2,1)S(1)} %copy-done.5), custom_call_target="tpu_custom_call" | custom-call | flops 1 | bytes 1 | tf_op jit(solution)/shard_map/decode/pallas_call | solution.py:424
  140.5 2.1 %collective-permute-start.22 = (f32[3,2,1024]{2,1,0:T(2,128)S(1)}, f32[3,2,1024]{2,1,0:T(2,128)S(1)}, u32[]{:S(2)}, u32[]{:S(2)}) collective-permute-start(f32[3,2,1024]{2,1,0:T(2,128)S(1)} %get-tuple-element.67), channel_id=1, source_target_pairs={{0,3},{1,2},{2,1},{3,0},{4,7},{5,6},{6,5},{7,4},{8,11},{9,10},{10,... | collective-permute-start | bytes 73736 | tf_op jit(solution)/shard_map/ppermute | solution.py:31
  142.6 1.5 collective-permute-start.21
  144.9 1.5 feed_near.1.near_ref
  147.8 2.6 %feed_far.1 = bf16[256,1024]{1,0:T(8,128)(2,1)S(1)} custom-call(s32[2]{0:T(128)S(1)} %pad_add_fusion.place_ref, bf16[256,1024]{1,0:T(8,128)(2,1)S(1)} %collective-permute-done.19.rows_ref, f32[256,1024]{1,0:T(8,128)S(1)} %feed_near.1.near_ref, bf16[1024,1024]{1,0:T(8,128)(2,1)S(1)} %constant_dynamic-update-slice_fusion.2.held_ref, ...), custom_call_target="tpu_custom_call" | custom-call | flops 1 | bytes 1 | tf_op jit(solution)/shard_map/feed_far/pallas_call | solution.py:330
  151.5 3.9 %feed_own.1.near_ref = f32[256,1024]{1,0:T(8,128)S(1)} custom-call(s32[2]{0:T(128)S(1)} %pad_add_fusion.place_ref, bf16[256,1024]{1,0:T(8,128)(2,1)S(1)} %first_norm.1.rows_ref.normed_ref, bf16[1024,1024]{1,0:T(8,128)(2,1)S(1)} %copy-done, bf16[1024,1024]{1,0:T(8,128)(2,1)S(1)} %copy-done.1, ...), custom_call_target="tpu_custom_call" | custom-call | flops 1 | bytes 1 | tf_op jit(solution)/shard_map/feed_own/pallas_call | solution.py:347
  156.0 7.1 %collective-permute-done.28.far_ref = bf16[256,1024]{1,0:T(8,128)(2,1)S(1)} collective-permute-done((bf16[256,1024]{1,0:T(8,128)(2,1)S(1)}, bf16[256,1024]{1,0:T(8,128)(2,1)S(1)}, u32[]{:S(2)}, u32[]{:S(2)}) %collective-permute-start.28) | collective-permute-done | bytes 524320 | tf_op jit(solution)/shard_map/ppermute | solution.py:31
  (113 shorter events, 32.0 us)
Async XLA Ops:
  0.6 63.9 %copy-start.2 = (bf16[256,1024]{1,0:T(8,128)(2,1)S(1)}, bf16[256,1024]{1,0:T(8,128)(2,1)}, u32[]{:S(2)}) copy-start(bf16[256,1024]{1,0:T(8,128)(2,1)} %hidden_ref.1) | copy-start | bytes 1572868
  2.5 17.2 %collective-permute-start.2 = (bf16[258,1024]{1,0:T(8,128)(2,1)S(1)}, bf16[258,1024]{1,0:T(8,128)(2,1)S(1)}, u32[]{:S(2)}, u32[]{:S(2)}) collective-permute-start(bf16[258,1024]{1,0:T(8,128)(2,1)S(1)} %constant_dynamic-update-slice_fusion), channel_id=1, source_target_pairs={{3,2},{2,1},{1,0},{7,6},{6,5},{5,4},{11,10},{10,9},{9,8},{15,14},{... | collective-permute-start | bytes 1585160 | tf_op jit(solution)/shard_map/ppermute | solution.py:496
  3.8 17.2 %collective-permute-start = (bf16[258,1024]{1,0:T(8,128)(2,1)S(1)}, bf16[258,1024]{1,0:T(8,128)(2,1)S(1)}, u32[]{:S(2)}, u32[]{:S(2)}) collective-permute-start(bf16[258,1024]{1,0:T(8,128)(2,1)S(1)} %constant_dynamic-update-slice_fusion), channel_id=1, source_target_pairs={{0,1},{1,2},{2,3},{4,5},{5,6},{6,7},{8,9},{9,10},{10,11},{12,13},{... | collective-permute-start | bytes 1585160 | tf_op jit(solution)/shard_map/ppermute | solution.py:495
  19.7 52.7 %copy-start.10 = (bf16[258,1024]{1,0:T(8,128)(2,1)}, bf16[258,1024]{1,0:T(8,128)(2,1)S(1)}, u32[]{:S(2)}) copy-start(bf16[258,1024]{1,0:T(8,128)(2,1)S(1)} %collective-permute-done.2.refs_4_) | copy-start | bytes 1585156
  19.7 15.3 %collective-permute-start.3 = (bf16[258,1024]{1,0:T(8,128)(2,1)S(1)}, bf16[258,1024]{1,0:T(8,128)(2,1)S(1)}, u32[]{:S(2)}, u32[]{:S(2)}) collective-permute-start(bf16[258,1024]{1,0:T(8,128)(2,1)S(1)} %collective-permute-done.2.refs_4_), channel_id=1, source_target_pairs={{2,1},{1,0},{6,5},{5,4},{10,9},{9,8},{14,13},{13,12},{18,17},{17,1... | collective-permute-start | bytes 1585160 | tf_op jit(solution)/shard_map/ppermute | solution.py:496
  21.0 43.5 %copy-start.11 = (bf16[258,1024]{1,0:T(8,128)(2,1)}, bf16[258,1024]{1,0:T(8,128)(2,1)S(1)}, u32[]{:S(2)}) copy-start(bf16[258,1024]{1,0:T(8,128)(2,1)S(1)} %collective-permute-done.refs_1_) | copy-start | bytes 1585156
  21.0 14.0 %collective-permute-start.1 = (bf16[258,1024]{1,0:T(8,128)(2,1)S(1)}, bf16[258,1024]{1,0:T(8,128)(2,1)}, u32[]{:S(2)}, u32[]{:S(2)}) collective-permute-start(bf16[258,1024]{1,0:T(8,128)(2,1)S(1)} %collective-permute-done.refs_1_), channel_id=1, source_target_pairs={{1,2},{2,3},{5,6},{6,7},{9,10},{10,11},{13,14},{14,15},{17,18},{18... | collective-permute-start | bytes 1585160 | tf_op jit(solution)/shard_map/ppermute | solution.py:495
  35.0 29.5 %collective-permute-start.4 = (bf16[256,1024]{1,0:T(8,128)(2,1)}, bf16[256,1024]{1,0:T(8,128)(2,1)}, u32[]{:S(2)}, u32[]{:S(2)}) collective-permute-start(bf16[256,1024]{1,0:T(8,128)(2,1)} %pad_maximum_fusion.1), channel_id=1, source_target_pairs={{0,2},{3,1},{4,6},{7,5},{8,10},{11,9},{12,14},{15,13},{16,18},{19,... | collective-permute-start | bytes 1572872 | tf_op jit(solution)/shard_map/ppermute | solution.py:506
  42.4 22.1 %collective-permute-start.8 = (bf16[258,1024]{1,0:T(8,128)(2,1)S(1)}, bf16[258,1024]{1,0:T(8,128)(2,1)}, u32[]{:S(2)}, u32[]{:S(2)}) collective-permute-start(bf16[258,1024]{1,0:T(8,128)(2,1)S(1)} %collective-permute-done.3.refs_5_), channel_id=1, source_target_pairs={{1,0},{5,4},{9,8},{13,12},{17,16},{21,20},{25,24},{29,28}} | collective-permute-start | bytes 1585160 | tf_op jit(solution)/shard_map/ppermute | solution.py:496
  43.7 20.8 %collective-permute-start.7 = (bf16[258,1024]{1,0:T(8,128)(2,1)}, bf16[258,1024]{1,0:T(8,128)(2,1)}, u32[]{:S(2)}, u32[]{:S(2)}) collective-permute-start(bf16[258,1024]{1,0:T(8,128)(2,1)} %collective-permute-done.1.refs_2_), channel_id=1, source_target_pairs={{2,3},{6,7},{10,11},{14,15},{18,19},{22,23},{26,27},{30,31}} | collective-permute-start | bytes 1585160 | tf_op jit(solution)/shard_map/ppermute | solution.py:495
  46.0 11.3 %collective-permute-start.5 = (bf16[32,1024]{1,0:T(8,128)(2,1)S(1)}, bf16[32,1024]{1,0:T(8,128)(2,1)S(1)}, u32[]{:S(2)}, u32[]{:S(2)}) collective-permute-start(bf16[32,1024]{1,0:T(8,128)(2,1)S(1)} %constant_dynamic-slice_fusion), channel_id=1, source_target_pairs={{0,1},{1,0},{2,3},{3,2},{4,5},{5,4},{6,7},{7,6},{8,9},{9,8},{10,11... | collective-permute-start | bytes 196616 | tf_op jit(solution)/shard_map/ppermute | solution.py:31
  57.4 6.4 %collective-permute-start.6 = (bf16[64,1024]{1,0:T(8,128)(2,1)S(1)}, bf16[64,1024]{1,0:T(8,128)(2,1)S(1)}, u32[]{:S(2)}, u32[]{:S(2)}) collective-permute-start(bf16[64,1024]{1,0:T(8,128)(2,1)S(1)} %pad_maximum_fusion.3), channel_id=1, source_target_pairs={{0,2},{1,3},{2,0},{3,1},{4,6},{5,7},{6,4},{7,5},{8,10},{9,11},{10,... | collective-permute-start | bytes 393224 | tf_op jit(solution)/shard_map/ppermute | solution.py:31
  72.4 10.1 %collective-permute-start.11 = (bf16[3,32,1024]{2,1,0:T(8,128)(2,1)}, bf16[3,32,1024]{2,1,0:T(8,128)(2,1)S(1)}, u32[]{:S(2)}, u32[]{:S(2)}) collective-permute-start(bf16[3,32,1024]{2,1,0:T(8,128)(2,1)} %bitcast.7), channel_id=1, source_target_pairs={{0,16},{4,20},{8,24},{12,28},{16,0},{20,4},{24,8},{28,12},{1,17},{... | collective-permute-start | bytes 589832 | tf_op jit(solution)/shard_map/ppermute | solution.py:31
  73.9 25.0 %collective-permute-start.9 = (bf16[256,1024]{1,0:T(8,128)(2,1)}, bf16[256,1024]{1,0:T(8,128)(2,1)}, u32[]{:S(2)}, u32[]{:S(2)}) collective-permute-start(bf16[256,1024]{1,0:T(8,128)(2,1)} %pad_maximum_fusion.1), channel_id=1, source_target_pairs={{1,3},{2,0},{5,7},{6,4},{9,11},{10,8},{13,15},{14,12},{17,19},{18,... | collective-permute-start | bytes 1572872 | tf_op jit(solution)/shard_map/ppermute | solution.py:507
  75.2 17.6 %collective-permute-start.12 = (bf16[256,512]{1,0:T(8,128)(2,1)}, bf16[256,512]{1,0:T(8,128)(2,1)S(1)}, u32[]{:S(2)}, u32[]{:S(2)}) collective-permute-start(bf16[256,512]{1,0:T(8,128)(2,1)} %get-tuple-element.40), channel_id=1, source_target_pairs={{0,4},{4,8},{8,12},{12,16},{16,20},{20,24},{24,28},{1,5},{5,9},{9,... | collective-permute-start | bytes 786440 | tf_op jit(solution)/shard_map/ppermute | solution.py:516
  76.5 16.2 %collective-permute-start.13 = (bf16[256,512]{1,0:T(8,128)(2,1)S(1)}, bf16[256,512]{1,0:T(8,128)(2,1)S(1)}, u32[]{:S(2)}, u32[]{:S(2)}) collective-permute-start(bf16[256,512]{1,0:T(8,128)(2,1)S(1)} %get-tuple-element.42), channel_id=1, source_target_pairs={{4,0},{8,4},{12,8},{16,12},{20,16},{24,20},{28,24},{5,1},{9,5},{13... | collective-permute-start | bytes 786440 | tf_op jit(solution)/shard_map/ppermute | solution.py:517
  78.0 14.8 %collective-permute-start.10 = (bf16[3,32,1024]{2,1,0:T(8,128)(2,1)}, bf16[3,32,1024]{2,1,0:T(8,128)(2,1)S(1)}, u32[]{:S(2)}, u32[]{:S(2)}) collective-permute-start(bf16[3,32,1024]{2,1,0:T(8,128)(2,1)} %bitcast.7), channel_id=1, source_target_pairs={{0,8},{4,12},{8,0},{12,4},{16,24},{20,28},{24,16},{28,20},{1,9},{5... | collective-permute-start | bytes 589832 | tf_op jit(solution)/shard_map/ppermute | solution.py:31
  82.5 15.4 %collective-permute-start.17 = (bf16[3,32,1024]{2,1,0:T(8,128)(2,1)S(1)}, bf16[3,32,1024]{2,1,0:T(8,128)(2,1)S(1)}, u32[]{:S(2)}, u32[]{:S(2)}) collective-permute-start(bf16[3,32,1024]{2,1,0:T(8,128)(2,1)S(1)} %collective-permute-done.11), channel_id=1, source_target_pairs={{0,8},{4,12},{8,0},{12,4},{16,24},{20,28},{24,16},{28,20},{1,9},{5... | collective-permute-start | bytes 589832 | tf_op jit(solution)/shard_map/ppermute | solution.py:31
  98.9 22.1 %collective-permute-start.18 = (bf16[4,3,32,1024]{3,2,1,0:T(8,128)(2,1)S(1)}, bf16[4,3,32,1024]{3,2,1,0:T(8,128)(2,1)S(1)}, u32[]{:S(2)}, u32[]{:S(2)}) collective-permute-start(bf16[4,3,32,1024]{3,2,1,0:T(8,128)(2,1)S(1)} %pad_maximum_fusion.refs_4_), channel_id=1, source_target_pairs={{0,4},{4,0},{8,12},{12,8},{16,20},{20,16},{24,28},{28,24},{1,5},{5... | collective-permute-start | bytes 2359304 | tf_op jit(solution)/shard_map/ppermute | solution.py:31
  101.3 22.2 %collective-permute-start.24 = (bf16[256,1024]{1,0:T(8,128)(2,1)}, bf16[256,1024]{1,0:T(8,128)(2,1)S(1)}, u32[]{:S(2)}, u32[]{:S(2)}) collective-permute-start(bf16[256,1024]{1,0:T(8,128)(2,1)} %get-tuple-element.63), channel_id=1, source_target_pairs={{0,16},{4,20},{8,24},{12,28},{16,0},{20,4},{24,8},{28,12},{1,17},{... | collective-permute-start | bytes 1572872 | tf_op jit(solution)/shard_map/ppermute | solution.py:31
  101.8 14.2 %collective-permute-start.15 = (bf16[256,256]{1,0:T(8,128)(2,1)S(1)}, bf16[256,256]{1,0:T(8,128)(2,1)S(1)}, u32[]{:S(2)}, u32[]{:S(2)}) collective-permute-start(bf16[256,256]{1,0:T(8,128)(2,1)S(1)} %get-tuple-element.44), channel_id=1, source_target_pairs={{0,2},{1,3},{2,0},{3,1},{4,6},{5,7},{6,4},{7,5},{8,10},{9,11},{10,... | collective-permute-start | bytes 393224 | tf_op jit(solution)/shard_map/ppermute | solution.py:31
  106.2 23.6 %collective-permute-start.23 = (bf16[256,1024]{1,0:T(8,128)(2,1)}, bf16[256,1024]{1,0:T(8,128)(2,1)}, u32[]{:S(2)}, u32[]{:S(2)}) collective-permute-start(bf16[256,1024]{1,0:T(8,128)(2,1)} %get-tuple-element.63), channel_id=1, source_target_pairs={{0,8},{4,12},{8,0},{12,4},{16,24},{20,28},{24,16},{28,20},{1,9},{5... | collective-permute-start | bytes 1572872 | tf_op jit(solution)/shard_map/ppermute | solution.py:31
  107.1 8.9 %collective-permute-start.16 = (bf16[256,256]{1,0:T(8,128)(2,1)S(1)}, bf16[256,256]{1,0:T(8,128)(2,1)S(1)}, u32[]{:S(2)}, u32[]{:S(2)}) collective-permute-start(bf16[256,256]{1,0:T(8,128)(2,1)S(1)} %get-tuple-element.43), channel_id=1, source_target_pairs={{0,3},{1,2},{2,1},{3,0},{4,7},{5,6},{6,5},{7,4},{8,11},{9,10},{10,... | collective-permute-start | bytes 393224 | tf_op jit(solution)/shard_map/ppermute | solution.py:31
  116.0 5.0 %collective-permute-start.14 = (bf16[256,256]{1,0:T(8,128)(2,1)S(1)}, bf16[256,256]{1,0:T(8,128)(2,1)S(1)}, u32[]{:S(2)}, u32[]{:S(2)}) collective-permute-start(bf16[256,256]{1,0:T(8,128)(2,1)S(1)} %get-tuple-element.48), channel_id=1, source_target_pairs={{0,1},{1,0},{2,3},{3,2},{4,5},{5,4},{6,7},{7,6},{8,9},{9,8},{10,11... | collective-permute-start | bytes 393224 | tf_op jit(solution)/shard_map/ppermute | solution.py:31
  123.5 16.9 %collective-permute-start.19 = (bf16[256,1024]{1,0:T(8,128)(2,1)S(1)}, bf16[256,1024]{1,0:T(8,128)(2,1)S(1)}, u32[]{:S(2)}, u32[]{:S(2)}) collective-permute-start(bf16[256,1024]{1,0:T(8,128)(2,1)S(1)} %first_norm.1.rows_ref.normed_ref), channel_id=1, source_target_pairs={{0,1},{1,0},{2,3},{3,2},{4,5},{5,4},{6,7},{7,6},{8,9},{9,8},{10,11... | collective-permute-start | bytes 1572872 | tf_op jit(solution)/shard_map/ppermute | solution.py:31
  124.3 15.0 %collective-permute-start.25 = (bf16[128,1024]{1,0:T(8,128)(2,1)}, bf16[128,1024]{1,0:T(8,128)(2,1)}, u32[]{:S(2)}, u32[]{:S(2)}) collective-permute-start(bf16[128,1024]{1,0:T(8,128)(2,1)} %slice.86), channel_id=1, source_target_pairs={{0,8},{4,12},{8,0},{12,4},{16,24},{20,28},{24,16},{28,20},{1,9},{5... | collective-permute-start | bytes 786440 | tf_op jit(solution)/shard_map/ppermute | solution.py:31
  130.7 9.6 %collective-permute-start.26 = (bf16[128,1024]{1,0:T(8,128)(2,1)S(1)}, bf16[128,1024]{1,0:T(8,128)(2,1)S(1)}, u32[]{:S(2)}, u32[]{:S(2)}) collective-permute-start(bf16[128,1024]{1,0:T(8,128)(2,1)S(1)} %slice.87), channel_id=1, source_target_pairs={{0,16},{4,20},{8,24},{12,28},{16,0},{20,4},{24,8},{28,12},{1,17},{... | collective-permute-start | bytes 786440 | tf_op jit(solution)/shard_map/ppermute | solution.py:31
  140.4 7.5 %collective-permute-start.27 = (bf16[1024,1024]{1,0:T(8,128)(2,1)S(1)}, bf16[1024,1024]{1,0:T(8,128)(2,1)S(1)}, u32[]{:S(2)}, u32[]{:S(2)}) collective-permute-start(bf16[1024,1024]{1,0:T(8,128)(2,1)S(1)} %constant_dynamic-update-slice_fusion.2.held_ref), channel_id=1, source_target_pairs={{0,4},{4,0},{8,12},{12,8},{16,20},{20,16},{24,28},{28,24},{1,5},{5... | collective-permute-start | bytes 6291464 | tf_op jit(solution)/shard_map/ppermute | solution.py:31
  140.5 6.0 %collective-permute-start.22 = (f32[3,2,1024]{2,1,0:T(2,128)S(1)}, f32[3,2,1024]{2,1,0:T(2,128)S(1)}, u32[]{:S(2)}, u32[]{:S(2)}) collective-permute-start(f32[3,2,1024]{2,1,0:T(2,128)S(1)} %get-tuple-element.67), channel_id=1, source_target_pairs={{0,3},{1,2},{2,1},{3,0},{4,7},{5,6},{6,5},{7,4},{8,11},{9,10},{10,... | collective-permute-start | bytes 73736 | tf_op jit(solution)/shard_map/ppermute | solution.py:31
  142.6 4.8 %collective-permute-start.21 = (f32[3,2,1024]{2,1,0:T(2,128)S(1)}, f32[3,2,1024]{2,1,0:T(2,128)S(1)}, u32[]{:S(2)}, u32[]{:S(2)}) collective-permute-start(f32[3,2,1024]{2,1,0:T(2,128)S(1)} %get-tuple-element.68), channel_id=1, source_target_pairs={{0,2},{1,3},{2,0},{3,1},{4,6},{5,7},{6,4},{7,5},{8,10},{9,11},{10,... | collective-permute-start | bytes 73736 | tf_op jit(solution)/shard_map/ppermute | solution.py:31
  144.0 3.8 %collective-permute-start.20 = (f32[3,2,1024]{2,1,0:T(2,128)S(1)}, f32[3,2,1024]{2,1,0:T(2,128)S(1)}, u32[]{:S(2)}, u32[]{:S(2)}) collective-permute-start(f32[3,2,1024]{2,1,0:T(2,128)S(1)} %get-tuple-element.69), channel_id=1, source_target_pairs={{0,1},{1,0},{2,3},{3,2},{4,5},{5,4},{6,7},{7,6},{8,9},{9,8},{10,11... | collective-permute-start | bytes 73736 | tf_op jit(solution)/shard_map/ppermute | solution.py:31
  150.5 12.7 %collective-permute-start.28 = (bf16[256,1024]{1,0:T(8,128)(2,1)S(1)}, bf16[256,1024]{1,0:T(8,128)(2,1)S(1)}, u32[]{:S(2)}, u32[]{:S(2)}) collective-permute-start(bf16[256,1024]{1,0:T(8,128)(2,1)S(1)} %feed_far.1), channel_id=1, source_target_pairs={{0,1},{1,0},{2,3},{3,2},{4,5},{5,4},{6,7},{7,6},{8,9},{9,8},{10,11... | collective-permute-start | bytes 1572872 | tf_op jit(solution)/shard_map/ppermute | solution.py:31
  (21 other events, 245.4 us)

commit v8 on v7

--- a/solution.py
+++ b/solution.py
@@ -42,15 +42,16 @@
 
 
 def project_kernel(place_ref, weight_ref, *refs):
-    shards, (query_ref, keyval_ref, top_ref, bottom_ref, rows_ref, sems) = refs[:-6], refs[-6:]
+    shards, (query_ref, keyval_ref, top_ref, bottom_ref, riders_ref, rows_ref, sems, rider_sems) = refs[:-8], refs[-8:]
     kv = place_ref[1]
     count = top_ref.shape[0]
     steps = (len(shards) - 1) // 2
     width = weight_ref.shape[2]
-    moves = [(shards[0], kv, None)]
+    depth = riders_ref.shape[1]
+    moves = [(shards[0], kv, None, None)]
     for step in range(1, steps + 1):
-        moves.append((shards[step], kv - step, kv >= step))
-        moves.append((shards[steps + step], kv + step, kv + step <= steps))
+        moves.append((shards[step], kv - step, kv >= step, steps - step))
+        moves.append((shards[steps + step], kv + step, kv + step <= steps, step - 1))
 
     def guarded(needed, act):
         if needed is None:
@@ -59,10 +60,13 @@
             pl.when(needed)(act)
 
     copies = []
-    for index, (source, owner, needed) in enumerate(moves):
+    for index, (source, owner, needed, turn) in enumerate(moves):
         safe = owner if needed is None else jnp.where(needed, owner, 0)
         at = pl.ds(pl.multiple_of(safe * count, count), count)
         copies.append((needed, pltpu.make_async_copy(source.at[0:count], rows_ref.at[at], sems.at[index])))
+        if turn is not None:
+            rider = source.at[count : count + depth]
+            copies.append((needed, pltpu.make_async_copy(rider, riders_ref.at[turn], rider_sems.at[index])))
     for needed, copy in copies:
         guarded(needed, copy.start)
     for needed, copy in copies:
@@ -77,7 +81,7 @@
     bottom_ref[...] = keyval_ref[steps * count :]
 
 
-def project(place, weight, shards):
+def project(place, weight, shards, depth):
     rows, width = shards[0].shape
     heads_width = weight.shape[2]
     blocks = (len(shards) + 1) // 2
@@ -89,10 +93,11 @@
             jax.ShapeDtypeStruct((blocks * rows, 2 * heads_width), BF16),
             edge,
             edge,
+            jax.ShapeDtypeStruct((blocks - 1, depth, width), BF16),
         ),
         in_specs=[SMEM, VMEM] + [ANY] * len(shards),
-        out_specs=(VMEM,) * 4,
-        scratch_shapes=[pltpu.VMEM((blocks * rows, width), BF16), pltpu.SemaphoreType.DMA((len(shards),))],
+        out_specs=(VMEM,) * 5,
+        scratch_shapes=[pltpu.VMEM((blocks * rows, width), BF16)] + [pltpu.SemaphoreType.DMA((len(shards),))] * 2,
         compiler_params=pltpu.CompilerParams(vmem_limit_bytes=14 * MIB),
         cost_estimate=SHORT,
         name="project",
@@ -192,19 +197,21 @@
 def first_norm_kernel(layout, place_ref, hidden_ref, own_out_ref, gain_ref, bias_ref, *refs):
     parts, pieces = refs[: -5 - len(layout)], refs[-5 - len(layout) : -5]
     normed_ref, all_ref, weight_ref, mixed_ref, sems = refs[-5:]
-    tok = place_ref[0]
+    tok, kv = place_ref[0], place_ref[1]
     quarters, heads_width, width = weight_ref.shape
-    copies = [pltpu.make_async_copy(own_out_ref, weight_ref.at[0], sems.at[0])]
+    copies = [pltpu.make_async_copy(own_out_ref, weight_ref.at[kv], sems.at[0])]
     for flips, piece in zip(layout, pieces):
         for index, flip in enumerate(flips):
-            depth = piece.shape[2]
-            at = pl.multiple_of((tok ^ flip) * depth, depth)
-            target = weight_ref.at[1:quarters, pl.ds(at, depth)]
-            copies.append(pltpu.make_async_copy(piece.at[index], target, sems.at[len(copies)]))
+            for turn in range(1, quarters):
+                depth = piece.shape[2]
+                at = pl.multiple_of((tok ^ flip) * depth, depth)
+                target = weight_ref.at[lax.rem(kv + turn, quarters), pl.ds(at, depth)]
+                copies.append(pltpu.make_async_copy(piece.at[index, turn - 1], target, sems.at[len(copies)]))
     for copy in copies:
         copy.start()
     for flip, part_ref in enumerate(parts):
-        all_ref[:, flip * heads_width : (flip + 1) * heads_width] = part_ref[...]
+        at = pl.multiple_of((kv ^ flip) * heads_width, heads_width)
+        all_ref[:, pl.ds(at, heads_width)] = part_ref[...]
     for copy in copies:
         copy.wait()
     weight = weight_ref[...].reshape(quarters * heads_width, width)
@@ -228,7 +235,7 @@
             pltpu.VMEM((rows, width), BF16),
             pltpu.VMEM((len(parts), heads_width, width), BF16),
             pltpu.VMEM((rows, width), F32),
-            pltpu.SemaphoreType.DMA((1 + sum(len(flips) for flips in layout),)),
+            pltpu.SemaphoreType.DMA((1 + (len(parts) - 1) * sum(len(flips) for flips in layout),)),
         ],
         compiler_params=pltpu.CompilerParams(vmem_limit_bytes=11 * MIB),
         cost_estimate=SHORT,
@@ -441,13 +448,12 @@
 
 
 def decode_partial(queries, own, kv_cache, piece_req, piece_used):
-    kv = lax.axis_index("kv")
+    kv, kvs = lax.axis_index("kv"), lax.axis_size("kv")
     owners = piece_req[0]
     home = owners // own
-    place = jnp.where(home <= kv, kv - home, lax.axis_size("kv") - 1 + home - kv)
-    sources = place * own + owners % own
+    sources = ((home + kvs - kv) % kvs) * own + owners % own
     slots = (home ^ kv) * own + owners % own
-    return decode(sources, slots, piece_used[0], queries, own * lax.axis_size("kv"), kv_cache)
+    return decode(sources, slots, piece_used[0], queries, own * kvs, kv_cache)
 
 
 def exchanged_partials(partial, own):
@@ -488,40 +494,38 @@
     place = jnp.stack([tok, kv]).astype(jnp.int32)
     eighth = lambda value: lax.dynamic_slice_in_dim(value, tok * (value.shape[0] // toks), value.shape[0] // toks, 0)
 
+    out_part = eighth(out_weight)
+    depth = out_part.shape[0]
     from_below, from_above = [], []
-    rising = falling = jnp.concatenate([hidden_in, dec_query], axis=0)
+    rising = falling = jnp.concatenate([hidden_in, out_part, dec_query], axis=0)
     for step in range(1, kvs):
         links = range(step - 1, kvs - 1)
         rising = lax.ppermute(rising, "kv", [(i, i + 1) for i in links])
         falling = lax.ppermute(falling, "kv", [(kvs - 1 - i, kvs - 2 - i) for i in links])
         from_below.append(rising)
         from_above.append(falling)
-
-    out_part = eighth(out_weight)
-    depth = out_part.shape[0]
-    out_one = swapped(after(out_part, from_below[0], from_above[0]), "kv", 1)
-    out_two = swapped(after(jnp.concatenate([out_part, out_one], axis=0), from_below[1], from_above[1]), "kv", 2)
-    out_here = jnp.concatenate([out_one, out_two], axis=0).reshape(kvs - 1, depth, width)
-    feed_part = jnp.concatenate([eighth(up_weight), eighth(down_weight)], axis=0)
-    feed_inner = lax.ppermute(after(feed_part, from_below[1], from_above[1]), "kv", [(0, 2), (3, 1)])
-    feed_outer = lax.ppermute(after(feed_part, rising, falling, feed_inner, out_two), "kv", [(1, 3), (2, 0)])
+    feed_up, feed_down = after((eighth(up_weight), eighth(down_weight)), from_below[1], from_above[1])
+    inner_up = lax.ppermute(feed_up, "kv", [(0, 2), (3, 1)])
+    inner_down = lax.ppermute(feed_down, "kv", [(0, 2), (3, 1)])
+    feed_part = after(jnp.concatenate([feed_up, feed_down], axis=0), rising, falling, inner_up, inner_down)
+    feed_outer = lax.ppermute(feed_part, "kv", [(1, 3), (2, 0)])
+    feed_inner = jnp.concatenate([inner_up, inner_down], axis=0)
 
     order = jnp.arange(stretch_len.shape[0])
     ends = jnp.sum(jnp.where(order[:, None] <= order[None, :], stretch_len[:, None], 0), axis=0, dtype=jnp.int32)
     starts = (ends - stretch_len)[None, :]
     ends = ends[None, :]
 
-    shards = [after(hidden_in, feed_inner, out_two)] + from_below + from_above
-    query, keyval, top, bottom = project(place, jnp.transpose(qkv_weight, (1, 0, 2)), shards)
+    shards = [after(hidden_in, inner_up, inner_down)] + from_below + from_above
+    query, keyval, top, bottom, out_here = project(place, jnp.transpose(qkv_weight, (1, 0, 2)), shards, depth)
     before = lax.ppermute(bottom, "tok", [(i, i + 1) for i in range(toks - 1)])
     behind = lax.ppermute(top, "tok", [(i + 1, i) for i in range(toks - 1)])
-    out_here = after(out_here, query)
     out_x, out_y = swapped(out_here, "tok", 2), swapped(out_here, "tok", 4)
-    window = (place, starts, ends, after(query, out_x, out_y), before, keyval, behind, rows)
+    window = (place, starts, ends, query, before, keyval, behind, rows)
     parts = [None] * kvs
     parts[3], parts[2] = attend_blocks(*window, (3, 2), "attend_far")
-    out_all = jnp.stack([out_here, out_x, out_y, swapped(out_y, "tok", 2)])
-    out_core = swapped(after(out_all, parts[3]), "tok", 1)
+    out_all = jnp.stack([out_here, out_x, out_y, swapped(after(out_y, parts[3]), "tok", 2)])
+    out_core = swapped(out_all, "tok", 1)
     inner = (kv == 1) | (kv == 2)
     feed_here = jnp.where(inner, feed_inner, after(feed_outer, parts[3], parts[2]))
     parts[3], parts[2] = swapped(parts[3], "kv", 3), swapped(parts[2], "kv", 2)
@@ -537,8 +541,11 @@
     far_up = swapped(after(feed_y, normed)[:half], "tok", 2)
     far_down = swapped(after(feed_x, normed)[half:], "tok", 4)
     own = dec_query.shape[0]
-    queries = jnp.concatenate([dec_query] + [shard[rows:] for shard in from_below + from_above], axis=0)
-    queries = after(queries.astype(F32), normed)
+    queries = [dec_query]
+    for turn in range(1, kvs):
+        above, below = from_above[turn - 1], from_below[kvs - 1 - turn]
+        queries.append(jnp.where(kv + turn < kvs, above[rows + depth :], below[rows + depth :]))
+    queries = after(jnp.concatenate(queries, axis=0).astype(F32), normed)
     partial = decode_partial(queries, own, kv_cache, piece_req, piece_used)
     dec_parts = exchanged_partials(after(partial, partner), own)
     held = jnp.concatenate([feed_here, feed_x, feed_y, after(far_up, partial), far_down], axis=0)

time: 166 us -> 151 us (0.910)
  local copies, waits for them, and re-layouts: 18.5 us -> 3.09 us
    ppermute x19 -> x17, waiting for transfers between devices: 39.4 us -> 26.5 us  [swapped(): return lax.ppermute(value, axis, [(i, i ^ flip) for i in range(count)])]
    unnamed x52 -> x31, local copies, waits for them, and re-layouts: 9.74 us -> 0.17 us
    ppermute x2 -> x3, waiting for transfers between devices: 0.01 us -> 6.47 us  [the longest x1 3.48 us: routed_body(): inner_up = lax.ppermute(feed_up, 'kv', [(0, 2), (3, 1)])]
    ppermute x3, waiting for transfers between devices: 21 us -> 25.8 us  [routed_body(): lax.ppermute(falling, 'kv', [(kvs - 1 - i, kvs - 2 - i) for i in links])]
    slice x6 -> x0, local copies, waits for them, and re-layouts: 4.33 us -> none  [routed_body(): shard[rows:]]
    ppermute x2 -> x3, starting transfers between devices: 8.65 us -> 11.6 us  [the longest x1 8.34 us: routed_body(): inner_up = lax.ppermute(feed_up, 'kv', [(0, 2), (3, 1)])]
    ppermute x19 -> x17, starting transfers between devices: 25 us -> 22.5 us  [swapped(): return lax.ppermute(value, axis, [(i, i ^ flip) for i in range(count)])]
    select_n x0 -> x3, other arithmetic: none -> 2.19 us  [routed_body(): jnp.where(kv + turn < kvs, above[rows + depth:], below[rows + depth:])]
  transfers between devices with their start and end apart: 29 -> 28, of which waited for: 10 -> 13; matrix products, arithmetic and copies ran while one was open for 10% -> 5% of each run, Pallas kernels for 13% -> 16%
where the time goes in v8:
time: 151 us
  waiting for transfers between devices  58.8 us (39%)
  starting transfers between devices  49.2 us (33%)
  Pallas kernels  31.2 us (21%)
  other arithmetic  7.26 us (5%)
  local copies, waits for them, and re-layouts  3.09 us (2%)
    ppermute x17, waiting for transfers between devices, swapped(): return lax.ppermute(value, axis, [(i, i ^ flip) for i in range(count)])  26.5 us
    ppermute x3, waiting for transfers between devices, routed_body(): lax.ppermute(falling, 'kv', [(kvs - 1 - i, kvs - 2 - i) for i in links])  25.8 us
    ppermute x17, starting transfers between devices, swapped(): return lax.ppermute(value, axis, [(i, i ^ flip) for i in range(count)])  22.5 us
    pallas_call x2, Pallas kernels, attend_blocks(): pl.pallas_call(functools.partial(attend_kernel, flips), out_shape=tuple((...  10.3 us
    ppermute x3, starting transfers between devices, routed_body(): rising = lax.ppermute(rising, 'kv', [(i, i + 1) for i in links])  8.59 us
    ppermute x1, starting transfers between devices, routed_body(): inner_up = lax.ppermute(feed_up, 'kv', [(0, 2), (3, 1)])  8.34 us
    pallas_call x1, Pallas kernels, first_norm(): pl.pallas_call(functools.partial(first_norm_kernel, layout), out_shape=ja...  3.97 us
    pallas_call x1, Pallas kernels, feed(): pl.pallas_call(feed_kernel, out_shape=jax.ShapeDtypeStruct((count, width)...  3.91 us
  transfers between devices with their start and end apart: 28, of which 13 were waited for; matrix products, arithmetic and copies ran while one was open for 5% of the time, Pallas kernels for 16%

profile of v8, /device:TPU:0, one launch (start us, length us, event | category | flops | bytes accessed | tf_op | source)
XLA Modules:
  0.0 150.6 jit_solution(11666231842200389335)
XLA Ops:
  2.8 1.3 collective-permute-start.2
  4.1 5.6 %collective-permute-start = (bf16[290,1024]{1,0:T(8,128)(2,1)S(1)}, bf16[290,1024]{1,0:T(8,128)(2,1)S(1)}, u32[]{:S(2)}, u32[]{:S(2)}) collective-permute-start(bf16[290,1024]{1,0:T(8,128)(2,1)S(1)} %pad_maximum_fusion.1), channel_id=1, source_target_pairs={{0,1},{1,2},{2,3},{4,5},{5,6},{6,7},{8,9},{9,10},{10,11},{12,13},{... | collective-permute-start | bytes 1781768 | tf_op jit(solution)/shard_map/ppermute | solution.py:503
  9.7 11.7 %collective-permute-done.2.refs_4_ = bf16[290,1024]{1,0:T(8,128)(2,1)S(1)} collective-permute-done((bf16[290,1024]{1,0:T(8,128)(2,1)S(1)}, bf16[290,1024]{1,0:T(8,128)(2,1)S(1)}, u32[]{:S(2)}, u32[]{:S(2)}) %collective-permute-start.2) | collective-permute-done | bytes 593952 | tf_op jit(solution)/shard_map/ppermute | solution.py:504
  22.7 1.5 collective-permute-start.1
  24.2 14.1 %collective-permute-done.3.refs_5_ = bf16[290,1024]{1,0:T(8,128)(2,1)} collective-permute-done((bf16[290,1024]{1,0:T(8,128)(2,1)S(1)}, bf16[290,1024]{1,0:T(8,128)(2,1)}, u32[]{:S(2)}, u32[]{:S(2)}) %collective-permute-start.3) | collective-permute-done | bytes 593952 | tf_op jit(solution)/shard_map/ppermute | solution.py:504
  39.5 1.5 %collective-permute-start.6 = (bf16[290,1024]{1,0:T(8,128)(2,1)}, bf16[290,1024]{1,0:T(8,128)(2,1)}, u32[]{:S(2)}, u32[]{:S(2)}) collective-permute-start(bf16[290,1024]{1,0:T(8,128)(2,1)} %collective-permute-done.1.refs_2_), channel_id=1, source_target_pairs={{2,3},{6,7},{10,11},{14,15},{18,19},{22,23},{26,27},{30,31}} | collective-permute-start | bytes 1781768 | tf_op jit(solution)/shard_map/ppermute | solution.py:503
  41.8 1.8 %constant_dynamic-slice_fusion.1 = (bf16[128,1024]{1,0:T(8,128)(2,1)}, bf16[128,1024]{1,0:T(8,128)(2,1)}) fusion(bf16[1024,1024]{1,0:T(8,128)(2,1)} %down_near_ref.1, s32[]{:T(128)S(6)} %select_n.58, bf16[1024,1024]{1,0:T(8,128)(2,1)} %up_near_ref.1), kind=kLoop, calls=%fused_computation.51 | loop fusion | bytes 1048580 | tf_op jit(solution)/shard_map/dynamic_slice | solution.py:495
  43.6 8.3 %collective-permute-start.4 = (bf16[128,1024]{1,0:T(8,128)(2,1)}, bf16[128,1024]{1,0:T(8,128)(2,1)}, u32[]{:S(2)}, u32[]{:S(2)}) collective-permute-start(bf16[128,1024]{1,0:T(8,128)(2,1)} %get-tuple-element.30), channel_id=1, source_target_pairs={{0,2},{3,1},{4,6},{7,5},{8,10},{11,9},{12,14},{15,13},{16,18},{19,... | collective-permute-start | bytes 786440 | tf_op jit(solution)/shard_map/ppermute | solution.py:508
  52.0 2.0 %collective-permute-start.5 = (bf16[128,1024]{1,0:T(8,128)(2,1)}, bf16[128,1024]{1,0:T(8,128)(2,1)}, u32[]{:S(2)}, u32[]{:S(2)}) collective-permute-start(bf16[128,1024]{1,0:T(8,128)(2,1)} %get-tuple-element.31), channel_id=1, source_target_pairs={{0,2},{3,1},{4,6},{7,5},{8,10},{11,9},{12,14},{15,13},{16,18},{19,... | collective-permute-start | bytes 786440 | tf_op jit(solution)/shard_map/ppermute | solution.py:509
  54.1 3.5 %collective-permute-done.4 = bf16[128,1024]{1,0:T(8,128)(2,1)} collective-permute-done((bf16[128,1024]{1,0:T(8,128)(2,1)}, bf16[128,1024]{1,0:T(8,128)(2,1)}, u32[]{:S(2)}, u32[]{:S(2)}) %collective-permute-start.4) | collective-permute-done | bytes 262176 | tf_op jit(solution)/shard_map/ppermute | solution.py:508
  57.6 2.8 %collective-permute-done.5 = bf16[128,1024]{1,0:T(8,128)(2,1)} collective-permute-done((bf16[128,1024]{1,0:T(8,128)(2,1)}, bf16[128,1024]{1,0:T(8,128)(2,1)}, u32[]{:S(2)}, u32[]{:S(2)}) %collective-permute-start.5) | collective-permute-done | bytes 262176 | tf_op jit(solution)/shard_map/ppermute | solution.py:509
  60.4 3.9 %project.1 = (bf16[1024,256]{1,0:T(8,128)(2,1)S(1)}, bf16[1024,512]{1,0:T(8,128)(2,1)S(1)}, bf16[256,512]{1,0:T(8,128)(2,1)S(1)}, bf16[256,512]{1,0:T(8,128)(2,1)S(1)}, bf16[3,32,1024]{2,1,0:T(8,128)(2,1)S(1)}) custom-call(s32[2]{0:T(128)S(1)} %pad_add_fusion.place_ref, bf16[3,1024,256]{2,1,0:T(8,128)(2,1)S(1)} %bitcast.136, ...), custom_call_target="tpu_custom_call" | custom-call | flops 1 | bytes 1 | tf_op jit(solution)/shard_map/project/pallas_call | solution.py:89
  64.3 1.3 collective-permute-start.9
  68.0 5.4 %collective-permute-start.15 = (bf16[3,32,1024]{2,1,0:T(8,128)(2,1)S(1)}, bf16[3,32,1024]{2,1,0:T(8,128)(2,1)S(1)}, u32[]{:S(2)}, u32[]{:S(2)}) collective-permute-start(bf16[3,32,1024]{2,1,0:T(8,128)(2,1)S(1)} %get-tuple-element.44), channel_id=1, source_target_pairs={{0,16},{4,20},{8,24},{12,28},{16,0},{20,4},{24,8},{28,12},{1,17},{... | collective-permute-start | bytes 589832 | tf_op jit(solution)/shard_map/ppermute | solution.py:31
  75.4 5.1 %attend_far.1 = (bf16[256,256]{1,0:T(8,128)(2,1)S(1)}, bf16[256,256]{1,0:T(8,128)(2,1)S(1)}) custom-call(s32[2]{0:T(128)S(1)} %pad_add_fusion.place_ref, s32[1,48]{1,0:T(1,128)S(1)} %subtract_bitcast_fusion.starts_ref, s32[1,48]{1,0:T(1,128)S(1)} %bitcast.142, bf16[1024,256]{1,0:T(8,128)(2,1)S(1)} %get-tuple-element.41.query_ref, ...), custom_call_target="tpu_custom_call" | custom-call | flops 1 | bytes 1 | tf_op jit(solution)/shard_map/attend_far/pallas_call | solution.py:179
  80.5 1.5 collective-permute-start.16
  82.0 6.0 %collective-permute-done.16 = bf16[3,32,1024]{2,1,0:T(8,128)(2,1)S(1)} collective-permute-done((bf16[3,32,1024]{2,1,0:T(8,128)(2,1)S(1)}, bf16[3,32,1024]{2,1,0:T(8,128)(2,1)S(1)}, u32[]{:S(2)}, u32[]{:S(2)}) %collective-permute-start.16) | collective-permute-done | bytes 196640 | tf_op jit(solution)/shard_map/ppermute | solution.py:31
  91.9 3.3 %collective-permute-start.12 = (bf16[256,256]{1,0:T(8,128)(2,1)S(1)}, bf16[256,256]{1,0:T(8,128)(2,1)S(1)}, u32[]{:S(2)}, u32[]{:S(2)}) collective-permute-start(bf16[256,256]{1,0:T(8,128)(2,1)S(1)} %get-tuple-element.39), channel_id=1, source_target_pairs={{0,2},{1,3},{2,0},{3,1},{4,6},{5,7},{6,4},{7,5},{8,10},{9,11},{10,... | collective-permute-start | bytes 393224 | tf_op jit(solution)/shard_map/ppermute | solution.py:31
  96.7 5.2 %attend_near.1 = (bf16[256,256]{1,0:T(8,128)(2,1)S(1)}, bf16[256,256]{1,0:T(8,128)(2,1)S(1)}) custom-call(s32[2]{0:T(128)S(1)} %pad_add_fusion.place_ref, s32[1,48]{1,0:T(1,128)S(1)} %subtract_bitcast_fusion.starts_ref, s32[1,48]{1,0:T(1,128)S(1)} %bitcast.143, bf16[1024,256]{1,0:T(8,128)(2,1)S(1)} %get-tuple-element.41.query_ref, ...), custom_call_target="tpu_custom_call" | custom-call | flops 1 | bytes 1 | tf_op jit(solution)/shard_map/attend_near/pallas_call | solution.py:179
  102.0 2.6 %collective-permute-done.12.refs_2_ = bf16[256,256]{1,0:T(8,128)(2,1)S(1)} collective-permute-done((bf16[256,256]{1,0:T(8,128)(2,1)S(1)}, bf16[256,256]{1,0:T(8,128)(2,1)S(1)}, u32[]{:S(2)}, u32[]{:S(2)}) %collective-permute-start.12) | collective-permute-done | bytes 131104 | tf_op jit(solution)/shard_map/ppermute | solution.py:31
  105.3 4.7 %collective-permute-done.11.refs_1_ = bf16[256,256]{1,0:T(8,128)(2,1)S(1)} collective-permute-done((bf16[256,256]{1,0:T(8,128)(2,1)S(1)}, bf16[256,256]{1,0:T(8,128)(2,1)S(1)}, u32[]{:S(2)}, u32[]{:S(2)}) %collective-permute-start.11) | collective-permute-done | bytes 131104 | tf_op jit(solution)/shard_map/ppermute | solution.py:31
  110.0 4.0 %first_norm.1.rows_ref.normed_ref = bf16[256,1024]{1,0:T(8,128)(2,1)S(1)} custom-call(s32[2]{0:T(128)S(1)} %pad_add_fusion.place_ref, bf16[256,1024]{1,0:T(8,128)(2,1)S(1)} %copy-done.2, bf16[256,1024]{1,0:T(8,128)(2,1)S(1)} %copy-done.5, f32[1,1024]{1,0:T(1,128)S(1)} %bitcast.140, f32[1,1024]{1,0:T(1,128)S(1)} %bitcast.141, ...), custom_call_target="tpu_custom_call" | custom-call | flops 1 | bytes 1 | tf_op jit(solution)/shard_map/first_norm/pallas_call | solution.py:229
  115.2 1.7 %collective-permute-start.25 = (bf16[128,1024]{1,0:T(8,128)(2,1)S(1)}, bf16[128,1024]{1,0:T(8,128)(2,1)S(1)}, u32[]{:S(2)}, u32[]{:S(2)}) collective-permute-start(bf16[128,1024]{1,0:T(8,128)(2,1)S(1)} %slice.87), channel_id=1, source_target_pairs={{0,16},{4,20},{8,24},{12,28},{16,0},{20,4},{24,8},{28,12},{1,17},{... | collective-permute-start | bytes 786440 | tf_op jit(solution)/shard_map/ppermute | solution.py:31
  117.0 3.8 %decode.1 = f32[3,8,1024]{2,1,0:T(8,128)S(1)} custom-call(s32[6]{0:T(128)S(1)} %fusion.13.source_ref, s32[6]{0:T(128)S(1)} %get-tuple-element.60.slot_ref, s32[6]{0:T(128)S(1)} %bitcast.144, f32[8,1024]{1,0:T(8,128)S(1)} %maximum_convert_fusion.query_ref, bf16[2,1,6,128,1024]{4,3,2,1,0:T(8,128)(2,1)S(1)} %copy-done.3), custom_call_target="tpu_custom_call" | custom-call | flops 1 | bytes 1 | tf_op jit(solution)/shard_map/decode/pallas_call | solution.py:431
  122.4 4.7 %collective-permute-done.18.rows_ref = bf16[256,1024]{1,0:T(8,128)(2,1)S(1)} collective-permute-done((bf16[256,1024]{1,0:T(8,128)(2,1)S(1)}, bf16[256,1024]{1,0:T(8,128)(2,1)S(1)}, u32[]{:S(2)}, u32[]{:S(2)}) %collective-permute-start.18) | collective-permute-done | bytes 524320 | tf_op jit(solution)/shard_map/ppermute | solution.py:31
  127.2 2.0 %collective-permute-start.20 = (f32[3,2,1024]{2,1,0:T(2,128)S(1)}, f32[3,2,1024]{2,1,0:T(2,128)S(1)}, u32[]{:S(2)}, u32[]{:S(2)}) collective-permute-start(f32[3,2,1024]{2,1,0:T(2,128)S(1)} %get-tuple-element.64), channel_id=1, source_target_pairs={{0,2},{1,3},{2,0},{3,1},{4,6},{5,7},{6,4},{7,5},{8,10},{9,11},{10,... | collective-permute-start | bytes 73736 | tf_op jit(solution)/shard_map/ppermute | solution.py:31
  129.3 2.3 %collective-permute-start.19 = (f32[3,2,1024]{2,1,0:T(2,128)S(1)}, f32[3,2,1024]{2,1,0:T(2,128)S(1)}, u32[]{:S(2)}, u32[]{:S(2)}) collective-permute-start(f32[3,2,1024]{2,1,0:T(2,128)S(1)} %get-tuple-element.65), channel_id=1, source_target_pairs={{0,1},{1,0},{2,3},{3,2},{4,5},{5,4},{6,7},{7,6},{8,9},{9,8},{10,11... | collective-permute-start | bytes 73736 | tf_op jit(solution)/shard_map/ppermute | solution.py:31
  131.6 1.5 feed_near.1.near_ref
  133.4 2.6 %feed_far.1 = bf16[256,1024]{1,0:T(8,128)(2,1)S(1)} custom-call(s32[2]{0:T(128)S(1)} %pad_add_fusion.place_ref, bf16[256,1024]{1,0:T(8,128)(2,1)S(1)} %collective-permute-done.18.rows_ref, f32[256,1024]{1,0:T(8,128)S(1)} %feed_near.1.near_ref, bf16[1024,1024]{1,0:T(8,128)(2,1)S(1)} %constant_dynamic-update-slice_fusion.held_ref, ...), custom_call_target="tpu_custom_call" | custom-call | flops 1 | bytes 1 | tf_op jit(solution)/shard_map/feed_far/pallas_call | solution.py:337
  136.0 2.1 %collective-permute-start.27 = (bf16[256,1024]{1,0:T(8,128)(2,1)S(1)}, bf16[256,1024]{1,0:T(8,128)(2,1)S(1)}, u32[]{:S(2)}, u32[]{:S(2)}) collective-permute-start(bf16[256,1024]{1,0:T(8,128)(2,1)S(1)} %feed_far.1), channel_id=1, source_target_pairs={{0,1},{1,0},{2,3},{3,2},{4,5},{5,4},{6,7},{7,6},{8,9},{9,8},{10,11... | collective-permute-start | bytes 1572872 | tf_op jit(solution)/shard_map/ppermute | solution.py:31
  138.1 3.9 %feed_own.1.near_ref = f32[256,1024]{1,0:T(8,128)S(1)} custom-call(s32[2]{0:T(128)S(1)} %pad_add_fusion.place_ref, bf16[256,1024]{1,0:T(8,128)(2,1)S(1)} %first_norm.1.rows_ref.normed_ref, bf16[1024,1024]{1,0:T(8,128)(2,1)S(1)} %copy-done, bf16[1024,1024]{1,0:T(8,128)(2,1)S(1)} %copy-done.1, ...), custom_call_target="tpu_custom_call" | custom-call | flops 1 | bytes 1 | tf_op jit(solution)/shard_map/feed_own/pallas_call | solution.py:354
  142.7 6.7 %collective-permute-done.27.far_ref = bf16[256,1024]{1,0:T(8,128)(2,1)S(1)} collective-permute-done((bf16[256,1024]{1,0:T(8,128)(2,1)S(1)}, bf16[256,1024]{1,0:T(8,128)(2,1)S(1)}, u32[]{:S(2)}, u32[]{:S(2)}) %collective-permute-start.27) | collective-permute-done | bytes 524320 | tf_op jit(solution)/shard_map/ppermute | solution.py:31
  (84 shorter events, 21.0 us)
Async XLA Ops:
  0.6 59.7 %copy-start.2 = (bf16[256,1024]{1,0:T(8,128)(2,1)S(1)}, bf16[256,1024]{1,0:T(8,128)(2,1)}, u32[]{:S(2)}) copy-start(bf16[256,1024]{1,0:T(8,128)(2,1)} %hidden_ref.1) | copy-start | bytes 1572868
  0.6 53.4 %copy-start.12 = (s32[1,6]{1,0:T(1,128)S(1)}, s32[1,6]{1,0:T(1,128)}, u32[]{:S(2)}) copy-start(s32[1,6]{1,0:T(1,128)} %param.26) | copy-start | bytes 76
  0.7 59.7 %copy-start.4 = (bf16[1024,3,256]{2,0,1:T(8,128)(2,1)S(1)}, bf16[1024,3,256]{2,0,1:T(8,128)(2,1)}, u32[]{:S(2)}) copy-start(bf16[1024,3,256]{2,0,1:T(8,128)(2,1)} %param.15) | copy-start | bytes 4718596
  2.8 18.6 %collective-permute-start.2 = (bf16[290,1024]{1,0:T(8,128)(2,1)S(1)}, bf16[290,1024]{1,0:T(8,128)(2,1)S(1)}, u32[]{:S(2)}, u32[]{:S(2)}) collective-permute-start(bf16[290,1024]{1,0:T(8,128)(2,1)S(1)} %pad_maximum_fusion.1), channel_id=1, source_target_pairs={{3,2},{2,1},{1,0},{7,6},{6,5},{5,4},{11,10},{10,9},{9,8},{15,14},{... | collective-permute-start | bytes 1781768 | tf_op jit(solution)/shard_map/ppermute | solution.py:504
  4.1 18.6 %collective-permute-start = (bf16[290,1024]{1,0:T(8,128)(2,1)S(1)}, bf16[290,1024]{1,0:T(8,128)(2,1)S(1)}, u32[]{:S(2)}, u32[]{:S(2)}) collective-permute-start(bf16[290,1024]{1,0:T(8,128)(2,1)S(1)} %pad_maximum_fusion.1), channel_id=1, source_target_pairs={{0,1},{1,2},{2,3},{4,5},{5,6},{6,7},{8,9},{9,10},{10,11},{12,13},{... | collective-permute-start | bytes 1781768 | tf_op jit(solution)/shard_map/ppermute | solution.py:503
  21.4 16.9 %collective-permute-start.3 = (bf16[290,1024]{1,0:T(8,128)(2,1)S(1)}, bf16[290,1024]{1,0:T(8,128)(2,1)}, u32[]{:S(2)}, u32[]{:S(2)}) collective-permute-start(bf16[290,1024]{1,0:T(8,128)(2,1)S(1)} %collective-permute-done.2.refs_4_), channel_id=1, source_target_pairs={{2,1},{1,0},{6,5},{5,4},{10,9},{9,8},{14,13},{13,12},{18,17},{17,1... | collective-permute-start | bytes 1781768 | tf_op jit(solution)/shard_map/ppermute | solution.py:504
  22.7 16.8 %collective-permute-start.1 = (bf16[290,1024]{1,0:T(8,128)(2,1)S(1)}, bf16[290,1024]{1,0:T(8,128)(2,1)}, u32[]{:S(2)}, u32[]{:S(2)}) collective-permute-start(bf16[290,1024]{1,0:T(8,128)(2,1)S(1)} %collective-permute-done.refs_1_), channel_id=1, source_target_pairs={{1,2},{2,3},{5,6},{6,7},{9,10},{10,11},{13,14},{14,15},{17,18},{18... | collective-permute-start | bytes 1781768 | tf_op jit(solution)/shard_map/ppermute | solution.py:503
  38.2 22.1 %collective-permute-start.7 = (bf16[290,1024]{1,0:T(8,128)(2,1)}, bf16[290,1024]{1,0:T(8,128)(2,1)}, u32[]{:S(2)}, u32[]{:S(2)}) collective-permute-start(bf16[290,1024]{1,0:T(8,128)(2,1)} %collective-permute-done.3.refs_5_), channel_id=1, source_target_pairs={{1,0},{5,4},{9,8},{13,12},{17,16},{21,20},{25,24},{29,28}} | collective-permute-start | bytes 1781768 | tf_op jit(solution)/shard_map/ppermute | solution.py:504
  39.5 20.8 %collective-permute-start.6 = (bf16[290,1024]{1,0:T(8,128)(2,1)}, bf16[290,1024]{1,0:T(8,128)(2,1)}, u32[]{:S(2)}, u32[]{:S(2)}) collective-permute-start(bf16[290,1024]{1,0:T(8,128)(2,1)} %collective-permute-done.1.refs_2_), channel_id=1, source_target_pairs={{2,3},{6,7},{10,11},{14,15},{18,19},{22,23},{26,27},{30,31}} | collective-permute-start | bytes 1781768 | tf_op jit(solution)/shard_map/ppermute | solution.py:503
  43.6 13.9 %collective-permute-start.4 = (bf16[128,1024]{1,0:T(8,128)(2,1)}, bf16[128,1024]{1,0:T(8,128)(2,1)}, u32[]{:S(2)}, u32[]{:S(2)}) collective-permute-start(bf16[128,1024]{1,0:T(8,128)(2,1)} %get-tuple-element.30), channel_id=1, source_target_pairs={{0,2},{3,1},{4,6},{7,5},{8,10},{11,9},{12,14},{15,13},{16,18},{19,... | collective-permute-start | bytes 786440 | tf_op jit(solution)/shard_map/ppermute | solution.py:508
  52.0 8.4 %collective-permute-start.5 = (bf16[128,1024]{1,0:T(8,128)(2,1)}, bf16[128,1024]{1,0:T(8,128)(2,1)}, u32[]{:S(2)}, u32[]{:S(2)}) collective-permute-start(bf16[128,1024]{1,0:T(8,128)(2,1)} %get-tuple-element.31), channel_id=1, source_target_pairs={{0,2},{3,1},{4,6},{7,5},{8,10},{11,9},{12,14},{15,13},{16,18},{19,... | collective-permute-start | bytes 786440 | tf_op jit(solution)/shard_map/ppermute | solution.py:509
  64.3 11.1 %collective-permute-start.9 = (bf16[256,512]{1,0:T(8,128)(2,1)S(1)}, bf16[256,512]{1,0:T(8,128)(2,1)S(1)}, u32[]{:S(2)}, u32[]{:S(2)}) collective-permute-start(bf16[256,512]{1,0:T(8,128)(2,1)S(1)} %get-tuple-element.35), channel_id=1, source_target_pairs={{0,4},{4,8},{8,12},{12,16},{16,20},{20,24},{24,28},{1,5},{5,9},{9,... | collective-permute-start | bytes 786440 | tf_op jit(solution)/shard_map/ppermute | solution.py:521
  65.6 9.8 %collective-permute-start.10 = (bf16[256,512]{1,0:T(8,128)(2,1)S(1)}, bf16[256,512]{1,0:T(8,128)(2,1)S(1)}, u32[]{:S(2)}, u32[]{:S(2)}) collective-permute-start(bf16[256,512]{1,0:T(8,128)(2,1)S(1)} %get-tuple-element.37), channel_id=1, source_target_pairs={{4,0},{8,4},{12,8},{16,12},{20,16},{24,20},{28,24},{5,1},{9,5},{13... | collective-permute-start | bytes 786440 | tf_op jit(solution)/shard_map/ppermute | solution.py:522
  68.0 12.5 %collective-permute-start.15 = (bf16[3,32,1024]{2,1,0:T(8,128)(2,1)S(1)}, bf16[3,32,1024]{2,1,0:T(8,128)(2,1)S(1)}, u32[]{:S(2)}, u32[]{:S(2)}) collective-permute-start(bf16[3,32,1024]{2,1,0:T(8,128)(2,1)S(1)} %get-tuple-element.44), channel_id=1, source_target_pairs={{0,16},{4,20},{8,24},{12,28},{16,0},{20,4},{24,8},{28,12},{1,17},{... | collective-permute-start | bytes 589832 | tf_op jit(solution)/shard_map/ppermute | solution.py:31
  73.4 15.4 %collective-permute-start.8 = (bf16[256,1024]{1,0:T(8,128)(2,1)S(1)}, bf16[256,1024]{1,0:T(8,128)(2,1)S(1)}, u32[]{:S(2)}, u32[]{:S(2)}) collective-permute-start(bf16[256,1024]{1,0:T(8,128)(2,1)S(1)} %pad_maximum_fusion.2), channel_id=1, source_target_pairs={{1,3},{2,0},{5,7},{6,4},{9,11},{10,8},{13,15},{14,12},{17,19},{18,... | collective-permute-start | bytes 1572872 | tf_op jit(solution)/shard_map/ppermute | solution.py:511
  74.7 7.3 %collective-permute-start.14 = (bf16[3,32,1024]{2,1,0:T(8,128)(2,1)S(1)}, bf16[3,32,1024]{2,1,0:T(8,128)(2,1)S(1)}, u32[]{:S(2)}, u32[]{:S(2)}) collective-permute-start(bf16[3,32,1024]{2,1,0:T(8,128)(2,1)S(1)} %get-tuple-element.44), channel_id=1, source_target_pairs={{0,8},{4,12},{8,0},{12,4},{16,24},{20,28},{24,16},{28,20},{1,9},{5... | collective-permute-start | bytes 589832 | tf_op jit(solution)/shard_map/ppermute | solution.py:31
  80.5 7.6 %collective-permute-start.16 = (bf16[3,32,1024]{2,1,0:T(8,128)(2,1)S(1)}, bf16[3,32,1024]{2,1,0:T(8,128)(2,1)S(1)}, u32[]{:S(2)}, u32[]{:S(2)}) collective-permute-start(bf16[3,32,1024]{2,1,0:T(8,128)(2,1)S(1)} %collective-permute-done.15), channel_id=1, source_target_pairs={{0,8},{4,12},{8,0},{12,4},{16,24},{20,28},{24,16},{28,20},{1,9},{5... | collective-permute-start | bytes 589832 | tf_op jit(solution)/shard_map/ppermute | solution.py:31
  88.1 21.9 %collective-permute-start.17 = (bf16[4,3,32,1024]{3,2,1,0:T(8,128)(2,1)S(1)}, bf16[4,3,32,1024]{3,2,1,0:T(8,128)(2,1)S(1)}, u32[]{:S(2)}, u32[]{:S(2)}) collective-permute-start(bf16[4,3,32,1024]{3,2,1,0:T(8,128)(2,1)S(1)} %pad_maximum_fusion.refs_4_), channel_id=1, source_target_pairs={{0,4},{4,0},{8,12},{12,8},{16,20},{20,16},{24,28},{28,24},{1,5},{5... | collective-permute-start | bytes 2359304 | tf_op jit(solution)/shard_map/ppermute | solution.py:31
  88.8 21.3 %copy-start.9 = (f32[1024]{0:T(1024)S(1)}, f32[1024]{0:T(1024)}, u32[]{:S(2)}) copy-start(f32[1024]{0:T(1024)} %param.19) | copy-start | bytes 12292
  90.1 24.3 %collective-permute-start.23 = (bf16[256,1024]{1,0:T(8,128)(2,1)S(1)}, bf16[256,1024]{1,0:T(8,128)(2,1)S(1)}, u32[]{:S(2)}, u32[]{:S(2)}) collective-permute-start(bf16[256,1024]{1,0:T(8,128)(2,1)S(1)} %get-tuple-element.59), channel_id=1, source_target_pairs={{0,16},{4,20},{8,24},{12,28},{16,0},{20,4},{24,8},{28,12},{1,17},{... | collective-permute-start | bytes 1572872 | tf_op jit(solution)/shard_map/ppermute | solution.py:31
  91.9 12.7 %collective-permute-start.12 = (bf16[256,256]{1,0:T(8,128)(2,1)S(1)}, bf16[256,256]{1,0:T(8,128)(2,1)S(1)}, u32[]{:S(2)}, u32[]{:S(2)}) collective-permute-start(bf16[256,256]{1,0:T(8,128)(2,1)S(1)} %get-tuple-element.39), channel_id=1, source_target_pairs={{0,2},{1,3},{2,0},{3,1},{4,6},{5,7},{6,4},{7,5},{8,10},{9,11},{10,... | collective-permute-start | bytes 393224 | tf_op jit(solution)/shard_map/ppermute | solution.py:31
  95.2 19.9 %collective-permute-start.22 = (bf16[256,1024]{1,0:T(8,128)(2,1)S(1)}, bf16[256,1024]{1,0:T(8,128)(2,1)S(1)}, u32[]{:S(2)}, u32[]{:S(2)}) collective-permute-start(bf16[256,1024]{1,0:T(8,128)(2,1)S(1)} %get-tuple-element.59), channel_id=1, source_target_pairs={{0,8},{4,12},{8,0},{12,4},{16,24},{20,28},{24,16},{28,20},{1,9},{5... | collective-permute-start | bytes 1572872 | tf_op jit(solution)/shard_map/ppermute | solution.py:31
  96.5 8.9 %collective-permute-start.13 = (bf16[256,256]{1,0:T(8,128)(2,1)S(1)}, bf16[256,256]{1,0:T(8,128)(2,1)S(1)}, u32[]{:S(2)}, u32[]{:S(2)}) collective-permute-start(bf16[256,256]{1,0:T(8,128)(2,1)S(1)} %get-tuple-element.38), channel_id=1, source_target_pairs={{0,3},{1,2},{2,1},{3,0},{4,7},{5,6},{6,5},{7,4},{8,11},{9,10},{10,... | collective-permute-start | bytes 393224 | tf_op jit(solution)/shard_map/ppermute | solution.py:31
  104.6 5.4 %collective-permute-start.11 = (bf16[256,256]{1,0:T(8,128)(2,1)S(1)}, bf16[256,256]{1,0:T(8,128)(2,1)S(1)}, u32[]{:S(2)}, u32[]{:S(2)}) collective-permute-start(bf16[256,256]{1,0:T(8,128)(2,1)S(1)} %get-tuple-element.43), channel_id=1, source_target_pairs={{0,1},{1,0},{2,3},{3,2},{4,5},{5,4},{6,7},{7,6},{8,9},{9,8},{10,11... | collective-permute-start | bytes 393224 | tf_op jit(solution)/shard_map/ppermute | solution.py:31
  114.0 13.0 %collective-permute-start.18 = (bf16[256,1024]{1,0:T(8,128)(2,1)S(1)}, bf16[256,1024]{1,0:T(8,128)(2,1)S(1)}, u32[]{:S(2)}, u32[]{:S(2)}) collective-permute-start(bf16[256,1024]{1,0:T(8,128)(2,1)S(1)} %first_norm.1.rows_ref.normed_ref), channel_id=1, source_target_pairs={{0,1},{1,0},{2,3},{3,2},{4,5},{5,4},{6,7},{7,6},{8,9},{9,8},{10,11... | collective-permute-start | bytes 1572872 | tf_op jit(solution)/shard_map/ppermute | solution.py:31
  114.4 7.5 %collective-permute-start.24 = (bf16[128,1024]{1,0:T(8,128)(2,1)S(1)}, bf16[128,1024]{1,0:T(8,128)(2,1)S(1)}, u32[]{:S(2)}, u32[]{:S(2)}) collective-permute-start(bf16[128,1024]{1,0:T(8,128)(2,1)S(1)} %slice.86), channel_id=1, source_target_pairs={{0,8},{4,12},{8,0},{12,4},{16,24},{20,28},{24,16},{28,20},{1,9},{5... | collective-permute-start | bytes 786440 | tf_op jit(solution)/shard_map/ppermute | solution.py:31
  115.2 7.2 %collective-permute-start.25 = (bf16[128,1024]{1,0:T(8,128)(2,1)S(1)}, bf16[128,1024]{1,0:T(8,128)(2,1)S(1)}, u32[]{:S(2)}, u32[]{:S(2)}) collective-permute-start(bf16[128,1024]{1,0:T(8,128)(2,1)S(1)} %slice.87), channel_id=1, source_target_pairs={{0,16},{4,20},{8,24},{12,28},{16,0},{20,4},{24,8},{28,12},{1,17},{... | collective-permute-start | bytes 786440 | tf_op jit(solution)/shard_map/ppermute | solution.py:31
  127.1 6.3 %collective-permute-start.26 = (bf16[1024,1024]{1,0:T(8,128)(2,1)S(1)}, bf16[1024,1024]{1,0:T(8,128)(2,1)S(1)}, u32[]{:S(2)}, u32[]{:S(2)}) collective-permute-start(bf16[1024,1024]{1,0:T(8,128)(2,1)S(1)} %constant_dynamic-update-slice_fusion.held_ref), channel_id=1, source_target_pairs={{0,4},{4,0},{8,12},{12,8},{16,20},{20,16},{24,28},{28,24},{1,5},{5... | collective-permute-start | bytes 6291464 | tf_op jit(solution)/shard_map/ppermute | solution.py:31
  127.1 6.0 %collective-permute-start.21 = (f32[3,2,1024]{2,1,0:T(2,128)S(1)}, f32[3,2,1024]{2,1,0:T(2,128)S(1)}, u32[]{:S(2)}, u32[]{:S(2)}) collective-permute-start(f32[3,2,1024]{2,1,0:T(2,128)S(1)} %get-tuple-element.63), channel_id=1, source_target_pairs={{0,3},{1,2},{2,1},{3,0},{4,7},{5,6},{6,5},{7,4},{8,11},{9,10},{10,... | collective-permute-start | bytes 73736 | tf_op jit(solution)/shard_map/ppermute | solution.py:31
  127.2 5.9 %collective-permute-start.20 = (f32[3,2,1024]{2,1,0:T(2,128)S(1)}, f32[3,2,1024]{2,1,0:T(2,128)S(1)}, u32[]{:S(2)}, u32[]{:S(2)}) collective-permute-start(f32[3,2,1024]{2,1,0:T(2,128)S(1)} %get-tuple-element.64), channel_id=1, source_target_pairs={{0,2},{1,3},{2,0},{3,1},{4,6},{5,7},{6,4},{7,5},{8,10},{9,11},{10,... | collective-permute-start | bytes 73736 | tf_op jit(solution)/shard_map/ppermute | solution.py:31
  129.3 4.1 %collective-permute-start.19 = (f32[3,2,1024]{2,1,0:T(2,128)S(1)}, f32[3,2,1024]{2,1,0:T(2,128)S(1)}, u32[]{:S(2)}, u32[]{:S(2)}) collective-permute-start(f32[3,2,1024]{2,1,0:T(2,128)S(1)} %get-tuple-element.65), channel_id=1, source_target_pairs={{0,1},{1,0},{2,3},{3,2},{4,5},{5,4},{6,7},{7,6},{8,9},{9,8},{10,11... | collective-permute-start | bytes 73736 | tf_op jit(solution)/shard_map/ppermute | solution.py:31
  136.0 13.3 %collective-permute-start.27 = (bf16[256,1024]{1,0:T(8,128)(2,1)S(1)}, bf16[256,1024]{1,0:T(8,128)(2,1)S(1)}, u32[]{:S(2)}, u32[]{:S(2)}) collective-permute-start(bf16[256,1024]{1,0:T(8,128)(2,1)S(1)} %feed_far.1), channel_id=1, source_target_pairs={{0,1},{1,0},{2,3},{3,2},{4,5},{5,4},{6,7},{7,6},{8,9},{9,8},{10,11... | collective-permute-start | bytes 1572872 | tf_op jit(solution)/shard_map/ppermute | solution.py:31
  (10 other events, 123.7 us)

commit v9 on v6

--- a/solution.py
+++ b/solution.py
@@ -44,7 +44,7 @@
 def project_kernel(place_ref, weight_ref, *refs):
     shards, (query_ref, keyval_ref, top_ref, bottom_ref, rows_ref, sems) = refs[:-6], refs[-6:]
     kv = place_ref[1]
-    count = shards[0].shape[0]
+    count = top_ref.shape[0]
     steps = (len(shards) - 1) // 2
     width = weight_ref.shape[2]
     moves = [(shards[0], kv, None)]
@@ -439,16 +439,10 @@
     )(slots, filled, queries, kv_cache)
 
 
-def gathered_queries(dec_query):
-    flips = range(1, lax.axis_size("kv"))
-    return [dec_query] + [swapped(dec_query, "kv", flip) for flip in flips]
-
-
-def decode_partial(queries, kv_cache, piece_req, piece_used):
-    own = queries[0].shape[0]
+def decode_partial(queries, own, kv_cache, piece_req, piece_used):
     owners = piece_req[0]
     slots = ((owners // own) ^ lax.axis_index("kv")) * own + owners % own
-    return decode(slots, piece_used[0], jnp.concatenate(queries).astype(F32), kv_cache)
+    return decode(slots, piece_used[0], queries, kv_cache)
 
 
 def exchanged_partials(partial, own):
@@ -489,50 +483,54 @@
     place = jnp.stack([tok, kv]).astype(jnp.int32)
     eighth = lambda value: lax.dynamic_slice_in_dim(value, tok * (value.shape[0] // toks), value.shape[0] // toks, 0)
 
-    queries = gathered_queries(dec_query)
-    partial = decode_partial(queries, kv_cache, piece_req, piece_used)
-    early = {2: queries[1:], 3: [partial]}
+    out_part = eighth(out_weight)
+    depth = out_part.shape[0]
+    small = jnp.concatenate([out_part, dec_query], axis=0)
+    others = [swapped(small, "kv", flip) for flip in range(1, kvs)]
+    queries = jnp.concatenate([dec_query] + [other[depth:] for other in others], axis=0).astype(F32)
+    partial = decode_partial(queries, dec_query.shape[0], kv_cache, piece_req, piece_used)
+    out_here = jnp.stack([other[:depth] for other in others])
+    out_x, out_y = swapped(out_here, "tok", 2), swapped(out_here, "tok", 4)
+    out_all = jnp.stack([out_here, out_x, out_y, swapped(out_y, "tok", 2)])
+    out_core = swapped(out_all, "tok", 1)
+
+    met = jnp.sum(out_core[0, 0].astype(F32))
+    beside = {1: others, 2: [partial], 3: [met]}
     from_below, from_above = [], []
     rising = falling = hidden_in
     for step in range(1, kvs):
-        rising, falling = after(rising, *early.get(step, ())), after(falling, *early.get(step, ()))
+        rising, falling = after(rising, *beside.get(step, ())), after(falling, *beside.get(step, ()))
         links = range(step - 1, kvs - 1)
         rising = lax.ppermute(rising, "kv", [(i, i + 1) for i in links])
         falling = lax.ppermute(falling, "kv", [(kvs - 1 - i, kvs - 2 - i) for i in links])
         from_below.append(rising)
         from_above.append(falling)
 
-    feed_part = jnp.concatenate([eighth(up_weight), eighth(down_weight), eighth(out_weight)], axis=0)
-    feed_inner = lax.ppermute(after(feed_part, from_below[1], from_above[1], partial), "kv", [(0, 2), (3, 1)])
-    feed_outer = lax.ppermute(after(feed_part, rising, falling, feed_inner), "kv", [(1, 3), (2, 0)])
-    out_part = after(eighth(out_weight), rising, falling)
-    out_near, out_far = swapped(out_part, "kv", 1), swapped(out_part, "kv", 3)
+    feed_up, feed_down = after((eighth(up_weight), eighth(down_weight)), from_below[1], from_above[1])
+    inner_up = lax.ppermute(feed_up, "kv", [(0, 2), (3, 1)])
+    inner_down = lax.ppermute(feed_down, "kv", [(0, 2), (3, 1)])
+    feed_part = after(jnp.concatenate([feed_up, feed_down], axis=0), rising, falling, inner_up, inner_down)
+    feed_outer = lax.ppermute(feed_part, "kv", [(1, 3), (2, 0)])
+    feed_inner = jnp.concatenate([inner_up, inner_down], axis=0)
 
     order = jnp.arange(stretch_len.shape[0])
     ends = jnp.sum(jnp.where(order[:, None] <= order[None, :], stretch_len[:, None], 0), axis=0, dtype=jnp.int32)
     starts = (ends - stretch_len)[None, :]
     ends = ends[None, :]
 
-    shards = [after(hidden_in, feed_inner)] + from_below + from_above
+    shards = [hidden_in] + from_below + from_above
     query, keyval, top, bottom = project(place, jnp.transpose(qkv_weight, (1, 0, 2)), shards)
     before = lax.ppermute(bottom, "tok", [(i, i + 1) for i in range(toks - 1)])
     behind = lax.ppermute(top, "tok", [(i + 1, i) for i in range(toks - 1)])
     window = (place, starts, ends, query, before, keyval, behind, rows)
     parts = [None] * kvs
     parts[3], parts[2] = attend_blocks(*window, (3, 2), "attend_far")
-    depth = out_part.shape[0]
+    window = (place, starts, ends, after(query, parts[3]), before, keyval, behind, rows)
+    parts[3], parts[2] = swapped(parts[3], "kv", 3), swapped(parts[2], "kv", 2)
+    parts[1], parts[0] = attend_blocks(*window, (1, 0), "attend_near")
     inner = (kv == 1) | (kv == 2)
-    feed_here = jnp.where(inner, feed_inner, after(feed_outer, parts[3], parts[2]))
-    out_here = jnp.stack([out_near, feed_here[-depth:], out_far])
-    feed_here = feed_here[:-depth]
-    parts[3], parts[2] = swapped(parts[3], "kv", 3), swapped(parts[2], "kv", 2)
-    out_x, out_y = swapped(out_here, "tok", 2), swapped(out_here, "tok", 4)
-    window = (place, starts, ends, after(query, out_here), before, keyval, behind, rows)
-    parts[1], parts[0] = attend_blocks(*window, (1, 0), "attend_near")
-    feed_here = after(feed_here, parts[0])
+    feed_here = jnp.where(inner, feed_inner, after(feed_outer, *parts[2:], parts[0]))
     parts[1] = swapped(parts[1], "kv", 1)
-    out_all = jnp.stack([out_here, out_x, out_y, swapped(after(out_y, parts[0], parts[3], parts[2]), "tok", 2)])
-    out_core = swapped(out_all, "tok", 1)
     feed_x, feed_y = swapped(feed_here, "tok", 2), swapped(feed_here, "tok", 4)
     out_pieces = [((0, 2, 4, 6), out_all), ((1, 3, 5, 7), out_core)]
     normed = first_norm(place, hidden_in, out_weight, ln1_gain[None, :], ln1_bias[None, :], parts, out_pieces)

time: 150 us -> 163 us (1.087)
  local copies, waits for them, and re-layouts: 4.13 us -> 10.7 us
  starting transfers between devices: 54.2 us -> 58.7 us
  Pallas kernels: 29 us -> 31.4 us
  waiting for transfers between devices: 58.3 us -> 55.9 us
    ppermute x22 -> x20, waiting for transfers between devices: 41 us -> 28.2 us  [swapped(): return lax.ppermute(value, axis, [(i, i ^ flip) for i in range(count)])]
    ppermute x2 -> x3, waiting for transfers between devices: 0.01 us -> 8.07 us  [the longest x1 4.58 us: routed_body(): inner_up = lax.ppermute(feed_up, 'kv', [(0, 2), (3, 1)])]
    unnamed x38 -> x57, local copies, waits for them, and re-layouts: 2.08 us -> 8.62 us
    ppermute x2 -> x3, starting transfers between devices: 3.92 us -> 8.26 us  [the longest x1 5.66 us: routed_body(): inner_up = lax.ppermute(feed_up, 'kv', [(0, 2), (3, 1)])]
    ppermute x1, waiting for transfers between devices: 0.01 us -> 2.77 us  [routed_body(): behind = lax.ppermute(top, 'tok', [(i + 1, i) for i in range(toks - 1)])]
    ppermute x22 -> x20, starting transfers between devices: 37.4 us -> 37.7 us  [swapped(): return lax.ppermute(value, axis, [(i, i ^ flip) for i in range(count)])]
  transfers between devices with their start and end apart: 32 -> 31, of which waited for: 15 -> 16; matrix products, arithmetic and copies ran while one was open for 3% -> 2% of each run, Pallas kernels for 17% -> 17%
where the time goes in v9:
time: 163 us; the launch traced here: 162 us
  starting transfers between devices  58.7 us (36%)
  waiting for transfers between devices  55.9 us (34%)
  Pallas kernels  31.4 us (19%)
  local copies, waits for them, and re-layouts  10.7 us (7%)
  other arithmetic  3.97 us (2%)
    ppermute x20, starting transfers between devices, swapped(): return lax.ppermute(value, axis, [(i, i ^ flip) for i in range(count)])  37.7 us
    ppermute x20, waiting for transfers between devices, swapped(): return lax.ppermute(value, axis, [(i, i ^ flip) for i in range(count)])  28.2 us
    ppermute x3, waiting for transfers between devices, routed_body(): lax.ppermute(falling, 'kv', [(kvs - 1 - i, kvs - 2 - i) for i in links])  16.3 us
    pallas_call x2, Pallas kernels, attend_blocks(): pl.pallas_call(functools.partial(attend_kernel, flips), out_shape=tuple((...  10.9 us
    unnamed x57, local copies, waits for them, and re-layouts  8.62 us
    ppermute x3, starting transfers between devices, routed_body(): rising = lax.ppermute(rising, 'kv', [(i, i + 1) for i in links])  6.25 us
    ppermute x1, starting transfers between devices, routed_body(): inner_up = lax.ppermute(feed_up, 'kv', [(0, 2), (3, 1)])  5.66 us
    ppermute x1, waiting for transfers between devices, routed_body(): inner_up = lax.ppermute(feed_up, 'kv', [(0, 2), (3, 1)])  4.58 us
  transfers between devices with their start and end apart: 31, of which 16 were waited for; matrix products, arithmetic and copies ran while one was open for 2% of the time, Pallas kernels for 17%

profile of v9, /device:TPU:0, one launch (start us, length us, event | category | flops | bytes accessed | tf_op | source)
XLA Modules:
  0.0 161.9 jit_solution(12185873143693674531)
XLA Ops:
  2.2 5.0 %collective-permute-start.2 = (bf16[34,1024]{1,0:T(8,128)(2,1)S(1)}, bf16[34,1024]{1,0:T(8,128)(2,1)S(1)}, u32[]{:S(2)}, u32[]{:S(2)}) collective-permute-start(bf16[34,1024]{1,0:T(8,128)(2,1)S(1)} %pad_maximum_fusion.3), channel_id=1, source_target_pairs={{0,3},{1,2},{2,1},{3,0},{4,7},{5,6},{6,5},{7,4},{8,11},{9,10},{10,... | collective-permute-start | bytes 208904 | tf_op jit(solution)/shard_map/ppermute | solution.py:31
  7.9 2.7 %collective-permute-done.2 = bf16[34,1024]{1,0:T(8,128)(2,1)S(1)} collective-permute-done((bf16[34,1024]{1,0:T(8,128)(2,1)S(1)}, bf16[34,1024]{1,0:T(8,128)(2,1)S(1)}, u32[]{:S(2)}, u32[]{:S(2)}) %collective-permute-start.2) | collective-permute-done | bytes 69664 | tf_op jit(solution)/shard_map/ppermute | solution.py:31
  10.6 2.7 %collective-permute-done.1 = bf16[34,1024]{1,0:T(8,128)(2,1)S(1)} collective-permute-done((bf16[34,1024]{1,0:T(8,128)(2,1)S(1)}, bf16[34,1024]{1,0:T(8,128)(2,1)S(1)}, u32[]{:S(2)}, u32[]{:S(2)}) %collective-permute-start.1) | collective-permute-done | bytes 69664 | tf_op jit(solution)/shard_map/ppermute | solution.py:31
  17.7 2.6 %collective-permute-done.6 = bf16[3,32,1024]{2,1,0:T(8,128)(2,1)S(1)} collective-permute-done((bf16[3,32,1024]{2,1,0:T(8,128)(2,1)S(1)}, bf16[3,32,1024]{2,1,0:T(8,128)(2,1)S(1)}, u32[]{:S(2)}, u32[]{:S(2)}) %collective-permute-start.6) | collective-permute-done | bytes 196640 | tf_op jit(solution)/shard_map/ppermute | solution.py:31
  21.9 3.3 %collective-permute-start.3 = (bf16[256,1024]{1,0:T(8,128)(2,1)}, bf16[256,1024]{1,0:T(8,128)(2,1)S(1)}, u32[]{:S(2)}, u32[]{:S(2)}) collective-permute-start(bf16[256,1024]{1,0:T(8,128)(2,1)} %hidden_ref.1), channel_id=1, source_target_pairs={{0,1},{1,2},{2,3},{4,5},{5,6},{6,7},{8,9},{9,10},{10,11},{12,13},{... | collective-permute-start | bytes 1572872 | tf_op jit(solution)/shard_map/ppermute | solution.py:504
  26.9 2.3 %copy-done.2 = bf16[2,1,6,128,1024]{4,3,2,1,0:T(8,128)(2,1)S(1)} copy-done((bf16[2,1,6,128,1024]{4,3,2,1,0:T(8,128)(2,1)S(1)}, bf16[2,1,6,128,1024]{4,3,2,1,0:T(8,128)(2,1)}, u32[]{:S(2)}) %copy-start.2) | copy-done | bytes 3145752
  29.2 3.8 %decode.1 = f32[3,8,1024]{2,1,0:T(8,128)S(1)} custom-call(s32[6]{0:T(128)S(1)} %fusion.12.slot_ref, s32[6]{0:T(128)S(1)} %bitcast.150, f32[8,1024]{1,0:T(8,128)S(1)} %maximum_convert_fusion.query_ref, bf16[2,1,6,128,1024]{4,3,2,1,0:T(8,128)(2,1)S(1)} %copy-done.2), custom_call_target="tpu_custom_call" | custom-call | flops 1 | bytes 1 | tf_op jit(solution)/shard_map/decode/pallas_call | solution.py:424
  35.0 3.2 %collective-permute-done.10.refs_4_ = bf16[256,1024]{1,0:T(8,128)(2,1)} collective-permute-done((bf16[256,1024]{1,0:T(8,128)(2,1)}, bf16[256,1024]{1,0:T(8,128)(2,1)}, u32[]{:S(2)}, u32[]{:S(2)}) %collective-permute-start.10) | collective-permute-done | bytes 524320 | tf_op jit(solution)/shard_map/ppermute | solution.py:505
  41.0 13.1 %collective-permute-done.11.refs_5_ = bf16[256,1024]{1,0:T(8,128)(2,1)} collective-permute-done((bf16[256,1024]{1,0:T(8,128)(2,1)}, bf16[256,1024]{1,0:T(8,128)(2,1)}, u32[]{:S(2)}, u32[]{:S(2)}) %collective-permute-start.11) | collective-permute-done | bytes 524320 | tf_op jit(solution)/shard_map/ppermute | solution.py:505
  56.5 5.7 %collective-permute-start.19 = (bf16[128,1024]{1,0:T(8,128)(2,1)S(1)}, bf16[128,1024]{1,0:T(8,128)(2,1)S(1)}, u32[]{:S(2)}, u32[]{:S(2)}) collective-permute-start(bf16[128,1024]{1,0:T(8,128)(2,1)S(1)} %get-tuple-element.43), channel_id=1, source_target_pairs={{0,2},{3,1},{4,6},{7,5},{8,10},{11,9},{12,14},{15,13},{16,18},{19,... | collective-permute-start | bytes 786440 | tf_op jit(solution)/shard_map/ppermute | solution.py:510
  64.3 4.6 %collective-permute-done.19 = bf16[128,1024]{1,0:T(8,128)(2,1)S(1)} collective-permute-done((bf16[128,1024]{1,0:T(8,128)(2,1)S(1)}, bf16[128,1024]{1,0:T(8,128)(2,1)S(1)}, u32[]{:S(2)}, u32[]{:S(2)}) %collective-permute-start.19) | collective-permute-done | bytes 262176 | tf_op jit(solution)/shard_map/ppermute | solution.py:510
  68.9 3.5 %collective-permute-done.20 = bf16[128,1024]{1,0:T(8,128)(2,1)S(1)} collective-permute-done((bf16[128,1024]{1,0:T(8,128)(2,1)S(1)}, bf16[128,1024]{1,0:T(8,128)(2,1)S(1)}, u32[]{:S(2)}, u32[]{:S(2)}) %collective-permute-start.20) | collective-permute-done | bytes 262176 | tf_op jit(solution)/shard_map/ppermute | solution.py:511
  75.9 3.8 %project.1 = (bf16[1024,256]{1,0:T(8,128)(2,1)S(1)}, bf16[1024,512]{1,0:T(8,128)(2,1)S(1)}, bf16[256,512]{1,0:T(8,128)(2,1)S(1)}, bf16[256,512]{1,0:T(8,128)(2,1)S(1)}) custom-call(s32[2]{0:T(128)S(1)} %pad_add_fusion.place_ref, bf16[3,1024,256]{2,1,0:T(8,128)(2,1)S(1)} %bitcast.143, bf16[256,1024]{1,0:T(8,128)(2,1)S(1)} %copy-done.7, ...), custom_call_target="tpu_custom_call" | custom-call | flops 1 | bytes 1 | tf_op jit(solution)/shard_map/project/pallas_call | solution.py:85
  82.4 2.8 %collective-permute-done.14.behind_ref = bf16[256,512]{1,0:T(8,128)(2,1)S(1)} collective-permute-done((bf16[256,512]{1,0:T(8,128)(2,1)S(1)}, bf16[256,512]{1,0:T(8,128)(2,1)S(1)}, u32[]{:S(2)}, u32[]{:S(2)}) %collective-permute-start.14) | collective-permute-done | bytes 262176 | tf_op jit(solution)/shard_map/ppermute | solution.py:524
  85.2 5.7 %attend_far.1 = (bf16[256,256]{1,0:T(8,128)(2,1)}, bf16[256,256]{1,0:T(8,128)(2,1)}) custom-call(s32[2]{0:T(128)S(1)} %pad_add_fusion.place_ref, s32[1,48]{1,0:T(1,128)S(1)} %subtract_bitcast_fusion.starts_ref, s32[1,48]{1,0:T(1,128)S(1)} %bitcast.148, bf16[1024,256]{1,0:T(8,128)(2,1)S(1)} %get-tuple-element.39.query_ref, ...), custom_call_target="tpu_custom_call" | custom-call | flops 1 | bytes 1 | tf_op jit(solution)/shard_map/attend_far/pallas_call | solution.py:174
  91.7 4.2 %collective-permute-start.16 = (bf16[256,256]{1,0:T(8,128)(2,1)}, bf16[256,256]{1,0:T(8,128)(2,1)}, u32[]{:S(2)}, u32[]{:S(2)}) collective-permute-start(bf16[256,256]{1,0:T(8,128)(2,1)} %get-tuple-element.42), channel_id=1, source_target_pairs={{0,2},{1,3},{2,0},{3,1},{4,6},{5,7},{6,4},{7,5},{8,10},{9,11},{10,... | collective-permute-start | bytes 393224 | tf_op jit(solution)/shard_map/ppermute | solution.py:31
  99.1 5.2 %attend_near.1 = (bf16[256,256]{1,0:T(8,128)(2,1)S(1)}, bf16[256,256]{1,0:T(8,128)(2,1)S(1)}) custom-call(s32[2]{0:T(128)S(1)} %pad_add_fusion.place_ref, s32[1,48]{1,0:T(1,128)S(1)} %subtract_bitcast_fusion.starts_ref, s32[1,48]{1,0:T(1,128)S(1)} %bitcast.149, bf16[1024,256]{1,0:T(8,128)(2,1)S(1)} %copy-done.6, ...), custom_call_target="tpu_custom_call" | custom-call | flops 1 | bytes 1 | tf_op jit(solution)/shard_map/attend_near/pallas_call | solution.py:174
  105.8 8.2 %collective-permute-start.23 = (bf16[256,1024]{1,0:T(8,128)(2,1)S(1)}, bf16[256,1024]{1,0:T(8,128)(2,1)S(1)}, u32[]{:S(2)}, u32[]{:S(2)}) collective-permute-start(bf16[256,1024]{1,0:T(8,128)(2,1)S(1)} %get-tuple-element.57), channel_id=1, source_target_pairs={{0,16},{4,20},{8,24},{12,28},{16,0},{20,4},{24,8},{28,12},{1,17},{... | collective-permute-start | bytes 1572872 | tf_op jit(solution)/shard_map/ppermute | solution.py:31
  114.0 2.5 %collective-permute-start.15 = (bf16[256,256]{1,0:T(8,128)(2,1)S(1)}, bf16[256,256]{1,0:T(8,128)(2,1)S(1)}, u32[]{:S(2)}, u32[]{:S(2)}) collective-permute-start(bf16[256,256]{1,0:T(8,128)(2,1)S(1)} %get-tuple-element.41), channel_id=1, source_target_pairs={{0,1},{1,0},{2,3},{3,2},{4,5},{5,4},{6,7},{7,6},{8,9},{9,8},{10,11... | collective-permute-start | bytes 393224 | tf_op jit(solution)/shard_map/ppermute | solution.py:31
  116.5 3.2 %collective-permute-done.15.refs_1_ = bf16[256,256]{1,0:T(8,128)(2,1)S(1)} collective-permute-done((bf16[256,256]{1,0:T(8,128)(2,1)S(1)}, bf16[256,256]{1,0:T(8,128)(2,1)S(1)}, u32[]{:S(2)}, u32[]{:S(2)}) %collective-permute-start.15) | collective-permute-done | bytes 131104 | tf_op jit(solution)/shard_map/ppermute | solution.py:31
  119.7 3.7 %first_norm.1.rows_ref.normed_ref = bf16[256,1024]{1,0:T(8,128)(2,1)S(1)} custom-call(s32[2]{0:T(128)S(1)} %pad_add_fusion.place_ref, bf16[256,1024]{1,0:T(8,128)(2,1)S(1)} %copy-done.8, bf16[256,1024]{1,0:T(8,128)(2,1)S(1)} %copy-done.12, f32[1,1024]{1,0:T(1,128)S(1)} %bitcast.146, f32[1,1024]{1,0:T(1,128)S(1)} %bitcast.147, ...), custom_call_target="tpu_custom_call" | custom-call | flops 1 | bytes 1 | tf_op jit(solution)/shard_map/first_norm/pallas_call | solution.py:222
  123.4 1.9 %collective-permute-start.18 = (bf16[256,1024]{1,0:T(8,128)(2,1)S(1)}, bf16[256,1024]{1,0:T(8,128)(2,1)S(1)}, u32[]{:S(2)}, u32[]{:S(2)}) collective-permute-start(bf16[256,1024]{1,0:T(8,128)(2,1)S(1)} %first_norm.1.rows_ref.normed_ref), channel_id=1, source_target_pairs={{0,1},{1,0},{2,3},{3,2},{4,5},{5,4},{6,7},{7,6},{8,9},{9,8},{10,11... | collective-permute-start | bytes 1572872 | tf_op jit(solution)/shard_map/ppermute | solution.py:31
  125.3 2.1 %collective-permute-start.24 = (bf16[128,1024]{1,0:T(8,128)(2,1)S(1)}, bf16[128,1024]{1,0:T(8,128)(2,1)S(1)}, u32[]{:S(2)}, u32[]{:S(2)}) collective-permute-start(bf16[128,1024]{1,0:T(8,128)(2,1)S(1)} %slice.86), channel_id=1, source_target_pairs={{0,8},{4,12},{8,0},{12,4},{16,24},{20,28},{24,16},{28,20},{1,9},{5... | collective-permute-start | bytes 786440 | tf_op jit(solution)/shard_map/ppermute | solution.py:31
  128.3 5.0 %collective-permute-done.24 = bf16[128,1024]{1,0:T(8,128)(2,1)S(1)} collective-permute-done((bf16[128,1024]{1,0:T(8,128)(2,1)S(1)}, bf16[128,1024]{1,0:T(8,128)(2,1)S(1)}, u32[]{:S(2)}, u32[]{:S(2)}) %collective-permute-start.24) | collective-permute-done | bytes 262176 | tf_op jit(solution)/shard_map/ppermute | solution.py:31
  137.7 2.7 %collective-permute-done.26.core_ref = bf16[1024,1024]{1,0:T(8,128)(2,1)S(1)} collective-permute-done((bf16[1024,1024]{1,0:T(8,128)(2,1)S(1)}, bf16[1024,1024]{1,0:T(8,128)(2,1)S(1)}, u32[]{:S(2)}, u32[]{:S(2)}) %collective-permute-start.26) | collective-permute-done | bytes 2097184 | tf_op jit(solution)/shard_map/ppermute | solution.py:31
  140.4 2.6 %feed_far.1 = bf16[256,1024]{1,0:T(8,128)(2,1)S(1)} custom-call(s32[2]{0:T(128)S(1)} %pad_add_fusion.place_ref, bf16[256,1024]{1,0:T(8,128)(2,1)S(1)} %collective-permute-done.18.rows_ref, f32[256,1024]{1,0:T(8,128)S(1)} %feed_near.1.near_ref, bf16[1024,1024]{1,0:T(8,128)(2,1)S(1)} %constant_dynamic-update-slice_fusion.held_ref, ...), custom_call_target="tpu_custom_call" | custom-call | flops 1 | bytes 1 | tf_op jit(solution)/shard_map/feed_far/pallas_call | solution.py:330
  143.0 2.1 %collective-permute-start.27 = (bf16[256,1024]{1,0:T(8,128)(2,1)S(1)}, bf16[256,1024]{1,0:T(8,128)(2,1)S(1)}, u32[]{:S(2)}, u32[]{:S(2)}) collective-permute-start(bf16[256,1024]{1,0:T(8,128)(2,1)S(1)} %feed_far.1), channel_id=1, source_target_pairs={{0,1},{1,0},{2,3},{3,2},{4,5},{5,4},{6,7},{7,6},{8,9},{9,8},{10,11... | collective-permute-start | bytes 1572872 | tf_op jit(solution)/shard_map/ppermute | solution.py:31
  145.2 1.9 %collective-permute-start.29 = (f32[3,2,1024]{2,1,0:T(2,128)S(1)}, f32[3,2,1024]{2,1,0:T(2,128)S(1)}, u32[]{:S(2)}, u32[]{:S(2)}) collective-permute-start(f32[3,2,1024]{2,1,0:T(2,128)S(1)} %get-tuple-element.61), channel_id=1, source_target_pairs={{0,2},{1,3},{2,0},{3,1},{4,6},{5,7},{6,4},{7,5},{8,10},{9,11},{10,... | collective-permute-start | bytes 73736 | tf_op jit(solution)/shard_map/ppermute | solution.py:31
  147.1 2.5 %collective-permute-start.30 = (f32[3,2,1024]{2,1,0:T(2,128)S(1)}, f32[3,2,1024]{2,1,0:T(2,128)S(1)}, u32[]{:S(2)}, u32[]{:S(2)}) collective-permute-start(f32[3,2,1024]{2,1,0:T(2,128)S(1)} %get-tuple-element.60), channel_id=1, source_target_pairs={{0,3},{1,2},{2,1},{3,0},{4,7},{5,6},{6,5},{7,4},{8,11},{9,10},{10,... | collective-permute-start | bytes 73736 | tf_op jit(solution)/shard_map/ppermute | solution.py:31
  149.6 3.9 %feed_own.1.near_ref = f32[256,1024]{1,0:T(8,128)S(1)} custom-call(s32[2]{0:T(128)S(1)} %pad_add_fusion.place_ref, bf16[256,1024]{1,0:T(8,128)(2,1)S(1)} %first_norm.1.rows_ref.normed_ref, bf16[1024,1024]{1,0:T(8,128)(2,1)S(1)} %copy-done, bf16[1024,1024]{1,0:T(8,128)(2,1)S(1)} %copy-done.1, ...), custom_call_target="tpu_custom_call" | custom-call | flops 1 | bytes 1 | tf_op jit(solution)/shard_map/feed_own/pallas_call | solution.py:347
  153.5 4.9 %collective-permute-done.28 = f32[3,2,1024]{2,1,0:T(2,128)S(1)} collective-permute-done((f32[3,2,1024]{2,1,0:T(2,128)S(1)}, f32[3,2,1024]{2,1,0:T(2,128)S(1)}, u32[]{:S(2)}, u32[]{:S(2)}) %collective-permute-start.28) | collective-permute-done | bytes 24608 | tf_op jit(solution)/shard_map/ppermute | solution.py:31
  158.3 1.6 collective-permute-done.30
  (121 shorter events, 37.9 us)
Async XLA Ops:
  2.2 8.4 %collective-permute-start.2 = (bf16[34,1024]{1,0:T(8,128)(2,1)S(1)}, bf16[34,1024]{1,0:T(8,128)(2,1)S(1)}, u32[]{:S(2)}, u32[]{:S(2)}) collective-permute-start(bf16[34,1024]{1,0:T(8,128)(2,1)S(1)} %pad_maximum_fusion.3), channel_id=1, source_target_pairs={{0,3},{1,2},{2,1},{3,0},{4,7},{5,6},{6,5},{7,4},{8,11},{9,10},{10,... | collective-permute-start | bytes 208904 | tf_op jit(solution)/shard_map/ppermute | solution.py:31
  7.3 6.7 %collective-permute-start = (bf16[34,1024]{1,0:T(8,128)(2,1)S(1)}, bf16[34,1024]{1,0:T(8,128)(2,1)S(1)}, u32[]{:S(2)}, u32[]{:S(2)}) collective-permute-start(bf16[34,1024]{1,0:T(8,128)(2,1)S(1)} %pad_maximum_fusion.3), channel_id=1, source_target_pairs={{0,1},{1,0},{2,3},{3,2},{4,5},{5,4},{6,7},{7,6},{8,9},{9,8},{10,11... | collective-permute-start | bytes 208904 | tf_op jit(solution)/shard_map/ppermute | solution.py:31
  7.3 6.0 %collective-permute-start.1 = (bf16[34,1024]{1,0:T(8,128)(2,1)S(1)}, bf16[34,1024]{1,0:T(8,128)(2,1)S(1)}, u32[]{:S(2)}, u32[]{:S(2)}) collective-permute-start(bf16[34,1024]{1,0:T(8,128)(2,1)S(1)} %pad_maximum_fusion.3), channel_id=1, source_target_pairs={{0,2},{1,3},{2,0},{3,1},{4,6},{5,7},{6,4},{7,5},{8,10},{9,11},{10,... | collective-permute-start | bytes 208904 | tf_op jit(solution)/shard_map/ppermute | solution.py:31
  14.6 5.7 %collective-permute-start.6 = (bf16[3,32,1024]{2,1,0:T(8,128)(2,1)S(1)}, bf16[3,32,1024]{2,1,0:T(8,128)(2,1)S(1)}, u32[]{:S(2)}, u32[]{:S(2)}) collective-permute-start(bf16[3,32,1024]{2,1,0:T(8,128)(2,1)S(1)} %get-tuple-element.59), channel_id=1, source_target_pairs={{0,16},{4,20},{8,24},{12,28},{16,0},{20,4},{24,8},{28,12},{1,17},{... | collective-permute-start | bytes 589832 | tf_op jit(solution)/shard_map/ppermute | solution.py:31
  16.2 10.3 %collective-permute-start.5 = (bf16[3,32,1024]{2,1,0:T(8,128)(2,1)S(1)}, bf16[3,32,1024]{2,1,0:T(8,128)(2,1)S(1)}, u32[]{:S(2)}, u32[]{:S(2)}) collective-permute-start(bf16[3,32,1024]{2,1,0:T(8,128)(2,1)S(1)} %get-tuple-element.59), channel_id=1, source_target_pairs={{0,8},{4,12},{8,0},{12,4},{16,24},{20,28},{24,16},{28,20},{1,9},{5... | collective-permute-start | bytes 589832 | tf_op jit(solution)/shard_map/ppermute | solution.py:31
  20.4 6.1 %collective-permute-start.7 = (bf16[3,32,1024]{2,1,0:T(8,128)(2,1)S(1)}, bf16[3,32,1024]{2,1,0:T(8,128)(2,1)S(1)}, u32[]{:S(2)}, u32[]{:S(2)}) collective-permute-start(bf16[3,32,1024]{2,1,0:T(8,128)(2,1)S(1)} %collective-permute-done.6), channel_id=1, source_target_pairs={{0,8},{4,12},{8,0},{12,4},{16,24},{20,28},{24,16},{28,20},{1,9},{5... | collective-permute-start | bytes 589832 | tf_op jit(solution)/shard_map/ppermute | solution.py:31
  21.9 11.6 %collective-permute-start.3 = (bf16[256,1024]{1,0:T(8,128)(2,1)}, bf16[256,1024]{1,0:T(8,128)(2,1)S(1)}, u32[]{:S(2)}, u32[]{:S(2)}) collective-permute-start(bf16[256,1024]{1,0:T(8,128)(2,1)} %hidden_ref.1), channel_id=1, source_target_pairs={{0,1},{1,2},{2,3},{4,5},{5,6},{6,7},{8,9},{9,10},{10,11},{12,13},{... | collective-permute-start | bytes 1572872 | tf_op jit(solution)/shard_map/ppermute | solution.py:504
  25.2 13.0 %collective-permute-start.10 = (bf16[256,1024]{1,0:T(8,128)(2,1)}, bf16[256,1024]{1,0:T(8,128)(2,1)}, u32[]{:S(2)}, u32[]{:S(2)}) collective-permute-start(bf16[256,1024]{1,0:T(8,128)(2,1)} %hidden_ref.1), channel_id=1, source_target_pairs={{3,2},{2,1},{1,0},{7,6},{6,5},{5,4},{11,10},{10,9},{9,8},{15,14},{... | collective-permute-start | bytes 1572872 | tf_op jit(solution)/shard_map/ppermute | solution.py:505
  26.6 12.8 %collective-permute-start.8 = (bf16[4,3,32,1024]{3,2,1,0:T(8,128)(2,1)S(1)}, bf16[4,3,32,1024]{3,2,1,0:T(8,128)(2,1)}, u32[]{:S(2)}, u32[]{:S(2)}) collective-permute-start(bf16[4,3,32,1024]{3,2,1,0:T(8,128)(2,1)S(1)} %pad_maximum_fusion.refs_4_), channel_id=1, source_target_pairs={{0,4},{4,0},{8,12},{12,8},{16,20},{20,16},{24,28},{28,24},{1,5},{5... | collective-permute-start | bytes 2359304 | tf_op jit(solution)/shard_map/ppermute | solution.py:31
  33.5 40.3 %copy-start.13 = (bf16[256,1024]{1,0:T(8,128)(2,1)}, bf16[256,1024]{1,0:T(8,128)(2,1)S(1)}, u32[]{:S(2)}) copy-start(bf16[256,1024]{1,0:T(8,128)(2,1)S(1)} %collective-permute-done.3.refs_1_) | copy-start | bytes 1572868
  33.5 5.9 %collective-permute-start.4 = (bf16[256,1024]{1,0:T(8,128)(2,1)S(1)}, bf16[256,1024]{1,0:T(8,128)(2,1)}, u32[]{:S(2)}, u32[]{:S(2)}) collective-permute-start(bf16[256,1024]{1,0:T(8,128)(2,1)S(1)} %collective-permute-done.3.refs_1_), channel_id=1, source_target_pairs={{1,2},{2,3},{5,6},{6,7},{9,10},{10,11},{13,14},{14,15},{17,18},{18... | collective-permute-start | bytes 1572872 | tf_op jit(solution)/shard_map/ppermute | solution.py:504
  38.2 15.9 %collective-permute-start.11 = (bf16[256,1024]{1,0:T(8,128)(2,1)}, bf16[256,1024]{1,0:T(8,128)(2,1)}, u32[]{:S(2)}, u32[]{:S(2)}) collective-permute-start(bf16[256,1024]{1,0:T(8,128)(2,1)} %collective-permute-done.10.refs_4_), channel_id=1, source_target_pairs={{2,1},{1,0},{6,5},{5,4},{10,9},{9,8},{14,13},{13,12},{18,17},{17,1... | collective-permute-start | bytes 1572872 | tf_op jit(solution)/shard_map/ppermute | solution.py:505
  39.5 33.0 %collective-permute-start.9 = (bf16[256,1024]{1,0:T(8,128)(2,1)}, bf16[256,1024]{1,0:T(8,128)(2,1)}, u32[]{:S(2)}, u32[]{:S(2)}) collective-permute-start(bf16[256,1024]{1,0:T(8,128)(2,1)} %collective-permute-done.4.refs_2_), channel_id=1, source_target_pairs={{2,3},{6,7},{10,11},{14,15},{18,19},{22,23},{26,27},{30,31}} | collective-permute-start | bytes 1572872 | tf_op jit(solution)/shard_map/ppermute | solution.py:504
  54.1 18.3 %collective-permute-start.12 = (bf16[256,1024]{1,0:T(8,128)(2,1)}, bf16[256,1024]{1,0:T(8,128)(2,1)}, u32[]{:S(2)}, u32[]{:S(2)}) collective-permute-start(bf16[256,1024]{1,0:T(8,128)(2,1)} %collective-permute-done.11.refs_5_), channel_id=1, source_target_pairs={{1,0},{5,4},{9,8},{13,12},{17,16},{21,20},{25,24},{29,28}} | collective-permute-start | bytes 1572872 | tf_op jit(solution)/shard_map/ppermute | solution.py:505
  56.5 12.4 %collective-permute-start.19 = (bf16[128,1024]{1,0:T(8,128)(2,1)S(1)}, bf16[128,1024]{1,0:T(8,128)(2,1)S(1)}, u32[]{:S(2)}, u32[]{:S(2)}) collective-permute-start(bf16[128,1024]{1,0:T(8,128)(2,1)S(1)} %get-tuple-element.43), channel_id=1, source_target_pairs={{0,2},{3,1},{4,6},{7,5},{8,10},{11,9},{12,14},{15,13},{16,18},{19,... | collective-permute-start | bytes 786440 | tf_op jit(solution)/shard_map/ppermute | solution.py:510
  62.2 10.2 %collective-permute-start.20 = (bf16[128,1024]{1,0:T(8,128)(2,1)S(1)}, bf16[128,1024]{1,0:T(8,128)(2,1)S(1)}, u32[]{:S(2)}, u32[]{:S(2)}) collective-permute-start(bf16[128,1024]{1,0:T(8,128)(2,1)S(1)} %get-tuple-element.44), channel_id=1, source_target_pairs={{0,2},{3,1},{4,6},{7,5},{8,10},{11,9},{12,14},{15,13},{16,18},{19,... | collective-permute-start | bytes 786440 | tf_op jit(solution)/shard_map/ppermute | solution.py:511
  72.4 31.9 %collective-permute-start.21 = (bf16[256,1024]{1,0:T(8,128)(2,1)}, bf16[256,1024]{1,0:T(8,128)(2,1)}, u32[]{:S(2)}, u32[]{:S(2)}) collective-permute-start(bf16[256,1024]{1,0:T(8,128)(2,1)} %pad_maximum_fusion.1), channel_id=1, source_target_pairs={{1,3},{2,0},{5,7},{6,4},{9,11},{10,8},{13,15},{14,12},{17,19},{18,... | collective-permute-start | bytes 1572872 | tf_op jit(solution)/shard_map/ppermute | solution.py:513
  79.7 2.7 %collective-permute-start.13 = (bf16[256,512]{1,0:T(8,128)(2,1)S(1)}, bf16[256,512]{1,0:T(8,128)(2,1)S(1)}, u32[]{:S(2)}, u32[]{:S(2)}) collective-permute-start(bf16[256,512]{1,0:T(8,128)(2,1)S(1)} %get-tuple-element.35), channel_id=1, source_target_pairs={{0,4},{4,8},{8,12},{12,16},{16,20},{20,24},{24,28},{1,5},{5,9},{9,... | collective-permute-start | bytes 786440 | tf_op jit(solution)/shard_map/ppermute | solution.py:523
  81.0 4.2 %collective-permute-start.14 = (bf16[256,512]{1,0:T(8,128)(2,1)S(1)}, bf16[256,512]{1,0:T(8,128)(2,1)S(1)}, u32[]{:S(2)}, u32[]{:S(2)}) collective-permute-start(bf16[256,512]{1,0:T(8,128)(2,1)S(1)} %get-tuple-element.37), channel_id=1, source_target_pairs={{4,0},{8,4},{12,8},{16,12},{20,16},{24,20},{28,24},{5,1},{9,5},{13... | collective-permute-start | bytes 786440 | tf_op jit(solution)/shard_map/ppermute | solution.py:524
  91.7 12.6 %collective-permute-start.16 = (bf16[256,256]{1,0:T(8,128)(2,1)}, bf16[256,256]{1,0:T(8,128)(2,1)}, u32[]{:S(2)}, u32[]{:S(2)}) collective-permute-start(bf16[256,256]{1,0:T(8,128)(2,1)} %get-tuple-element.42), channel_id=1, source_target_pairs={{0,2},{1,3},{2,0},{3,1},{4,6},{5,7},{6,4},{7,5},{8,10},{9,11},{10,... | collective-permute-start | bytes 393224 | tf_op jit(solution)/shard_map/ppermute | solution.py:31
  95.9 8.4 %collective-permute-start.17 = (bf16[256,256]{1,0:T(8,128)(2,1)}, bf16[256,256]{1,0:T(8,128)(2,1)}, u32[]{:S(2)}, u32[]{:S(2)}) collective-permute-start(bf16[256,256]{1,0:T(8,128)(2,1)} %get-tuple-element.38), channel_id=1, source_target_pairs={{0,3},{1,2},{2,1},{3,0},{4,7},{5,6},{6,5},{7,4},{8,11},{9,10},{10,... | collective-permute-start | bytes 393224 | tf_op jit(solution)/shard_map/ppermute | solution.py:31
  105.8 19.5 %collective-permute-start.23 = (bf16[256,1024]{1,0:T(8,128)(2,1)S(1)}, bf16[256,1024]{1,0:T(8,128)(2,1)S(1)}, u32[]{:S(2)}, u32[]{:S(2)}) collective-permute-start(bf16[256,1024]{1,0:T(8,128)(2,1)S(1)} %get-tuple-element.57), channel_id=1, source_target_pairs={{0,16},{4,20},{8,24},{12,28},{16,0},{20,4},{24,8},{28,12},{1,17},{... | collective-permute-start | bytes 1572872 | tf_op jit(solution)/shard_map/ppermute | solution.py:31
  114.0 13.3 %collective-permute-start.22 = (bf16[256,1024]{1,0:T(8,128)(2,1)S(1)}, bf16[256,1024]{1,0:T(8,128)(2,1)S(1)}, u32[]{:S(2)}, u32[]{:S(2)}) collective-permute-start(bf16[256,1024]{1,0:T(8,128)(2,1)S(1)} %get-tuple-element.57), channel_id=1, source_target_pairs={{0,8},{4,12},{8,0},{12,4},{16,24},{20,28},{24,16},{28,20},{1,9},{5... | collective-permute-start | bytes 1572872 | tf_op jit(solution)/shard_map/ppermute | solution.py:31
  114.0 5.7 %collective-permute-start.15 = (bf16[256,256]{1,0:T(8,128)(2,1)S(1)}, bf16[256,256]{1,0:T(8,128)(2,1)S(1)}, u32[]{:S(2)}, u32[]{:S(2)}) collective-permute-start(bf16[256,256]{1,0:T(8,128)(2,1)S(1)} %get-tuple-element.41), channel_id=1, source_target_pairs={{0,1},{1,0},{2,3},{3,2},{4,5},{5,4},{6,7},{7,6},{8,9},{9,8},{10,11... | collective-permute-start | bytes 393224 | tf_op jit(solution)/shard_map/ppermute | solution.py:31
  123.4 12.8 %collective-permute-start.18 = (bf16[256,1024]{1,0:T(8,128)(2,1)S(1)}, bf16[256,1024]{1,0:T(8,128)(2,1)S(1)}, u32[]{:S(2)}, u32[]{:S(2)}) collective-permute-start(bf16[256,1024]{1,0:T(8,128)(2,1)S(1)} %first_norm.1.rows_ref.normed_ref), channel_id=1, source_target_pairs={{0,1},{1,0},{2,3},{3,2},{4,5},{5,4},{6,7},{7,6},{8,9},{9,8},{10,11... | collective-permute-start | bytes 1572872 | tf_op jit(solution)/shard_map/ppermute | solution.py:31
  125.3 8.1 %collective-permute-start.24 = (bf16[128,1024]{1,0:T(8,128)(2,1)S(1)}, bf16[128,1024]{1,0:T(8,128)(2,1)S(1)}, u32[]{:S(2)}, u32[]{:S(2)}) collective-permute-start(bf16[128,1024]{1,0:T(8,128)(2,1)S(1)} %slice.86), channel_id=1, source_target_pairs={{0,8},{4,12},{8,0},{12,4},{16,24},{20,28},{24,16},{28,20},{1,9},{5... | collective-permute-start | bytes 786440 | tf_op jit(solution)/shard_map/ppermute | solution.py:31
  127.4 7.5 %collective-permute-start.25 = (bf16[128,1024]{1,0:T(8,128)(2,1)S(1)}, bf16[128,1024]{1,0:T(8,128)(2,1)S(1)}, u32[]{:S(2)}, u32[]{:S(2)}) collective-permute-start(bf16[128,1024]{1,0:T(8,128)(2,1)S(1)} %slice.87), channel_id=1, source_target_pairs={{0,16},{4,20},{8,24},{12,28},{16,0},{20,4},{24,8},{28,12},{1,17},{... | collective-permute-start | bytes 786440 | tf_op jit(solution)/shard_map/ppermute | solution.py:31
  136.2 4.2 %collective-permute-start.26 = (bf16[1024,1024]{1,0:T(8,128)(2,1)S(1)}, bf16[1024,1024]{1,0:T(8,128)(2,1)S(1)}, u32[]{:S(2)}, u32[]{:S(2)}) collective-permute-start(bf16[1024,1024]{1,0:T(8,128)(2,1)S(1)} %constant_dynamic-update-slice_fusion.held_ref), channel_id=1, source_target_pairs={{0,4},{4,0},{8,12},{12,8},{16,20},{20,16},{24,28},{28,24},{1,5},{5... | collective-permute-start | bytes 6291464 | tf_op jit(solution)/shard_map/ppermute | solution.py:31
  143.0 17.6 %collective-permute-start.27 = (bf16[256,1024]{1,0:T(8,128)(2,1)S(1)}, bf16[256,1024]{1,0:T(8,128)(2,1)S(1)}, u32[]{:S(2)}, u32[]{:S(2)}) collective-permute-start(bf16[256,1024]{1,0:T(8,128)(2,1)S(1)} %feed_far.1), channel_id=1, source_target_pairs={{0,1},{1,0},{2,3},{3,2},{4,5},{5,4},{6,7},{7,6},{8,9},{9,8},{10,11... | collective-permute-start | bytes 1572872 | tf_op jit(solution)/shard_map/ppermute | solution.py:31
  145.1 13.2 %collective-permute-start.28 = (f32[3,2,1024]{2,1,0:T(2,128)S(1)}, f32[3,2,1024]{2,1,0:T(2,128)S(1)}, u32[]{:S(2)}, u32[]{:S(2)}) collective-permute-start(f32[3,2,1024]{2,1,0:T(2,128)S(1)} %get-tuple-element.62), channel_id=1, source_target_pairs={{0,1},{1,0},{2,3},{3,2},{4,5},{5,4},{6,7},{7,6},{8,9},{9,8},{10,11... | collective-permute-start | bytes 73736 | tf_op jit(solution)/shard_map/ppermute | solution.py:31
  145.2 13.2 %collective-permute-start.29 = (f32[3,2,1024]{2,1,0:T(2,128)S(1)}, f32[3,2,1024]{2,1,0:T(2,128)S(1)}, u32[]{:S(2)}, u32[]{:S(2)}) collective-permute-start(f32[3,2,1024]{2,1,0:T(2,128)S(1)} %get-tuple-element.61), channel_id=1, source_target_pairs={{0,2},{1,3},{2,0},{3,1},{4,6},{5,7},{6,4},{7,5},{8,10},{9,11},{10,... | collective-permute-start | bytes 73736 | tf_op jit(solution)/shard_map/ppermute | solution.py:31
  147.1 12.8 %collective-permute-start.30 = (f32[3,2,1024]{2,1,0:T(2,128)S(1)}, f32[3,2,1024]{2,1,0:T(2,128)S(1)}, u32[]{:S(2)}, u32[]{:S(2)}) collective-permute-start(f32[3,2,1024]{2,1,0:T(2,128)S(1)} %get-tuple-element.60), channel_id=1, source_target_pairs={{0,3},{1,2},{2,1},{3,0},{4,7},{5,6},{6,5},{7,4},{8,11},{9,10},{10,... | collective-permute-start | bytes 73736 | tf_op jit(solution)/shard_map/ppermute | solution.py:31
  (28 other events, 350.0 us)

commit v10 on v9

--- a/solution.py
+++ b/solution.py
@@ -31,6 +31,20 @@
     return lax.ppermute(value, axis, [(i, i ^ flip) for i in range(count)])
 
 
+def over_edges(value, axis, first):
+    count = lax.axis_size(axis)
+    edges = [(i, i + 1) for i in range(first, count - 1, 2)]
+    return lax.ppermute(value, axis, edges + [(j, i) for i, j in edges])
+
+
+def chain(value):
+    outward = [(1, 0), (2, 3)]
+    a1, b1 = over_edges(value, "kv", 0), over_edges(value, "kv", 1)
+    a2, b2 = lax.ppermute(b1, "kv", outward), over_edges(a1, "kv", 1)
+    a3 = lax.ppermute(b2, "kv", outward)
+    return a1, a2, a3, b1, b2
+
+
 def after(value, *earlier):
     return lax.optimization_barrier((value,) + earlier)[0]
 
@@ -42,45 +56,48 @@
 
 
 def project_kernel(place_ref, weight_ref, *refs):
-    shards, (query_ref, keyval_ref, top_ref, bottom_ref, rows_ref, sems) = refs[:-6], refs[-6:]
-    kv = place_ref[1]
-    count = top_ref.shape[0]
-    steps = (len(shards) - 1) // 2
+    shards, (query_ref, keyval_ref, even_ref, odd_ref, riders_ref, rows_ref, sems, rider_sems) = refs[:-8], refs[-8:]
+    own, a1, a2, a3, b1, b2 = shards
+    tok, kv = place_ref[0], place_ref[1]
+    count, depth = even_ref.shape[0], riders_ref.shape[1]
+    blocks = rows_ref.shape[0] // count
     width = weight_ref.shape[2]
-    moves = [(shards[0], kv, None)]
-    for step in range(1, steps + 1):
-        moves.append((shards[step], kv - step, kv >= step))
-        moves.append((shards[steps + step], kv + step, kv + step <= steps))
-
-    def guarded(needed, act):
-        if needed is None:
-            act()
-        else:
-            pl.when(needed)(act)
-
+    inner = (kv == 1) | (kv == 2)
+    outer = jnp.logical_not(inner)
     copies = []
-    for index, (source, owner, needed) in enumerate(moves):
-        safe = owner if needed is None else jnp.where(needed, owner, 0)
-        at = pl.ds(pl.multiple_of(safe * count, count), count)
-        copies.append((needed, pltpu.make_async_copy(source, rows_ref.at[at], sems.at[index])))
+    for source, flip, needed in ((own, 0, kv >= 0), (a1, 1, kv >= 0), (a2, 2, outer), (b2, 2, inner), (a3, 3, outer), (b1, 3, inner)):
+        at = pl.ds(pl.multiple_of((kv ^ flip) * count, count), count)
+        copies.append((needed, pltpu.make_async_copy(source.at[0:count], rows_ref.at[at], sems.at[len(copies)])))
+        if flip:
+            rider = source.at[count : count + depth]
+            target = riders_ref.at[flip - 1]
+            copies.append((needed, pltpu.make_async_copy(rider, target, rider_sems.at[len(copies)])))
     for needed, copy in copies:
-        guarded(needed, copy.start)
+        pl.when(needed)(copy.start)
     for needed, copy in copies:
-        guarded(needed, copy.wait)
+        pl.when(needed)(copy.wait)
     rows = rows_ref[...]
     query = jnp.dot(rows, weight_ref[0], preferred_element_type=F32) * (1.0 / math.sqrt(HD))
     query_ref[...] = query.astype(BF16)
     for part in range(2):
         at = slice(part * width, (part + 1) * width)
         keyval_ref[:, at] = jnp.dot(rows, weight_ref[part + 1], preferred_element_type=F32).astype(BF16)
-    top_ref[...] = keyval_ref[:count]
-    bottom_ref[...] = keyval_ref[steps * count :]
-
-
-def project(place, weight, shards):
+    top, bottom = slice(0, count), slice((blocks - 1) * count, blocks * count)
+
+    @pl.when(tok % 2 == 0)
+    def _():
+        even_ref[...] = keyval_ref[bottom]
+        odd_ref[...] = keyval_ref[top]
+
+    @pl.when(tok % 2 == 1)
+    def _():
+        even_ref[...] = keyval_ref[top]
+        odd_ref[...] = keyval_ref[bottom]
+
+
+def project(place, weight, shards, blocks, depth):
     rows, width = shards[0].shape
     heads_width = weight.shape[2]
-    blocks = (len(shards) + 1) // 2
     edge = jax.ShapeDtypeStruct((rows, 2 * heads_width), BF16)
     return pl.pallas_call(
         project_kernel,
@@ -89,10 +106,15 @@
             jax.ShapeDtypeStruct((blocks * rows, 2 * heads_width), BF16),
             edge,
             edge,
+            jax.ShapeDtypeStruct((blocks - 1, depth, width), BF16),
         ),
         in_specs=[SMEM, VMEM] + [ANY] * len(shards),
-        out_specs=(VMEM,) * 4,
-        scratch_shapes=[pltpu.VMEM((blocks * rows, width), BF16), pltpu.SemaphoreType.DMA((len(shards),))],
+        out_specs=(VMEM,) * 5,
+        scratch_shapes=[
+            pltpu.VMEM((blocks * rows, width), BF16),
+            pltpu.SemaphoreType.DMA((2 * len(shards),)),
+            pltpu.SemaphoreType.DMA((2 * len(shards),)),
+        ],
         compiler_params=pltpu.CompilerParams(vmem_limit_bytes=14 * MIB),
         cost_estimate=SHORT,
         name="project",
@@ -135,7 +157,7 @@
         out_ref[:, start : start + 2 * HD] = jnp.where(lane < HD, halves[0], halves[1]).astype(BF16)
 
 
-def attend_kernel(flips, place_ref, starts_ref, ends_ref, query_ref, before_ref, keyval_ref, behind_ref, *refs):
+def attend_kernel(flips, place_ref, starts_ref, ends_ref, query_ref, keyval_ref, even_ref, odd_ref, *refs):
     outs = refs[: len(flips)]
     window_ref, bias_ref, scores_ref, weights_ref, sems = refs[len(flips) :]
     tok, kv = place_ref[0], place_ref[1]
@@ -152,10 +174,11 @@
             safe = jnp.where(inner, at, 0)
             source = keyval_ref.at[pl.ds(pl.multiple_of(safe * count, count), count)]
             copies.append((index, inner, pltpu.make_async_copy(source, target, sem)))
-            if part == 0:
-                copies.append((index, at < 0, pltpu.make_async_copy(before_ref, target, sem)))
-            if part == 2:
-                copies.append((index, at >= blocks, pltpu.make_async_copy(behind_ref, target, sem)))
+            for first_edge, outside in ((tok % 2 == 1, at < 0), (tok % 2 == 0, at >= blocks)):
+                if part != 1:
+                    copies.append((index, outside & first_edge, pltpu.make_async_copy(even_ref, target, sem)))
+                    other = jnp.logical_not(first_edge)
+                    copies.append((index, outside & other, pltpu.make_async_copy(odd_ref, target, sem)))
     for _, needed, copy in copies:
         pl.when(needed)(copy.start)
     for index, flip in enumerate(flips):
@@ -169,7 +192,7 @@
         attend(query, window_ref.at[index], bias_ref, scores_ref, weights_ref, outs[index])
 
 
-def attend_blocks(place, starts, ends, query, before, keyval, behind, rows, flips, name):
+def attend_blocks(place, starts, ends, query, keyval, even, odd, rows, flips, name):
     heads_width = query.shape[1]
     return pl.pallas_call(
         functools.partial(attend_kernel, flips),
@@ -186,7 +209,7 @@
         compiler_params=pltpu.CompilerParams(vmem_limit_bytes=14 * MIB),
         cost_estimate=SHORT,
         name=name,
-    )(place, starts, ends, query, before, keyval, behind)
+    )(place, starts, ends, query, keyval, even, odd)
 
 
 def first_norm_kernel(layout, place_ref, hidden_ref, own_out_ref, gain_ref, bias_ref, *refs):
@@ -485,31 +508,14 @@
 
     out_part = eighth(out_weight)
     depth = out_part.shape[0]
-    small = jnp.concatenate([out_part, dec_query], axis=0)
-    others = [swapped(small, "kv", flip) for flip in range(1, kvs)]
-    queries = jnp.concatenate([dec_query] + [other[depth:] for other in others], axis=0).astype(F32)
-    partial = decode_partial(queries, dec_query.shape[0], kv_cache, piece_req, piece_used)
-    out_here = jnp.stack([other[:depth] for other in others])
-    out_x, out_y = swapped(out_here, "tok", 2), swapped(out_here, "tok", 4)
-    out_all = jnp.stack([out_here, out_x, out_y, swapped(out_y, "tok", 2)])
-    out_core = swapped(out_all, "tok", 1)
-
-    met = jnp.sum(out_core[0, 0].astype(F32))
-    beside = {1: others, 2: [partial], 3: [met]}
-    from_below, from_above = [], []
-    rising = falling = hidden_in
-    for step in range(1, kvs):
-        rising, falling = after(rising, *beside.get(step, ())), after(falling, *beside.get(step, ()))
-        links = range(step - 1, kvs - 1)
-        rising = lax.ppermute(rising, "kv", [(i, i + 1) for i in links])
-        falling = lax.ppermute(falling, "kv", [(kvs - 1 - i, kvs - 2 - i) for i in links])
-        from_below.append(rising)
-        from_above.append(falling)
-
-    feed_up, feed_down = after((eighth(up_weight), eighth(down_weight)), from_below[1], from_above[1])
+    shards = chain(jnp.concatenate([hidden_in, out_part, dec_query], axis=0))
+    a1, a2, a3, b1, b2 = shards
+    inner = (kv == 1) | (kv == 2)
+
+    feed_up, feed_down = after((eighth(up_weight), eighth(down_weight)), a2, b2)
     inner_up = lax.ppermute(feed_up, "kv", [(0, 2), (3, 1)])
     inner_down = lax.ppermute(feed_down, "kv", [(0, 2), (3, 1)])
-    feed_part = after(jnp.concatenate([feed_up, feed_down], axis=0), rising, falling, inner_up, inner_down)
+    feed_part = after(jnp.concatenate([feed_up, feed_down], axis=0), a3, inner_up, inner_down)
     feed_outer = lax.ppermute(feed_part, "kv", [(1, 3), (2, 0)])
     feed_inner = jnp.concatenate([inner_up, inner_down], axis=0)
 
@@ -518,17 +524,19 @@
     starts = (ends - stretch_len)[None, :]
     ends = ends[None, :]
 
-    shards = [hidden_in] + from_below + from_above
-    query, keyval, top, bottom = project(place, jnp.transpose(qkv_weight, (1, 0, 2)), shards)
-    before = lax.ppermute(bottom, "tok", [(i, i + 1) for i in range(toks - 1)])
-    behind = lax.ppermute(top, "tok", [(i + 1, i) for i in range(toks - 1)])
-    window = (place, starts, ends, query, before, keyval, behind, rows)
+    weight = jnp.transpose(qkv_weight, (1, 0, 2))
+    query, keyval, even, odd, out_here = project(place, weight, (hidden_in,) + shards, kvs, depth)
+    even, odd = over_edges(even, "tok", 0), over_edges(odd, "tok", 1)
+    window = (place, starts, ends, query, keyval, even, odd, rows)
     parts = [None] * kvs
     parts[3], parts[2] = attend_blocks(*window, (3, 2), "attend_far")
-    window = (place, starts, ends, after(query, parts[3]), before, keyval, behind, rows)
+    out_here = after(out_here, parts[3])
+    out_all = [out_here] + [swapped(out_here, "tok", flip) for flip in (2, 4, 6)]
+    window = (place, starts, ends, after(query, parts[3]), keyval, even, odd, rows)
     parts[3], parts[2] = swapped(parts[3], "kv", 3), swapped(parts[2], "kv", 2)
     parts[1], parts[0] = attend_blocks(*window, (1, 0), "attend_near")
-    inner = (kv == 1) | (kv == 2)
+    out_all = after(jnp.stack(out_all), parts[0])
+    out_core = swapped(out_all, "tok", 1)
     feed_here = jnp.where(inner, feed_inner, after(feed_outer, *parts[2:], parts[0]))
     parts[1] = swapped(parts[1], "kv", 1)
     feed_x, feed_y = swapped(feed_here, "tok", 2), swapped(feed_here, "tok", 4)
@@ -539,7 +547,11 @@
     half = feed_here.shape[0] // 2
     far_up = swapped(after(feed_y, normed)[:half], "tok", 2)
     far_down = swapped(after(feed_x, normed)[half:], "tok", 4)
-    held = jnp.concatenate([feed_here, feed_x, feed_y, far_up, far_down], axis=0)
+    ends_of = lambda outer_one, inner_one: jnp.where(inner, inner_one[rows + depth :], outer_one[rows + depth :])
+    queries = [dec_query, a1[rows + depth :], ends_of(a2, b2), ends_of(a3, b1)]
+    queries = after(jnp.concatenate(queries, axis=0).astype(F32), normed)
+    partial = decode_partial(queries, dec_query.shape[0], kv_cache, piece_req, piece_used)
+    held = jnp.concatenate([feed_here, feed_x, feed_y, after(far_up, partial), far_down], axis=0)
     near_away = feed_near(partner, up_weight, down_weight)
     feed_pieces = (held, swapped(after(held, partner), "tok", 1))
     away = feed_far(place, partner, near_away, feed_pieces)

time: 163 us -> 148 us (0.908)
  starting transfers between devices: 58.7 us -> 36 us
  waiting for transfers between devices: 55.9 us -> 61.9 us
  other arithmetic: 3.97 us -> 6.76 us
  Pallas kernels: 31.4 us -> 29.3 us
  local copies, waits for them, and re-layouts: 10.7 us -> 12.5 us
    ppermute x8 -> x7, waiting for transfers between devices: 19.6 us -> 36.1 us  [the longest x1 16.1 us: chain(): a2, b2 = (lax.ppermute(b1, 'kv', outward), over_edges(a1, 'kv', 1))]
    ppermute x20 -> x17, starting transfers between devices: 37.7 us -> 23.4 us  [swapped(): return lax.ppermute(value, axis, [(i, i ^ flip) for i in range(count)])]
    ppermute x8 -> x7, starting transfers between devices: 12.7 us -> 7.79 us  [the longest x5 5.21 us: over_edges(): return lax.ppermute(value, axis, edges + [(j, i) for i, j in edges])]
    ppermute x1, waiting for transfers between devices: 4.58 us -> 0.01 us  [routed_body(): inner_up = lax.ppermute(feed_up, 'kv', [(0, 2), (3, 1)])]
    ppermute x1, waiting for transfers between devices: 3.49 us -> 0.01 us  [routed_body(): inner_down = lax.ppermute(feed_down, 'kv', [(0, 2), (3, 1)])]
    ppermute x1, starting transfers between devices: 5.66 us -> 2.18 us  [routed_body(): inner_up = lax.ppermute(feed_up, 'kv', [(0, 2), (3, 1)])]
    ppermute x20 -> x17, waiting for transfers between devices: 28.2 us -> 25.8 us  [swapped(): return lax.ppermute(value, axis, [(i, i ^ flip) for i in range(count)])]
    unnamed x57 -> x61, local copies, waits for them, and re-layouts: 8.62 us -> 9.67 us
  transfers between devices with their start and end apart: 31 -> 27, of which waited for: 16 -> 14; matrix products, arithmetic and copies ran while one was open for 2% -> 5% of each run, Pallas kernels for 17% -> 17%
where the time goes in v10:
time: 148 us; the launch traced here: 147 us
  waiting for transfers between devices  61.9 us (42%)
  starting transfers between devices  36 us (24%)
  Pallas kernels  29.3 us (20%)
  local copies, waits for them, and re-layouts  12.5 us (8%)
  other arithmetic  6.76 us (5%)
    ppermute x17, waiting for transfers between devices, swapped(): return lax.ppermute(value, axis, [(i, i ^ flip) for i in range(count)])  25.8 us
    ppermute x17, starting transfers between devices, swapped(): return lax.ppermute(value, axis, [(i, i ^ flip) for i in range(count)])  23.4 us
    ppermute x1, waiting for transfers between devices, chain(): a2, b2 = (lax.ppermute(b1, 'kv', outward), over_edges(a1, 'kv', 1))  16.1 us
    ppermute x5, waiting for transfers between devices, over_edges(): return lax.ppermute(value, axis, edges + [(j, i) for i, j in edges])  13 us
    pallas_call x2, Pallas kernels, attend_blocks(): pl.pallas_call(functools.partial(attend_kernel, flips), out_shape=tuple((...  10.5 us
    unnamed x61, local copies, waits for them, and re-layouts  9.67 us
    ppermute x1, waiting for transfers between devices, chain(): a3 = lax.ppermute(b2, 'kv', outward)  7.02 us
    ppermute x5, starting transfers between devices, over_edges(): return lax.ppermute(value, axis, edges + [(j, i) for i, j in edges])  5.21 us
  transfers between devices with their start and end apart: 27, of which 14 were waited for; matrix products, arithmetic and copies ran while one was open for 5% of the time, Pallas kernels for 17%

profile of v10, /device:TPU:0, one launch (start us, length us, event | category | flops | bytes accessed | tf_op | source)
XLA Modules:
  0.0 147.5 jit_solution(3633778555395368734)
XLA Ops:
  2.7 3.1 %collective-permute-start = (bf16[290,1024]{1,0:T(8,128)(2,1)S(1)}, bf16[290,1024]{1,0:T(8,128)(2,1)S(1)}, u32[]{:S(2)}, u32[]{:S(2)}) collective-permute-start(bf16[290,1024]{1,0:T(8,128)(2,1)S(1)} %pad_maximum_fusion.1), channel_id=1, source_target_pairs={{0,1},{2,3},{1,0},{3,2},{4,5},{6,7},{5,4},{7,6},{8,9},{10,11},{9,8... | collective-permute-start | bytes 1781768 | tf_op jit(solution)/shard_map/ppermute | solution.py:37
  6.5 13.0 %collective-permute-done.refs_1_ = bf16[290,1024]{1,0:T(8,128)(2,1)S(1)} collective-permute-done((bf16[290,1024]{1,0:T(8,128)(2,1)S(1)}, bf16[290,1024]{1,0:T(8,128)(2,1)S(1)}, u32[]{:S(2)}, u32[]{:S(2)}) %collective-permute-start) | collective-permute-done | bytes 593952 | tf_op jit(solution)/shard_map/ppermute | solution.py:37
  21.0 1.3 collective-permute-start.2
  22.3 1.3 collective-permute-start.4
  24.7 16.1 %collective-permute-done.2.refs_2_ = bf16[290,1024]{1,0:T(8,128)(2,1)S(1)} collective-permute-done((bf16[290,1024]{1,0:T(8,128)(2,1)S(1)}, bf16[290,1024]{1,0:T(8,128)(2,1)S(1)}, u32[]{:S(2)}, u32[]{:S(2)}) %collective-permute-start.2) | collective-permute-done | bytes 593952 | tf_op jit(solution)/shard_map/ppermute | solution.py:43
  41.6 2.2 %collective-permute-start.15 = (bf16[128,1024]{1,0:T(8,128)(2,1)S(1)}, bf16[128,1024]{1,0:T(8,128)(2,1)S(1)}, u32[]{:S(2)}, u32[]{:S(2)}) collective-permute-start(bf16[128,1024]{1,0:T(8,128)(2,1)S(1)} %get-tuple-element.41), channel_id=1, source_target_pairs={{0,2},{3,1},{4,6},{7,5},{8,10},{11,9},{12,14},{15,13},{16,18},{19,... | collective-permute-start | bytes 786440 | tf_op jit(solution)/shard_map/ppermute | solution.py:516
  43.8 1.3 collective-permute-start.16
  45.3 7.0 %collective-permute-done.4.refs_3_ = bf16[290,1024]{1,0:T(8,128)(2,1)S(1)} collective-permute-done((bf16[290,1024]{1,0:T(8,128)(2,1)S(1)}, bf16[290,1024]{1,0:T(8,128)(2,1)S(1)}, u32[]{:S(2)}, u32[]{:S(2)}) %collective-permute-start.4) | collective-permute-done | bytes 593952 | tf_op jit(solution)/shard_map/ppermute | solution.py:44
  53.1 1.4 copy-done.4
  58.8 3.0 %project.1 = (bf16[1024,256]{1,0:T(8,128)(2,1)S(1)}, bf16[1024,512]{1,0:T(8,128)(2,1)S(1)}, bf16[256,512]{1,0:T(8,128)(2,1)S(1)}, bf16[256,512]{1,0:T(8,128)(2,1)S(1)}, bf16[3,32,1024]{2,1,0:T(8,128)(2,1)S(1)}) custom-call(s32[2]{0:T(128)S(1)} %pad_add_fusion.place_ref, bf16[3,1024,256]{2,1,0:T(8,128)(2,1)S(1)} %bitcast.136, ...), custom_call_target="tpu_custom_call" | custom-call | flops 1 | bytes 1 | tf_op jit(solution)/shard_map/project/pallas_call | solution.py:102
  63.4 1.3 collective-permute-start.17
  64.8 5.2 %attend_far.1 = (bf16[256,256]{1,0:T(8,128)(2,1)S(1)}, bf16[256,256]{1,0:T(8,128)(2,1)S(1)}) custom-call(s32[2]{0:T(128)S(1)} %pad_add_fusion.place_ref, s32[1,48]{1,0:T(1,128)S(1)} %subtract_bitcast_fusion.starts_ref, s32[1,48]{1,0:T(1,128)S(1)} %bitcast.142, bf16[1024,256]{1,0:T(8,128)(2,1)S(1)} %get-tuple-element.34.query_ref, ...), custom_call_target="tpu_custom_call" | custom-call | flops 1 | bytes 1 | tf_op jit(solution)/shard_map/attend_far/pallas_call | solution.py:197
  71.3 9.5 %collective-permute-start.12 = (bf16[3,32,1024]{2,1,0:T(8,128)(2,1)S(1)}, bf16[3,32,1024]{2,1,0:T(8,128)(2,1)}, u32[]{:S(2)}, u32[]{:S(2)}) collective-permute-start(bf16[3,32,1024]{2,1,0:T(8,128)(2,1)S(1)} %get-tuple-element.39), channel_id=1, source_target_pairs={{0,24},{4,28},{8,16},{12,20},{16,8},{20,12},{24,0},{28,4},{1,25},{... | collective-permute-start | bytes 589832 | tf_op jit(solution)/shard_map/ppermute | solution.py:31
  81.0 1.5 %collective-permute-start.10 = (bf16[3,32,1024]{2,1,0:T(8,128)(2,1)S(1)}, bf16[3,32,1024]{2,1,0:T(8,128)(2,1)}, u32[]{:S(2)}, u32[]{:S(2)}) collective-permute-start(bf16[3,32,1024]{2,1,0:T(8,128)(2,1)S(1)} %get-tuple-element.39), channel_id=1, source_target_pairs={{0,8},{4,12},{8,0},{12,4},{16,24},{20,28},{24,16},{28,20},{1,9},{5... | collective-permute-start | bytes 589832 | tf_op jit(solution)/shard_map/ppermute | solution.py:31
  82.6 1.9 %collective-permute-start.9 = (bf16[256,256]{1,0:T(8,128)(2,1)}, bf16[256,256]{1,0:T(8,128)(2,1)S(1)}, u32[]{:S(2)}, u32[]{:S(2)}) collective-permute-start(bf16[256,256]{1,0:T(8,128)(2,1)} %copy-done.19), channel_id=1, source_target_pairs={{0,3},{1,2},{2,1},{3,0},{4,7},{5,6},{6,5},{7,4},{8,11},{9,10},{10,... | collective-permute-start | bytes 393224 | tf_op jit(solution)/shard_map/ppermute | solution.py:31
  84.5 5.4 %attend_near.1 = (bf16[256,256]{1,0:T(8,128)(2,1)S(1)}, bf16[256,256]{1,0:T(8,128)(2,1)S(1)}) custom-call(s32[2]{0:T(128)S(1)} %pad_add_fusion.place_ref, s32[1,48]{1,0:T(1,128)S(1)} %subtract_bitcast_fusion.starts_ref, s32[1,48]{1,0:T(1,128)S(1)} %bitcast.143, bf16[1024,256]{1,0:T(8,128)(2,1)S(1)} %get-tuple-element.34.query_ref, ...), custom_call_target="tpu_custom_call" | custom-call | flops 1 | bytes 1 | tf_op jit(solution)/shard_map/attend_near/pallas_call | solution.py:197
  92.3 5.8 %collective-permute-done.8.refs_2_ = bf16[256,256]{1,0:T(8,128)(2,1)S(1)} collective-permute-done((bf16[256,256]{1,0:T(8,128)(2,1)S(1)}, bf16[256,256]{1,0:T(8,128)(2,1)S(1)}, u32[]{:S(2)}, u32[]{:S(2)}) %collective-permute-start.8) | collective-permute-done | bytes 131104 | tf_op jit(solution)/shard_map/ppermute | solution.py:31
  98.1 1.3 constant_dynamic-update-slice_fusion.4
  100.7 1.5 %collective-permute-start.18 = (bf16[256,1024]{1,0:T(8,128)(2,1)S(1)}, bf16[256,1024]{1,0:T(8,128)(2,1)S(1)}, u32[]{:S(2)}, u32[]{:S(2)}) collective-permute-start(bf16[256,1024]{1,0:T(8,128)(2,1)S(1)} %get-tuple-element.57), channel_id=1, source_target_pairs={{0,8},{4,12},{8,0},{12,4},{16,24},{20,28},{24,16},{28,20},{1,9},{5... | collective-permute-start | bytes 1572872 | tf_op jit(solution)/shard_map/ppermute | solution.py:31
  103.8 4.2 %collective-permute-done.7.refs_1_ = bf16[256,256]{1,0:T(8,128)(2,1)S(1)} collective-permute-done((bf16[256,256]{1,0:T(8,128)(2,1)S(1)}, bf16[256,256]{1,0:T(8,128)(2,1)S(1)}, u32[]{:S(2)}, u32[]{:S(2)}) %collective-permute-start.7) | collective-permute-done | bytes 131104 | tf_op jit(solution)/shard_map/ppermute | solution.py:31
  108.0 2.6 %first_norm.1.rows_ref.normed_ref = bf16[256,1024]{1,0:T(8,128)(2,1)S(1)} custom-call(s32[2]{0:T(128)S(1)} %pad_add_fusion.place_ref, bf16[256,1024]{1,0:T(8,128)(2,1)S(1)} %copy-done.2, bf16[256,1024]{1,0:T(8,128)(2,1)S(1)} %copy-done.5, f32[1,1024]{1,0:T(1,128)S(1)} %bitcast.140, f32[1,1024]{1,0:T(1,128)S(1)} %bitcast.141, ...), custom_call_target="tpu_custom_call" | custom-call | flops 1 | bytes 1 | tf_op jit(solution)/shard_map/first_norm/pallas_call | solution.py:245
  110.9 2.4 %collective-permute-done.19 = bf16[256,1024]{1,0:T(8,128)(2,1)S(1)} collective-permute-done((bf16[256,1024]{1,0:T(8,128)(2,1)S(1)}, bf16[256,1024]{1,0:T(8,128)(2,1)S(1)}, u32[]{:S(2)}, u32[]{:S(2)}) %collective-permute-start.19) | collective-permute-done | bytes 524320 | tf_op jit(solution)/shard_map/ppermute | solution.py:31
  113.3 1.7 %collective-permute-start.20 = (bf16[128,1024]{1,0:T(8,128)(2,1)S(1)}, bf16[128,1024]{1,0:T(8,128)(2,1)S(1)}, u32[]{:S(2)}, u32[]{:S(2)}) collective-permute-start(bf16[128,1024]{1,0:T(8,128)(2,1)S(1)} %slice.73), channel_id=1, source_target_pairs={{0,8},{4,12},{8,0},{12,4},{16,24},{20,28},{24,16},{28,20},{1,9},{5... | collective-permute-start | bytes 786440 | tf_op jit(solution)/shard_map/ppermute | solution.py:31
  116.3 3.8 %decode.1 = f32[3,8,1024]{2,1,0:T(8,128)S(1)} custom-call(s32[6]{0:T(128)S(1)} %fusion.12.slot_ref, s32[6]{0:T(128)S(1)} %bitcast.144, f32[8,1024]{1,0:T(8,128)S(1)} %maximum_convert_fusion.query_ref, bf16[2,1,6,128,1024]{4,3,2,1,0:T(8,128)(2,1)S(1)} %copy-done.3), custom_call_target="tpu_custom_call" | custom-call | flops 1 | bytes 1 | tf_op jit(solution)/shard_map/decode/pallas_call | solution.py:447
  120.8 1.5 %collective-permute-done.21 = bf16[128,1024]{1,0:T(8,128)(2,1)S(1)} collective-permute-done((bf16[128,1024]{1,0:T(8,128)(2,1)S(1)}, bf16[128,1024]{1,0:T(8,128)(2,1)S(1)}, u32[]{:S(2)}, u32[]{:S(2)}) %collective-permute-start.21) | collective-permute-done | bytes 262176 | tf_op jit(solution)/shard_map/ppermute | solution.py:31
  123.2 1.5 %feed_near.1.near_ref = f32[256,1024]{1,0:T(8,128)S(1)} custom-call(bf16[256,1024]{1,0:T(8,128)(2,1)S(1)} %collective-permute-done.14.rows_ref, bf16[1024,1024]{1,0:T(8,128)(2,1)S(1)} %copy-done, bf16[1024,1024]{1,0:T(8,128)(2,1)S(1)} %copy-done.1), custom_call_target="tpu_custom_call" | custom-call | flops 1 | bytes 1 | tf_op jit(solution)/shard_map/feed_near/pallas_call | solution.py:338
  124.7 2.6 %collective-permute-done.22.core_ref = bf16[1024,1024]{1,0:T(8,128)(2,1)S(1)} collective-permute-done((bf16[1024,1024]{1,0:T(8,128)(2,1)S(1)}, bf16[1024,1024]{1,0:T(8,128)(2,1)S(1)}, u32[]{:S(2)}, u32[]{:S(2)}) %collective-permute-start.22) | collective-permute-done | bytes 2097184 | tf_op jit(solution)/shard_map/ppermute | solution.py:31
  127.3 2.6 %feed_far.1 = bf16[256,1024]{1,0:T(8,128)(2,1)S(1)} custom-call(s32[2]{0:T(128)S(1)} %pad_add_fusion.place_ref, bf16[256,1024]{1,0:T(8,128)(2,1)S(1)} %collective-permute-done.14.rows_ref, f32[256,1024]{1,0:T(8,128)S(1)} %feed_near.1.near_ref, bf16[1024,1024]{1,0:T(8,128)(2,1)S(1)} %constant_dynamic-update-slice_fusion.held_ref, ...), custom_call_target="tpu_custom_call" | custom-call | flops 1 | bytes 1 | tf_op jit(solution)/shard_map/feed_far/pallas_call | solution.py:353
  130.5 1.9 %collective-permute-start.26 = (f32[3,2,1024]{2,1,0:T(2,128)S(1)}, f32[3,2,1024]{2,1,0:T(2,128)S(1)}, u32[]{:S(2)}, u32[]{:S(2)}) collective-permute-start(f32[3,2,1024]{2,1,0:T(2,128)S(1)} %get-tuple-element.58), channel_id=1, source_target_pairs={{0,3},{1,2},{2,1},{3,0},{4,7},{5,6},{6,5},{7,4},{8,11},{9,10},{10,... | collective-permute-start | bytes 73736 | tf_op jit(solution)/shard_map/ppermute | solution.py:31
  133.6 1.3 collective-permute-start.24
  134.9 3.9 %feed_own.1.near_ref = f32[256,1024]{1,0:T(8,128)S(1)} custom-call(s32[2]{0:T(128)S(1)} %pad_add_fusion.place_ref, bf16[256,1024]{1,0:T(8,128)(2,1)S(1)} %first_norm.1.rows_ref.normed_ref, bf16[1024,1024]{1,0:T(8,128)(2,1)S(1)} %copy-done, bf16[1024,1024]{1,0:T(8,128)(2,1)S(1)} %copy-done.1, ...), custom_call_target="tpu_custom_call" | custom-call | flops 1 | bytes 1 | tf_op jit(solution)/shard_map/feed_own/pallas_call | solution.py:370
  138.8 6.6 %collective-permute-done.26 = f32[3,2,1024]{2,1,0:T(2,128)S(1)} collective-permute-done((f32[3,2,1024]{2,1,0:T(2,128)S(1)}, f32[3,2,1024]{2,1,0:T(2,128)S(1)}, u32[]{:S(2)}, u32[]{:S(2)}) %collective-permute-start.26) | collective-permute-done | bytes 24608 | tf_op jit(solution)/shard_map/ppermute | solution.py:31
  (111 shorter events, 26.7 us)
Async XLA Ops:
  0.6 52.5 %copy-start.2 = (bf16[256,1024]{1,0:T(8,128)(2,1)S(1)}, bf16[256,1024]{1,0:T(8,128)(2,1)}, u32[]{:S(2)}) copy-start(bf16[256,1024]{1,0:T(8,128)(2,1)} %hidden_ref.1) | copy-start | bytes 1572868
  0.6 44.5 %copy-start.27 = (s32[48]{0:T(128)S(1)}, s32[48]{0:T(128)}, u32[]{:S(2)}) copy-start(s32[48]{0:T(128)} %param.16) | copy-start | bytes 580
  2.7 16.8 %collective-permute-start = (bf16[290,1024]{1,0:T(8,128)(2,1)S(1)}, bf16[290,1024]{1,0:T(8,128)(2,1)S(1)}, u32[]{:S(2)}, u32[]{:S(2)}) collective-permute-start(bf16[290,1024]{1,0:T(8,128)(2,1)S(1)} %pad_maximum_fusion.1), channel_id=1, source_target_pairs={{0,1},{2,3},{1,0},{3,2},{4,5},{6,7},{5,4},{7,6},{8,9},{10,11},{9,8... | collective-permute-start | bytes 1781768 | tf_op jit(solution)/shard_map/ppermute | solution.py:37
  5.8 15.2 %collective-permute-start.1 = (bf16[290,1024]{1,0:T(8,128)(2,1)S(1)}, bf16[290,1024]{1,0:T(8,128)(2,1)S(1)}, u32[]{:S(2)}, u32[]{:S(2)}) collective-permute-start(bf16[290,1024]{1,0:T(8,128)(2,1)S(1)} %pad_maximum_fusion.1), channel_id=1, source_target_pairs={{1,2},{2,1},{5,6},{6,5},{9,10},{10,9},{13,14},{14,13},{17,18},{18,... | collective-permute-start | bytes 1781768 | tf_op jit(solution)/shard_map/ppermute | solution.py:37
  19.4 2.8 %collective-permute-start.3 = (bf16[290,1024]{1,0:T(8,128)(2,1)S(1)}, bf16[290,1024]{1,0:T(8,128)(2,1)S(1)}, u32[]{:S(2)}, u32[]{:S(2)}) collective-permute-start(bf16[290,1024]{1,0:T(8,128)(2,1)S(1)} %collective-permute-done.refs_1_), channel_id=1, source_target_pairs={{1,2},{2,1},{5,6},{6,5},{9,10},{10,9},{13,14},{14,13},{17,18},{18,... | collective-permute-start | bytes 1781768 | tf_op jit(solution)/shard_map/ppermute | solution.py:37
  21.0 19.8 %collective-permute-start.2 = (bf16[290,1024]{1,0:T(8,128)(2,1)S(1)}, bf16[290,1024]{1,0:T(8,128)(2,1)S(1)}, u32[]{:S(2)}, u32[]{:S(2)}) collective-permute-start(bf16[290,1024]{1,0:T(8,128)(2,1)S(1)} %collective-permute-done.1.refs_4_), channel_id=1, source_target_pairs={{1,0},{2,3},{5,4},{6,7},{9,8},{10,11},{13,12},{14,15},{17,16},{18,... | collective-permute-start | bytes 1781768 | tf_op jit(solution)/shard_map/ppermute | solution.py:43
  22.3 30.0 %copy-start.6 = (bf16[290,1024]{1,0:T(8,128)(2,1)}, bf16[290,1024]{1,0:T(8,128)(2,1)S(1)}, u32[]{:S(2)}) copy-start(bf16[290,1024]{1,0:T(8,128)(2,1)S(1)} %collective-permute-done.3.refs_5_) | copy-start | bytes 1781764
  22.3 30.0 %collective-permute-start.4 = (bf16[290,1024]{1,0:T(8,128)(2,1)S(1)}, bf16[290,1024]{1,0:T(8,128)(2,1)S(1)}, u32[]{:S(2)}, u32[]{:S(2)}) collective-permute-start(bf16[290,1024]{1,0:T(8,128)(2,1)S(1)} %collective-permute-done.3.refs_5_), channel_id=1, source_target_pairs={{1,0},{2,3},{5,4},{6,7},{9,8},{10,11},{13,12},{14,15},{17,16},{18,... | collective-permute-start | bytes 1781768 | tf_op jit(solution)/shard_map/ppermute | solution.py:44
  41.6 21.8 %collective-permute-start.15 = (bf16[128,1024]{1,0:T(8,128)(2,1)S(1)}, bf16[128,1024]{1,0:T(8,128)(2,1)S(1)}, u32[]{:S(2)}, u32[]{:S(2)}) collective-permute-start(bf16[128,1024]{1,0:T(8,128)(2,1)S(1)} %get-tuple-element.41), channel_id=1, source_target_pairs={{0,2},{3,1},{4,6},{7,5},{8,10},{11,9},{12,14},{15,13},{16,18},{19,... | collective-permute-start | bytes 786440 | tf_op jit(solution)/shard_map/ppermute | solution.py:516
  43.8 19.6 %collective-permute-start.16 = (bf16[128,1024]{1,0:T(8,128)(2,1)S(1)}, bf16[128,1024]{1,0:T(8,128)(2,1)S(1)}, u32[]{:S(2)}, u32[]{:S(2)}) collective-permute-start(bf16[128,1024]{1,0:T(8,128)(2,1)S(1)} %get-tuple-element.42), channel_id=1, source_target_pairs={{0,2},{3,1},{4,6},{7,5},{8,10},{11,9},{12,14},{15,13},{16,18},{19,... | collective-permute-start | bytes 786440 | tf_op jit(solution)/shard_map/ppermute | solution.py:517
  61.8 2.9 %collective-permute-start.5 = (bf16[256,512]{1,0:T(8,128)(2,1)S(1)}, bf16[256,512]{1,0:T(8,128)(2,1)S(1)}, u32[]{:S(2)}, u32[]{:S(2)}) collective-permute-start(bf16[256,512]{1,0:T(8,128)(2,1)S(1)} %get-tuple-element.31), channel_id=1, source_target_pairs={{0,4},{8,12},{16,20},{24,28},{4,0},{12,8},{20,16},{28,24},{1,5},{9... | collective-permute-start | bytes 786440 | tf_op jit(solution)/shard_map/ppermute | solution.py:37
  61.9 2.9 %collective-permute-start.6 = (bf16[256,512]{1,0:T(8,128)(2,1)S(1)}, bf16[256,512]{1,0:T(8,128)(2,1)S(1)}, u32[]{:S(2)}, u32[]{:S(2)}) collective-permute-start(bf16[256,512]{1,0:T(8,128)(2,1)S(1)} %get-tuple-element.32), channel_id=1, source_target_pairs={{4,8},{12,16},{20,24},{8,4},{16,12},{24,20},{5,9},{13,17},{21,25},... | collective-permute-start | bytes 786440 | tf_op jit(solution)/shard_map/ppermute | solution.py:37
  63.4 34.6 %collective-permute-start.17 = (bf16[256,1024]{1,0:T(8,128)(2,1)}, bf16[256,1024]{1,0:T(8,128)(2,1)}, u32[]{:S(2)}, u32[]{:S(2)}) collective-permute-start(bf16[256,1024]{1,0:T(8,128)(2,1)} %pad_maximum_fusion.2), channel_id=1, source_target_pairs={{1,3},{2,0},{5,7},{6,4},{9,11},{10,8},{13,15},{14,12},{17,19},{18,... | collective-permute-start | bytes 1572872 | tf_op jit(solution)/shard_map/ppermute | solution.py:519
  71.3 18.6 %collective-permute-start.12 = (bf16[3,32,1024]{2,1,0:T(8,128)(2,1)S(1)}, bf16[3,32,1024]{2,1,0:T(8,128)(2,1)}, u32[]{:S(2)}, u32[]{:S(2)}) collective-permute-start(bf16[3,32,1024]{2,1,0:T(8,128)(2,1)S(1)} %get-tuple-element.39), channel_id=1, source_target_pairs={{0,24},{4,28},{8,16},{12,20},{16,8},{20,12},{24,0},{28,4},{1,25},{... | collective-permute-start | bytes 589832 | tf_op jit(solution)/shard_map/ppermute | solution.py:31
  80.8 10.1 %collective-permute-start.11 = (bf16[3,32,1024]{2,1,0:T(8,128)(2,1)S(1)}, bf16[3,32,1024]{2,1,0:T(8,128)(2,1)}, u32[]{:S(2)}, u32[]{:S(2)}) collective-permute-start(bf16[3,32,1024]{2,1,0:T(8,128)(2,1)S(1)} %get-tuple-element.39), channel_id=1, source_target_pairs={{0,16},{4,20},{8,24},{12,28},{16,0},{20,4},{24,8},{28,12},{1,17},{... | collective-permute-start | bytes 589832 | tf_op jit(solution)/shard_map/ppermute | solution.py:31
  81.0 9.9 %collective-permute-start.10 = (bf16[3,32,1024]{2,1,0:T(8,128)(2,1)S(1)}, bf16[3,32,1024]{2,1,0:T(8,128)(2,1)}, u32[]{:S(2)}, u32[]{:S(2)}) collective-permute-start(bf16[3,32,1024]{2,1,0:T(8,128)(2,1)S(1)} %get-tuple-element.39), channel_id=1, source_target_pairs={{0,8},{4,12},{8,0},{12,4},{16,24},{20,28},{24,16},{28,20},{1,9},{5... | collective-permute-start | bytes 589832 | tf_op jit(solution)/shard_map/ppermute | solution.py:31
  82.6 15.5 %collective-permute-start.9 = (bf16[256,256]{1,0:T(8,128)(2,1)}, bf16[256,256]{1,0:T(8,128)(2,1)S(1)}, u32[]{:S(2)}, u32[]{:S(2)}) collective-permute-start(bf16[256,256]{1,0:T(8,128)(2,1)} %copy-done.19), channel_id=1, source_target_pairs={{0,3},{1,2},{2,1},{3,0},{4,7},{5,6},{6,5},{7,4},{8,11},{9,10},{10,... | collective-permute-start | bytes 393224 | tf_op jit(solution)/shard_map/ppermute | solution.py:31
  89.8 18.2 %copy-start.5 = (bf16[256,1024]{1,0:T(8,128)(2,1)S(1)}, bf16[256,1024]{1,0:T(8,128)(2,1)}, u32[]{:S(2)}) copy-start(bf16[256,1024]{1,0:T(8,128)(2,1)} %own_out_ref.1) | copy-start | bytes 1572868
  89.8 18.1 %copy-start.16 = (f32[1024]{0:T(1024)S(1)}, f32[1024]{0:T(1024)}, u32[]{:S(2)}) copy-start(f32[1024]{0:T(1024)} %param.18) | copy-start | bytes 12292
  89.9 8.2 %collective-permute-start.8 = (bf16[256,256]{1,0:T(8,128)(2,1)S(1)}, bf16[256,256]{1,0:T(8,128)(2,1)S(1)}, u32[]{:S(2)}, u32[]{:S(2)}) collective-permute-start(bf16[256,256]{1,0:T(8,128)(2,1)S(1)} %copy-done.21), channel_id=1, source_target_pairs={{0,2},{1,3},{2,0},{3,1},{4,6},{5,7},{6,4},{7,5},{8,10},{9,11},{10,... | collective-permute-start | bytes 393224 | tf_op jit(solution)/shard_map/ppermute | solution.py:31
  92.2 15.8 %collective-permute-start.13 = (bf16[4,3,32,1024]{3,2,1,0:T(8,128)(2,1)S(1)}, bf16[4,3,32,1024]{3,2,1,0:T(8,128)(2,1)S(1)}, u32[]{:S(2)}, u32[]{:S(2)}) collective-permute-start(bf16[4,3,32,1024]{3,2,1,0:T(8,128)(2,1)S(1)} %pad_maximum_fusion.refs_4_), channel_id=1, source_target_pairs={{0,4},{4,0},{8,12},{12,8},{16,20},{20,16},{24,28},{28,24},{1,5},{5... | collective-permute-start | bytes 2359304 | tf_op jit(solution)/shard_map/ppermute | solution.py:31
  99.4 13.9 %collective-permute-start.19 = (bf16[256,1024]{1,0:T(8,128)(2,1)S(1)}, bf16[256,1024]{1,0:T(8,128)(2,1)S(1)}, u32[]{:S(2)}, u32[]{:S(2)}) collective-permute-start(bf16[256,1024]{1,0:T(8,128)(2,1)S(1)} %get-tuple-element.57), channel_id=1, source_target_pairs={{0,16},{4,20},{8,24},{12,28},{16,0},{20,4},{24,8},{28,12},{1,17},{... | collective-permute-start | bytes 1572872 | tf_op jit(solution)/shard_map/ppermute | solution.py:31
  100.7 14.3 %collective-permute-start.18 = (bf16[256,1024]{1,0:T(8,128)(2,1)S(1)}, bf16[256,1024]{1,0:T(8,128)(2,1)S(1)}, u32[]{:S(2)}, u32[]{:S(2)}) collective-permute-start(bf16[256,1024]{1,0:T(8,128)(2,1)S(1)} %get-tuple-element.57), channel_id=1, source_target_pairs={{0,8},{4,12},{8,0},{12,4},{16,24},{20,28},{24,16},{28,20},{1,9},{5... | collective-permute-start | bytes 1572872 | tf_op jit(solution)/shard_map/ppermute | solution.py:31
  103.0 5.0 %collective-permute-start.7 = (bf16[256,256]{1,0:T(8,128)(2,1)S(1)}, bf16[256,256]{1,0:T(8,128)(2,1)S(1)}, u32[]{:S(2)}, u32[]{:S(2)}) collective-permute-start(bf16[256,256]{1,0:T(8,128)(2,1)S(1)} %get-tuple-element.36), channel_id=1, source_target_pairs={{0,1},{1,0},{2,3},{3,2},{4,5},{5,4},{6,7},{7,6},{8,9},{9,8},{10,11... | collective-permute-start | bytes 393224 | tf_op jit(solution)/shard_map/ppermute | solution.py:31
  110.7 12.5 %collective-permute-start.14 = (bf16[256,1024]{1,0:T(8,128)(2,1)S(1)}, bf16[256,1024]{1,0:T(8,128)(2,1)S(1)}, u32[]{:S(2)}, u32[]{:S(2)}) collective-permute-start(bf16[256,1024]{1,0:T(8,128)(2,1)S(1)} %first_norm.1.rows_ref.normed_ref), channel_id=1, source_target_pairs={{0,1},{1,0},{2,3},{3,2},{4,5},{5,4},{6,7},{7,6},{8,9},{9,8},{10,11... | collective-permute-start | bytes 1572872 | tf_op jit(solution)/shard_map/ppermute | solution.py:31
  113.3 7.4 %collective-permute-start.20 = (bf16[128,1024]{1,0:T(8,128)(2,1)S(1)}, bf16[128,1024]{1,0:T(8,128)(2,1)S(1)}, u32[]{:S(2)}, u32[]{:S(2)}) collective-permute-start(bf16[128,1024]{1,0:T(8,128)(2,1)S(1)} %slice.73), channel_id=1, source_target_pairs={{0,8},{4,12},{8,0},{12,4},{16,24},{20,28},{24,16},{28,20},{1,9},{5... | collective-permute-start | bytes 786440 | tf_op jit(solution)/shard_map/ppermute | solution.py:31
  115.0 7.3 %collective-permute-start.21 = (bf16[128,1024]{1,0:T(8,128)(2,1)S(1)}, bf16[128,1024]{1,0:T(8,128)(2,1)S(1)}, u32[]{:S(2)}, u32[]{:S(2)}) collective-permute-start(bf16[128,1024]{1,0:T(8,128)(2,1)S(1)} %slice.79), channel_id=1, source_target_pairs={{0,16},{4,20},{8,24},{12,28},{16,0},{20,4},{24,8},{28,12},{1,17},{... | collective-permute-start | bytes 786440 | tf_op jit(solution)/shard_map/ppermute | solution.py:31
  123.2 4.2 %collective-permute-start.22 = (bf16[1024,1024]{1,0:T(8,128)(2,1)S(1)}, bf16[1024,1024]{1,0:T(8,128)(2,1)S(1)}, u32[]{:S(2)}, u32[]{:S(2)}) collective-permute-start(bf16[1024,1024]{1,0:T(8,128)(2,1)S(1)} %constant_dynamic-update-slice_fusion.held_ref), channel_id=1, source_target_pairs={{0,4},{4,0},{8,12},{12,8},{16,20},{20,16},{24,28},{28,24},{1,5},{5... | collective-permute-start | bytes 6291464 | tf_op jit(solution)/shard_map/ppermute | solution.py:31
  130.0 16.2 %collective-permute-start.23 = (bf16[256,1024]{1,0:T(8,128)(2,1)S(1)}, bf16[256,1024]{1,0:T(8,128)(2,1)S(1)}, u32[]{:S(2)}, u32[]{:S(2)}) collective-permute-start(bf16[256,1024]{1,0:T(8,128)(2,1)S(1)} %feed_far.1), channel_id=1, source_target_pairs={{0,1},{1,0},{2,3},{3,2},{4,5},{5,4},{6,7},{7,6},{8,9},{9,8},{10,11... | collective-permute-start | bytes 1572872 | tf_op jit(solution)/shard_map/ppermute | solution.py:31
  130.5 14.9 %collective-permute-start.26 = (f32[3,2,1024]{2,1,0:T(2,128)S(1)}, f32[3,2,1024]{2,1,0:T(2,128)S(1)}, u32[]{:S(2)}, u32[]{:S(2)}) collective-permute-start(f32[3,2,1024]{2,1,0:T(2,128)S(1)} %get-tuple-element.58), channel_id=1, source_target_pairs={{0,3},{1,2},{2,1},{3,0},{4,7},{5,6},{6,5},{7,4},{8,11},{9,10},{10,... | collective-permute-start | bytes 73736 | tf_op jit(solution)/shard_map/ppermute | solution.py:31
  132.4 13.0 %collective-permute-start.25 = (f32[3,2,1024]{2,1,0:T(2,128)S(1)}, f32[3,2,1024]{2,1,0:T(2,128)S(1)}, u32[]{:S(2)}, u32[]{:S(2)}) collective-permute-start(f32[3,2,1024]{2,1,0:T(2,128)S(1)} %get-tuple-element.59), channel_id=1, source_target_pairs={{0,2},{1,3},{2,0},{3,1},{4,6},{5,7},{6,4},{7,5},{8,10},{9,11},{10,... | collective-permute-start | bytes 73736 | tf_op jit(solution)/shard_map/ppermute | solution.py:31
  133.6 11.9 %collective-permute-start.24 = (f32[3,2,1024]{2,1,0:T(2,128)S(1)}, f32[3,2,1024]{2,1,0:T(2,128)S(1)}, u32[]{:S(2)}, u32[]{:S(2)}) collective-permute-start(f32[3,2,1024]{2,1,0:T(2,128)S(1)} %get-tuple-element.60), channel_id=1, source_target_pairs={{0,1},{1,0},{2,3},{3,2},{4,5},{5,4},{6,7},{7,6},{8,9},{9,8},{10,11... | collective-permute-start | bytes 73736 | tf_op jit(solution)/shard_map/ppermute | solution.py:31
  (24 other events, 168.2 us)

commit v11 on v10

--- a/solution.py
+++ b/solution.py
@@ -37,14 +37,6 @@
     return lax.ppermute(value, axis, edges + [(j, i) for i, j in edges])
 
 
-def chain(value):
-    outward = [(1, 0), (2, 3)]
-    a1, b1 = over_edges(value, "kv", 0), over_edges(value, "kv", 1)
-    a2, b2 = lax.ppermute(b1, "kv", outward), over_edges(a1, "kv", 1)
-    a3 = lax.ppermute(b2, "kv", outward)
-    return a1, a2, a3, b1, b2
-
-
 def after(value, *earlier):
     return lax.optimization_barrier((value,) + earlier)[0]
 
@@ -55,69 +47,80 @@
     return center * lax.rsqrt(spread + LN_EPS) * gain + bias
 
 
-def project_kernel(place_ref, weight_ref, *refs):
-    shards, (query_ref, keyval_ref, even_ref, odd_ref, riders_ref, rows_ref, sems, rider_sems) = refs[:-8], refs[-8:]
+def shard_copies(kv, shards, rows_ref, sems, first, step):
     own, a1, a2, a3, b1, b2 = shards
-    tok, kv = place_ref[0], place_ref[1]
-    count, depth = even_ref.shape[0], riders_ref.shape[1]
-    blocks = rows_ref.shape[0] // count
-    width = weight_ref.shape[2]
+    count = own.shape[0]
     inner = (kv == 1) | (kv == 2)
     outer = jnp.logical_not(inner)
+    always = kv >= 0
+    sources = ((own, 0, always), (a1, 1, always), (a2, 2, outer), (b2, 2, inner), (a3, 3, outer), (b1, 3, inner))
     copies = []
-    for source, flip, needed in ((own, 0, kv >= 0), (a1, 1, kv >= 0), (a2, 2, outer), (b2, 2, inner), (a3, 3, outer), (b1, 3, inner)):
-        at = pl.ds(pl.multiple_of((kv ^ flip) * count, count), count)
-        copies.append((needed, pltpu.make_async_copy(source.at[0:count], rows_ref.at[at], sems.at[len(copies)])))
-        if flip:
-            rider = source.at[count : count + depth]
-            target = riders_ref.at[flip - 1]
-            copies.append((needed, pltpu.make_async_copy(rider, target, rider_sems.at[len(copies)])))
+    for index, (source, flip, held) in enumerate(sources):
+        for slot in range(rows_ref.shape[0] // count):
+            needed = held & ((kv ^ flip) == first + slot * step)
+            target = rows_ref.at[slot * count : (slot + 1) * count]
+            copies.append((needed, pltpu.make_async_copy(source, target, sems.at[index])))
     for needed, copy in copies:
         pl.when(needed)(copy.start)
     for needed, copy in copies:
         pl.when(needed)(copy.wait)
-    rows = rows_ref[...]
-    query = jnp.dot(rows, weight_ref[0], preferred_element_type=F32) * (1.0 / math.sqrt(HD))
-    query_ref[...] = query.astype(BF16)
+
+
+def keys_values(rows, weight_ref, keyval_ref):
+    width = weight_ref.shape[2]
     for part in range(2):
         at = slice(part * width, (part + 1) * width)
         keyval_ref[:, at] = jnp.dot(rows, weight_ref[part + 1], preferred_element_type=F32).astype(BF16)
-    top, bottom = slice(0, count), slice((blocks - 1) * count, blocks * count)
+
+
+def project_edges_kernel(place_ref, weight_ref, *refs):
+    shards, (keyval_ref, even_ref, odd_ref, rows_ref, sems) = refs[:-5], refs[-5:]
+    tok, kv = place_ref[0], place_ref[1]
+    count = even_ref.shape[0]
+    shard_copies(kv, shards, rows_ref, sems, 0, 3)
+    keys_values(rows_ref[...], weight_ref, keyval_ref)
 
     @pl.when(tok % 2 == 0)
     def _():
-        even_ref[...] = keyval_ref[bottom]
-        odd_ref[...] = keyval_ref[top]
+        even_ref[...] = keyval_ref[count:]
+        odd_ref[...] = keyval_ref[:count]
 
     @pl.when(tok % 2 == 1)
     def _():
-        even_ref[...] = keyval_ref[top]
-        odd_ref[...] = keyval_ref[bottom]
-
-
-def project(place, weight, shards, blocks, depth):
+        even_ref[...] = keyval_ref[:count]
+        odd_ref[...] = keyval_ref[count:]
+
+
+def project_rest_kernel(place_ref, weight_ref, *refs):
+    shards, (query_ref, keyval_ref, rows_ref, sems) = refs[:-4], refs[-4:]
+    count = shards[0].shape[0]
+    shard_copies(place_ref[1], shards, rows_ref, sems, 0, 1)
+    keys_values(rows_ref[count:-count], weight_ref, keyval_ref)
+    query = jnp.dot(rows_ref[...], weight_ref[0], preferred_element_type=F32) * (1.0 / math.sqrt(HD))
+    query_ref[...] = query.astype(BF16)
+
+
+def project(place, weight, shards, blocks, edges):
     rows, width = shards[0].shape
     heads_width = weight.shape[2]
-    edge = jax.ShapeDtypeStruct((rows, 2 * heads_width), BF16)
+    shape = lambda count, columns: jax.ShapeDtypeStruct((count * rows, columns), BF16)
+    keyval = shape(2, 2 * heads_width)
+    if edges:
+        outs = (keyval, shape(1, 2 * heads_width), shape(1, 2 * heads_width))
+    else:
+        outs = (shape(blocks, heads_width), keyval)
     return pl.pallas_call(
-        project_kernel,
-        out_shape=(
-            jax.ShapeDtypeStruct((blocks * rows, heads_width), BF16),
-            jax.ShapeDtypeStruct((blocks * rows, 2 * heads_width), BF16),
-            edge,
-            edge,
-            jax.ShapeDtypeStruct((blocks - 1, depth, width), BF16),
-        ),
+        project_edges_kernel if edges else project_rest_kernel,
+        out_shape=outs,
         in_specs=[SMEM, VMEM] + [ANY] * len(shards),
-        out_specs=(VMEM,) * 5,
+        out_specs=(VMEM,) * len(outs),
         scratch_shapes=[
-            pltpu.VMEM((blocks * rows, width), BF16),
-            pltpu.SemaphoreType.DMA((2 * len(shards),)),
-            pltpu.SemaphoreType.DMA((2 * len(shards),)),
+            pltpu.VMEM((2 * rows if edges else blocks * rows, width), BF16),
+            pltpu.SemaphoreType.DMA((len(shards),)),
         ],
-        compiler_params=pltpu.CompilerParams(vmem_limit_bytes=14 * MIB),
+        compiler_params=pltpu.CompilerParams(vmem_limit_bytes=12 * MIB),
         cost_estimate=SHORT,
-        name="project",
+        name="project_edges" if edges else "project_rest",
     )(place, weight, *shards)
 
 
@@ -157,7 +160,7 @@
         out_ref[:, start : start + 2 * HD] = jnp.where(lane < HD, halves[0], halves[1]).astype(BF16)
 
 
-def attend_kernel(flips, place_ref, starts_ref, ends_ref, query_ref, keyval_ref, even_ref, odd_ref, *refs):
+def attend_kernel(flips, place_ref, starts_ref, ends_ref, query_ref, middle_ref, edges_ref, even_ref, odd_ref, *refs):
     outs = refs[: len(flips)]
     window_ref, bias_ref, scores_ref, weights_ref, sems = refs[len(flips) :]
     tok, kv = place_ref[0], place_ref[1]
@@ -170,10 +173,13 @@
             target = window_ref.at[index, part * count : (part + 1) * count]
             sem = sems.at[index, part]
             at = block + part - 1
-            inner = (at >= 0) & (at < blocks)
-            safe = jnp.where(inner, at, 0)
-            source = keyval_ref.at[pl.ds(pl.multiple_of(safe * count, count), count)]
-            copies.append((index, inner, pltpu.make_async_copy(source, target, sem)))
+            middle = (at > 0) & (at < blocks - 1)
+            start = jnp.where(middle, at - 1, 0)
+            source = middle_ref.at[pl.ds(pl.multiple_of(start * count, count), count)]
+            copies.append((index, middle, pltpu.make_async_copy(source, target, sem)))
+            for slot, edge in enumerate((0, blocks - 1)):
+                source = edges_ref.at[slot * count : (slot + 1) * count]
+                copies.append((index, at == edge, pltpu.make_async_copy(source, target, sem)))
             for first_edge, outside in ((tok % 2 == 1, at < 0), (tok % 2 == 0, at >= blocks)):
                 if part != 1:
                     copies.append((index, outside & first_edge, pltpu.make_async_copy(even_ref, target, sem)))
@@ -192,12 +198,12 @@
         attend(query, window_ref.at[index], bias_ref, scores_ref, weights_ref, outs[index])
 
 
-def attend_blocks(place, starts, ends, query, keyval, even, odd, rows, flips, name):
+def attend_blocks(place, starts, ends, query, middle, edges, even, odd, rows, flips, name):
     heads_width = query.shape[1]
     return pl.pallas_call(
         functools.partial(attend_kernel, flips),
         out_shape=tuple(jax.ShapeDtypeStruct((rows, heads_width), BF16) for _ in flips),
-        in_specs=[SMEM, VMEM, VMEM, VMEM, ANY, ANY, ANY],
+        in_specs=[SMEM, VMEM, VMEM, VMEM, ANY, ANY, ANY, ANY],
         out_specs=(VMEM,) * len(flips),
         scratch_shapes=[
             pltpu.VMEM((len(flips), 3 * rows, 2 * heads_width), BF16),
@@ -209,7 +215,7 @@
         compiler_params=pltpu.CompilerParams(vmem_limit_bytes=14 * MIB),
         cost_estimate=SHORT,
         name=name,
-    )(place, starts, ends, query, keyval, even, odd)
+    )(place, starts, ends, query, middle, edges, even, odd)
 
 
 def first_norm_kernel(layout, place_ref, hidden_ref, own_out_ref, gain_ref, bias_ref, *refs):
@@ -506,10 +512,21 @@
     place = jnp.stack([tok, kv]).astype(jnp.int32)
     eighth = lambda value: lax.dynamic_slice_in_dim(value, tok * (value.shape[0] // toks), value.shape[0] // toks, 0)
 
+    outward = [(1, 0), (2, 3)]
+    a1, b1 = over_edges(hidden_in, "kv", 0), over_edges(hidden_in, "kv", 1)
     out_part = eighth(out_weight)
     depth = out_part.shape[0]
-    shards = chain(jnp.concatenate([hidden_in, out_part, dec_query], axis=0))
-    a1, a2, a3, b1, b2 = shards
+    small = jnp.concatenate([out_part, dec_query], axis=0)
+    others = [swapped(small, "kv", flip) for flip in range(1, kvs)]
+    a2, b2 = lax.ppermute(b1, "kv", outward), over_edges(a1, "kv", 1)
+    queries = jnp.concatenate([dec_query] + [other[depth:] for other in others], axis=0).astype(F32)
+    partial = decode_partial(queries, dec_query.shape[0], kv_cache, piece_req, piece_used)
+    out_here = jnp.stack([other[:depth] for other in others])
+    out_x, out_y = swapped(out_here, "tok", 2), swapped(out_here, "tok", 4)
+    out_all = jnp.stack([out_here, out_x, out_y, swapped(out_y, "tok", 2)])
+    out_core = swapped(out_all, "tok", 1)
+    a3 = lax.ppermute(after(b2, partial), "kv", outward)
+    shards = (after(hidden_in, out_x, out_y), a1, a2, a3, b1, b2)
     inner = (kv == 1) | (kv == 2)
 
     feed_up, feed_down = after((eighth(up_weight), eighth(down_weight)), a2, b2)
@@ -525,18 +542,15 @@
     ends = ends[None, :]
 
     weight = jnp.transpose(qkv_weight, (1, 0, 2))
-    query, keyval, even, odd, out_here = project(place, weight, (hidden_in,) + shards, kvs, depth)
+    edges, even, odd = project(place, weight, shards, kvs, True)
     even, odd = over_edges(even, "tok", 0), over_edges(odd, "tok", 1)
-    window = (place, starts, ends, query, keyval, even, odd, rows)
+    query, middle = project(place, weight, (after(hidden_in, edges),) + shards[1:], kvs, False)
+    window = (middle, edges, even, odd, rows)
     parts = [None] * kvs
-    parts[3], parts[2] = attend_blocks(*window, (3, 2), "attend_far")
-    out_here = after(out_here, parts[3])
-    out_all = [out_here] + [swapped(out_here, "tok", flip) for flip in (2, 4, 6)]
-    window = (place, starts, ends, after(query, parts[3]), keyval, even, odd, rows)
+    parts[3], parts[2] = attend_blocks(place, starts, ends, query, *window, (3, 2), "attend_far")
+    query = after(query, parts[3])
     parts[3], parts[2] = swapped(parts[3], "kv", 3), swapped(parts[2], "kv", 2)
-    parts[1], parts[0] = attend_blocks(*window, (1, 0), "attend_near")
-    out_all = after(jnp.stack(out_all), parts[0])
-    out_core = swapped(out_all, "tok", 1)
+    parts[1], parts[0] = attend_blocks(place, starts, ends, query, *window, (1, 0), "attend_near")
     feed_here = jnp.where(inner, feed_inner, after(feed_outer, *parts[2:], parts[0]))
     parts[1] = swapped(parts[1], "kv", 1)
     feed_x, feed_y = swapped(feed_here, "tok", 2), swapped(feed_here, "tok", 4)
@@ -547,11 +561,7 @@
     half = feed_here.shape[0] // 2
     far_up = swapped(after(feed_y, normed)[:half], "tok", 2)
     far_down = swapped(after(feed_x, normed)[half:], "tok", 4)
-    ends_of = lambda outer_one, inner_one: jnp.where(inner, inner_one[rows + depth :], outer_one[rows + depth :])
-    queries = [dec_query, a1[rows + depth :], ends_of(a2, b2), ends_of(a3, b1)]
-    queries = after(jnp.concatenate(queries, axis=0).astype(F32), normed)
-    partial = decode_partial(queries, dec_query.shape[0], kv_cache, piece_req, piece_used)
-    held = jnp.concatenate([feed_here, feed_x, feed_y, after(far_up, partial), far_down], axis=0)
+    held = jnp.concatenate([feed_here, feed_x, feed_y, far_up, far_down], axis=0)
     near_away = feed_near(partner, up_weight, down_weight)
     feed_pieces = (held, swapped(after(held, partner), "tok", 1))
     away = feed_far(place, partner, near_away, feed_pieces)

time: 148 us -> 138 us (0.932)
  waiting for transfers between devices: 61.9 us -> 40.6 us
  starting transfers between devices: 36 us -> 52.1 us
  local copies, waits for them, and re-layouts: 12.5 us -> 6.72 us
  Pallas kernels: 29.3 us -> 31.8 us
    ppermute x2, waiting for transfers between devices: 23.1 us -> 3.55 us  [the longest x1 3.55 us: routed_body(): a2, b2 = (lax.ppermute(b1, 'kv', outward), over_edges(a1, 'kv', 1))]
    ppermute x17 -> x20, starting transfers between devices: 23.4 us -> 38.1 us  [swapped(): return lax.ppermute(value, axis, [(i, i ^ flip) for i in range(count)])]
    ppermute x5, waiting for transfers between devices: 13 us -> 3.93 us  [over_edges(): return lax.ppermute(value, axis, edges + [(j, i) for i, j in edges])]
    unnamed x61 -> x39, local copies, waits for them, and re-layouts: 9.67 us -> 4.68 us
    ppermute x1, waiting for transfers between devices: 0.01 us -> 3.23 us  [routed_body(): inner_down = lax.ppermute(feed_down, 'kv', [(0, 2), (3, 1)])]
    ppermute x17 -> x20, waiting for transfers between devices: 25.8 us -> 28.5 us  [swapped(): return lax.ppermute(value, axis, [(i, i ^ flip) for i in range(count)])]
    pallas_call x1 -> x2, Pallas kernels: 3 us -> 3.62 us  [project(): pl.pallas_call(project_edges_kernel if edges else project_rest_kernel, ou...]
  transfers between devices with their start and end apart: 27 -> 30, of which waited for: 14 -> 14; matrix products, arithmetic and copies ran while one was open for 5% -> 5% of each run, Pallas kernels for 17% -> 20%
where the time goes in v11:
time: 138 us
  starting transfers between devices  52.1 us (38%)
  waiting for transfers between devices  40.6 us (29%)
  Pallas kernels  31.8 us (23%)
  local copies, waits for them, and re-layouts  6.72 us (5%)
  other arithmetic  5.29 us (4%)
    ppermute x20, starting transfers between devices, swapped(): return lax.ppermute(value, axis, [(i, i ^ flip) for i in range(count)])  38.1 us
    ppermute x20, waiting for transfers between devices, swapped(): return lax.ppermute(value, axis, [(i, i ^ flip) for i in range(count)])  28.5 us
    pallas_call x2, Pallas kernels, attend_blocks(): pl.pallas_call(functools.partial(attend_kernel, flips), out_shape=tuple((...  11.4 us
    ppermute x5, starting transfers between devices, over_edges(): return lax.ppermute(value, axis, edges + [(j, i) for i, j in edges])  5.2 us
    unnamed x39, local copies, waits for them, and re-layouts  4.68 us
    ppermute x5, waiting for transfers between devices, over_edges(): return lax.ppermute(value, axis, edges + [(j, i) for i, j in edges])  3.93 us
    pallas_call x1, Pallas kernels, feed(): pl.pallas_call(feed_kernel, out_shape=jax.ShapeDtypeStruct((count, width)...  3.92 us
    pallas_call x1, Pallas kernels, decode(): pl.pallas_call(decode_kernel, grid=(pieces,), out_shape=jax.ShapeDtypeStr...  3.78 us
  transfers between devices with their start and end apart: 30, of which 14 were waited for; matrix products, arithmetic and copies ran while one was open for 5% of the time, Pallas kernels for 20%

profile of v11, /device:TPU:0, one launch (start us, length us, event | category | flops | bytes accessed | tf_op | source)
XLA Modules:
  0.0 137.6 jit_solution(14513309697620220039)
XLA Ops:
  0.6 3.1 %collective-permute-start.5 = (bf16[256,1024]{1,0:T(8,128)(2,1)}, bf16[256,1024]{1,0:T(8,128)(2,1)S(1)}, u32[]{:S(2)}, u32[]{:S(2)}) collective-permute-start(bf16[256,1024]{1,0:T(8,128)(2,1)} %hidden_ref.1), channel_id=1, source_target_pairs={{0,1},{2,3},{1,0},{3,2},{4,5},{6,7},{5,4},{7,6},{8,9},{10,11},{9,8... | collective-permute-start | bytes 1572872 | tf_op jit(solution)/shard_map/ppermute | solution.py:37
  6.0 4.4 %collective-permute-start = (bf16[34,1024]{1,0:T(8,128)(2,1)S(1)}, bf16[34,1024]{1,0:T(8,128)(2,1)S(1)}, u32[]{:S(2)}, u32[]{:S(2)}) collective-permute-start(bf16[34,1024]{1,0:T(8,128)(2,1)S(1)} %pad_maximum_fusion.3), channel_id=1, source_target_pairs={{0,1},{1,0},{2,3},{3,2},{4,5},{5,4},{6,7},{7,6},{8,9},{9,8},{10,11... | collective-permute-start | bytes 208904 | tf_op jit(solution)/shard_map/ppermute | solution.py:31
  10.3 2.4 %collective-permute-start.2 = (bf16[34,1024]{1,0:T(8,128)(2,1)S(1)}, bf16[34,1024]{1,0:T(8,128)(2,1)S(1)}, u32[]{:S(2)}, u32[]{:S(2)}) collective-permute-start(bf16[34,1024]{1,0:T(8,128)(2,1)S(1)} %pad_maximum_fusion.3), channel_id=1, source_target_pairs={{0,3},{1,2},{2,1},{3,0},{4,7},{5,6},{6,5},{7,4},{8,11},{9,10},{10,... | collective-permute-start | bytes 208904 | tf_op jit(solution)/shard_map/ppermute | solution.py:31
  12.8 3.9 %collective-permute-done.5.refs_1_ = bf16[256,1024]{1,0:T(8,128)(2,1)S(1)} collective-permute-done((bf16[256,1024]{1,0:T(8,128)(2,1)}, bf16[256,1024]{1,0:T(8,128)(2,1)S(1)}, u32[]{:S(2)}, u32[]{:S(2)}) %collective-permute-start.5) | collective-permute-done | bytes 524320 | tf_op jit(solution)/shard_map/ppermute | solution.py:37
  19.1 7.3 %collective-permute-done.1 = bf16[34,1024]{1,0:T(8,128)(2,1)S(1)} collective-permute-done((bf16[34,1024]{1,0:T(8,128)(2,1)S(1)}, bf16[34,1024]{1,0:T(8,128)(2,1)S(1)}, u32[]{:S(2)}, u32[]{:S(2)}) %collective-permute-start.1) | collective-permute-done | bytes 69664 | tf_op jit(solution)/shard_map/ppermute | solution.py:31
  28.5 1.9 %copy-done.4 = bf16[2,1,6,128,1024]{4,3,2,1,0:T(8,128)(2,1)S(1)} copy-done((bf16[2,1,6,128,1024]{4,3,2,1,0:T(8,128)(2,1)S(1)}, bf16[2,1,6,128,1024]{4,3,2,1,0:T(8,128)(2,1)}, u32[]{:S(2)}) %copy-start.4) | copy-done | bytes 3145752
  31.1 3.8 %decode.1 = f32[3,8,1024]{2,1,0:T(8,128)S(1)} custom-call(s32[6]{0:T(128)S(1)} %fusion.12.slot_ref, s32[6]{0:T(128)S(1)} %bitcast.151, f32[8,1024]{1,0:T(8,128)S(1)} %maximum_convert_fusion.query_ref, bf16[2,1,6,128,1024]{4,3,2,1,0:T(8,128)(2,1)S(1)} %copy-done.4), custom_call_target="tpu_custom_call" | custom-call | flops 1 | bytes 1 | tf_op jit(solution)/shard_map/decode/pallas_call | solution.py:453
  36.2 3.6 %collective-permute-done.7.refs_2_ = bf16[256,1024]{1,0:T(8,128)(2,1)S(1)} collective-permute-done((bf16[256,1024]{1,0:T(8,128)(2,1)S(1)}, bf16[256,1024]{1,0:T(8,128)(2,1)S(1)}, u32[]{:S(2)}, u32[]{:S(2)}) %collective-permute-start.7) | collective-permute-done | bytes 524320 | tf_op jit(solution)/shard_map/ppermute | solution.py:521
  39.7 3.6 %collective-permute-start.18 = (bf16[128,1024]{1,0:T(8,128)(2,1)S(1)}, bf16[128,1024]{1,0:T(8,128)(2,1)S(1)}, u32[]{:S(2)}, u32[]{:S(2)}) collective-permute-start(bf16[128,1024]{1,0:T(8,128)(2,1)S(1)} %get-tuple-element.41), channel_id=1, source_target_pairs={{0,2},{3,1},{4,6},{7,5},{8,10},{11,9},{12,14},{15,13},{16,18},{19,... | collective-permute-start | bytes 786440 | tf_op jit(solution)/shard_map/ppermute | solution.py:533
  44.7 1.6 %collective-permute-start.4 = (bf16[3,32,1024]{2,1,0:T(8,128)(2,1)S(1)}, bf16[3,32,1024]{2,1,0:T(8,128)(2,1)S(1)}, u32[]{:S(2)}, u32[]{:S(2)}) collective-permute-start(bf16[3,32,1024]{2,1,0:T(8,128)(2,1)S(1)} %get-tuple-element.57), channel_id=1, source_target_pairs={{0,16},{4,20},{8,24},{12,28},{16,0},{20,4},{24,8},{28,12},{1,17},{... | collective-permute-start | bytes 589832 | tf_op jit(solution)/shard_map/ppermute | solution.py:31
  46.3 1.5 %collective-permute-start.3 = (bf16[3,32,1024]{2,1,0:T(8,128)(2,1)S(1)}, bf16[3,32,1024]{2,1,0:T(8,128)(2,1)S(1)}, u32[]{:S(2)}, u32[]{:S(2)}) collective-permute-start(bf16[3,32,1024]{2,1,0:T(8,128)(2,1)S(1)} %get-tuple-element.57), channel_id=1, source_target_pairs={{0,8},{4,12},{8,0},{12,4},{16,24},{20,28},{24,16},{28,20},{1,9},{5... | collective-permute-start | bytes 589832 | tf_op jit(solution)/shard_map/ppermute | solution.py:31
  50.0 3.2 %collective-permute-done.19 = bf16[128,1024]{1,0:T(8,128)(2,1)S(1)} collective-permute-done((bf16[128,1024]{1,0:T(8,128)(2,1)S(1)}, bf16[128,1024]{1,0:T(8,128)(2,1)S(1)}, u32[]{:S(2)}, u32[]{:S(2)}) %collective-permute-start.19) | collective-permute-done | bytes 262176 | tf_op jit(solution)/shard_map/ppermute | solution.py:534
  57.0 3.4 %collective-permute-start.15 = (bf16[3,32,1024]{2,1,0:T(8,128)(2,1)S(1)}, bf16[3,32,1024]{2,1,0:T(8,128)(2,1)S(1)}, u32[]{:S(2)}, u32[]{:S(2)}) collective-permute-start(bf16[3,32,1024]{2,1,0:T(8,128)(2,1)S(1)} %collective-permute-done.4), channel_id=1, source_target_pairs={{0,8},{4,12},{8,0},{12,4},{16,24},{20,28},{24,16},{28,20},{1,9},{5... | collective-permute-start | bytes 589832 | tf_op jit(solution)/shard_map/ppermute | solution.py:31
  60.5 2.2 %project_rest.1 = (bf16[1024,256]{1,0:T(8,128)(2,1)S(1)}, bf16[512,512]{1,0:T(8,128)(2,1)S(1)}) custom-call(s32[2]{0:T(128)S(1)} %pad_add_fusion.place_ref, bf16[3,1024,256]{2,1,0:T(8,128)(2,1)S(1)} %bitcast.144, bf16[256,1024]{1,0:T(8,128)(2,1)S(1)} %copy-done.3, bf16[256,1024]{1,0:T(8,128)(2,1)S(1)} %collective-permute-done.5.refs_1_, ...), custom_call_target="tpu_custom_call" | custom-call | flops 1 | bytes 1 | tf_op jit(solution)/shard_map/project_rest/pallas_call | solution.py:112
  62.7 6.0 %attend_far.1 = (bf16[256,256]{1,0:T(8,128)(2,1)}, bf16[256,256]{1,0:T(8,128)(2,1)}) custom-call(s32[2]{0:T(128)S(1)} %pad_add_fusion.place_ref, s32[1,48]{1,0:T(1,128)S(1)} %subtract_bitcast_fusion.starts_ref, s32[1,48]{1,0:T(1,128)S(1)} %bitcast.149, bf16[1024,256]{1,0:T(8,128)(2,1)S(1)} %get-tuple-element.37.query_ref, ...), custom_call_target="tpu_custom_call" | custom-call | flops 1 | bytes 1 | tf_op jit(solution)/shard_map/attend_far/pallas_call | solution.py:203
  68.6 4.4 %collective-permute-start.13 = (bf16[256,256]{1,0:T(8,128)(2,1)}, bf16[256,256]{1,0:T(8,128)(2,1)}, u32[]{:S(2)}, u32[]{:S(2)}) collective-permute-start(bf16[256,256]{1,0:T(8,128)(2,1)} %get-tuple-element.40), channel_id=1, source_target_pairs={{0,2},{1,3},{2,0},{3,1},{4,6},{5,7},{6,4},{7,5},{8,10},{9,11},{10,... | collective-permute-start | bytes 393224 | tf_op jit(solution)/shard_map/ppermute | solution.py:31
  73.0 1.5 %collective-permute-start.14 = (bf16[256,256]{1,0:T(8,128)(2,1)}, bf16[256,256]{1,0:T(8,128)(2,1)}, u32[]{:S(2)}, u32[]{:S(2)}) collective-permute-start(bf16[256,256]{1,0:T(8,128)(2,1)} %get-tuple-element.36), channel_id=1, source_target_pairs={{0,3},{1,2},{2,1},{3,0},{4,7},{5,6},{6,5},{7,4},{8,11},{9,10},{10,... | collective-permute-start | bytes 393224 | tf_op jit(solution)/shard_map/ppermute | solution.py:31
  74.6 3.8 %collective-permute-start.16 = (bf16[4,3,32,1024]{3,2,1,0:T(8,128)(2,1)S(1)}, bf16[4,3,32,1024]{3,2,1,0:T(8,128)(2,1)}, u32[]{:S(2)}, u32[]{:S(2)}) collective-permute-start(bf16[4,3,32,1024]{3,2,1,0:T(8,128)(2,1)S(1)} %pad_maximum_fusion.refs_4_), channel_id=1, source_target_pairs={{0,4},{4,0},{8,12},{12,8},{16,20},{20,16},{24,28},{28,24},{1,5},{5... | collective-permute-start | bytes 2359304 | tf_op jit(solution)/shard_map/ppermute | solution.py:31
  80.4 5.5 %attend_near.1 = (bf16[256,256]{1,0:T(8,128)(2,1)S(1)}, bf16[256,256]{1,0:T(8,128)(2,1)S(1)}) custom-call(s32[2]{0:T(128)S(1)} %pad_add_fusion.place_ref, s32[1,48]{1,0:T(1,128)S(1)} %subtract_bitcast_fusion.starts_ref, s32[1,48]{1,0:T(1,128)S(1)} %bitcast.150, bf16[1024,256]{1,0:T(8,128)(2,1)S(1)} %get-tuple-element.37.query_ref, ...), custom_call_target="tpu_custom_call" | custom-call | flops 1 | bytes 1 | tf_op jit(solution)/shard_map/attend_near/pallas_call | solution.py:203
  87.4 3.8 %collective-permute-start.22 = (bf16[256,1024]{1,0:T(8,128)(2,1)S(1)}, bf16[256,1024]{1,0:T(8,128)(2,1)S(1)}, u32[]{:S(2)}, u32[]{:S(2)}) collective-permute-start(bf16[256,1024]{1,0:T(8,128)(2,1)S(1)} %get-tuple-element.55), channel_id=1, source_target_pairs={{0,16},{4,20},{8,24},{12,28},{16,0},{20,4},{24,8},{28,12},{1,17},{... | collective-permute-start | bytes 1572872 | tf_op jit(solution)/shard_map/ppermute | solution.py:31
  91.2 1.8 %collective-permute-start.12 = (bf16[256,256]{1,0:T(8,128)(2,1)S(1)}, bf16[256,256]{1,0:T(8,128)(2,1)S(1)}, u32[]{:S(2)}, u32[]{:S(2)}) collective-permute-start(bf16[256,256]{1,0:T(8,128)(2,1)S(1)} %get-tuple-element.39), channel_id=1, source_target_pairs={{0,1},{1,0},{2,3},{3,2},{4,5},{5,4},{6,7},{7,6},{8,9},{9,8},{10,11... | collective-permute-start | bytes 393224 | tf_op jit(solution)/shard_map/ppermute | solution.py:31
  93.0 3.1 %collective-permute-done.12.refs_1_ = bf16[256,256]{1,0:T(8,128)(2,1)S(1)} collective-permute-done((bf16[256,256]{1,0:T(8,128)(2,1)S(1)}, bf16[256,256]{1,0:T(8,128)(2,1)S(1)}, u32[]{:S(2)}, u32[]{:S(2)}) %collective-permute-start.12) | collective-permute-done | bytes 131104 | tf_op jit(solution)/shard_map/ppermute | solution.py:31
  96.2 3.7 %first_norm.1.rows_ref.normed_ref = bf16[256,1024]{1,0:T(8,128)(2,1)S(1)} custom-call(s32[2]{0:T(128)S(1)} %pad_add_fusion.place_ref, bf16[256,1024]{1,0:T(8,128)(2,1)S(1)} %copy-done.3, bf16[256,1024]{1,0:T(8,128)(2,1)S(1)} %copy-done.9, f32[1,1024]{1,0:T(1,128)S(1)} %bitcast.147, f32[1,1024]{1,0:T(1,128)S(1)} %bitcast.148, ...), custom_call_target="tpu_custom_call" | custom-call | flops 1 | bytes 1 | tf_op jit(solution)/shard_map/first_norm/pallas_call | solution.py:251
  99.9 1.9 %collective-permute-start.17 = (bf16[256,1024]{1,0:T(8,128)(2,1)S(1)}, bf16[256,1024]{1,0:T(8,128)(2,1)S(1)}, u32[]{:S(2)}, u32[]{:S(2)}) collective-permute-start(bf16[256,1024]{1,0:T(8,128)(2,1)S(1)} %first_norm.1.rows_ref.normed_ref), channel_id=1, source_target_pairs={{0,1},{1,0},{2,3},{3,2},{4,5},{5,4},{6,7},{7,6},{8,9},{9,8},{10,11... | collective-permute-start | bytes 1572872 | tf_op jit(solution)/shard_map/ppermute | solution.py:31
  104.9 5.2 %collective-permute-done.23 = bf16[128,1024]{1,0:T(8,128)(2,1)S(1)} collective-permute-done((bf16[128,1024]{1,0:T(8,128)(2,1)S(1)}, bf16[128,1024]{1,0:T(8,128)(2,1)S(1)}, u32[]{:S(2)}, u32[]{:S(2)}) %collective-permute-start.23) | collective-permute-done | bytes 262176 | tf_op jit(solution)/shard_map/ppermute | solution.py:31
  113.7 2.7 %collective-permute-done.25.core_ref = bf16[1024,1024]{1,0:T(8,128)(2,1)S(1)} collective-permute-done((bf16[1024,1024]{1,0:T(8,128)(2,1)S(1)}, bf16[1024,1024]{1,0:T(8,128)(2,1)S(1)}, u32[]{:S(2)}, u32[]{:S(2)}) %collective-permute-start.25) | collective-permute-done | bytes 2097184 | tf_op jit(solution)/shard_map/ppermute | solution.py:31
  116.4 2.6 %feed_far.1 = bf16[256,1024]{1,0:T(8,128)(2,1)S(1)} custom-call(s32[2]{0:T(128)S(1)} %pad_add_fusion.place_ref, bf16[256,1024]{1,0:T(8,128)(2,1)S(1)} %collective-permute-done.17.rows_ref, f32[256,1024]{1,0:T(8,128)S(1)} %feed_near.1.near_ref, bf16[1024,1024]{1,0:T(8,128)(2,1)S(1)} %constant_dynamic-update-slice_fusion.held_ref, ...), custom_call_target="tpu_custom_call" | custom-call | flops 1 | bytes 1 | tf_op jit(solution)/shard_map/feed_far/pallas_call | solution.py:359
  121.2 1.6 %collective-permute-start.28 = (f32[3,2,1024]{2,1,0:T(2,128)S(1)}, f32[3,2,1024]{2,1,0:T(2,128)S(1)}, u32[]{:S(2)}, u32[]{:S(2)}) collective-permute-start(f32[3,2,1024]{2,1,0:T(2,128)S(1)} %get-tuple-element.59), channel_id=1, source_target_pairs={{0,2},{1,3},{2,0},{3,1},{4,6},{5,7},{6,4},{7,5},{8,10},{9,11},{10,... | collective-permute-start | bytes 73736 | tf_op jit(solution)/shard_map/ppermute | solution.py:31
  122.8 2.1 %collective-permute-start.29 = (f32[3,2,1024]{2,1,0:T(2,128)S(1)}, f32[3,2,1024]{2,1,0:T(2,128)S(1)}, u32[]{:S(2)}, u32[]{:S(2)}) collective-permute-start(f32[3,2,1024]{2,1,0:T(2,128)S(1)} %get-tuple-element.58), channel_id=1, source_target_pairs={{0,3},{1,2},{2,1},{3,0},{4,7},{5,6},{6,5},{7,4},{8,11},{9,10},{10,... | collective-permute-start | bytes 73736 | tf_op jit(solution)/shard_map/ppermute | solution.py:31
  124.9 3.9 %feed_own.1.near_ref = f32[256,1024]{1,0:T(8,128)S(1)} custom-call(s32[2]{0:T(128)S(1)} %pad_add_fusion.place_ref, bf16[256,1024]{1,0:T(8,128)(2,1)S(1)} %first_norm.1.rows_ref.normed_ref, bf16[1024,1024]{1,0:T(8,128)(2,1)S(1)} %copy-done, bf16[1024,1024]{1,0:T(8,128)(2,1)S(1)} %copy-done.1, ...), custom_call_target="tpu_custom_call" | custom-call | flops 1 | bytes 1 | tf_op jit(solution)/shard_map/feed_own/pallas_call | solution.py:376
  128.9 5.2 %collective-permute-done.27 = f32[3,2,1024]{2,1,0:T(2,128)S(1)} collective-permute-done((f32[3,2,1024]{2,1,0:T(2,128)S(1)}, f32[3,2,1024]{2,1,0:T(2,128)S(1)}, u32[]{:S(2)}, u32[]{:S(2)}) %collective-permute-start.27) | collective-permute-done | bytes 24608 | tf_op jit(solution)/shard_map/ppermute | solution.py:31
  134.1 1.6 %collective-permute-done.29 = f32[3,2,1024]{2,1,0:T(2,128)S(1)} collective-permute-done((f32[3,2,1024]{2,1,0:T(2,128)S(1)}, f32[3,2,1024]{2,1,0:T(2,128)S(1)}, u32[]{:S(2)}, u32[]{:S(2)}) %collective-permute-start.29) | collective-permute-done | bytes 24608 | tf_op jit(solution)/shard_map/ppermute | solution.py:31
  (100 shorter events, 30.3 us)
Async XLA Ops:
  0.6 16.1 %collective-permute-start.5 = (bf16[256,1024]{1,0:T(8,128)(2,1)}, bf16[256,1024]{1,0:T(8,128)(2,1)S(1)}, u32[]{:S(2)}, u32[]{:S(2)}) collective-permute-start(bf16[256,1024]{1,0:T(8,128)(2,1)} %hidden_ref.1), channel_id=1, source_target_pairs={{0,1},{2,3},{1,0},{3,2},{4,5},{6,7},{5,4},{7,6},{8,9},{10,11},{9,8... | collective-permute-start | bytes 1572872 | tf_op jit(solution)/shard_map/ppermute | solution.py:37
  3.7 22.8 %collective-permute-start.6 = (bf16[256,1024]{1,0:T(8,128)(2,1)}, bf16[256,1024]{1,0:T(8,128)(2,1)S(1)}, u32[]{:S(2)}, u32[]{:S(2)}) collective-permute-start(bf16[256,1024]{1,0:T(8,128)(2,1)} %hidden_ref.1), channel_id=1, source_target_pairs={{1,2},{2,1},{5,6},{6,5},{9,10},{10,9},{13,14},{14,13},{17,18},{18,... | collective-permute-start | bytes 1572872 | tf_op jit(solution)/shard_map/ppermute | solution.py:37
  6.0 13.2 %collective-permute-start = (bf16[34,1024]{1,0:T(8,128)(2,1)S(1)}, bf16[34,1024]{1,0:T(8,128)(2,1)S(1)}, u32[]{:S(2)}, u32[]{:S(2)}) collective-permute-start(bf16[34,1024]{1,0:T(8,128)(2,1)S(1)} %pad_maximum_fusion.3), channel_id=1, source_target_pairs={{0,1},{1,0},{2,3},{3,2},{4,5},{5,4},{6,7},{7,6},{8,9},{9,8},{10,11... | collective-permute-start | bytes 208904 | tf_op jit(solution)/shard_map/ppermute | solution.py:31
  10.3 16.1 %collective-permute-start.1 = (bf16[34,1024]{1,0:T(8,128)(2,1)S(1)}, bf16[34,1024]{1,0:T(8,128)(2,1)S(1)}, u32[]{:S(2)}, u32[]{:S(2)}) collective-permute-start(bf16[34,1024]{1,0:T(8,128)(2,1)S(1)} %pad_maximum_fusion.3), channel_id=1, source_target_pairs={{0,2},{1,3},{2,0},{3,1},{4,6},{5,7},{6,4},{7,5},{8,10},{9,11},{10,... | collective-permute-start | bytes 208904 | tf_op jit(solution)/shard_map/ppermute | solution.py:31
  10.3 16.1 %collective-permute-start.2 = (bf16[34,1024]{1,0:T(8,128)(2,1)S(1)}, bf16[34,1024]{1,0:T(8,128)(2,1)S(1)}, u32[]{:S(2)}, u32[]{:S(2)}) collective-permute-start(bf16[34,1024]{1,0:T(8,128)(2,1)S(1)} %pad_maximum_fusion.3), channel_id=1, source_target_pairs={{0,3},{1,2},{2,1},{3,0},{4,7},{5,6},{6,5},{7,4},{8,11},{9,10},{10,... | collective-permute-start | bytes 208904 | tf_op jit(solution)/shard_map/ppermute | solution.py:31
  16.7 18.2 %collective-permute-start.8 = (bf16[256,1024]{1,0:T(8,128)(2,1)S(1)}, bf16[256,1024]{1,0:T(8,128)(2,1)S(1)}, u32[]{:S(2)}, u32[]{:S(2)}) collective-permute-start(bf16[256,1024]{1,0:T(8,128)(2,1)S(1)} %collective-permute-done.5.refs_1_), channel_id=1, source_target_pairs={{1,2},{2,1},{5,6},{6,5},{9,10},{10,9},{13,14},{14,13},{17,18},{18,... | collective-permute-start | bytes 1572872 | tf_op jit(solution)/shard_map/ppermute | solution.py:37
  26.5 13.2 %collective-permute-start.7 = (bf16[256,1024]{1,0:T(8,128)(2,1)S(1)}, bf16[256,1024]{1,0:T(8,128)(2,1)S(1)}, u32[]{:S(2)}, u32[]{:S(2)}) collective-permute-start(bf16[256,1024]{1,0:T(8,128)(2,1)S(1)} %collective-permute-done.6.refs_4_), channel_id=1, source_target_pairs={{1,0},{2,3},{5,4},{6,7},{9,8},{10,11},{13,12},{14,15},{17,16},{18,... | collective-permute-start | bytes 1572872 | tf_op jit(solution)/shard_map/ppermute | solution.py:521
  31.1 23.6 %copy-start.2 = (bf16[1024,3,256]{2,0,1:T(8,128)(2,1)S(1)}, bf16[1024,3,256]{2,0,1:T(8,128)(2,1)}, u32[]{:S(2)}) copy-start(bf16[1024,3,256]{2,0,1:T(8,128)(2,1)} %param.15) | copy-start | bytes 4718596
  31.1 23.6 %copy-start.3 = (bf16[256,1024]{1,0:T(8,128)(2,1)S(1)}, bf16[256,1024]{1,0:T(8,128)(2,1)}, u32[]{:S(2)}) copy-start(bf16[256,1024]{1,0:T(8,128)(2,1)} %hidden_ref.1) | copy-start | bytes 1572868
  34.9 18.4 %collective-permute-start.9 = (bf16[256,1024]{1,0:T(8,128)(2,1)S(1)}, bf16[256,1024]{1,0:T(8,128)(2,1)S(1)}, u32[]{:S(2)}, u32[]{:S(2)}) collective-permute-start(bf16[256,1024]{1,0:T(8,128)(2,1)S(1)} %collective-permute-done.8.refs_5_), channel_id=1, source_target_pairs={{1,0},{2,3},{5,4},{6,7},{9,8},{10,11},{13,12},{14,15},{17,16},{18,... | collective-permute-start | bytes 1572872 | tf_op jit(solution)/shard_map/ppermute | solution.py:528
  39.7 10.3 %collective-permute-start.18 = (bf16[128,1024]{1,0:T(8,128)(2,1)S(1)}, bf16[128,1024]{1,0:T(8,128)(2,1)S(1)}, u32[]{:S(2)}, u32[]{:S(2)}) collective-permute-start(bf16[128,1024]{1,0:T(8,128)(2,1)S(1)} %get-tuple-element.41), channel_id=1, source_target_pairs={{0,2},{3,1},{4,6},{7,5},{8,10},{11,9},{12,14},{15,13},{16,18},{19,... | collective-permute-start | bytes 786440 | tf_op jit(solution)/shard_map/ppermute | solution.py:533
  43.3 10.0 %collective-permute-start.19 = (bf16[128,1024]{1,0:T(8,128)(2,1)S(1)}, bf16[128,1024]{1,0:T(8,128)(2,1)S(1)}, u32[]{:S(2)}, u32[]{:S(2)}) collective-permute-start(bf16[128,1024]{1,0:T(8,128)(2,1)S(1)} %get-tuple-element.42), channel_id=1, source_target_pairs={{0,2},{3,1},{4,6},{7,5},{8,10},{11,9},{12,14},{15,13},{16,18},{19,... | collective-permute-start | bytes 786440 | tf_op jit(solution)/shard_map/ppermute | solution.py:534
  44.7 10.0 %collective-permute-start.4 = (bf16[3,32,1024]{2,1,0:T(8,128)(2,1)S(1)}, bf16[3,32,1024]{2,1,0:T(8,128)(2,1)S(1)}, u32[]{:S(2)}, u32[]{:S(2)}) collective-permute-start(bf16[3,32,1024]{2,1,0:T(8,128)(2,1)S(1)} %get-tuple-element.57), channel_id=1, source_target_pairs={{0,16},{4,20},{8,24},{12,28},{16,0},{20,4},{24,8},{28,12},{1,17},{... | collective-permute-start | bytes 589832 | tf_op jit(solution)/shard_map/ppermute | solution.py:31
  46.3 8.4 %collective-permute-start.3 = (bf16[3,32,1024]{2,1,0:T(8,128)(2,1)S(1)}, bf16[3,32,1024]{2,1,0:T(8,128)(2,1)S(1)}, u32[]{:S(2)}, u32[]{:S(2)}) collective-permute-start(bf16[3,32,1024]{2,1,0:T(8,128)(2,1)S(1)} %get-tuple-element.57), channel_id=1, source_target_pairs={{0,8},{4,12},{8,0},{12,4},{16,24},{20,28},{24,16},{28,20},{1,9},{5... | collective-permute-start | bytes 589832 | tf_op jit(solution)/shard_map/ppermute | solution.py:31
  53.3 32.7 %collective-permute-start.20 = (bf16[256,1024]{1,0:T(8,128)(2,1)}, bf16[256,1024]{1,0:T(8,128)(2,1)}, u32[]{:S(2)}, u32[]{:S(2)}) collective-permute-start(bf16[256,1024]{1,0:T(8,128)(2,1)} %pad_maximum_fusion.1), channel_id=1, source_target_pairs={{1,3},{2,0},{5,7},{6,4},{9,11},{10,8},{13,15},{14,12},{17,19},{18,... | collective-permute-start | bytes 1572872 | tf_op jit(solution)/shard_map/ppermute | solution.py:536
  56.2 6.5 %collective-permute-start.10 = (bf16[256,512]{1,0:T(8,128)(2,1)S(1)}, bf16[256,512]{1,0:T(8,128)(2,1)S(1)}, u32[]{:S(2)}, u32[]{:S(2)}) collective-permute-start(bf16[256,512]{1,0:T(8,128)(2,1)S(1)} %get-tuple-element.34), channel_id=1, source_target_pairs={{0,4},{8,12},{16,20},{24,28},{4,0},{12,8},{20,16},{28,24},{1,5},{9... | collective-permute-start | bytes 786440 | tf_op jit(solution)/shard_map/ppermute | solution.py:37
  56.3 6.4 %collective-permute-start.11 = (bf16[256,512]{1,0:T(8,128)(2,1)S(1)}, bf16[256,512]{1,0:T(8,128)(2,1)S(1)}, u32[]{:S(2)}, u32[]{:S(2)}) collective-permute-start(bf16[256,512]{1,0:T(8,128)(2,1)S(1)} %get-tuple-element.35), channel_id=1, source_target_pairs={{4,8},{12,16},{20,24},{8,4},{16,12},{24,20},{5,9},{13,17},{21,25},... | collective-permute-start | bytes 786440 | tf_op jit(solution)/shard_map/ppermute | solution.py:37
  57.0 17.5 %collective-permute-start.15 = (bf16[3,32,1024]{2,1,0:T(8,128)(2,1)S(1)}, bf16[3,32,1024]{2,1,0:T(8,128)(2,1)S(1)}, u32[]{:S(2)}, u32[]{:S(2)}) collective-permute-start(bf16[3,32,1024]{2,1,0:T(8,128)(2,1)S(1)} %collective-permute-done.4), channel_id=1, source_target_pairs={{0,8},{4,12},{8,0},{12,4},{16,24},{20,28},{24,16},{28,20},{1,9},{5... | collective-permute-start | bytes 589832 | tf_op jit(solution)/shard_map/ppermute | solution.py:31
  68.6 17.3 %collective-permute-start.13 = (bf16[256,256]{1,0:T(8,128)(2,1)}, bf16[256,256]{1,0:T(8,128)(2,1)}, u32[]{:S(2)}, u32[]{:S(2)}) collective-permute-start(bf16[256,256]{1,0:T(8,128)(2,1)} %get-tuple-element.40), channel_id=1, source_target_pairs={{0,2},{1,3},{2,0},{3,1},{4,6},{5,7},{6,4},{7,5},{8,10},{9,11},{10,... | collective-permute-start | bytes 393224 | tf_op jit(solution)/shard_map/ppermute | solution.py:31
  73.0 12.9 %collective-permute-start.14 = (bf16[256,256]{1,0:T(8,128)(2,1)}, bf16[256,256]{1,0:T(8,128)(2,1)}, u32[]{:S(2)}, u32[]{:S(2)}) collective-permute-start(bf16[256,256]{1,0:T(8,128)(2,1)} %get-tuple-element.36), channel_id=1, source_target_pairs={{0,3},{1,2},{2,1},{3,0},{4,7},{5,6},{6,5},{7,4},{8,11},{9,10},{10,... | collective-permute-start | bytes 393224 | tf_op jit(solution)/shard_map/ppermute | solution.py:31
  74.6 18.4 %collective-permute-start.16 = (bf16[4,3,32,1024]{3,2,1,0:T(8,128)(2,1)S(1)}, bf16[4,3,32,1024]{3,2,1,0:T(8,128)(2,1)}, u32[]{:S(2)}, u32[]{:S(2)}) collective-permute-start(bf16[4,3,32,1024]{3,2,1,0:T(8,128)(2,1)S(1)} %pad_maximum_fusion.refs_4_), channel_id=1, source_target_pairs={{0,4},{4,0},{8,12},{12,8},{16,20},{20,16},{24,28},{28,24},{1,5},{5... | collective-permute-start | bytes 2359304 | tf_op jit(solution)/shard_map/ppermute | solution.py:31
  87.4 15.5 %collective-permute-start.22 = (bf16[256,1024]{1,0:T(8,128)(2,1)S(1)}, bf16[256,1024]{1,0:T(8,128)(2,1)S(1)}, u32[]{:S(2)}, u32[]{:S(2)}) collective-permute-start(bf16[256,1024]{1,0:T(8,128)(2,1)S(1)} %get-tuple-element.55), channel_id=1, source_target_pairs={{0,16},{4,20},{8,24},{12,28},{16,0},{20,4},{24,8},{28,12},{1,17},{... | collective-permute-start | bytes 1572872 | tf_op jit(solution)/shard_map/ppermute | solution.py:31
  91.2 13.1 %collective-permute-start.21 = (bf16[256,1024]{1,0:T(8,128)(2,1)S(1)}, bf16[256,1024]{1,0:T(8,128)(2,1)S(1)}, u32[]{:S(2)}, u32[]{:S(2)}) collective-permute-start(bf16[256,1024]{1,0:T(8,128)(2,1)S(1)} %get-tuple-element.55), channel_id=1, source_target_pairs={{0,8},{4,12},{8,0},{12,4},{16,24},{20,28},{24,16},{28,20},{1,9},{5... | collective-permute-start | bytes 1572872 | tf_op jit(solution)/shard_map/ppermute | solution.py:31
  91.2 5.0 %collective-permute-start.12 = (bf16[256,256]{1,0:T(8,128)(2,1)S(1)}, bf16[256,256]{1,0:T(8,128)(2,1)S(1)}, u32[]{:S(2)}, u32[]{:S(2)}) collective-permute-start(bf16[256,256]{1,0:T(8,128)(2,1)S(1)} %get-tuple-element.39), channel_id=1, source_target_pairs={{0,1},{1,0},{2,3},{3,2},{4,5},{5,4},{6,7},{7,6},{8,9},{9,8},{10,11... | collective-permute-start | bytes 393224 | tf_op jit(solution)/shard_map/ppermute | solution.py:31
  99.9 12.3 %collective-permute-start.17 = (bf16[256,1024]{1,0:T(8,128)(2,1)S(1)}, bf16[256,1024]{1,0:T(8,128)(2,1)S(1)}, u32[]{:S(2)}, u32[]{:S(2)}) collective-permute-start(bf16[256,1024]{1,0:T(8,128)(2,1)S(1)} %first_norm.1.rows_ref.normed_ref), channel_id=1, source_target_pairs={{0,1},{1,0},{2,3},{3,2},{4,5},{5,4},{6,7},{7,6},{8,9},{9,8},{10,11... | collective-permute-start | bytes 1572872 | tf_op jit(solution)/shard_map/ppermute | solution.py:31
  102.9 7.2 %collective-permute-start.23 = (bf16[128,1024]{1,0:T(8,128)(2,1)S(1)}, bf16[128,1024]{1,0:T(8,128)(2,1)S(1)}, u32[]{:S(2)}, u32[]{:S(2)}) collective-permute-start(bf16[128,1024]{1,0:T(8,128)(2,1)S(1)} %slice.82), channel_id=1, source_target_pairs={{0,8},{4,12},{8,0},{12,4},{16,24},{20,28},{24,16},{28,20},{1,9},{5... | collective-permute-start | bytes 786440 | tf_op jit(solution)/shard_map/ppermute | solution.py:31
  104.3 7.1 %collective-permute-start.24 = (bf16[128,1024]{1,0:T(8,128)(2,1)S(1)}, bf16[128,1024]{1,0:T(8,128)(2,1)S(1)}, u32[]{:S(2)}, u32[]{:S(2)}) collective-permute-start(bf16[128,1024]{1,0:T(8,128)(2,1)S(1)} %slice.83), channel_id=1, source_target_pairs={{0,16},{4,20},{8,24},{12,28},{16,0},{20,4},{24,8},{28,12},{1,17},{... | collective-permute-start | bytes 786440 | tf_op jit(solution)/shard_map/ppermute | solution.py:31
  112.2 4.2 %collective-permute-start.25 = (bf16[1024,1024]{1,0:T(8,128)(2,1)S(1)}, bf16[1024,1024]{1,0:T(8,128)(2,1)S(1)}, u32[]{:S(2)}, u32[]{:S(2)}) collective-permute-start(bf16[1024,1024]{1,0:T(8,128)(2,1)S(1)} %constant_dynamic-update-slice_fusion.held_ref), channel_id=1, source_target_pairs={{0,4},{4,0},{8,12},{12,8},{16,20},{20,16},{24,28},{28,24},{1,5},{5... | collective-permute-start | bytes 6291464 | tf_op jit(solution)/shard_map/ppermute | solution.py:31
  119.0 17.3 %collective-permute-start.26 = (bf16[256,1024]{1,0:T(8,128)(2,1)S(1)}, bf16[256,1024]{1,0:T(8,128)(2,1)S(1)}, u32[]{:S(2)}, u32[]{:S(2)}) collective-permute-start(bf16[256,1024]{1,0:T(8,128)(2,1)S(1)} %feed_far.1), channel_id=1, source_target_pairs={{0,1},{1,0},{2,3},{3,2},{4,5},{5,4},{6,7},{7,6},{8,9},{9,8},{10,11... | collective-permute-start | bytes 1572872 | tf_op jit(solution)/shard_map/ppermute | solution.py:31
  120.5 13.6 %collective-permute-start.27 = (f32[3,2,1024]{2,1,0:T(2,128)S(1)}, f32[3,2,1024]{2,1,0:T(2,128)S(1)}, u32[]{:S(2)}, u32[]{:S(2)}) collective-permute-start(f32[3,2,1024]{2,1,0:T(2,128)S(1)} %get-tuple-element.60), channel_id=1, source_target_pairs={{0,1},{1,0},{2,3},{3,2},{4,5},{5,4},{6,7},{7,6},{8,9},{9,8},{10,11... | collective-permute-start | bytes 73736 | tf_op jit(solution)/shard_map/ppermute | solution.py:31
  121.2 12.9 %collective-permute-start.28 = (f32[3,2,1024]{2,1,0:T(2,128)S(1)}, f32[3,2,1024]{2,1,0:T(2,128)S(1)}, u32[]{:S(2)}, u32[]{:S(2)}) collective-permute-start(f32[3,2,1024]{2,1,0:T(2,128)S(1)} %get-tuple-element.59), channel_id=1, source_target_pairs={{0,2},{1,3},{2,0},{3,1},{4,6},{5,7},{6,4},{7,5},{8,10},{9,11},{10,... | collective-permute-start | bytes 73736 | tf_op jit(solution)/shard_map/ppermute | solution.py:31
  122.8 12.8 %collective-permute-start.29 = (f32[3,2,1024]{2,1,0:T(2,128)S(1)}, f32[3,2,1024]{2,1,0:T(2,128)S(1)}, u32[]{:S(2)}, u32[]{:S(2)}) collective-permute-start(f32[3,2,1024]{2,1,0:T(2,128)S(1)} %get-tuple-element.58), channel_id=1, source_target_pairs={{0,3},{1,2},{2,1},{3,0},{4,7},{5,6},{6,5},{7,4},{8,11},{9,10},{10,... | collective-permute-start | bytes 73736 | tf_op jit(solution)/shard_map/ppermute | solution.py:31
  (16 other events, 138.6 us)

commit v12 on v11

--- a/solution.py
+++ b/solution.py
@@ -161,10 +161,9 @@
 
 
 def attend_kernel(flips, place_ref, starts_ref, ends_ref, query_ref, middle_ref, edges_ref, even_ref, odd_ref, *refs):
-    outs = refs[: len(flips)]
-    window_ref, bias_ref, scores_ref, weights_ref, sems = refs[len(flips) :]
+    out_ref, window_ref, bias_ref, scores_ref, weights_ref, sems = refs
     tok, kv = place_ref[0], place_ref[1]
-    count = outs[0].shape[0]
+    count = out_ref.shape[0] // len(flips)
     blocks = query_ref.shape[0] // count
     copies = []
     for index, flip in enumerate(flips):
@@ -195,16 +194,17 @@
             if owner == index:
                 pl.when(needed)(copy.wait)
         query = query_ref[pl.ds(pl.multiple_of(block * count, count), count)]
-        attend(query, window_ref.at[index], bias_ref, scores_ref, weights_ref, outs[index])
+        out = out_ref.at[index * count : (index + 1) * count]
+        attend(query, window_ref.at[index], bias_ref, scores_ref, weights_ref, out)
 
 
 def attend_blocks(place, starts, ends, query, middle, edges, even, odd, rows, flips, name):
     heads_width = query.shape[1]
     return pl.pallas_call(
         functools.partial(attend_kernel, flips),
-        out_shape=tuple(jax.ShapeDtypeStruct((rows, heads_width), BF16) for _ in flips),
+        out_shape=jax.ShapeDtypeStruct((len(flips) * rows, heads_width), BF16),
         in_specs=[SMEM, VMEM, VMEM, VMEM, ANY, ANY, ANY, ANY],
-        out_specs=(VMEM,) * len(flips),
+        out_specs=VMEM,
         scratch_shapes=[
             pltpu.VMEM((len(flips), 3 * rows, 2 * heads_width), BF16),
             pltpu.VMEM((rows, 3 * rows), F32),
@@ -218,11 +218,12 @@
     )(place, starts, ends, query, middle, edges, even, odd)
 
 
-def first_norm_kernel(layout, place_ref, hidden_ref, own_out_ref, gain_ref, bias_ref, *refs):
-    parts, pieces = refs[: -5 - len(layout)], refs[-5 - len(layout) : -5]
-    normed_ref, all_ref, weight_ref, mixed_ref, sems = refs[-5:]
+def first_norm_kernel(layout, place_ref, own_ref, partner_ref, own_out_ref, gain_ref, bias_ref, *refs):
+    parts, pieces = refs[:4], refs[4 : 4 + len(layout)]
+    normed_ref, away_ref, all_ref, weight_ref, mixed_ref, sems = refs[4 + len(layout) :]
     tok = place_ref[0]
     quarters, heads_width, width = weight_ref.shape
+    count = own_ref.shape[0]
     copies = [pltpu.make_async_copy(own_out_ref, weight_ref.at[0], sems.at[0])]
     for flips, piece in zip(layout, pieces):
         for index, flip in enumerate(flips):
@@ -233,36 +234,40 @@
     for copy in copies:
         copy.start()
     for flip, part_ref in enumerate(parts):
-        all_ref[:, flip * heads_width : (flip + 1) * heads_width] = part_ref[...]
+        columns = slice(flip * heads_width, (flip + 1) * heads_width)
+        for half in range(2):
+            turned = half ^ (flip % 2)
+            all_ref[half * count : (half + 1) * count, columns] = part_ref[turned * count : (turned + 1) * count]
     for copy in copies:
         copy.wait()
     weight = weight_ref[...].reshape(quarters * heads_width, width)
     mixed_ref[...] = jnp.dot(all_ref[...], weight, preferred_element_type=F32)
-    for row in range(0, hidden_ref.shape[0], STRIP):
-        at = slice(row, row + STRIP)
-        mixed = hidden_ref[at].astype(F32) + mixed_ref[at]
-        normed_ref[at] = normalized(mixed, gain_ref[...], bias_ref[...]).astype(BF16)
-
-
-def first_norm(place, hidden, own_out, gain, bias, parts, pieces):
-    rows, width = hidden.shape
+    for half, (hidden_ref, result_ref) in enumerate(((own_ref, normed_ref), (partner_ref, away_ref))):
+        for row in range(0, count, STRIP):
+            at = slice(row, row + STRIP)
+            mixed = hidden_ref[at].astype(F32) + mixed_ref[half * count + row : half * count + row + STRIP]
+            result_ref[at] = normalized(mixed, gain_ref[...], bias_ref[...]).astype(BF16)
+
+
+def first_norm(place, own, partner, own_out, gain, bias, parts, pieces):
+    rows, width = own.shape
     heads_width = own_out.shape[0]
     layout = tuple(flips for flips, _ in pieces)
     return pl.pallas_call(
         functools.partial(first_norm_kernel, layout),
-        out_shape=jax.ShapeDtypeStruct((rows, width), BF16),
-        in_specs=[SMEM, VMEM, ANY, VMEM, VMEM] + [VMEM] * len(parts) + [ANY] * len(pieces),
-        out_specs=VMEM,
+        out_shape=(jax.ShapeDtypeStruct((rows, width), BF16),) * 2,
+        in_specs=[SMEM, VMEM, VMEM, ANY, VMEM, VMEM] + [VMEM] * len(parts) + [ANY] * len(pieces),
+        out_specs=(VMEM,) * 2,
         scratch_shapes=[
-            pltpu.VMEM((rows, width), BF16),
+            pltpu.VMEM((2 * rows, width), BF16),
             pltpu.VMEM((len(parts), heads_width, width), BF16),
-            pltpu.VMEM((rows, width), F32),
+            pltpu.VMEM((2 * rows, width), F32),
             pltpu.SemaphoreType.DMA((1 + sum(len(flips) for flips in layout),)),
         ],
-        compiler_params=pltpu.CompilerParams(vmem_limit_bytes=11 * MIB),
+        compiler_params=pltpu.CompilerParams(vmem_limit_bytes=14 * MIB),
         cost_estimate=SHORT,
         name="first_norm",
-    )(place, hidden, own_out, gain, bias, *parts, *[value for _, value in pieces])
+    )(place, own, partner, own_out, gain, bias, *parts, *[value for _, value in pieces])
 
 
 def gelu(values):
@@ -292,98 +297,47 @@
     return copies
 
 
-def feed_near_kernel(rows_ref, up_ref, down_ref, sum_ref, wide_ref, units_ref):
-    rows = rows_ref[...]
-    for index in range(up_ref.shape[1] // CHUNK):
-        at = slice(index * CHUNK, (index + 1) * CHUNK)
-        product = feed_chunk(rows, up_ref[:, at], down_ref.at[at], wide_ref.at[index % 2], units_ref.at[index % 2])
-        if index == 0:
-            sum_ref[...] = product
-        else:
-            sum_ref[...] += product
-
-
-def feed_far_kernel(
-    place_ref, rows_ref, near_ref, held_ref, core_ref, sum_ref, up_ref, down_ref, wide_ref, units_ref, total_ref, sems
-):
+def feed_kernel(place_ref, rows_ref, up_near_ref, down_near_ref, held_ref, core_ref, *refs):
+    sum_ref, up_ref, down_ref, wide_ref, units_ref, total_ref, sems = refs
     copies = far_copies(place_ref[0], held_ref, core_ref, up_ref, down_ref, sems)
     for copy in copies:
         copy.start()
     rows = rows_ref[...]
-    total_ref[...] = near_ref[...]
-    for copy in copies:
-        copy.wait()
-    for index in range(up_ref.shape[1] // CHUNK):
-        at = slice(index * CHUNK, (index + 1) * CHUNK)
-        slot = index % 2
-        total_ref[...] += feed_chunk(rows, up_ref[:, at], down_ref.at[at], wide_ref.at[slot], units_ref.at[slot])
-    sum_ref[...] = total_ref[...].astype(sum_ref.dtype)
-
-
-def feed_kernel(
-    place_ref, rows_ref, up_near_ref, down_near_ref, held_ref, core_ref, sum_ref, up_ref, down_ref, wide_ref, units_ref, sems
-):
-    copies = far_copies(place_ref[0], held_ref, core_ref, up_ref, down_ref, sems)
-    for copy in copies:
-        copy.start()
-    feed_near_kernel(rows_ref, up_near_ref, down_near_ref, sum_ref, wide_ref, units_ref)
-    rows = rows_ref[...]
-    for copy in copies:
-        copy.wait()
-    for index in range(up_ref.shape[1] // CHUNK):
-        at = slice(index * CHUNK, (index + 1) * CHUNK)
-        slot = index % 2
-        sum_ref[...] += feed_chunk(rows, up_ref[:, at], down_ref.at[at], wide_ref.at[slot], units_ref.at[slot])
-
-
-def feed_scratch(count):
-    return [pltpu.VMEM((2, count, CHUNK), F32), pltpu.VMEM((2, count, CHUNK), BF16)]
-
-
-def feed_near(rows, up_weight, down_weight):
-    return pl.pallas_call(
-        feed_near_kernel,
-        out_shape=jax.ShapeDtypeStruct(rows.shape, F32),
-        in_specs=[VMEM] * 3,
-        out_specs=VMEM,
-        scratch_shapes=feed_scratch(rows.shape[0]),
-        compiler_params=pltpu.CompilerParams(vmem_limit_bytes=14 * MIB),
-        cost_estimate=SHORT,
-        name="feed_near",
-    )(rows, up_weight, down_weight)
-
-
-def feed_far(place, rows, near, pieces):
-    count, width = rows.shape
-    units = pieces[0].shape[0]
-    return pl.pallas_call(
-        feed_far_kernel,
-        out_shape=jax.ShapeDtypeStruct((count, width), BF16),
-        in_specs=[SMEM] + [VMEM] * 2 + [ANY] * 2,
-        out_specs=VMEM,
-        scratch_shapes=[pltpu.VMEM((width, units), BF16), pltpu.VMEM((units, width), BF16)]
-        + feed_scratch(count)
-        + [pltpu.VMEM((count, width), F32), pltpu.SemaphoreType.DMA((16,))],
-        compiler_params=pltpu.CompilerParams(vmem_limit_bytes=14 * MIB),
-        cost_estimate=SHORT,
-        name="feed_far",
-    )(place, rows, near, *pieces)
-
-
-def feed(place, rows, up_weight, down_weight, pieces):
+    chunks = up_ref.shape[1] // CHUNK
+    for index in range(2 * chunks):
+        if index == chunks:
+            for copy in copies:
+                copy.wait()
+        up, down = (up_near_ref, down_near_ref) if index < chunks else (up_ref, down_ref)
+        at = slice(index % chunks * CHUNK, (index % chunks + 1) * CHUNK)
+        product = feed_chunk(rows, up[:, at], down.at[at], wide_ref.at[index % 2], units_ref.at[index % 2])
+        if index == 0:
+            total_ref[...] = product
+        elif index < 2 * chunks - 1:
+            total_ref[...] += product
+        else:
+            sum_ref[...] = (total_ref[...] + product).astype(sum_ref.dtype)
+
+
+def feed(place, rows, up_weight, down_weight, pieces, dtype, name):
     count, width = rows.shape
     units = up_weight.shape[1]
     return pl.pallas_call(
         feed_kernel,
-        out_shape=jax.ShapeDtypeStruct((count, width), F32),
+        out_shape=jax.ShapeDtypeStruct((count, width), dtype),
         in_specs=[SMEM] + [VMEM] * 3 + [ANY] * 2,
         out_specs=VMEM,
-        scratch_shapes=[pltpu.VMEM((width, units), BF16), pltpu.VMEM((units, width), BF16)]
-        + feed_scratch(count)
-        + [pltpu.SemaphoreType.DMA((16,))],
+        scratch_shapes=[
+            pltpu.VMEM((width, units), BF16),
+            pltpu.VMEM((units, width), BF16),
+            pltpu.VMEM((2, count, CHUNK), F32),
+            pltpu.VMEM((2, count, CHUNK), BF16),
+            pltpu.VMEM((count, width), F32),
+            pltpu.SemaphoreType.DMA((16,)),
+        ],
         compiler_params=pltpu.CompilerParams(vmem_limit_bytes=18 * MIB),
         cost_estimate=SHORT,
-        name="feed_own",
+        name=name,
     )(place, rows, up_weight, down_weight, *pieces)
 
 
@@ -523,18 +477,14 @@
     partial = decode_partial(queries, dec_query.shape[0], kv_cache, piece_req, piece_used)
     out_here = jnp.stack([other[:depth] for other in others])
     out_x, out_y = swapped(out_here, "tok", 2), swapped(out_here, "tok", 4)
-    out_all = jnp.stack([out_here, out_x, out_y, swapped(out_y, "tok", 2)])
-    out_core = swapped(out_all, "tok", 1)
     a3 = lax.ppermute(after(b2, partial), "kv", outward)
-    shards = (after(hidden_in, out_x, out_y), a1, a2, a3, b1, b2)
+    out_far = swapped(out_here, "tok", 6)
+    shards = (after(hidden_in, out_x, out_y, out_far), a1, a2, a3, b1, b2)
     inner = (kv == 1) | (kv == 2)
 
-    feed_up, feed_down = after((eighth(up_weight), eighth(down_weight)), a2, b2)
-    inner_up = lax.ppermute(feed_up, "kv", [(0, 2), (3, 1)])
-    inner_down = lax.ppermute(feed_down, "kv", [(0, 2), (3, 1)])
-    feed_part = after(jnp.concatenate([feed_up, feed_down], axis=0), a3, inner_up, inner_down)
-    feed_outer = lax.ppermute(feed_part, "kv", [(1, 3), (2, 0)])
-    feed_inner = jnp.concatenate([inner_up, inner_down], axis=0)
+    feed_part = jnp.concatenate([eighth(up_weight), eighth(down_weight)], axis=0)
+    feed_inner = lax.ppermute(after(feed_part, a2, b2), "kv", [(0, 2), (3, 1)])
+    feed_outer = lax.ppermute(after(feed_part, a3, feed_inner), "kv", [(1, 3), (2, 0)])
 
     order = jnp.arange(stretch_len.shape[0])
     ends = jnp.sum(jnp.where(order[:, None] <= order[None, :], stretch_len[:, None], 0), axis=0, dtype=jnp.int32)
@@ -546,28 +496,28 @@
     even, odd = over_edges(even, "tok", 0), over_edges(odd, "tok", 1)
     query, middle = project(place, weight, (after(hidden_in, edges),) + shards[1:], kvs, False)
     window = (middle, edges, even, odd, rows)
-    parts = [None] * kvs
-    parts[3], parts[2] = attend_blocks(place, starts, ends, query, *window, (3, 2), "attend_far")
-    query = after(query, parts[3])
-    parts[3], parts[2] = swapped(parts[3], "kv", 3), swapped(parts[2], "kv", 2)
-    parts[1], parts[0] = attend_blocks(place, starts, ends, query, *window, (1, 0), "attend_near")
-    feed_here = jnp.where(inner, feed_inner, after(feed_outer, *parts[2:], parts[0]))
-    parts[1] = swapped(parts[1], "kv", 1)
+    far = attend_blocks(place, starts, ends, query, *window, (2, 3), "attend_far")
+    far_heads = swapped(far, "kv", 2)
+    feed_here = jnp.where(inner, feed_inner, after(feed_outer, far))
     feed_x, feed_y = swapped(feed_here, "tok", 2), swapped(feed_here, "tok", 4)
-    out_pieces = [((0, 2, 4, 6), out_all), ((1, 3, 5, 7), out_core)]
-    normed = first_norm(place, hidden_in, out_weight, ln1_gain[None, :], ln1_bias[None, :], parts, out_pieces)
-
-    partner = swapped(normed, "kv", 1)
+    near = attend_blocks(place, starts, ends, after(query, feed_here), *window, (0, 1), "attend_near")
+    partner_heads, passed_heads = swapped(near, "kv", 1), swapped(far_heads, "kv", 1)
+    parts = (near, partner_heads, far_heads, passed_heads)
+
+    out_all = jnp.stack([out_here, out_x, out_y, out_far])
+    out_pieces = [((0, 2, 4, 6), out_all), ((1, 3, 5, 7), swapped(after(out_all, near, far_heads), "tok", 1))]
     half = feed_here.shape[0] // 2
-    far_up = swapped(after(feed_y, normed)[:half], "tok", 2)
-    far_down = swapped(after(feed_x, normed)[half:], "tok", 4)
+    far_up = swapped(after(feed_y, far_heads, partner_heads)[:half], "tok", 2)
+    far_down = swapped(after(feed_x, far_heads, partner_heads)[half:], "tok", 4)
     held = jnp.concatenate([feed_here, feed_x, feed_y, far_up, far_down], axis=0)
-    near_away = feed_near(partner, up_weight, down_weight)
-    feed_pieces = (held, swapped(after(held, partner), "tok", 1))
-    away = feed_far(place, partner, near_away, feed_pieces)
+    feed_pieces = (held, swapped(after(held, passed_heads), "tok", 1))
+
+    gain, bias = ln1_gain[None, :], ln1_bias[None, :]
+    normed, partner = first_norm(place, hidden_in, a1, out_weight, gain, bias, parts, out_pieces)
+    away = feed(place, partner, up_weight, down_weight, feed_pieces, BF16, "feed_partner")
     arrived = swapped(away, "kv", 1)
     dec_parts = exchanged_partials(after(partial, away), dec_query.shape[0])
-    mine = feed(place, after(normed, away), up_weight, down_weight, feed_pieces)
+    mine = feed(place, after(normed, away), up_weight, down_weight, feed_pieces, F32, "feed_own")
     prefill_out = finish(normed, mine, arrived, ln2_gain[None, :], ln2_bias[None, :])
 
     return prefill_out, merged_partials(after(tuple(dec_parts), mine))

time: 138 us -> 137 us (level)
  starting transfers between devices: 52.1 us -> 46 us
  waiting for transfers between devices: 40.6 us -> 44.5 us
    ppermute x20 -> x19, starting transfers between devices: 38.1 us -> 27 us  [swapped(): return lax.ppermute(value, axis, [(i, i ^ flip) for i in range(count)])]
    pallas_call x5 -> x3, Pallas kernels: 19.2 us -> 14.1 us  [the longest x2 10.9 us: attend_blocks(): pl.pallas_call(functools.partial(attend_kernel, flips), out_shape=jax.Sha...]
    pallas_call x1 -> x2, Pallas kernels: 3.92 us -> 7.8 us  [feed(): pl.pallas_call(feed_kernel, out_shape=jax.ShapeDtypeStruct((count, width)...]
    ppermute x5, starting transfers between devices: 5.2 us -> 8.74 us  [over_edges(): return lax.ppermute(value, axis, edges + [(j, i) for i, j in edges])]
    ppermute x20 -> x19, waiting for transfers between devices: 28.5 us -> 31.6 us  [swapped(): return lax.ppermute(value, axis, [(i, i ^ flip) for i in range(count)])]
    ppermute x1, waiting for transfers between devices: 0.01 us -> 2.61 us  [routed_body(): a3 = lax.ppermute(after(b2, partial), 'kv', outward)]
    ppermute x5, waiting for transfers between devices: 3.93 us -> 6.26 us  [over_edges(): return lax.ppermute(value, axis, edges + [(j, i) for i, j in edges])]
    ppermute x3 -> x2, waiting for transfers between devices: 4.69 us -> 2.56 us  [the longest x1 2.56 us: routed_body(): feed_inner = lax.ppermute(after(feed_part, a2, b2), 'kv', [(0, 2), (3, 1)])]
  transfers between devices with their start and end apart: 30 -> 28, of which waited for: 14 -> 12; matrix products, arithmetic and copies ran while one was open for 5% -> 4% of each run, Pallas kernels for 20% -> 19%
where the time goes in v12:
time: 137 us; the launch traced here: 136 us
  starting transfers between devices  46 us (34%)
  waiting for transfers between devices  44.5 us (32%)
  Pallas kernels  31.4 us (23%)
  local copies, waits for them, and re-layouts  8.05 us (6%)
  other arithmetic  5.11 us (4%)
    ppermute x19, waiting for transfers between devices, swapped(): return lax.ppermute(value, axis, [(i, i ^ flip) for i in range(count)])  31.6 us
    ppermute x19, starting transfers between devices, swapped(): return lax.ppermute(value, axis, [(i, i ^ flip) for i in range(count)])  27 us
    pallas_call x2, Pallas kernels, attend_blocks(): pl.pallas_call(functools.partial(attend_kernel, flips), out_shape=jax.Sha...  10.9 us
    ppermute x5, starting transfers between devices, over_edges(): return lax.ppermute(value, axis, edges + [(j, i) for i, j in edges])  8.74 us
    pallas_call x2, Pallas kernels, feed(): pl.pallas_call(feed_kernel, out_shape=jax.ShapeDtypeStruct((count, width)...  7.8 us
    ppermute x1, starting transfers between devices, routed_body(): feed_inner = lax.ppermute(after(feed_part, a2, b2), 'kv', [(0, 2), (3, 1)])  6.4 us
    ppermute x5, waiting for transfers between devices, over_edges(): return lax.ppermute(value, axis, edges + [(j, i) for i, j in edges])  6.26 us
    unnamed x63, local copies, waits for them, and re-layouts  6.01 us
  transfers between devices with their start and end apart: 28, of which 12 were waited for; matrix products, arithmetic and copies ran while one was open for 4% of the time, Pallas kernels for 19%

profile of v12, /device:TPU:0, one launch (start us, length us, event | category | flops | bytes accessed | tf_op | source)
XLA Modules:
  0.0 136.3 jit_solution(17397914251928022814)
XLA Ops:
  1.5 5.9 %collective-permute-start = (bf16[256,1024]{1,0:T(8,128)(2,1)}, bf16[256,1024]{1,0:T(8,128)(2,1)S(1)}, u32[]{:S(2)}, u32[]{:S(2)}) collective-permute-start(bf16[256,1024]{1,0:T(8,128)(2,1)} %own_ref.1), channel_id=1, source_target_pairs={{0,1},{2,3},{1,0},{3,2},{4,5},{6,7},{5,4},{7,6},{8,9},{10,11},{9,8... | collective-permute-start | bytes 1572872 | tf_op jit(solution)/shard_map/ppermute | solution.py:37
  10.4 2.9 %collective-permute-start.1 = (bf16[34,1024]{1,0:T(8,128)(2,1)S(1)}, bf16[34,1024]{1,0:T(8,128)(2,1)S(1)}, u32[]{:S(2)}, u32[]{:S(2)}) collective-permute-start(bf16[34,1024]{1,0:T(8,128)(2,1)S(1)} %pad_maximum_fusion.3), channel_id=1, source_target_pairs={{0,1},{1,0},{2,3},{3,2},{4,5},{5,4},{6,7},{7,6},{8,9},{9,8},{10,11... | collective-permute-start | bytes 208904 | tf_op jit(solution)/shard_map/ppermute | solution.py:31
  15.3 6.2 %collective-permute-done.refs_1_.partner_ref = bf16[256,1024]{1,0:T(8,128)(2,1)S(1)} collective-permute-done((bf16[256,1024]{1,0:T(8,128)(2,1)}, bf16[256,1024]{1,0:T(8,128)(2,1)S(1)}, u32[]{:S(2)}, u32[]{:S(2)}) %collective-permute-start) | collective-permute-done | bytes 524320 | tf_op jit(solution)/shard_map/ppermute | solution.py:37
  24.1 3.0 %collective-permute-done.2 = bf16[34,1024]{1,0:T(8,128)(2,1)S(1)} collective-permute-done((bf16[34,1024]{1,0:T(8,128)(2,1)S(1)}, bf16[34,1024]{1,0:T(8,128)(2,1)S(1)}, u32[]{:S(2)}, u32[]{:S(2)}) %collective-permute-start.2) | collective-permute-done | bytes 69664 | tf_op jit(solution)/shard_map/ppermute | solution.py:31
  27.3 1.9 %copy-done.4 = bf16[2,1,6,128,1024]{4,3,2,1,0:T(8,128)(2,1)S(1)} copy-done((bf16[2,1,6,128,1024]{4,3,2,1,0:T(8,128)(2,1)S(1)}, bf16[2,1,6,128,1024]{4,3,2,1,0:T(8,128)(2,1)}, u32[]{:S(2)}) %copy-start.4) | copy-done | bytes 3145752
  29.2 3.8 %decode.1 = f32[3,8,1024]{2,1,0:T(8,128)S(1)} custom-call(s32[6]{0:T(128)S(1)} %fusion.12.slot_ref, s32[6]{0:T(128)S(1)} %bitcast.151, f32[8,1024]{1,0:T(8,128)S(1)} %maximum_convert_fusion.query_ref, bf16[2,1,6,128,1024]{4,3,2,1,0:T(8,128)(2,1)S(1)} %copy-done.4), custom_call_target="tpu_custom_call" | custom-call | flops 1 | bytes 1 | tf_op jit(solution)/shard_map/decode/pallas_call | solution.py:407
  34.3 1.4 %collective-permute-done.8.refs_2_ = bf16[256,1024]{1,0:T(8,128)(2,1)S(1)} collective-permute-done((bf16[256,1024]{1,0:T(8,128)(2,1)S(1)}, bf16[256,1024]{1,0:T(8,128)(2,1)S(1)}, u32[]{:S(2)}, u32[]{:S(2)}) %collective-permute-start.8) | collective-permute-done | bytes 524320 | tf_op jit(solution)/shard_map/ppermute | solution.py:475
  35.7 6.4 %collective-permute-start.11 = (bf16[256,1024]{1,0:T(8,128)(2,1)}, bf16[256,1024]{1,0:T(8,128)(2,1)S(1)}, u32[]{:S(2)}, u32[]{:S(2)}) collective-permute-start(bf16[256,1024]{1,0:T(8,128)(2,1)} %pad_maximum_fusion.1), channel_id=1, source_target_pairs={{0,2},{3,1},{4,6},{7,5},{8,10},{11,9},{12,14},{15,13},{16,18},{19,... | collective-permute-start | bytes 1572872 | tf_op jit(solution)/shard_map/ppermute | solution.py:486
  42.9 1.5 %collective-permute-start.4 = (bf16[3,32,1024]{2,1,0:T(8,128)(2,1)S(1)}, bf16[3,32,1024]{2,1,0:T(8,128)(2,1)S(1)}, u32[]{:S(2)}, u32[]{:S(2)}) collective-permute-start(bf16[3,32,1024]{2,1,0:T(8,128)(2,1)S(1)} %get-tuple-element.53), channel_id=1, source_target_pairs={{0,8},{4,12},{8,0},{12,4},{16,24},{20,28},{24,16},{28,20},{1,9},{5... | collective-permute-start | bytes 589832 | tf_op jit(solution)/shard_map/ppermute | solution.py:31
  44.4 1.5 %collective-permute-start.5 = (bf16[3,32,1024]{2,1,0:T(8,128)(2,1)S(1)}, bf16[3,32,1024]{2,1,0:T(8,128)(2,1)S(1)}, u32[]{:S(2)}, u32[]{:S(2)}) collective-permute-start(bf16[3,32,1024]{2,1,0:T(8,128)(2,1)S(1)} %get-tuple-element.53), channel_id=1, source_target_pairs={{0,16},{4,20},{8,24},{12,28},{16,0},{20,4},{24,8},{28,12},{1,17},{... | collective-permute-start | bytes 589832 | tf_op jit(solution)/shard_map/ppermute | solution.py:31
  46.4 2.6 %collective-permute-done.10.refs_3_ = bf16[256,1024]{1,0:T(8,128)(2,1)S(1)} collective-permute-done((bf16[256,1024]{1,0:T(8,128)(2,1)S(1)}, bf16[256,1024]{1,0:T(8,128)(2,1)S(1)}, u32[]{:S(2)}, u32[]{:S(2)}) %collective-permute-start.10) | collective-permute-done | bytes 524320 | tf_op jit(solution)/shard_map/ppermute | solution.py:480
  49.0 2.6 %collective-permute-done.11 = bf16[256,1024]{1,0:T(8,128)(2,1)S(1)} collective-permute-done((bf16[256,1024]{1,0:T(8,128)(2,1)}, bf16[256,1024]{1,0:T(8,128)(2,1)S(1)}, u32[]{:S(2)}, u32[]{:S(2)}) %collective-permute-start.11) | collective-permute-done | bytes 524320 | tf_op jit(solution)/shard_map/ppermute | solution.py:486
  53.0 2.3 %project_edges.1 = (bf16[512,512]{1,0:T(8,128)(2,1)S(1)}, bf16[256,512]{1,0:T(8,128)(2,1)}, bf16[256,512]{1,0:T(8,128)(2,1)}) custom-call(s32[2]{0:T(128)S(1)} %pad_add_fusion.place_ref, bf16[3,1024,256]{2,1,0:T(8,128)(2,1)S(1)} %bitcast.143, bf16[256,1024]{1,0:T(8,128)(2,1)S(1)} %copy-done.3, ...), custom_call_target="tpu_custom_call" | custom-call | flops 1 | bytes 1 | tf_op jit(solution)/shard_map/project_edges/pallas_call | solution.py:112
  56.2 1.3 collective-permute-start.14
  60.8 2.2 %project_rest.1 = (bf16[1024,256]{1,0:T(8,128)(2,1)S(1)}, bf16[512,512]{1,0:T(8,128)(2,1)S(1)}) custom-call(s32[2]{0:T(128)S(1)} %pad_add_fusion.place_ref, bf16[3,1024,256]{2,1,0:T(8,128)(2,1)S(1)} %bitcast.144, bf16[256,1024]{1,0:T(8,128)(2,1)S(1)} %copy-done.3, bf16[256,1024]{1,0:T(8,128)(2,1)S(1)} %collective-permute-done.refs_1_.partner_ref, ...), custom_call_target="tpu_custom_call" | custom-call | flops 1 | bytes 1 | tf_op jit(solution)/shard_map/project_rest/pallas_call | solution.py:112
  63.0 5.3 %attend_far.1 = bf16[512,256]{1,0:T(8,128)(2,1)S(1)} custom-call(s32[2]{0:T(128)S(1)} %pad_add_fusion.place_ref, s32[1,48]{1,0:T(1,128)S(1)} %subtract_bitcast_fusion.starts_ref, s32[1,48]{1,0:T(1,128)S(1)} %bitcast.149, bf16[1024,256]{1,0:T(8,128)(2,1)S(1)} %get-tuple-element.37.query_ref, bf16[512,512]{1,0:T(8,128)(2,1)S(1)} %get-tuple-element.33.middle_ref, ...), custom_call_target="tpu_custom_call" | custom-call | flops 1 | bytes 1 | tf_op jit(solution)/shard_map/attend_far/pallas_call | solution.py:203
  69.5 6.2 %collective-permute-start.20 = (bf16[256,1024]{1,0:T(8,128)(2,1)S(1)}, bf16[256,1024]{1,0:T(8,128)(2,1)S(1)}, u32[]{:S(2)}, u32[]{:S(2)}) collective-permute-start(bf16[256,1024]{1,0:T(8,128)(2,1)S(1)} %get-tuple-element.51), channel_id=1, source_target_pairs={{0,16},{4,20},{8,24},{12,28},{16,0},{20,4},{24,8},{28,12},{1,17},{... | collective-permute-start | bytes 1572872 | tf_op jit(solution)/shard_map/ppermute | solution.py:31
  76.0 3.6 %collective-permute-start.16 = (bf16[512,256]{1,0:T(8,128)(2,1)S(1)}, bf16[512,256]{1,0:T(8,128)(2,1)S(1)}, u32[]{:S(2)}, u32[]{:S(2)}) collective-permute-start(bf16[512,256]{1,0:T(8,128)(2,1)S(1)} %attend_far.1), channel_id=1, source_target_pairs={{0,2},{1,3},{2,0},{3,1},{4,6},{5,7},{6,4},{7,5},{8,10},{9,11},{10,... | collective-permute-start | bytes 786440 | tf_op jit(solution)/shard_map/ppermute | solution.py:31
  79.6 5.6 %attend_near.1.refs_0_ = bf16[512,256]{1,0:T(8,128)(2,1)S(1)} custom-call(s32[2]{0:T(128)S(1)} %pad_add_fusion.place_ref, s32[1,48]{1,0:T(1,128)S(1)} %subtract_bitcast_fusion.starts_ref, s32[1,48]{1,0:T(1,128)S(1)} %bitcast.150, bf16[1024,256]{1,0:T(8,128)(2,1)S(1)} %get-tuple-element.37.query_ref, bf16[512,512]{1,0:T(8,128)(2,1)S(1)} %get-tuple-element.33.middle_ref, ...), custom_call_target="tpu_custom_call" | custom-call | flops 1 | bytes 1 | tf_op jit(solution)/shard_map/attend_near/pallas_call | solution.py:203
  85.4 5.7 %collective-permute-done.16.refs_2_ = bf16[512,256]{1,0:T(8,128)(2,1)S(1)} collective-permute-done((bf16[512,256]{1,0:T(8,128)(2,1)S(1)}, bf16[512,256]{1,0:T(8,128)(2,1)S(1)}, u32[]{:S(2)}, u32[]{:S(2)}) %collective-permute-start.16) | collective-permute-done | bytes 262176 | tf_op jit(solution)/shard_map/ppermute | solution.py:31
  91.1 5.3 %collective-permute-done.15.refs_1_ = bf16[512,256]{1,0:T(8,128)(2,1)S(1)} collective-permute-done((bf16[512,256]{1,0:T(8,128)(2,1)S(1)}, bf16[512,256]{1,0:T(8,128)(2,1)S(1)}, u32[]{:S(2)}, u32[]{:S(2)}) %collective-permute-start.15) | collective-permute-done | bytes 262176 | tf_op jit(solution)/shard_map/ppermute | solution.py:31
  96.9 1.6 %collective-permute-start.22 = (bf16[128,1024]{1,0:T(8,128)(2,1)S(1)}, bf16[128,1024]{1,0:T(8,128)(2,1)S(1)}, u32[]{:S(2)}, u32[]{:S(2)}) collective-permute-start(bf16[128,1024]{1,0:T(8,128)(2,1)S(1)} %slice.83), channel_id=1, source_target_pairs={{0,16},{4,20},{8,24},{12,28},{16,0},{20,4},{24,8},{28,12},{1,17},{... | collective-permute-start | bytes 786440 | tf_op jit(solution)/shard_map/ppermute | solution.py:31
  98.7 5.9 %collective-permute-done.21 = bf16[128,1024]{1,0:T(8,128)(2,1)S(1)} collective-permute-done((bf16[128,1024]{1,0:T(8,128)(2,1)S(1)}, bf16[128,1024]{1,0:T(8,128)(2,1)S(1)}, u32[]{:S(2)}, u32[]{:S(2)}) %collective-permute-start.21) | collective-permute-done | bytes 262176 | tf_op jit(solution)/shard_map/ppermute | solution.py:31
  105.7 4.6 %collective-permute-done.18.refs_5_ = bf16[4,3,32,1024]{3,2,1,0:T(8,128)(2,1)S(1)} collective-permute-done((bf16[4,3,32,1024]{3,2,1,0:T(8,128)(2,1)S(1)}, bf16[4,3,32,1024]{3,2,1,0:T(8,128)(2,1)S(1)}, u32[]{:S(2)}, u32[]{:S(2)}) %collective-permute-start.18) | collective-permute-done | bytes 786464 | tf_op jit(solution)/shard_map/ppermute | solution.py:31
  110.4 3.3 %first_norm.1 = (bf16[256,1024]{1,0:T(8,128)(2,1)S(1)}, bf16[256,1024]{1,0:T(8,128)(2,1)S(1)}) custom-call(s32[2]{0:T(128)S(1)} %pad_add_fusion.place_ref, bf16[256,1024]{1,0:T(8,128)(2,1)S(1)} %copy-done.3, bf16[256,1024]{1,0:T(8,128)(2,1)S(1)} %collective-permute-done.refs_1_.partner_ref, bf16[256,1024]{1,0:T(8,128)(2,1)S(1)} %copy-done.13, ...), custom_call_target="tpu_custom_call" | custom-call | flops 1 | bytes 1 | tf_op jit(solution)/shard_map/first_norm/pallas_call | solution.py:256
  113.6 3.9 %feed_partner.1 = bf16[256,1024]{1,0:T(8,128)(2,1)S(1)} custom-call(s32[2]{0:T(128)S(1)} %pad_add_fusion.place_ref, bf16[256,1024]{1,0:T(8,128)(2,1)S(1)} %get-tuple-element.40.rows_ref, bf16[1024,1024]{1,0:T(8,128)(2,1)S(1)} %copy-done, bf16[1024,1024]{1,0:T(8,128)(2,1)S(1)} %copy-done.1, bf16[1024,1024]{1,0:T(8,128)(2,1)S(1)} %constant_dynamic-update-slice_fusion.held_ref, ...), custom_call_target="tpu_custom_call" | custom-call | flops 1 | bytes 1 | tf_op jit(solution)/shard_map/feed_partner/pallas_call | solution.py:325
  117.6 1.8 %collective-permute-start.24 = (bf16[256,1024]{1,0:T(8,128)(2,1)S(1)}, bf16[256,1024]{1,0:T(8,128)(2,1)S(1)}, u32[]{:S(2)}, u32[]{:S(2)}) collective-permute-start(bf16[256,1024]{1,0:T(8,128)(2,1)S(1)} %feed_partner.1), channel_id=1, source_target_pairs={{0,1},{1,0},{2,3},{3,2},{4,5},{5,4},{6,7},{7,6},{8,9},{9,8},{10,11... | collective-permute-start | bytes 1572872 | tf_op jit(solution)/shard_map/ppermute | solution.py:31
  119.7 1.8 %collective-permute-start.26 = (f32[3,2,1024]{2,1,0:T(2,128)S(1)}, f32[3,2,1024]{2,1,0:T(2,128)S(1)}, u32[]{:S(2)}, u32[]{:S(2)}) collective-permute-start(f32[3,2,1024]{2,1,0:T(2,128)S(1)} %get-tuple-element.55), channel_id=1, source_target_pairs={{0,2},{1,3},{2,0},{3,1},{4,6},{5,7},{6,4},{7,5},{8,10},{9,11},{10,... | collective-permute-start | bytes 73736 | tf_op jit(solution)/shard_map/ppermute | solution.py:31
  121.5 2.3 %collective-permute-start.27 = (f32[3,2,1024]{2,1,0:T(2,128)S(1)}, f32[3,2,1024]{2,1,0:T(2,128)S(1)}, u32[]{:S(2)}, u32[]{:S(2)}) collective-permute-start(f32[3,2,1024]{2,1,0:T(2,128)S(1)} %get-tuple-element.54), channel_id=1, source_target_pairs={{0,3},{1,2},{2,1},{3,0},{4,7},{5,6},{6,5},{7,4},{8,11},{9,10},{10,... | collective-permute-start | bytes 73736 | tf_op jit(solution)/shard_map/ppermute | solution.py:31
  123.8 3.9 %feed_own.1.near_ref = f32[256,1024]{1,0:T(8,128)S(1)} custom-call(s32[2]{0:T(128)S(1)} %pad_add_fusion.place_ref, bf16[256,1024]{1,0:T(8,128)(2,1)S(1)} %get-tuple-element.44.rows_ref.normed_ref, bf16[1024,1024]{1,0:T(8,128)(2,1)S(1)} %copy-done, bf16[1024,1024]{1,0:T(8,128)(2,1)S(1)} %copy-done.1, ...), custom_call_target="tpu_custom_call" | custom-call | flops 1 | bytes 1 | tf_op jit(solution)/shard_map/feed_own/pallas_call | solution.py:325
  127.7 4.9 %collective-permute-done.25 = f32[3,2,1024]{2,1,0:T(2,128)S(1)} collective-permute-done((f32[3,2,1024]{2,1,0:T(2,128)S(1)}, f32[3,2,1024]{2,1,0:T(2,128)S(1)}, u32[]{:S(2)}, u32[]{:S(2)}) %collective-permute-start.25) | collective-permute-done | bytes 24608 | tf_op jit(solution)/shard_map/ppermute | solution.py:31
  132.6 1.8 %collective-permute-done.27 = f32[3,2,1024]{2,1,0:T(2,128)S(1)} collective-permute-done((f32[3,2,1024]{2,1,0:T(2,128)S(1)}, f32[3,2,1024]{2,1,0:T(2,128)S(1)}, u32[]{:S(2)}, u32[]{:S(2)}) %collective-permute-start.27) | collective-permute-done | bytes 24608 | tf_op jit(solution)/shard_map/ppermute | solution.py:31
  (119 shorter events, 22.1 us)
Async XLA Ops:
  0.6 26.6 %copy-start.28 = (bf16[2,1024]{1,0:T(2,128)(2,1)S(1)}, bf16[2,1024]{1,0:T(2,128)(2,1)}, u32[]{:S(2)}) copy-start(bf16[2,1024]{1,0:T(2,128)(2,1)} %param.24) | copy-start | bytes 12292
  0.6 26.6 %copy-start.18 = (s32[1,6]{1,0:T(1,128)S(1)}, s32[1,6]{1,0:T(1,128)}, u32[]{:S(2)}) copy-start(s32[1,6]{1,0:T(1,128)} %param.27) | copy-start | bytes 76
  0.7 13.3 %collective-permute-start.7 = (bf16[256,1024]{1,0:T(8,128)(2,1)}, bf16[256,1024]{1,0:T(8,128)(2,1)S(1)}, u32[]{:S(2)}, u32[]{:S(2)}) collective-permute-start(bf16[256,1024]{1,0:T(8,128)(2,1)} %own_ref.1), channel_id=1, source_target_pairs={{1,2},{2,1},{5,6},{6,5},{9,10},{10,9},{13,14},{14,13},{17,18},{18,... | collective-permute-start | bytes 1572872 | tf_op jit(solution)/shard_map/ppermute | solution.py:37
  1.5 20.0 %collective-permute-start = (bf16[256,1024]{1,0:T(8,128)(2,1)}, bf16[256,1024]{1,0:T(8,128)(2,1)S(1)}, u32[]{:S(2)}, u32[]{:S(2)}) collective-permute-start(bf16[256,1024]{1,0:T(8,128)(2,1)} %own_ref.1), channel_id=1, source_target_pairs={{0,1},{2,3},{1,0},{3,2},{4,5},{6,7},{5,4},{7,6},{8,9},{10,11},{9,8... | collective-permute-start | bytes 1572872 | tf_op jit(solution)/shard_map/ppermute | solution.py:37
  8.9 15.2 %collective-permute-start.3 = (bf16[34,1024]{1,0:T(8,128)(2,1)S(1)}, bf16[34,1024]{1,0:T(8,128)(2,1)S(1)}, u32[]{:S(2)}, u32[]{:S(2)}) collective-permute-start(bf16[34,1024]{1,0:T(8,128)(2,1)S(1)} %pad_maximum_fusion.3), channel_id=1, source_target_pairs={{0,3},{1,2},{2,1},{3,0},{4,7},{5,6},{6,5},{7,4},{8,11},{9,10},{10,... | collective-permute-start | bytes 208904 | tf_op jit(solution)/shard_map/ppermute | solution.py:31
  10.3 16.9 %collective-permute-start.2 = (bf16[34,1024]{1,0:T(8,128)(2,1)S(1)}, bf16[34,1024]{1,0:T(8,128)(2,1)S(1)}, u32[]{:S(2)}, u32[]{:S(2)}) collective-permute-start(bf16[34,1024]{1,0:T(8,128)(2,1)S(1)} %pad_maximum_fusion.3), channel_id=1, source_target_pairs={{0,2},{1,3},{2,0},{3,1},{4,6},{5,7},{6,4},{7,5},{8,10},{9,11},{10,... | collective-permute-start | bytes 208904 | tf_op jit(solution)/shard_map/ppermute | solution.py:31
  10.4 16.8 %collective-permute-start.1 = (bf16[34,1024]{1,0:T(8,128)(2,1)S(1)}, bf16[34,1024]{1,0:T(8,128)(2,1)S(1)}, u32[]{:S(2)}, u32[]{:S(2)}) collective-permute-start(bf16[34,1024]{1,0:T(8,128)(2,1)S(1)} %pad_maximum_fusion.3), channel_id=1, source_target_pairs={{0,1},{1,0},{2,3},{3,2},{4,5},{5,4},{6,7},{7,6},{8,9},{9,8},{10,11... | collective-permute-start | bytes 208904 | tf_op jit(solution)/shard_map/ppermute | solution.py:31
  14.0 21.8 %collective-permute-start.8 = (bf16[256,1024]{1,0:T(8,128)(2,1)S(1)}, bf16[256,1024]{1,0:T(8,128)(2,1)S(1)}, u32[]{:S(2)}, u32[]{:S(2)}) collective-permute-start(bf16[256,1024]{1,0:T(8,128)(2,1)S(1)} %collective-permute-done.7.refs_4_), channel_id=1, source_target_pairs={{1,0},{2,3},{5,4},{6,7},{9,8},{10,11},{13,12},{14,15},{17,16},{18,... | collective-permute-start | bytes 1572872 | tf_op jit(solution)/shard_map/ppermute | solution.py:475
  21.5 11.4 %collective-permute-start.9 = (bf16[256,1024]{1,0:T(8,128)(2,1)S(1)}, bf16[256,1024]{1,0:T(8,128)(2,1)S(1)}, u32[]{:S(2)}, u32[]{:S(2)}) collective-permute-start(bf16[256,1024]{1,0:T(8,128)(2,1)S(1)} %collective-permute-done.refs_1_.partner_ref), channel_id=1, source_target_pairs={{1,2},{2,1},{5,6},{6,5},{9,10},{10,9},{13,14},{14,13},{17,18},{18,... | collective-permute-start | bytes 1572872 | tf_op jit(solution)/shard_map/ppermute | solution.py:37
  29.2 23.8 %copy-start.2 = (bf16[1024,3,256]{2,0,1:T(8,128)(2,1)S(1)}, bf16[1024,3,256]{2,0,1:T(8,128)(2,1)}, u32[]{:S(2)}) copy-start(bf16[1024,3,256]{2,0,1:T(8,128)(2,1)} %param.15) | copy-start | bytes 4718596
  29.2 23.8 %copy-start.3 = (bf16[256,1024]{1,0:T(8,128)(2,1)S(1)}, bf16[256,1024]{1,0:T(8,128)(2,1)}, u32[]{:S(2)}) copy-start(bf16[256,1024]{1,0:T(8,128)(2,1)} %own_ref.1) | copy-start | bytes 1572868
  33.0 16.0 %collective-permute-start.10 = (bf16[256,1024]{1,0:T(8,128)(2,1)S(1)}, bf16[256,1024]{1,0:T(8,128)(2,1)S(1)}, u32[]{:S(2)}, u32[]{:S(2)}) collective-permute-start(bf16[256,1024]{1,0:T(8,128)(2,1)S(1)} %collective-permute-done.9.refs_5_), channel_id=1, source_target_pairs={{1,0},{2,3},{5,4},{6,7},{9,8},{10,11},{13,12},{14,15},{17,16},{18,... | collective-permute-start | bytes 1572872 | tf_op jit(solution)/shard_map/ppermute | solution.py:480
  35.7 15.8 %collective-permute-start.11 = (bf16[256,1024]{1,0:T(8,128)(2,1)}, bf16[256,1024]{1,0:T(8,128)(2,1)S(1)}, u32[]{:S(2)}, u32[]{:S(2)}) collective-permute-start(bf16[256,1024]{1,0:T(8,128)(2,1)} %pad_maximum_fusion.1), channel_id=1, source_target_pairs={{0,2},{3,1},{4,6},{7,5},{8,10},{11,9},{12,14},{15,13},{16,18},{19,... | collective-permute-start | bytes 1572872 | tf_op jit(solution)/shard_map/ppermute | solution.py:486
  42.9 10.0 %collective-permute-start.4 = (bf16[3,32,1024]{2,1,0:T(8,128)(2,1)S(1)}, bf16[3,32,1024]{2,1,0:T(8,128)(2,1)S(1)}, u32[]{:S(2)}, u32[]{:S(2)}) collective-permute-start(bf16[3,32,1024]{2,1,0:T(8,128)(2,1)S(1)} %get-tuple-element.53), channel_id=1, source_target_pairs={{0,8},{4,12},{8,0},{12,4},{16,24},{20,28},{24,16},{28,20},{1,9},{5... | collective-permute-start | bytes 589832 | tf_op jit(solution)/shard_map/ppermute | solution.py:31
  44.4 8.6 %collective-permute-start.5 = (bf16[3,32,1024]{2,1,0:T(8,128)(2,1)S(1)}, bf16[3,32,1024]{2,1,0:T(8,128)(2,1)S(1)}, u32[]{:S(2)}, u32[]{:S(2)}) collective-permute-start(bf16[3,32,1024]{2,1,0:T(8,128)(2,1)S(1)} %get-tuple-element.53), channel_id=1, source_target_pairs={{0,16},{4,20},{8,24},{12,28},{16,0},{20,4},{24,8},{28,12},{1,17},{... | collective-permute-start | bytes 589832 | tf_op jit(solution)/shard_map/ppermute | solution.py:31
  45.9 7.0 %collective-permute-start.6 = (bf16[3,32,1024]{2,1,0:T(8,128)(2,1)S(1)}, bf16[3,32,1024]{2,1,0:T(8,128)(2,1)S(1)}, u32[]{:S(2)}, u32[]{:S(2)}) collective-permute-start(bf16[3,32,1024]{2,1,0:T(8,128)(2,1)S(1)} %get-tuple-element.53), channel_id=1, source_target_pairs={{0,24},{4,28},{8,16},{12,20},{16,8},{20,12},{24,0},{28,4},{1,25},{... | collective-permute-start | bytes 589832 | tf_op jit(solution)/shard_map/ppermute | solution.py:31
  51.5 16.7 %collective-permute-start.12 = (bf16[256,1024]{1,0:T(8,128)(2,1)}, bf16[256,1024]{1,0:T(8,128)(2,1)}, u32[]{:S(2)}, u32[]{:S(2)}) collective-permute-start(bf16[256,1024]{1,0:T(8,128)(2,1)} %pad_maximum_fusion.1), channel_id=1, source_target_pairs={{1,3},{2,0},{5,7},{6,4},{9,11},{10,8},{13,15},{14,12},{17,19},{18,... | collective-permute-start | bytes 1572872 | tf_op jit(solution)/shard_map/ppermute | solution.py:487
  56.2 6.8 %collective-permute-start.13 = (bf16[256,512]{1,0:T(8,128)(2,1)}, bf16[256,512]{1,0:T(8,128)(2,1)S(1)}, u32[]{:S(2)}, u32[]{:S(2)}) collective-permute-start(bf16[256,512]{1,0:T(8,128)(2,1)} %get-tuple-element.34), channel_id=1, source_target_pairs={{0,4},{8,12},{16,20},{24,28},{4,0},{12,8},{20,16},{28,24},{1,5},{9... | collective-permute-start | bytes 786440 | tf_op jit(solution)/shard_map/ppermute | solution.py:37
  56.2 6.8 %collective-permute-start.14 = (bf16[256,512]{1,0:T(8,128)(2,1)}, bf16[256,512]{1,0:T(8,128)(2,1)}, u32[]{:S(2)}, u32[]{:S(2)}) collective-permute-start(bf16[256,512]{1,0:T(8,128)(2,1)} %get-tuple-element.35), channel_id=1, source_target_pairs={{4,8},{12,16},{20,24},{8,4},{16,12},{24,20},{5,9},{13,17},{21,25},... | collective-permute-start | bytes 786440 | tf_op jit(solution)/shard_map/ppermute | solution.py:37
  69.5 26.9 %collective-permute-start.20 = (bf16[256,1024]{1,0:T(8,128)(2,1)S(1)}, bf16[256,1024]{1,0:T(8,128)(2,1)S(1)}, u32[]{:S(2)}, u32[]{:S(2)}) collective-permute-start(bf16[256,1024]{1,0:T(8,128)(2,1)S(1)} %get-tuple-element.51), channel_id=1, source_target_pairs={{0,16},{4,20},{8,24},{12,28},{16,0},{20,4},{24,8},{28,12},{1,17},{... | collective-permute-start | bytes 1572872 | tf_op jit(solution)/shard_map/ppermute | solution.py:31
  75.7 21.2 %collective-permute-start.19 = (bf16[256,1024]{1,0:T(8,128)(2,1)S(1)}, bf16[256,1024]{1,0:T(8,128)(2,1)S(1)}, u32[]{:S(2)}, u32[]{:S(2)}) collective-permute-start(bf16[256,1024]{1,0:T(8,128)(2,1)S(1)} %get-tuple-element.51), channel_id=1, source_target_pairs={{0,8},{4,12},{8,0},{12,4},{16,24},{20,28},{24,16},{28,20},{1,9},{5... | collective-permute-start | bytes 1572872 | tf_op jit(solution)/shard_map/ppermute | solution.py:31
  76.0 15.1 %collective-permute-start.16 = (bf16[512,256]{1,0:T(8,128)(2,1)S(1)}, bf16[512,256]{1,0:T(8,128)(2,1)S(1)}, u32[]{:S(2)}, u32[]{:S(2)}) collective-permute-start(bf16[512,256]{1,0:T(8,128)(2,1)S(1)} %attend_far.1), channel_id=1, source_target_pairs={{0,2},{1,3},{2,0},{3,1},{4,6},{5,7},{6,4},{7,5},{8,10},{9,11},{10,... | collective-permute-start | bytes 786440 | tf_op jit(solution)/shard_map/ppermute | solution.py:31
  85.3 11.1 %collective-permute-start.15 = (bf16[512,256]{1,0:T(8,128)(2,1)S(1)}, bf16[512,256]{1,0:T(8,128)(2,1)S(1)}, u32[]{:S(2)}, u32[]{:S(2)}) collective-permute-start(bf16[512,256]{1,0:T(8,128)(2,1)S(1)} %attend_near.1.refs_0_), channel_id=1, source_target_pairs={{0,1},{1,0},{2,3},{3,2},{4,5},{5,4},{6,7},{7,6},{8,9},{9,8},{10,11... | collective-permute-start | bytes 786440 | tf_op jit(solution)/shard_map/ppermute | solution.py:31
  96.4 8.1 %collective-permute-start.21 = (bf16[128,1024]{1,0:T(8,128)(2,1)S(1)}, bf16[128,1024]{1,0:T(8,128)(2,1)S(1)}, u32[]{:S(2)}, u32[]{:S(2)}) collective-permute-start(bf16[128,1024]{1,0:T(8,128)(2,1)S(1)} %slice.82), channel_id=1, source_target_pairs={{0,8},{4,12},{8,0},{12,4},{16,24},{20,28},{24,16},{28,20},{1,9},{5... | collective-permute-start | bytes 786440 | tf_op jit(solution)/shard_map/ppermute | solution.py:31
  96.9 8.1 %collective-permute-start.17 = (bf16[512,256]{1,0:T(8,128)(2,1)S(1)}, bf16[512,256]{1,0:T(8,128)(2,1)S(1)}, u32[]{:S(2)}, u32[]{:S(2)}) collective-permute-start(bf16[512,256]{1,0:T(8,128)(2,1)S(1)} %collective-permute-done.16.refs_2_), channel_id=1, source_target_pairs={{0,1},{1,0},{2,3},{3,2},{4,5},{5,4},{6,7},{7,6},{8,9},{9,8},{10,11... | collective-permute-start | bytes 786440 | tf_op jit(solution)/shard_map/ppermute | solution.py:31
  96.9 8.0 %collective-permute-start.22 = (bf16[128,1024]{1,0:T(8,128)(2,1)S(1)}, bf16[128,1024]{1,0:T(8,128)(2,1)S(1)}, u32[]{:S(2)}, u32[]{:S(2)}) collective-permute-start(bf16[128,1024]{1,0:T(8,128)(2,1)S(1)} %slice.83), channel_id=1, source_target_pairs={{0,16},{4,20},{8,24},{12,28},{16,0},{20,4},{24,8},{28,12},{1,17},{... | collective-permute-start | bytes 786440 | tf_op jit(solution)/shard_map/ppermute | solution.py:31
  105.0 8.6 %collective-permute-start.23 = (bf16[1024,1024]{1,0:T(8,128)(2,1)S(1)}, bf16[1024,1024]{1,0:T(8,128)(2,1)S(1)}, u32[]{:S(2)}, u32[]{:S(2)}) collective-permute-start(bf16[1024,1024]{1,0:T(8,128)(2,1)S(1)} %constant_dynamic-update-slice_fusion.held_ref), channel_id=1, source_target_pairs={{0,4},{4,0},{8,12},{12,8},{16,20},{20,16},{24,28},{28,24},{1,5},{5... | collective-permute-start | bytes 6291464 | tf_op jit(solution)/shard_map/ppermute | solution.py:31
  105.2 5.1 %collective-permute-start.18 = (bf16[4,3,32,1024]{3,2,1,0:T(8,128)(2,1)S(1)}, bf16[4,3,32,1024]{3,2,1,0:T(8,128)(2,1)S(1)}, u32[]{:S(2)}, u32[]{:S(2)}) collective-permute-start(bf16[4,3,32,1024]{3,2,1,0:T(8,128)(2,1)S(1)} %pad_maximum_fusion.refs_4_), channel_id=1, source_target_pairs={{0,4},{4,0},{8,12},{12,8},{16,20},{20,16},{24,28},{28,24},{1,5},{5... | collective-permute-start | bytes 2359304 | tf_op jit(solution)/shard_map/ppermute | solution.py:31
  117.6 17.5 %collective-permute-start.24 = (bf16[256,1024]{1,0:T(8,128)(2,1)S(1)}, bf16[256,1024]{1,0:T(8,128)(2,1)S(1)}, u32[]{:S(2)}, u32[]{:S(2)}) collective-permute-start(bf16[256,1024]{1,0:T(8,128)(2,1)S(1)} %feed_partner.1), channel_id=1, source_target_pairs={{0,1},{1,0},{2,3},{3,2},{4,5},{5,4},{6,7},{7,6},{8,9},{9,8},{10,11... | collective-permute-start | bytes 1572872 | tf_op jit(solution)/shard_map/ppermute | solution.py:31
  119.4 13.3 %collective-permute-start.25 = (f32[3,2,1024]{2,1,0:T(2,128)S(1)}, f32[3,2,1024]{2,1,0:T(2,128)S(1)}, u32[]{:S(2)}, u32[]{:S(2)}) collective-permute-start(f32[3,2,1024]{2,1,0:T(2,128)S(1)} %get-tuple-element.56), channel_id=1, source_target_pairs={{0,1},{1,0},{2,3},{3,2},{4,5},{5,4},{6,7},{7,6},{8,9},{9,8},{10,11... | collective-permute-start | bytes 73736 | tf_op jit(solution)/shard_map/ppermute | solution.py:31
  119.7 12.9 %collective-permute-start.26 = (f32[3,2,1024]{2,1,0:T(2,128)S(1)}, f32[3,2,1024]{2,1,0:T(2,128)S(1)}, u32[]{:S(2)}, u32[]{:S(2)}) collective-permute-start(f32[3,2,1024]{2,1,0:T(2,128)S(1)} %get-tuple-element.55), channel_id=1, source_target_pairs={{0,2},{1,3},{2,0},{3,1},{4,6},{5,7},{6,4},{7,5},{8,10},{9,11},{10,... | collective-permute-start | bytes 73736 | tf_op jit(solution)/shard_map/ppermute | solution.py:31
  121.5 12.9 %collective-permute-start.27 = (f32[3,2,1024]{2,1,0:T(2,128)S(1)}, f32[3,2,1024]{2,1,0:T(2,128)S(1)}, u32[]{:S(2)}, u32[]{:S(2)}) collective-permute-start(f32[3,2,1024]{2,1,0:T(2,128)S(1)} %get-tuple-element.54), channel_id=1, source_target_pairs={{0,3},{1,2},{2,1},{3,0},{4,7},{5,6},{6,5},{7,4},{8,11},{9,10},{10,... | collective-permute-start | bytes 73736 | tf_op jit(solution)/shard_map/ppermute | solution.py:31
  (26 other events, 220.5 us)

commit v13 on v12

--- a/solution.py
+++ b/solution.py
@@ -47,81 +47,75 @@
     return center * lax.rsqrt(spread + LN_EPS) * gain + bias
 
 
-def shard_copies(kv, shards, rows_ref, sems, first, step):
-    own, a1, a2, a3, b1, b2 = shards
+def project_early_kernel(place_ref, weight_ref, own, a1, a2, b1, b2, query_ref, keyval_ref, rows_ref, sems):
+    kv = place_ref[1]
     count = own.shape[0]
     inner = (kv == 1) | (kv == 2)
     outer = jnp.logical_not(inner)
-    always = kv >= 0
-    sources = ((own, 0, always), (a1, 1, always), (a2, 2, outer), (b2, 2, inner), (a3, 3, outer), (b1, 3, inner))
     copies = []
-    for index, (source, flip, held) in enumerate(sources):
-        for slot in range(rows_ref.shape[0] // count):
-            needed = held & ((kv ^ flip) == first + slot * step)
-            target = rows_ref.at[slot * count : (slot + 1) * count]
-            copies.append((needed, pltpu.make_async_copy(source, target, sems.at[index])))
+    for source, flip, needed in ((own, 0, None), (a1, 1, None), (a2, 2, outer), (b2, 2, inner), (b1, 3, inner)):
+        at = pl.ds(pl.multiple_of((kv ^ flip) * count, count), count)
+        copies.append((needed, pltpu.make_async_copy(source, rows_ref.at[at], sems.at[len(copies)])))
     for needed, copy in copies:
-        pl.when(needed)(copy.start)
+        copy.start() if needed is None else pl.when(needed)(copy.start)
     for needed, copy in copies:
-        pl.when(needed)(copy.wait)
-
-
-def keys_values(rows, weight_ref, keyval_ref):
+        copy.wait() if needed is None else pl.when(needed)(copy.wait)
+    project_rows(rows_ref[...], weight_ref, query_ref, keyval_ref)
+
+
+def project_rows(rows, weight_ref, query_ref, keyval_ref):
     width = weight_ref.shape[2]
+    query = jnp.dot(rows, weight_ref[0], preferred_element_type=F32) * (1.0 / math.sqrt(HD))
+    query_ref[...] = query.astype(BF16)
     for part in range(2):
         at = slice(part * width, (part + 1) * width)
         keyval_ref[:, at] = jnp.dot(rows, weight_ref[part + 1], preferred_element_type=F32).astype(BF16)
 
 
-def project_edges_kernel(place_ref, weight_ref, *refs):
-    shards, (keyval_ref, even_ref, odd_ref, rows_ref, sems) = refs[:-5], refs[-5:]
+def project_last_kernel(place_ref, weight_ref, keyval_ref, a3_ref, query_ref, last_ref, even_ref, odd_ref):
     tok, kv = place_ref[0], place_ref[1]
-    count = even_ref.shape[0]
-    shard_copies(kv, shards, rows_ref, sems, 0, 3)
-    keys_values(rows_ref[...], weight_ref, keyval_ref)
-
-    @pl.when(tok % 2 == 0)
-    def _():
-        even_ref[...] = keyval_ref[count:]
-        odd_ref[...] = keyval_ref[:count]
-
-    @pl.when(tok % 2 == 1)
-    def _():
-        even_ref[...] = keyval_ref[:count]
-        odd_ref[...] = keyval_ref[count:]
-
-
-def project_rest_kernel(place_ref, weight_ref, *refs):
-    shards, (query_ref, keyval_ref, rows_ref, sems) = refs[:-4], refs[-4:]
-    count = shards[0].shape[0]
-    shard_copies(place_ref[1], shards, rows_ref, sems, 0, 1)
-    keys_values(rows_ref[count:-count], weight_ref, keyval_ref)
-    query = jnp.dot(rows_ref[...], weight_ref[0], preferred_element_type=F32) * (1.0 / math.sqrt(HD))
-    query_ref[...] = query.astype(BF16)
-
-
-def project(place, weight, shards, blocks, edges):
+    count = a3_ref.shape[0]
+    project_rows(a3_ref[...], weight_ref, query_ref, last_ref)
+    last = last_ref[...]
+    blocks = keyval_ref.shape[0] // count
+    top = jnp.where(kv == blocks - 1, last, keyval_ref[:count])
+    bottom = jnp.where(kv == 0, last, keyval_ref[(blocks - 1) * count :])
+    even_tok = tok % 2 == 0
+    even_ref[...] = jnp.where(even_tok, bottom, top)
+    odd_ref[...] = jnp.where(even_tok, top, bottom)
+
+
+def project_early(place, weight, blocks, shards):
     rows, width = shards[0].shape
     heads_width = weight.shape[2]
-    shape = lambda count, columns: jax.ShapeDtypeStruct((count * rows, columns), BF16)
-    keyval = shape(2, 2 * heads_width)
-    if edges:
-        outs = (keyval, shape(1, 2 * heads_width), shape(1, 2 * heads_width))
-    else:
-        outs = (shape(blocks, heads_width), keyval)
     return pl.pallas_call(
-        project_edges_kernel if edges else project_rest_kernel,
-        out_shape=outs,
+        project_early_kernel,
+        out_shape=(
+            jax.ShapeDtypeStruct((blocks * rows, heads_width), BF16),
+            jax.ShapeDtypeStruct((blocks * rows, 2 * heads_width), BF16),
+        ),
         in_specs=[SMEM, VMEM] + [ANY] * len(shards),
-        out_specs=(VMEM,) * len(outs),
-        scratch_shapes=[
-            pltpu.VMEM((2 * rows if edges else blocks * rows, width), BF16),
-            pltpu.SemaphoreType.DMA((len(shards),)),
-        ],
+        out_specs=(VMEM,) * 2,
+        scratch_shapes=[pltpu.VMEM((blocks * rows, width), BF16), pltpu.SemaphoreType.DMA((len(shards),))],
         compiler_params=pltpu.CompilerParams(vmem_limit_bytes=12 * MIB),
         cost_estimate=SHORT,
-        name="project_edges" if edges else "project_rest",
+        name="project_early",
     )(place, weight, *shards)
+
+
+def project_last(place, weight, keyval, a3):
+    rows = a3.shape[0]
+    heads_width = weight.shape[2]
+    keyvals = jax.ShapeDtypeStruct((rows, 2 * heads_width), BF16)
+    return pl.pallas_call(
+        project_last_kernel,
+        out_shape=(jax.ShapeDtypeStruct((rows, heads_width), BF16), keyvals, keyvals, keyvals),
+        in_specs=[SMEM] + [VMEM] * 3,
+        out_specs=(VMEM,) * 4,
+        compiler_params=pltpu.CompilerParams(vmem_limit_bytes=8 * MIB),
+        cost_estimate=SHORT,
+        name="project_last",
+    )(place, weight, keyval, a3)
 
 
 def window_bias(first, count, starts, ends):
@@ -160,62 +154,68 @@
         out_ref[:, start : start + 2 * HD] = jnp.where(lane < HD, halves[0], halves[1]).astype(BF16)
 
 
-def attend_kernel(flips, place_ref, starts_ref, ends_ref, query_ref, middle_ref, edges_ref, even_ref, odd_ref, *refs):
+def attend_kernel(flips, has_last, has_halo, joins, place_ref, starts_ref, ends_ref, query_ref, keyval_ref, *refs):
+    refs = list(refs)
+    last_query_ref, last_ref = (refs.pop(0), refs.pop(0)) if has_last else (None, None)
+    even_ref, odd_ref = (refs.pop(0), refs.pop(0)) if has_halo else (None, None)
+    earlier_ref = refs.pop(0) if joins else None
     out_ref, window_ref, bias_ref, scores_ref, weights_ref, sems = refs
     tok, kv = place_ref[0], place_ref[1]
-    count = out_ref.shape[0] // len(flips)
+    count = bias_ref.shape[0]
     blocks = query_ref.shape[0] // count
+    inner = (kv == 1) | (kv == 2)
+    block = kv ^ jnp.where(inner, flips[1], flips[0])
+    missing = jnp.where(inner, -1, kv ^ 3)
     copies = []
-    for index, flip in enumerate(flips):
-        block = kv ^ flip
-        for part in range(3):
-            target = window_ref.at[index, part * count : (part + 1) * count]
-            sem = sems.at[index, part]
-            at = block + part - 1
-            middle = (at > 0) & (at < blocks - 1)
-            start = jnp.where(middle, at - 1, 0)
-            source = middle_ref.at[pl.ds(pl.multiple_of(start * count, count), count)]
-            copies.append((index, middle, pltpu.make_async_copy(source, target, sem)))
-            for slot, edge in enumerate((0, blocks - 1)):
-                source = edges_ref.at[slot * count : (slot + 1) * count]
-                copies.append((index, at == edge, pltpu.make_async_copy(source, target, sem)))
-            for first_edge, outside in ((tok % 2 == 1, at < 0), (tok % 2 == 0, at >= blocks)):
-                if part != 1:
-                    copies.append((index, outside & first_edge, pltpu.make_async_copy(even_ref, target, sem)))
-                    other = jnp.logical_not(first_edge)
-                    copies.append((index, outside & other, pltpu.make_async_copy(odd_ref, target, sem)))
-    for _, needed, copy in copies:
+    for part in range(3):
+        target = window_ref.at[part * count : (part + 1) * count]
+        sem = sems.at[part]
+        at = block + part - 1
+        held = (at >= 0) & (at < blocks) & (at != missing)
+        source = keyval_ref.at[pl.ds(pl.multiple_of(jnp.where(held, at, 0) * count, count), count)]
+        copies.append((held, pltpu.make_async_copy(source, target, sem)))
+        if has_last:
+            copies.append((at == missing, pltpu.make_async_copy(last_ref, target, sem)))
+        if has_halo and part != 1:
+            outside = at < 0 if part == 0 else at >= blocks
+            over_even = tok % 2 == (1 if part == 0 else 0)
+            copies.append((outside & over_even, pltpu.make_async_copy(even_ref, target, sem)))
+            copies.append((outside & jnp.logical_not(over_even), pltpu.make_async_copy(odd_ref, target, sem)))
+    for needed, copy in copies:
         pl.when(needed)(copy.start)
-    for index, flip in enumerate(flips):
-        block = kv ^ flip
-        first = (tok * blocks + block) * count
-        bias_ref[...] = window_bias(first, count, starts_ref[...], ends_ref[...])
-        for owner, needed, copy in copies:
-            if owner == index:
-                pl.when(needed)(copy.wait)
-        query = query_ref[pl.ds(pl.multiple_of(block * count, count), count)]
-        out = out_ref.at[index * count : (index + 1) * count]
-        attend(query, window_ref.at[index], bias_ref, scores_ref, weights_ref, out)
-
-
-def attend_blocks(place, starts, ends, query, middle, edges, even, odd, rows, flips, name):
+    first = (tok * blocks + block) * count
+    bias_ref[...] = window_bias(first, count, starts_ref[...], ends_ref[...])
+    query = query_ref[pl.ds(pl.multiple_of(block * count, count), count)]
+    if has_last:
+        query = jnp.where(block == missing, last_query_ref[...], query)
+    for needed, copy in copies:
+        pl.when(needed)(copy.wait)
+    if joins:
+        half = jnp.where(inner, flips[1] % 2, flips[0] % 2)
+        out_ref[pl.ds(pl.multiple_of((1 - half) * count, count), count)] = earlier_ref[...]
+        out_ref = out_ref.at[pl.ds(pl.multiple_of(half * count, count), count)]
+    attend(query, window_ref, bias_ref, scores_ref, weights_ref, out_ref)
+
+
+def attend_block(place, starts, ends, query, keyval, flips, name, last=(), halo=(), earlier=()):
+    rows = query.shape[0] // lax.axis_size("kv")
     heads_width = query.shape[1]
     return pl.pallas_call(
-        functools.partial(attend_kernel, flips),
-        out_shape=jax.ShapeDtypeStruct((len(flips) * rows, heads_width), BF16),
-        in_specs=[SMEM, VMEM, VMEM, VMEM, ANY, ANY, ANY, ANY],
+        functools.partial(attend_kernel, flips, bool(last), bool(halo), bool(earlier)),
+        out_shape=jax.ShapeDtypeStruct(((1 + len(earlier)) * rows, heads_width), BF16),
+        in_specs=[SMEM, VMEM, VMEM, VMEM, ANY] + [VMEM, ANY][: len(last)] + [ANY] * len(halo) + [VMEM] * len(earlier),
         out_specs=VMEM,
         scratch_shapes=[
-            pltpu.VMEM((len(flips), 3 * rows, 2 * heads_width), BF16),
+            pltpu.VMEM((3 * rows, 2 * heads_width), BF16),
             pltpu.VMEM((rows, 3 * rows), F32),
             pltpu.VMEM((heads_width // HD, rows, 3 * rows), F32),
             pltpu.VMEM((heads_width // HD, rows, 3 * rows), BF16),
-            pltpu.SemaphoreType.DMA((len(flips), 3)),
+            pltpu.SemaphoreType.DMA((3,)),
         ],
-        compiler_params=pltpu.CompilerParams(vmem_limit_bytes=14 * MIB),
+        compiler_params=pltpu.CompilerParams(vmem_limit_bytes=12 * MIB),
         cost_estimate=SHORT,
         name=name,
-    )(place, starts, ends, query, middle, edges, even, odd)
+    )(place, starts, ends, query, keyval, *last, *halo, *earlier)
 
 
 def first_norm_kernel(layout, place_ref, own_ref, partner_ref, own_out_ref, gain_ref, bias_ref, *refs):
@@ -479,12 +479,7 @@
     out_x, out_y = swapped(out_here, "tok", 2), swapped(out_here, "tok", 4)
     a3 = lax.ppermute(after(b2, partial), "kv", outward)
     out_far = swapped(out_here, "tok", 6)
-    shards = (after(hidden_in, out_x, out_y, out_far), a1, a2, a3, b1, b2)
     inner = (kv == 1) | (kv == 2)
-
-    feed_part = jnp.concatenate([eighth(up_weight), eighth(down_weight)], axis=0)
-    feed_inner = lax.ppermute(after(feed_part, a2, b2), "kv", [(0, 2), (3, 1)])
-    feed_outer = lax.ppermute(after(feed_part, a3, feed_inner), "kv", [(1, 3), (2, 0)])
 
     order = jnp.arange(stretch_len.shape[0])
     ends = jnp.sum(jnp.where(order[:, None] <= order[None, :], stretch_len[:, None], 0), axis=0, dtype=jnp.int32)
@@ -492,20 +487,29 @@
     ends = ends[None, :]
 
     weight = jnp.transpose(qkv_weight, (1, 0, 2))
-    edges, even, odd = project(place, weight, shards, kvs, True)
-    even, odd = over_edges(even, "tok", 0), over_edges(odd, "tok", 1)
-    query, middle = project(place, weight, (after(hidden_in, edges),) + shards[1:], kvs, False)
-    window = (middle, edges, even, odd, rows)
-    far = attend_blocks(place, starts, ends, query, *window, (2, 3), "attend_far")
+    query, keyval = project_early(place, weight, kvs, (hidden_in, a1, a2, b1, b2))
+    block = (place, starts, ends, query, keyval)
+    one = attend_block(*block, (1, 0), "attend_early")
+
+    feed_part = jnp.concatenate([eighth(up_weight), eighth(down_weight)], axis=0)
+    feed_inner = lax.ppermute(after(feed_part, query), "kv", [(0, 2), (3, 1)])
+    feed_outer = lax.ppermute(after(feed_part, a3, one, feed_inner), "kv", [(1, 3), (2, 0)])
+
+    *last, even, odd = project_last(place, weight, keyval, after(a3, out_x, out_y, out_far))
+    halo = over_edges(even, "tok", 0), over_edges(odd, "tok", 1)
+    two = attend_block(*block, (2, 3), "attend_last", last)
+    out_all = jnp.stack([out_here, out_x, out_y, out_far])
+    out_core = swapped(out_all, "tok", 1)
+    far = attend_block(*block, (3, 2), "attend_far", last, halo, (two,))
     far_heads = swapped(far, "kv", 2)
-    feed_here = jnp.where(inner, feed_inner, after(feed_outer, far))
+    block = (place, starts, ends, after(query, far, out_core), keyval)
+    near = attend_block(*block, (0, 1), "attend_near", last, halo, (one,))
+    feed_here = jnp.where(inner, feed_inner, after(feed_outer, near))
     feed_x, feed_y = swapped(feed_here, "tok", 2), swapped(feed_here, "tok", 4)
-    near = attend_blocks(place, starts, ends, after(query, feed_here), *window, (0, 1), "attend_near")
     partner_heads, passed_heads = swapped(near, "kv", 1), swapped(far_heads, "kv", 1)
     parts = (near, partner_heads, far_heads, passed_heads)
 
-    out_all = jnp.stack([out_here, out_x, out_y, out_far])
-    out_pieces = [((0, 2, 4, 6), out_all), ((1, 3, 5, 7), swapped(after(out_all, near, far_heads), "tok", 1))]
+    out_pieces = [((0, 2, 4, 6), out_all), ((1, 3, 5, 7), out_core)]
     half = feed_here.shape[0] // 2
     far_up = swapped(after(feed_y, far_heads, partner_heads)[:half], "tok", 2)
     far_down = swapped(after(feed_x, far_heads, partner_heads)[half:], "tok", 4)

time: 137 us -> 141 us (1.029)
  waiting for transfers between devices: 44.5 us -> 49.7 us
  local copies, waits for them, and re-layouts: 8.05 us -> 3 us
  Pallas kernels: 31.4 us -> 34.6 us
    ppermute x19, waiting for transfers between devices: 31.6 us -> 40.1 us  [swapped(): return lax.ppermute(value, axis, [(i, i ^ flip) for i in range(count)])]
    ppermute x5, waiting for transfers between devices: 6.26 us -> 0.01 us  [over_edges(): return lax.ppermute(value, axis, edges + [(j, i) for i, j in edges])]
    unnamed x63 -> x35, local copies, waits for them, and re-layouts: 6.01 us -> 0.96 us
    ppermute x2, waiting for transfers between devices: 2.56 us -> 5.95 us  [the longest x1 5.57 us: routed_body(): feed_inner = lax.ppermute(after(feed_part, query), 'kv', [(0, 2), (3, 1)])]
    ppermute x5, starting transfers between devices: 8.74 us -> 5.91 us  [over_edges(): return lax.ppermute(value, axis, edges + [(j, i) for i, j in edges])]
    ppermute x19, starting transfers between devices: 27 us -> 29.6 us  [swapped(): return lax.ppermute(value, axis, [(i, i ^ flip) for i in range(count)])]
    ppermute x1, waiting for transfers between devices: 2.61 us -> 0.01 us  [routed_body(): a3 = lax.ppermute(after(b2, partial), 'kv', outward)]
    ppermute x1, waiting for transfers between devices: 1.45 us -> 3.69 us  [routed_body(): a2, b2 = (lax.ppermute(b1, 'kv', outward), over_edges(a1, 'kv', 1))]
  transfers between devices with their start and end apart: 28 -> 28, of which waited for: 12 -> 11; matrix products, arithmetic and copies ran while one was open for 4% -> 4% of each run, Pallas kernels for 19% -> 21%
where the time goes in v13:
time: 141 us; the launch traced here: 140 us
  waiting for transfers between devices  49.7 us (35%)
  starting transfers between devices  47.4 us (34%)
  Pallas kernels  34.6 us (25%)
  other arithmetic  4.46 us (3%)
  local copies, waits for them, and re-layouts  3 us (2%)
    ppermute x19, waiting for transfers between devices, swapped(): return lax.ppermute(value, axis, [(i, i ^ flip) for i in range(count)])  40.1 us
    ppermute x19, starting transfers between devices, swapped(): return lax.ppermute(value, axis, [(i, i ^ flip) for i in range(count)])  29.6 us
    pallas_call x4, Pallas kernels, attend_block(): pl.pallas_call(functools.partial(attend_kernel, flips, bool(last), bool(h...  11.7 us
    ppermute x1, starting transfers between devices, routed_body(): feed_inner = lax.ppermute(after(feed_part, query), 'kv', [(0, 2), (3, 1)])  8.01 us
    pallas_call x2, Pallas kernels, feed(): pl.pallas_call(feed_kernel, out_shape=jax.ShapeDtypeStruct((count, width)...  7.82 us
    ppermute x5, starting transfers between devices, over_edges(): return lax.ppermute(value, axis, edges + [(j, i) for i, j in edges])  5.91 us
    ppermute x1, waiting for transfers between devices, routed_body(): feed_inner = lax.ppermute(after(feed_part, query), 'kv', [(0, 2), (3, 1)])  5.57 us
    pallas_call x1, Pallas kernels, first_norm(): pl.pallas_call(functools.partial(first_norm_kernel, layout), out_shape=(j...  4.72 us
  transfers between devices with their start and end apart: 28, of which 11 were waited for; matrix products, arithmetic and copies ran while one was open for 4% of the time, Pallas kernels for 21%

profile of v13, /device:TPU:0, one launch (start us, length us, event | category | flops | bytes accessed | tf_op | source)
XLA Modules:
  0.0 140.4 jit_solution(1061171310504488815)
XLA Ops:
  0.7 3.1 %collective-permute-start = (bf16[256,1024]{1,0:T(8,128)(2,1)}, bf16[256,1024]{1,0:T(8,128)(2,1)}, u32[]{:S(2)}, u32[]{:S(2)}) collective-permute-start(bf16[256,1024]{1,0:T(8,128)(2,1)} %own_ref.1), channel_id=1, source_target_pairs={{0,1},{2,3},{1,0},{3,2},{4,5},{6,7},{5,4},{7,6},{8,9},{10,11},{9,8... | collective-permute-start | bytes 1572872 | tf_op jit(solution)/shard_map/ppermute | solution.py:37
  6.7 2.6 %collective-permute-start.6 = (bf16[34,1024]{1,0:T(8,128)(2,1)S(1)}, bf16[34,1024]{1,0:T(8,128)(2,1)S(1)}, u32[]{:S(2)}, u32[]{:S(2)}) collective-permute-start(bf16[34,1024]{1,0:T(8,128)(2,1)S(1)} %pad_maximum_fusion.3), channel_id=1, source_target_pairs={{0,3},{1,2},{2,1},{3,0},{4,7},{5,6},{6,5},{7,4},{8,11},{9,10},{10,... | collective-permute-start | bytes 208904 | tf_op jit(solution)/shard_map/ppermute | solution.py:31
  9.4 2.5 %collective-permute-start.5 = (bf16[34,1024]{1,0:T(8,128)(2,1)S(1)}, bf16[34,1024]{1,0:T(8,128)(2,1)S(1)}, u32[]{:S(2)}, u32[]{:S(2)}) collective-permute-start(bf16[34,1024]{1,0:T(8,128)(2,1)S(1)} %pad_maximum_fusion.3), channel_id=1, source_target_pairs={{0,2},{1,3},{2,0},{3,1},{4,6},{5,7},{6,4},{7,5},{8,10},{9,11},{10,... | collective-permute-start | bytes 208904 | tf_op jit(solution)/shard_map/ppermute | solution.py:31
  14.4 6.6 %collective-permute-done.6 = bf16[34,1024]{1,0:T(8,128)(2,1)S(1)} collective-permute-done((bf16[34,1024]{1,0:T(8,128)(2,1)S(1)}, bf16[34,1024]{1,0:T(8,128)(2,1)S(1)}, u32[]{:S(2)}, u32[]{:S(2)}) %collective-permute-start.6) | collective-permute-done | bytes 69664 | tf_op jit(solution)/shard_map/ppermute | solution.py:31
  21.0 6.1 %collective-permute-done.5 = bf16[34,1024]{1,0:T(8,128)(2,1)S(1)} collective-permute-done((bf16[34,1024]{1,0:T(8,128)(2,1)S(1)}, bf16[34,1024]{1,0:T(8,128)(2,1)S(1)}, u32[]{:S(2)}, u32[]{:S(2)}) %collective-permute-start.5) | collective-permute-done | bytes 69664 | tf_op jit(solution)/shard_map/ppermute | solution.py:31
  29.2 1.6 %collective-permute-start.8 = (bf16[3,32,1024]{2,1,0:T(8,128)(2,1)S(1)}, bf16[3,32,1024]{2,1,0:T(8,128)(2,1)S(1)}, u32[]{:S(2)}, u32[]{:S(2)}) collective-permute-start(bf16[3,32,1024]{2,1,0:T(8,128)(2,1)S(1)} %get-tuple-element.51), channel_id=1, source_target_pairs={{0,8},{4,12},{8,0},{12,4},{16,24},{20,28},{24,16},{28,20},{1,9},{5... | collective-permute-start | bytes 589832 | tf_op jit(solution)/shard_map/ppermute | solution.py:31
  30.8 1.5 %collective-permute-start.9 = (bf16[3,32,1024]{2,1,0:T(8,128)(2,1)S(1)}, bf16[3,32,1024]{2,1,0:T(8,128)(2,1)S(1)}, u32[]{:S(2)}, u32[]{:S(2)}) collective-permute-start(bf16[3,32,1024]{2,1,0:T(8,128)(2,1)S(1)} %get-tuple-element.51), channel_id=1, source_target_pairs={{0,16},{4,20},{8,24},{12,28},{16,0},{20,4},{24,8},{28,12},{1,17},{... | collective-permute-start | bytes 589832 | tf_op jit(solution)/shard_map/ppermute | solution.py:31
  32.9 3.8 %decode.1 = f32[3,8,1024]{2,1,0:T(8,128)S(1)} custom-call(s32[6]{0:T(128)S(1)} %fusion.12.slot_ref, s32[6]{0:T(128)S(1)} %bitcast.153, f32[8,1024]{1,0:T(8,128)S(1)} %maximum_convert_fusion.query_ref, bf16[2,1,6,128,1024]{4,3,2,1,0:T(8,128)(2,1)S(1)} %copy-done.3), custom_call_target="tpu_custom_call" | custom-call | flops 1 | bytes 1 | tf_op jit(solution)/shard_map/decode/pallas_call | solution.py:407
  38.0 3.7 %collective-permute-done.2.a2 = bf16[256,1024]{1,0:T(8,128)(2,1)S(1)} collective-permute-done((bf16[256,1024]{1,0:T(8,128)(2,1)}, bf16[256,1024]{1,0:T(8,128)(2,1)S(1)}, u32[]{:S(2)}, u32[]{:S(2)}) %collective-permute-start.2) | collective-permute-done | bytes 524320 | tf_op jit(solution)/shard_map/ppermute | solution.py:475
  41.7 3.5 %project_early.1 = (bf16[1024,256]{1,0:T(8,128)(2,1)S(1)}, bf16[1024,512]{1,0:T(8,128)(2,1)S(1)}) custom-call(s32[2]{0:T(128)S(1)} %pad_add_fusion.place_ref, bf16[3,1024,256]{2,1,0:T(8,128)(2,1)S(1)} %bitcast.143, bf16[256,1024]{1,0:T(8,128)(2,1)S(1)} %copy-done.4, bf16[256,1024]{1,0:T(8,128)(2,1)} %collective-permute-done.a1.partner_ref, ...), custom_call_target="tpu_custom_call" | custom-call | flops 1 | bytes 1 | tf_op jit(solution)/shard_map/project_early/pallas_call | solution.py:91
  45.2 8.0 %collective-permute-start.17 = (bf16[256,1024]{1,0:T(8,128)(2,1)}, bf16[256,1024]{1,0:T(8,128)(2,1)S(1)}, u32[]{:S(2)}, u32[]{:S(2)}) collective-permute-start(bf16[256,1024]{1,0:T(8,128)(2,1)} %pad_maximum_fusion.1), channel_id=1, source_target_pairs={{0,2},{3,1},{4,6},{7,5},{8,10},{11,9},{12,14},{15,13},{16,18},{19,... | collective-permute-start | bytes 1572872 | tf_op jit(solution)/shard_map/ppermute | solution.py:495
  53.6 2.8 %attend_early.1.refs_4_ = bf16[256,256]{1,0:T(8,128)(2,1)S(1)} custom-call(s32[2]{0:T(128)S(1)} %pad_add_fusion.place_ref, s32[1,48]{1,0:T(1,128)S(1)} %subtract_bitcast_fusion.starts_ref, s32[1,48]{1,0:T(1,128)S(1)} %bitcast.145, bf16[1024,256]{1,0:T(8,128)(2,1)S(1)} %get-tuple-element.33.query_ref, bf16[1024,512]{1,0:T(8,128)(2,1)S(1)} %get-tuple-element.26.keyval_ref), custom_call_target="tpu_custom_call" | custom-call | flops 1 | bytes 1 | tf_op jit(solution)/shard_map/attend_early/pallas_call | solution.py:203
  56.4 5.6 %collective-permute-done.17 = bf16[256,1024]{1,0:T(8,128)(2,1)S(1)} collective-permute-done((bf16[256,1024]{1,0:T(8,128)(2,1)}, bf16[256,1024]{1,0:T(8,128)(2,1)S(1)}, u32[]{:S(2)}, u32[]{:S(2)}) %collective-permute-start.17) | collective-permute-done | bytes 524320 | tf_op jit(solution)/shard_map/ppermute | solution.py:495
  64.1 1.9 %project_last.1 = (bf16[256,256]{1,0:T(8,128)(2,1)S(1)}, bf16[256,512]{1,0:T(8,128)(2,1)S(1)}, bf16[256,512]{1,0:T(8,128)(2,1)}, bf16[256,512]{1,0:T(8,128)(2,1)}) custom-call(s32[2]{0:T(128)S(1)} %pad_add_fusion.place_ref, bf16[3,1024,256]{2,1,0:T(8,128)(2,1)S(1)} %bitcast.144, bf16[1024,512]{1,0:T(8,128)(2,1)S(1)} %get-tuple-element.26.keyval_ref, ...), custom_call_target="tpu_custom_call" | custom-call | flops 1 | bytes 1 | tf_op jit(solution)/shard_map/project_last/pallas_call | solution.py:110
  66.7 2.9 %attend_last.1.refs_4_ = bf16[256,256]{1,0:T(8,128)(2,1)S(1)} custom-call(s32[2]{0:T(128)S(1)} %pad_add_fusion.place_ref, s32[1,48]{1,0:T(1,128)S(1)} %subtract_bitcast_fusion.starts_ref, s32[1,48]{1,0:T(1,128)S(1)} %bitcast.146, bf16[1024,256]{1,0:T(8,128)(2,1)S(1)} %get-tuple-element.33.query_ref, bf16[1024,512]{1,0:T(8,128)(2,1)S(1)} %get-tuple-element.26.keyval_ref, ...), custom_call_target="tpu_custom_call" | custom-call | flops 1 | bytes 1 | tf_op jit(solution)/shard_map/attend_last/pallas_call | solution.py:203
  69.6 2.9 %attend_far.1 = bf16[512,256]{1,0:T(8,128)(2,1)S(1)} custom-call(s32[2]{0:T(128)S(1)} %pad_add_fusion.place_ref, s32[1,48]{1,0:T(1,128)S(1)} %subtract_bitcast_fusion.starts_ref, s32[1,48]{1,0:T(1,128)S(1)} %bitcast.147, bf16[1024,256]{1,0:T(8,128)(2,1)S(1)} %get-tuple-element.33.query_ref, bf16[1024,512]{1,0:T(8,128)(2,1)S(1)} %get-tuple-element.26.keyval_ref, ...), custom_call_target="tpu_custom_call" | custom-call | flops 1 | bytes 1 | tf_op jit(solution)/shard_map/attend_far/pallas_call | solution.py:203
  72.5 3.1 %attend_near.1.refs_0_ = bf16[512,256]{1,0:T(8,128)(2,1)S(1)} custom-call(s32[2]{0:T(128)S(1)} %pad_add_fusion.place_ref, s32[1,48]{1,0:T(1,128)S(1)} %subtract_bitcast_fusion.starts_ref, s32[1,48]{1,0:T(1,128)S(1)} %bitcast.148, bf16[1024,256]{1,0:T(8,128)(2,1)S(1)} %get-tuple-element.33.query_ref, bf16[1024,512]{1,0:T(8,128)(2,1)S(1)} %get-tuple-element.26.keyval_ref, ...), custom_call_target="tpu_custom_call" | custom-call | flops 1 | bytes 1 | tf_op jit(solution)/shard_map/attend_near/pallas_call | solution.py:203
  77.3 9.0 %collective-permute-start.20 = (bf16[256,1024]{1,0:T(8,128)(2,1)S(1)}, bf16[256,1024]{1,0:T(8,128)(2,1)S(1)}, u32[]{:S(2)}, u32[]{:S(2)}) collective-permute-start(bf16[256,1024]{1,0:T(8,128)(2,1)S(1)} %get-tuple-element.49), channel_id=1, source_target_pairs={{0,16},{4,20},{8,24},{12,28},{16,0},{20,4},{24,8},{28,12},{1,17},{... | collective-permute-start | bytes 1572872 | tf_op jit(solution)/shard_map/ppermute | solution.py:31
  86.5 2.8 %collective-permute-start.14 = (bf16[512,256]{1,0:T(8,128)(2,1)S(1)}, bf16[512,256]{1,0:T(8,128)(2,1)S(1)}, u32[]{:S(2)}, u32[]{:S(2)}) collective-permute-start(bf16[512,256]{1,0:T(8,128)(2,1)S(1)} %attend_near.1.refs_0_), channel_id=1, source_target_pairs={{0,1},{1,0},{2,3},{3,2},{4,5},{5,4},{6,7},{7,6},{8,9},{9,8},{10,11... | collective-permute-start | bytes 786440 | tf_op jit(solution)/shard_map/ppermute | solution.py:31
  89.9 10.6 %collective-permute-done.14.refs_1_ = bf16[512,256]{1,0:T(8,128)(2,1)S(1)} collective-permute-done((bf16[512,256]{1,0:T(8,128)(2,1)S(1)}, bf16[512,256]{1,0:T(8,128)(2,1)S(1)}, u32[]{:S(2)}, u32[]{:S(2)}) %collective-permute-start.14) | collective-permute-done | bytes 262176 | tf_op jit(solution)/shard_map/ppermute | solution.py:31
  100.5 3.0 %collective-permute-done.15.refs_2_ = bf16[512,256]{1,0:T(8,128)(2,1)S(1)} collective-permute-done((bf16[512,256]{1,0:T(8,128)(2,1)S(1)}, bf16[512,256]{1,0:T(8,128)(2,1)S(1)}, u32[]{:S(2)}, u32[]{:S(2)}) %collective-permute-start.15) | collective-permute-done | bytes 262176 | tf_op jit(solution)/shard_map/ppermute | solution.py:31
  104.0 1.7 %collective-permute-start.22 = (bf16[128,1024]{1,0:T(8,128)(2,1)S(1)}, bf16[128,1024]{1,0:T(8,128)(2,1)S(1)}, u32[]{:S(2)}, u32[]{:S(2)}) collective-permute-start(bf16[128,1024]{1,0:T(8,128)(2,1)S(1)} %slice.83), channel_id=1, source_target_pairs={{0,16},{4,20},{8,24},{12,28},{16,0},{20,4},{24,8},{28,12},{1,17},{... | collective-permute-start | bytes 786440 | tf_op jit(solution)/shard_map/ppermute | solution.py:31
  105.7 4.3 %collective-permute-done.21 = bf16[128,1024]{1,0:T(8,128)(2,1)S(1)} collective-permute-done((bf16[128,1024]{1,0:T(8,128)(2,1)S(1)}, bf16[128,1024]{1,0:T(8,128)(2,1)S(1)}, u32[]{:S(2)}, u32[]{:S(2)}) %collective-permute-start.21) | collective-permute-done | bytes 262176 | tf_op jit(solution)/shard_map/ppermute | solution.py:31
  110.0 2.0 %collective-permute-done.22 = bf16[128,1024]{1,0:T(8,128)(2,1)S(1)} collective-permute-done((bf16[128,1024]{1,0:T(8,128)(2,1)S(1)}, bf16[128,1024]{1,0:T(8,128)(2,1)S(1)}, u32[]{:S(2)}, u32[]{:S(2)}) %collective-permute-start.22) | collective-permute-done | bytes 262176 | tf_op jit(solution)/shard_map/ppermute | solution.py:31
  112.2 4.7 %first_norm.1 = (bf16[256,1024]{1,0:T(8,128)(2,1)S(1)}, bf16[256,1024]{1,0:T(8,128)(2,1)S(1)}) custom-call(s32[2]{0:T(128)S(1)} %pad_add_fusion.place_ref, bf16[256,1024]{1,0:T(8,128)(2,1)S(1)} %copy-done.5, bf16[256,1024]{1,0:T(8,128)(2,1)} %collective-permute-done.a1.partner_ref, bf16[256,1024]{1,0:T(8,128)(2,1)S(1)} %copy-done.6, ...), custom_call_target="tpu_custom_call" | custom-call | flops 1 | bytes 1 | tf_op jit(solution)/shard_map/first_norm/pallas_call | solution.py:256
  116.9 3.9 %feed_partner.1 = bf16[256,1024]{1,0:T(8,128)(2,1)S(1)} custom-call(s32[2]{0:T(128)S(1)} %pad_add_fusion.place_ref, bf16[256,1024]{1,0:T(8,128)(2,1)S(1)} %get-tuple-element.35.rows_ref, bf16[1024,1024]{1,0:T(8,128)(2,1)S(1)} %copy-done, bf16[1024,1024]{1,0:T(8,128)(2,1)S(1)} %copy-done.1, bf16[1024,1024]{1,0:T(8,128)(2,1)S(1)} %constant_dynamic-update-slice_fusion.held_ref, ...), custom_call_target="tpu_custom_call" | custom-call | flops 1 | bytes 1 | tf_op jit(solution)/shard_map/feed_partner/pallas_call | solution.py:325
  120.8 1.8 %collective-permute-start.24 = (bf16[256,1024]{1,0:T(8,128)(2,1)S(1)}, bf16[256,1024]{1,0:T(8,128)(2,1)S(1)}, u32[]{:S(2)}, u32[]{:S(2)}) collective-permute-start(bf16[256,1024]{1,0:T(8,128)(2,1)S(1)} %feed_partner.1), channel_id=1, source_target_pairs={{0,1},{1,0},{2,3},{3,2},{4,5},{5,4},{6,7},{7,6},{8,9},{9,8},{10,11... | collective-permute-start | bytes 1572872 | tf_op jit(solution)/shard_map/ppermute | solution.py:31
  123.0 2.3 %collective-permute-start.26 = (f32[3,2,1024]{2,1,0:T(2,128)S(1)}, f32[3,2,1024]{2,1,0:T(2,128)S(1)}, u32[]{:S(2)}, u32[]{:S(2)}) collective-permute-start(f32[3,2,1024]{2,1,0:T(2,128)S(1)} %get-tuple-element.53), channel_id=1, source_target_pairs={{0,2},{1,3},{2,0},{3,1},{4,6},{5,7},{6,4},{7,5},{8,10},{9,11},{10,... | collective-permute-start | bytes 73736 | tf_op jit(solution)/shard_map/ppermute | solution.py:31
  125.3 1.8 %collective-permute-start.27 = (f32[3,2,1024]{2,1,0:T(2,128)S(1)}, f32[3,2,1024]{2,1,0:T(2,128)S(1)}, u32[]{:S(2)}, u32[]{:S(2)}) collective-permute-start(f32[3,2,1024]{2,1,0:T(2,128)S(1)} %get-tuple-element.52), channel_id=1, source_target_pairs={{0,3},{1,2},{2,1},{3,0},{4,7},{5,6},{6,5},{7,4},{8,11},{9,10},{10,... | collective-permute-start | bytes 73736 | tf_op jit(solution)/shard_map/ppermute | solution.py:31
  127.1 3.9 %feed_own.1.near_ref = f32[256,1024]{1,0:T(8,128)S(1)} custom-call(s32[2]{0:T(128)S(1)} %pad_add_fusion.place_ref, bf16[256,1024]{1,0:T(8,128)(2,1)S(1)} %get-tuple-element.42.rows_ref.normed_ref, bf16[1024,1024]{1,0:T(8,128)(2,1)S(1)} %copy-done, bf16[1024,1024]{1,0:T(8,128)(2,1)S(1)} %copy-done.1, ...), custom_call_target="tpu_custom_call" | custom-call | flops 1 | bytes 1 | tf_op jit(solution)/shard_map/feed_own/pallas_call | solution.py:325
  131.0 5.2 %collective-permute-done.25 = f32[3,2,1024]{2,1,0:T(2,128)S(1)} collective-permute-done((f32[3,2,1024]{2,1,0:T(2,128)S(1)}, f32[3,2,1024]{2,1,0:T(2,128)S(1)}, u32[]{:S(2)}, u32[]{:S(2)}) %collective-permute-start.25) | collective-permute-done | bytes 24608 | tf_op jit(solution)/shard_map/ppermute | solution.py:31
  136.3 2.2 %collective-permute-done.27 = f32[3,2,1024]{2,1,0:T(2,128)S(1)} collective-permute-done((f32[3,2,1024]{2,1,0:T(2,128)S(1)}, f32[3,2,1024]{2,1,0:T(2,128)S(1)}, u32[]{:S(2)}, u32[]{:S(2)}) %collective-permute-start.27) | collective-permute-done | bytes 24608 | tf_op jit(solution)/shard_map/ppermute | solution.py:31
  (93 shorter events, 18.0 us)
Async XLA Ops:
  0.7 27.8 %collective-permute-start = (bf16[256,1024]{1,0:T(8,128)(2,1)}, bf16[256,1024]{1,0:T(8,128)(2,1)}, u32[]{:S(2)}, u32[]{:S(2)}) collective-permute-start(bf16[256,1024]{1,0:T(8,128)(2,1)} %own_ref.1), channel_id=1, source_target_pairs={{0,1},{2,3},{1,0},{3,2},{4,5},{6,7},{5,4},{7,6},{8,9},{10,11},{9,8... | collective-permute-start | bytes 1572872 | tf_op jit(solution)/shard_map/ppermute | solution.py:37
  3.8 23.4 %collective-permute-start.1 = (bf16[256,1024]{1,0:T(8,128)(2,1)}, bf16[256,1024]{1,0:T(8,128)(2,1)}, u32[]{:S(2)}, u32[]{:S(2)}) collective-permute-start(bf16[256,1024]{1,0:T(8,128)(2,1)} %own_ref.1), channel_id=1, source_target_pairs={{1,2},{2,1},{5,6},{6,5},{9,10},{10,9},{13,14},{14,13},{17,18},{18,... | collective-permute-start | bytes 1572872 | tf_op jit(solution)/shard_map/ppermute | solution.py:37
  6.7 14.3 %collective-permute-start.6 = (bf16[34,1024]{1,0:T(8,128)(2,1)S(1)}, bf16[34,1024]{1,0:T(8,128)(2,1)S(1)}, u32[]{:S(2)}, u32[]{:S(2)}) collective-permute-start(bf16[34,1024]{1,0:T(8,128)(2,1)S(1)} %pad_maximum_fusion.3), channel_id=1, source_target_pairs={{0,3},{1,2},{2,1},{3,0},{4,7},{5,6},{6,5},{7,4},{8,11},{9,10},{10,... | collective-permute-start | bytes 208904 | tf_op jit(solution)/shard_map/ppermute | solution.py:31
  9.4 17.8 %collective-permute-start.5 = (bf16[34,1024]{1,0:T(8,128)(2,1)S(1)}, bf16[34,1024]{1,0:T(8,128)(2,1)S(1)}, u32[]{:S(2)}, u32[]{:S(2)}) collective-permute-start(bf16[34,1024]{1,0:T(8,128)(2,1)S(1)} %pad_maximum_fusion.3), channel_id=1, source_target_pairs={{0,2},{1,3},{2,0},{3,1},{4,6},{5,7},{6,4},{7,5},{8,10},{9,11},{10,... | collective-permute-start | bytes 208904 | tf_op jit(solution)/shard_map/ppermute | solution.py:31
  11.8 17.3 %collective-permute-start.4 = (bf16[34,1024]{1,0:T(8,128)(2,1)S(1)}, bf16[34,1024]{1,0:T(8,128)(2,1)S(1)}, u32[]{:S(2)}, u32[]{:S(2)}) collective-permute-start(bf16[34,1024]{1,0:T(8,128)(2,1)S(1)} %pad_maximum_fusion.3), channel_id=1, source_target_pairs={{0,1},{1,0},{2,3},{3,2},{4,5},{5,4},{6,7},{7,6},{8,9},{9,8},{10,11... | collective-permute-start | bytes 208904 | tf_op jit(solution)/shard_map/ppermute | solution.py:31
  27.1 14.6 %collective-permute-start.2 = (bf16[256,1024]{1,0:T(8,128)(2,1)}, bf16[256,1024]{1,0:T(8,128)(2,1)S(1)}, u32[]{:S(2)}, u32[]{:S(2)}) collective-permute-start(bf16[256,1024]{1,0:T(8,128)(2,1)} %collective-permute-done.1.b1), channel_id=1, source_target_pairs={{1,0},{2,3},{5,4},{6,7},{9,8},{10,11},{13,12},{14,15},{17,16},{18,... | collective-permute-start | bytes 1572872 | tf_op jit(solution)/shard_map/ppermute | solution.py:475
  28.4 8.3 %collective-permute-start.3 = (bf16[256,1024]{1,0:T(8,128)(2,1)}, bf16[256,1024]{1,0:T(8,128)(2,1)S(1)}, u32[]{:S(2)}, u32[]{:S(2)}) collective-permute-start(bf16[256,1024]{1,0:T(8,128)(2,1)} %collective-permute-done.a1.partner_ref), channel_id=1, source_target_pairs={{1,2},{2,1},{5,6},{6,5},{9,10},{10,9},{13,14},{14,13},{17,18},{18,... | collective-permute-start | bytes 1572872 | tf_op jit(solution)/shard_map/ppermute | solution.py:37
  29.2 24.0 %collective-permute-start.8 = (bf16[3,32,1024]{2,1,0:T(8,128)(2,1)S(1)}, bf16[3,32,1024]{2,1,0:T(8,128)(2,1)S(1)}, u32[]{:S(2)}, u32[]{:S(2)}) collective-permute-start(bf16[3,32,1024]{2,1,0:T(8,128)(2,1)S(1)} %get-tuple-element.51), channel_id=1, source_target_pairs={{0,8},{4,12},{8,0},{12,4},{16,24},{20,28},{24,16},{28,20},{1,9},{5... | collective-permute-start | bytes 589832 | tf_op jit(solution)/shard_map/ppermute | solution.py:31
  30.8 22.5 %collective-permute-start.9 = (bf16[3,32,1024]{2,1,0:T(8,128)(2,1)S(1)}, bf16[3,32,1024]{2,1,0:T(8,128)(2,1)S(1)}, u32[]{:S(2)}, u32[]{:S(2)}) collective-permute-start(bf16[3,32,1024]{2,1,0:T(8,128)(2,1)S(1)} %get-tuple-element.51), channel_id=1, source_target_pairs={{0,16},{4,20},{8,24},{12,28},{16,0},{20,4},{24,8},{28,12},{1,17},{... | collective-permute-start | bytes 589832 | tf_op jit(solution)/shard_map/ppermute | solution.py:31
  32.3 21.0 %collective-permute-start.10 = (bf16[3,32,1024]{2,1,0:T(8,128)(2,1)S(1)}, bf16[3,32,1024]{2,1,0:T(8,128)(2,1)S(1)}, u32[]{:S(2)}, u32[]{:S(2)}) collective-permute-start(bf16[3,32,1024]{2,1,0:T(8,128)(2,1)S(1)} %get-tuple-element.51), channel_id=1, source_target_pairs={{0,24},{4,28},{8,16},{12,20},{16,8},{20,12},{24,0},{28,4},{1,25},{... | collective-permute-start | bytes 589832 | tf_op jit(solution)/shard_map/ppermute | solution.py:31
  36.7 19.7 %collective-permute-start.7 = (bf16[256,1024]{1,0:T(8,128)(2,1)S(1)}, bf16[256,1024]{1,0:T(8,128)(2,1)S(1)}, u32[]{:S(2)}, u32[]{:S(2)}) collective-permute-start(bf16[256,1024]{1,0:T(8,128)(2,1)S(1)} %collective-permute-done.3.b2), channel_id=1, source_target_pairs={{1,0},{2,3},{5,4},{6,7},{9,8},{10,11},{13,12},{14,15},{17,16},{18,... | collective-permute-start | bytes 1572872 | tf_op jit(solution)/shard_map/ppermute | solution.py:480
  45.2 16.8 %collective-permute-start.17 = (bf16[256,1024]{1,0:T(8,128)(2,1)}, bf16[256,1024]{1,0:T(8,128)(2,1)S(1)}, u32[]{:S(2)}, u32[]{:S(2)}) collective-permute-start(bf16[256,1024]{1,0:T(8,128)(2,1)} %pad_maximum_fusion.1), channel_id=1, source_target_pairs={{0,2},{3,1},{4,6},{7,5},{8,10},{11,9},{12,14},{15,13},{16,18},{19,... | collective-permute-start | bytes 1572872 | tf_op jit(solution)/shard_map/ppermute | solution.py:495
  53.4 19.1 %collective-permute-start.13 = (bf16[4,3,32,1024]{3,2,1,0:T(8,128)(2,1)S(1)}, bf16[4,3,32,1024]{3,2,1,0:T(8,128)(2,1)}, u32[]{:S(2)}, u32[]{:S(2)}) collective-permute-start(bf16[4,3,32,1024]{3,2,1,0:T(8,128)(2,1)S(1)} %pad_maximum_fusion.refs_4_), channel_id=1, source_target_pairs={{0,4},{4,0},{8,12},{12,8},{16,20},{20,16},{24,28},{28,24},{1,5},{5... | collective-permute-start | bytes 2359304 | tf_op jit(solution)/shard_map/ppermute | solution.py:31
  62.8 13.2 %collective-permute-start.18 = (bf16[256,1024]{1,0:T(8,128)(2,1)}, bf16[256,1024]{1,0:T(8,128)(2,1)}, u32[]{:S(2)}, u32[]{:S(2)}) collective-permute-start(bf16[256,1024]{1,0:T(8,128)(2,1)} %pad_maximum_fusion.1), channel_id=1, source_target_pairs={{1,3},{2,0},{5,7},{6,4},{9,11},{10,8},{13,15},{14,12},{17,19},{18,... | collective-permute-start | bytes 1572872 | tf_op jit(solution)/shard_map/ppermute | solution.py:496
  66.0 3.6 %collective-permute-start.11 = (bf16[256,512]{1,0:T(8,128)(2,1)}, bf16[256,512]{1,0:T(8,128)(2,1)S(1)}, u32[]{:S(2)}, u32[]{:S(2)}) collective-permute-start(bf16[256,512]{1,0:T(8,128)(2,1)} %get-tuple-element.31), channel_id=1, source_target_pairs={{0,4},{8,12},{16,20},{24,28},{4,0},{12,8},{20,16},{28,24},{1,5},{9... | collective-permute-start | bytes 786440 | tf_op jit(solution)/shard_map/ppermute | solution.py:37
  66.0 3.6 %collective-permute-start.12 = (bf16[256,512]{1,0:T(8,128)(2,1)}, bf16[256,512]{1,0:T(8,128)(2,1)S(1)}, u32[]{:S(2)}, u32[]{:S(2)}) collective-permute-start(bf16[256,512]{1,0:T(8,128)(2,1)} %get-tuple-element.32), channel_id=1, source_target_pairs={{4,8},{12,16},{20,24},{8,4},{16,12},{24,20},{5,9},{13,17},{21,25},... | collective-permute-start | bytes 786440 | tf_op jit(solution)/shard_map/ppermute | solution.py:37
  77.2 34.9 %copy-start.5 = (bf16[256,1024]{1,0:T(8,128)(2,1)S(1)}, bf16[256,1024]{1,0:T(8,128)(2,1)}, u32[]{:S(2)}) copy-start(bf16[256,1024]{1,0:T(8,128)(2,1)} %own_ref.1) | copy-start | bytes 1572868
  77.3 34.9 %copy-start.6 = (bf16[256,1024]{1,0:T(8,128)(2,1)S(1)}, bf16[256,1024]{1,0:T(8,128)(2,1)}, u32[]{:S(2)}) copy-start(bf16[256,1024]{1,0:T(8,128)(2,1)} %own_out_ref.1) | copy-start | bytes 1572868
  77.3 34.8 %copy-start.9 = (f32[1024]{0:T(1024)S(1)}, f32[1024]{0:T(1024)}, u32[]{:S(2)}) copy-start(f32[1024]{0:T(1024)} %param.18) | copy-start | bytes 12292
  77.3 34.8 %copy-start.10 = (f32[1024]{0:T(1024)S(1)}, f32[1024]{0:T(1024)}, u32[]{:S(2)}) copy-start(f32[1024]{0:T(1024)} %param.19) | copy-start | bytes 12292
  77.3 26.2 %collective-permute-start.20 = (bf16[256,1024]{1,0:T(8,128)(2,1)S(1)}, bf16[256,1024]{1,0:T(8,128)(2,1)S(1)}, u32[]{:S(2)}, u32[]{:S(2)}) collective-permute-start(bf16[256,1024]{1,0:T(8,128)(2,1)S(1)} %get-tuple-element.49), channel_id=1, source_target_pairs={{0,16},{4,20},{8,24},{12,28},{16,0},{20,4},{24,8},{28,12},{1,17},{... | collective-permute-start | bytes 1572872 | tf_op jit(solution)/shard_map/ppermute | solution.py:31
  86.3 17.7 %collective-permute-start.19 = (bf16[256,1024]{1,0:T(8,128)(2,1)S(1)}, bf16[256,1024]{1,0:T(8,128)(2,1)S(1)}, u32[]{:S(2)}, u32[]{:S(2)}) collective-permute-start(bf16[256,1024]{1,0:T(8,128)(2,1)S(1)} %get-tuple-element.49), channel_id=1, source_target_pairs={{0,8},{4,12},{8,0},{12,4},{16,24},{20,28},{24,16},{28,20},{1,9},{5... | collective-permute-start | bytes 1572872 | tf_op jit(solution)/shard_map/ppermute | solution.py:31
  86.5 13.9 %collective-permute-start.14 = (bf16[512,256]{1,0:T(8,128)(2,1)S(1)}, bf16[512,256]{1,0:T(8,128)(2,1)S(1)}, u32[]{:S(2)}, u32[]{:S(2)}) collective-permute-start(bf16[512,256]{1,0:T(8,128)(2,1)S(1)} %attend_near.1.refs_0_), channel_id=1, source_target_pairs={{0,1},{1,0},{2,3},{3,2},{4,5},{5,4},{6,7},{7,6},{8,9},{9,8},{10,11... | collective-permute-start | bytes 786440 | tf_op jit(solution)/shard_map/ppermute | solution.py:31
  89.4 14.2 %collective-permute-start.15 = (bf16[512,256]{1,0:T(8,128)(2,1)S(1)}, bf16[512,256]{1,0:T(8,128)(2,1)S(1)}, u32[]{:S(2)}, u32[]{:S(2)}) collective-permute-start(bf16[512,256]{1,0:T(8,128)(2,1)S(1)} %attend_far.1), channel_id=1, source_target_pairs={{0,2},{1,3},{2,0},{3,1},{4,6},{5,7},{6,4},{7,5},{8,10},{9,11},{10,... | collective-permute-start | bytes 786440 | tf_op jit(solution)/shard_map/ppermute | solution.py:31
  103.5 6.4 %collective-permute-start.21 = (bf16[128,1024]{1,0:T(8,128)(2,1)S(1)}, bf16[128,1024]{1,0:T(8,128)(2,1)S(1)}, u32[]{:S(2)}, u32[]{:S(2)}) collective-permute-start(bf16[128,1024]{1,0:T(8,128)(2,1)S(1)} %slice.82), channel_id=1, source_target_pairs={{0,8},{4,12},{8,0},{12,4},{16,24},{20,28},{24,16},{28,20},{1,9},{5... | collective-permute-start | bytes 786440 | tf_op jit(solution)/shard_map/ppermute | solution.py:31
  103.9 8.1 %collective-permute-start.16 = (bf16[512,256]{1,0:T(8,128)(2,1)S(1)}, bf16[512,256]{1,0:T(8,128)(2,1)S(1)}, u32[]{:S(2)}, u32[]{:S(2)}) collective-permute-start(bf16[512,256]{1,0:T(8,128)(2,1)S(1)} %collective-permute-done.15.refs_2_), channel_id=1, source_target_pairs={{0,1},{1,0},{2,3},{3,2},{4,5},{5,4},{6,7},{7,6},{8,9},{9,8},{10,11... | collective-permute-start | bytes 786440 | tf_op jit(solution)/shard_map/ppermute | solution.py:31
  104.0 8.0 %collective-permute-start.22 = (bf16[128,1024]{1,0:T(8,128)(2,1)S(1)}, bf16[128,1024]{1,0:T(8,128)(2,1)S(1)}, u32[]{:S(2)}, u32[]{:S(2)}) collective-permute-start(bf16[128,1024]{1,0:T(8,128)(2,1)S(1)} %slice.83), channel_id=1, source_target_pairs={{0,16},{4,20},{8,24},{12,28},{16,0},{20,4},{24,8},{28,12},{1,17},{... | collective-permute-start | bytes 786440 | tf_op jit(solution)/shard_map/ppermute | solution.py:31
  112.0 4.9 %collective-permute-start.23 = (bf16[1024,1024]{1,0:T(8,128)(2,1)S(1)}, bf16[1024,1024]{1,0:T(8,128)(2,1)S(1)}, u32[]{:S(2)}, u32[]{:S(2)}) collective-permute-start(bf16[1024,1024]{1,0:T(8,128)(2,1)S(1)} %constant_dynamic-update-slice_fusion.held_ref), channel_id=1, source_target_pairs={{0,4},{4,0},{8,12},{12,8},{16,20},{20,16},{24,28},{28,24},{1,5},{5... | collective-permute-start | bytes 6291464 | tf_op jit(solution)/shard_map/ppermute | solution.py:31
  120.8 18.3 %collective-permute-start.24 = (bf16[256,1024]{1,0:T(8,128)(2,1)S(1)}, bf16[256,1024]{1,0:T(8,128)(2,1)S(1)}, u32[]{:S(2)}, u32[]{:S(2)}) collective-permute-start(bf16[256,1024]{1,0:T(8,128)(2,1)S(1)} %feed_partner.1), channel_id=1, source_target_pairs={{0,1},{1,0},{2,3},{3,2},{4,5},{5,4},{6,7},{7,6},{8,9},{9,8},{10,11... | collective-permute-start | bytes 1572872 | tf_op jit(solution)/shard_map/ppermute | solution.py:31
  122.7 13.6 %collective-permute-start.25 = (f32[3,2,1024]{2,1,0:T(2,128)S(1)}, f32[3,2,1024]{2,1,0:T(2,128)S(1)}, u32[]{:S(2)}, u32[]{:S(2)}) collective-permute-start(f32[3,2,1024]{2,1,0:T(2,128)S(1)} %get-tuple-element.54), channel_id=1, source_target_pairs={{0,1},{1,0},{2,3},{3,2},{4,5},{5,4},{6,7},{7,6},{8,9},{9,8},{10,11... | collective-permute-start | bytes 73736 | tf_op jit(solution)/shard_map/ppermute | solution.py:31
  123.0 13.2 %collective-permute-start.26 = (f32[3,2,1024]{2,1,0:T(2,128)S(1)}, f32[3,2,1024]{2,1,0:T(2,128)S(1)}, u32[]{:S(2)}, u32[]{:S(2)}) collective-permute-start(f32[3,2,1024]{2,1,0:T(2,128)S(1)} %get-tuple-element.53), channel_id=1, source_target_pairs={{0,2},{1,3},{2,0},{3,1},{4,6},{5,7},{6,4},{7,5},{8,10},{9,11},{10,... | collective-permute-start | bytes 73736 | tf_op jit(solution)/shard_map/ppermute | solution.py:31
  125.3 13.2 %collective-permute-start.27 = (f32[3,2,1024]{2,1,0:T(2,128)S(1)}, f32[3,2,1024]{2,1,0:T(2,128)S(1)}, u32[]{:S(2)}, u32[]{:S(2)}) collective-permute-start(f32[3,2,1024]{2,1,0:T(2,128)S(1)} %get-tuple-element.52), channel_id=1, source_target_pairs={{0,3},{1,2},{2,1},{3,0},{4,7},{5,6},{6,5},{7,4},{8,11},{9,10},{10,... | collective-permute-start | bytes 73736 | tf_op jit(solution)/shard_map/ppermute | solution.py:31
  (12 other events, 187.7 us)

commit v14 on v13

--- a/solution.py
+++ b/solution.py
@@ -191,18 +191,20 @@
     for needed, copy in copies:
         pl.when(needed)(copy.wait)
     if joins:
+        if out_ref.shape[0] > 2 * count:
+            out_ref[2 * count :] = jnp.zeros_like(out_ref[2 * count :])
         half = jnp.where(inner, flips[1] % 2, flips[0] % 2)
         out_ref[pl.ds(pl.multiple_of((1 - half) * count, count), count)] = earlier_ref[...]
         out_ref = out_ref.at[pl.ds(pl.multiple_of(half * count, count), count)]
     attend(query, window_ref, bias_ref, scores_ref, weights_ref, out_ref)
 
 
-def attend_block(place, starts, ends, query, keyval, flips, name, last=(), halo=(), earlier=()):
+def attend_block(place, starts, ends, query, keyval, flips, name, last=(), halo=(), earlier=(), spare=0):
     rows = query.shape[0] // lax.axis_size("kv")
     heads_width = query.shape[1]
     return pl.pallas_call(
         functools.partial(attend_kernel, flips, bool(last), bool(halo), bool(earlier)),
-        out_shape=jax.ShapeDtypeStruct(((1 + len(earlier)) * rows, heads_width), BF16),
+        out_shape=jax.ShapeDtypeStruct(((1 + len(earlier)) * rows + spare, heads_width), BF16),
         in_specs=[SMEM, VMEM, VMEM, VMEM, ANY] + [VMEM, ANY][: len(last)] + [ANY] * len(halo) + [VMEM] * len(earlier),
         out_specs=VMEM,
         scratch_shapes=[
@@ -473,12 +475,10 @@
     small = jnp.concatenate([out_part, dec_query], axis=0)
     others = [swapped(small, "kv", flip) for flip in range(1, kvs)]
     a2, b2 = lax.ppermute(b1, "kv", outward), over_edges(a1, "kv", 1)
-    queries = jnp.concatenate([dec_query] + [other[depth:] for other in others], axis=0).astype(F32)
-    partial = decode_partial(queries, dec_query.shape[0], kv_cache, piece_req, piece_used)
-    out_here = jnp.stack([other[:depth] for other in others])
+    out_here = after(jnp.stack([other[:depth] for other in others]), b2)
     out_x, out_y = swapped(out_here, "tok", 2), swapped(out_here, "tok", 4)
-    a3 = lax.ppermute(after(b2, partial), "kv", outward)
-    out_far = swapped(out_here, "tok", 6)
+    a3 = lax.ppermute(b2, "kv", outward)
+    out_far = swapped(out_y, "tok", 2)
     inner = (kv == 1) | (kv == 2)
 
     order = jnp.arange(stretch_len.shape[0])
@@ -491,28 +491,36 @@
     block = (place, starts, ends, query, keyval)
     one = attend_block(*block, (1, 0), "attend_early")
 
-    feed_part = jnp.concatenate([eighth(up_weight), eighth(down_weight)], axis=0)
-    feed_inner = lax.ppermute(after(feed_part, query), "kv", [(0, 2), (3, 1)])
-    feed_outer = lax.ppermute(after(feed_part, a3, one, feed_inner), "kv", [(1, 3), (2, 0)])
-
-    *last, even, odd = project_last(place, weight, keyval, after(a3, out_x, out_y, out_far))
+    feed_up, feed_down = after((eighth(up_weight), eighth(down_weight)), a2, b2)
+    inner_up = lax.ppermute(feed_up, "kv", [(0, 2), (3, 1)])
+    inner_down = lax.ppermute(feed_down, "kv", [(0, 2), (3, 1)])
+    feed_part = jnp.concatenate([feed_up, feed_down], axis=0)
+    feed_part = after(feed_part, a3, one, out_x, out_y, inner_up, inner_down)
+    feed_outer = lax.ppermute(feed_part, "kv", [(1, 3), (2, 0)])
+    feed_inner = jnp.concatenate([inner_up, inner_down], axis=0)
+
+    *last, even, odd = project_last(place, weight, keyval, a3)
     halo = over_edges(even, "tok", 0), over_edges(odd, "tok", 1)
     two = attend_block(*block, (2, 3), "attend_last", last)
     out_all = jnp.stack([out_here, out_x, out_y, out_far])
     out_core = swapped(out_all, "tok", 1)
-    far = attend_block(*block, (3, 2), "attend_far", last, halo, (two,))
+    feed_here = jnp.where(inner, feed_inner, after(feed_outer, two))
+    feed_x, feed_y = swapped(feed_here, "tok", 2), swapped(feed_here, "tok", 4)
+    block = (place, starts, ends, after(query, feed_here, out_core), keyval)
+    far = attend_block(*block, (3, 2), "attend_far", last, halo, (two,), 16)
     far_heads = swapped(far, "kv", 2)
-    block = (place, starts, ends, after(query, far, out_core), keyval)
+    block = (place, starts, ends, after(query, far), keyval)
     near = attend_block(*block, (0, 1), "attend_near", last, halo, (one,))
-    feed_here = jnp.where(inner, feed_inner, after(feed_outer, near))
-    feed_x, feed_y = swapped(feed_here, "tok", 2), swapped(feed_here, "tok", 4)
     partner_heads, passed_heads = swapped(near, "kv", 1), swapped(far_heads, "kv", 1)
     parts = (near, partner_heads, far_heads, passed_heads)
 
     out_pieces = [((0, 2, 4, 6), out_all), ((1, 3, 5, 7), out_core)]
+    queries = jnp.concatenate([dec_query] + [other[depth:] for other in others], axis=0)
+    queries = after(queries, near).astype(F32)
+    partial = decode_partial(queries, dec_query.shape[0], kv_cache, piece_req, piece_used)
     half = feed_here.shape[0] // 2
-    far_up = swapped(after(feed_y, far_heads, partner_heads)[:half], "tok", 2)
-    far_down = swapped(after(feed_x, far_heads, partner_heads)[half:], "tok", 4)
+    far_up = swapped(after(feed_y, far_heads, partner_heads, partial)[:half], "tok", 2)
+    far_down = swapped(after(feed_x, far_heads, partner_heads, partial)[half:], "tok", 4)
     held = jnp.concatenate([feed_here, feed_x, feed_y, far_up, far_down], axis=0)
     feed_pieces = (held, swapped(after(held, passed_heads), "tok", 1))
 

time: 141 us -> 139 us (0.986)
  starting transfers between devices: 47.4 us -> 40.7 us
  local copies, waits for them, and re-layouts: 3 us -> 9.29 us
  other arithmetic: 4.46 us -> 8.83 us
  waiting for transfers between devices: 49.7 us -> 45.5 us
  Pallas kernels: 34.6 us -> 32.9 us
    ppermute x19, waiting for transfers between devices: 40.1 us -> 30.4 us  [swapped(): return lax.ppermute(value, axis, [(i, i ^ flip) for i in range(count)])]
    ppermute x19, starting transfers between devices: 29.6 us -> 21.6 us  [swapped(): return lax.ppermute(value, axis, [(i, i ^ flip) for i in range(count)])]
    unnamed x35 -> x53, local copies, waits for them, and re-layouts: 0.96 us -> 6.57 us
    ppermute x1, waiting for transfers between devices: 3.69 us -> 7.97 us  [routed_body(): a2, b2 = (lax.ppermute(b1, 'kv', outward), over_edges(a1, 'kv', 1))]
    another operation x2 -> x1, other arithmetic: 0.14 us -> 2.05 us  [routed_body(): out_all = jnp.stack([out_here, out_x, out_y, out_far])]
    ppermute x5, waiting for transfers between devices: 0.01 us -> 1.76 us  [over_edges(): return lax.ppermute(value, axis, edges + [(j, i) for i, j in edges])]
    ppermute x3 -> x4, starting transfers between devices: 10.6 us -> 11.3 us  [the longest x1 6.7 us: routed_body(): inner_up = lax.ppermute(feed_up, 'kv', [(0, 2), (3, 1)])]
    ppermute x3 -> x4, waiting for transfers between devices: 5.95 us -> 5.36 us  [the longest x1 5.35 us: routed_body(): feed_outer = lax.ppermute(feed_part, 'kv', [(1, 3), (2, 0)])]
  transfers between devices with their start and end apart: 28 -> 29, of which waited for: 11 -> 10; matrix products, arithmetic and copies ran while one was open for 4% -> 8% of each run, Pallas kernels for 21% -> 20%
where the time goes in v14:
time: 139 us; the launch traced here: 138 us
  waiting for transfers between devices  45.5 us (33%)
  starting transfers between devices  40.7 us (29%)
  Pallas kernels  32.9 us (24%)
  local copies, waits for them, and re-layouts  9.29 us (7%)
  other arithmetic  8.83 us (6%)
    ppermute x19, waiting for transfers between devices, swapped(): return lax.ppermute(value, axis, [(i, i ^ flip) for i in range(count)])  30.4 us
    ppermute x19, starting transfers between devices, swapped(): return lax.ppermute(value, axis, [(i, i ^ flip) for i in range(count)])  21.6 us
    pallas_call x4, Pallas kernels, attend_block(): pl.pallas_call(functools.partial(attend_kernel, flips, bool(last), bool(h...  11.7 us
    ppermute x1, waiting for transfers between devices, routed_body(): a2, b2 = (lax.ppermute(b1, 'kv', outward), over_edges(a1, 'kv', 1))  7.97 us
    pallas_call x2, Pallas kernels, feed(): pl.pallas_call(feed_kernel, out_shape=jax.ShapeDtypeStruct((count, width)...  7.8 us
    ppermute x1, starting transfers between devices, routed_body(): inner_up = lax.ppermute(feed_up, 'kv', [(0, 2), (3, 1)])  6.7 us
    unnamed x53, local copies, waits for them, and re-layouts  6.57 us
    ppermute x5, starting transfers between devices, over_edges(): return lax.ppermute(value, axis, edges + [(j, i) for i, j in edges])  6.48 us
  transfers between devices with their start and end apart: 29, of which 10 were waited for; matrix products, arithmetic and copies ran while one was open for 8% of the time, Pallas kernels for 20%

profile of v14, /device:TPU:0, one launch (start us, length us, event | category | flops | bytes accessed | tf_op | source)
XLA Modules:
  0.0 138.5 jit_solution(16838694264333595598)
XLA Ops:
  0.7 3.1 %collective-permute-start = (bf16[256,1024]{1,0:T(8,128)(2,1)}, bf16[256,1024]{1,0:T(8,128)(2,1)S(1)}, u32[]{:S(2)}, u32[]{:S(2)}) collective-permute-start(bf16[256,1024]{1,0:T(8,128)(2,1)} %own_ref.1), channel_id=1, source_target_pairs={{0,1},{2,3},{1,0},{3,2},{4,5},{6,7},{5,4},{7,6},{8,9},{10,11},{9,8... | collective-permute-start | bytes 1572872 | tf_op jit(solution)/shard_map/ppermute | solution.py:37
  6.6 2.5 %collective-permute-start.9 = (bf16[34,1024]{1,0:T(8,128)(2,1)}, bf16[34,1024]{1,0:T(8,128)(2,1)S(1)}, u32[]{:S(2)}, u32[]{:S(2)}) collective-permute-start(bf16[34,1024]{1,0:T(8,128)(2,1)} %pad_maximum_fusion.3), channel_id=1, source_target_pairs={{0,3},{1,2},{2,1},{3,0},{4,7},{5,6},{6,5},{7,4},{8,11},{9,10},{10,... | collective-permute-start | bytes 208904 | tf_op jit(solution)/shard_map/ppermute | solution.py:31
  9.1 3.4 %collective-permute-start.8 = (bf16[34,1024]{1,0:T(8,128)(2,1)}, bf16[34,1024]{1,0:T(8,128)(2,1)S(1)}, u32[]{:S(2)}, u32[]{:S(2)}) collective-permute-start(bf16[34,1024]{1,0:T(8,128)(2,1)} %pad_maximum_fusion.3), channel_id=1, source_target_pairs={{0,2},{1,3},{2,0},{3,1},{4,6},{5,7},{6,4},{7,5},{8,10},{9,11},{10,... | collective-permute-start | bytes 208904 | tf_op jit(solution)/shard_map/ppermute | solution.py:31
  12.4 1.8 %constant_dynamic-slice_fusion.1 = (bf16[128,1024]{1,0:T(8,128)(2,1)S(1)}, bf16[128,1024]{1,0:T(8,128)(2,1)}) fusion(bf16[1024,1024]{1,0:T(8,128)(2,1)} %down_near_ref.3, s32[]{:T(128)S(6)} %select_n.33, bf16[1024,1024]{1,0:T(8,128)(2,1)} %up_near_ref.3), kind=kLoop, calls=%fused_computation.49 | loop fusion | bytes 1048580 | tf_op jit(solution)/shard_map/dynamic_slice | solution.py:469
  15.0 1.8 %collective-permute-done.a1.partner_ref = bf16[256,1024]{1,0:T(8,128)(2,1)S(1)} collective-permute-done((bf16[256,1024]{1,0:T(8,128)(2,1)}, bf16[256,1024]{1,0:T(8,128)(2,1)S(1)}, u32[]{:S(2)}, u32[]{:S(2)}) %collective-permute-start) | collective-permute-done | bytes 524320 | tf_op jit(solution)/shard_map/ppermute | solution.py:37
  18.2 2.8 %collective-permute-done.9 = bf16[34,1024]{1,0:T(8,128)(2,1)S(1)} collective-permute-done((bf16[34,1024]{1,0:T(8,128)(2,1)}, bf16[34,1024]{1,0:T(8,128)(2,1)S(1)}, u32[]{:S(2)}, u32[]{:S(2)}) %collective-permute-start.9) | collective-permute-done | bytes 69664 | tf_op jit(solution)/shard_map/ppermute | solution.py:31
  23.2 5.1 %collective-permute-done.8 = bf16[34,1024]{1,0:T(8,128)(2,1)S(1)} collective-permute-done((bf16[34,1024]{1,0:T(8,128)(2,1)}, bf16[34,1024]{1,0:T(8,128)(2,1)S(1)}, u32[]{:S(2)}, u32[]{:S(2)}) %collective-permute-start.8) | collective-permute-done | bytes 69664 | tf_op jit(solution)/shard_map/ppermute | solution.py:31
  30.9 8.0 %collective-permute-done.2.a2 = bf16[256,1024]{1,0:T(8,128)(2,1)S(1)} collective-permute-done((bf16[256,1024]{1,0:T(8,128)(2,1)S(1)}, bf16[256,1024]{1,0:T(8,128)(2,1)S(1)}, u32[]{:S(2)}, u32[]{:S(2)}) %collective-permute-start.2) | collective-permute-done | bytes 524320 | tf_op jit(solution)/shard_map/ppermute | solution.py:477
  39.7 1.5 %collective-permute-start.11 = (bf16[3,32,1024]{2,1,0:T(8,128)(2,1)}, bf16[3,32,1024]{2,1,0:T(8,128)(2,1)}, u32[]{:S(2)}, u32[]{:S(2)}) collective-permute-start(bf16[3,32,1024]{2,1,0:T(8,128)(2,1)} %pad_maximum_fusion.2), channel_id=1, source_target_pairs={{0,16},{4,20},{8,24},{12,28},{16,0},{20,4},{24,8},{28,12},{1,17},{... | collective-permute-start | bytes 589832 | tf_op jit(solution)/shard_map/ppermute | solution.py:31
  41.2 6.7 %collective-permute-start.4 = (bf16[128,1024]{1,0:T(8,128)(2,1)}, bf16[128,1024]{1,0:T(8,128)(2,1)}, u32[]{:S(2)}, u32[]{:S(2)}) collective-permute-start(bf16[128,1024]{1,0:T(8,128)(2,1)} %get-tuple-element.28), channel_id=1, source_target_pairs={{0,2},{3,1},{4,6},{7,5},{8,10},{11,9},{12,14},{15,13},{16,18},{19,... | collective-permute-start | bytes 786440 | tf_op jit(solution)/shard_map/ppermute | solution.py:495
  47.9 2.0 %collective-permute-start.5 = (bf16[128,1024]{1,0:T(8,128)(2,1)S(1)}, bf16[128,1024]{1,0:T(8,128)(2,1)}, u32[]{:S(2)}, u32[]{:S(2)}) collective-permute-start(bf16[128,1024]{1,0:T(8,128)(2,1)S(1)} %get-tuple-element.29), channel_id=1, source_target_pairs={{0,2},{3,1},{4,6},{7,5},{8,10},{11,9},{12,14},{15,13},{16,18},{19,... | collective-permute-start | bytes 786440 | tf_op jit(solution)/shard_map/ppermute | solution.py:496
  49.9 1.5 %collective-permute-start.10 = (bf16[3,32,1024]{2,1,0:T(8,128)(2,1)}, bf16[3,32,1024]{2,1,0:T(8,128)(2,1)S(1)}, u32[]{:S(2)}, u32[]{:S(2)}) collective-permute-start(bf16[3,32,1024]{2,1,0:T(8,128)(2,1)} %pad_maximum_fusion.2), channel_id=1, source_target_pairs={{0,8},{4,12},{8,0},{12,4},{16,24},{20,28},{24,16},{28,20},{1,9},{5... | collective-permute-start | bytes 589832 | tf_op jit(solution)/shard_map/ppermute | solution.py:31
  56.2 2.5 %project_early.1 = (bf16[1024,256]{1,0:T(8,128)(2,1)S(1)}, bf16[1024,512]{1,0:T(8,128)(2,1)S(1)}) custom-call(s32[2]{0:T(128)S(1)} %pad_add_fusion.place_ref, bf16[3,1024,256]{2,1,0:T(8,128)(2,1)S(1)} %bitcast.142, bf16[256,1024]{1,0:T(8,128)(2,1)S(1)} %copy-done.4, bf16[256,1024]{1,0:T(8,128)(2,1)S(1)} %copy-done.7, bf16[256,1024]{1,0:T(8,128)(2,1)S(1)} %copy-done.13, ...), custom_call_target="tpu_custom_call" | custom-call | flops 1 | bytes 1 | tf_op jit(solution)/shard_map/project_early/pallas_call | solution.py:91
  58.7 2.8 %attend_early.1.refs_4_ = bf16[256,256]{1,0:T(8,128)(2,1)S(1)} custom-call(s32[2]{0:T(128)S(1)} %pad_add_fusion.place_ref, s32[1,48]{1,0:T(1,128)S(1)} %subtract_bitcast_fusion.starts_ref, s32[1,48]{1,0:T(1,128)S(1)} %bitcast.144, bf16[1024,256]{1,0:T(8,128)(2,1)S(1)} %get-tuple-element.39.query_ref, bf16[1024,512]{1,0:T(8,128)(2,1)S(1)} %get-tuple-element.30.keyval_ref), custom_call_target="tpu_custom_call" | custom-call | flops 1 | bytes 1 | tf_op jit(solution)/shard_map/attend_early/pallas_call | solution.py:205
  61.5 1.8 %pad_maximum_fusion.1 = bf16[256,1024]{1,0:T(8,128)(2,1)} fusion(bf16[128,1024]{1,0:T(8,128)(2,1)S(1)} %get-tuple-element.29, bf16[128,1024]{1,0:T(8,128)(2,1)} %get-tuple-element.28), kind=kLoop, calls=%fused_computation.2 | loop fusion | flops 1048576 | bytes 1048576 | tf_op jit(solution)/shard_map/concatenate | solution.py:497
  64.7 2.0 %pad_maximum_fusion.refs_4_ = bf16[4,3,32,1024]{3,2,1,0:T(8,128)(2,1)} fusion(bf16[1,3,32,1024]{3,2,1,0:T(8,128)(2,1)S(1)} %bitcast.154, bf16[1,3,32,1024]{3,2,1,0:T(8,128)(2,1)} %bitcast.12, bf16[1,3,32,1024]{3,2,1,0:T(8,128)(2,1)S(1)} %bitcast.153, bf16[1,3,32,1024]{3,2,1,0:T(8,128)(2,1)} %bitcast.10), kind=kLoop, calls=%fused_computation | loop fusion | flops 1179648 | bytes 1572864 | tf_op jit(solution)/shard_map/stack | solution.py:505
  66.7 1.6 %project_last.1 = (bf16[256,256]{1,0:T(8,128)(2,1)S(1)}, bf16[256,512]{1,0:T(8,128)(2,1)S(1)}, bf16[256,512]{1,0:T(8,128)(2,1)S(1)}, bf16[256,512]{1,0:T(8,128)(2,1)S(1)}) custom-call(s32[2]{0:T(128)S(1)} %pad_add_fusion.place_ref, bf16[3,1024,256]{2,1,0:T(8,128)(2,1)S(1)} %bitcast.143, bf16[1024,512]{1,0:T(8,128)(2,1)S(1)} %get-tuple-element.30.keyval_ref, ...), custom_call_target="tpu_custom_call" | custom-call | flops 1 | bytes 1 | tf_op jit(solution)/shard_map/project_last/pallas_call | solution.py:110
  69.6 2.9 %attend_last.1.refs_4_ = bf16[256,256]{1,0:T(8,128)(2,1)S(1)} custom-call(s32[2]{0:T(128)S(1)} %pad_add_fusion.place_ref, s32[1,48]{1,0:T(1,128)S(1)} %subtract_bitcast_fusion.starts_ref, s32[1,48]{1,0:T(1,128)S(1)} %bitcast.145, bf16[1024,256]{1,0:T(8,128)(2,1)S(1)} %get-tuple-element.39.query_ref, bf16[1024,512]{1,0:T(8,128)(2,1)S(1)} %get-tuple-element.30.keyval_ref, ...), custom_call_target="tpu_custom_call" | custom-call | flops 1 | bytes 1 | tf_op jit(solution)/shard_map/attend_last/pallas_call | solution.py:205
  72.5 5.3 %collective-permute-done.12 = bf16[256,1024]{1,0:T(8,128)(2,1)} collective-permute-done((bf16[256,1024]{1,0:T(8,128)(2,1)}, bf16[256,1024]{1,0:T(8,128)(2,1)}, u32[]{:S(2)}, u32[]{:S(2)}) %collective-permute-start.12) | collective-permute-done | bytes 524320 | tf_op jit(solution)/shard_map/ppermute | solution.py:499
  79.8 1.5 %collective-permute-start.20 = (bf16[256,1024]{1,0:T(8,128)(2,1)S(1)}, bf16[256,1024]{1,0:T(8,128)(2,1)S(1)}, u32[]{:S(2)}, u32[]{:S(2)}) collective-permute-start(bf16[256,1024]{1,0:T(8,128)(2,1)S(1)} %get-tuple-element.53), channel_id=1, source_target_pairs={{0,8},{4,12},{8,0},{12,4},{16,24},{20,28},{24,16},{28,20},{1,9},{5... | collective-permute-start | bytes 1572872 | tf_op jit(solution)/shard_map/ppermute | solution.py:31
  81.4 2.9 %attend_far.1 = bf16[528,256]{1,0:T(8,128)(2,1)S(1)} custom-call(s32[2]{0:T(128)S(1)} %pad_add_fusion.place_ref, s32[1,48]{1,0:T(1,128)S(1)} %subtract_bitcast_fusion.starts_ref, s32[1,48]{1,0:T(1,128)S(1)} %bitcast.146, bf16[1024,256]{1,0:T(8,128)(2,1)S(1)} %get-tuple-element.39.query_ref, bf16[1024,512]{1,0:T(8,128)(2,1)S(1)} %get-tuple-element.30.keyval_ref, ...), custom_call_target="tpu_custom_call" | custom-call | flops 1 | bytes 1 | tf_op jit(solution)/shard_map/attend_far/pallas_call | solution.py:205
  85.1 3.1 %attend_near.1.refs_0_ = bf16[512,256]{1,0:T(8,128)(2,1)S(1)} custom-call(s32[2]{0:T(128)S(1)} %pad_add_fusion.place_ref, s32[1,48]{1,0:T(1,128)S(1)} %subtract_bitcast_fusion.starts_ref, s32[1,48]{1,0:T(1,128)S(1)} %bitcast.147, bf16[1024,256]{1,0:T(8,128)(2,1)S(1)} %get-tuple-element.39.query_ref, bf16[1024,512]{1,0:T(8,128)(2,1)S(1)} %get-tuple-element.30.keyval_ref, ...), custom_call_target="tpu_custom_call" | custom-call | flops 1 | bytes 1 | tf_op jit(solution)/shard_map/attend_near/pallas_call | solution.py:205
  89.7 3.8 %decode.1 = f32[3,8,1024]{2,1,0:T(8,128)S(1)} custom-call(s32[6]{0:T(128)S(1)} %fusion.12.slot_ref, s32[6]{0:T(128)S(1)} %bitcast.152, f32[8,1024]{1,0:T(8,128)S(1)} %convert_element_type.6.query_ref, bf16[2,1,6,128,1024]{4,3,2,1,0:T(8,128)(2,1)S(1)} %copy-done.3), custom_call_target="tpu_custom_call" | custom-call | flops 1 | bytes 1 | tf_op jit(solution)/shard_map/decode/pallas_call | solution.py:409
  93.6 9.0 %collective-permute-done.17.refs_1_ = bf16[512,256]{1,0:T(8,128)(2,1)S(1)} collective-permute-done((bf16[512,256]{1,0:T(8,128)(2,1)S(1)}, bf16[512,256]{1,0:T(8,128)(2,1)S(1)}, u32[]{:S(2)}, u32[]{:S(2)}) %collective-permute-start.17) | collective-permute-done | bytes 262176 | tf_op jit(solution)/shard_map/ppermute | solution.py:31
  102.6 1.6 %collective-permute-start.22 = (bf16[128,1024]{1,0:T(8,128)(2,1)S(1)}, bf16[128,1024]{1,0:T(8,128)(2,1)S(1)}, u32[]{:S(2)}, u32[]{:S(2)}) collective-permute-start(bf16[128,1024]{1,0:T(8,128)(2,1)S(1)} %slice.82), channel_id=1, source_target_pairs={{0,8},{4,12},{8,0},{12,4},{16,24},{20,28},{24,16},{28,20},{1,9},{5... | collective-permute-start | bytes 786440 | tf_op jit(solution)/shard_map/ppermute | solution.py:31
  104.4 6.7 %collective-permute-done.22 = bf16[128,1024]{1,0:T(8,128)(2,1)S(1)} collective-permute-done((bf16[128,1024]{1,0:T(8,128)(2,1)S(1)}, bf16[128,1024]{1,0:T(8,128)(2,1)S(1)}, u32[]{:S(2)}, u32[]{:S(2)}) %collective-permute-start.22) | collective-permute-done | bytes 262176 | tf_op jit(solution)/shard_map/ppermute | solution.py:31
  112.4 4.3 %first_norm.1 = (bf16[256,1024]{1,0:T(8,128)(2,1)S(1)}, bf16[256,1024]{1,0:T(8,128)(2,1)S(1)}) custom-call(s32[2]{0:T(128)S(1)} %pad_add_fusion.place_ref, bf16[256,1024]{1,0:T(8,128)(2,1)S(1)} %copy-done.5, bf16[256,1024]{1,0:T(8,128)(2,1)S(1)} %copy-done.8, bf16[256,1024]{1,0:T(8,128)(2,1)S(1)} %copy-done.9, f32[1,1024]{1,0:T(1,128)S(1)} %bitcast.150, ...), custom_call_target="tpu_custom_call" | custom-call | flops 1 | bytes 1 | tf_op jit(solution)/shard_map/first_norm/pallas_call | solution.py:258
  116.7 3.9 %feed_partner.1 = bf16[256,1024]{1,0:T(8,128)(2,1)S(1)} custom-call(s32[2]{0:T(128)S(1)} %pad_add_fusion.place_ref, bf16[256,1024]{1,0:T(8,128)(2,1)S(1)} %get-tuple-element.41.rows_ref, bf16[1024,1024]{1,0:T(8,128)(2,1)S(1)} %copy-done, bf16[1024,1024]{1,0:T(8,128)(2,1)S(1)} %copy-done.1, bf16[1024,1024]{1,0:T(8,128)(2,1)S(1)} %constant_dynamic-update-slice_fusion.held_ref, ...), custom_call_target="tpu_custom_call" | custom-call | flops 1 | bytes 1 | tf_op jit(solution)/shard_map/feed_partner/pallas_call | solution.py:327
  120.6 1.8 %collective-permute-start.25 = (bf16[256,1024]{1,0:T(8,128)(2,1)S(1)}, bf16[256,1024]{1,0:T(8,128)(2,1)S(1)}, u32[]{:S(2)}, u32[]{:S(2)}) collective-permute-start(bf16[256,1024]{1,0:T(8,128)(2,1)S(1)} %feed_partner.1), channel_id=1, source_target_pairs={{0,1},{1,0},{2,3},{3,2},{4,5},{5,4},{6,7},{7,6},{8,9},{9,8},{10,11... | collective-permute-start | bytes 1572872 | tf_op jit(solution)/shard_map/ppermute | solution.py:31
  122.8 4.1 %collective-permute-start.28 = (f32[3,2,1024]{2,1,0:T(2,128)S(1)}, f32[3,2,1024]{2,1,0:T(2,128)S(1)}, u32[]{:S(2)}, u32[]{:S(2)}) collective-permute-start(f32[3,2,1024]{2,1,0:T(2,128)S(1)} %get-tuple-element.54), channel_id=1, source_target_pairs={{0,3},{1,2},{2,1},{3,0},{4,7},{5,6},{6,5},{7,4},{8,11},{9,10},{10,... | collective-permute-start | bytes 73736 | tf_op jit(solution)/shard_map/ppermute | solution.py:31
  126.9 3.9 %feed_own.1.near_ref = f32[256,1024]{1,0:T(8,128)S(1)} custom-call(s32[2]{0:T(128)S(1)} %pad_add_fusion.place_ref, bf16[256,1024]{1,0:T(8,128)(2,1)S(1)} %get-tuple-element.46.rows_ref.normed_ref, bf16[1024,1024]{1,0:T(8,128)(2,1)S(1)} %copy-done, bf16[1024,1024]{1,0:T(8,128)(2,1)S(1)} %copy-done.1, ...), custom_call_target="tpu_custom_call" | custom-call | flops 1 | bytes 1 | tf_op jit(solution)/shard_map/feed_own/pallas_call | solution.py:327
  130.8 5.7 %collective-permute-done.26 = f32[3,2,1024]{2,1,0:T(2,128)S(1)} collective-permute-done((f32[3,2,1024]{2,1,0:T(2,128)S(1)}, f32[3,2,1024]{2,1,0:T(2,128)S(1)}, u32[]{:S(2)}, u32[]{:S(2)}) %collective-permute-start.26) | collective-permute-done | bytes 24608 | tf_op jit(solution)/shard_map/ppermute | solution.py:31
  (117 shorter events, 25.9 us)
Async XLA Ops:
  0.6 49.2 %copy-start.23 = (s32[48]{0:T(128)S(1)}, s32[48]{0:T(128)}, u32[]{:S(2)}) copy-start(s32[48]{0:T(128)} %param.16) | copy-start | bytes 580
  0.6 51.3 %copy-start.2 = (bf16[1024,3,256]{2,0,1:T(8,128)(2,1)S(1)}, bf16[1024,3,256]{2,0,1:T(8,128)(2,1)}, u32[]{:S(2)}) copy-start(bf16[1024,3,256]{2,0,1:T(8,128)(2,1)} %param.15) | copy-start | bytes 4718596
  0.7 16.1 %collective-permute-start = (bf16[256,1024]{1,0:T(8,128)(2,1)}, bf16[256,1024]{1,0:T(8,128)(2,1)S(1)}, u32[]{:S(2)}, u32[]{:S(2)}) collective-permute-start(bf16[256,1024]{1,0:T(8,128)(2,1)} %own_ref.1), channel_id=1, source_target_pairs={{0,1},{2,3},{1,0},{3,2},{4,5},{6,7},{5,4},{7,6},{8,9},{10,11},{9,8... | collective-permute-start | bytes 1572872 | tf_op jit(solution)/shard_map/ppermute | solution.py:37
  3.7 17.3 %collective-permute-start.1 = (bf16[256,1024]{1,0:T(8,128)(2,1)}, bf16[256,1024]{1,0:T(8,128)(2,1)S(1)}, u32[]{:S(2)}, u32[]{:S(2)}) collective-permute-start(bf16[256,1024]{1,0:T(8,128)(2,1)} %own_ref.1), channel_id=1, source_target_pairs={{1,2},{2,1},{5,6},{6,5},{9,10},{10,9},{13,14},{14,13},{17,18},{18,... | collective-permute-start | bytes 1572872 | tf_op jit(solution)/shard_map/ppermute | solution.py:37
  6.6 14.4 %collective-permute-start.9 = (bf16[34,1024]{1,0:T(8,128)(2,1)}, bf16[34,1024]{1,0:T(8,128)(2,1)S(1)}, u32[]{:S(2)}, u32[]{:S(2)}) collective-permute-start(bf16[34,1024]{1,0:T(8,128)(2,1)} %pad_maximum_fusion.3), channel_id=1, source_target_pairs={{0,3},{1,2},{2,1},{3,0},{4,7},{5,6},{6,5},{7,4},{8,11},{9,10},{10,... | collective-permute-start | bytes 208904 | tf_op jit(solution)/shard_map/ppermute | solution.py:31
  9.1 19.2 %collective-permute-start.8 = (bf16[34,1024]{1,0:T(8,128)(2,1)}, bf16[34,1024]{1,0:T(8,128)(2,1)S(1)}, u32[]{:S(2)}, u32[]{:S(2)}) collective-permute-start(bf16[34,1024]{1,0:T(8,128)(2,1)} %pad_maximum_fusion.3), channel_id=1, source_target_pairs={{0,2},{1,3},{2,0},{3,1},{4,6},{5,7},{6,4},{7,5},{8,10},{9,11},{10,... | collective-permute-start | bytes 208904 | tf_op jit(solution)/shard_map/ppermute | solution.py:31
  12.4 16.4 %collective-permute-start.7 = (bf16[34,1024]{1,0:T(8,128)(2,1)}, bf16[34,1024]{1,0:T(8,128)(2,1)S(1)}, u32[]{:S(2)}, u32[]{:S(2)}) collective-permute-start(bf16[34,1024]{1,0:T(8,128)(2,1)} %pad_maximum_fusion.3), channel_id=1, source_target_pairs={{0,1},{1,0},{2,3},{3,2},{4,5},{5,4},{6,7},{7,6},{8,9},{9,8},{10,11... | collective-permute-start | bytes 208904 | tf_op jit(solution)/shard_map/ppermute | solution.py:31
  16.7 35.3 %copy-start.6 = (bf16[256,1024]{1,0:T(8,128)(2,1)}, bf16[256,1024]{1,0:T(8,128)(2,1)S(1)}, u32[]{:S(2)}) copy-start(bf16[256,1024]{1,0:T(8,128)(2,1)S(1)} %collective-permute-done.a1.partner_ref) | copy-start | bytes 1572868
  16.7 12.2 %collective-permute-start.3 = (bf16[256,1024]{1,0:T(8,128)(2,1)S(1)}, bf16[256,1024]{1,0:T(8,128)(2,1)}, u32[]{:S(2)}, u32[]{:S(2)}) collective-permute-start(bf16[256,1024]{1,0:T(8,128)(2,1)S(1)} %collective-permute-done.a1.partner_ref), channel_id=1, source_target_pairs={{1,2},{2,1},{5,6},{6,5},{9,10},{10,9},{13,14},{14,13},{17,18},{18,... | collective-permute-start | bytes 1572872 | tf_op jit(solution)/shard_map/ppermute | solution.py:37
  21.0 17.8 %collective-permute-start.2 = (bf16[256,1024]{1,0:T(8,128)(2,1)S(1)}, bf16[256,1024]{1,0:T(8,128)(2,1)S(1)}, u32[]{:S(2)}, u32[]{:S(2)}) collective-permute-start(bf16[256,1024]{1,0:T(8,128)(2,1)S(1)} %collective-permute-done.1.b1), channel_id=1, source_target_pairs={{1,0},{2,3},{5,4},{6,7},{9,8},{10,11},{13,12},{14,15},{17,16},{18,... | collective-permute-start | bytes 1572872 | tf_op jit(solution)/shard_map/ppermute | solution.py:477
  28.9 34.5 %collective-permute-start.6 = (bf16[256,1024]{1,0:T(8,128)(2,1)}, bf16[256,1024]{1,0:T(8,128)(2,1)}, u32[]{:S(2)}, u32[]{:S(2)}) collective-permute-start(bf16[256,1024]{1,0:T(8,128)(2,1)} %collective-permute-done.3.b2), channel_id=1, source_target_pairs={{1,0},{2,3},{5,4},{6,7},{9,8},{10,11},{13,12},{14,15},{17,16},{18,... | collective-permute-start | bytes 1572872 | tf_op jit(solution)/shard_map/ppermute | solution.py:480
  39.7 11.7 %collective-permute-start.11 = (bf16[3,32,1024]{2,1,0:T(8,128)(2,1)}, bf16[3,32,1024]{2,1,0:T(8,128)(2,1)}, u32[]{:S(2)}, u32[]{:S(2)}) collective-permute-start(bf16[3,32,1024]{2,1,0:T(8,128)(2,1)} %pad_maximum_fusion.2), channel_id=1, source_target_pairs={{0,16},{4,20},{8,24},{12,28},{16,0},{20,4},{24,8},{28,12},{1,17},{... | collective-permute-start | bytes 589832 | tf_op jit(solution)/shard_map/ppermute | solution.py:31
  41.2 22.2 %collective-permute-start.4 = (bf16[128,1024]{1,0:T(8,128)(2,1)}, bf16[128,1024]{1,0:T(8,128)(2,1)}, u32[]{:S(2)}, u32[]{:S(2)}) collective-permute-start(bf16[128,1024]{1,0:T(8,128)(2,1)} %get-tuple-element.28), channel_id=1, source_target_pairs={{0,2},{3,1},{4,6},{7,5},{8,10},{11,9},{12,14},{15,13},{16,18},{19,... | collective-permute-start | bytes 786440 | tf_op jit(solution)/shard_map/ppermute | solution.py:495
  47.9 15.5 %collective-permute-start.5 = (bf16[128,1024]{1,0:T(8,128)(2,1)S(1)}, bf16[128,1024]{1,0:T(8,128)(2,1)}, u32[]{:S(2)}, u32[]{:S(2)}) collective-permute-start(bf16[128,1024]{1,0:T(8,128)(2,1)S(1)} %get-tuple-element.29), channel_id=1, source_target_pairs={{0,2},{3,1},{4,6},{7,5},{8,10},{11,9},{12,14},{15,13},{16,18},{19,... | collective-permute-start | bytes 786440 | tf_op jit(solution)/shard_map/ppermute | solution.py:496
  49.9 13.5 %collective-permute-start.10 = (bf16[3,32,1024]{2,1,0:T(8,128)(2,1)}, bf16[3,32,1024]{2,1,0:T(8,128)(2,1)S(1)}, u32[]{:S(2)}, u32[]{:S(2)}) collective-permute-start(bf16[3,32,1024]{2,1,0:T(8,128)(2,1)} %pad_maximum_fusion.2), channel_id=1, source_target_pairs={{0,8},{4,12},{8,0},{12,4},{16,24},{20,28},{24,16},{28,20},{1,9},{5... | collective-permute-start | bytes 589832 | tf_op jit(solution)/shard_map/ppermute | solution.py:31
  51.4 13.3 %collective-permute-start.13 = (bf16[3,32,1024]{2,1,0:T(8,128)(2,1)}, bf16[3,32,1024]{2,1,0:T(8,128)(2,1)S(1)}, u32[]{:S(2)}, u32[]{:S(2)}) collective-permute-start(bf16[3,32,1024]{2,1,0:T(8,128)(2,1)} %collective-permute-done.11), channel_id=1, source_target_pairs={{0,8},{4,12},{8,0},{12,4},{16,24},{20,28},{24,16},{28,20},{1,9},{5... | collective-permute-start | bytes 589832 | tf_op jit(solution)/shard_map/ppermute | solution.py:31
  63.4 14.5 %collective-permute-start.12 = (bf16[256,1024]{1,0:T(8,128)(2,1)}, bf16[256,1024]{1,0:T(8,128)(2,1)}, u32[]{:S(2)}, u32[]{:S(2)}) collective-permute-start(bf16[256,1024]{1,0:T(8,128)(2,1)} %pad_maximum_fusion.1), channel_id=1, source_target_pairs={{1,3},{2,0},{5,7},{6,4},{9,11},{10,8},{13,15},{14,12},{17,19},{18,... | collective-permute-start | bytes 1572872 | tf_op jit(solution)/shard_map/ppermute | solution.py:499
  66.7 14.6 %collective-permute-start.14 = (bf16[4,3,32,1024]{3,2,1,0:T(8,128)(2,1)}, bf16[4,3,32,1024]{3,2,1,0:T(8,128)(2,1)}, u32[]{:S(2)}, u32[]{:S(2)}) collective-permute-start(bf16[4,3,32,1024]{3,2,1,0:T(8,128)(2,1)} %pad_maximum_fusion.refs_4_), channel_id=1, source_target_pairs={{0,4},{4,0},{8,12},{12,8},{16,20},{20,16},{24,28},{28,24},{1,5},{5... | collective-permute-start | bytes 2359304 | tf_op jit(solution)/shard_map/ppermute | solution.py:31
  68.4 13.0 %collective-permute-start.15 = (bf16[256,512]{1,0:T(8,128)(2,1)S(1)}, bf16[256,512]{1,0:T(8,128)(2,1)S(1)}, u32[]{:S(2)}, u32[]{:S(2)}) collective-permute-start(bf16[256,512]{1,0:T(8,128)(2,1)S(1)} %get-tuple-element.37), channel_id=1, source_target_pairs={{0,4},{8,12},{16,20},{24,28},{4,0},{12,8},{20,16},{28,24},{1,5},{9... | collective-permute-start | bytes 786440 | tf_op jit(solution)/shard_map/ppermute | solution.py:37
  68.9 12.4 %collective-permute-start.16 = (bf16[256,512]{1,0:T(8,128)(2,1)S(1)}, bf16[256,512]{1,0:T(8,128)(2,1)S(1)}, u32[]{:S(2)}, u32[]{:S(2)}) collective-permute-start(bf16[256,512]{1,0:T(8,128)(2,1)S(1)} %get-tuple-element.38), channel_id=1, source_target_pairs={{4,8},{12,16},{20,24},{8,4},{16,12},{24,20},{5,9},{13,17},{21,25},... | collective-permute-start | bytes 786440 | tf_op jit(solution)/shard_map/ppermute | solution.py:37
  79.3 23.3 %collective-permute-start.21 = (bf16[256,1024]{1,0:T(8,128)(2,1)S(1)}, bf16[256,1024]{1,0:T(8,128)(2,1)S(1)}, u32[]{:S(2)}, u32[]{:S(2)}) collective-permute-start(bf16[256,1024]{1,0:T(8,128)(2,1)S(1)} %get-tuple-element.53), channel_id=1, source_target_pairs={{0,16},{4,20},{8,24},{12,28},{16,0},{20,4},{24,8},{28,12},{1,17},{... | collective-permute-start | bytes 1572872 | tf_op jit(solution)/shard_map/ppermute | solution.py:31
  79.8 24.4 %collective-permute-start.20 = (bf16[256,1024]{1,0:T(8,128)(2,1)S(1)}, bf16[256,1024]{1,0:T(8,128)(2,1)S(1)}, u32[]{:S(2)}, u32[]{:S(2)}) collective-permute-start(bf16[256,1024]{1,0:T(8,128)(2,1)S(1)} %get-tuple-element.53), channel_id=1, source_target_pairs={{0,8},{4,12},{8,0},{12,4},{16,24},{20,28},{24,16},{28,20},{1,9},{5... | collective-permute-start | bytes 1572872 | tf_op jit(solution)/shard_map/ppermute | solution.py:31
  84.3 18.3 %collective-permute-start.18 = (bf16[528,256]{1,0:T(8,128)(2,1)S(1)}, bf16[528,256]{1,0:T(8,128)(2,1)S(1)}, u32[]{:S(2)}, u32[]{:S(2)}) collective-permute-start(bf16[528,256]{1,0:T(8,128)(2,1)S(1)} %attend_far.1), channel_id=1, source_target_pairs={{0,2},{1,3},{2,0},{3,1},{4,6},{5,7},{6,4},{7,5},{8,10},{9,11},{10,... | collective-permute-start | bytes 811016 | tf_op jit(solution)/shard_map/ppermute | solution.py:31
  88.2 14.4 %collective-permute-start.17 = (bf16[512,256]{1,0:T(8,128)(2,1)S(1)}, bf16[512,256]{1,0:T(8,128)(2,1)S(1)}, u32[]{:S(2)}, u32[]{:S(2)}) collective-permute-start(bf16[512,256]{1,0:T(8,128)(2,1)S(1)} %attend_near.1.refs_0_), channel_id=1, source_target_pairs={{0,1},{1,0},{2,3},{3,2},{4,5},{5,4},{6,7},{7,6},{8,9},{9,8},{10,11... | collective-permute-start | bytes 786440 | tf_op jit(solution)/shard_map/ppermute | solution.py:31
  102.6 8.6 %collective-permute-start.22 = (bf16[128,1024]{1,0:T(8,128)(2,1)S(1)}, bf16[128,1024]{1,0:T(8,128)(2,1)S(1)}, u32[]{:S(2)}, u32[]{:S(2)}) collective-permute-start(bf16[128,1024]{1,0:T(8,128)(2,1)S(1)} %slice.82), channel_id=1, source_target_pairs={{0,8},{4,12},{8,0},{12,4},{16,24},{20,28},{24,16},{28,20},{1,9},{5... | collective-permute-start | bytes 786440 | tf_op jit(solution)/shard_map/ppermute | solution.py:31
  104.2 8.0 %collective-permute-start.19 = (bf16[528,256]{1,0:T(8,128)(2,1)S(1)}, bf16[528,256]{1,0:T(8,128)(2,1)S(1)}, u32[]{:S(2)}, u32[]{:S(2)}) collective-permute-start(bf16[528,256]{1,0:T(8,128)(2,1)S(1)} %collective-permute-done.18.refs_2_), channel_id=1, source_target_pairs={{0,1},{1,0},{2,3},{3,2},{4,5},{5,4},{6,7},{7,6},{8,9},{9,8},{10,11... | collective-permute-start | bytes 811016 | tf_op jit(solution)/shard_map/ppermute | solution.py:31
  104.3 7.9 %collective-permute-start.23 = (bf16[128,1024]{1,0:T(8,128)(2,1)S(1)}, bf16[128,1024]{1,0:T(8,128)(2,1)S(1)}, u32[]{:S(2)}, u32[]{:S(2)}) collective-permute-start(bf16[128,1024]{1,0:T(8,128)(2,1)S(1)} %slice.83), channel_id=1, source_target_pairs={{0,16},{4,20},{8,24},{12,28},{16,0},{20,4},{24,8},{28,12},{1,17},{... | collective-permute-start | bytes 786440 | tf_op jit(solution)/shard_map/ppermute | solution.py:31
  112.3 4.4 %collective-permute-start.24 = (bf16[1024,1024]{1,0:T(8,128)(2,1)S(1)}, bf16[1024,1024]{1,0:T(8,128)(2,1)S(1)}, u32[]{:S(2)}, u32[]{:S(2)}) collective-permute-start(bf16[1024,1024]{1,0:T(8,128)(2,1)S(1)} %constant_dynamic-update-slice_fusion.held_ref), channel_id=1, source_target_pairs={{0,4},{4,0},{8,12},{12,8},{16,20},{20,16},{24,28},{28,24},{1,5},{5... | collective-permute-start | bytes 6291464 | tf_op jit(solution)/shard_map/ppermute | solution.py:31
  120.6 16.6 %collective-permute-start.25 = (bf16[256,1024]{1,0:T(8,128)(2,1)S(1)}, bf16[256,1024]{1,0:T(8,128)(2,1)S(1)}, u32[]{:S(2)}, u32[]{:S(2)}) collective-permute-start(bf16[256,1024]{1,0:T(8,128)(2,1)S(1)} %feed_partner.1), channel_id=1, source_target_pairs={{0,1},{1,0},{2,3},{3,2},{4,5},{5,4},{6,7},{7,6},{8,9},{9,8},{10,11... | collective-permute-start | bytes 1572872 | tf_op jit(solution)/shard_map/ppermute | solution.py:31
  122.4 14.1 %collective-permute-start.26 = (f32[3,2,1024]{2,1,0:T(2,128)S(1)}, f32[3,2,1024]{2,1,0:T(2,128)S(1)}, u32[]{:S(2)}, u32[]{:S(2)}) collective-permute-start(f32[3,2,1024]{2,1,0:T(2,128)S(1)} %get-tuple-element.56), channel_id=1, source_target_pairs={{0,1},{1,0},{2,3},{3,2},{4,5},{5,4},{6,7},{7,6},{8,9},{9,8},{10,11... | collective-permute-start | bytes 73736 | tf_op jit(solution)/shard_map/ppermute | solution.py:31
  122.8 13.8 %collective-permute-start.27 = (f32[3,2,1024]{2,1,0:T(2,128)S(1)}, f32[3,2,1024]{2,1,0:T(2,128)S(1)}, u32[]{:S(2)}, u32[]{:S(2)}) collective-permute-start(f32[3,2,1024]{2,1,0:T(2,128)S(1)} %get-tuple-element.55), channel_id=1, source_target_pairs={{0,2},{1,3},{2,0},{3,1},{4,6},{5,7},{6,4},{7,5},{8,10},{9,11},{10,... | collective-permute-start | bytes 73736 | tf_op jit(solution)/shard_map/ppermute | solution.py:31
  122.8 13.8 %collective-permute-start.28 = (f32[3,2,1024]{2,1,0:T(2,128)S(1)}, f32[3,2,1024]{2,1,0:T(2,128)S(1)}, u32[]{:S(2)}, u32[]{:S(2)}) collective-permute-start(f32[3,2,1024]{2,1,0:T(2,128)S(1)} %get-tuple-element.54), channel_id=1, source_target_pairs={{0,3},{1,2},{2,1},{3,0},{4,7},{5,6},{6,5},{7,4},{8,11},{9,10},{10,... | collective-permute-start | bytes 73736 | tf_op jit(solution)/shard_map/ppermute | solution.py:31
  (25 other events, 194.5 us)

commit v15 on v14

--- a/solution.py
+++ b/solution.py
@@ -47,22 +47,6 @@
     return center * lax.rsqrt(spread + LN_EPS) * gain + bias
 
 
-def project_early_kernel(place_ref, weight_ref, own, a1, a2, b1, b2, query_ref, keyval_ref, rows_ref, sems):
-    kv = place_ref[1]
-    count = own.shape[0]
-    inner = (kv == 1) | (kv == 2)
-    outer = jnp.logical_not(inner)
-    copies = []
-    for source, flip, needed in ((own, 0, None), (a1, 1, None), (a2, 2, outer), (b2, 2, inner), (b1, 3, inner)):
-        at = pl.ds(pl.multiple_of((kv ^ flip) * count, count), count)
-        copies.append((needed, pltpu.make_async_copy(source, rows_ref.at[at], sems.at[len(copies)])))
-    for needed, copy in copies:
-        copy.start() if needed is None else pl.when(needed)(copy.start)
-    for needed, copy in copies:
-        copy.wait() if needed is None else pl.when(needed)(copy.wait)
-    project_rows(rows_ref[...], weight_ref, query_ref, keyval_ref)
-
-
 def project_rows(rows, weight_ref, query_ref, keyval_ref):
     width = weight_ref.shape[2]
     query = jnp.dot(rows, weight_ref[0], preferred_element_type=F32) * (1.0 / math.sqrt(HD))
@@ -72,50 +56,48 @@
         keyval_ref[:, at] = jnp.dot(rows, weight_ref[part + 1], preferred_element_type=F32).astype(BF16)
 
 
-def project_last_kernel(place_ref, weight_ref, keyval_ref, a3_ref, query_ref, last_ref, even_ref, odd_ref):
+def is_inner(kv):
+    return (kv == 1) | (kv == 2)
+
+
+def project_first_kernel(weight_ref, own_ref, a1_ref, b1_ref, query_ref, keyval_ref, rows_ref):
+    count = own_ref.shape[0]
+    for index, source in enumerate((own_ref, a1_ref, b1_ref)):
+        rows_ref[index * count : (index + 1) * count] = source[...]
+    project_rows(rows_ref[...], weight_ref, query_ref, keyval_ref)
+
+
+def project_second_kernel(place_ref, weight_ref, a2_ref, b2_ref, query_ref, keyval_ref):
+    rows = jnp.where(is_inner(place_ref[1]), b2_ref[...], a2_ref[...])
+    project_rows(rows, weight_ref, query_ref, keyval_ref)
+
+
+def project_last_kernel(place_ref, weight_ref, first_ref, second_ref, a3_ref, query_ref, last_ref, even_ref, odd_ref):
     tok, kv = place_ref[0], place_ref[1]
     count = a3_ref.shape[0]
     project_rows(a3_ref[...], weight_ref, query_ref, last_ref)
-    last = last_ref[...]
-    blocks = keyval_ref.shape[0] // count
-    top = jnp.where(kv == blocks - 1, last, keyval_ref[:count])
-    bottom = jnp.where(kv == 0, last, keyval_ref[(blocks - 1) * count :])
-    even_tok = tok % 2 == 0
+    inner = is_inner(kv)
+    close = jnp.where(inner, first_ref[count : 2 * count], first_ref[:count])
+    other = jnp.where(inner, second_ref[...], last_ref[...])
+    low, even_tok = kv < 2, tok % 2 == 0
+    top, bottom = jnp.where(low, close, other), jnp.where(low, other, close)
     even_ref[...] = jnp.where(even_tok, bottom, top)
     odd_ref[...] = jnp.where(even_tok, top, bottom)
 
 
-def project_early(place, weight, blocks, shards):
-    rows, width = shards[0].shape
-    heads_width = weight.shape[2]
+def project_call(kernel, name, rows, width, heads_width, operands, extra=0, scratch=()):
+    keyval = lambda count: jax.ShapeDtypeStruct((count, 2 * heads_width), BF16)
+    edge = operands[-1].shape[0]
     return pl.pallas_call(
-        project_early_kernel,
-        out_shape=(
-            jax.ShapeDtypeStruct((blocks * rows, heads_width), BF16),
-            jax.ShapeDtypeStruct((blocks * rows, 2 * heads_width), BF16),
-        ),
-        in_specs=[SMEM, VMEM] + [ANY] * len(shards),
-        out_specs=(VMEM,) * 2,
-        scratch_shapes=[pltpu.VMEM((blocks * rows, width), BF16), pltpu.SemaphoreType.DMA((len(shards),))],
-        compiler_params=pltpu.CompilerParams(vmem_limit_bytes=12 * MIB),
+        kernel,
+        out_shape=(jax.ShapeDtypeStruct((rows, heads_width), BF16), keyval(rows)) + (keyval(edge),) * extra,
+        in_specs=[SMEM if operand.ndim == 1 else VMEM for operand in operands],
+        out_specs=(VMEM,) * (2 + extra),
+        scratch_shapes=list(scratch),
+        compiler_params=pltpu.CompilerParams(vmem_limit_bytes=10 * MIB),
         cost_estimate=SHORT,
-        name="project_early",
-    )(place, weight, *shards)
-
-
-def project_last(place, weight, keyval, a3):
-    rows = a3.shape[0]
-    heads_width = weight.shape[2]
-    keyvals = jax.ShapeDtypeStruct((rows, 2 * heads_width), BF16)
-    return pl.pallas_call(
-        project_last_kernel,
-        out_shape=(jax.ShapeDtypeStruct((rows, heads_width), BF16), keyvals, keyvals, keyvals),
-        in_specs=[SMEM] + [VMEM] * 3,
-        out_specs=(VMEM,) * 4,
-        compiler_params=pltpu.CompilerParams(vmem_limit_bytes=8 * MIB),
-        cost_estimate=SHORT,
-        name="project_last",
-    )(place, weight, keyval, a3)
+        name=name,
+    )(*operands)
 
 
 def window_bias(first, count, starts, ends):
@@ -154,28 +136,29 @@
         out_ref[:, start : start + 2 * HD] = jnp.where(lane < HD, halves[0], halves[1]).astype(BF16)
 
 
-def attend_kernel(flips, has_last, has_halo, joins, place_ref, starts_ref, ends_ref, query_ref, keyval_ref, *refs):
-    refs = list(refs)
-    last_query_ref, last_ref = (refs.pop(0), refs.pop(0)) if has_last else (None, None)
-    even_ref, odd_ref = (refs.pop(0), refs.pop(0)) if has_halo else (None, None)
-    earlier_ref = refs.pop(0) if joins else None
-    out_ref, window_ref, bias_ref, scores_ref, weights_ref, sems = refs
+def attend_kernel(flips, has_halo, *refs):
+    place_ref, starts_ref, ends_ref, query0_ref, keyval0_ref, query1_ref, keyval1_ref, query2_ref, keyval2_ref = refs[:9]
+    even_ref, odd_ref = refs[9:11] if has_halo else (None, None)
+    out_ref, window_ref, bias_ref, scores_ref, weights_ref, sems = refs[-6:]
     tok, kv = place_ref[0], place_ref[1]
-    count = bias_ref.shape[0]
-    blocks = query_ref.shape[0] // count
-    inner = (kv == 1) | (kv == 2)
+    count = out_ref.shape[0]
+    blocks = 4
+    inner = is_inner(kv)
+    outer = jnp.logical_not(inner)
     block = kv ^ jnp.where(inner, flips[1], flips[0])
-    missing = jnp.where(inner, -1, kv ^ 3)
     copies = []
     for part in range(3):
         target = window_ref.at[part * count : (part + 1) * count]
         sem = sems.at[part]
         at = block + part - 1
-        held = (at >= 0) & (at < blocks) & (at != missing)
-        source = keyval_ref.at[pl.ds(pl.multiple_of(jnp.where(held, at, 0) * count, count), count)]
-        copies.append((held, pltpu.make_async_copy(source, target, sem)))
-        if has_last:
-            copies.append((at == missing, pltpu.make_async_copy(last_ref, target, sem)))
+        here = (at >= 0) & (at < blocks)
+        flip = at ^ kv
+        first = here & ((flip == 0) | (flip == 1) | (inner & (flip == 3)))
+        slot = jnp.where(first, jnp.minimum(flip, 2), 0)
+        source = keyval0_ref.at[pl.ds(pl.multiple_of(slot * count, count), count)]
+        copies.append((first, pltpu.make_async_copy(source, target, sem)))
+        copies.append((here & (flip == 2), pltpu.make_async_copy(keyval1_ref, target, sem)))
+        copies.append((here & outer & (flip == 3), pltpu.make_async_copy(keyval2_ref, target, sem)))
         if has_halo and part != 1:
             outside = at < 0 if part == 0 else at >= blocks
             over_even = tok % 2 == (1 if part == 0 else 0)
@@ -183,29 +166,28 @@
             copies.append((outside & jnp.logical_not(over_even), pltpu.make_async_copy(odd_ref, target, sem)))
     for needed, copy in copies:
         pl.when(needed)(copy.start)
-    first = (tok * blocks + block) * count
-    bias_ref[...] = window_bias(first, count, starts_ref[...], ends_ref[...])
-    query = query_ref[pl.ds(pl.multiple_of(block * count, count), count)]
-    if has_last:
-        query = jnp.where(block == missing, last_query_ref[...], query)
+    bias_ref[...] = window_bias((tok * blocks + block) * count, count, starts_ref[...], ends_ref[...])
+
+    def query_of(flip, is_inner_one):
+        if flip == 2:
+            return query1_ref[...]
+        if flip == 3 and not is_inner_one:
+            return query2_ref[...]
+        slot = min(flip, 2)
+        return query0_ref[slot * count : (slot + 1) * count]
+
+    query = jnp.where(inner, query_of(flips[1], True), query_of(flips[0], False))
     for needed, copy in copies:
         pl.when(needed)(copy.wait)
-    if joins:
-        if out_ref.shape[0] > 2 * count:
-            out_ref[2 * count :] = jnp.zeros_like(out_ref[2 * count :])
-        half = jnp.where(inner, flips[1] % 2, flips[0] % 2)
-        out_ref[pl.ds(pl.multiple_of((1 - half) * count, count), count)] = earlier_ref[...]
-        out_ref = out_ref.at[pl.ds(pl.multiple_of(half * count, count), count)]
     attend(query, window_ref, bias_ref, scores_ref, weights_ref, out_ref)
 
 
-def attend_block(place, starts, ends, query, keyval, flips, name, last=(), halo=(), earlier=(), spare=0):
-    rows = query.shape[0] // lax.axis_size("kv")
-    heads_width = query.shape[1]
+def attend_block(place, starts, ends, projected, flips, name, halo=()):
+    rows, heads_width = projected[-2].shape
     return pl.pallas_call(
-        functools.partial(attend_kernel, flips, bool(last), bool(halo), bool(earlier)),
-        out_shape=jax.ShapeDtypeStruct(((1 + len(earlier)) * rows + spare, heads_width), BF16),
-        in_specs=[SMEM, VMEM, VMEM, VMEM, ANY] + [VMEM, ANY][: len(last)] + [ANY] * len(halo) + [VMEM] * len(earlier),
+        functools.partial(attend_kernel, flips, bool(halo)),
+        out_shape=jax.ShapeDtypeStruct((rows, heads_width), BF16),
+        in_specs=[SMEM, VMEM, VMEM] + [VMEM, ANY] * 3 + [ANY] * len(halo),
         out_specs=VMEM,
         scratch_shapes=[
             pltpu.VMEM((3 * rows, 2 * heads_width), BF16),
@@ -217,13 +199,13 @@
         compiler_params=pltpu.CompilerParams(vmem_limit_bytes=12 * MIB),
         cost_estimate=SHORT,
         name=name,
-    )(place, starts, ends, query, keyval, *last, *halo, *earlier)
+    )(place, starts, ends, *projected, *halo)
 
 
 def first_norm_kernel(layout, place_ref, own_ref, partner_ref, own_out_ref, gain_ref, bias_ref, *refs):
-    parts, pieces = refs[:4], refs[4 : 4 + len(layout)]
-    normed_ref, away_ref, all_ref, weight_ref, mixed_ref, sems = refs[4 + len(layout) :]
-    tok = place_ref[0]
+    parts, pieces = refs[:8], refs[8 : 8 + len(layout)]
+    normed_ref, away_ref, all_ref, weight_ref, mixed_ref, sems = refs[8 + len(layout) :]
+    tok, kv = place_ref[0], place_ref[1]
     quarters, heads_width, width = weight_ref.shape
     count = own_ref.shape[0]
     copies = [pltpu.make_async_copy(own_out_ref, weight_ref.at[0], sems.at[0])]
@@ -235,11 +217,12 @@
             copies.append(pltpu.make_async_copy(piece.at[index], target, sems.at[len(copies)]))
     for copy in copies:
         copy.start()
-    for flip, part_ref in enumerate(parts):
-        columns = slice(flip * heads_width, (flip + 1) * heads_width)
-        for half in range(2):
-            turned = half ^ (flip % 2)
-            all_ref[half * count : (half + 1) * count, columns] = part_ref[turned * count : (turned + 1) * count]
+    early = jnp.where(is_inner(kv), 0, 1)
+    for index, part_ref in enumerate(parts):
+        flip = index % 4
+        half = early if index < 4 else 1 - early
+        at = pl.ds(pl.multiple_of(half * count, count), count)
+        all_ref[at, flip * heads_width : (flip + 1) * heads_width] = part_ref[...]
     for copy in copies:
         copy.wait()
     weight = weight_ref[...].reshape(quarters * heads_width, width)
@@ -262,7 +245,7 @@
         out_specs=(VMEM,) * 2,
         scratch_shapes=[
             pltpu.VMEM((2 * rows, width), BF16),
-            pltpu.VMEM((len(parts), heads_width, width), BF16),
+            pltpu.VMEM((width // heads_width, heads_width, width), BF16),
             pltpu.VMEM((2 * rows, width), F32),
             pltpu.SemaphoreType.DMA((1 + sum(len(flips) for flips in layout),)),
         ],
@@ -465,6 +448,7 @@
     kv = lax.axis_index("kv")
     toks, kvs = lax.axis_size("tok"), lax.axis_size("kv")
     rows, width = hidden_in.shape
+    heads_width = out_weight.shape[0]
     place = jnp.stack([tok, kv]).astype(jnp.int32)
     eighth = lambda value: lax.dynamic_slice_in_dim(value, tok * (value.shape[0] // toks), value.shape[0] // toks, 0)
 
@@ -477,7 +461,13 @@
     a2, b2 = lax.ppermute(b1, "kv", outward), over_edges(a1, "kv", 1)
     out_here = after(jnp.stack([other[:depth] for other in others]), b2)
     out_x, out_y = swapped(out_here, "tok", 2), swapped(out_here, "tok", 4)
-    a3 = lax.ppermute(b2, "kv", outward)
+    weight = jnp.transpose(qkv_weight, (1, 0, 2))
+    sizes = (width, heads_width)
+    first = project_call(
+        project_first_kernel, "project_first", 3 * rows, *sizes, (weight, hidden_in, a1, b1), 0, [pltpu.VMEM((3 * rows, width), BF16)]
+    )
+    a3 = lax.ppermute(after(b2, first[0]), "kv", outward)
+    second = project_call(project_second_kernel, "project_second", rows, *sizes, (place, weight, a2, b2))
     out_far = swapped(out_y, "tok", 2)
     inner = (kv == 1) | (kv == 2)
 
@@ -486,43 +476,42 @@
     starts = (ends - stretch_len)[None, :]
     ends = ends[None, :]
 
-    weight = jnp.transpose(qkv_weight, (1, 0, 2))
-    query, keyval = project_early(place, weight, kvs, (hidden_in, a1, a2, b1, b2))
-    block = (place, starts, ends, query, keyval)
-    one = attend_block(*block, (1, 0), "attend_early")
-
     feed_up, feed_down = after((eighth(up_weight), eighth(down_weight)), a2, b2)
     inner_up = lax.ppermute(feed_up, "kv", [(0, 2), (3, 1)])
     inner_down = lax.ppermute(feed_down, "kv", [(0, 2), (3, 1)])
     feed_part = jnp.concatenate([feed_up, feed_down], axis=0)
-    feed_part = after(feed_part, a3, one, out_x, out_y, inner_up, inner_down)
+    feed_part = after(feed_part, a3, second[0], out_x, out_y, inner_up, inner_down)
     feed_outer = lax.ppermute(feed_part, "kv", [(1, 3), (2, 0)])
     feed_inner = jnp.concatenate([inner_up, inner_down], axis=0)
 
-    *last, even, odd = project_last(place, weight, keyval, a3)
+    *last, even, odd = project_call(
+        project_last_kernel, "project_last", rows, *sizes, (place, weight, first[1], second[1], a3), 2
+    )
     halo = over_edges(even, "tok", 0), over_edges(odd, "tok", 1)
-    two = attend_block(*block, (2, 3), "attend_last", last)
+    projected = (*first, *second, *last)
+    two = attend_block(place, starts, ends, projected, (2, 3), "attend_two")
+    two_there = swapped(two, "kv", 2)
     out_all = jnp.stack([out_here, out_x, out_y, out_far])
     out_core = swapped(out_all, "tok", 1)
     feed_here = jnp.where(inner, feed_inner, after(feed_outer, two))
     feed_x, feed_y = swapped(feed_here, "tok", 2), swapped(feed_here, "tok", 4)
-    block = (place, starts, ends, after(query, feed_here, out_core), keyval)
-    far = attend_block(*block, (3, 2), "attend_far", last, halo, (two,), 16)
-    far_heads = swapped(far, "kv", 2)
-    block = (place, starts, ends, after(query, far), keyval)
-    near = attend_block(*block, (0, 1), "attend_near", last, halo, (one,))
-    partner_heads, passed_heads = swapped(near, "kv", 1), swapped(far_heads, "kv", 1)
-    parts = (near, partner_heads, far_heads, passed_heads)
-
+    far = attend_block(after(place, feed_here, out_core), starts, ends, projected, (3, 2), "attend_far", halo)
+    far_there = swapped(far, "kv", 2)
+    two_passed = swapped(after(two_there, far), "kv", 1)
+    one = attend_block(after(place, far, two_there), starts, ends, projected, (1, 0), "attend_one")
+    one_there = swapped(one, "kv", 1)
+    near = attend_block(after(place, one), starts, ends, projected, (0, 1), "attend_near", halo)
+    near_there, far_passed = swapped(near, "kv", 1), swapped(far_there, "kv", 1)
+    parts = (one, one_there, two_there, two_passed, near, near_there, far_there, far_passed)
     out_pieces = [((0, 2, 4, 6), out_all), ((1, 3, 5, 7), out_core)]
     queries = jnp.concatenate([dec_query] + [other[depth:] for other in others], axis=0)
-    queries = after(queries, near).astype(F32)
+    queries = after(queries, near, two_passed).astype(F32)
     partial = decode_partial(queries, dec_query.shape[0], kv_cache, piece_req, piece_used)
     half = feed_here.shape[0] // 2
-    far_up = swapped(after(feed_y, far_heads, partner_heads, partial)[:half], "tok", 2)
-    far_down = swapped(after(feed_x, far_heads, partner_heads, partial)[half:], "tok", 4)
+    far_up = swapped(after(feed_y, far_there, near_there, partial)[:half], "tok", 2)
+    far_down = swapped(after(feed_x, far_there, near_there, partial)[half:], "tok", 4)
     held = jnp.concatenate([feed_here, feed_x, feed_y, far_up, far_down], axis=0)
-    feed_pieces = (held, swapped(after(held, passed_heads), "tok", 1))
+    feed_pieces = (held, swapped(after(held, far_passed, one_there), "tok", 1))
 
     gain, bias = ln1_gain[None, :], ln1_bias[None, :]
     normed, partner = first_norm(place, hidden_in, a1, out_weight, gain, bias, parts, out_pieces)

time: 139 us -> 137 us (0.986)
  waiting for transfers between devices: 45.5 us -> 32.3 us
  starting transfers between devices: 40.7 us -> 53.8 us
  local copies, waits for them, and re-layouts: 9.29 us -> 6.7 us
  Pallas kernels: 32.9 us -> 35 us
    ppermute x19 -> x22, starting transfers between devices: 21.6 us -> 31.1 us  [swapped(): return lax.ppermute(value, axis, [(i, i ^ flip) for i in range(count)])]
    ppermute x1, waiting for transfers between devices: 7.97 us -> 0.01 us  [routed_body(): a2, b2 = (lax.ppermute(b1, 'kv', outward), over_edges(a1, 'kv', 1))]
    ppermute x19 -> x22, waiting for transfers between devices: 30.4 us -> 22.8 us  [swapped(): return lax.ppermute(value, axis, [(i, i ^ flip) for i in range(count)])]
    ppermute x5, waiting for transfers between devices: 1.76 us -> 4.9 us  [over_edges(): return lax.ppermute(value, axis, edges + [(j, i) for i, j in edges])]
    ppermute x1, starting transfers between devices: 6.7 us -> 9.66 us  [routed_body(): inner_up = lax.ppermute(feed_up, 'kv', [(0, 2), (3, 1)])]
    unnamed x53 -> x45, local copies, waits for them, and re-layouts: 6.57 us -> 3.89 us
    pallas_call x6 -> x7, Pallas kernels: 15.8 us -> 17.8 us  [the longest x4 11.8 us: attend_block(): pl.pallas_call(functools.partial(attend_kernel, flips, bool(halo)), out_s...]
  transfers between devices with their start and end apart: 29 -> 32, of which waited for: 10 -> 12; matrix products, arithmetic and copies ran while one was open for 8% -> 8% of each run, Pallas kernels for 20% -> 22%
where the time goes in v15:
time: 137 us
  starting transfers between devices  53.8 us (39%)
  Pallas kernels  35 us (26%)
  waiting for transfers between devices  32.3 us (24%)
  other arithmetic  7.58 us (6%)
  local copies, waits for them, and re-layouts  6.7 us (5%)
    ppermute x22, starting transfers between devices, swapped(): return lax.ppermute(value, axis, [(i, i ^ flip) for i in range(count)])  31.1 us
    ppermute x22, waiting for transfers between devices, swapped(): return lax.ppermute(value, axis, [(i, i ^ flip) for i in range(count)])  22.8 us
    pallas_call x4, Pallas kernels, attend_block(): pl.pallas_call(functools.partial(attend_kernel, flips, bool(halo)), out_s...  11.8 us
    ppermute x1, starting transfers between devices, routed_body(): inner_up = lax.ppermute(feed_up, 'kv', [(0, 2), (3, 1)])  9.66 us
    pallas_call x2, Pallas kernels, feed(): pl.pallas_call(feed_kernel, out_shape=jax.ShapeDtypeStruct((count, width)...  7.82 us
    ppermute x5, starting transfers between devices, over_edges(): return lax.ppermute(value, axis, edges + [(j, i) for i, j in edges])  7.27 us
    pallas_call x3, Pallas kernels, project_call(): pl.pallas_call(kernel, out_shape=(jax.ShapeDtypeStruct((rows, heads_width...  6 us
    ppermute x5, waiting for transfers between devices, over_edges(): return lax.ppermute(value, axis, edges + [(j, i) for i, j in edges])  4.9 us
  transfers between devices with their start and end apart: 32, of which 12 were waited for; matrix products, arithmetic and copies ran while one was open for 8% of the time, Pallas kernels for 22%

profile of v15, /device:TPU:0, one launch (start us, length us, event | category | flops | bytes accessed | tf_op | source)
XLA Modules:
  0.0 136.6 jit_solution(3435873157912307686)
XLA Ops:
  0.6 3.1 %collective-permute-start = (bf16[256,1024]{1,0:T(8,128)(2,1)}, bf16[256,1024]{1,0:T(8,128)(2,1)S(1)}, u32[]{:S(2)}, u32[]{:S(2)}) collective-permute-start(bf16[256,1024]{1,0:T(8,128)(2,1)} %own_ref.3), channel_id=1, source_target_pairs={{0,1},{2,3},{1,0},{3,2},{4,5},{6,7},{5,4},{7,6},{8,9},{10,11},{9,8... | collective-permute-start | bytes 1572872 | tf_op jit(solution)/shard_map/ppermute | solution.py:37
  6.7 2.5 %collective-permute-start.9 = (bf16[34,1024]{1,0:T(8,128)(2,1)S(1)}, bf16[34,1024]{1,0:T(8,128)(2,1)S(1)}, u32[]{:S(2)}, u32[]{:S(2)}) collective-permute-start(bf16[34,1024]{1,0:T(8,128)(2,1)S(1)} %pad_maximum_fusion.3), channel_id=1, source_target_pairs={{0,3},{1,2},{2,1},{3,0},{4,7},{5,6},{6,5},{7,4},{8,11},{9,10},{10,... | collective-permute-start | bytes 208904 | tf_op jit(solution)/shard_map/ppermute | solution.py:31
  9.2 2.6 %collective-permute-start.8 = (bf16[34,1024]{1,0:T(8,128)(2,1)S(1)}, bf16[34,1024]{1,0:T(8,128)(2,1)S(1)}, u32[]{:S(2)}, u32[]{:S(2)}) collective-permute-start(bf16[34,1024]{1,0:T(8,128)(2,1)S(1)} %pad_maximum_fusion.3), channel_id=1, source_target_pairs={{0,2},{1,3},{2,0},{3,1},{4,6},{5,7},{6,4},{7,5},{8,10},{9,11},{10,... | collective-permute-start | bytes 208904 | tf_op jit(solution)/shard_map/ppermute | solution.py:31
  11.8 4.9 %collective-permute-done.a1_ref.partner_ref = bf16[256,1024]{1,0:T(8,128)(2,1)S(1)} collective-permute-done((bf16[256,1024]{1,0:T(8,128)(2,1)}, bf16[256,1024]{1,0:T(8,128)(2,1)S(1)}, u32[]{:S(2)}, u32[]{:S(2)}) %collective-permute-start) | collective-permute-done | bytes 524320 | tf_op jit(solution)/shard_map/ppermute | solution.py:37
  18.2 2.8 %collective-permute-done.9 = bf16[34,1024]{1,0:T(8,128)(2,1)S(1)} collective-permute-done((bf16[34,1024]{1,0:T(8,128)(2,1)S(1)}, bf16[34,1024]{1,0:T(8,128)(2,1)S(1)}, u32[]{:S(2)}, u32[]{:S(2)}) %collective-permute-start.9) | collective-permute-done | bytes 69664 | tf_op jit(solution)/shard_map/ppermute | solution.py:31
  22.3 5.9 %collective-permute-done.8 = bf16[34,1024]{1,0:T(8,128)(2,1)S(1)} collective-permute-done((bf16[34,1024]{1,0:T(8,128)(2,1)S(1)}, bf16[34,1024]{1,0:T(8,128)(2,1)S(1)}, u32[]{:S(2)}, u32[]{:S(2)}) %collective-permute-start.8) | collective-permute-done | bytes 69664 | tf_op jit(solution)/shard_map/ppermute | solution.py:31
  31.3 2.6 %project_first.1 = (bf16[768,256]{1,0:T(8,128)(2,1)S(1)}, bf16[768,512]{1,0:T(8,128)(2,1)S(1)}) custom-call(bf16[3,1024,256]{2,1,0:T(8,128)(2,1)S(1)} %bitcast.142, bf16[256,1024]{1,0:T(8,128)(2,1)S(1)} %copy-done.5, bf16[256,1024]{1,0:T(8,128)(2,1)S(1)} %collective-permute-done.a1_ref.partner_ref, bf16[256,1024]{1,0:T(8,128)(2,1)} %collective-permute-done.1.b1_ref), custom_call_target="tpu_custom_call" | custom-call | flops 1 | bytes 1 | tf_op jit(solution)/shard_map/project_first/pallas_call | solution.py:91
  37.4 1.9 %constant_dynamic-slice_fusion.1 = (bf16[128,1024]{1,0:T(8,128)(2,1)}, bf16[128,1024]{1,0:T(8,128)(2,1)}) fusion(bf16[1024,1024]{1,0:T(8,128)(2,1)} %down_near_ref.3, s32[]{:T(128)S(6)} %select_n.32, bf16[1024,1024]{1,0:T(8,128)(2,1)} %up_near_ref.3), kind=kLoop, calls=%fused_computation.49 | loop fusion | bytes 1048580 | tf_op jit(solution)/shard_map/dynamic_slice | solution.py:453
  39.3 9.7 %collective-permute-start.4 = (bf16[128,1024]{1,0:T(8,128)(2,1)}, bf16[128,1024]{1,0:T(8,128)(2,1)}, u32[]{:S(2)}, u32[]{:S(2)}) collective-permute-start(bf16[128,1024]{1,0:T(8,128)(2,1)} %get-tuple-element.32), channel_id=1, source_target_pairs={{0,2},{3,1},{4,6},{7,5},{8,10},{11,9},{12,14},{15,13},{16,18},{19,... | collective-permute-start | bytes 786440 | tf_op jit(solution)/shard_map/ppermute | solution.py:480
  48.9 2.0 %collective-permute-start.5 = (bf16[128,1024]{1,0:T(8,128)(2,1)}, bf16[128,1024]{1,0:T(8,128)(2,1)}, u32[]{:S(2)}, u32[]{:S(2)}) collective-permute-start(bf16[128,1024]{1,0:T(8,128)(2,1)} %get-tuple-element.33), channel_id=1, source_target_pairs={{0,2},{3,1},{4,6},{7,5},{8,10},{11,9},{12,14},{15,13},{16,18},{19,... | collective-permute-start | bytes 786440 | tf_op jit(solution)/shard_map/ppermute | solution.py:481
  53.0 1.8 %project_second.1 = (bf16[256,256]{1,0:T(8,128)(2,1)S(1)}, bf16[256,512]{1,0:T(8,128)(2,1)S(1)}) custom-call(s32[2]{0:T(128)S(1)} %pad_add_fusion.place_ref.refs_0_, bf16[3,1024,256]{2,1,0:T(8,128)(2,1)S(1)} %bitcast.143, bf16[256,1024]{1,0:T(8,128)(2,1)} %collective-permute-done.2.a2_ref, bf16[256,1024]{1,0:T(8,128)(2,1)} %collective-permute-done.3.b2_ref), custom_call_target="tpu_custom_call" | custom-call | flops 1 | bytes 1 | tf_op jit(solution)/shard_map/project_second/pallas_call | solution.py:91
  55.5 1.9 %pad_maximum_fusion.1 = bf16[256,1024]{1,0:T(8,128)(2,1)} fusion(bf16[128,1024]{1,0:T(8,128)(2,1)} %get-tuple-element.33, bf16[128,1024]{1,0:T(8,128)(2,1)} %get-tuple-element.32), kind=kLoop, calls=%fused_computation.2 | loop fusion | flops 1048576 | bytes 1048576 | tf_op jit(solution)/shard_map/concatenate | solution.py:482
  60.2 2.0 %pad_maximum_fusion.refs_8_ = bf16[4,3,32,1024]{3,2,1,0:T(8,128)(2,1)} fusion(bf16[1,3,32,1024]{3,2,1,0:T(8,128)(2,1)S(1)} %bitcast.155, bf16[1,3,32,1024]{3,2,1,0:T(8,128)(2,1)} %bitcast.12, bf16[1,3,32,1024]{3,2,1,0:T(8,128)(2,1)S(1)} %bitcast.154, bf16[1,3,32,1024]{3,2,1,0:T(8,128)(2,1)} %bitcast.10), kind=kLoop, calls=%fused_computation | loop fusion | flops 1179648 | bytes 1572864 | tf_op jit(solution)/shard_map/stack | solution.py:494
  65.3 2.9 %attend_two.1 = bf16[256,256]{1,0:T(8,128)(2,1)S(1)} custom-call(s32[2]{0:T(128)S(1)} %pad_add_fusion.place_ref.refs_0_, s32[1,48]{1,0:T(1,128)S(1)} %subtract_bitcast_fusion.refs_1_, s32[1,48]{1,0:T(1,128)S(1)} %bitcast.145, bf16[768,256]{1,0:T(8,128)(2,1)S(1)} %get-tuple-element.34.refs_3_, bf16[768,512]{1,0:T(8,128)(2,1)S(1)} %get-tuple-element.39.first_ref.refs_4_, ...), custom_call_target="tpu_custom_call" | custom-call | flops 1 | bytes 1 | tf_op jit(solution)/shard_map/attend_two/pallas_call | solution.py:187
  68.2 4.5 %collective-permute-done.12 = bf16[256,1024]{1,0:T(8,128)(2,1)} collective-permute-done((bf16[256,1024]{1,0:T(8,128)(2,1)}, bf16[256,1024]{1,0:T(8,128)(2,1)}, u32[]{:S(2)}, u32[]{:S(2)}) %collective-permute-start.12) | collective-permute-done | bytes 524320 | tf_op jit(solution)/shard_map/ppermute | solution.py:484
  77.0 2.9 %attend_far.1 = bf16[256,256]{1,0:T(8,128)(2,1)S(1)} custom-call(s32[2]{0:T(128)S(1)} %pad_add_fusion.place_ref.refs_0_, s32[1,48]{1,0:T(1,128)S(1)} %subtract_bitcast_fusion.refs_1_, s32[1,48]{1,0:T(1,128)S(1)} %bitcast.146, bf16[768,256]{1,0:T(8,128)(2,1)S(1)} %get-tuple-element.34.refs_3_, bf16[768,512]{1,0:T(8,128)(2,1)S(1)} %get-tuple-element.39.first_ref.refs_4_, ...), custom_call_target="tpu_custom_call" | custom-call | flops 1 | bytes 1 | tf_op jit(solution)/shard_map/attend_far/pallas_call | solution.py:187
  80.0 2.2 %collective-permute-start.21 = (bf16[256,256]{1,0:T(8,128)(2,1)S(1)}, bf16[256,256]{1,0:T(8,128)(2,1)S(1)}, u32[]{:S(2)}, u32[]{:S(2)}) collective-permute-start(bf16[256,256]{1,0:T(8,128)(2,1)S(1)} %attend_far.1), channel_id=1, source_target_pairs={{0,2},{1,3},{2,0},{3,1},{4,6},{5,7},{6,4},{7,5},{8,10},{9,11},{10,... | collective-permute-start | bytes 393224 | tf_op jit(solution)/shard_map/ppermute | solution.py:31
  82.9 2.9 %attend_one.1.refs_0_ = bf16[256,256]{1,0:T(8,128)(2,1)S(1)} custom-call(s32[2]{0:T(128)S(1)} %pad_add_fusion.place_ref.refs_0_, s32[1,48]{1,0:T(1,128)S(1)} %subtract_bitcast_fusion.refs_1_, s32[1,48]{1,0:T(1,128)S(1)} %bitcast.147, bf16[768,256]{1,0:T(8,128)(2,1)S(1)} %get-tuple-element.34.refs_3_, ...), custom_call_target="tpu_custom_call" | custom-call | flops 1 | bytes 1 | tf_op jit(solution)/shard_map/attend_one/pallas_call | solution.py:187
  86.2 3.1 %attend_near.1.refs_4_ = bf16[256,256]{1,0:T(8,128)(2,1)S(1)} custom-call(s32[2]{0:T(128)S(1)} %pad_add_fusion.place_ref.refs_0_, s32[1,48]{1,0:T(1,128)S(1)} %subtract_bitcast_fusion.refs_1_, s32[1,48]{1,0:T(1,128)S(1)} %bitcast.148, bf16[768,256]{1,0:T(8,128)(2,1)S(1)} %get-tuple-element.34.refs_3_, ...), custom_call_target="tpu_custom_call" | custom-call | flops 1 | bytes 1 | tf_op jit(solution)/shard_map/attend_near/pallas_call | solution.py:187
  89.3 1.8 %collective-permute-start.20 = (bf16[256,256]{1,0:T(8,128)(2,1)S(1)}, bf16[256,256]{1,0:T(8,128)(2,1)S(1)}, u32[]{:S(2)}, u32[]{:S(2)}) collective-permute-start(bf16[256,256]{1,0:T(8,128)(2,1)S(1)} %attend_near.1.refs_4_), channel_id=1, source_target_pairs={{0,1},{1,0},{2,3},{3,2},{4,5},{5,4},{6,7},{7,6},{8,9},{9,8},{10,11... | collective-permute-start | bytes 393224 | tf_op jit(solution)/shard_map/ppermute | solution.py:31
  92.3 3.8 %decode.1 = f32[3,8,1024]{2,1,0:T(8,128)S(1)} custom-call(s32[6]{0:T(128)S(1)} %fusion.12.slot_ref, s32[6]{0:T(128)S(1)} %bitcast.153, f32[8,1024]{1,0:T(8,128)S(1)} %convert_element_type.6.query_ref, bf16[2,1,6,128,1024]{4,3,2,1,0:T(8,128)(2,1)S(1)} %copy-done.4), custom_call_target="tpu_custom_call" | custom-call | flops 1 | bytes 1 | tf_op jit(solution)/shard_map/decode/pallas_call | solution.py:392
  96.2 1.8 %collective-permute-start.25 = (bf16[128,1024]{1,0:T(8,128)(2,1)S(1)}, bf16[128,1024]{1,0:T(8,128)(2,1)S(1)}, u32[]{:S(2)}, u32[]{:S(2)}) collective-permute-start(bf16[128,1024]{1,0:T(8,128)(2,1)S(1)} %slice.82), channel_id=1, source_target_pairs={{0,8},{4,12},{8,0},{12,4},{16,24},{20,28},{24,16},{28,20},{1,9},{5... | collective-permute-start | bytes 786440 | tf_op jit(solution)/shard_map/ppermute | solution.py:31
  98.0 2.0 %collective-permute-start.22 = (bf16[256,256]{1,0:T(8,128)(2,1)S(1)}, bf16[256,256]{1,0:T(8,128)(2,1)S(1)}, u32[]{:S(2)}, u32[]{:S(2)}) collective-permute-start(bf16[256,256]{1,0:T(8,128)(2,1)S(1)} %collective-permute-done.21.refs_6_), channel_id=1, source_target_pairs={{0,1},{1,0},{2,3},{3,2},{4,5},{5,4},{6,7},{7,6},{8,9},{9,8},{10,11... | collective-permute-start | bytes 393224 | tf_op jit(solution)/shard_map/ppermute | solution.py:31
  100.0 4.8 %collective-permute-start.26 = (bf16[128,1024]{1,0:T(8,128)(2,1)S(1)}, bf16[128,1024]{1,0:T(8,128)(2,1)S(1)}, u32[]{:S(2)}, u32[]{:S(2)}) collective-permute-start(bf16[128,1024]{1,0:T(8,128)(2,1)S(1)} %slice.83), channel_id=1, source_target_pairs={{0,16},{4,20},{8,24},{12,28},{16,0},{20,4},{24,8},{28,12},{1,17},{... | collective-permute-start | bytes 786440 | tf_op jit(solution)/shard_map/ppermute | solution.py:31
  105.0 4.2 %collective-permute-done.26 = bf16[128,1024]{1,0:T(8,128)(2,1)S(1)} collective-permute-done((bf16[128,1024]{1,0:T(8,128)(2,1)S(1)}, bf16[128,1024]{1,0:T(8,128)(2,1)S(1)}, u32[]{:S(2)}, u32[]{:S(2)}) %collective-permute-start.26) | collective-permute-done | bytes 262176 | tf_op jit(solution)/shard_map/ppermute | solution.py:31
  109.4 4.3 %first_norm.1 = (bf16[256,1024]{1,0:T(8,128)(2,1)S(1)}, bf16[256,1024]{1,0:T(8,128)(2,1)S(1)}) custom-call(s32[2]{0:T(128)S(1)} %pad_add_fusion.place_ref.refs_0_, bf16[256,1024]{1,0:T(8,128)(2,1)S(1)} %copy-done.6, bf16[256,1024]{1,0:T(8,128)(2,1)S(1)} %collective-permute-done.a1_ref.partner_ref, bf16[256,1024]{1,0:T(8,128)(2,1)S(1)} %copy-done.9, ...), custom_call_target="tpu_custom_call" | custom-call | flops 1 | bytes 1 | tf_op jit(solution)/shard_map/first_norm/pallas_call | solution.py:241
  113.7 3.9 %feed_partner.1 = bf16[256,1024]{1,0:T(8,128)(2,1)S(1)} custom-call(s32[2]{0:T(128)S(1)} %pad_add_fusion.place_ref.refs_0_, bf16[256,1024]{1,0:T(8,128)(2,1)S(1)} %get-tuple-element.51.rows_ref, bf16[1024,1024]{1,0:T(8,128)(2,1)S(1)} %copy-done.2, bf16[1024,1024]{1,0:T(8,128)(2,1)S(1)} %copy-done.3, ...), custom_call_target="tpu_custom_call" | custom-call | flops 1 | bytes 1 | tf_op jit(solution)/shard_map/feed_partner/pallas_call | solution.py:310
  117.6 2.1 %collective-permute-start.28 = (bf16[256,1024]{1,0:T(8,128)(2,1)S(1)}, bf16[256,1024]{1,0:T(8,128)(2,1)S(1)}, u32[]{:S(2)}, u32[]{:S(2)}) collective-permute-start(bf16[256,1024]{1,0:T(8,128)(2,1)S(1)} %feed_partner.1), channel_id=1, source_target_pairs={{0,1},{1,0},{2,3},{3,2},{4,5},{5,4},{6,7},{7,6},{8,9},{9,8},{10,11... | collective-permute-start | bytes 1572872 | tf_op jit(solution)/shard_map/ppermute | solution.py:31
  119.8 1.7 %collective-permute-start.30 = (f32[3,2,1024]{2,1,0:T(2,128)S(1)}, f32[3,2,1024]{2,1,0:T(2,128)S(1)}, u32[]{:S(2)}, u32[]{:S(2)}) collective-permute-start(f32[3,2,1024]{2,1,0:T(2,128)S(1)} %get-tuple-element.65), channel_id=1, source_target_pairs={{0,2},{1,3},{2,0},{3,1},{4,6},{5,7},{6,4},{7,5},{8,10},{9,11},{10,... | collective-permute-start | bytes 73736 | tf_op jit(solution)/shard_map/ppermute | solution.py:31
  121.5 2.7 %collective-permute-start.31 = (f32[3,2,1024]{2,1,0:T(2,128)S(1)}, f32[3,2,1024]{2,1,0:T(2,128)S(1)}, u32[]{:S(2)}, u32[]{:S(2)}) collective-permute-start(f32[3,2,1024]{2,1,0:T(2,128)S(1)} %get-tuple-element.64), channel_id=1, source_target_pairs={{0,3},{1,2},{2,1},{3,0},{4,7},{5,6},{6,5},{7,4},{8,11},{9,10},{10,... | collective-permute-start | bytes 73736 | tf_op jit(solution)/shard_map/ppermute | solution.py:31
  124.2 3.9 %feed_own.1.near_ref = f32[256,1024]{1,0:T(8,128)S(1)} custom-call(s32[2]{0:T(128)S(1)} %pad_add_fusion.place_ref.refs_0_, bf16[256,1024]{1,0:T(8,128)(2,1)S(1)} %get-tuple-element.56.rows_ref.normed_ref, bf16[1024,1024]{1,0:T(8,128)(2,1)S(1)} %copy-done.2, bf16[1024,1024]{1,0:T(8,128)(2,1)S(1)} %copy-done.3, ...), custom_call_target="tpu_custom_call" | custom-call | flops 1 | bytes 1 | tf_op jit(solution)/shard_map/feed_own/pallas_call | solution.py:310
  128.1 5.2 %collective-permute-done.29 = f32[3,2,1024]{2,1,0:T(2,128)S(1)} collective-permute-done((f32[3,2,1024]{2,1,0:T(2,128)S(1)}, f32[3,2,1024]{2,1,0:T(2,128)S(1)}, u32[]{:S(2)}, u32[]{:S(2)}) %collective-permute-start.29) | collective-permute-done | bytes 24608 | tf_op jit(solution)/shard_map/ppermute | solution.py:31
  (116 shorter events, 31.2 us)
Async XLA Ops:
  0.6 16.1 %collective-permute-start = (bf16[256,1024]{1,0:T(8,128)(2,1)}, bf16[256,1024]{1,0:T(8,128)(2,1)S(1)}, u32[]{:S(2)}, u32[]{:S(2)}) collective-permute-start(bf16[256,1024]{1,0:T(8,128)(2,1)} %own_ref.3), channel_id=1, source_target_pairs={{0,1},{2,3},{1,0},{3,2},{4,5},{6,7},{5,4},{7,6},{8,9},{10,11},{9,8... | collective-permute-start | bytes 1572872 | tf_op jit(solution)/shard_map/ppermute | solution.py:37
  3.7 17.3 %collective-permute-start.1 = (bf16[256,1024]{1,0:T(8,128)(2,1)}, bf16[256,1024]{1,0:T(8,128)(2,1)}, u32[]{:S(2)}, u32[]{:S(2)}) collective-permute-start(bf16[256,1024]{1,0:T(8,128)(2,1)} %own_ref.3), channel_id=1, source_target_pairs={{1,2},{2,1},{5,6},{6,5},{9,10},{10,9},{13,14},{14,13},{17,18},{18,... | collective-permute-start | bytes 1572872 | tf_op jit(solution)/shard_map/ppermute | solution.py:37
  6.7 14.3 %collective-permute-start.9 = (bf16[34,1024]{1,0:T(8,128)(2,1)S(1)}, bf16[34,1024]{1,0:T(8,128)(2,1)S(1)}, u32[]{:S(2)}, u32[]{:S(2)}) collective-permute-start(bf16[34,1024]{1,0:T(8,128)(2,1)S(1)} %pad_maximum_fusion.3), channel_id=1, source_target_pairs={{0,3},{1,2},{2,1},{3,0},{4,7},{5,6},{6,5},{7,4},{8,11},{9,10},{10,... | collective-permute-start | bytes 208904 | tf_op jit(solution)/shard_map/ppermute | solution.py:31
  9.2 19.0 %collective-permute-start.8 = (bf16[34,1024]{1,0:T(8,128)(2,1)S(1)}, bf16[34,1024]{1,0:T(8,128)(2,1)S(1)}, u32[]{:S(2)}, u32[]{:S(2)}) collective-permute-start(bf16[34,1024]{1,0:T(8,128)(2,1)S(1)} %pad_maximum_fusion.3), channel_id=1, source_target_pairs={{0,2},{1,3},{2,0},{3,1},{4,6},{5,7},{6,4},{7,5},{8,10},{9,11},{10,... | collective-permute-start | bytes 208904 | tf_op jit(solution)/shard_map/ppermute | solution.py:31
  11.8 16.4 %collective-permute-start.7 = (bf16[34,1024]{1,0:T(8,128)(2,1)S(1)}, bf16[34,1024]{1,0:T(8,128)(2,1)S(1)}, u32[]{:S(2)}, u32[]{:S(2)}) collective-permute-start(bf16[34,1024]{1,0:T(8,128)(2,1)S(1)} %pad_maximum_fusion.3), channel_id=1, source_target_pairs={{0,1},{1,0},{2,3},{3,2},{4,5},{5,4},{6,7},{7,6},{8,9},{9,8},{10,11... | collective-permute-start | bytes 208904 | tf_op jit(solution)/shard_map/ppermute | solution.py:31
  16.7 17.2 %collective-permute-start.3 = (bf16[256,1024]{1,0:T(8,128)(2,1)S(1)}, bf16[256,1024]{1,0:T(8,128)(2,1)}, u32[]{:S(2)}, u32[]{:S(2)}) collective-permute-start(bf16[256,1024]{1,0:T(8,128)(2,1)S(1)} %collective-permute-done.a1_ref.partner_ref), channel_id=1, source_target_pairs={{1,2},{2,1},{5,6},{6,5},{9,10},{10,9},{13,14},{14,13},{17,18},{18,... | collective-permute-start | bytes 1572872 | tf_op jit(solution)/shard_map/ppermute | solution.py:37
  21.0 18.3 %collective-permute-start.2 = (bf16[256,1024]{1,0:T(8,128)(2,1)}, bf16[256,1024]{1,0:T(8,128)(2,1)}, u32[]{:S(2)}, u32[]{:S(2)}) collective-permute-start(bf16[256,1024]{1,0:T(8,128)(2,1)} %collective-permute-done.1.b1_ref), channel_id=1, source_target_pairs={{1,0},{2,3},{5,4},{6,7},{9,8},{10,11},{13,12},{14,15},{17,16},{18,... | collective-permute-start | bytes 1572872 | tf_op jit(solution)/shard_map/ppermute | solution.py:461
  33.9 24.3 %collective-permute-start.6 = (bf16[256,1024]{1,0:T(8,128)(2,1)}, bf16[256,1024]{1,0:T(8,128)(2,1)}, u32[]{:S(2)}, u32[]{:S(2)}) collective-permute-start(bf16[256,1024]{1,0:T(8,128)(2,1)} %collective-permute-done.3.b2_ref), channel_id=1, source_target_pairs={{1,0},{2,3},{5,4},{6,7},{9,8},{10,11},{13,12},{14,15},{17,16},{18,... | collective-permute-start | bytes 1572872 | tf_op jit(solution)/shard_map/ppermute | solution.py:469
  35.9 16.5 %collective-permute-start.11 = (bf16[3,32,1024]{2,1,0:T(8,128)(2,1)}, bf16[3,32,1024]{2,1,0:T(8,128)(2,1)}, u32[]{:S(2)}, u32[]{:S(2)}) collective-permute-start(bf16[3,32,1024]{2,1,0:T(8,128)(2,1)} %pad_maximum_fusion.2), channel_id=1, source_target_pairs={{0,16},{4,20},{8,24},{12,28},{16,0},{20,4},{24,8},{28,12},{1,17},{... | collective-permute-start | bytes 589832 | tf_op jit(solution)/shard_map/ppermute | solution.py:31
  39.3 18.9 %collective-permute-start.4 = (bf16[128,1024]{1,0:T(8,128)(2,1)}, bf16[128,1024]{1,0:T(8,128)(2,1)}, u32[]{:S(2)}, u32[]{:S(2)}) collective-permute-start(bf16[128,1024]{1,0:T(8,128)(2,1)} %get-tuple-element.32), channel_id=1, source_target_pairs={{0,2},{3,1},{4,6},{7,5},{8,10},{11,9},{12,14},{15,13},{16,18},{19,... | collective-permute-start | bytes 786440 | tf_op jit(solution)/shard_map/ppermute | solution.py:480
  48.9 9.3 %collective-permute-start.5 = (bf16[128,1024]{1,0:T(8,128)(2,1)}, bf16[128,1024]{1,0:T(8,128)(2,1)}, u32[]{:S(2)}, u32[]{:S(2)}) collective-permute-start(bf16[128,1024]{1,0:T(8,128)(2,1)} %get-tuple-element.33), channel_id=1, source_target_pairs={{0,2},{3,1},{4,6},{7,5},{8,10},{11,9},{12,14},{15,13},{16,18},{19,... | collective-permute-start | bytes 786440 | tf_op jit(solution)/shard_map/ppermute | solution.py:481
  50.9 7.2 %collective-permute-start.10 = (bf16[3,32,1024]{2,1,0:T(8,128)(2,1)}, bf16[3,32,1024]{2,1,0:T(8,128)(2,1)S(1)}, u32[]{:S(2)}, u32[]{:S(2)}) collective-permute-start(bf16[3,32,1024]{2,1,0:T(8,128)(2,1)} %pad_maximum_fusion.2), channel_id=1, source_target_pairs={{0,8},{4,12},{8,0},{12,4},{16,24},{20,28},{24,16},{28,20},{1,9},{5... | collective-permute-start | bytes 589832 | tf_op jit(solution)/shard_map/ppermute | solution.py:31
  52.4 7.8 %collective-permute-start.13 = (bf16[3,32,1024]{2,1,0:T(8,128)(2,1)}, bf16[3,32,1024]{2,1,0:T(8,128)(2,1)S(1)}, u32[]{:S(2)}, u32[]{:S(2)}) collective-permute-start(bf16[3,32,1024]{2,1,0:T(8,128)(2,1)} %collective-permute-done.11), channel_id=1, source_target_pairs={{0,8},{4,12},{8,0},{12,4},{16,24},{20,28},{24,16},{28,20},{1,9},{5... | collective-permute-start | bytes 589832 | tf_op jit(solution)/shard_map/ppermute | solution.py:31
  58.2 14.5 %collective-permute-start.12 = (bf16[256,1024]{1,0:T(8,128)(2,1)}, bf16[256,1024]{1,0:T(8,128)(2,1)}, u32[]{:S(2)}, u32[]{:S(2)}) collective-permute-start(bf16[256,1024]{1,0:T(8,128)(2,1)} %pad_maximum_fusion.1), channel_id=1, source_target_pairs={{1,3},{2,0},{5,7},{6,4},{9,11},{10,8},{13,15},{14,12},{17,19},{18,... | collective-permute-start | bytes 1572872 | tf_op jit(solution)/shard_map/ppermute | solution.py:484
  62.3 14.0 %collective-permute-start.14 = (bf16[4,3,32,1024]{3,2,1,0:T(8,128)(2,1)}, bf16[4,3,32,1024]{3,2,1,0:T(8,128)(2,1)}, u32[]{:S(2)}, u32[]{:S(2)}) collective-permute-start(bf16[4,3,32,1024]{3,2,1,0:T(8,128)(2,1)} %pad_maximum_fusion.refs_8_), channel_id=1, source_target_pairs={{0,4},{4,0},{8,12},{12,8},{16,20},{20,16},{24,28},{28,24},{1,5},{5... | collective-permute-start | bytes 2359304 | tf_op jit(solution)/shard_map/ppermute | solution.py:31
  64.0 13.0 %collective-permute-start.15 = (bf16[256,512]{1,0:T(8,128)(2,1)S(1)}, bf16[256,512]{1,0:T(8,128)(2,1)S(1)}, u32[]{:S(2)}, u32[]{:S(2)}) collective-permute-start(bf16[256,512]{1,0:T(8,128)(2,1)S(1)} %get-tuple-element.45), channel_id=1, source_target_pairs={{0,4},{8,12},{16,20},{24,28},{4,0},{12,8},{20,16},{28,24},{1,5},{9... | collective-permute-start | bytes 786440 | tf_op jit(solution)/shard_map/ppermute | solution.py:37
  64.6 12.4 %collective-permute-start.16 = (bf16[256,512]{1,0:T(8,128)(2,1)S(1)}, bf16[256,512]{1,0:T(8,128)(2,1)S(1)}, u32[]{:S(2)}, u32[]{:S(2)}) collective-permute-start(bf16[256,512]{1,0:T(8,128)(2,1)S(1)} %get-tuple-element.46), channel_id=1, source_target_pairs={{4,8},{12,16},{20,24},{8,4},{16,12},{24,20},{5,9},{13,17},{21,25},... | collective-permute-start | bytes 786440 | tf_op jit(solution)/shard_map/ppermute | solution.py:37
  74.2 22.0 %collective-permute-start.24 = (bf16[256,1024]{1,0:T(8,128)(2,1)S(1)}, bf16[256,1024]{1,0:T(8,128)(2,1)S(1)}, u32[]{:S(2)}, u32[]{:S(2)}) collective-permute-start(bf16[256,1024]{1,0:T(8,128)(2,1)S(1)} %get-tuple-element.63), channel_id=1, source_target_pairs={{0,16},{4,20},{8,24},{12,28},{16,0},{20,4},{24,8},{28,12},{1,17},{... | collective-permute-start | bytes 1572872 | tf_op jit(solution)/shard_map/ppermute | solution.py:31
  74.7 25.2 %collective-permute-start.23 = (bf16[256,1024]{1,0:T(8,128)(2,1)S(1)}, bf16[256,1024]{1,0:T(8,128)(2,1)S(1)}, u32[]{:S(2)}, u32[]{:S(2)}) collective-permute-start(bf16[256,1024]{1,0:T(8,128)(2,1)S(1)} %get-tuple-element.63), channel_id=1, source_target_pairs={{0,8},{4,12},{8,0},{12,4},{16,24},{20,28},{24,16},{28,20},{1,9},{5... | collective-permute-start | bytes 1572872 | tf_op jit(solution)/shard_map/ppermute | solution.py:31
  76.2 6.7 %collective-permute-start.17 = (bf16[256,256]{1,0:T(8,128)(2,1)S(1)}, bf16[256,256]{1,0:T(8,128)(2,1)S(1)}, u32[]{:S(2)}, u32[]{:S(2)}) collective-permute-start(bf16[256,256]{1,0:T(8,128)(2,1)S(1)} %attend_two.1), channel_id=1, source_target_pairs={{0,2},{1,3},{2,0},{3,1},{4,6},{5,7},{6,4},{7,5},{8,10},{9,11},{10,... | collective-permute-start | bytes 393224 | tf_op jit(solution)/shard_map/ppermute | solution.py:31
  80.0 16.1 %collective-permute-start.21 = (bf16[256,256]{1,0:T(8,128)(2,1)S(1)}, bf16[256,256]{1,0:T(8,128)(2,1)S(1)}, u32[]{:S(2)}, u32[]{:S(2)}) collective-permute-start(bf16[256,256]{1,0:T(8,128)(2,1)S(1)} %attend_far.1), channel_id=1, source_target_pairs={{0,2},{1,3},{2,0},{3,1},{4,6},{5,7},{6,4},{7,5},{8,10},{9,11},{10,... | collective-permute-start | bytes 393224 | tf_op jit(solution)/shard_map/ppermute | solution.py:31
  85.8 6.4 %collective-permute-start.19 = (bf16[256,256]{1,0:T(8,128)(2,1)S(1)}, bf16[256,256]{1,0:T(8,128)(2,1)S(1)}, u32[]{:S(2)}, u32[]{:S(2)}) collective-permute-start(bf16[256,256]{1,0:T(8,128)(2,1)S(1)} %collective-permute-done.17.refs_2_), channel_id=1, source_target_pairs={{0,1},{1,0},{2,3},{3,2},{4,5},{5,4},{6,7},{7,6},{8,9},{9,8},{10,11... | collective-permute-start | bytes 393224 | tf_op jit(solution)/shard_map/ppermute | solution.py:31
  89.3 6.8 %collective-permute-start.20 = (bf16[256,256]{1,0:T(8,128)(2,1)S(1)}, bf16[256,256]{1,0:T(8,128)(2,1)S(1)}, u32[]{:S(2)}, u32[]{:S(2)}) collective-permute-start(bf16[256,256]{1,0:T(8,128)(2,1)S(1)} %attend_near.1.refs_4_), channel_id=1, source_target_pairs={{0,1},{1,0},{2,3},{3,2},{4,5},{5,4},{6,7},{7,6},{8,9},{9,8},{10,11... | collective-permute-start | bytes 393224 | tf_op jit(solution)/shard_map/ppermute | solution.py:31
  96.2 8.8 %collective-permute-start.25 = (bf16[128,1024]{1,0:T(8,128)(2,1)S(1)}, bf16[128,1024]{1,0:T(8,128)(2,1)S(1)}, u32[]{:S(2)}, u32[]{:S(2)}) collective-permute-start(bf16[128,1024]{1,0:T(8,128)(2,1)S(1)} %slice.82), channel_id=1, source_target_pairs={{0,8},{4,12},{8,0},{12,4},{16,24},{20,28},{24,16},{28,20},{1,9},{5... | collective-permute-start | bytes 786440 | tf_op jit(solution)/shard_map/ppermute | solution.py:31
  97.9 11.3 %collective-permute-start.18 = (bf16[256,256]{1,0:T(8,128)(2,1)S(1)}, bf16[256,256]{1,0:T(8,128)(2,1)S(1)}, u32[]{:S(2)}, u32[]{:S(2)}) collective-permute-start(bf16[256,256]{1,0:T(8,128)(2,1)S(1)} %attend_one.1.refs_0_), channel_id=1, source_target_pairs={{0,1},{1,0},{2,3},{3,2},{4,5},{5,4},{6,7},{7,6},{8,9},{9,8},{10,11... | collective-permute-start | bytes 393224 | tf_op jit(solution)/shard_map/ppermute | solution.py:31
  98.0 11.3 %collective-permute-start.22 = (bf16[256,256]{1,0:T(8,128)(2,1)S(1)}, bf16[256,256]{1,0:T(8,128)(2,1)S(1)}, u32[]{:S(2)}, u32[]{:S(2)}) collective-permute-start(bf16[256,256]{1,0:T(8,128)(2,1)S(1)} %collective-permute-done.21.refs_6_), channel_id=1, source_target_pairs={{0,1},{1,0},{2,3},{3,2},{4,5},{5,4},{6,7},{7,6},{8,9},{9,8},{10,11... | collective-permute-start | bytes 393224 | tf_op jit(solution)/shard_map/ppermute | solution.py:31
  100.0 9.2 %collective-permute-start.26 = (bf16[128,1024]{1,0:T(8,128)(2,1)S(1)}, bf16[128,1024]{1,0:T(8,128)(2,1)S(1)}, u32[]{:S(2)}, u32[]{:S(2)}) collective-permute-start(bf16[128,1024]{1,0:T(8,128)(2,1)S(1)} %slice.83), channel_id=1, source_target_pairs={{0,16},{4,20},{8,24},{12,28},{16,0},{20,4},{24,8},{28,12},{1,17},{... | collective-permute-start | bytes 786440 | tf_op jit(solution)/shard_map/ppermute | solution.py:31
  109.2 4.4 %collective-permute-start.27 = (bf16[1024,1024]{1,0:T(8,128)(2,1)S(1)}, bf16[1024,1024]{1,0:T(8,128)(2,1)S(1)}, u32[]{:S(2)}, u32[]{:S(2)}) collective-permute-start(bf16[1024,1024]{1,0:T(8,128)(2,1)S(1)} %constant_dynamic-update-slice_fusion.held_ref), channel_id=1, source_target_pairs={{0,4},{4,0},{8,12},{12,8},{16,20},{20,16},{24,28},{28,24},{1,5},{5... | collective-permute-start | bytes 6291464 | tf_op jit(solution)/shard_map/ppermute | solution.py:31
  117.6 17.7 %collective-permute-start.28 = (bf16[256,1024]{1,0:T(8,128)(2,1)S(1)}, bf16[256,1024]{1,0:T(8,128)(2,1)S(1)}, u32[]{:S(2)}, u32[]{:S(2)}) collective-permute-start(bf16[256,1024]{1,0:T(8,128)(2,1)S(1)} %feed_partner.1), channel_id=1, source_target_pairs={{0,1},{1,0},{2,3},{3,2},{4,5},{5,4},{6,7},{7,6},{8,9},{9,8},{10,11... | collective-permute-start | bytes 1572872 | tf_op jit(solution)/shard_map/ppermute | solution.py:31
  119.7 13.6 %collective-permute-start.29 = (f32[3,2,1024]{2,1,0:T(2,128)S(1)}, f32[3,2,1024]{2,1,0:T(2,128)S(1)}, u32[]{:S(2)}, u32[]{:S(2)}) collective-permute-start(f32[3,2,1024]{2,1,0:T(2,128)S(1)} %get-tuple-element.66), channel_id=1, source_target_pairs={{0,1},{1,0},{2,3},{3,2},{4,5},{5,4},{6,7},{7,6},{8,9},{9,8},{10,11... | collective-permute-start | bytes 73736 | tf_op jit(solution)/shard_map/ppermute | solution.py:31
  119.8 13.5 %collective-permute-start.30 = (f32[3,2,1024]{2,1,0:T(2,128)S(1)}, f32[3,2,1024]{2,1,0:T(2,128)S(1)}, u32[]{:S(2)}, u32[]{:S(2)}) collective-permute-start(f32[3,2,1024]{2,1,0:T(2,128)S(1)} %get-tuple-element.65), channel_id=1, source_target_pairs={{0,2},{1,3},{2,0},{3,1},{4,6},{5,7},{6,4},{7,5},{8,10},{9,11},{10,... | collective-permute-start | bytes 73736 | tf_op jit(solution)/shard_map/ppermute | solution.py:31
  121.5 13.2 %collective-permute-start.31 = (f32[3,2,1024]{2,1,0:T(2,128)S(1)}, f32[3,2,1024]{2,1,0:T(2,128)S(1)}, u32[]{:S(2)}, u32[]{:S(2)}) collective-permute-start(f32[3,2,1024]{2,1,0:T(2,128)S(1)} %get-tuple-element.64), channel_id=1, source_target_pairs={{0,3},{1,2},{2,1},{3,0},{4,7},{5,6},{6,5},{7,4},{8,11},{9,10},{10,... | collective-permute-start | bytes 73736 | tf_op jit(solution)/shard_map/ppermute | solution.py:31
  (24 other events, 204.0 us)

commit v16 on v15

--- a/solution.py
+++ b/solution.py
@@ -136,13 +136,17 @@
         out_ref[:, start : start + 2 * HD] = jnp.where(lane < HD, halves[0], halves[1]).astype(BF16)
 
 
-def attend_kernel(flips, has_halo, *refs):
+def attend_kernel(flips, has_halo, joins, *refs):
     place_ref, starts_ref, ends_ref, query0_ref, keyval0_ref, query1_ref, keyval1_ref, query2_ref, keyval2_ref = refs[:9]
     even_ref, odd_ref = refs[9:11] if has_halo else (None, None)
     out_ref, window_ref, bias_ref, scores_ref, weights_ref, sems = refs[-6:]
     tok, kv = place_ref[0], place_ref[1]
-    count = out_ref.shape[0]
+    count = bias_ref.shape[0]
     blocks = 4
+    if joins:
+        out_ref[:count] = refs[-7][...]
+        out_ref[2 * count :] = jnp.zeros_like(out_ref[2 * count :])
+        out_ref = out_ref.at[count : 2 * count]
     inner = is_inner(kv)
     outer = jnp.logical_not(inner)
     block = kv ^ jnp.where(inner, flips[1], flips[0])
@@ -182,12 +186,12 @@
     attend(query, window_ref, bias_ref, scores_ref, weights_ref, out_ref)
 
 
-def attend_block(place, starts, ends, projected, flips, name, halo=()):
+def attend_block(place, starts, ends, projected, flips, name, halo=(), earlier=(), spare=0):
     rows, heads_width = projected[-2].shape
     return pl.pallas_call(
-        functools.partial(attend_kernel, flips, bool(halo)),
-        out_shape=jax.ShapeDtypeStruct((rows, heads_width), BF16),
-        in_specs=[SMEM, VMEM, VMEM] + [VMEM, ANY] * 3 + [ANY] * len(halo),
+        functools.partial(attend_kernel, flips, bool(halo), bool(earlier)),
+        out_shape=jax.ShapeDtypeStruct(((1 + len(earlier)) * rows + spare, heads_width), BF16),
+        in_specs=[SMEM, VMEM, VMEM] + [VMEM, ANY] * 3 + [ANY] * len(halo) + [VMEM] * len(earlier),
         out_specs=VMEM,
         scratch_shapes=[
             pltpu.VMEM((3 * rows, 2 * heads_width), BF16),
@@ -199,12 +203,12 @@
         compiler_params=pltpu.CompilerParams(vmem_limit_bytes=12 * MIB),
         cost_estimate=SHORT,
         name=name,
-    )(place, starts, ends, *projected, *halo)
+    )(place, starts, ends, *projected, *halo, *earlier)
 
 
 def first_norm_kernel(layout, place_ref, own_ref, partner_ref, own_out_ref, gain_ref, bias_ref, *refs):
-    parts, pieces = refs[:8], refs[8 : 8 + len(layout)]
-    normed_ref, away_ref, all_ref, weight_ref, mixed_ref, sems = refs[8 + len(layout) :]
+    parts, pieces = refs[:4], refs[4 : 4 + len(layout)]
+    normed_ref, away_ref, all_ref, weight_ref, mixed_ref, sems = refs[4 + len(layout) :]
     tok, kv = place_ref[0], place_ref[1]
     quarters, heads_width, width = weight_ref.shape
     count = own_ref.shape[0]
@@ -218,11 +222,11 @@
     for copy in copies:
         copy.start()
     early = jnp.where(is_inner(kv), 0, 1)
-    for index, part_ref in enumerate(parts):
-        flip = index % 4
-        half = early if index < 4 else 1 - early
-        at = pl.ds(pl.multiple_of(half * count, count), count)
-        all_ref[at, flip * heads_width : (flip + 1) * heads_width] = part_ref[...]
+    for flip, part_ref in enumerate(parts):
+        for half, place in enumerate((early, 1 - early)):
+            at = pl.ds(pl.multiple_of(place * count, count), count)
+            columns = slice(flip * heads_width, (flip + 1) * heads_width)
+            all_ref[at, columns] = part_ref[half * count : (half + 1) * count]
     for copy in copies:
         copy.wait()
     weight = weight_ref[...].reshape(quarters * heads_width, width)
@@ -270,21 +274,21 @@
     return jnp.dot(units_ref[...], down_ref[...], preferred_element_type=F32)
 
 
-def far_copies(tok, held_ref, core_ref, up_ref, down_ref, sems):
+def far_copies(tok, pieces, up_ref, down_ref, sems):
     block = 128
     copies = []
-    for side, piece in enumerate((held_ref, core_ref)):
-        for index in range(4):
-            at = pl.ds(pl.multiple_of((tok ^ (2 * index + side)) * block, block), block)
-            for part, target in enumerate((up_ref, down_ref)):
-                source = piece.at[pl.ds((2 * index + part) * block, block)]
+    for target, sides in ((up_ref, pieces[:2]), (down_ref, pieces[2:])):
+        for side, piece in enumerate(sides):
+            for index in range(4):
+                at = pl.ds(pl.multiple_of((tok ^ (2 * index + side)) * block, block), block)
+                source = piece.at[pl.ds(index * block, block)]
                 copies.append(pltpu.make_async_copy(source, target.at[at], sems.at[len(copies)]))
     return copies
 
 
-def feed_kernel(place_ref, rows_ref, up_near_ref, down_near_ref, held_ref, core_ref, *refs):
-    sum_ref, up_ref, down_ref, wide_ref, units_ref, total_ref, sems = refs
-    copies = far_copies(place_ref[0], held_ref, core_ref, up_ref, down_ref, sems)
+def feed_kernel(place_ref, rows_ref, up_near_ref, down_near_ref, *refs):
+    pieces, (sum_ref, up_ref, down_ref, wide_ref, units_ref, total_ref, sems) = refs[:4], refs[4:]
+    copies = far_copies(place_ref[0], pieces, up_ref, down_ref, sems)
     for copy in copies:
         copy.start()
     rows = rows_ref[...]
@@ -310,7 +314,7 @@
     return pl.pallas_call(
         feed_kernel,
         out_shape=jax.ShapeDtypeStruct((count, width), dtype),
-        in_specs=[SMEM] + [VMEM] * 3 + [ANY] * 2,
+        in_specs=[SMEM] + [VMEM] * 3 + [ANY] * len(pieces),
         out_specs=VMEM,
         scratch_shapes=[
             pltpu.VMEM((width, units), BF16),
@@ -466,52 +470,48 @@
     first = project_call(
         project_first_kernel, "project_first", 3 * rows, *sizes, (weight, hidden_in, a1, b1), 0, [pltpu.VMEM((3 * rows, width), BF16)]
     )
-    a3 = lax.ppermute(after(b2, first[0]), "kv", outward)
+    a3 = lax.ppermute(after(b2, a2, first[0]), "kv", outward)
     second = project_call(project_second_kernel, "project_second", rows, *sizes, (place, weight, a2, b2))
     out_far = swapped(out_y, "tok", 2)
-    inner = (kv == 1) | (kv == 2)
 
     order = jnp.arange(stretch_len.shape[0])
     ends = jnp.sum(jnp.where(order[:, None] <= order[None, :], stretch_len[:, None], 0), axis=0, dtype=jnp.int32)
     starts = (ends - stretch_len)[None, :]
     ends = ends[None, :]
 
-    feed_up, feed_down = after((eighth(up_weight), eighth(down_weight)), a2, b2)
-    inner_up = lax.ppermute(feed_up, "kv", [(0, 2), (3, 1)])
-    inner_down = lax.ppermute(feed_down, "kv", [(0, 2), (3, 1)])
-    feed_part = jnp.concatenate([feed_up, feed_down], axis=0)
-    feed_part = after(feed_part, a3, second[0], out_x, out_y, inner_up, inner_down)
-    feed_outer = lax.ppermute(feed_part, "kv", [(1, 3), (2, 0)])
-    feed_inner = jnp.concatenate([inner_up, inner_down], axis=0)
+    up_here = swapped(after(eighth(up_weight), a3), "kv", 2)
+    down_here = swapped(after(eighth(down_weight), a3), "kv", 2)
 
     *last, even, odd = project_call(
         project_last_kernel, "project_last", rows, *sizes, (place, weight, first[1], second[1], a3), 2
     )
     halo = over_edges(even, "tok", 0), over_edges(odd, "tok", 1)
     projected = (*first, *second, *last)
-    two = attend_block(place, starts, ends, projected, (2, 3), "attend_two")
-    two_there = swapped(two, "kv", 2)
+    two = attend_block(after(place, halo[0]), starts, ends, projected, (2, 3), "attend_two")
+    up_late = after(up_here, two)
+    up_x, up_y = swapped(up_late, "tok", 2), swapped(up_late, "tok", 4)
     out_all = jnp.stack([out_here, out_x, out_y, out_far])
     out_core = swapped(out_all, "tok", 1)
-    feed_here = jnp.where(inner, feed_inner, after(feed_outer, two))
-    feed_x, feed_y = swapped(feed_here, "tok", 2), swapped(feed_here, "tok", 4)
-    far = attend_block(after(place, feed_here, out_core), starts, ends, projected, (3, 2), "attend_far", halo)
+    queries = jnp.concatenate([dec_query] + [other[depth:] for other in others], axis=0)
+    queries = after(queries, two).astype(F32)
+    partial = decode_partial(queries, dec_query.shape[0], kv_cache, piece_req, piece_used)
+    far = attend_block(after(place, up_late, out_core, partial), starts, ends, projected, (3, 2), "attend_far", halo, (two,), 32)
     far_there = swapped(far, "kv", 2)
-    two_passed = swapped(after(two_there, far), "kv", 1)
-    one = attend_block(after(place, far, two_there), starts, ends, projected, (1, 0), "attend_one")
-    one_there = swapped(one, "kv", 1)
-    near = attend_block(after(place, one), starts, ends, projected, (0, 1), "attend_near", halo)
-    near_there, far_passed = swapped(near, "kv", 1), swapped(far_there, "kv", 1)
-    parts = (one, one_there, two_there, two_passed, near, near_there, far_there, far_passed)
+    one = attend_block(after(place, far), starts, ends, projected, (1, 0), "attend_one")
+    near = attend_block(after(place, one, down_here, up_x, up_y), starts, ends, projected, (0, 1), "attend_near", halo, (one,), 16)
+    near_there = swapped(near, "kv", 1)
+    down_late = after(down_here, near)
+    down_x, down_y = swapped(down_late, "tok", 2), swapped(down_late, "tok", 4)
+    far_passed = swapped(far_there, "kv", 1)
+    parts = (near, near_there, far_there, far_passed)
     out_pieces = [((0, 2, 4, 6), out_all), ((1, 3, 5, 7), out_core)]
-    queries = jnp.concatenate([dec_query] + [other[depth:] for other in others], axis=0)
-    queries = after(queries, near, two_passed).astype(F32)
-    partial = decode_partial(queries, dec_query.shape[0], kv_cache, piece_req, piece_used)
-    half = feed_here.shape[0] // 2
-    far_up = swapped(after(feed_y, far_there, near_there, partial)[:half], "tok", 2)
-    far_down = swapped(after(feed_x, far_there, near_there, partial)[half:], "tok", 4)
-    held = jnp.concatenate([feed_here, feed_x, feed_y, far_up, far_down], axis=0)
-    feed_pieces = (held, swapped(after(held, far_passed, one_there), "tok", 1))
+    up_far = swapped(after(up_y, near_there, far_there), "tok", 2)
+    down_far = swapped(after(down_x, near_there, far_there), "tok", 4)
+    up_held = jnp.concatenate([up_late, up_x, up_y, up_far], axis=0)
+    down_held = jnp.concatenate([down_late, down_x, down_y, down_far], axis=0)
+    up_core = swapped(after(up_held, near_there), "tok", 1)
+    down_core = swapped(after(down_held, far_passed), "tok", 1)
+    feed_pieces = (up_held, up_core, down_held, down_core)
 
     gain, bias = ln1_gain[None, :], ln1_bias[None, :]
     normed, partner = first_norm(place, hidden_in, a1, out_weight, gain, bias, parts, out_pieces)

time: 137 us -> 145 us (1.058)
  waiting for transfers between devices: 32.3 us -> 61.6 us
  starting transfers between devices: 53.8 us -> 39.4 us
  other arithmetic: 7.58 us -> 2.8 us
    ppermute x22 -> x24, waiting for transfers between devices: 22.8 us -> 52.1 us  [swapped(): return lax.ppermute(value, axis, [(i, i ^ flip) for i in range(count)])]
    ppermute x4 -> x1, starting transfers between devices: 14.2 us -> 1.28 us  [routed_body(): a3 = lax.ppermute(after(b2, a2, first[0]), 'kv', outward)]
    ppermute x5, waiting for transfers between devices: 4.9 us -> 0.17 us  [over_edges(): return lax.ppermute(value, axis, edges + [(j, i) for i, j in edges])]
    ppermute x1, waiting for transfers between devices: 0.01 us -> 4.39 us  [routed_body(): a2, b2 = (lax.ppermute(b1, 'kv', outward), over_edges(a1, 'kv', 1))]
    ppermute x22 -> x24, starting transfers between devices: 31.1 us -> 27.8 us  [swapped(): return lax.ppermute(value, axis, [(i, i ^ flip) for i in range(count)])]
    concatenate x1 -> x0, other arithmetic: 1.86 us -> none  [routed_body(): feed_part = jnp.concatenate([feed_up, feed_down], axis=0)]
    ppermute x5, starting transfers between devices: 7.27 us -> 9 us  [over_edges(): return lax.ppermute(value, axis, edges + [(j, i) for i, j in edges])]
    unnamed x45 -> x46, local copies, waits for them, and re-layouts: 3.89 us -> 3.44 us
  transfers between devices with their start and end apart: 32 -> 31, of which waited for: 12 -> 12; matrix products, arithmetic and copies ran while one was open for 8% -> 3% of each run, Pallas kernels for 22% -> 20%
where the time goes in v16:
time: 145 us; the launch traced here: 144 us
  waiting for transfers between devices  61.6 us (42%)
  starting transfers between devices  39.4 us (27%)
  Pallas kernels  33.8 us (23%)
  local copies, waits for them, and re-layouts  5.46 us (4%)
  other arithmetic  2.8 us (2%)
    ppermute x24, waiting for transfers between devices, swapped(): return lax.ppermute(value, axis, [(i, i ^ flip) for i in range(count)])  52.1 us
    ppermute x24, starting transfers between devices, swapped(): return lax.ppermute(value, axis, [(i, i ^ flip) for i in range(count)])  27.8 us
    pallas_call x4, Pallas kernels, attend_block(): pl.pallas_call(functools.partial(attend_kernel, flips, bool(halo), bool(e...  11.8 us
    ppermute x5, starting transfers between devices, over_edges(): return lax.ppermute(value, axis, edges + [(j, i) for i, j in edges])  9 us
    pallas_call x2, Pallas kernels, feed(): pl.pallas_call(feed_kernel, out_shape=jax.ShapeDtypeStruct((count, width)...  7.8 us
    pallas_call x3, Pallas kernels, project_call(): pl.pallas_call(kernel, out_shape=(jax.ShapeDtypeStruct((rows, heads_width...  5.83 us
    ppermute x1, waiting for transfers between devices, routed_body(): a3 = lax.ppermute(after(b2, a2, first[0]), 'kv', outward)  4.88 us
    ppermute x1, waiting for transfers between devices, routed_body(): a2, b2 = (lax.ppermute(b1, 'kv', outward), over_edges(a1, 'kv', 1))  4.39 us
  transfers between devices with their start and end apart: 31, of which 12 were waited for; matrix products, arithmetic and copies ran while one was open for 3% of the time, Pallas kernels for 20%

profile of v16, /device:TPU:0, one launch (start us, length us, event | category | flops | bytes accessed | tf_op | source)
XLA Modules:
  0.0 144.2 jit_solution(8038405330722518745)
XLA Ops:
  0.6 1.5 %collective-permute-start.2 = (bf16[256,1024]{1,0:T(8,128)(2,1)}, bf16[256,1024]{1,0:T(8,128)(2,1)}, u32[]{:S(2)}, u32[]{:S(2)}) collective-permute-start(bf16[256,1024]{1,0:T(8,128)(2,1)} %own_ref.3), channel_id=1, source_target_pairs={{1,2},{2,1},{5,6},{6,5},{9,10},{10,9},{13,14},{14,13},{17,18},{18,... | collective-permute-start | bytes 1572872 | tf_op jit(solution)/shard_map/ppermute | solution.py:37
  2.1 5.1 %collective-permute-start = (bf16[256,1024]{1,0:T(8,128)(2,1)}, bf16[256,1024]{1,0:T(8,128)(2,1)S(1)}, u32[]{:S(2)}, u32[]{:S(2)}) collective-permute-start(bf16[256,1024]{1,0:T(8,128)(2,1)} %own_ref.3), channel_id=1, source_target_pairs={{0,1},{2,3},{1,0},{3,2},{4,5},{6,7},{5,4},{7,6},{8,9},{10,11},{9,8... | collective-permute-start | bytes 1572872 | tf_op jit(solution)/shard_map/ppermute | solution.py:37
  10.2 2.9 %collective-permute-start.7 = (bf16[34,1024]{1,0:T(8,128)(2,1)S(1)}, bf16[34,1024]{1,0:T(8,128)(2,1)S(1)}, u32[]{:S(2)}, u32[]{:S(2)}) collective-permute-start(bf16[34,1024]{1,0:T(8,128)(2,1)S(1)} %pad_maximum_fusion.2), channel_id=1, source_target_pairs={{0,1},{1,0},{2,3},{3,2},{4,5},{5,4},{6,7},{7,6},{8,9},{9,8},{10,11... | collective-permute-start | bytes 208904 | tf_op jit(solution)/shard_map/ppermute | solution.py:31
  13.1 10.2 %collective-permute-done.9 = bf16[34,1024]{1,0:T(8,128)(2,1)S(1)} collective-permute-done((bf16[34,1024]{1,0:T(8,128)(2,1)S(1)}, bf16[34,1024]{1,0:T(8,128)(2,1)S(1)}, u32[]{:S(2)}, u32[]{:S(2)}) %collective-permute-start.9) | collective-permute-done | bytes 69664 | tf_op jit(solution)/shard_map/ppermute | solution.py:31
  26.2 1.6 %collective-permute-start.11 = (bf16[3,32,1024]{2,1,0:T(8,128)(2,1)S(1)}, bf16[3,32,1024]{2,1,0:T(8,128)(2,1)}, u32[]{:S(2)}, u32[]{:S(2)}) collective-permute-start(bf16[3,32,1024]{2,1,0:T(8,128)(2,1)S(1)} %pad_maximum_fusion.1), channel_id=1, source_target_pairs={{0,16},{4,20},{8,24},{12,28},{16,0},{20,4},{24,8},{28,12},{1,17},{... | collective-permute-start | bytes 589832 | tf_op jit(solution)/shard_map/ppermute | solution.py:31
  30.3 2.4 %project_first.1 = (bf16[768,256]{1,0:T(8,128)(2,1)S(1)}, bf16[768,512]{1,0:T(8,128)(2,1)S(1)}) custom-call(bf16[3,1024,256]{2,1,0:T(8,128)(2,1)S(1)} %bitcast.142, bf16[256,1024]{1,0:T(8,128)(2,1)S(1)} %copy-done.5, bf16[256,1024]{1,0:T(8,128)(2,1)S(1)} %collective-permute-done.a1_ref.partner_ref, bf16[256,1024]{1,0:T(8,128)(2,1)} %collective-permute-done.2.b1_ref), custom_call_target="tpu_custom_call" | custom-call | flops 1 | bytes 1 | tf_op jit(solution)/shard_map/project_first/pallas_call | solution.py:91
  32.7 4.4 %collective-permute-done.3.a2_ref = bf16[256,1024]{1,0:T(8,128)(2,1)S(1)} collective-permute-done((bf16[256,1024]{1,0:T(8,128)(2,1)}, bf16[256,1024]{1,0:T(8,128)(2,1)S(1)}, u32[]{:S(2)}, u32[]{:S(2)}) %collective-permute-start.3) | collective-permute-done | bytes 524320 | tf_op jit(solution)/shard_map/ppermute | solution.py:465
  39.2 1.6 %collective-permute-start.10 = (bf16[3,32,1024]{2,1,0:T(8,128)(2,1)S(1)}, bf16[3,32,1024]{2,1,0:T(8,128)(2,1)}, u32[]{:S(2)}, u32[]{:S(2)}) collective-permute-start(bf16[3,32,1024]{2,1,0:T(8,128)(2,1)S(1)} %pad_maximum_fusion.1), channel_id=1, source_target_pairs={{0,8},{4,12},{8,0},{12,4},{16,24},{20,28},{24,16},{28,20},{1,9},{5... | collective-permute-start | bytes 589832 | tf_op jit(solution)/shard_map/ppermute | solution.py:31
  41.4 3.8 %collective-permute-done.10 = bf16[3,32,1024]{2,1,0:T(8,128)(2,1)} collective-permute-done((bf16[3,32,1024]{2,1,0:T(8,128)(2,1)S(1)}, bf16[3,32,1024]{2,1,0:T(8,128)(2,1)}, u32[]{:S(2)}, u32[]{:S(2)}) %collective-permute-start.10) | collective-permute-done | bytes 196640 | tf_op jit(solution)/shard_map/ppermute | solution.py:31
  45.2 2.1 %collective-permute-done.12 = bf16[3,32,1024]{2,1,0:T(8,128)(2,1)} collective-permute-done((bf16[3,32,1024]{2,1,0:T(8,128)(2,1)}, bf16[3,32,1024]{2,1,0:T(8,128)(2,1)}, u32[]{:S(2)}, u32[]{:S(2)}) %collective-permute-start.12) | collective-permute-done | bytes 196640 | tf_op jit(solution)/shard_map/ppermute | solution.py:31
  49.7 1.6 %project_second.1 = (bf16[256,256]{1,0:T(8,128)(2,1)S(1)}, bf16[256,512]{1,0:T(8,128)(2,1)S(1)}) custom-call(s32[2]{0:T(128)S(1)} %pad_add_fusion.place_ref.refs_0_, bf16[3,1024,256]{2,1,0:T(8,128)(2,1)S(1)} %bitcast.143, bf16[256,1024]{1,0:T(8,128)(2,1)S(1)} %copy-done.9, bf16[256,1024]{1,0:T(8,128)(2,1)} %collective-permute-done.1.b2_ref), custom_call_target="tpu_custom_call" | custom-call | flops 1 | bytes 1 | tf_op jit(solution)/shard_map/project_second/pallas_call | solution.py:91
  51.3 4.9 %collective-permute-done.4.a3_ref = bf16[256,1024]{1,0:T(8,128)(2,1)} collective-permute-done((bf16[256,1024]{1,0:T(8,128)(2,1)}, bf16[256,1024]{1,0:T(8,128)(2,1)}, u32[]{:S(2)}, u32[]{:S(2)}) %collective-permute-start.4) | collective-permute-done | bytes 524320 | tf_op jit(solution)/shard_map/ppermute | solution.py:473
  56.2 6.0 %collective-permute-start.5 = (bf16[128,1024]{1,0:T(8,128)(2,1)S(1)}, bf16[128,1024]{1,0:T(8,128)(2,1)S(1)}, u32[]{:S(2)}, u32[]{:S(2)}) collective-permute-start(bf16[128,1024]{1,0:T(8,128)(2,1)S(1)} %get-tuple-element.35), channel_id=1, source_target_pairs={{0,2},{1,3},{2,0},{3,1},{4,6},{5,7},{6,4},{7,5},{8,10},{9,11},{10,... | collective-permute-start | bytes 786440 | tf_op jit(solution)/shard_map/ppermute | solution.py:31
  62.2 1.8 %project_last.1 = (bf16[256,256]{1,0:T(8,128)(2,1)S(1)}, bf16[256,512]{1,0:T(8,128)(2,1)S(1)}, bf16[256,512]{1,0:T(8,128)(2,1)S(1)}, bf16[256,512]{1,0:T(8,128)(2,1)S(1)}) custom-call(s32[2]{0:T(128)S(1)} %pad_add_fusion.place_ref.refs_0_, bf16[3,1024,256]{2,1,0:T(8,128)(2,1)S(1)} %bitcast.144, bf16[768,512]{1,0:T(8,128)(2,1)S(1)} %get-tuple-element.36.first_ref.refs_4_, ...), custom_call_target="tpu_custom_call" | custom-call | flops 1 | bytes 1 | tf_op jit(solution)/shard_map/project_last/pallas_call | solution.py:91
  65.6 2.9 %attend_two.1.refs_11_ = bf16[256,256]{1,0:T(8,128)(2,1)S(1)} custom-call(s32[2]{0:T(128)S(1)} %pad_add_fusion.place_ref.refs_0_, s32[1,48]{1,0:T(1,128)S(1)} %subtract_bitcast_fusion.refs_1_, s32[1,48]{1,0:T(1,128)S(1)} %bitcast.145, bf16[768,256]{1,0:T(8,128)(2,1)S(1)} %get-tuple-element.33.refs_3_, ...), custom_call_target="tpu_custom_call" | custom-call | flops 1 | bytes 1 | tf_op jit(solution)/shard_map/attend_two/pallas_call | solution.py:191
  68.5 12.1 %collective-permute-done.5 = bf16[128,1024]{1,0:T(8,128)(2,1)S(1)} collective-permute-done((bf16[128,1024]{1,0:T(8,128)(2,1)S(1)}, bf16[128,1024]{1,0:T(8,128)(2,1)S(1)}, u32[]{:S(2)}, u32[]{:S(2)}) %collective-permute-start.5) | collective-permute-done | bytes 262176 | tf_op jit(solution)/shard_map/ppermute | solution.py:31
  81.1 1.5 %collective-permute-start.16 = (bf16[128,1024]{1,0:T(8,128)(2,1)S(1)}, bf16[128,1024]{1,0:T(8,128)(2,1)S(1)}, u32[]{:S(2)}, u32[]{:S(2)}) collective-permute-start(bf16[128,1024]{1,0:T(8,128)(2,1)S(1)} %collective-permute-done.5), channel_id=1, source_target_pairs={{0,8},{4,12},{8,0},{12,4},{16,24},{20,28},{24,16},{28,20},{1,9},{5... | collective-permute-start | bytes 786440 | tf_op jit(solution)/shard_map/ppermute | solution.py:31
  82.7 3.8 %decode.1 = f32[3,8,1024]{2,1,0:T(8,128)S(1)} custom-call(s32[6]{0:T(128)S(1)} %fusion.12.slot_ref, s32[6]{0:T(128)S(1)} %bitcast.153, f32[8,1024]{1,0:T(8,128)S(1)} %convert_element_type.6.query_ref, bf16[2,1,6,128,1024]{4,3,2,1,0:T(8,128)(2,1)S(1)} %copy-done.4), custom_call_target="tpu_custom_call" | custom-call | flops 1 | bytes 1 | tf_op jit(solution)/shard_map/decode/pallas_call | solution.py:396
  86.5 2.9 %attend_far.1 = bf16[544,256]{1,0:T(8,128)(2,1)S(1)} custom-call(s32[2]{0:T(128)S(1)} %pad_add_fusion.place_ref.refs_0_, s32[1,48]{1,0:T(1,128)S(1)} %subtract_bitcast_fusion.refs_1_, s32[1,48]{1,0:T(1,128)S(1)} %bitcast.146, bf16[768,256]{1,0:T(8,128)(2,1)S(1)} %get-tuple-element.33.refs_3_, bf16[768,512]{1,0:T(8,128)(2,1)S(1)} %get-tuple-element.36.first_ref.refs_4_, ...), custom_call_target="tpu_custom_call" | custom-call | flops 1 | bytes 1 | tf_op jit(solution)/shard_map/attend_far/pallas_call | solution.py:191
  89.6 2.9 %attend_one.1.refs_11_ = bf16[256,256]{1,0:T(8,128)(2,1)S(1)} custom-call(s32[2]{0:T(128)S(1)} %pad_add_fusion.place_ref.refs_0_, s32[1,48]{1,0:T(1,128)S(1)} %subtract_bitcast_fusion.refs_1_, s32[1,48]{1,0:T(1,128)S(1)} %bitcast.147, bf16[768,256]{1,0:T(8,128)(2,1)S(1)} %get-tuple-element.33.refs_3_, ...), custom_call_target="tpu_custom_call" | custom-call | flops 1 | bytes 1 | tf_op jit(solution)/shard_map/attend_one/pallas_call | solution.py:191
  92.5 3.1 %attend_near.1.refs_0_ = bf16[528,256]{1,0:T(8,128)(2,1)S(1)} custom-call(s32[2]{0:T(128)S(1)} %pad_add_fusion.place_ref.refs_0_, s32[1,48]{1,0:T(1,128)S(1)} %subtract_bitcast_fusion.refs_1_, s32[1,48]{1,0:T(1,128)S(1)} %bitcast.148, bf16[768,256]{1,0:T(8,128)(2,1)S(1)} %get-tuple-element.33.refs_3_, ...), custom_call_target="tpu_custom_call" | custom-call | flops 1 | bytes 1 | tf_op jit(solution)/shard_map/attend_near/pallas_call | solution.py:191
  95.7 2.0 %collective-permute-start.18 = (bf16[528,256]{1,0:T(8,128)(2,1)S(1)}, bf16[528,256]{1,0:T(8,128)(2,1)S(1)}, u32[]{:S(2)}, u32[]{:S(2)}) collective-permute-start(bf16[528,256]{1,0:T(8,128)(2,1)S(1)} %attend_near.1.refs_0_), channel_id=1, source_target_pairs={{0,1},{1,0},{2,3},{3,2},{4,5},{5,4},{6,7},{7,6},{8,9},{9,8},{10,11... | collective-permute-start | bytes 811016 | tf_op jit(solution)/shard_map/ppermute | solution.py:31
  98.2 1.6 %collective-permute-start.24 = (bf16[128,1024]{1,0:T(8,128)(2,1)S(1)}, bf16[128,1024]{1,0:T(8,128)(2,1)S(1)}, u32[]{:S(2)}, u32[]{:S(2)}) collective-permute-start(bf16[128,1024]{1,0:T(8,128)(2,1)S(1)} %collective-permute-done.15), channel_id=1, source_target_pairs={{0,16},{4,20},{8,24},{12,28},{16,0},{20,4},{24,8},{28,12},{1,17},{... | collective-permute-start | bytes 786440 | tf_op jit(solution)/shard_map/ppermute | solution.py:31
  99.9 8.8 %collective-permute-done.18.refs_1_ = bf16[528,256]{1,0:T(8,128)(2,1)S(1)} collective-permute-done((bf16[528,256]{1,0:T(8,128)(2,1)S(1)}, bf16[528,256]{1,0:T(8,128)(2,1)S(1)}, u32[]{:S(2)}, u32[]{:S(2)}) %collective-permute-start.18) | collective-permute-done | bytes 270368 | tf_op jit(solution)/shard_map/ppermute | solution.py:31
  109.2 1.6 %collective-permute-start.25 = (bf16[128,1024]{1,0:T(8,128)(2,1)S(1)}, bf16[128,1024]{1,0:T(8,128)(2,1)S(1)}, u32[]{:S(2)}, u32[]{:S(2)}) collective-permute-start(bf16[128,1024]{1,0:T(8,128)(2,1)S(1)} %collective-permute-done.23), channel_id=1, source_target_pairs={{0,16},{4,20},{8,24},{12,28},{16,0},{20,4},{24,8},{28,12},{1,17},{... | collective-permute-start | bytes 786440 | tf_op jit(solution)/shard_map/ppermute | solution.py:31
  110.9 5.9 %collective-permute-done.21 = bf16[128,1024]{1,0:T(8,128)(2,1)S(1)} collective-permute-done((bf16[128,1024]{1,0:T(8,128)(2,1)S(1)}, bf16[128,1024]{1,0:T(8,128)(2,1)S(1)}, u32[]{:S(2)}, u32[]{:S(2)}) %collective-permute-start.21) | collective-permute-done | bytes 262176 | tf_op jit(solution)/shard_map/ppermute | solution.py:31
  117.2 1.7 %collective-permute-done.20.refs_3_ = bf16[544,256]{1,0:T(8,128)(2,1)S(1)} collective-permute-done((bf16[544,256]{1,0:T(8,128)(2,1)S(1)}, bf16[544,256]{1,0:T(8,128)(2,1)S(1)}, u32[]{:S(2)}, u32[]{:S(2)}) %collective-permute-start.20) | collective-permute-done | bytes 278560 | tf_op jit(solution)/shard_map/ppermute | solution.py:31
  118.9 3.3 %first_norm.1 = (bf16[256,1024]{1,0:T(8,128)(2,1)S(1)}, bf16[256,1024]{1,0:T(8,128)(2,1)S(1)}) custom-call(s32[2]{0:T(128)S(1)} %pad_add_fusion.place_ref.refs_0_, bf16[256,1024]{1,0:T(8,128)(2,1)S(1)} %copy-done.6, bf16[256,1024]{1,0:T(8,128)(2,1)S(1)} %collective-permute-done.a1_ref.partner_ref, bf16[256,1024]{1,0:T(8,128)(2,1)S(1)} %copy-done.7, ...), custom_call_target="tpu_custom_call" | custom-call | flops 1 | bytes 1 | tf_op jit(solution)/shard_map/first_norm/pallas_call | solution.py:245
  122.3 3.9 %feed_partner.1 = bf16[256,1024]{1,0:T(8,128)(2,1)S(1)} custom-call(s32[2]{0:T(128)S(1)} %pad_add_fusion.place_ref.refs_0_, bf16[256,1024]{1,0:T(8,128)(2,1)S(1)} %get-tuple-element.52.rows_ref, bf16[1024,1024]{1,0:T(8,128)(2,1)S(1)} %copy-done.2, bf16[1024,1024]{1,0:T(8,128)(2,1)S(1)} %copy-done.3, ...), custom_call_target="tpu_custom_call" | custom-call | flops 1 | bytes 1 | tf_op jit(solution)/shard_map/feed_partner/pallas_call | solution.py:314
  126.6 2.5 %collective-permute-start.30 = (f32[3,2,1024]{2,1,0:T(2,128)S(1)}, f32[3,2,1024]{2,1,0:T(2,128)S(1)}, u32[]{:S(2)}, u32[]{:S(2)}) collective-permute-start(f32[3,2,1024]{2,1,0:T(2,128)S(1)} %get-tuple-element.64), channel_id=1, source_target_pairs={{0,3},{1,2},{2,1},{3,0},{4,7},{5,6},{6,5},{7,4},{8,11},{9,10},{10,... | collective-permute-start | bytes 73736 | tf_op jit(solution)/shard_map/ppermute | solution.py:31
  131.1 3.9 %feed_own.1.near_ref = f32[256,1024]{1,0:T(8,128)S(1)} custom-call(s32[2]{0:T(128)S(1)} %pad_add_fusion.place_ref.refs_0_, bf16[256,1024]{1,0:T(8,128)(2,1)S(1)} %get-tuple-element.58.rows_ref.normed_ref, bf16[1024,1024]{1,0:T(8,128)(2,1)S(1)} %copy-done.2, bf16[1024,1024]{1,0:T(8,128)(2,1)S(1)} %copy-done.3, ...), custom_call_target="tpu_custom_call" | custom-call | flops 1 | bytes 1 | tf_op jit(solution)/shard_map/feed_own/pallas_call | solution.py:314
  135.0 7.3 %collective-permute-done.30 = f32[3,2,1024]{2,1,0:T(2,128)S(1)} collective-permute-done((f32[3,2,1024]{2,1,0:T(2,128)S(1)}, f32[3,2,1024]{2,1,0:T(2,128)S(1)}, u32[]{:S(2)}, u32[]{:S(2)}) %collective-permute-start.30) | collective-permute-done | bytes 24608 | tf_op jit(solution)/shard_map/ppermute | solution.py:31
  (111 shorter events, 21.5 us)
Async XLA Ops:
  0.6 22.7 %collective-permute-start.2 = (bf16[256,1024]{1,0:T(8,128)(2,1)}, bf16[256,1024]{1,0:T(8,128)(2,1)}, u32[]{:S(2)}, u32[]{:S(2)}) collective-permute-start(bf16[256,1024]{1,0:T(8,128)(2,1)} %own_ref.3), channel_id=1, source_target_pairs={{1,2},{2,1},{5,6},{6,5},{9,10},{10,9},{13,14},{14,13},{17,18},{18,... | collective-permute-start | bytes 1572872 | tf_op jit(solution)/shard_map/ppermute | solution.py:37
  2.1 22.6 %collective-permute-start = (bf16[256,1024]{1,0:T(8,128)(2,1)}, bf16[256,1024]{1,0:T(8,128)(2,1)S(1)}, u32[]{:S(2)}, u32[]{:S(2)}) collective-permute-start(bf16[256,1024]{1,0:T(8,128)(2,1)} %own_ref.3), channel_id=1, source_target_pairs={{0,1},{2,3},{1,0},{3,2},{4,5},{6,7},{5,4},{7,6},{8,9},{10,11},{9,8... | collective-permute-start | bytes 1572872 | tf_op jit(solution)/shard_map/ppermute | solution.py:37
  8.8 14.6 %collective-permute-start.9 = (bf16[34,1024]{1,0:T(8,128)(2,1)S(1)}, bf16[34,1024]{1,0:T(8,128)(2,1)S(1)}, u32[]{:S(2)}, u32[]{:S(2)}) collective-permute-start(bf16[34,1024]{1,0:T(8,128)(2,1)S(1)} %pad_maximum_fusion.2), channel_id=1, source_target_pairs={{0,3},{1,2},{2,1},{3,0},{4,7},{5,6},{6,5},{7,4},{8,11},{9,10},{10,... | collective-permute-start | bytes 208904 | tf_op jit(solution)/shard_map/ppermute | solution.py:31
  10.1 16.1 %collective-permute-start.8 = (bf16[34,1024]{1,0:T(8,128)(2,1)S(1)}, bf16[34,1024]{1,0:T(8,128)(2,1)S(1)}, u32[]{:S(2)}, u32[]{:S(2)}) collective-permute-start(bf16[34,1024]{1,0:T(8,128)(2,1)S(1)} %pad_maximum_fusion.2), channel_id=1, source_target_pairs={{0,2},{1,3},{2,0},{3,1},{4,6},{5,7},{6,4},{7,5},{8,10},{9,11},{10,... | collective-permute-start | bytes 208904 | tf_op jit(solution)/shard_map/ppermute | solution.py:31
  10.2 15.9 %collective-permute-start.7 = (bf16[34,1024]{1,0:T(8,128)(2,1)S(1)}, bf16[34,1024]{1,0:T(8,128)(2,1)S(1)}, u32[]{:S(2)}, u32[]{:S(2)}) collective-permute-start(bf16[34,1024]{1,0:T(8,128)(2,1)S(1)} %pad_maximum_fusion.2), channel_id=1, source_target_pairs={{0,1},{1,0},{2,3},{3,2},{4,5},{5,4},{6,7},{7,6},{8,9},{9,8},{10,11... | collective-permute-start | bytes 208904 | tf_op jit(solution)/shard_map/ppermute | solution.py:31
  23.4 13.8 %collective-permute-start.3 = (bf16[256,1024]{1,0:T(8,128)(2,1)}, bf16[256,1024]{1,0:T(8,128)(2,1)S(1)}, u32[]{:S(2)}, u32[]{:S(2)}) collective-permute-start(bf16[256,1024]{1,0:T(8,128)(2,1)} %collective-permute-done.2.b1_ref), channel_id=1, source_target_pairs={{1,0},{2,3},{5,4},{6,7},{9,8},{10,11},{13,12},{14,15},{17,16},{18,... | collective-permute-start | bytes 1572872 | tf_op jit(solution)/shard_map/ppermute | solution.py:465
  24.7 1.6 %collective-permute-start.1 = (bf16[256,1024]{1,0:T(8,128)(2,1)S(1)}, bf16[256,1024]{1,0:T(8,128)(2,1)}, u32[]{:S(2)}, u32[]{:S(2)}) collective-permute-start(bf16[256,1024]{1,0:T(8,128)(2,1)S(1)} %collective-permute-done.a1_ref.partner_ref), channel_id=1, source_target_pairs={{1,2},{2,1},{5,6},{6,5},{9,10},{10,9},{13,14},{14,13},{17,18},{18,... | collective-permute-start | bytes 1572872 | tf_op jit(solution)/shard_map/ppermute | solution.py:37
  26.2 14.5 %collective-permute-start.11 = (bf16[3,32,1024]{2,1,0:T(8,128)(2,1)S(1)}, bf16[3,32,1024]{2,1,0:T(8,128)(2,1)}, u32[]{:S(2)}, u32[]{:S(2)}) collective-permute-start(bf16[3,32,1024]{2,1,0:T(8,128)(2,1)S(1)} %pad_maximum_fusion.1), channel_id=1, source_target_pairs={{0,16},{4,20},{8,24},{12,28},{16,0},{20,4},{24,8},{28,12},{1,17},{... | collective-permute-start | bytes 589832 | tf_op jit(solution)/shard_map/ppermute | solution.py:31
  37.9 18.3 %collective-permute-start.4 = (bf16[256,1024]{1,0:T(8,128)(2,1)}, bf16[256,1024]{1,0:T(8,128)(2,1)}, u32[]{:S(2)}, u32[]{:S(2)}) collective-permute-start(bf16[256,1024]{1,0:T(8,128)(2,1)} %collective-permute-done.1.b2_ref), channel_id=1, source_target_pairs={{1,0},{2,3},{5,4},{6,7},{9,8},{10,11},{13,12},{14,15},{17,16},{18,... | collective-permute-start | bytes 1572872 | tf_op jit(solution)/shard_map/ppermute | solution.py:473
  39.2 6.0 %collective-permute-start.10 = (bf16[3,32,1024]{2,1,0:T(8,128)(2,1)S(1)}, bf16[3,32,1024]{2,1,0:T(8,128)(2,1)}, u32[]{:S(2)}, u32[]{:S(2)}) collective-permute-start(bf16[3,32,1024]{2,1,0:T(8,128)(2,1)S(1)} %pad_maximum_fusion.1), channel_id=1, source_target_pairs={{0,8},{4,12},{8,0},{12,4},{16,24},{20,28},{24,16},{28,20},{1,9},{5... | collective-permute-start | bytes 589832 | tf_op jit(solution)/shard_map/ppermute | solution.py:31
  40.8 6.5 %collective-permute-start.12 = (bf16[3,32,1024]{2,1,0:T(8,128)(2,1)}, bf16[3,32,1024]{2,1,0:T(8,128)(2,1)}, u32[]{:S(2)}, u32[]{:S(2)}) collective-permute-start(bf16[3,32,1024]{2,1,0:T(8,128)(2,1)} %collective-permute-done.11), channel_id=1, source_target_pairs={{0,8},{4,12},{8,0},{12,4},{16,24},{20,28},{24,16},{28,20},{1,9},{5... | collective-permute-start | bytes 589832 | tf_op jit(solution)/shard_map/ppermute | solution.py:31
  48.5 38.0 %collective-permute-start.13 = (bf16[4,3,32,1024]{3,2,1,0:T(8,128)(2,1)S(1)}, bf16[4,3,32,1024]{3,2,1,0:T(8,128)(2,1)S(1)}, u32[]{:S(2)}, u32[]{:S(2)}) collective-permute-start(bf16[4,3,32,1024]{3,2,1,0:T(8,128)(2,1)S(1)} %pad_maximum_fusion.refs_4_), channel_id=1, source_target_pairs={{0,4},{4,0},{8,12},{12,8},{16,20},{20,16},{24,28},{28,24},{1,5},{5... | collective-permute-start | bytes 2359304 | tf_op jit(solution)/shard_map/ppermute | solution.py:31
  56.2 24.4 %collective-permute-start.5 = (bf16[128,1024]{1,0:T(8,128)(2,1)S(1)}, bf16[128,1024]{1,0:T(8,128)(2,1)S(1)}, u32[]{:S(2)}, u32[]{:S(2)}) collective-permute-start(bf16[128,1024]{1,0:T(8,128)(2,1)S(1)} %get-tuple-element.35), channel_id=1, source_target_pairs={{0,2},{1,3},{2,0},{3,1},{4,6},{5,7},{6,4},{7,5},{8,10},{9,11},{10,... | collective-permute-start | bytes 786440 | tf_op jit(solution)/shard_map/ppermute | solution.py:31
  64.0 1.6 %collective-permute-start.6 = (bf16[256,512]{1,0:T(8,128)(2,1)S(1)}, bf16[256,512]{1,0:T(8,128)(2,1)S(1)}, u32[]{:S(2)}, u32[]{:S(2)}) collective-permute-start(bf16[256,512]{1,0:T(8,128)(2,1)S(1)} %get-tuple-element.38), channel_id=1, source_target_pairs={{0,4},{8,12},{16,20},{24,28},{4,0},{12,8},{20,16},{28,24},{1,5},{9... | collective-permute-start | bytes 786440 | tf_op jit(solution)/shard_map/ppermute | solution.py:37
  64.4 28.1 %collective-permute-start.15 = (bf16[128,1024]{1,0:T(8,128)(2,1)S(1)}, bf16[128,1024]{1,0:T(8,128)(2,1)S(1)}, u32[]{:S(2)}, u32[]{:S(2)}) collective-permute-start(bf16[128,1024]{1,0:T(8,128)(2,1)S(1)} %get-tuple-element.49), channel_id=1, source_target_pairs={{0,2},{1,3},{2,0},{3,1},{4,6},{5,7},{6,4},{7,5},{8,10},{9,11},{10,... | collective-permute-start | bytes 786440 | tf_op jit(solution)/shard_map/ppermute | solution.py:31
  64.8 21.7 %collective-permute-start.14 = (bf16[256,512]{1,0:T(8,128)(2,1)S(1)}, bf16[256,512]{1,0:T(8,128)(2,1)S(1)}, u32[]{:S(2)}, u32[]{:S(2)}) collective-permute-start(bf16[256,512]{1,0:T(8,128)(2,1)S(1)} %get-tuple-element.47), channel_id=1, source_target_pairs={{4,8},{12,16},{20,24},{8,4},{16,12},{24,20},{5,9},{13,17},{21,25},... | collective-permute-start | bytes 786440 | tf_op jit(solution)/shard_map/ppermute | solution.py:37
  80.6 11.9 %collective-permute-start.17 = (bf16[128,1024]{1,0:T(8,128)(2,1)S(1)}, bf16[128,1024]{1,0:T(8,128)(2,1)S(1)}, u32[]{:S(2)}, u32[]{:S(2)}) collective-permute-start(bf16[128,1024]{1,0:T(8,128)(2,1)S(1)} %collective-permute-done.5), channel_id=1, source_target_pairs={{0,16},{4,20},{8,24},{12,28},{16,0},{20,4},{24,8},{28,12},{1,17},{... | collective-permute-start | bytes 786440 | tf_op jit(solution)/shard_map/ppermute | solution.py:31
  81.1 11.4 %collective-permute-start.16 = (bf16[128,1024]{1,0:T(8,128)(2,1)S(1)}, bf16[128,1024]{1,0:T(8,128)(2,1)S(1)}, u32[]{:S(2)}, u32[]{:S(2)}) collective-permute-start(bf16[128,1024]{1,0:T(8,128)(2,1)S(1)} %collective-permute-done.5), channel_id=1, source_target_pairs={{0,8},{4,12},{8,0},{12,4},{16,24},{20,28},{24,16},{28,20},{1,9},{5... | collective-permute-start | bytes 786440 | tf_op jit(solution)/shard_map/ppermute | solution.py:31
  89.5 19.2 %collective-permute-start.19 = (bf16[544,256]{1,0:T(8,128)(2,1)S(1)}, bf16[544,256]{1,0:T(8,128)(2,1)S(1)}, u32[]{:S(2)}, u32[]{:S(2)}) collective-permute-start(bf16[544,256]{1,0:T(8,128)(2,1)S(1)} %attend_far.1), channel_id=1, source_target_pairs={{0,2},{1,3},{2,0},{3,1},{4,6},{5,7},{6,4},{7,5},{8,10},{9,11},{10,... | collective-permute-start | bytes 835592 | tf_op jit(solution)/shard_map/ppermute | solution.py:31
  95.6 23.3 %copy-start.6 = (bf16[256,1024]{1,0:T(8,128)(2,1)S(1)}, bf16[256,1024]{1,0:T(8,128)(2,1)}, u32[]{:S(2)}) copy-start(bf16[256,1024]{1,0:T(8,128)(2,1)} %own_ref.3) | copy-start | bytes 1572868
  95.7 13.0 %collective-permute-start.18 = (bf16[528,256]{1,0:T(8,128)(2,1)S(1)}, bf16[528,256]{1,0:T(8,128)(2,1)S(1)}, u32[]{:S(2)}, u32[]{:S(2)}) collective-permute-start(bf16[528,256]{1,0:T(8,128)(2,1)S(1)} %attend_near.1.refs_0_), channel_id=1, source_target_pairs={{0,1},{1,0},{2,3},{3,2},{4,5},{5,4},{6,7},{7,6},{8,9},{9,8},{10,11... | collective-permute-start | bytes 811016 | tf_op jit(solution)/shard_map/ppermute | solution.py:31
  97.6 11.5 %collective-permute-start.23 = (bf16[128,1024]{1,0:T(8,128)(2,1)S(1)}, bf16[128,1024]{1,0:T(8,128)(2,1)S(1)}, u32[]{:S(2)}, u32[]{:S(2)}) collective-permute-start(bf16[128,1024]{1,0:T(8,128)(2,1)S(1)} %collective-permute-done.15), channel_id=1, source_target_pairs={{0,8},{4,12},{8,0},{12,4},{16,24},{20,28},{24,16},{28,20},{1,9},{5... | collective-permute-start | bytes 786440 | tf_op jit(solution)/shard_map/ppermute | solution.py:31
  98.2 12.6 %collective-permute-start.24 = (bf16[128,1024]{1,0:T(8,128)(2,1)S(1)}, bf16[128,1024]{1,0:T(8,128)(2,1)S(1)}, u32[]{:S(2)}, u32[]{:S(2)}) collective-permute-start(bf16[128,1024]{1,0:T(8,128)(2,1)S(1)} %collective-permute-done.15), channel_id=1, source_target_pairs={{0,16},{4,20},{8,24},{12,28},{16,0},{20,4},{24,8},{28,12},{1,17},{... | collective-permute-start | bytes 786440 | tf_op jit(solution)/shard_map/ppermute | solution.py:31
  108.6 8.2 %collective-permute-start.21 = (bf16[128,1024]{1,0:T(8,128)(2,1)S(1)}, bf16[128,1024]{1,0:T(8,128)(2,1)S(1)}, u32[]{:S(2)}, u32[]{:S(2)}) collective-permute-start(bf16[128,1024]{1,0:T(8,128)(2,1)S(1)} %collective-permute-done.17), channel_id=1, source_target_pairs={{0,8},{4,12},{8,0},{12,4},{16,24},{20,28},{24,16},{28,20},{1,9},{5... | collective-permute-start | bytes 786440 | tf_op jit(solution)/shard_map/ppermute | solution.py:31
  109.2 8.0 %collective-permute-start.25 = (bf16[128,1024]{1,0:T(8,128)(2,1)S(1)}, bf16[128,1024]{1,0:T(8,128)(2,1)S(1)}, u32[]{:S(2)}, u32[]{:S(2)}) collective-permute-start(bf16[128,1024]{1,0:T(8,128)(2,1)S(1)} %collective-permute-done.23), channel_id=1, source_target_pairs={{0,16},{4,20},{8,24},{12,28},{16,0},{20,4},{24,8},{28,12},{1,17},{... | collective-permute-start | bytes 786440 | tf_op jit(solution)/shard_map/ppermute | solution.py:31
  110.8 8.1 %collective-permute-start.20 = (bf16[544,256]{1,0:T(8,128)(2,1)S(1)}, bf16[544,256]{1,0:T(8,128)(2,1)S(1)}, u32[]{:S(2)}, u32[]{:S(2)}) collective-permute-start(bf16[544,256]{1,0:T(8,128)(2,1)S(1)} %collective-permute-done.19.refs_2_), channel_id=1, source_target_pairs={{0,1},{1,0},{2,3},{3,2},{4,5},{5,4},{6,7},{7,6},{8,9},{9,8},{10,11... | collective-permute-start | bytes 835592 | tf_op jit(solution)/shard_map/ppermute | solution.py:31
  116.9 5.4 %collective-permute-start.22 = (bf16[512,1024]{1,0:T(8,128)(2,1)S(1)}, bf16[512,1024]{1,0:T(8,128)(2,1)S(1)}, u32[]{:S(2)}, u32[]{:S(2)}) collective-permute-start(bf16[512,1024]{1,0:T(8,128)(2,1)S(1)} %constant_dynamic-update-slice_fusion.refs_0_), channel_id=1, source_target_pairs={{0,4},{4,0},{8,12},{12,8},{16,20},{20,16},{24,28},{28,24},{1,5},{5... | collective-permute-start | bytes 3145736 | tf_op jit(solution)/shard_map/ppermute | solution.py:31
  118.9 3.4 %collective-permute-start.26 = (bf16[512,1024]{1,0:T(8,128)(2,1)S(1)}, bf16[512,1024]{1,0:T(8,128)(2,1)S(1)}, u32[]{:S(2)}, u32[]{:S(2)}) collective-permute-start(bf16[512,1024]{1,0:T(8,128)(2,1)S(1)} %constant_dynamic-update-slice_fusion.4.refs_2_), channel_id=1, source_target_pairs={{0,4},{4,0},{8,12},{12,8},{16,20},{20,16},{24,28},{28,24},{1,5},{5... | collective-permute-start | bytes 3145736 | tf_op jit(solution)/shard_map/ppermute | solution.py:31
  126.2 16.7 %collective-permute-start.27 = (bf16[256,1024]{1,0:T(8,128)(2,1)S(1)}, bf16[256,1024]{1,0:T(8,128)(2,1)S(1)}, u32[]{:S(2)}, u32[]{:S(2)}) collective-permute-start(bf16[256,1024]{1,0:T(8,128)(2,1)S(1)} %feed_partner.1), channel_id=1, source_target_pairs={{0,1},{1,0},{2,3},{3,2},{4,5},{5,4},{6,7},{7,6},{8,9},{9,8},{10,11... | collective-permute-start | bytes 1572872 | tf_op jit(solution)/shard_map/ppermute | solution.py:31
  126.6 15.7 %collective-permute-start.30 = (f32[3,2,1024]{2,1,0:T(2,128)S(1)}, f32[3,2,1024]{2,1,0:T(2,128)S(1)}, u32[]{:S(2)}, u32[]{:S(2)}) collective-permute-start(f32[3,2,1024]{2,1,0:T(2,128)S(1)} %get-tuple-element.64), channel_id=1, source_target_pairs={{0,3},{1,2},{2,1},{3,0},{4,7},{5,6},{6,5},{7,4},{8,11},{9,10},{10,... | collective-permute-start | bytes 73736 | tf_op jit(solution)/shard_map/ppermute | solution.py:31
  129.2 13.1 %collective-permute-start.29 = (f32[3,2,1024]{2,1,0:T(2,128)S(1)}, f32[3,2,1024]{2,1,0:T(2,128)S(1)}, u32[]{:S(2)}, u32[]{:S(2)}) collective-permute-start(f32[3,2,1024]{2,1,0:T(2,128)S(1)} %get-tuple-element.65), channel_id=1, source_target_pairs={{0,2},{1,3},{2,0},{3,1},{4,6},{5,7},{6,4},{7,5},{8,10},{9,11},{10,... | collective-permute-start | bytes 73736 | tf_op jit(solution)/shard_map/ppermute | solution.py:31
  129.9 12.4 %collective-permute-start.28 = (f32[3,2,1024]{2,1,0:T(2,128)S(1)}, f32[3,2,1024]{2,1,0:T(2,128)S(1)}, u32[]{:S(2)}, u32[]{:S(2)}) collective-permute-start(f32[3,2,1024]{2,1,0:T(2,128)S(1)} %get-tuple-element.66), channel_id=1, source_target_pairs={{0,1},{1,0},{2,3},{3,2},{4,5},{5,4},{6,7},{7,6},{8,9},{9,8},{10,11... | collective-permute-start | bytes 73736 | tf_op jit(solution)/shard_map/ppermute | solution.py:31
  (21 other events, 267.8 us)

commit v17 on v15

--- a/solution.py
+++ b/solution.py
@@ -141,8 +141,11 @@
     even_ref, odd_ref = refs[9:11] if has_halo else (None, None)
     out_ref, window_ref, bias_ref, scores_ref, weights_ref, sems = refs[-6:]
     tok, kv = place_ref[0], place_ref[1]
-    count = out_ref.shape[0]
+    count = bias_ref.shape[0]
     blocks = 4
+    if out_ref.shape[0] > count:
+        out_ref[count:] = jnp.zeros_like(out_ref[count:])
+        out_ref = out_ref.at[:count]
     inner = is_inner(kv)
     outer = jnp.logical_not(inner)
     block = kv ^ jnp.where(inner, flips[1], flips[0])
@@ -182,11 +185,11 @@
     attend(query, window_ref, bias_ref, scores_ref, weights_ref, out_ref)
 
 
-def attend_block(place, starts, ends, projected, flips, name, halo=()):
+def attend_block(place, starts, ends, projected, flips, name, halo=(), spare=0):
     rows, heads_width = projected[-2].shape
     return pl.pallas_call(
         functools.partial(attend_kernel, flips, bool(halo)),
-        out_shape=jax.ShapeDtypeStruct((rows, heads_width), BF16),
+        out_shape=jax.ShapeDtypeStruct((rows + spare, heads_width), BF16),
         in_specs=[SMEM, VMEM, VMEM] + [VMEM, ANY] * 3 + [ANY] * len(halo),
         out_specs=VMEM,
         scratch_shapes=[
@@ -222,7 +225,7 @@
         flip = index % 4
         half = early if index < 4 else 1 - early
         at = pl.ds(pl.multiple_of(half * count, count), count)
-        all_ref[at, flip * heads_width : (flip + 1) * heads_width] = part_ref[...]
+        all_ref[at, flip * heads_width : (flip + 1) * heads_width] = part_ref[:count]
     for copy in copies:
         copy.wait()
     weight = weight_ref[...].reshape(quarters * heads_width, width)
@@ -468,7 +471,7 @@
     )
     a3 = lax.ppermute(after(b2, first[0]), "kv", outward)
     second = project_call(project_second_kernel, "project_second", rows, *sizes, (place, weight, a2, b2))
-    out_far = swapped(out_y, "tok", 2)
+    out_far = swapped(out_here, "tok", 6)
     inner = (kv == 1) | (kv == 2)
 
     order = jnp.arange(stretch_len.shape[0])
@@ -476,26 +479,28 @@
     starts = (ends - stretch_len)[None, :]
     ends = ends[None, :]
 
-    feed_up, feed_down = after((eighth(up_weight), eighth(down_weight)), a2, b2)
-    inner_up = lax.ppermute(feed_up, "kv", [(0, 2), (3, 1)])
-    inner_down = lax.ppermute(feed_down, "kv", [(0, 2), (3, 1)])
-    feed_part = jnp.concatenate([feed_up, feed_down], axis=0)
-    feed_part = after(feed_part, a3, second[0], out_x, out_y, inner_up, inner_down)
+    feed_up, feed_down = eighth(up_weight), eighth(down_weight)
+    inner_up = lax.ppermute(after(feed_up, second[0]), "kv", [(0, 2), (3, 1)])
+    inner_down = lax.ppermute(after(feed_down, second[0]), "kv", [(0, 2), (3, 1)])
+    feed_part = after(jnp.concatenate([feed_up, feed_down], axis=0), a3, inner_up, inner_down)
     feed_outer = lax.ppermute(feed_part, "kv", [(1, 3), (2, 0)])
     feed_inner = jnp.concatenate([inner_up, inner_down], axis=0)
 
     *last, even, odd = project_call(
-        project_last_kernel, "project_last", rows, *sizes, (place, weight, first[1], second[1], a3), 2
+        project_last_kernel, "project_last", rows, *sizes, (place, weight, first[1], second[1], after(a3, out_x, out_y, out_far)), 2
     )
     halo = over_edges(even, "tok", 0), over_edges(odd, "tok", 1)
     projected = (*first, *second, *last)
-    two = attend_block(place, starts, ends, projected, (2, 3), "attend_two")
+    two = attend_block(after(place, halo[0]), starts, ends, projected, (2, 3), "attend_two")
     two_there = swapped(two, "kv", 2)
     out_all = jnp.stack([out_here, out_x, out_y, out_far])
     out_core = swapped(out_all, "tok", 1)
-    feed_here = jnp.where(inner, feed_inner, after(feed_outer, two))
+    queries = jnp.concatenate([dec_query] + [other[depth:] for other in others], axis=0)
+    queries = after(queries, two, *halo).astype(F32)
+    partial = decode_partial(queries, dec_query.shape[0], kv_cache, piece_req, piece_used)
+    feed_here = jnp.where(inner, feed_inner, after(feed_outer, partial))
     feed_x, feed_y = swapped(feed_here, "tok", 2), swapped(feed_here, "tok", 4)
-    far = attend_block(after(place, feed_here, out_core), starts, ends, projected, (3, 2), "attend_far", halo)
+    far = attend_block(after(place, feed_here, out_core, partial), starts, ends, projected, (3, 2), "attend_far", halo, 32)
     far_there = swapped(far, "kv", 2)
     two_passed = swapped(after(two_there, far), "kv", 1)
     one = attend_block(after(place, far, two_there), starts, ends, projected, (1, 0), "attend_one")
@@ -504,14 +509,11 @@
     near_there, far_passed = swapped(near, "kv", 1), swapped(far_there, "kv", 1)
     parts = (one, one_there, two_there, two_passed, near, near_there, far_there, far_passed)
     out_pieces = [((0, 2, 4, 6), out_all), ((1, 3, 5, 7), out_core)]
-    queries = jnp.concatenate([dec_query] + [other[depth:] for other in others], axis=0)
-    queries = after(queries, near, two_passed).astype(F32)
-    partial = decode_partial(queries, dec_query.shape[0], kv_cache, piece_req, piece_used)
     half = feed_here.shape[0] // 2
-    far_up = swapped(after(feed_y, far_there, near_there, partial)[:half], "tok", 2)
-    far_down = swapped(after(feed_x, far_there, near_there, partial)[half:], "tok", 4)
+    far_up = swapped(after(feed_y, far_there, near_there, two_passed)[:half], "tok", 2)
+    far_down = swapped(after(feed_x, far_there, near_there, two_passed)[half:], "tok", 4)
     held = jnp.concatenate([feed_here, feed_x, feed_y, far_up, far_down], axis=0)
-    feed_pieces = (held, swapped(after(held, far_passed, one_there), "tok", 1))
+    feed_pieces = (held, swapped(after(held, far_passed, two_passed, one_there, near_there), "tok", 1))
 
     gain, bias = ln1_gain[None, :], ln1_bias[None, :]
     normed, partner = first_norm(place, hidden_in, a1, out_weight, gain, bias, parts, out_pieces)

time: 137 us -> 144 us (1.051)
  waiting for transfers between devices: 32.3 us -> 41.7 us
  starting transfers between devices: 53.8 us -> 50.6 us
    ppermute x1, waiting for transfers between devices: 0.01 us -> 9.43 us  [routed_body(): a2, b2 = (lax.ppermute(b1, 'kv', outward), over_edges(a1, 'kv', 1))]
    ppermute x2, starting transfers between devices: 11.6 us -> 6.96 us  [the longest x1 5.66 us: routed_body(): inner_up = lax.ppermute(after(feed_up, second[0]), 'kv', [(0, 2), (3, 1)])]
    ppermute x1, waiting for transfers between devices: 4.53 us -> 0.01 us  [routed_body(): feed_outer = lax.ppermute(feed_part, 'kv', [(1, 3), (2, 0)])]
    ppermute x22, waiting for transfers between devices: 22.8 us -> 26.8 us  [swapped(): return lax.ppermute(value, axis, [(i, i ^ flip) for i in range(count)])]
    ppermute x2, waiting for transfers between devices: 0.11 us -> 3.04 us  [the longest x1 2.26 us: routed_body(): inner_up = lax.ppermute(after(feed_up, second[0]), 'kv', [(0, 2), (3, 1)])]
    ppermute x5, waiting for transfers between devices: 4.9 us -> 2.42 us  [over_edges(): return lax.ppermute(value, axis, edges + [(j, i) for i, j in edges])]
    ppermute x22, starting transfers between devices: 31.1 us -> 33.4 us  [swapped(): return lax.ppermute(value, axis, [(i, i ^ flip) for i in range(count)])]
    slice x6 -> x3, local copies, waits for them, and re-layouts: 0.01 us -> 2.17 us  [routed_body(): other[depth:]]
  transfers between devices with their start and end apart: 32 -> 32, of which waited for: 12 -> 14; matrix products, arithmetic and copies ran while one was open for 8% -> 8% of each run, Pallas kernels for 22% -> 21%
where the time goes in v17:
time: 144 us; the launch traced here: 143 us
  starting transfers between devices  50.6 us (35%)
  waiting for transfers between devices  41.7 us (29%)
  Pallas kernels  35.1 us (24%)
  local copies, waits for them, and re-layouts  7.75 us (5%)
  other arithmetic  6.68 us (5%)
    ppermute x22, starting transfers between devices, swapped(): return lax.ppermute(value, axis, [(i, i ^ flip) for i in range(count)])  33.4 us
    ppermute x22, waiting for transfers between devices, swapped(): return lax.ppermute(value, axis, [(i, i ^ flip) for i in range(count)])  26.8 us
    pallas_call x4, Pallas kernels, attend_block(): pl.pallas_call(functools.partial(attend_kernel, flips, bool(halo)), out_s...  11.8 us
    ppermute x1, waiting for transfers between devices, routed_body(): a2, b2 = (lax.ppermute(b1, 'kv', outward), over_edges(a1, 'kv', 1))  9.43 us
    pallas_call x2, Pallas kernels, feed(): pl.pallas_call(feed_kernel, out_shape=jax.ShapeDtypeStruct((count, width)...  7.81 us
    ppermute x5, starting transfers between devices, over_edges(): return lax.ppermute(value, axis, edges + [(j, i) for i, j in edges])  6.39 us
    ppermute x1, starting transfers between devices, routed_body(): inner_up = lax.ppermute(after(feed_up, second[0]), 'kv', [(0, 2), (3, 1)])  5.66 us
    pallas_call x3, Pallas kernels, project_call(): pl.pallas_call(kernel, out_shape=(jax.ShapeDtypeStruct((rows, heads_width...  5.65 us
  transfers between devices with their start and end apart: 32, of which 14 were waited for; matrix products, arithmetic and copies ran while one was open for 8% of the time, Pallas kernels for 21%

profile of v17, /device:TPU:0, one launch (start us, length us, event | category | flops | bytes accessed | tf_op | source)
XLA Modules:
  0.0 143.0 jit_solution(14014097935773250071)
XLA Ops:
  0.7 3.1 %collective-permute-start = (bf16[256,1024]{1,0:T(8,128)(2,1)}, bf16[256,1024]{1,0:T(8,128)(2,1)}, u32[]{:S(2)}, u32[]{:S(2)}) collective-permute-start(bf16[256,1024]{1,0:T(8,128)(2,1)} %own_ref.3), channel_id=1, source_target_pairs={{0,1},{2,3},{1,0},{3,2},{4,5},{6,7},{5,4},{7,6},{8,9},{10,11},{9,8... | collective-permute-start | bytes 1572872 | tf_op jit(solution)/shard_map/ppermute | solution.py:37
  7.4 2.6 %collective-permute-start.10 = (bf16[34,1024]{1,0:T(8,128)(2,1)}, bf16[34,1024]{1,0:T(8,128)(2,1)S(1)}, u32[]{:S(2)}, u32[]{:S(2)}) collective-permute-start(bf16[34,1024]{1,0:T(8,128)(2,1)} %pad_maximum_fusion.3), channel_id=1, source_target_pairs={{0,3},{1,2},{2,1},{3,0},{4,7},{5,6},{6,5},{7,4},{8,11},{9,10},{10,... | collective-permute-start | bytes 208904 | tf_op jit(solution)/shard_map/ppermute | solution.py:31
  10.0 2.5 %collective-permute-start.9 = (bf16[34,1024]{1,0:T(8,128)(2,1)}, bf16[34,1024]{1,0:T(8,128)(2,1)S(1)}, u32[]{:S(2)}, u32[]{:S(2)}) collective-permute-start(bf16[34,1024]{1,0:T(8,128)(2,1)} %pad_maximum_fusion.3), channel_id=1, source_target_pairs={{0,2},{1,3},{2,0},{3,1},{4,6},{5,7},{6,4},{7,5},{8,10},{9,11},{10,... | collective-permute-start | bytes 208904 | tf_op jit(solution)/shard_map/ppermute | solution.py:31
  14.4 2.4 %collective-permute-done.a1_ref.partner_ref = bf16[256,1024]{1,0:T(8,128)(2,1)} collective-permute-done((bf16[256,1024]{1,0:T(8,128)(2,1)}, bf16[256,1024]{1,0:T(8,128)(2,1)}, u32[]{:S(2)}, u32[]{:S(2)}) %collective-permute-start) | collective-permute-done | bytes 524320 | tf_op jit(solution)/shard_map/ppermute | solution.py:37
  21.7 2.6 %project_first.1 = (bf16[768,256]{1,0:T(8,128)(2,1)S(1)}, bf16[768,512]{1,0:T(8,128)(2,1)S(1)}) custom-call(bf16[3,1024,256]{2,1,0:T(8,128)(2,1)S(1)} %bitcast.142, bf16[256,1024]{1,0:T(8,128)(2,1)S(1)} %copy-done.4, bf16[256,1024]{1,0:T(8,128)(2,1)} %collective-permute-done.a1_ref.partner_ref, bf16[256,1024]{1,0:T(8,128)(2,1)} %collective-permute-done.1.b1_ref), custom_call_target="tpu_custom_call" | custom-call | flops 1 | bytes 1 | tf_op jit(solution)/shard_map/project_first/pallas_call | solution.py:91
  25.6 2.7 %collective-permute-done.9 = bf16[34,1024]{1,0:T(8,128)(2,1)S(1)} collective-permute-done((bf16[34,1024]{1,0:T(8,128)(2,1)}, bf16[34,1024]{1,0:T(8,128)(2,1)S(1)}, u32[]{:S(2)}, u32[]{:S(2)}) %collective-permute-start.9) | collective-permute-done | bytes 69664 | tf_op jit(solution)/shard_map/ppermute | solution.py:31
  28.3 9.4 %collective-permute-done.2.a2_ref = bf16[256,1024]{1,0:T(8,128)(2,1)S(1)} collective-permute-done((bf16[256,1024]{1,0:T(8,128)(2,1)}, bf16[256,1024]{1,0:T(8,128)(2,1)S(1)}, u32[]{:S(2)}, u32[]{:S(2)}) %collective-permute-start.2) | collective-permute-done | bytes 524320 | tf_op jit(solution)/shard_map/ppermute | solution.py:464
  38.8 5.7 %collective-permute-start.4 = (bf16[128,1024]{1,0:T(8,128)(2,1)S(1)}, bf16[128,1024]{1,0:T(8,128)(2,1)S(1)}, u32[]{:S(2)}, u32[]{:S(2)}) collective-permute-start(bf16[128,1024]{1,0:T(8,128)(2,1)S(1)} %constant_dynamic-slice_fusion.2), channel_id=1, source_target_pairs={{0,2},{3,1},{4,6},{7,5},{8,10},{11,9},{12,14},{15,13},{16,18},{19,... | collective-permute-start | bytes 786440 | tf_op jit(solution)/shard_map/ppermute | solution.py:483
  49.0 2.3 %collective-permute-done.4 = bf16[128,1024]{1,0:T(8,128)(2,1)S(1)} collective-permute-done((bf16[128,1024]{1,0:T(8,128)(2,1)S(1)}, bf16[128,1024]{1,0:T(8,128)(2,1)S(1)}, u32[]{:S(2)}, u32[]{:S(2)}) %collective-permute-start.4) | collective-permute-done | bytes 262176 | tf_op jit(solution)/shard_map/ppermute | solution.py:483
  51.2 2.5 %collective-permute-start.13 = (bf16[3,32,1024]{2,1,0:T(8,128)(2,1)S(1)}, bf16[3,32,1024]{2,1,0:T(8,128)(2,1)S(1)}, u32[]{:S(2)}, u32[]{:S(2)}) collective-permute-start(bf16[3,32,1024]{2,1,0:T(8,128)(2,1)S(1)} %pad_maximum_fusion.2), channel_id=1, source_target_pairs={{0,24},{4,28},{8,16},{12,20},{16,8},{20,12},{24,0},{28,4},{1,25},{... | collective-permute-start | bytes 589832 | tf_op jit(solution)/shard_map/ppermute | solution.py:31
  55.8 2.0 %collective-permute-done.13 = bf16[3,32,1024]{2,1,0:T(8,128)(2,1)S(1)} collective-permute-done((bf16[3,32,1024]{2,1,0:T(8,128)(2,1)S(1)}, bf16[3,32,1024]{2,1,0:T(8,128)(2,1)S(1)}, u32[]{:S(2)}, u32[]{:S(2)}) %collective-permute-start.13) | collective-permute-done | bytes 196640 | tf_op jit(solution)/shard_map/ppermute | solution.py:31
  58.8 1.9 %project_last.1 = (bf16[256,256]{1,0:T(8,128)(2,1)S(1)}, bf16[256,512]{1,0:T(8,128)(2,1)S(1)}, bf16[256,512]{1,0:T(8,128)(2,1)}, bf16[256,512]{1,0:T(8,128)(2,1)}) custom-call(s32[2]{0:T(128)S(1)} %pad_add_fusion.place_ref.refs_0_, bf16[3,1024,256]{2,1,0:T(8,128)(2,1)S(1)} %bitcast.144, bf16[768,512]{1,0:T(8,128)(2,1)S(1)} %get-tuple-element.40.first_ref.refs_4_, ...), custom_call_target="tpu_custom_call" | custom-call | flops 1 | bytes 1 | tf_op jit(solution)/shard_map/project_last/pallas_call | solution.py:91
  64.9 2.9 %attend_two.1 = bf16[256,256]{1,0:T(8,128)(2,1)S(1)} custom-call(s32[2]{0:T(128)S(1)} %pad_add_fusion.place_ref.refs_0_, s32[1,48]{1,0:T(1,128)S(1)} %subtract_bitcast_fusion.refs_1_, s32[1,48]{1,0:T(1,128)S(1)} %bitcast.145, bf16[768,256]{1,0:T(8,128)(2,1)S(1)} %get-tuple-element.37.refs_3_, bf16[768,512]{1,0:T(8,128)(2,1)S(1)} %get-tuple-element.40.first_ref.refs_4_, ...), custom_call_target="tpu_custom_call" | custom-call | flops 1 | bytes 1 | tf_op jit(solution)/shard_map/attend_two/pallas_call | solution.py:190
  69.7 3.8 %decode.1 = f32[3,8,1024]{2,1,0:T(8,128)S(1)} custom-call(s32[6]{0:T(128)S(1)} %fusion.12.slot_ref, s32[6]{0:T(128)S(1)} %bitcast.153, f32[8,1024]{1,0:T(8,128)S(1)} %convert_element_type.6.query_ref, bf16[2,1,6,128,1024]{4,3,2,1,0:T(8,128)(2,1)S(1)} %copy-done.3), custom_call_target="tpu_custom_call" | custom-call | flops 1 | bytes 1 | tf_op jit(solution)/shard_map/decode/pallas_call | solution.py:395
  74.8 5.9 %collective-permute-start.24 = (bf16[256,1024]{1,0:T(8,128)(2,1)S(1)}, bf16[256,1024]{1,0:T(8,128)(2,1)S(1)}, u32[]{:S(2)}, u32[]{:S(2)}) collective-permute-start(bf16[256,1024]{1,0:T(8,128)(2,1)S(1)} %get-tuple-element.67), channel_id=1, source_target_pairs={{0,16},{4,20},{8,24},{12,28},{16,0},{20,4},{24,8},{28,12},{1,17},{... | collective-permute-start | bytes 1572872 | tf_op jit(solution)/shard_map/ppermute | solution.py:31
  81.9 2.3 %collective-permute-start.17 = (bf16[256,256]{1,0:T(8,128)(2,1)S(1)}, bf16[256,256]{1,0:T(8,128)(2,1)S(1)}, u32[]{:S(2)}, u32[]{:S(2)}) collective-permute-start(bf16[256,256]{1,0:T(8,128)(2,1)S(1)} %attend_two.1), channel_id=1, source_target_pairs={{0,2},{1,3},{2,0},{3,1},{4,6},{5,7},{6,4},{7,5},{8,10},{9,11},{10,... | collective-permute-start | bytes 393224 | tf_op jit(solution)/shard_map/ppermute | solution.py:31
  84.2 2.9 %attend_far.1 = bf16[288,256]{1,0:T(8,128)(2,1)S(1)} custom-call(s32[2]{0:T(128)S(1)} %pad_add_fusion.place_ref.refs_0_, s32[1,48]{1,0:T(1,128)S(1)} %subtract_bitcast_fusion.refs_1_, s32[1,48]{1,0:T(1,128)S(1)} %bitcast.146, bf16[768,256]{1,0:T(8,128)(2,1)S(1)} %get-tuple-element.37.refs_3_, bf16[768,512]{1,0:T(8,128)(2,1)S(1)} %get-tuple-element.40.first_ref.refs_4_, ...), custom_call_target="tpu_custom_call" | custom-call | flops 1 | bytes 1 | tf_op jit(solution)/shard_map/attend_far/pallas_call | solution.py:190
  87.8 6.3 %collective-permute-done.17.refs_2_ = bf16[256,256]{1,0:T(8,128)(2,1)S(1)} collective-permute-done((bf16[256,256]{1,0:T(8,128)(2,1)S(1)}, bf16[256,256]{1,0:T(8,128)(2,1)S(1)}, u32[]{:S(2)}, u32[]{:S(2)}) %collective-permute-start.17) | collective-permute-done | bytes 131104 | tf_op jit(solution)/shard_map/ppermute | solution.py:31
  94.1 2.9 %attend_one.1.refs_0_ = bf16[256,256]{1,0:T(8,128)(2,1)S(1)} custom-call(s32[2]{0:T(128)S(1)} %pad_add_fusion.place_ref.refs_0_, s32[1,48]{1,0:T(1,128)S(1)} %subtract_bitcast_fusion.refs_1_, s32[1,48]{1,0:T(1,128)S(1)} %bitcast.147, bf16[768,256]{1,0:T(8,128)(2,1)S(1)} %get-tuple-element.37.refs_3_, ...), custom_call_target="tpu_custom_call" | custom-call | flops 1 | bytes 1 | tf_op jit(solution)/shard_map/attend_one/pallas_call | solution.py:190
  97.1 3.1 %attend_near.1.refs_4_ = bf16[256,256]{1,0:T(8,128)(2,1)S(1)} custom-call(s32[2]{0:T(128)S(1)} %pad_add_fusion.place_ref.refs_0_, s32[1,48]{1,0:T(1,128)S(1)} %subtract_bitcast_fusion.refs_1_, s32[1,48]{1,0:T(1,128)S(1)} %bitcast.148, bf16[768,256]{1,0:T(8,128)(2,1)S(1)} %get-tuple-element.37.refs_3_, ...), custom_call_target="tpu_custom_call" | custom-call | flops 1 | bytes 1 | tf_op jit(solution)/shard_map/attend_near/pallas_call | solution.py:190
  100.3 2.1 %collective-permute-start.20 = (bf16[256,256]{1,0:T(8,128)(2,1)S(1)}, bf16[256,256]{1,0:T(8,128)(2,1)S(1)}, u32[]{:S(2)}, u32[]{:S(2)}) collective-permute-start(bf16[256,256]{1,0:T(8,128)(2,1)S(1)} %attend_near.1.refs_4_), channel_id=1, source_target_pairs={{0,1},{1,0},{2,3},{3,2},{4,5},{5,4},{6,7},{7,6},{8,9},{9,8},{10,11... | collective-permute-start | bytes 393224 | tf_op jit(solution)/shard_map/ppermute | solution.py:31
  102.6 2.7 %collective-permute-done.20.refs_5_ = bf16[256,256]{1,0:T(8,128)(2,1)S(1)} collective-permute-done((bf16[256,256]{1,0:T(8,128)(2,1)S(1)}, bf16[256,256]{1,0:T(8,128)(2,1)S(1)}, u32[]{:S(2)}, u32[]{:S(2)}) %collective-permute-start.20) | collective-permute-done | bytes 131104 | tf_op jit(solution)/shard_map/ppermute | solution.py:31
  105.9 2.0 %collective-permute-start.18 = (bf16[256,256]{1,0:T(8,128)(2,1)S(1)}, bf16[256,256]{1,0:T(8,128)(2,1)S(1)}, u32[]{:S(2)}, u32[]{:S(2)}) collective-permute-start(bf16[256,256]{1,0:T(8,128)(2,1)S(1)} %attend_one.1.refs_0_), channel_id=1, source_target_pairs={{0,1},{1,0},{2,3},{3,2},{4,5},{5,4},{6,7},{7,6},{8,9},{9,8},{10,11... | collective-permute-start | bytes 393224 | tf_op jit(solution)/shard_map/ppermute | solution.py:31
  109.5 2.3 %collective-permute-done.25 = bf16[128,1024]{1,0:T(8,128)(2,1)S(1)} collective-permute-done((bf16[128,1024]{1,0:T(8,128)(2,1)S(1)}, bf16[128,1024]{1,0:T(8,128)(2,1)S(1)}, u32[]{:S(2)}, u32[]{:S(2)}) %collective-permute-start.25) | collective-permute-done | bytes 262176 | tf_op jit(solution)/shard_map/ppermute | solution.py:31
  111.8 2.6 %collective-permute-done.26 = bf16[128,1024]{1,0:T(8,128)(2,1)S(1)} collective-permute-done((bf16[128,1024]{1,0:T(8,128)(2,1)S(1)}, bf16[128,1024]{1,0:T(8,128)(2,1)S(1)}, u32[]{:S(2)}, u32[]{:S(2)}) %collective-permute-start.26) | collective-permute-done | bytes 262176 | tf_op jit(solution)/shard_map/ppermute | solution.py:31
  114.6 4.7 %first_norm.1 = (bf16[256,1024]{1,0:T(8,128)(2,1)S(1)}, bf16[256,1024]{1,0:T(8,128)(2,1)S(1)}) custom-call(s32[2]{0:T(128)S(1)} %pad_add_fusion.place_ref.refs_0_, bf16[256,1024]{1,0:T(8,128)(2,1)S(1)} %copy-done.5, bf16[256,1024]{1,0:T(8,128)(2,1)} %collective-permute-done.a1_ref.partner_ref, bf16[256,1024]{1,0:T(8,128)(2,1)S(1)} %copy-done.6, ...), custom_call_target="tpu_custom_call" | custom-call | flops 1 | bytes 1 | tf_op jit(solution)/shard_map/first_norm/pallas_call | solution.py:244
  119.4 3.9 %feed_partner.1 = bf16[256,1024]{1,0:T(8,128)(2,1)S(1)} custom-call(s32[2]{0:T(128)S(1)} %pad_add_fusion.place_ref.refs_0_, bf16[256,1024]{1,0:T(8,128)(2,1)S(1)} %get-tuple-element.56.rows_ref, bf16[1024,1024]{1,0:T(8,128)(2,1)S(1)} %copy-done.1, bf16[1024,1024]{1,0:T(8,128)(2,1)S(1)} %copy-done.2, ...), custom_call_target="tpu_custom_call" | custom-call | flops 1 | bytes 1 | tf_op jit(solution)/shard_map/feed_partner/pallas_call | solution.py:313
  123.3 2.1 %collective-permute-start.28 = (bf16[256,1024]{1,0:T(8,128)(2,1)S(1)}, bf16[256,1024]{1,0:T(8,128)(2,1)S(1)}, u32[]{:S(2)}, u32[]{:S(2)}) collective-permute-start(bf16[256,1024]{1,0:T(8,128)(2,1)S(1)} %feed_partner.1), channel_id=1, source_target_pairs={{0,1},{1,0},{2,3},{3,2},{4,5},{5,4},{6,7},{7,6},{8,9},{9,8},{10,11... | collective-permute-start | bytes 1572872 | tf_op jit(solution)/shard_map/ppermute | solution.py:31
  125.5 2.4 %collective-permute-start.30 = (f32[3,2,1024]{2,1,0:T(2,128)S(1)}, f32[3,2,1024]{2,1,0:T(2,128)S(1)}, u32[]{:S(2)}, u32[]{:S(2)}) collective-permute-start(f32[3,2,1024]{2,1,0:T(2,128)S(1)} %get-tuple-element.69), channel_id=1, source_target_pairs={{0,2},{1,3},{2,0},{3,1},{4,6},{5,7},{6,4},{7,5},{8,10},{9,11},{10,... | collective-permute-start | bytes 73736 | tf_op jit(solution)/shard_map/ppermute | solution.py:31
  129.8 3.9 %feed_own.1.near_ref = f32[256,1024]{1,0:T(8,128)S(1)} custom-call(s32[2]{0:T(128)S(1)} %pad_add_fusion.place_ref.refs_0_, bf16[256,1024]{1,0:T(8,128)(2,1)S(1)} %get-tuple-element.60.rows_ref.normed_ref, bf16[1024,1024]{1,0:T(8,128)(2,1)S(1)} %copy-done.1, bf16[1024,1024]{1,0:T(8,128)(2,1)S(1)} %copy-done.2, ...), custom_call_target="tpu_custom_call" | custom-call | flops 1 | bytes 1 | tf_op jit(solution)/shard_map/feed_own/pallas_call | solution.py:313
  133.7 5.2 %collective-permute-done.29 = f32[3,2,1024]{2,1,0:T(2,128)S(1)} collective-permute-done((f32[3,2,1024]{2,1,0:T(2,128)S(1)}, f32[3,2,1024]{2,1,0:T(2,128)S(1)}, u32[]{:S(2)}, u32[]{:S(2)}) %collective-permute-start.29) | collective-permute-done | bytes 24608 | tf_op jit(solution)/shard_map/ppermute | solution.py:31
  138.9 2.1 %collective-permute-done.31 = f32[3,2,1024]{2,1,0:T(2,128)S(1)} collective-permute-done((f32[3,2,1024]{2,1,0:T(2,128)S(1)}, f32[3,2,1024]{2,1,0:T(2,128)S(1)}, u32[]{:S(2)}, u32[]{:S(2)}) %collective-permute-start.31) | collective-permute-done | bytes 24608 | tf_op jit(solution)/shard_map/ppermute | solution.py:31
  (114 shorter events, 36.1 us)
Async XLA Ops:
  0.7 16.2 %collective-permute-start = (bf16[256,1024]{1,0:T(8,128)(2,1)}, bf16[256,1024]{1,0:T(8,128)(2,1)}, u32[]{:S(2)}, u32[]{:S(2)}) collective-permute-start(bf16[256,1024]{1,0:T(8,128)(2,1)} %own_ref.3), channel_id=1, source_target_pairs={{0,1},{2,3},{1,0},{3,2},{4,5},{6,7},{5,4},{7,6},{8,9},{10,11},{9,8... | collective-permute-start | bytes 1572872 | tf_op jit(solution)/shard_map/ppermute | solution.py:37
  3.7 15.3 %collective-permute-start.1 = (bf16[256,1024]{1,0:T(8,128)(2,1)}, bf16[256,1024]{1,0:T(8,128)(2,1)}, u32[]{:S(2)}, u32[]{:S(2)}) collective-permute-start(bf16[256,1024]{1,0:T(8,128)(2,1)} %own_ref.3), channel_id=1, source_target_pairs={{1,2},{2,1},{5,6},{6,5},{9,10},{10,9},{13,14},{14,13},{17,18},{18,... | collective-permute-start | bytes 1572872 | tf_op jit(solution)/shard_map/ppermute | solution.py:37
  7.4 13.6 %collective-permute-start.10 = (bf16[34,1024]{1,0:T(8,128)(2,1)}, bf16[34,1024]{1,0:T(8,128)(2,1)S(1)}, u32[]{:S(2)}, u32[]{:S(2)}) collective-permute-start(bf16[34,1024]{1,0:T(8,128)(2,1)} %pad_maximum_fusion.3), channel_id=1, source_target_pairs={{0,3},{1,2},{2,1},{3,0},{4,7},{5,6},{6,5},{7,4},{8,11},{9,10},{10,... | collective-permute-start | bytes 208904 | tf_op jit(solution)/shard_map/ppermute | solution.py:31
  10.0 18.3 %collective-permute-start.9 = (bf16[34,1024]{1,0:T(8,128)(2,1)}, bf16[34,1024]{1,0:T(8,128)(2,1)S(1)}, u32[]{:S(2)}, u32[]{:S(2)}) collective-permute-start(bf16[34,1024]{1,0:T(8,128)(2,1)} %pad_maximum_fusion.3), channel_id=1, source_target_pairs={{0,2},{1,3},{2,0},{3,1},{4,6},{5,7},{6,4},{7,5},{8,10},{9,11},{10,... | collective-permute-start | bytes 208904 | tf_op jit(solution)/shard_map/ppermute | solution.py:31
  12.4 33.4 %collective-permute-start.8 = (bf16[34,1024]{1,0:T(8,128)(2,1)}, bf16[34,1024]{1,0:T(8,128)(2,1)S(1)}, u32[]{:S(2)}, u32[]{:S(2)}) collective-permute-start(bf16[34,1024]{1,0:T(8,128)(2,1)} %pad_maximum_fusion.3), channel_id=1, source_target_pairs={{0,1},{1,0},{2,3},{3,2},{4,5},{5,4},{6,7},{7,6},{8,9},{9,8},{10,11... | collective-permute-start | bytes 208904 | tf_op jit(solution)/shard_map/ppermute | solution.py:31
  16.8 7.5 %collective-permute-start.3 = (bf16[256,1024]{1,0:T(8,128)(2,1)}, bf16[256,1024]{1,0:T(8,128)(2,1)S(1)}, u32[]{:S(2)}, u32[]{:S(2)}) collective-permute-start(bf16[256,1024]{1,0:T(8,128)(2,1)} %collective-permute-done.a1_ref.partner_ref), channel_id=1, source_target_pairs={{1,2},{2,1},{5,6},{6,5},{9,10},{10,9},{13,14},{14,13},{17,18},{18,... | collective-permute-start | bytes 1572872 | tf_op jit(solution)/shard_map/ppermute | solution.py:37
  19.1 18.6 %collective-permute-start.2 = (bf16[256,1024]{1,0:T(8,128)(2,1)}, bf16[256,1024]{1,0:T(8,128)(2,1)S(1)}, u32[]{:S(2)}, u32[]{:S(2)}) collective-permute-start(bf16[256,1024]{1,0:T(8,128)(2,1)} %collective-permute-done.1.b1_ref), channel_id=1, source_target_pairs={{1,0},{2,3},{5,4},{6,7},{9,8},{10,11},{13,12},{14,15},{17,16},{18,... | collective-permute-start | bytes 1572872 | tf_op jit(solution)/shard_map/ppermute | solution.py:464
  24.3 30.2 %collective-permute-start.6 = (bf16[256,1024]{1,0:T(8,128)(2,1)S(1)}, bf16[256,1024]{1,0:T(8,128)(2,1)S(1)}, u32[]{:S(2)}, u32[]{:S(2)}) collective-permute-start(bf16[256,1024]{1,0:T(8,128)(2,1)S(1)} %collective-permute-done.3.b2_ref), channel_id=1, source_target_pairs={{1,0},{2,3},{5,4},{6,7},{9,8},{10,11},{13,12},{14,15},{17,16},{18,... | collective-permute-start | bytes 1572872 | tf_op jit(solution)/shard_map/ppermute | solution.py:472
  38.8 12.4 %collective-permute-start.4 = (bf16[128,1024]{1,0:T(8,128)(2,1)S(1)}, bf16[128,1024]{1,0:T(8,128)(2,1)S(1)}, u32[]{:S(2)}, u32[]{:S(2)}) collective-permute-start(bf16[128,1024]{1,0:T(8,128)(2,1)S(1)} %constant_dynamic-slice_fusion.2), channel_id=1, source_target_pairs={{0,2},{3,1},{4,6},{7,5},{8,10},{11,9},{12,14},{15,13},{16,18},{19,... | collective-permute-start | bytes 786440 | tf_op jit(solution)/shard_map/ppermute | solution.py:483
  44.5 10.0 %collective-permute-start.5 = (bf16[128,1024]{1,0:T(8,128)(2,1)S(1)}, bf16[128,1024]{1,0:T(8,128)(2,1)S(1)}, u32[]{:S(2)}, u32[]{:S(2)}) collective-permute-start(bf16[128,1024]{1,0:T(8,128)(2,1)S(1)} %constant_dynamic-slice_fusion.1), channel_id=1, source_target_pairs={{0,2},{3,1},{4,6},{7,5},{8,10},{11,9},{12,14},{15,13},{16,18},{19,... | collective-permute-start | bytes 786440 | tf_op jit(solution)/shard_map/ppermute | solution.py:484
  45.9 9.9 %collective-permute-start.11 = (bf16[3,32,1024]{2,1,0:T(8,128)(2,1)S(1)}, bf16[3,32,1024]{2,1,0:T(8,128)(2,1)S(1)}, u32[]{:S(2)}, u32[]{:S(2)}) collective-permute-start(bf16[3,32,1024]{2,1,0:T(8,128)(2,1)S(1)} %pad_maximum_fusion.2), channel_id=1, source_target_pairs={{0,8},{4,12},{8,0},{12,4},{16,24},{20,28},{24,16},{28,20},{1,9},{5... | collective-permute-start | bytes 589832 | tf_op jit(solution)/shard_map/ppermute | solution.py:31
  47.4 8.4 %collective-permute-start.12 = (bf16[3,32,1024]{2,1,0:T(8,128)(2,1)S(1)}, bf16[3,32,1024]{2,1,0:T(8,128)(2,1)S(1)}, u32[]{:S(2)}, u32[]{:S(2)}) collective-permute-start(bf16[3,32,1024]{2,1,0:T(8,128)(2,1)S(1)} %pad_maximum_fusion.2), channel_id=1, source_target_pairs={{0,16},{4,20},{8,24},{12,28},{16,0},{20,4},{24,8},{28,12},{1,17},{... | collective-permute-start | bytes 589832 | tf_op jit(solution)/shard_map/ppermute | solution.py:31
  51.2 6.6 %collective-permute-start.13 = (bf16[3,32,1024]{2,1,0:T(8,128)(2,1)S(1)}, bf16[3,32,1024]{2,1,0:T(8,128)(2,1)S(1)}, u32[]{:S(2)}, u32[]{:S(2)}) collective-permute-start(bf16[3,32,1024]{2,1,0:T(8,128)(2,1)S(1)} %pad_maximum_fusion.2), channel_id=1, source_target_pairs={{0,24},{4,28},{8,16},{12,20},{16,8},{20,12},{24,0},{28,4},{1,25},{... | collective-permute-start | bytes 589832 | tf_op jit(solution)/shard_map/ppermute | solution.py:31
  54.5 19.0 %collective-permute-start.7 = (bf16[256,1024]{1,0:T(8,128)(2,1)}, bf16[256,1024]{1,0:T(8,128)(2,1)}, u32[]{:S(2)}, u32[]{:S(2)}) collective-permute-start(bf16[256,1024]{1,0:T(8,128)(2,1)} %pad_maximum_fusion.1), channel_id=1, source_target_pairs={{1,3},{2,0},{5,7},{6,4},{9,11},{10,8},{13,15},{14,12},{17,19},{18,... | collective-permute-start | bytes 1572872 | tf_op jit(solution)/shard_map/ppermute | solution.py:486
  58.8 25.4 %collective-permute-start.16 = (bf16[4,3,32,1024]{3,2,1,0:T(8,128)(2,1)}, bf16[4,3,32,1024]{3,2,1,0:T(8,128)(2,1)}, u32[]{:S(2)}, u32[]{:S(2)}) collective-permute-start(bf16[4,3,32,1024]{3,2,1,0:T(8,128)(2,1)} %pad_maximum_fusion.refs_8_), channel_id=1, source_target_pairs={{0,4},{4,0},{8,12},{12,8},{16,20},{20,16},{24,28},{28,24},{1,5},{5... | collective-permute-start | bytes 2359304 | tf_op jit(solution)/shard_map/ppermute | solution.py:31
  60.8 4.1 %collective-permute-start.14 = (bf16[256,512]{1,0:T(8,128)(2,1)}, bf16[256,512]{1,0:T(8,128)(2,1)S(1)}, u32[]{:S(2)}, u32[]{:S(2)}) collective-permute-start(bf16[256,512]{1,0:T(8,128)(2,1)} %get-tuple-element.44), channel_id=1, source_target_pairs={{0,4},{8,12},{16,20},{24,28},{4,0},{12,8},{20,16},{28,24},{1,5},{9... | collective-permute-start | bytes 786440 | tf_op jit(solution)/shard_map/ppermute | solution.py:37
  61.2 6.5 %collective-permute-start.15 = (bf16[256,512]{1,0:T(8,128)(2,1)}, bf16[256,512]{1,0:T(8,128)(2,1)S(1)}, u32[]{:S(2)}, u32[]{:S(2)}) collective-permute-start(bf16[256,512]{1,0:T(8,128)(2,1)} %get-tuple-element.48), channel_id=1, source_target_pairs={{4,8},{12,16},{20,24},{8,4},{16,12},{24,20},{5,9},{13,17},{21,25},... | collective-permute-start | bytes 786440 | tf_op jit(solution)/shard_map/ppermute | solution.py:37
  74.8 30.5 %collective-permute-start.24 = (bf16[256,1024]{1,0:T(8,128)(2,1)S(1)}, bf16[256,1024]{1,0:T(8,128)(2,1)S(1)}, u32[]{:S(2)}, u32[]{:S(2)}) collective-permute-start(bf16[256,1024]{1,0:T(8,128)(2,1)S(1)} %get-tuple-element.67), channel_id=1, source_target_pairs={{0,16},{4,20},{8,24},{12,28},{16,0},{20,4},{24,8},{28,12},{1,17},{... | collective-permute-start | bytes 1572872 | tf_op jit(solution)/shard_map/ppermute | solution.py:31
  80.7 27.2 %collective-permute-start.23 = (bf16[256,1024]{1,0:T(8,128)(2,1)S(1)}, bf16[256,1024]{1,0:T(8,128)(2,1)S(1)}, u32[]{:S(2)}, u32[]{:S(2)}) collective-permute-start(bf16[256,1024]{1,0:T(8,128)(2,1)S(1)} %get-tuple-element.67), channel_id=1, source_target_pairs={{0,8},{4,12},{8,0},{12,4},{16,24},{20,28},{24,16},{28,20},{1,9},{5... | collective-permute-start | bytes 1572872 | tf_op jit(solution)/shard_map/ppermute | solution.py:31
  81.9 12.2 %collective-permute-start.17 = (bf16[256,256]{1,0:T(8,128)(2,1)S(1)}, bf16[256,256]{1,0:T(8,128)(2,1)S(1)}, u32[]{:S(2)}, u32[]{:S(2)}) collective-permute-start(bf16[256,256]{1,0:T(8,128)(2,1)S(1)} %attend_two.1), channel_id=1, source_target_pairs={{0,2},{1,3},{2,0},{3,1},{4,6},{5,7},{6,4},{7,5},{8,10},{9,11},{10,... | collective-permute-start | bytes 393224 | tf_op jit(solution)/shard_map/ppermute | solution.py:31
  87.2 18.1 %collective-permute-start.21 = (bf16[288,256]{1,0:T(8,128)(2,1)S(1)}, bf16[288,256]{1,0:T(8,128)(2,1)S(1)}, u32[]{:S(2)}, u32[]{:S(2)}) collective-permute-start(bf16[288,256]{1,0:T(8,128)(2,1)S(1)} %attend_far.1), channel_id=1, source_target_pairs={{0,2},{1,3},{2,0},{3,1},{4,6},{5,7},{6,4},{7,5},{8,10},{9,11},{10,... | collective-permute-start | bytes 442376 | tf_op jit(solution)/shard_map/ppermute | solution.py:31
  97.0 5.6 %collective-permute-start.19 = (bf16[256,256]{1,0:T(8,128)(2,1)S(1)}, bf16[256,256]{1,0:T(8,128)(2,1)S(1)}, u32[]{:S(2)}, u32[]{:S(2)}) collective-permute-start(bf16[256,256]{1,0:T(8,128)(2,1)S(1)} %collective-permute-done.17.refs_2_), channel_id=1, source_target_pairs={{0,1},{1,0},{2,3},{3,2},{4,5},{5,4},{6,7},{7,6},{8,9},{9,8},{10,11... | collective-permute-start | bytes 393224 | tf_op jit(solution)/shard_map/ppermute | solution.py:31
  100.3 5.0 %collective-permute-start.20 = (bf16[256,256]{1,0:T(8,128)(2,1)S(1)}, bf16[256,256]{1,0:T(8,128)(2,1)S(1)}, u32[]{:S(2)}, u32[]{:S(2)}) collective-permute-start(bf16[256,256]{1,0:T(8,128)(2,1)S(1)} %attend_near.1.refs_4_), channel_id=1, source_target_pairs={{0,1},{1,0},{2,3},{3,2},{4,5},{5,4},{6,7},{7,6},{8,9},{9,8},{10,11... | collective-permute-start | bytes 393224 | tf_op jit(solution)/shard_map/ppermute | solution.py:31
  105.4 6.4 %collective-permute-start.25 = (bf16[128,1024]{1,0:T(8,128)(2,1)S(1)}, bf16[128,1024]{1,0:T(8,128)(2,1)S(1)}, u32[]{:S(2)}, u32[]{:S(2)}) collective-permute-start(bf16[128,1024]{1,0:T(8,128)(2,1)S(1)} %slice.82), channel_id=1, source_target_pairs={{0,8},{4,12},{8,0},{12,4},{16,24},{20,28},{24,16},{28,20},{1,9},{5... | collective-permute-start | bytes 786440 | tf_op jit(solution)/shard_map/ppermute | solution.py:31
  105.9 8.5 %collective-permute-start.18 = (bf16[256,256]{1,0:T(8,128)(2,1)S(1)}, bf16[256,256]{1,0:T(8,128)(2,1)S(1)}, u32[]{:S(2)}, u32[]{:S(2)}) collective-permute-start(bf16[256,256]{1,0:T(8,128)(2,1)S(1)} %attend_one.1.refs_0_), channel_id=1, source_target_pairs={{0,1},{1,0},{2,3},{3,2},{4,5},{5,4},{6,7},{7,6},{8,9},{9,8},{10,11... | collective-permute-start | bytes 393224 | tf_op jit(solution)/shard_map/ppermute | solution.py:31
  107.9 6.5 %collective-permute-start.22 = (bf16[288,256]{1,0:T(8,128)(2,1)S(1)}, bf16[288,256]{1,0:T(8,128)(2,1)S(1)}, u32[]{:S(2)}, u32[]{:S(2)}) collective-permute-start(bf16[288,256]{1,0:T(8,128)(2,1)S(1)} %collective-permute-done.21.refs_6_), channel_id=1, source_target_pairs={{0,1},{1,0},{2,3},{3,2},{4,5},{5,4},{6,7},{7,6},{8,9},{9,8},{10,11... | collective-permute-start | bytes 442376 | tf_op jit(solution)/shard_map/ppermute | solution.py:31
  108.0 6.4 %collective-permute-start.26 = (bf16[128,1024]{1,0:T(8,128)(2,1)S(1)}, bf16[128,1024]{1,0:T(8,128)(2,1)S(1)}, u32[]{:S(2)}, u32[]{:S(2)}) collective-permute-start(bf16[128,1024]{1,0:T(8,128)(2,1)S(1)} %slice.83), channel_id=1, source_target_pairs={{0,16},{4,20},{8,24},{12,28},{16,0},{20,4},{24,8},{28,12},{1,17},{... | collective-permute-start | bytes 786440 | tf_op jit(solution)/shard_map/ppermute | solution.py:31
  114.4 4.9 %collective-permute-start.27 = (bf16[1024,1024]{1,0:T(8,128)(2,1)S(1)}, bf16[1024,1024]{1,0:T(8,128)(2,1)S(1)}, u32[]{:S(2)}, u32[]{:S(2)}) collective-permute-start(bf16[1024,1024]{1,0:T(8,128)(2,1)S(1)} %constant_dynamic-update-slice_fusion.held_ref), channel_id=1, source_target_pairs={{0,4},{4,0},{8,12},{12,8},{16,20},{20,16},{24,28},{28,24},{1,5},{5... | collective-permute-start | bytes 6291464 | tf_op jit(solution)/shard_map/ppermute | solution.py:31
  123.3 18.5 %collective-permute-start.28 = (bf16[256,1024]{1,0:T(8,128)(2,1)S(1)}, bf16[256,1024]{1,0:T(8,128)(2,1)S(1)}, u32[]{:S(2)}, u32[]{:S(2)}) collective-permute-start(bf16[256,1024]{1,0:T(8,128)(2,1)S(1)} %feed_partner.1), channel_id=1, source_target_pairs={{0,1},{1,0},{2,3},{3,2},{4,5},{5,4},{6,7},{7,6},{8,9},{9,8},{10,11... | collective-permute-start | bytes 1572872 | tf_op jit(solution)/shard_map/ppermute | solution.py:31
  125.4 13.6 %collective-permute-start.29 = (f32[3,2,1024]{2,1,0:T(2,128)S(1)}, f32[3,2,1024]{2,1,0:T(2,128)S(1)}, u32[]{:S(2)}, u32[]{:S(2)}) collective-permute-start(f32[3,2,1024]{2,1,0:T(2,128)S(1)} %get-tuple-element.70), channel_id=1, source_target_pairs={{0,1},{1,0},{2,3},{3,2},{4,5},{5,4},{6,7},{7,6},{8,9},{9,8},{10,11... | collective-permute-start | bytes 73736 | tf_op jit(solution)/shard_map/ppermute | solution.py:31
  125.5 13.5 %collective-permute-start.30 = (f32[3,2,1024]{2,1,0:T(2,128)S(1)}, f32[3,2,1024]{2,1,0:T(2,128)S(1)}, u32[]{:S(2)}, u32[]{:S(2)}) collective-permute-start(f32[3,2,1024]{2,1,0:T(2,128)S(1)} %get-tuple-element.69), channel_id=1, source_target_pairs={{0,2},{1,3},{2,0},{3,1},{4,6},{5,7},{6,4},{7,5},{8,10},{9,11},{10,... | collective-permute-start | bytes 73736 | tf_op jit(solution)/shard_map/ppermute | solution.py:31
  127.9 13.2 %collective-permute-start.31 = (f32[3,2,1024]{2,1,0:T(2,128)S(1)}, f32[3,2,1024]{2,1,0:T(2,128)S(1)}, u32[]{:S(2)}, u32[]{:S(2)}) collective-permute-start(f32[3,2,1024]{2,1,0:T(2,128)S(1)} %get-tuple-element.68), channel_id=1, source_target_pairs={{0,3},{1,2},{2,1},{3,0},{4,7},{5,6},{6,5},{7,4},{8,11},{9,10},{10,... | collective-permute-start | bytes 73736 | tf_op jit(solution)/shard_map/ppermute | solution.py:31
  (21 other events, 250.5 us)

commit v18 on v12

--- a/solution.py
+++ b/solution.py
@@ -163,7 +163,8 @@
 def attend_kernel(flips, place_ref, starts_ref, ends_ref, query_ref, middle_ref, edges_ref, even_ref, odd_ref, *refs):
     out_ref, window_ref, bias_ref, scores_ref, weights_ref, sems = refs
     tok, kv = place_ref[0], place_ref[1]
-    count = out_ref.shape[0] // len(flips)
+    count = bias_ref.shape[0]
+    out_ref[len(flips) * count :] = jnp.zeros_like(out_ref[len(flips) * count :])
     blocks = query_ref.shape[0] // count
     copies = []
     for index, flip in enumerate(flips):
@@ -198,11 +199,11 @@
         attend(query, window_ref.at[index], bias_ref, scores_ref, weights_ref, out)
 
 
-def attend_blocks(place, starts, ends, query, middle, edges, even, odd, rows, flips, name):
+def attend_blocks(place, starts, ends, query, middle, edges, even, odd, rows, flips, name, spare):
     heads_width = query.shape[1]
     return pl.pallas_call(
         functools.partial(attend_kernel, flips),
-        out_shape=jax.ShapeDtypeStruct((len(flips) * rows, heads_width), BF16),
+        out_shape=jax.ShapeDtypeStruct((len(flips) * rows + spare, heads_width), BF16),
         in_specs=[SMEM, VMEM, VMEM, VMEM, ANY, ANY, ANY, ANY],
         out_specs=VMEM,
         scratch_shapes=[
@@ -496,21 +497,22 @@
     even, odd = over_edges(even, "tok", 0), over_edges(odd, "tok", 1)
     query, middle = project(place, weight, (after(hidden_in, edges),) + shards[1:], kvs, False)
     window = (middle, edges, even, odd, rows)
-    far = attend_blocks(place, starts, ends, query, *window, (2, 3), "attend_far")
+    out_all = jnp.stack([out_here, out_x, out_y, out_far])
+    far = attend_blocks(place, starts, ends, query, *window, (2, 3), "attend_far", 32)
     far_heads = swapped(far, "kv", 2)
     feed_here = jnp.where(inner, feed_inner, after(feed_outer, far))
     feed_x, feed_y = swapped(feed_here, "tok", 2), swapped(feed_here, "tok", 4)
-    near = attend_blocks(place, starts, ends, after(query, feed_here), *window, (0, 1), "attend_near")
+    near = attend_blocks(place, starts, ends, after(query, feed_here), *window, (0, 1), "attend_near", 16)
     partner_heads, passed_heads = swapped(near, "kv", 1), swapped(far_heads, "kv", 1)
     parts = (near, partner_heads, far_heads, passed_heads)
-
-    out_all = jnp.stack([out_here, out_x, out_y, out_far])
-    out_pieces = [((0, 2, 4, 6), out_all), ((1, 3, 5, 7), swapped(after(out_all, near, far_heads), "tok", 1))]
+    out_core = swapped(after(out_all, near, far_heads), "tok", 1)
+    out_pieces = [((0, 2, 4, 6), out_all), ((1, 3, 5, 7), out_core)]
+
     half = feed_here.shape[0] // 2
     far_up = swapped(after(feed_y, far_heads, partner_heads)[:half], "tok", 2)
     far_down = swapped(after(feed_x, far_heads, partner_heads)[half:], "tok", 4)
     held = jnp.concatenate([feed_here, feed_x, feed_y, far_up, far_down], axis=0)
-    feed_pieces = (held, swapped(after(held, passed_heads), "tok", 1))
+    feed_pieces = (held, swapped(after(held, passed_heads, out_core), "tok", 1))
 
     gain, bias = ln1_gain[None, :], ln1_bias[None, :]
     normed, partner = first_norm(place, hidden_in, a1, out_weight, gain, bias, parts, out_pieces)

time: 137 us -> 133 us (0.971)
  waiting for transfers between devices: 44.5 us -> 38.7 us
  starting transfers between devices: 46 us -> 47.8 us
    ppermute x19, waiting for transfers between devices: 31.6 us -> 25.9 us  [swapped(): return lax.ppermute(value, axis, [(i, i ^ flip) for i in range(count)])]
    ppermute x19, starting transfers between devices: 27 us -> 28.8 us  [swapped(): return lax.ppermute(value, axis, [(i, i ^ flip) for i in range(count)])]
  transfers between devices with their start and end apart: 28 -> 28, of which waited for: 12 -> 11; matrix products, arithmetic and copies ran while one was open for 4% -> 6% of each run, Pallas kernels for 19% -> 20%
where the time goes in v18:
time: 133 us; the launch traced here: 132 us
  starting transfers between devices  47.8 us (36%)
  waiting for transfers between devices  38.7 us (29%)
  Pallas kernels  31.3 us (24%)
  local copies, waits for them, and re-layouts  8.06 us (6%)
  other arithmetic  5.16 us (4%)
    ppermute x19, starting transfers between devices, swapped(): return lax.ppermute(value, axis, [(i, i ^ flip) for i in range(count)])  28.8 us
    ppermute x19, waiting for transfers between devices, swapped(): return lax.ppermute(value, axis, [(i, i ^ flip) for i in range(count)])  25.9 us
    pallas_call x2, Pallas kernels, attend_blocks(): pl.pallas_call(functools.partial(attend_kernel, flips), out_shape=jax.Sha...  10.8 us
    ppermute x5, starting transfers between devices, over_edges(): return lax.ppermute(value, axis, edges + [(j, i) for i, j in edges])  8.74 us
    pallas_call x2, Pallas kernels, feed(): pl.pallas_call(feed_kernel, out_shape=jax.ShapeDtypeStruct((count, width)...  7.81 us
    ppermute x1, starting transfers between devices, routed_body(): feed_inner = lax.ppermute(after(feed_part, a2, b2), 'kv', [(0, 2), (3, 1)])  6.4 us
    ppermute x5, waiting for transfers between devices, over_edges(): return lax.ppermute(value, axis, edges + [(j, i) for i, j in edges])  6.26 us
    unnamed x63, local copies, waits for them, and re-layouts  6.02 us
  transfers between devices with their start and end apart: 28, of which 11 were waited for; matrix products, arithmetic and copies ran while one was open for 6% of the time, Pallas kernels for 20%

profile of v18, /device:TPU:0, one launch (start us, length us, event | category | flops | bytes accessed | tf_op | source)
XLA Modules:
  0.0 132.3 jit_solution(2634618924996586648)
XLA Ops:
  1.5 5.9 %collective-permute-start = (bf16[256,1024]{1,0:T(8,128)(2,1)}, bf16[256,1024]{1,0:T(8,128)(2,1)S(1)}, u32[]{:S(2)}, u32[]{:S(2)}) collective-permute-start(bf16[256,1024]{1,0:T(8,128)(2,1)} %own_ref.1), channel_id=1, source_target_pairs={{0,1},{2,3},{1,0},{3,2},{4,5},{6,7},{5,4},{7,6},{8,9},{10,11},{9,8... | collective-permute-start | bytes 1572872 | tf_op jit(solution)/shard_map/ppermute | solution.py:37
  8.9 1.3 %collective-permute-start.3 = (bf16[34,1024]{1,0:T(8,128)(2,1)S(1)}, bf16[34,1024]{1,0:T(8,128)(2,1)S(1)}, u32[]{:S(2)}, u32[]{:S(2)}) collective-permute-start(bf16[34,1024]{1,0:T(8,128)(2,1)S(1)} %pad_maximum_fusion.3), channel_id=1, source_target_pairs={{0,3},{1,2},{2,1},{3,0},{4,7},{5,6},{6,5},{7,4},{8,11},{9,10},{10,... | collective-permute-start | bytes 208904 | tf_op jit(solution)/shard_map/ppermute | solution.py:31
  10.4 2.9 %collective-permute-start.1 = (bf16[34,1024]{1,0:T(8,128)(2,1)S(1)}, bf16[34,1024]{1,0:T(8,128)(2,1)S(1)}, u32[]{:S(2)}, u32[]{:S(2)}) collective-permute-start(bf16[34,1024]{1,0:T(8,128)(2,1)S(1)} %pad_maximum_fusion.3), channel_id=1, source_target_pairs={{0,1},{1,0},{2,3},{3,2},{4,5},{5,4},{6,7},{7,6},{8,9},{9,8},{10,11... | collective-permute-start | bytes 208904 | tf_op jit(solution)/shard_map/ppermute | solution.py:31
  14.0 1.3 collective-permute-start.8
  15.3 6.2 %collective-permute-done.refs_1_.partner_ref = bf16[256,1024]{1,0:T(8,128)(2,1)S(1)} collective-permute-done((bf16[256,1024]{1,0:T(8,128)(2,1)}, bf16[256,1024]{1,0:T(8,128)(2,1)S(1)}, u32[]{:S(2)}, u32[]{:S(2)}) %collective-permute-start) | collective-permute-done | bytes 524320 | tf_op jit(solution)/shard_map/ppermute | solution.py:37
  24.1 3.0 %collective-permute-done.2 = bf16[34,1024]{1,0:T(8,128)(2,1)S(1)} collective-permute-done((bf16[34,1024]{1,0:T(8,128)(2,1)S(1)}, bf16[34,1024]{1,0:T(8,128)(2,1)S(1)}, u32[]{:S(2)}, u32[]{:S(2)}) %collective-permute-start.2) | collective-permute-done | bytes 69664 | tf_op jit(solution)/shard_map/ppermute | solution.py:31
  27.3 1.9 %copy-done.4 = bf16[2,1,6,128,1024]{4,3,2,1,0:T(8,128)(2,1)S(1)} copy-done((bf16[2,1,6,128,1024]{4,3,2,1,0:T(8,128)(2,1)S(1)}, bf16[2,1,6,128,1024]{4,3,2,1,0:T(8,128)(2,1)}, u32[]{:S(2)}) %copy-start.4) | copy-done | bytes 3145752
  29.2 3.8 %decode.1 = f32[3,8,1024]{2,1,0:T(8,128)S(1)} custom-call(s32[6]{0:T(128)S(1)} %fusion.12.slot_ref, s32[6]{0:T(128)S(1)} %bitcast.151, f32[8,1024]{1,0:T(8,128)S(1)} %maximum_convert_fusion.query_ref, bf16[2,1,6,128,1024]{4,3,2,1,0:T(8,128)(2,1)S(1)} %copy-done.4), custom_call_target="tpu_custom_call" | custom-call | flops 1 | bytes 1 | tf_op jit(solution)/shard_map/decode/pallas_call | solution.py:408
  33.0 1.3 collective-permute-start.10
  34.3 1.4 %collective-permute-done.8.refs_2_ = bf16[256,1024]{1,0:T(8,128)(2,1)S(1)} collective-permute-done((bf16[256,1024]{1,0:T(8,128)(2,1)S(1)}, bf16[256,1024]{1,0:T(8,128)(2,1)S(1)}, u32[]{:S(2)}, u32[]{:S(2)}) %collective-permute-start.8) | collective-permute-done | bytes 524320 | tf_op jit(solution)/shard_map/ppermute | solution.py:476
  35.7 6.4 %collective-permute-start.11 = (bf16[256,1024]{1,0:T(8,128)(2,1)}, bf16[256,1024]{1,0:T(8,128)(2,1)S(1)}, u32[]{:S(2)}, u32[]{:S(2)}) collective-permute-start(bf16[256,1024]{1,0:T(8,128)(2,1)} %pad_maximum_fusion.1), channel_id=1, source_target_pairs={{0,2},{3,1},{4,6},{7,5},{8,10},{11,9},{12,14},{15,13},{16,18},{19,... | collective-permute-start | bytes 1572872 | tf_op jit(solution)/shard_map/ppermute | solution.py:487
  42.9 1.5 %collective-permute-start.4 = (bf16[3,32,1024]{2,1,0:T(8,128)(2,1)S(1)}, bf16[3,32,1024]{2,1,0:T(8,128)(2,1)S(1)}, u32[]{:S(2)}, u32[]{:S(2)}) collective-permute-start(bf16[3,32,1024]{2,1,0:T(8,128)(2,1)S(1)} %get-tuple-element.53), channel_id=1, source_target_pairs={{0,8},{4,12},{8,0},{12,4},{16,24},{20,28},{24,16},{28,20},{1,9},{5... | collective-permute-start | bytes 589832 | tf_op jit(solution)/shard_map/ppermute | solution.py:31
  44.4 1.5 %collective-permute-start.5 = (bf16[3,32,1024]{2,1,0:T(8,128)(2,1)S(1)}, bf16[3,32,1024]{2,1,0:T(8,128)(2,1)S(1)}, u32[]{:S(2)}, u32[]{:S(2)}) collective-permute-start(bf16[3,32,1024]{2,1,0:T(8,128)(2,1)S(1)} %get-tuple-element.53), channel_id=1, source_target_pairs={{0,16},{4,20},{8,24},{12,28},{16,0},{20,4},{24,8},{28,12},{1,17},{... | collective-permute-start | bytes 589832 | tf_op jit(solution)/shard_map/ppermute | solution.py:31
  46.4 2.6 %collective-permute-done.10.refs_3_ = bf16[256,1024]{1,0:T(8,128)(2,1)S(1)} collective-permute-done((bf16[256,1024]{1,0:T(8,128)(2,1)S(1)}, bf16[256,1024]{1,0:T(8,128)(2,1)S(1)}, u32[]{:S(2)}, u32[]{:S(2)}) %collective-permute-start.10) | collective-permute-done | bytes 524320 | tf_op jit(solution)/shard_map/ppermute | solution.py:481
  49.0 2.6 %collective-permute-done.11 = bf16[256,1024]{1,0:T(8,128)(2,1)S(1)} collective-permute-done((bf16[256,1024]{1,0:T(8,128)(2,1)}, bf16[256,1024]{1,0:T(8,128)(2,1)S(1)}, u32[]{:S(2)}, u32[]{:S(2)}) %collective-permute-start.11) | collective-permute-done | bytes 524320 | tf_op jit(solution)/shard_map/ppermute | solution.py:487
  53.0 2.3 %project_edges.1 = (bf16[512,512]{1,0:T(8,128)(2,1)S(1)}, bf16[256,512]{1,0:T(8,128)(2,1)}, bf16[256,512]{1,0:T(8,128)(2,1)}) custom-call(s32[2]{0:T(128)S(1)} %pad_add_fusion.place_ref, bf16[3,1024,256]{2,1,0:T(8,128)(2,1)S(1)} %bitcast.143, bf16[256,1024]{1,0:T(8,128)(2,1)S(1)} %copy-done.3, ...), custom_call_target="tpu_custom_call" | custom-call | flops 1 | bytes 1 | tf_op jit(solution)/shard_map/project_edges/pallas_call | solution.py:112
  56.2 1.3 %collective-permute-start.14 = (bf16[256,512]{1,0:T(8,128)(2,1)}, bf16[256,512]{1,0:T(8,128)(2,1)}, u32[]{:S(2)}, u32[]{:S(2)}) collective-permute-start(bf16[256,512]{1,0:T(8,128)(2,1)} %get-tuple-element.35), channel_id=1, source_target_pairs={{4,8},{12,16},{20,24},{8,4},{16,12},{24,20},{5,9},{13,17},{21,25},... | collective-permute-start | bytes 786440 | tf_op jit(solution)/shard_map/ppermute | solution.py:37
  60.8 2.2 %project_rest.1 = (bf16[1024,256]{1,0:T(8,128)(2,1)S(1)}, bf16[512,512]{1,0:T(8,128)(2,1)S(1)}) custom-call(s32[2]{0:T(128)S(1)} %pad_add_fusion.place_ref, bf16[3,1024,256]{2,1,0:T(8,128)(2,1)S(1)} %bitcast.144, bf16[256,1024]{1,0:T(8,128)(2,1)S(1)} %copy-done.3, bf16[256,1024]{1,0:T(8,128)(2,1)S(1)} %collective-permute-done.refs_1_.partner_ref, ...), custom_call_target="tpu_custom_call" | custom-call | flops 1 | bytes 1 | tf_op jit(solution)/shard_map/project_rest/pallas_call | solution.py:112
  63.0 5.2 %attend_far.1 = bf16[544,256]{1,0:T(8,128)(2,1)S(1)} custom-call(s32[2]{0:T(128)S(1)} %pad_add_fusion.place_ref, s32[1,48]{1,0:T(1,128)S(1)} %subtract_bitcast_fusion.starts_ref, s32[1,48]{1,0:T(1,128)S(1)} %bitcast.149, bf16[1024,256]{1,0:T(8,128)(2,1)S(1)} %get-tuple-element.37.query_ref, bf16[512,512]{1,0:T(8,128)(2,1)S(1)} %get-tuple-element.33.middle_ref, ...), custom_call_target="tpu_custom_call" | custom-call | flops 1 | bytes 1 | tf_op jit(solution)/shard_map/attend_far/pallas_call | solution.py:204
  68.2 4.7 %collective-permute-start.16 = (bf16[544,256]{1,0:T(8,128)(2,1)S(1)}, bf16[544,256]{1,0:T(8,128)(2,1)S(1)}, u32[]{:S(2)}, u32[]{:S(2)}) collective-permute-start(bf16[544,256]{1,0:T(8,128)(2,1)S(1)} %attend_far.1), channel_id=1, source_target_pairs={{0,2},{1,3},{2,0},{3,1},{4,6},{5,7},{6,4},{7,5},{8,10},{9,11},{10,... | collective-permute-start | bytes 835592 | tf_op jit(solution)/shard_map/ppermute | solution.py:31
  74.3 6.2 %collective-permute-start.20 = (bf16[256,1024]{1,0:T(8,128)(2,1)S(1)}, bf16[256,1024]{1,0:T(8,128)(2,1)S(1)}, u32[]{:S(2)}, u32[]{:S(2)}) collective-permute-start(bf16[256,1024]{1,0:T(8,128)(2,1)S(1)} %get-tuple-element.51), channel_id=1, source_target_pairs={{0,16},{4,20},{8,24},{12,28},{16,0},{20,4},{24,8},{28,12},{1,17},{... | collective-permute-start | bytes 1572872 | tf_op jit(solution)/shard_map/ppermute | solution.py:31
  80.9 5.6 %attend_near.1.refs_0_ = bf16[528,256]{1,0:T(8,128)(2,1)S(1)} custom-call(s32[2]{0:T(128)S(1)} %pad_add_fusion.place_ref, s32[1,48]{1,0:T(1,128)S(1)} %subtract_bitcast_fusion.starts_ref, s32[1,48]{1,0:T(1,128)S(1)} %bitcast.150, bf16[1024,256]{1,0:T(8,128)(2,1)S(1)} %get-tuple-element.37.query_ref, bf16[512,512]{1,0:T(8,128)(2,1)S(1)} %get-tuple-element.33.middle_ref, ...), custom_call_target="tpu_custom_call" | custom-call | flops 1 | bytes 1 | tf_op jit(solution)/shard_map/attend_near/pallas_call | solution.py:204
  86.7 8.8 %collective-permute-done.15.refs_1_ = bf16[528,256]{1,0:T(8,128)(2,1)S(1)} collective-permute-done((bf16[528,256]{1,0:T(8,128)(2,1)S(1)}, bf16[528,256]{1,0:T(8,128)(2,1)S(1)}, u32[]{:S(2)}, u32[]{:S(2)}) %collective-permute-start.15) | collective-permute-done | bytes 270368 | tf_op jit(solution)/shard_map/ppermute | solution.py:31
  95.5 3.2 %collective-permute-start.21 = (bf16[128,1024]{1,0:T(8,128)(2,1)S(1)}, bf16[128,1024]{1,0:T(8,128)(2,1)S(1)}, u32[]{:S(2)}, u32[]{:S(2)}) collective-permute-start(bf16[128,1024]{1,0:T(8,128)(2,1)S(1)} %slice.82), channel_id=1, source_target_pairs={{0,8},{4,12},{8,0},{12,4},{16,24},{20,28},{24,16},{28,20},{1,9},{5... | collective-permute-start | bytes 786440 | tf_op jit(solution)/shard_map/ppermute | solution.py:31
  99.2 5.1 %collective-permute-done.21 = bf16[128,1024]{1,0:T(8,128)(2,1)S(1)} collective-permute-done((bf16[128,1024]{1,0:T(8,128)(2,1)S(1)}, bf16[128,1024]{1,0:T(8,128)(2,1)S(1)}, u32[]{:S(2)}, u32[]{:S(2)}) %collective-permute-start.21) | collective-permute-done | bytes 262176 | tf_op jit(solution)/shard_map/ppermute | solution.py:31
  104.3 1.9 %collective-permute-done.22 = bf16[128,1024]{1,0:T(8,128)(2,1)S(1)} collective-permute-done((bf16[128,1024]{1,0:T(8,128)(2,1)S(1)}, bf16[128,1024]{1,0:T(8,128)(2,1)S(1)}, u32[]{:S(2)}, u32[]{:S(2)}) %collective-permute-start.22) | collective-permute-done | bytes 262176 | tf_op jit(solution)/shard_map/ppermute | solution.py:31
  106.4 3.3 %first_norm.1 = (bf16[256,1024]{1,0:T(8,128)(2,1)S(1)}, bf16[256,1024]{1,0:T(8,128)(2,1)S(1)}) custom-call(s32[2]{0:T(128)S(1)} %pad_add_fusion.place_ref, bf16[256,1024]{1,0:T(8,128)(2,1)S(1)} %copy-done.3, bf16[256,1024]{1,0:T(8,128)(2,1)S(1)} %collective-permute-done.refs_1_.partner_ref, bf16[256,1024]{1,0:T(8,128)(2,1)S(1)} %copy-done.13, ...), custom_call_target="tpu_custom_call" | custom-call | flops 1 | bytes 1 | tf_op jit(solution)/shard_map/first_norm/pallas_call | solution.py:257
  110.5 3.9 %feed_partner.1 = bf16[256,1024]{1,0:T(8,128)(2,1)S(1)} custom-call(s32[2]{0:T(128)S(1)} %pad_add_fusion.place_ref, bf16[256,1024]{1,0:T(8,128)(2,1)S(1)} %get-tuple-element.40.rows_ref, bf16[1024,1024]{1,0:T(8,128)(2,1)S(1)} %copy-done, bf16[1024,1024]{1,0:T(8,128)(2,1)S(1)} %copy-done.1, bf16[1024,1024]{1,0:T(8,128)(2,1)S(1)} %constant_dynamic-update-slice_fusion.held_ref, ...), custom_call_target="tpu_custom_call" | custom-call | flops 1 | bytes 1 | tf_op jit(solution)/shard_map/feed_partner/pallas_call | solution.py:326
  114.4 1.5 %collective-permute-start.24 = (bf16[256,1024]{1,0:T(8,128)(2,1)S(1)}, bf16[256,1024]{1,0:T(8,128)(2,1)S(1)}, u32[]{:S(2)}, u32[]{:S(2)}) collective-permute-start(bf16[256,1024]{1,0:T(8,128)(2,1)S(1)} %feed_partner.1), channel_id=1, source_target_pairs={{0,1},{1,0},{2,3},{3,2},{4,5},{5,4},{6,7},{7,6},{8,9},{9,8},{10,11... | collective-permute-start | bytes 1572872 | tf_op jit(solution)/shard_map/ppermute | solution.py:31
  117.5 2.8 %collective-permute-start.27 = (f32[3,2,1024]{2,1,0:T(2,128)S(1)}, f32[3,2,1024]{2,1,0:T(2,128)S(1)}, u32[]{:S(2)}, u32[]{:S(2)}) collective-permute-start(f32[3,2,1024]{2,1,0:T(2,128)S(1)} %get-tuple-element.54), channel_id=1, source_target_pairs={{0,3},{1,2},{2,1},{3,0},{4,7},{5,6},{6,5},{7,4},{8,11},{9,10},{10,... | collective-permute-start | bytes 73736 | tf_op jit(solution)/shard_map/ppermute | solution.py:31
  120.4 3.9 %feed_own.1.near_ref = f32[256,1024]{1,0:T(8,128)S(1)} custom-call(s32[2]{0:T(128)S(1)} %pad_add_fusion.place_ref, bf16[256,1024]{1,0:T(8,128)(2,1)S(1)} %get-tuple-element.44.rows_ref.normed_ref, bf16[1024,1024]{1,0:T(8,128)(2,1)S(1)} %copy-done, bf16[1024,1024]{1,0:T(8,128)(2,1)S(1)} %copy-done.1, ...), custom_call_target="tpu_custom_call" | custom-call | flops 1 | bytes 1 | tf_op jit(solution)/shard_map/feed_own/pallas_call | solution.py:326
  124.3 5.5 %collective-permute-done.25 = f32[3,2,1024]{2,1,0:T(2,128)S(1)} collective-permute-done((f32[3,2,1024]{2,1,0:T(2,128)S(1)}, f32[3,2,1024]{2,1,0:T(2,128)S(1)}, u32[]{:S(2)}, u32[]{:S(2)}) %collective-permute-start.25) | collective-permute-done | bytes 24608 | tf_op jit(solution)/shard_map/ppermute | solution.py:31
  (119 shorter events, 20.0 us)
Async XLA Ops:
  0.6 26.6 %copy-start.28 = (bf16[2,1024]{1,0:T(2,128)(2,1)S(1)}, bf16[2,1024]{1,0:T(2,128)(2,1)}, u32[]{:S(2)}) copy-start(bf16[2,1024]{1,0:T(2,128)(2,1)} %param.24) | copy-start | bytes 12292
  0.6 26.6 %copy-start.18 = (s32[1,6]{1,0:T(1,128)S(1)}, s32[1,6]{1,0:T(1,128)}, u32[]{:S(2)}) copy-start(s32[1,6]{1,0:T(1,128)} %param.27) | copy-start | bytes 76
  0.7 13.3 %collective-permute-start.7 = (bf16[256,1024]{1,0:T(8,128)(2,1)}, bf16[256,1024]{1,0:T(8,128)(2,1)S(1)}, u32[]{:S(2)}, u32[]{:S(2)}) collective-permute-start(bf16[256,1024]{1,0:T(8,128)(2,1)} %own_ref.1), channel_id=1, source_target_pairs={{1,2},{2,1},{5,6},{6,5},{9,10},{10,9},{13,14},{14,13},{17,18},{18,... | collective-permute-start | bytes 1572872 | tf_op jit(solution)/shard_map/ppermute | solution.py:37
  1.5 20.0 %collective-permute-start = (bf16[256,1024]{1,0:T(8,128)(2,1)}, bf16[256,1024]{1,0:T(8,128)(2,1)S(1)}, u32[]{:S(2)}, u32[]{:S(2)}) collective-permute-start(bf16[256,1024]{1,0:T(8,128)(2,1)} %own_ref.1), channel_id=1, source_target_pairs={{0,1},{2,3},{1,0},{3,2},{4,5},{6,7},{5,4},{7,6},{8,9},{10,11},{9,8... | collective-permute-start | bytes 1572872 | tf_op jit(solution)/shard_map/ppermute | solution.py:37
  8.9 15.2 %collective-permute-start.3 = (bf16[34,1024]{1,0:T(8,128)(2,1)S(1)}, bf16[34,1024]{1,0:T(8,128)(2,1)S(1)}, u32[]{:S(2)}, u32[]{:S(2)}) collective-permute-start(bf16[34,1024]{1,0:T(8,128)(2,1)S(1)} %pad_maximum_fusion.3), channel_id=1, source_target_pairs={{0,3},{1,2},{2,1},{3,0},{4,7},{5,6},{6,5},{7,4},{8,11},{9,10},{10,... | collective-permute-start | bytes 208904 | tf_op jit(solution)/shard_map/ppermute | solution.py:31
  10.3 16.9 %collective-permute-start.2 = (bf16[34,1024]{1,0:T(8,128)(2,1)S(1)}, bf16[34,1024]{1,0:T(8,128)(2,1)S(1)}, u32[]{:S(2)}, u32[]{:S(2)}) collective-permute-start(bf16[34,1024]{1,0:T(8,128)(2,1)S(1)} %pad_maximum_fusion.3), channel_id=1, source_target_pairs={{0,2},{1,3},{2,0},{3,1},{4,6},{5,7},{6,4},{7,5},{8,10},{9,11},{10,... | collective-permute-start | bytes 208904 | tf_op jit(solution)/shard_map/ppermute | solution.py:31
  10.4 16.8 %collective-permute-start.1 = (bf16[34,1024]{1,0:T(8,128)(2,1)S(1)}, bf16[34,1024]{1,0:T(8,128)(2,1)S(1)}, u32[]{:S(2)}, u32[]{:S(2)}) collective-permute-start(bf16[34,1024]{1,0:T(8,128)(2,1)S(1)} %pad_maximum_fusion.3), channel_id=1, source_target_pairs={{0,1},{1,0},{2,3},{3,2},{4,5},{5,4},{6,7},{7,6},{8,9},{9,8},{10,11... | collective-permute-start | bytes 208904 | tf_op jit(solution)/shard_map/ppermute | solution.py:31
  14.0 21.8 %collective-permute-start.8 = (bf16[256,1024]{1,0:T(8,128)(2,1)S(1)}, bf16[256,1024]{1,0:T(8,128)(2,1)S(1)}, u32[]{:S(2)}, u32[]{:S(2)}) collective-permute-start(bf16[256,1024]{1,0:T(8,128)(2,1)S(1)} %collective-permute-done.7.refs_4_), channel_id=1, source_target_pairs={{1,0},{2,3},{5,4},{6,7},{9,8},{10,11},{13,12},{14,15},{17,16},{18,... | collective-permute-start | bytes 1572872 | tf_op jit(solution)/shard_map/ppermute | solution.py:476
  21.5 11.4 %collective-permute-start.9 = (bf16[256,1024]{1,0:T(8,128)(2,1)S(1)}, bf16[256,1024]{1,0:T(8,128)(2,1)S(1)}, u32[]{:S(2)}, u32[]{:S(2)}) collective-permute-start(bf16[256,1024]{1,0:T(8,128)(2,1)S(1)} %collective-permute-done.refs_1_.partner_ref), channel_id=1, source_target_pairs={{1,2},{2,1},{5,6},{6,5},{9,10},{10,9},{13,14},{14,13},{17,18},{18,... | collective-permute-start | bytes 1572872 | tf_op jit(solution)/shard_map/ppermute | solution.py:37
  29.2 23.8 %copy-start.2 = (bf16[1024,3,256]{2,0,1:T(8,128)(2,1)S(1)}, bf16[1024,3,256]{2,0,1:T(8,128)(2,1)}, u32[]{:S(2)}) copy-start(bf16[1024,3,256]{2,0,1:T(8,128)(2,1)} %param.15) | copy-start | bytes 4718596
  29.2 23.8 %copy-start.3 = (bf16[256,1024]{1,0:T(8,128)(2,1)S(1)}, bf16[256,1024]{1,0:T(8,128)(2,1)}, u32[]{:S(2)}) copy-start(bf16[256,1024]{1,0:T(8,128)(2,1)} %own_ref.1) | copy-start | bytes 1572868
  33.0 16.0 %collective-permute-start.10 = (bf16[256,1024]{1,0:T(8,128)(2,1)S(1)}, bf16[256,1024]{1,0:T(8,128)(2,1)S(1)}, u32[]{:S(2)}, u32[]{:S(2)}) collective-permute-start(bf16[256,1024]{1,0:T(8,128)(2,1)S(1)} %collective-permute-done.9.refs_5_), channel_id=1, source_target_pairs={{1,0},{2,3},{5,4},{6,7},{9,8},{10,11},{13,12},{14,15},{17,16},{18,... | collective-permute-start | bytes 1572872 | tf_op jit(solution)/shard_map/ppermute | solution.py:481
  35.7 15.8 %collective-permute-start.11 = (bf16[256,1024]{1,0:T(8,128)(2,1)}, bf16[256,1024]{1,0:T(8,128)(2,1)S(1)}, u32[]{:S(2)}, u32[]{:S(2)}) collective-permute-start(bf16[256,1024]{1,0:T(8,128)(2,1)} %pad_maximum_fusion.1), channel_id=1, source_target_pairs={{0,2},{3,1},{4,6},{7,5},{8,10},{11,9},{12,14},{15,13},{16,18},{19,... | collective-permute-start | bytes 1572872 | tf_op jit(solution)/shard_map/ppermute | solution.py:487
  42.9 10.0 %collective-permute-start.4 = (bf16[3,32,1024]{2,1,0:T(8,128)(2,1)S(1)}, bf16[3,32,1024]{2,1,0:T(8,128)(2,1)S(1)}, u32[]{:S(2)}, u32[]{:S(2)}) collective-permute-start(bf16[3,32,1024]{2,1,0:T(8,128)(2,1)S(1)} %get-tuple-element.53), channel_id=1, source_target_pairs={{0,8},{4,12},{8,0},{12,4},{16,24},{20,28},{24,16},{28,20},{1,9},{5... | collective-permute-start | bytes 589832 | tf_op jit(solution)/shard_map/ppermute | solution.py:31
  44.4 8.6 %collective-permute-start.5 = (bf16[3,32,1024]{2,1,0:T(8,128)(2,1)S(1)}, bf16[3,32,1024]{2,1,0:T(8,128)(2,1)S(1)}, u32[]{:S(2)}, u32[]{:S(2)}) collective-permute-start(bf16[3,32,1024]{2,1,0:T(8,128)(2,1)S(1)} %get-tuple-element.53), channel_id=1, source_target_pairs={{0,16},{4,20},{8,24},{12,28},{16,0},{20,4},{24,8},{28,12},{1,17},{... | collective-permute-start | bytes 589832 | tf_op jit(solution)/shard_map/ppermute | solution.py:31
  45.9 7.0 %collective-permute-start.6 = (bf16[3,32,1024]{2,1,0:T(8,128)(2,1)S(1)}, bf16[3,32,1024]{2,1,0:T(8,128)(2,1)S(1)}, u32[]{:S(2)}, u32[]{:S(2)}) collective-permute-start(bf16[3,32,1024]{2,1,0:T(8,128)(2,1)S(1)} %get-tuple-element.53), channel_id=1, source_target_pairs={{0,24},{4,28},{8,16},{12,20},{16,8},{20,12},{24,0},{28,4},{1,25},{... | collective-permute-start | bytes 589832 | tf_op jit(solution)/shard_map/ppermute | solution.py:31
  51.5 21.4 %collective-permute-start.12 = (bf16[256,1024]{1,0:T(8,128)(2,1)}, bf16[256,1024]{1,0:T(8,128)(2,1)}, u32[]{:S(2)}, u32[]{:S(2)}) collective-permute-start(bf16[256,1024]{1,0:T(8,128)(2,1)} %pad_maximum_fusion.1), channel_id=1, source_target_pairs={{1,3},{2,0},{5,7},{6,4},{9,11},{10,8},{13,15},{14,12},{17,19},{18,... | collective-permute-start | bytes 1572872 | tf_op jit(solution)/shard_map/ppermute | solution.py:488
  56.2 6.8 %collective-permute-start.13 = (bf16[256,512]{1,0:T(8,128)(2,1)}, bf16[256,512]{1,0:T(8,128)(2,1)S(1)}, u32[]{:S(2)}, u32[]{:S(2)}) collective-permute-start(bf16[256,512]{1,0:T(8,128)(2,1)} %get-tuple-element.34), channel_id=1, source_target_pairs={{0,4},{8,12},{16,20},{24,28},{4,0},{12,8},{20,16},{28,24},{1,5},{9... | collective-permute-start | bytes 786440 | tf_op jit(solution)/shard_map/ppermute | solution.py:37
  56.2 6.8 %collective-permute-start.14 = (bf16[256,512]{1,0:T(8,128)(2,1)}, bf16[256,512]{1,0:T(8,128)(2,1)}, u32[]{:S(2)}, u32[]{:S(2)}) collective-permute-start(bf16[256,512]{1,0:T(8,128)(2,1)} %get-tuple-element.35), channel_id=1, source_target_pairs={{4,8},{12,16},{20,24},{8,4},{16,12},{24,20},{5,9},{13,17},{21,25},... | collective-permute-start | bytes 786440 | tf_op jit(solution)/shard_map/ppermute | solution.py:37
  68.2 18.3 %collective-permute-start.16 = (bf16[544,256]{1,0:T(8,128)(2,1)S(1)}, bf16[544,256]{1,0:T(8,128)(2,1)S(1)}, u32[]{:S(2)}, u32[]{:S(2)}) collective-permute-start(bf16[544,256]{1,0:T(8,128)(2,1)S(1)} %attend_far.1), channel_id=1, source_target_pairs={{0,2},{1,3},{2,0},{3,1},{4,6},{5,7},{6,4},{7,5},{8,10},{9,11},{10,... | collective-permute-start | bytes 835592 | tf_op jit(solution)/shard_map/ppermute | solution.py:31
  74.3 21.2 %collective-permute-start.20 = (bf16[256,1024]{1,0:T(8,128)(2,1)S(1)}, bf16[256,1024]{1,0:T(8,128)(2,1)S(1)}, u32[]{:S(2)}, u32[]{:S(2)}) collective-permute-start(bf16[256,1024]{1,0:T(8,128)(2,1)S(1)} %get-tuple-element.51), channel_id=1, source_target_pairs={{0,16},{4,20},{8,24},{12,28},{16,0},{20,4},{24,8},{28,12},{1,17},{... | collective-permute-start | bytes 1572872 | tf_op jit(solution)/shard_map/ppermute | solution.py:31
  80.5 18.5 %collective-permute-start.19 = (bf16[256,1024]{1,0:T(8,128)(2,1)S(1)}, bf16[256,1024]{1,0:T(8,128)(2,1)S(1)}, u32[]{:S(2)}, u32[]{:S(2)}) collective-permute-start(bf16[256,1024]{1,0:T(8,128)(2,1)S(1)} %get-tuple-element.51), channel_id=1, source_target_pairs={{0,8},{4,12},{8,0},{12,4},{16,24},{20,28},{24,16},{28,20},{1,9},{5... | collective-permute-start | bytes 1572872 | tf_op jit(solution)/shard_map/ppermute | solution.py:31
  86.5 19.7 %collective-permute-start.18 = (bf16[4,3,32,1024]{3,2,1,0:T(8,128)(2,1)S(1)}, bf16[4,3,32,1024]{3,2,1,0:T(8,128)(2,1)S(1)}, u32[]{:S(2)}, u32[]{:S(2)}) collective-permute-start(bf16[4,3,32,1024]{3,2,1,0:T(8,128)(2,1)S(1)} %pad_maximum_fusion.refs_4_), channel_id=1, source_target_pairs={{0,4},{4,0},{8,12},{12,8},{16,20},{20,16},{24,28},{28,24},{1,5},{5... | collective-permute-start | bytes 2359304 | tf_op jit(solution)/shard_map/ppermute | solution.py:31
  86.6 8.9 %collective-permute-start.15 = (bf16[528,256]{1,0:T(8,128)(2,1)S(1)}, bf16[528,256]{1,0:T(8,128)(2,1)S(1)}, u32[]{:S(2)}, u32[]{:S(2)}) collective-permute-start(bf16[528,256]{1,0:T(8,128)(2,1)S(1)} %attend_near.1.refs_0_), channel_id=1, source_target_pairs={{0,1},{1,0},{2,3},{3,2},{4,5},{5,4},{6,7},{7,6},{8,9},{9,8},{10,11... | collective-permute-start | bytes 811016 | tf_op jit(solution)/shard_map/ppermute | solution.py:31
  95.5 8.8 %collective-permute-start.21 = (bf16[128,1024]{1,0:T(8,128)(2,1)S(1)}, bf16[128,1024]{1,0:T(8,128)(2,1)S(1)}, u32[]{:S(2)}, u32[]{:S(2)}) collective-permute-start(bf16[128,1024]{1,0:T(8,128)(2,1)S(1)} %slice.82), channel_id=1, source_target_pairs={{0,8},{4,12},{8,0},{12,4},{16,24},{20,28},{24,16},{28,20},{1,9},{5... | collective-permute-start | bytes 786440 | tf_op jit(solution)/shard_map/ppermute | solution.py:31
  98.7 7.5 %collective-permute-start.17 = (bf16[544,256]{1,0:T(8,128)(2,1)S(1)}, bf16[544,256]{1,0:T(8,128)(2,1)S(1)}, u32[]{:S(2)}, u32[]{:S(2)}) collective-permute-start(bf16[544,256]{1,0:T(8,128)(2,1)S(1)} %collective-permute-done.16.refs_2_), channel_id=1, source_target_pairs={{0,1},{1,0},{2,3},{3,2},{4,5},{5,4},{6,7},{7,6},{8,9},{9,8},{10,11... | collective-permute-start | bytes 835592 | tf_op jit(solution)/shard_map/ppermute | solution.py:31
  99.0 7.2 %collective-permute-start.22 = (bf16[128,1024]{1,0:T(8,128)(2,1)S(1)}, bf16[128,1024]{1,0:T(8,128)(2,1)S(1)}, u32[]{:S(2)}, u32[]{:S(2)}) collective-permute-start(bf16[128,1024]{1,0:T(8,128)(2,1)S(1)} %slice.83), channel_id=1, source_target_pairs={{0,16},{4,20},{8,24},{12,28},{16,0},{20,4},{24,8},{28,12},{1,17},{... | collective-permute-start | bytes 786440 | tf_op jit(solution)/shard_map/ppermute | solution.py:31
  106.2 4.2 %collective-permute-start.23 = (bf16[1024,1024]{1,0:T(8,128)(2,1)S(1)}, bf16[1024,1024]{1,0:T(8,128)(2,1)S(1)}, u32[]{:S(2)}, u32[]{:S(2)}) collective-permute-start(bf16[1024,1024]{1,0:T(8,128)(2,1)S(1)} %constant_dynamic-update-slice_fusion.held_ref), channel_id=1, source_target_pairs={{0,4},{4,0},{8,12},{12,8},{16,20},{20,16},{24,28},{28,24},{1,5},{5... | collective-permute-start | bytes 6291464 | tf_op jit(solution)/shard_map/ppermute | solution.py:31
  114.4 16.7 %collective-permute-start.24 = (bf16[256,1024]{1,0:T(8,128)(2,1)S(1)}, bf16[256,1024]{1,0:T(8,128)(2,1)S(1)}, u32[]{:S(2)}, u32[]{:S(2)}) collective-permute-start(bf16[256,1024]{1,0:T(8,128)(2,1)S(1)} %feed_partner.1), channel_id=1, source_target_pairs={{0,1},{1,0},{2,3},{3,2},{4,5},{5,4},{6,7},{7,6},{8,9},{9,8},{10,11... | collective-permute-start | bytes 1572872 | tf_op jit(solution)/shard_map/ppermute | solution.py:31
  115.9 13.8 %collective-permute-start.25 = (f32[3,2,1024]{2,1,0:T(2,128)S(1)}, f32[3,2,1024]{2,1,0:T(2,128)S(1)}, u32[]{:S(2)}, u32[]{:S(2)}) collective-permute-start(f32[3,2,1024]{2,1,0:T(2,128)S(1)} %get-tuple-element.56), channel_id=1, source_target_pairs={{0,1},{1,0},{2,3},{3,2},{4,5},{5,4},{6,7},{7,6},{8,9},{9,8},{10,11... | collective-permute-start | bytes 73736 | tf_op jit(solution)/shard_map/ppermute | solution.py:31
  116.6 13.2 %collective-permute-start.26 = (f32[3,2,1024]{2,1,0:T(2,128)S(1)}, f32[3,2,1024]{2,1,0:T(2,128)S(1)}, u32[]{:S(2)}, u32[]{:S(2)}) collective-permute-start(f32[3,2,1024]{2,1,0:T(2,128)S(1)} %get-tuple-element.55), channel_id=1, source_target_pairs={{0,2},{1,3},{2,0},{3,1},{4,6},{5,7},{6,4},{7,5},{8,10},{9,11},{10,... | collective-permute-start | bytes 73736 | tf_op jit(solution)/shard_map/ppermute | solution.py:31
  117.5 12.9 %collective-permute-start.27 = (f32[3,2,1024]{2,1,0:T(2,128)S(1)}, f32[3,2,1024]{2,1,0:T(2,128)S(1)}, u32[]{:S(2)}, u32[]{:S(2)}) collective-permute-start(f32[3,2,1024]{2,1,0:T(2,128)S(1)} %get-tuple-element.54), channel_id=1, source_target_pairs={{0,3},{1,2},{2,1},{3,0},{4,7},{5,6},{6,5},{7,4},{8,11},{9,10},{10,... | collective-permute-start | bytes 73736 | tf_op jit(solution)/shard_map/ppermute | solution.py:31
  (26 other events, 242.1 us)

commit v19 on v18

--- a/solution.py
+++ b/solution.py
@@ -509,7 +509,7 @@
     out_pieces = [((0, 2, 4, 6), out_all), ((1, 3, 5, 7), out_core)]
 
     half = feed_here.shape[0] // 2
-    far_up = swapped(after(feed_y, far_heads, partner_heads)[:half], "tok", 2)
+    far_up = swapped(after(feed_y, far_heads)[:half], "tok", 2)
     far_down = swapped(after(feed_x, far_heads, partner_heads)[half:], "tok", 4)
     held = jnp.concatenate([feed_here, feed_x, feed_y, far_up, far_down], axis=0)
     feed_pieces = (held, swapped(after(held, passed_heads, out_core), "tok", 1))

time: 133 us -> 131 us (0.985)
  waiting for transfers between devices: 38.7 us -> 36.6 us
    ppermute x19, waiting for transfers between devices: 25.9 us -> 23.7 us  [swapped(): return lax.ppermute(value, axis, [(i, i ^ flip) for i in range(count)])]
  transfers between devices with their start and end apart: 28 -> 28, of which waited for: 11 -> 12; matrix products, arithmetic and copies ran while one was open for 6% -> 6% of each run, Pallas kernels for 20% -> 20%
where the time goes in v19:
time: 131 us
  starting transfers between devices  48.3 us (37%)
  waiting for transfers between devices  36.6 us (28%)
  Pallas kernels  31.3 us (24%)
  local copies, waits for them, and re-layouts  8.05 us (6%)
  other arithmetic  5.16 us (4%)
    ppermute x19, starting transfers between devices, swapped(): return lax.ppermute(value, axis, [(i, i ^ flip) for i in range(count)])  29.3 us
    ppermute x19, waiting for transfers between devices, swapped(): return lax.ppermute(value, axis, [(i, i ^ flip) for i in range(count)])  23.7 us
    pallas_call x2, Pallas kernels, attend_blocks(): pl.pallas_call(functools.partial(attend_kernel, flips), out_shape=jax.Sha...  10.8 us
    ppermute x5, starting transfers between devices, over_edges(): return lax.ppermute(value, axis, edges + [(j, i) for i, j in edges])  8.74 us
    pallas_call x2, Pallas kernels, feed(): pl.pallas_call(feed_kernel, out_shape=jax.ShapeDtypeStruct((count, width)...  7.8 us
    ppermute x1, starting transfers between devices, routed_body(): feed_inner = lax.ppermute(after(feed_part, a2, b2), 'kv', [(0, 2), (3, 1)])  6.4 us
    ppermute x5, waiting for transfers between devices, over_edges(): return lax.ppermute(value, axis, edges + [(j, i) for i, j in edges])  6.26 us
    unnamed x63, local copies, waits for them, and re-layouts  6.01 us
  transfers between devices with their start and end apart: 28, of which 12 were waited for; matrix products, arithmetic and copies ran while one was open for 6% of the time, Pallas kernels for 20%

profile of v19, /device:TPU:0, one launch (start us, length us, event | category | flops | bytes accessed | tf_op | source)
XLA Modules:
  0.0 130.6 jit_solution(6510222770807237401)
XLA Ops:
  1.5 5.9 %collective-permute-start = (bf16[256,1024]{1,0:T(8,128)(2,1)}, bf16[256,1024]{1,0:T(8,128)(2,1)S(1)}, u32[]{:S(2)}, u32[]{:S(2)}) collective-permute-start(bf16[256,1024]{1,0:T(8,128)(2,1)} %own_ref.1), channel_id=1, source_target_pairs={{0,1},{2,3},{1,0},{3,2},{4,5},{6,7},{5,4},{7,6},{8,9},{10,11},{9,8... | collective-permute-start | bytes 1572872 | tf_op jit(solution)/shard_map/ppermute | solution.py:37
  8.9 1.3 %collective-permute-start.3 = (bf16[34,1024]{1,0:T(8,128)(2,1)S(1)}, bf16[34,1024]{1,0:T(8,128)(2,1)S(1)}, u32[]{:S(2)}, u32[]{:S(2)}) collective-permute-start(bf16[34,1024]{1,0:T(8,128)(2,1)S(1)} %pad_maximum_fusion.3), channel_id=1, source_target_pairs={{0,3},{1,2},{2,1},{3,0},{4,7},{5,6},{6,5},{7,4},{8,11},{9,10},{10,... | collective-permute-start | bytes 208904 | tf_op jit(solution)/shard_map/ppermute | solution.py:31
  10.4 2.9 %collective-permute-start.1 = (bf16[34,1024]{1,0:T(8,128)(2,1)S(1)}, bf16[34,1024]{1,0:T(8,128)(2,1)S(1)}, u32[]{:S(2)}, u32[]{:S(2)}) collective-permute-start(bf16[34,1024]{1,0:T(8,128)(2,1)S(1)} %pad_maximum_fusion.3), channel_id=1, source_target_pairs={{0,1},{1,0},{2,3},{3,2},{4,5},{5,4},{6,7},{7,6},{8,9},{9,8},{10,11... | collective-permute-start | bytes 208904 | tf_op jit(solution)/shard_map/ppermute | solution.py:31
  14.0 1.3 collective-permute-start.8
  15.3 6.2 %collective-permute-done.refs_1_.partner_ref = bf16[256,1024]{1,0:T(8,128)(2,1)S(1)} collective-permute-done((bf16[256,1024]{1,0:T(8,128)(2,1)}, bf16[256,1024]{1,0:T(8,128)(2,1)S(1)}, u32[]{:S(2)}, u32[]{:S(2)}) %collective-permute-start) | collective-permute-done | bytes 524320 | tf_op jit(solution)/shard_map/ppermute | solution.py:37
  24.1 3.0 %collective-permute-done.2 = bf16[34,1024]{1,0:T(8,128)(2,1)S(1)} collective-permute-done((bf16[34,1024]{1,0:T(8,128)(2,1)S(1)}, bf16[34,1024]{1,0:T(8,128)(2,1)S(1)}, u32[]{:S(2)}, u32[]{:S(2)}) %collective-permute-start.2) | collective-permute-done | bytes 69664 | tf_op jit(solution)/shard_map/ppermute | solution.py:31
  27.3 1.9 %copy-done.4 = bf16[2,1,6,128,1024]{4,3,2,1,0:T(8,128)(2,1)S(1)} copy-done((bf16[2,1,6,128,1024]{4,3,2,1,0:T(8,128)(2,1)S(1)}, bf16[2,1,6,128,1024]{4,3,2,1,0:T(8,128)(2,1)}, u32[]{:S(2)}) %copy-start.4) | copy-done | bytes 3145752
  29.2 3.8 %decode.1 = f32[3,8,1024]{2,1,0:T(8,128)S(1)} custom-call(s32[6]{0:T(128)S(1)} %fusion.12.slot_ref, s32[6]{0:T(128)S(1)} %bitcast.151, f32[8,1024]{1,0:T(8,128)S(1)} %maximum_convert_fusion.query_ref, bf16[2,1,6,128,1024]{4,3,2,1,0:T(8,128)(2,1)S(1)} %copy-done.4), custom_call_target="tpu_custom_call" | custom-call | flops 1 | bytes 1 | tf_op jit(solution)/shard_map/decode/pallas_call | solution.py:408
  34.3 1.4 %collective-permute-done.8.refs_2_ = bf16[256,1024]{1,0:T(8,128)(2,1)S(1)} collective-permute-done((bf16[256,1024]{1,0:T(8,128)(2,1)S(1)}, bf16[256,1024]{1,0:T(8,128)(2,1)S(1)}, u32[]{:S(2)}, u32[]{:S(2)}) %collective-permute-start.8) | collective-permute-done | bytes 524320 | tf_op jit(solution)/shard_map/ppermute | solution.py:476
  35.7 6.4 %collective-permute-start.11 = (bf16[256,1024]{1,0:T(8,128)(2,1)}, bf16[256,1024]{1,0:T(8,128)(2,1)S(1)}, u32[]{:S(2)}, u32[]{:S(2)}) collective-permute-start(bf16[256,1024]{1,0:T(8,128)(2,1)} %pad_maximum_fusion.1), channel_id=1, source_target_pairs={{0,2},{3,1},{4,6},{7,5},{8,10},{11,9},{12,14},{15,13},{16,18},{19,... | collective-permute-start | bytes 1572872 | tf_op jit(solution)/shard_map/ppermute | solution.py:487
  42.9 1.5 %collective-permute-start.4 = (bf16[3,32,1024]{2,1,0:T(8,128)(2,1)S(1)}, bf16[3,32,1024]{2,1,0:T(8,128)(2,1)S(1)}, u32[]{:S(2)}, u32[]{:S(2)}) collective-permute-start(bf16[3,32,1024]{2,1,0:T(8,128)(2,1)S(1)} %get-tuple-element.53), channel_id=1, source_target_pairs={{0,8},{4,12},{8,0},{12,4},{16,24},{20,28},{24,16},{28,20},{1,9},{5... | collective-permute-start | bytes 589832 | tf_op jit(solution)/shard_map/ppermute | solution.py:31
  44.4 1.5 %collective-permute-start.5 = (bf16[3,32,1024]{2,1,0:T(8,128)(2,1)S(1)}, bf16[3,32,1024]{2,1,0:T(8,128)(2,1)S(1)}, u32[]{:S(2)}, u32[]{:S(2)}) collective-permute-start(bf16[3,32,1024]{2,1,0:T(8,128)(2,1)S(1)} %get-tuple-element.53), channel_id=1, source_target_pairs={{0,16},{4,20},{8,24},{12,28},{16,0},{20,4},{24,8},{28,12},{1,17},{... | collective-permute-start | bytes 589832 | tf_op jit(solution)/shard_map/ppermute | solution.py:31
  46.4 2.6 %collective-permute-done.10.refs_3_ = bf16[256,1024]{1,0:T(8,128)(2,1)S(1)} collective-permute-done((bf16[256,1024]{1,0:T(8,128)(2,1)S(1)}, bf16[256,1024]{1,0:T(8,128)(2,1)S(1)}, u32[]{:S(2)}, u32[]{:S(2)}) %collective-permute-start.10) | collective-permute-done | bytes 524320 | tf_op jit(solution)/shard_map/ppermute | solution.py:481
  49.0 2.6 %collective-permute-done.11 = bf16[256,1024]{1,0:T(8,128)(2,1)S(1)} collective-permute-done((bf16[256,1024]{1,0:T(8,128)(2,1)}, bf16[256,1024]{1,0:T(8,128)(2,1)S(1)}, u32[]{:S(2)}, u32[]{:S(2)}) %collective-permute-start.11) | collective-permute-done | bytes 524320 | tf_op jit(solution)/shard_map/ppermute | solution.py:487
  53.0 2.3 %project_edges.1 = (bf16[512,512]{1,0:T(8,128)(2,1)S(1)}, bf16[256,512]{1,0:T(8,128)(2,1)}, bf16[256,512]{1,0:T(8,128)(2,1)}) custom-call(s32[2]{0:T(128)S(1)} %pad_add_fusion.place_ref, bf16[3,1024,256]{2,1,0:T(8,128)(2,1)S(1)} %bitcast.143, bf16[256,1024]{1,0:T(8,128)(2,1)S(1)} %copy-done.3, ...), custom_call_target="tpu_custom_call" | custom-call | flops 1 | bytes 1 | tf_op jit(solution)/shard_map/project_edges/pallas_call | solution.py:112
  56.2 1.3 %collective-permute-start.14 = (bf16[256,512]{1,0:T(8,128)(2,1)}, bf16[256,512]{1,0:T(8,128)(2,1)}, u32[]{:S(2)}, u32[]{:S(2)}) collective-permute-start(bf16[256,512]{1,0:T(8,128)(2,1)} %get-tuple-element.35), channel_id=1, source_target_pairs={{4,8},{12,16},{20,24},{8,4},{16,12},{24,20},{5,9},{13,17},{21,25},... | collective-permute-start | bytes 786440 | tf_op jit(solution)/shard_map/ppermute | solution.py:37
  60.8 2.2 %project_rest.1 = (bf16[1024,256]{1,0:T(8,128)(2,1)S(1)}, bf16[512,512]{1,0:T(8,128)(2,1)S(1)}) custom-call(s32[2]{0:T(128)S(1)} %pad_add_fusion.place_ref, bf16[3,1024,256]{2,1,0:T(8,128)(2,1)S(1)} %bitcast.144, bf16[256,1024]{1,0:T(8,128)(2,1)S(1)} %copy-done.3, bf16[256,1024]{1,0:T(8,128)(2,1)S(1)} %collective-permute-done.refs_1_.partner_ref, ...), custom_call_target="tpu_custom_call" | custom-call | flops 1 | bytes 1 | tf_op jit(solution)/shard_map/project_rest/pallas_call | solution.py:112
  63.0 5.2 %attend_far.1 = bf16[544,256]{1,0:T(8,128)(2,1)S(1)} custom-call(s32[2]{0:T(128)S(1)} %pad_add_fusion.place_ref, s32[1,48]{1,0:T(1,128)S(1)} %subtract_bitcast_fusion.starts_ref, s32[1,48]{1,0:T(1,128)S(1)} %bitcast.149, bf16[1024,256]{1,0:T(8,128)(2,1)S(1)} %get-tuple-element.37.query_ref, bf16[512,512]{1,0:T(8,128)(2,1)S(1)} %get-tuple-element.33.middle_ref, ...), custom_call_target="tpu_custom_call" | custom-call | flops 1 | bytes 1 | tf_op jit(solution)/shard_map/attend_far/pallas_call | solution.py:204
  68.2 4.7 %collective-permute-start.16 = (bf16[544,256]{1,0:T(8,128)(2,1)S(1)}, bf16[544,256]{1,0:T(8,128)(2,1)S(1)}, u32[]{:S(2)}, u32[]{:S(2)}) collective-permute-start(bf16[544,256]{1,0:T(8,128)(2,1)S(1)} %attend_far.1), channel_id=1, source_target_pairs={{0,2},{1,3},{2,0},{3,1},{4,6},{5,7},{6,4},{7,5},{8,10},{9,11},{10,... | collective-permute-start | bytes 835592 | tf_op jit(solution)/shard_map/ppermute | solution.py:31
  74.3 6.2 %collective-permute-start.20 = (bf16[256,1024]{1,0:T(8,128)(2,1)S(1)}, bf16[256,1024]{1,0:T(8,128)(2,1)S(1)}, u32[]{:S(2)}, u32[]{:S(2)}) collective-permute-start(bf16[256,1024]{1,0:T(8,128)(2,1)S(1)} %get-tuple-element.51), channel_id=1, source_target_pairs={{0,16},{4,20},{8,24},{12,28},{16,0},{20,4},{24,8},{28,12},{1,17},{... | collective-permute-start | bytes 1572872 | tf_op jit(solution)/shard_map/ppermute | solution.py:31
  80.9 5.6 %attend_near.1.refs_0_ = bf16[528,256]{1,0:T(8,128)(2,1)S(1)} custom-call(s32[2]{0:T(128)S(1)} %pad_add_fusion.place_ref, s32[1,48]{1,0:T(1,128)S(1)} %subtract_bitcast_fusion.starts_ref, s32[1,48]{1,0:T(1,128)S(1)} %bitcast.150, bf16[1024,256]{1,0:T(8,128)(2,1)S(1)} %get-tuple-element.37.query_ref, bf16[512,512]{1,0:T(8,128)(2,1)S(1)} %get-tuple-element.33.middle_ref, ...), custom_call_target="tpu_custom_call" | custom-call | flops 1 | bytes 1 | tf_op jit(solution)/shard_map/attend_near/pallas_call | solution.py:204
  86.7 5.1 %collective-permute-done.20 = bf16[256,1024]{1,0:T(8,128)(2,1)S(1)} collective-permute-done((bf16[256,1024]{1,0:T(8,128)(2,1)S(1)}, bf16[256,1024]{1,0:T(8,128)(2,1)S(1)}, u32[]{:S(2)}, u32[]{:S(2)}) %collective-permute-start.20) | collective-permute-done | bytes 524320 | tf_op jit(solution)/shard_map/ppermute | solution.py:31
  91.8 1.6 %collective-permute-start.21 = (bf16[128,1024]{1,0:T(8,128)(2,1)S(1)}, bf16[128,1024]{1,0:T(8,128)(2,1)S(1)}, u32[]{:S(2)}, u32[]{:S(2)}) collective-permute-start(bf16[128,1024]{1,0:T(8,128)(2,1)S(1)} %slice.82), channel_id=1, source_target_pairs={{0,8},{4,12},{8,0},{12,4},{16,24},{20,28},{24,16},{28,20},{1,9},{5... | collective-permute-start | bytes 786440 | tf_op jit(solution)/shard_map/ppermute | solution.py:31
  93.4 2.1 %collective-permute-done.15.refs_1_ = bf16[528,256]{1,0:T(8,128)(2,1)S(1)} collective-permute-done((bf16[528,256]{1,0:T(8,128)(2,1)S(1)}, bf16[528,256]{1,0:T(8,128)(2,1)S(1)}, u32[]{:S(2)}, u32[]{:S(2)}) %collective-permute-start.15) | collective-permute-done | bytes 270368 | tf_op jit(solution)/shard_map/ppermute | solution.py:31
  95.5 3.3 %collective-permute-start.22 = (bf16[128,1024]{1,0:T(8,128)(2,1)S(1)}, bf16[128,1024]{1,0:T(8,128)(2,1)S(1)}, u32[]{:S(2)}, u32[]{:S(2)}) collective-permute-start(bf16[128,1024]{1,0:T(8,128)(2,1)S(1)} %slice.83), channel_id=1, source_target_pairs={{0,16},{4,20},{8,24},{12,28},{16,0},{20,4},{24,8},{28,12},{1,17},{... | collective-permute-start | bytes 786440 | tf_op jit(solution)/shard_map/ppermute | solution.py:31
  100.2 4.4 %collective-permute-done.22 = bf16[128,1024]{1,0:T(8,128)(2,1)S(1)} collective-permute-done((bf16[128,1024]{1,0:T(8,128)(2,1)S(1)}, bf16[128,1024]{1,0:T(8,128)(2,1)S(1)}, u32[]{:S(2)}, u32[]{:S(2)}) %collective-permute-start.22) | collective-permute-done | bytes 262176 | tf_op jit(solution)/shard_map/ppermute | solution.py:31
  104.8 3.3 %first_norm.1 = (bf16[256,1024]{1,0:T(8,128)(2,1)S(1)}, bf16[256,1024]{1,0:T(8,128)(2,1)S(1)}) custom-call(s32[2]{0:T(128)S(1)} %pad_add_fusion.place_ref, bf16[256,1024]{1,0:T(8,128)(2,1)S(1)} %copy-done.3, bf16[256,1024]{1,0:T(8,128)(2,1)S(1)} %collective-permute-done.refs_1_.partner_ref, bf16[256,1024]{1,0:T(8,128)(2,1)S(1)} %copy-done.13, ...), custom_call_target="tpu_custom_call" | custom-call | flops 1 | bytes 1 | tf_op jit(solution)/shard_map/first_norm/pallas_call | solution.py:257
  108.9 3.9 %feed_partner.1 = bf16[256,1024]{1,0:T(8,128)(2,1)S(1)} custom-call(s32[2]{0:T(128)S(1)} %pad_add_fusion.place_ref, bf16[256,1024]{1,0:T(8,128)(2,1)S(1)} %get-tuple-element.40.rows_ref, bf16[1024,1024]{1,0:T(8,128)(2,1)S(1)} %copy-done, bf16[1024,1024]{1,0:T(8,128)(2,1)S(1)} %copy-done.1, bf16[1024,1024]{1,0:T(8,128)(2,1)S(1)} %constant_dynamic-update-slice_fusion.held_ref, ...), custom_call_target="tpu_custom_call" | custom-call | flops 1 | bytes 1 | tf_op jit(solution)/shard_map/feed_partner/pallas_call | solution.py:326
  113.4 1.6 %collective-permute-start.25 = (f32[3,2,1024]{2,1,0:T(2,128)S(1)}, f32[3,2,1024]{2,1,0:T(2,128)S(1)}, u32[]{:S(2)}, u32[]{:S(2)}) collective-permute-start(f32[3,2,1024]{2,1,0:T(2,128)S(1)} %get-tuple-element.56), channel_id=1, source_target_pairs={{0,1},{1,0},{2,3},{3,2},{4,5},{5,4},{6,7},{7,6},{8,9},{9,8},{10,11... | collective-permute-start | bytes 73736 | tf_op jit(solution)/shard_map/ppermute | solution.py:31
  115.8 2.0 %collective-permute-start.27 = (f32[3,2,1024]{2,1,0:T(2,128)S(1)}, f32[3,2,1024]{2,1,0:T(2,128)S(1)}, u32[]{:S(2)}, u32[]{:S(2)}) collective-permute-start(f32[3,2,1024]{2,1,0:T(2,128)S(1)} %get-tuple-element.54), channel_id=1, source_target_pairs={{0,3},{1,2},{2,1},{3,0},{4,7},{5,6},{6,5},{7,4},{8,11},{9,10},{10,... | collective-permute-start | bytes 73736 | tf_op jit(solution)/shard_map/ppermute | solution.py:31
  117.9 3.9 %feed_own.1.near_ref = f32[256,1024]{1,0:T(8,128)S(1)} custom-call(s32[2]{0:T(128)S(1)} %pad_add_fusion.place_ref, bf16[256,1024]{1,0:T(8,128)(2,1)S(1)} %get-tuple-element.44.rows_ref.normed_ref, bf16[1024,1024]{1,0:T(8,128)(2,1)S(1)} %copy-done, bf16[1024,1024]{1,0:T(8,128)(2,1)S(1)} %copy-done.1, ...), custom_call_target="tpu_custom_call" | custom-call | flops 1 | bytes 1 | tf_op jit(solution)/shard_map/feed_own/pallas_call | solution.py:326
  121.8 6.4 %collective-permute-done.25 = f32[3,2,1024]{2,1,0:T(2,128)S(1)} collective-permute-done((f32[3,2,1024]{2,1,0:T(2,128)S(1)}, f32[3,2,1024]{2,1,0:T(2,128)S(1)}, u32[]{:S(2)}, u32[]{:S(2)}) %collective-permute-start.25) | collective-permute-done | bytes 24608 | tf_op jit(solution)/shard_map/ppermute | solution.py:31
  (119 shorter events, 21.8 us)
Async XLA Ops:
  0.6 26.6 %copy-start.28 = (bf16[2,1024]{1,0:T(2,128)(2,1)S(1)}, bf16[2,1024]{1,0:T(2,128)(2,1)}, u32[]{:S(2)}) copy-start(bf16[2,1024]{1,0:T(2,128)(2,1)} %param.24) | copy-start | bytes 12292
  0.6 26.6 %copy-start.18 = (s32[1,6]{1,0:T(1,128)S(1)}, s32[1,6]{1,0:T(1,128)}, u32[]{:S(2)}) copy-start(s32[1,6]{1,0:T(1,128)} %param.27) | copy-start | bytes 76
  0.7 13.3 %collective-permute-start.7 = (bf16[256,1024]{1,0:T(8,128)(2,1)}, bf16[256,1024]{1,0:T(8,128)(2,1)S(1)}, u32[]{:S(2)}, u32[]{:S(2)}) collective-permute-start(bf16[256,1024]{1,0:T(8,128)(2,1)} %own_ref.1), channel_id=1, source_target_pairs={{1,2},{2,1},{5,6},{6,5},{9,10},{10,9},{13,14},{14,13},{17,18},{18,... | collective-permute-start | bytes 1572872 | tf_op jit(solution)/shard_map/ppermute | solution.py:37
  1.5 20.0 %collective-permute-start = (bf16[256,1024]{1,0:T(8,128)(2,1)}, bf16[256,1024]{1,0:T(8,128)(2,1)S(1)}, u32[]{:S(2)}, u32[]{:S(2)}) collective-permute-start(bf16[256,1024]{1,0:T(8,128)(2,1)} %own_ref.1), channel_id=1, source_target_pairs={{0,1},{2,3},{1,0},{3,2},{4,5},{6,7},{5,4},{7,6},{8,9},{10,11},{9,8... | collective-permute-start | bytes 1572872 | tf_op jit(solution)/shard_map/ppermute | solution.py:37
  8.9 15.2 %collective-permute-start.3 = (bf16[34,1024]{1,0:T(8,128)(2,1)S(1)}, bf16[34,1024]{1,0:T(8,128)(2,1)S(1)}, u32[]{:S(2)}, u32[]{:S(2)}) collective-permute-start(bf16[34,1024]{1,0:T(8,128)(2,1)S(1)} %pad_maximum_fusion.3), channel_id=1, source_target_pairs={{0,3},{1,2},{2,1},{3,0},{4,7},{5,6},{6,5},{7,4},{8,11},{9,10},{10,... | collective-permute-start | bytes 208904 | tf_op jit(solution)/shard_map/ppermute | solution.py:31
  10.3 16.9 %collective-permute-start.2 = (bf16[34,1024]{1,0:T(8,128)(2,1)S(1)}, bf16[34,1024]{1,0:T(8,128)(2,1)S(1)}, u32[]{:S(2)}, u32[]{:S(2)}) collective-permute-start(bf16[34,1024]{1,0:T(8,128)(2,1)S(1)} %pad_maximum_fusion.3), channel_id=1, source_target_pairs={{0,2},{1,3},{2,0},{3,1},{4,6},{5,7},{6,4},{7,5},{8,10},{9,11},{10,... | collective-permute-start | bytes 208904 | tf_op jit(solution)/shard_map/ppermute | solution.py:31
  10.4 16.8 %collective-permute-start.1 = (bf16[34,1024]{1,0:T(8,128)(2,1)S(1)}, bf16[34,1024]{1,0:T(8,128)(2,1)S(1)}, u32[]{:S(2)}, u32[]{:S(2)}) collective-permute-start(bf16[34,1024]{1,0:T(8,128)(2,1)S(1)} %pad_maximum_fusion.3), channel_id=1, source_target_pairs={{0,1},{1,0},{2,3},{3,2},{4,5},{5,4},{6,7},{7,6},{8,9},{9,8},{10,11... | collective-permute-start | bytes 208904 | tf_op jit(solution)/shard_map/ppermute | solution.py:31
  14.0 21.8 %collective-permute-start.8 = (bf16[256,1024]{1,0:T(8,128)(2,1)S(1)}, bf16[256,1024]{1,0:T(8,128)(2,1)S(1)}, u32[]{:S(2)}, u32[]{:S(2)}) collective-permute-start(bf16[256,1024]{1,0:T(8,128)(2,1)S(1)} %collective-permute-done.7.refs_4_), channel_id=1, source_target_pairs={{1,0},{2,3},{5,4},{6,7},{9,8},{10,11},{13,12},{14,15},{17,16},{18,... | collective-permute-start | bytes 1572872 | tf_op jit(solution)/shard_map/ppermute | solution.py:476
  21.5 11.4 %collective-permute-start.9 = (bf16[256,1024]{1,0:T(8,128)(2,1)S(1)}, bf16[256,1024]{1,0:T(8,128)(2,1)S(1)}, u32[]{:S(2)}, u32[]{:S(2)}) collective-permute-start(bf16[256,1024]{1,0:T(8,128)(2,1)S(1)} %collective-permute-done.refs_1_.partner_ref), channel_id=1, source_target_pairs={{1,2},{2,1},{5,6},{6,5},{9,10},{10,9},{13,14},{14,13},{17,18},{18,... | collective-permute-start | bytes 1572872 | tf_op jit(solution)/shard_map/ppermute | solution.py:37
  29.2 23.8 %copy-start.2 = (bf16[1024,3,256]{2,0,1:T(8,128)(2,1)S(1)}, bf16[1024,3,256]{2,0,1:T(8,128)(2,1)}, u32[]{:S(2)}) copy-start(bf16[1024,3,256]{2,0,1:T(8,128)(2,1)} %param.15) | copy-start | bytes 4718596
  29.2 23.8 %copy-start.3 = (bf16[256,1024]{1,0:T(8,128)(2,1)S(1)}, bf16[256,1024]{1,0:T(8,128)(2,1)}, u32[]{:S(2)}) copy-start(bf16[256,1024]{1,0:T(8,128)(2,1)} %own_ref.1) | copy-start | bytes 1572868
  33.0 16.0 %collective-permute-start.10 = (bf16[256,1024]{1,0:T(8,128)(2,1)S(1)}, bf16[256,1024]{1,0:T(8,128)(2,1)S(1)}, u32[]{:S(2)}, u32[]{:S(2)}) collective-permute-start(bf16[256,1024]{1,0:T(8,128)(2,1)S(1)} %collective-permute-done.9.refs_5_), channel_id=1, source_target_pairs={{1,0},{2,3},{5,4},{6,7},{9,8},{10,11},{13,12},{14,15},{17,16},{18,... | collective-permute-start | bytes 1572872 | tf_op jit(solution)/shard_map/ppermute | solution.py:481
  35.7 15.8 %collective-permute-start.11 = (bf16[256,1024]{1,0:T(8,128)(2,1)}, bf16[256,1024]{1,0:T(8,128)(2,1)S(1)}, u32[]{:S(2)}, u32[]{:S(2)}) collective-permute-start(bf16[256,1024]{1,0:T(8,128)(2,1)} %pad_maximum_fusion.1), channel_id=1, source_target_pairs={{0,2},{3,1},{4,6},{7,5},{8,10},{11,9},{12,14},{15,13},{16,18},{19,... | collective-permute-start | bytes 1572872 | tf_op jit(solution)/shard_map/ppermute | solution.py:487
  42.9 10.0 %collective-permute-start.4 = (bf16[3,32,1024]{2,1,0:T(8,128)(2,1)S(1)}, bf16[3,32,1024]{2,1,0:T(8,128)(2,1)S(1)}, u32[]{:S(2)}, u32[]{:S(2)}) collective-permute-start(bf16[3,32,1024]{2,1,0:T(8,128)(2,1)S(1)} %get-tuple-element.53), channel_id=1, source_target_pairs={{0,8},{4,12},{8,0},{12,4},{16,24},{20,28},{24,16},{28,20},{1,9},{5... | collective-permute-start | bytes 589832 | tf_op jit(solution)/shard_map/ppermute | solution.py:31
  44.4 8.6 %collective-permute-start.5 = (bf16[3,32,1024]{2,1,0:T(8,128)(2,1)S(1)}, bf16[3,32,1024]{2,1,0:T(8,128)(2,1)S(1)}, u32[]{:S(2)}, u32[]{:S(2)}) collective-permute-start(bf16[3,32,1024]{2,1,0:T(8,128)(2,1)S(1)} %get-tuple-element.53), channel_id=1, source_target_pairs={{0,16},{4,20},{8,24},{12,28},{16,0},{20,4},{24,8},{28,12},{1,17},{... | collective-permute-start | bytes 589832 | tf_op jit(solution)/shard_map/ppermute | solution.py:31
  45.9 7.0 %collective-permute-start.6 = (bf16[3,32,1024]{2,1,0:T(8,128)(2,1)S(1)}, bf16[3,32,1024]{2,1,0:T(8,128)(2,1)S(1)}, u32[]{:S(2)}, u32[]{:S(2)}) collective-permute-start(bf16[3,32,1024]{2,1,0:T(8,128)(2,1)S(1)} %get-tuple-element.53), channel_id=1, source_target_pairs={{0,24},{4,28},{8,16},{12,20},{16,8},{20,12},{24,0},{28,4},{1,25},{... | collective-permute-start | bytes 589832 | tf_op jit(solution)/shard_map/ppermute | solution.py:31
  51.5 21.4 %collective-permute-start.12 = (bf16[256,1024]{1,0:T(8,128)(2,1)}, bf16[256,1024]{1,0:T(8,128)(2,1)}, u32[]{:S(2)}, u32[]{:S(2)}) collective-permute-start(bf16[256,1024]{1,0:T(8,128)(2,1)} %pad_maximum_fusion.1), channel_id=1, source_target_pairs={{1,3},{2,0},{5,7},{6,4},{9,11},{10,8},{13,15},{14,12},{17,19},{18,... | collective-permute-start | bytes 1572872 | tf_op jit(solution)/shard_map/ppermute | solution.py:488
  56.2 6.8 %collective-permute-start.13 = (bf16[256,512]{1,0:T(8,128)(2,1)}, bf16[256,512]{1,0:T(8,128)(2,1)S(1)}, u32[]{:S(2)}, u32[]{:S(2)}) collective-permute-start(bf16[256,512]{1,0:T(8,128)(2,1)} %get-tuple-element.34), channel_id=1, source_target_pairs={{0,4},{8,12},{16,20},{24,28},{4,0},{12,8},{20,16},{28,24},{1,5},{9... | collective-permute-start | bytes 786440 | tf_op jit(solution)/shard_map/ppermute | solution.py:37
  56.2 6.8 %collective-permute-start.14 = (bf16[256,512]{1,0:T(8,128)(2,1)}, bf16[256,512]{1,0:T(8,128)(2,1)}, u32[]{:S(2)}, u32[]{:S(2)}) collective-permute-start(bf16[256,512]{1,0:T(8,128)(2,1)} %get-tuple-element.35), channel_id=1, source_target_pairs={{4,8},{12,16},{20,24},{8,4},{16,12},{24,20},{5,9},{13,17},{21,25},... | collective-permute-start | bytes 786440 | tf_op jit(solution)/shard_map/ppermute | solution.py:37
  68.2 18.3 %collective-permute-start.16 = (bf16[544,256]{1,0:T(8,128)(2,1)S(1)}, bf16[544,256]{1,0:T(8,128)(2,1)S(1)}, u32[]{:S(2)}, u32[]{:S(2)}) collective-permute-start(bf16[544,256]{1,0:T(8,128)(2,1)S(1)} %attend_far.1), channel_id=1, source_target_pairs={{0,2},{1,3},{2,0},{3,1},{4,6},{5,7},{6,4},{7,5},{8,10},{9,11},{10,... | collective-permute-start | bytes 835592 | tf_op jit(solution)/shard_map/ppermute | solution.py:31
  74.3 17.5 %collective-permute-start.20 = (bf16[256,1024]{1,0:T(8,128)(2,1)S(1)}, bf16[256,1024]{1,0:T(8,128)(2,1)S(1)}, u32[]{:S(2)}, u32[]{:S(2)}) collective-permute-start(bf16[256,1024]{1,0:T(8,128)(2,1)S(1)} %get-tuple-element.51), channel_id=1, source_target_pairs={{0,16},{4,20},{8,24},{12,28},{16,0},{20,4},{24,8},{28,12},{1,17},{... | collective-permute-start | bytes 1572872 | tf_op jit(solution)/shard_map/ppermute | solution.py:31
  80.5 15.0 %collective-permute-start.19 = (bf16[256,1024]{1,0:T(8,128)(2,1)S(1)}, bf16[256,1024]{1,0:T(8,128)(2,1)S(1)}, u32[]{:S(2)}, u32[]{:S(2)}) collective-permute-start(bf16[256,1024]{1,0:T(8,128)(2,1)S(1)} %get-tuple-element.51), channel_id=1, source_target_pairs={{0,8},{4,12},{8,0},{12,4},{16,24},{20,28},{24,16},{28,20},{1,9},{5... | collective-permute-start | bytes 1572872 | tf_op jit(solution)/shard_map/ppermute | solution.py:31
  86.5 18.2 %collective-permute-start.18 = (bf16[4,3,32,1024]{3,2,1,0:T(8,128)(2,1)S(1)}, bf16[4,3,32,1024]{3,2,1,0:T(8,128)(2,1)S(1)}, u32[]{:S(2)}, u32[]{:S(2)}) collective-permute-start(bf16[4,3,32,1024]{3,2,1,0:T(8,128)(2,1)S(1)} %pad_maximum_fusion.refs_4_), channel_id=1, source_target_pairs={{0,4},{4,0},{8,12},{12,8},{16,20},{20,16},{24,28},{28,24},{1,5},{5... | collective-permute-start | bytes 2359304 | tf_op jit(solution)/shard_map/ppermute | solution.py:31
  86.6 8.9 %collective-permute-start.15 = (bf16[528,256]{1,0:T(8,128)(2,1)S(1)}, bf16[528,256]{1,0:T(8,128)(2,1)S(1)}, u32[]{:S(2)}, u32[]{:S(2)}) collective-permute-start(bf16[528,256]{1,0:T(8,128)(2,1)S(1)} %attend_near.1.refs_0_), channel_id=1, source_target_pairs={{0,1},{1,0},{2,3},{3,2},{4,5},{5,4},{6,7},{7,6},{8,9},{9,8},{10,11... | collective-permute-start | bytes 811016 | tf_op jit(solution)/shard_map/ppermute | solution.py:31
  91.8 8.4 %collective-permute-start.21 = (bf16[128,1024]{1,0:T(8,128)(2,1)S(1)}, bf16[128,1024]{1,0:T(8,128)(2,1)S(1)}, u32[]{:S(2)}, u32[]{:S(2)}) collective-permute-start(bf16[128,1024]{1,0:T(8,128)(2,1)S(1)} %slice.82), channel_id=1, source_target_pairs={{0,8},{4,12},{8,0},{12,4},{16,24},{20,28},{24,16},{28,20},{1,9},{5... | collective-permute-start | bytes 786440 | tf_op jit(solution)/shard_map/ppermute | solution.py:31
  93.4 11.3 %collective-permute-start.17 = (bf16[544,256]{1,0:T(8,128)(2,1)S(1)}, bf16[544,256]{1,0:T(8,128)(2,1)S(1)}, u32[]{:S(2)}, u32[]{:S(2)}) collective-permute-start(bf16[544,256]{1,0:T(8,128)(2,1)S(1)} %collective-permute-done.16.refs_2_), channel_id=1, source_target_pairs={{0,1},{1,0},{2,3},{3,2},{4,5},{5,4},{6,7},{7,6},{8,9},{9,8},{10,11... | collective-permute-start | bytes 835592 | tf_op jit(solution)/shard_map/ppermute | solution.py:31
  95.5 9.2 %collective-permute-start.22 = (bf16[128,1024]{1,0:T(8,128)(2,1)S(1)}, bf16[128,1024]{1,0:T(8,128)(2,1)S(1)}, u32[]{:S(2)}, u32[]{:S(2)}) collective-permute-start(bf16[128,1024]{1,0:T(8,128)(2,1)S(1)} %slice.83), channel_id=1, source_target_pairs={{0,16},{4,20},{8,24},{12,28},{16,0},{20,4},{24,8},{28,12},{1,17},{... | collective-permute-start | bytes 786440 | tf_op jit(solution)/shard_map/ppermute | solution.py:31
  104.7 4.2 %collective-permute-start.23 = (bf16[1024,1024]{1,0:T(8,128)(2,1)S(1)}, bf16[1024,1024]{1,0:T(8,128)(2,1)S(1)}, u32[]{:S(2)}, u32[]{:S(2)}) collective-permute-start(bf16[1024,1024]{1,0:T(8,128)(2,1)S(1)} %constant_dynamic-update-slice_fusion.held_ref), channel_id=1, source_target_pairs={{0,4},{4,0},{8,12},{12,8},{16,20},{20,16},{24,28},{28,24},{1,5},{5... | collective-permute-start | bytes 6291464 | tf_op jit(solution)/shard_map/ppermute | solution.py:31
  112.8 16.5 %collective-permute-start.24 = (bf16[256,1024]{1,0:T(8,128)(2,1)S(1)}, bf16[256,1024]{1,0:T(8,128)(2,1)S(1)}, u32[]{:S(2)}, u32[]{:S(2)}) collective-permute-start(bf16[256,1024]{1,0:T(8,128)(2,1)S(1)} %feed_partner.1), channel_id=1, source_target_pairs={{0,1},{1,0},{2,3},{3,2},{4,5},{5,4},{6,7},{7,6},{8,9},{9,8},{10,11... | collective-permute-start | bytes 1572872 | tf_op jit(solution)/shard_map/ppermute | solution.py:31
  113.4 14.8 %collective-permute-start.25 = (f32[3,2,1024]{2,1,0:T(2,128)S(1)}, f32[3,2,1024]{2,1,0:T(2,128)S(1)}, u32[]{:S(2)}, u32[]{:S(2)}) collective-permute-start(f32[3,2,1024]{2,1,0:T(2,128)S(1)} %get-tuple-element.56), channel_id=1, source_target_pairs={{0,1},{1,0},{2,3},{3,2},{4,5},{5,4},{6,7},{7,6},{8,9},{9,8},{10,11... | collective-permute-start | bytes 73736 | tf_op jit(solution)/shard_map/ppermute | solution.py:31
  115.0 13.2 %collective-permute-start.26 = (f32[3,2,1024]{2,1,0:T(2,128)S(1)}, f32[3,2,1024]{2,1,0:T(2,128)S(1)}, u32[]{:S(2)}, u32[]{:S(2)}) collective-permute-start(f32[3,2,1024]{2,1,0:T(2,128)S(1)} %get-tuple-element.55), channel_id=1, source_target_pairs={{0,2},{1,3},{2,0},{3,1},{4,6},{5,7},{6,4},{7,5},{8,10},{9,11},{10,... | collective-permute-start | bytes 73736 | tf_op jit(solution)/shard_map/ppermute | solution.py:31
  115.8 12.8 %collective-permute-start.27 = (f32[3,2,1024]{2,1,0:T(2,128)S(1)}, f32[3,2,1024]{2,1,0:T(2,128)S(1)}, u32[]{:S(2)}, u32[]{:S(2)}) collective-permute-start(f32[3,2,1024]{2,1,0:T(2,128)S(1)} %get-tuple-element.54), channel_id=1, source_target_pairs={{0,3},{1,2},{2,1},{3,0},{4,7},{5,6},{6,5},{7,4},{8,11},{9,10},{10,... | collective-permute-start | bytes 73736 | tf_op jit(solution)/shard_map/ppermute | solution.py:31
  (26 other events, 239.0 us)
